TPU v7x, 32 devices: a whole 2x2x4 slice. The times are simulated.
32 devices in a mesh: groups: 2 (over y), adapter: 4 (over z), segment: 2 (over x), replica: 2 (over core).
Axes of the slice: x: 2, y: 2, z: 4, core: 2. Of those that a mesh axis runs over, the one named last changes fastest.
Arguments:
- saved_layer_input: bfloat16 [2, 2816, 4096], P('segment', ('groups', 'adapter', 'replica')), parts along dimension 1, may hold values from -6 to 6
- value_output_gradient: bfloat16 [2, 2816, 1024], P('segment', ('groups', 'adapter', 'replica')), parts along dimension 1, may hold values from -6 to 6
- token_adapter_index: int32 [2, 2816, 1], P('segment', ('groups', 'adapter', 'replica')), parts along dimension 1, may hold values from 0 to 7; in each aligned block of 176 rows (0 to 175, 176 to 351, ..., all dimensions but the last counted through in order) at most 33 rows name the same one
- adapter_slot_index: int32 [16], P('groups'), parts along dimension 0, may hold values from 0 to 7, each once
- frozen_value_weight: bfloat16 [2, 4096, 1024], P('segment', 'adapter'), may hold values from -0.1875 to 0.1875
- adapter_down_weight: bfloat16 [2, 8, 16, 4096], P('segment', 'adapter'), may hold values from -0.09375 to 0.09375
- adapter_up_weight: bfloat16 [2, 8, 16, 1024], P('segment', 'adapter'), may hold values from -0.1875 to 0.1875
Outputs:
- passed_grads: bfloat16 [2, 2816, 4096], P('segment', ('groups', 'adapter', 'replica')), parts along dimension 1
- grad_down: bfloat16 [4, 8, 16, 4096], P(('groups', 'segment'), 'adapter'), parts along dimension 0
- grad_up: bfloat16 [4, 8, 16, 1024], P(('groups', 'segment'), 'adapter'), parts along dimension 0
There are 2 independent parts, one for each index of `groups`. A program takes and returns all parts, laid end to end along the dimension named above; an argument that names none is the same for every part. Nothing has to cross between parts.
Inputs may be any that keep to these rules, and one draw needn't show every extreme that they name: `token_adapter_index`: within the 176 tokens of one device no adapter is named by more than 33 tokens. `adapter_slot_index`: each slot is taken by exactly one adapter.
All inputs are finite; a program needn't handle non-finite values.
Results may differ from a plain program's by a relative error of at most 0.0085.
Values may be sent and summed in bfloat16 or wider, within the bound.
No kernel may reach another device: no remote copies, remote signals or barrier semaphores. Data moves between devices by JAX's collectives and lax.ppermute only.
A program may use at most 64 MiB of HBM per device.

v0:
```python
import jax
import jax.numpy as jnp
from jax import lax
from jax.sharding import PartitionSpec as P

ADAPTER_SCALE = 2.0


def passed_along(x, axis, by):
    size = lax.axis_size(axis)
    return lax.ppermute(x, axis, [(i, (i + by) % size) for i in range(size)])


def on_device(
    saved_layer_input,
    value_output_gradient,
    token_adapter_index,
    adapter_slot_index,
    frozen_value_weight,
    adapter_down_weight,
    adapter_up_weight,
):
    inputs = saved_layer_input[0]
    grad_rows = value_output_gradient[0]
    row_ids = token_adapter_index[0, :, 0]
    row_count = inputs.shape[0]
    hidden_width = inputs.shape[1]
    value_proj_width = grad_rows.shape[1]
    count_adapters = adapter_slot_index.shape[0]
    holder_count = lax.axis_size("adapter")
    slots_per_holder = adapter_down_weight.shape[1]
    slot_capacity = (3 * row_count + 2 * count_adapters - 1) // (2 * count_adapters)
    local_frozen = frozen_value_weight[0]
    part = jnp.einsum(
        "tk,dk->td",
        grad_rows,
        lax.all_gather(local_frozen, "adapter", axis=0, tiled=True),
        preferred_element_type=jnp.float32,
    )
    frozen_matrix = part.astype(jnp.bfloat16)
    slot_range = jnp.arange(count_adapters, dtype=jnp.int32)
    onehot = (row_ids[:, None] == slot_range[None, :]).astype(jnp.int32)
    slot_row = jnp.sum(onehot * adapter_slot_index[None, :], axis=1)
    row_rank = jnp.sum((jnp.cumsum(onehot, axis=0) - onehot) * onehot, axis=1)
    token_position = slot_row * slot_capacity + row_rank
    send_in = (
        jnp.zeros((count_adapters * slot_capacity, hidden_width), jnp.bfloat16)
        .at[token_position]
        .set(inputs)
    )
    send_grad = (
        jnp.zeros((count_adapters * slot_capacity, value_proj_width), jnp.bfloat16)
        .at[token_position]
        .set(grad_rows)
    )
    send_in = send_in.reshape(holder_count, slots_per_holder * slot_capacity, hidden_width)
    send_grad = send_grad.reshape(holder_count, slots_per_holder * slot_capacity, value_proj_width)
    recv_in, recv_grad = (
        lax.all_to_all(send_in, "adapter", split_axis=0, concat_axis=0, tiled=True),
        lax.all_to_all(send_grad, "adapter", split_axis=0, concat_axis=0, tiled=True),
    )
    recv_in = recv_in.reshape(holder_count, slots_per_holder, slot_capacity, hidden_width)
    recv_grad = recv_grad.reshape(holder_count, slots_per_holder, slot_capacity, value_proj_width)
    resident_down_maps = adapter_down_weight[0]
    resident_up_maps = adapter_up_weight[0]
    proj_in = jnp.einsum(
        "nacd,ard->nacr", recv_in, resident_down_maps, preferred_element_type=jnp.float32
    ).astype(jnp.bfloat16)
    proj_grad = jnp.einsum(
        "nack,ark->nacr", recv_grad, resident_up_maps, preferred_element_type=jnp.float32
    ).astype(jnp.bfloat16)
    adapter_backward = (
        ADAPTER_SCALE
        * jnp.einsum(
            "nacr,ard->nacd", proj_grad, resident_down_maps, preferred_element_type=jnp.float32
        )
    ).astype(jnp.bfloat16)
    returned_gradient = lax.all_to_all(
        adapter_backward.reshape(holder_count, slots_per_holder * slot_capacity, hidden_width),
        "adapter",
        split_axis=0,
        concat_axis=0,
        tiled=True,
    )
    adapter_row_block = returned_gradient.reshape(count_adapters * slot_capacity, hidden_width)[
        token_position
    ]
    down_grad = ADAPTER_SCALE * jnp.einsum(
        "nacr,nacd->ard", proj_grad, recv_in, preferred_element_type=jnp.float32
    )
    up_grad = ADAPTER_SCALE * jnp.einsum(
        "nacr,nack->ark", proj_in, recv_grad, preferred_element_type=jnp.float32
    )
    down_grad, up_grad = lax.psum((down_grad, up_grad), "replica")
    gradient_total = (
        frozen_matrix.astype(jnp.float32) + adapter_row_block.astype(jnp.float32)
    ).astype(jnp.bfloat16)
    passed = passed_along(gradient_total, "segment", -1)
    return (passed[None], down_grad.astype(jnp.bfloat16)[None], up_grad.astype(jnp.bfloat16)[None])


def solution(mesh):
    placed = (
        P("segment", ("groups", "adapter", "replica"), None),
        P("segment", ("groups", "adapter", "replica"), None),
        P("segment", ("groups", "adapter", "replica"), None),
        P("groups"),
        P("segment", "adapter", None),
        P("segment", "adapter", None, None),
        P("segment", "adapter", None, None),
    )
    return jax.shard_map(
        on_device,
        mesh=mesh,
        in_specs=placed,
        out_specs=(
            P("segment", ("groups", "adapter", "replica"), None),
            P(("groups", "segment"), "adapter", None, None),
            P(("groups", "segment"), "adapter", None, None),
        ),
        check_vma=False,
    )
```

profile of v0, /device:TPU:0, one launch (start us, length us, event | category | flops | bytes accessed | tf_op | source)
XLA Modules:
  0.0 319.6 jit_solution(17803317795890405798)
XLA Ops:
  7.2 0.7 all-gather.3.cloned.1.call-update
  7.9 0.7 iota_compare_fusion
  8.6 0.6 reduce-window.6
  9.2 0.2 slice_reduce_fusion
  9.5 0.1 add_bitcast_fusion
  9.5 0.8 select_reduce_fusion
  10.4 1.5 scatter_custom_fusion
  11.9 0.1 reshape.65
  12.0 38.3 %all_to_all.15 = bf16[4,66,1024]{2,1,0:T(8,128)(2,1)S(1)} all-to-all(bf16[4,66,1024]{2,1,0:T(8,128)(2,1)S(1)} %reshape.65), channel_id=1, replica_groups=mesh['groups'=2,'adapter'=4,'segment'=2,'replica'=2] {'adapter'}, dimensions={0} | all-to-all | bytes 1081344 | tf_op jit(solution)/shard_map/all_to_all | solution.py:60
  50.3 0.4 copy.17
  50.8 0.8 copy-done.3
  51.6 0.5 fusion.26
  52.0 0.9 fusion.3
  52.9 1.7 copy.19
  54.6 2.6 copy.20
  57.2 4.5 %all-to-all-start.1 = ((bf16[4,66,4096]{2,1,0:T(8,128)(2,1)}), bf16[4,66,4096]{2,1,0:T(8,128)(2,1)}, u32[]{:S(2)}, u32[]{:S(2)}) async-start(bf16[4,66,4096]{2,1,0:T(8,128)(2,1)} %copy.20), calls=%async_computation.1 | async-start | bytes 4718592 | tf_op jit(solution)/shard_map/all_to_all | solution.py:78
  61.7 4.1 %scatter_custom_fusion.1 = bf16[264,4096]{1,0:T(8,128)(2,1)} fusion(s32[176]{0:T(256)S(1)} %bitcast.82, bf16[1,176,4096]{2,1,0:T(8,128)(2,1)S(1)} %copy-done, bf16[]{:T(256)} %constant.6.clone.1), kind=kCustom, calls=%fused_computation.17 | custom fusion | bytes 3604482 | tf_op jit(solution)/shard_map/scatter | solution.py:49
  65.9 3.7 %reshape.69 = bf16[4,66,4096]{2,1,0:T(8,128)(2,1)} reshape(bf16[264,4096]{1,0:T(8,128)(2,1)} %scatter_custom_fusion.1) | data formatting | bytes 4325376 | tf_op jit(solution)/shard_map/reshape | solution.py:56
  69.5 109.9 %all-to-all-done.1 = bf16[4,66,4096]{2,1,0:T(8,128)(2,1)} async-done(((bf16[4,66,4096]{2,1,0:T(8,128)(2,1)}), bf16[4,66,4096]{2,1,0:T(8,128)(2,1)}, u32[]{:S(2)}, u32[]{:S(2)}) %all-to-all-start.1) | async-done | bytes 2162720 | tf_op jit(solution)/shard_map/all_to_all | solution.py:78
  179.4 4.7 %all-to-all-start.2 = ((bf16[4,66,4096]{2,1,0:T(8,128)(2,1)}), bf16[4,66,4096]{2,1,0:T(8,128)(2,1)}, u32[]{:S(2)}, u32[]{:S(2)}) async-start(bf16[4,66,4096]{2,1,0:T(8,128)(2,1)} %reshape.69), calls=%async_computation.2 | async-start | bytes 4718592 | tf_op jit(solution)/shard_map/all_to_all | solution.py:59
  184.2 3.6 %reshape.68 = bf16[264,4096]{1,0:T(8,128)(2,1)} reshape(bf16[4,66,4096]{2,1,0:T(8,128)(2,1)} %all-to-all-done.1) | data formatting | bytes 4325376 | tf_op jit(solution)/shard_map/reshape | solution.py:85
  187.8 4.7 %gather_fusion = bf16[176,4096]{1,0:T(8,128)(2,1)S(1)} fusion(bf16[264,4096]{1,0:T(8,128)(2,1)} %reshape.68, s32[1024]{0:T(1024)S(1)} %pad_clamp_fusion), kind=kCustom, calls=%fused_computation | custom fusion | bytes 2884288 | tf_op jit(solution)/shard_map/gather | solution.py:85
  192.5 77.9 %all-gather.3.cloned.1.call-done = bf16[1,4096,1024]{2,1,0:T(8,128)(2,1)} async-done(((bf16[1,1024,1024]{2,1,0:T(8,128)(2,1)}), bf16[1,4096,1024]{2,1,0:T(8,128)(2,1)}) %all-gather.3.cloned.1.call-update) | async-done | bytes 8388624 | tf_op jit(solution)/shard_map/all_gather | solution.py:37
  270.5 7.4 %fusion.13 = bf16[176,4096]{1,0:T(8,128)(2,1)} fusion(bf16[1,4096,1024]{2,1,0:T(8,128)(2,1)} %all-gather.3.cloned.1.call-done, bf16[176,4096]{1,0:T(8,128)(2,1)S(1)} %gather_fusion, bf16[1,176,1024]{2,1,0:T(8,128)(2,1)S(1)} %copy-done.2), kind=kOutput, calls=%fused_computation.11 | convolution fusion | flops 1479999488 | bytes 11632640 | tf_op jit(solution)/shard_map/tk,dk->td/dot_general | solution.py:34
  277.9 1.5 collective-permute-start
  279.4 3.3 %copy.21 = bf16[4,66,4096]{2,0,1:T(4,128)(2,1)S(1)} copy(bf16[4,66,4096]{2,1,0:T(8,128)(2,1)} %all-to-all-done.2) | data formatting | bytes 4325376 | tf_op jit(solution)/shard_map/all_to_all | solution.py:59
  282.7 1.3 copy-done.1
  284.0 1.4 fusion.16
  285.4 3.6 %fusion.22 = f32[2,16,1024]{2,1,0:T(8,128)S(1)} fusion(bf16[4,2,33,4096]{3,0,2,1:T(4,128)(2,1)} %bitcast.74, bf16[4,2,33,1024]{3,0,2,1:T(4,128)(2,1)} %bitcast.78, bf16[1,2,16,4096]{3,2,1,0:T(8,128)(2,1)} %param.12), kind=kOutput, calls=%fused_computation.20 | convolution fusion | flops 43290752 | bytes 3096576 | tf_op jit(solution)/shard_map/nacr,nack->ark/dot_general | solution.py:91
  289.0 5.7 %all-reduce.3 = (bf16[2,16,4096]{2,1,0:T(8,128)(2,1)}, bf16[2,16,1024]{2,1,0:T(8,128)(2,1)}) all-reduce(f32[2,16,4096]{2,1,0:T(8,128)S(1)} %fusion.16, f32[2,16,1024]{2,1,0:T(8,128)S(1)} %fusion.22), channel_id=1, replica_groups=mesh['groups'=2,'adapter'=4,'segment'=2,'replica'=2] {'replica'}, use_global_device_ids=true, to_apply=%region_6.7 | all-reduce | flops 163840 | bytes 983040 | tf_op jit(solution)/shard_map/psum | solution.py:94
  294.6 17.0 %collective-permute-done = bf16[176,4096]{1,0:T(8,128)(2,1)S(1)} collective-permute-done((bf16[176,4096]{1,0:T(8,128)(2,1)}, bf16[176,4096]{1,0:T(8,128)(2,1)S(1)}, u32[]{:S(2)}, u32[]{:S(2)}) %collective-permute-start) | collective-permute-done | bytes 1441824 | tf_op jit(solution)/shard_map/ppermute | solution.py:11
  311.6 1.1 copy.48
  (18 shorter events, 0.1 us)
Async XLA Ops:
  7.2 54.6 %copy-start = (bf16[1,176,4096]{2,1,0:T(8,128)(2,1)S(1)}, bf16[1,176,4096]{2,1,0:T(8,128)(2,1)}, u32[]{:S(2)}) copy-start(bf16[1,176,4096]{2,1,0:T(8,128)(2,1)} %param.7) | copy-start | bytes 4325380
  7.2 3.2 copy-start.2
  7.2 263.3 %all-gather.3.cloned.1.call-start = ((), (), s32[]{:S(2)}) async-start(), calls=%async_computation.3 | async-start | bytes 10485760 | tf_op jit(solution)/shard_map/all_gather | solution.py:37
  10.4 41.2 %copy-start.5 = (bf16[1,2,16,1024]{3,2,1,0:T(8,128)(2,1)S(1)}, bf16[1,2,16,1024]{3,2,1,0:T(8,128)(2,1)}, u32[]{:S(2)}) copy-start(bf16[1,2,16,1024]{3,2,1,0:T(8,128)(2,1)} %param.13) | copy-start | bytes 196612
  11.9 40.2 %copy-start.4 = (bf16[1,2,16,4096]{3,2,1,0:T(8,128)(2,1)S(1)}, bf16[1,2,16,4096]{3,2,1,0:T(8,128)(2,1)}, u32[]{:S(2)}) copy-start(bf16[1,2,16,4096]{3,2,1,0:T(8,128)(2,1)} %param.12) | copy-start | bytes 786436
  50.8 0.8 copy-start.3
  57.2 122.2 %all-to-all-start.1 = ((bf16[4,66,4096]{2,1,0:T(8,128)(2,1)}), bf16[4,66,4096]{2,1,0:T(8,128)(2,1)}, u32[]{:S(2)}, u32[]{:S(2)}) async-start(bf16[4,66,4096]{2,1,0:T(8,128)(2,1)} %copy.20), calls=%async_computation.1 | async-start | bytes 4718592 | tf_op jit(solution)/shard_map/all_to_all | solution.py:78
  179.4 99.9 %all-to-all-start.2 = ((bf16[4,66,4096]{2,1,0:T(8,128)(2,1)}), bf16[4,66,4096]{2,1,0:T(8,128)(2,1)}, u32[]{:S(2)}, u32[]{:S(2)}) async-start(bf16[4,66,4096]{2,1,0:T(8,128)(2,1)} %reshape.69), calls=%async_computation.2 | async-start | bytes 4718592 | tf_op jit(solution)/shard_map/all_to_all | solution.py:59
  277.9 33.8 %collective-permute-start = (bf16[176,4096]{1,0:T(8,128)(2,1)}, bf16[176,4096]{1,0:T(8,128)(2,1)S(1)}, u32[]{:S(2)}, u32[]{:S(2)}) collective-permute-start(bf16[176,4096]{1,0:T(8,128)(2,1)} %fusion.13), channel_id=1, source_target_pairs={{0,2},{2,0},{1,3},{3,1},{4,6},{6,4},{5,7},{7,5},{8,10},{10,8},{9,1... | collective-permute-start | bytes 4325384 | tf_op jit(solution)/shard_map/ppermute | solution.py:11
  282.7 1.4 copy-start.1
Sparse Core Ops, SparseCore 0:
  9.6 260.8 all-gather.2
where the time goes:
time: 320 us
  waiting for transfers between devices  205 us (64%)
  blocking collectives  44 us (14%)
  local copies, waits for them, and re-layouts  29.3 us (9%)
  between operations  14.2 us (4%)
  matrix products  13.7 us (4%)
  starting transfers between devices  10.7 us (3%)
    all_to_all x1, waiting for transfers between devices, on_device(): lax.all_to_all(adapter_backward.reshape(holder_count, slots_per_holder *...  110 us
    all_gather x1, waiting for transfers between devices, on_device(): lax.all_gather(local_frozen, 'adapter', axis=0, tiled=True)  77.9 us
    all_to_all x1, blocking collectives, on_device(): lax.all_to_all(send_grad, 'adapter', split_axis=0, concat_axis=0, tiled=T...  38.3 us
    ppermute x1, waiting for transfers between devices, passed_along(): return lax.ppermute(x, axis, [(i, (i + by) % size) for i in range(size)])  17 us
    dot_general x1, matrix products, on_device(): jnp.einsum('tk,dk->td', grad_rows, lax.all_gather(local_frozen, 'adapter'...  7.4 us
  transfers between devices with their start and end apart: 4, of which 3 were waited for; matrix products, arithmetic and copies ran while one was open for 13% of the time, Pallas kernels for 0%

commit v1 on v0

v1 whole, which is shorter than its diff:
```python
import jax
import jax.numpy as jnp
from jax import lax
from jax.sharding import PartitionSpec as P

ADAPTER_SCALE = 2.0
COPIES = ("groups", "replica")
LINE = ("adapter", "groups", "replica")


def passed_along(x, axis, by):
    size = lax.axis_size(axis)
    return lax.ppermute(x, axis, [(i, (i + by) % size) for i in range(size)])


def my_piece(x, parts):
    rows = x.shape[0] // parts
    piece = lax.axis_index("groups") * lax.axis_size("replica") + lax.axis_index("replica")
    return lax.dynamic_slice_in_dim(x, piece * rows, rows, axis=0)


def on_device(
    saved_layer_input,
    value_output_gradient,
    token_adapter_index,
    adapter_slot_index,
    frozen_value_weight,
    adapter_down_weight,
    adapter_up_weight,
):
    inputs = saved_layer_input[0]
    grad_rows = value_output_gradient[0]
    row_ids = token_adapter_index[0, :, 0]
    width = inputs.shape[1]
    value_width = grad_rows.shape[1]
    adapters = adapter_slot_index.shape[0]
    holders = lax.axis_size("adapter")
    copies = lax.axis_size("groups") * lax.axis_size("replica")
    slots, rank = adapter_down_weight.shape[1:3]
    frozen = frozen_value_weight[0]
    shard = frozen.shape[0]
    chunks = max(1, shard // 256)
    step = shard // chunks

    both = jnp.concatenate(
        [
            adapter_down_weight[0].reshape(slots * rank, width),
            adapter_up_weight[0].reshape(slots * rank, value_width),
        ],
        axis=1,
    )
    both = lax.all_gather(my_piece(both, copies), LINE, axis=0, tiled=True)
    down, up = both[:, :width], both[:, width:]

    weights = [
        lax.all_gather(
            my_piece(frozen[c * step : (c + 1) * step], copies), LINE, axis=0, tiled=True
        )
        for c in range(chunks)
    ]

    slot_range = jnp.arange(adapters, dtype=jnp.int32)
    slot_row = jnp.sum(
        jnp.where(row_ids[:, None] == slot_range[None, :], adapter_slot_index[None, :], 0), axis=1
    )
    owner = jnp.arange(adapters * rank, dtype=jnp.int32) // rank
    keep = slot_row[:, None] == owner[None, :]

    proj_in = jnp.einsum("td,rd->tr", inputs, down, preferred_element_type=jnp.float32)
    proj_grad = jnp.einsum("tk,rk->tr", grad_rows, up, preferred_element_type=jnp.float32)
    in_sel = jnp.where(keep, proj_in, 0.0).astype(jnp.bfloat16)
    grad_sel = jnp.where(keep, proj_grad, 0.0).astype(jnp.bfloat16)
    part = jnp.concatenate(
        [
            jnp.einsum("tr,td->rd", grad_sel, inputs, preferred_element_type=jnp.float32),
            jnp.einsum("tr,tk->rk", in_sel, grad_rows, preferred_element_type=jnp.float32),
        ],
        axis=1,
    ).astype(jnp.bfloat16)

    half = part.shape[1] // 2
    core = lax.axis_index("replica")
    mine = lax.dynamic_slice_in_dim(part, core * half, half, axis=1)
    other = lax.dynamic_slice_in_dim(part, (1 - core) * half, half, axis=1)
    came = passed_along(other, "replica", 1)
    chip = mine.astype(jnp.float32) + came.astype(jnp.float32)

    rows = slots * rank
    here = lax.axis_index("adapter")
    total = lax.dynamic_slice_in_dim(chip, here * rows, rows, axis=0)
    chip_out = chip.astype(jnp.bfloat16)
    for by in range(1, holders):
        block = lax.dynamic_slice_in_dim(chip_out, ((here + by) % holders) * rows, rows, axis=0)
        total = total + passed_along(block, "adapter", by).astype(jnp.float32)
    total = (ADAPTER_SCALE * total).astype(jnp.bfloat16)
    partner = passed_along(total, "replica", 1)
    summed = jnp.concatenate(
        [jnp.where(core == 0, total, partner), jnp.where(core == 0, partner, total)], axis=1
    )
    down_grad = summed[:, :width].reshape(1, slots, rank, width)
    up_grad = summed[:, width:].reshape(1, slots, rank, value_width)

    down_blocks = down.reshape(adapters * rank, holders, chunks, step)
    passed = []
    for c in range(chunks):
        part = jnp.einsum(
            "tk,dk->td", grad_rows, weights[c], preferred_element_type=jnp.float32
        ).astype(jnp.bfloat16)
        lora = (
            ADAPTER_SCALE
            * jnp.einsum(
                "tr,rd->td",
                grad_sel,
                down_blocks[:, :, c].reshape(adapters * rank, holders * step),
                preferred_element_type=jnp.float32,
            )
        ).astype(jnp.bfloat16)
        sent = (part.astype(jnp.float32) + lora.astype(jnp.float32)).astype(jnp.bfloat16)
        passed.append(passed_along(sent, "segment", -1).reshape(-1, holders, step))
    passed = jnp.stack(passed, axis=2).reshape(1, -1, width)
    return passed, down_grad, up_grad


def solution(mesh):
    placed = (
        P("segment", ("groups", "adapter", "replica"), None),
        P("segment", ("groups", "adapter", "replica"), None),
        P("segment", ("groups", "adapter", "replica"), None),
        P("groups"),
        P("segment", "adapter", None),
        P("segment", "adapter", None, None),
        P("segment", "adapter", None, None),
    )
    return jax.shard_map(
        on_device,
        mesh=mesh,
        in_specs=placed,
        out_specs=(
            P("segment", ("groups", "adapter", "replica"), None),
            P(("groups", "segment"), "adapter", None, None),
            P(("groups", "segment"), "adapter", None, None),
        ),
        check_vma=False,
    )
```

time: 320 us -> 256 us (0.80)
  blocking collectives: 44 us -> 0 us
  waiting for transfers between devices: 205 us -> 186 us
  local copies, waits for them, and re-layouts: 29.3 us -> 19.1 us
  other arithmetic: 2.2 us -> 8.46 us
  matrix products: 13.7 us -> 17.6 us
    all_to_all x2 -> x0, waiting for transfers between devices: 110 us -> none  [the longest x1 110 us: on_device(): lax.all_to_all(adapter_backward.reshape(holder_count, slots_per_holder *...]
    all_gather x1 -> x5, waiting for transfers between devices: 77.9 us -> 165 us  [the longest x4 126 us: on_device(): lax.all_gather(my_piece(frozen[c * step:(c + 1) * step], copies), LINE, a...]
    all_to_all x1 -> x0, blocking collectives: 38.3 us -> none  [on_device(): lax.all_to_all(send_grad, 'adapter', split_axis=0, concat_axis=0, tiled=T...]
    all_to_all x2 -> x0, starting transfers between devices: 9.22 us -> none  [the longest x1 4.72 us: on_device(): lax.all_to_all(send_in, 'adapter', split_axis=0, concat_axis=0, tiled=True)]
    ppermute x1 -> x9, starting transfers between devices: 1.49 us -> 10 us  [passed_along(): return lax.ppermute(x, axis, [(i, (i + by) % size) for i in range(size)])]
    reshape x4 -> x1, local copies, waits for them, and re-layouts: 10 us -> 1.91 us  [on_device(): passed = jnp.stack(passed, axis=2).reshape(1, -1, width)]
    slice x1 -> x5, local copies, waits for them, and re-layouts: 0.21 us -> 8 us  [the longest x2 3.9 us: on_device(): down, up = (both[:, :width], both[:, width:])]
    psum x1 -> x0, blocking collectives: 5.68 us -> none  [on_device(): down_grad, up_grad = lax.psum((down_grad, up_grad), 'replica')]
  transfers between devices with their start and end apart: 4 -> 14, of which waited for: 3 -> 11; matrix products, arithmetic and copies ran while one was open for 13% -> 15% of each run, Pallas kernels for 0% -> 0%
where the time goes in v1:
time: 256 us
  waiting for transfers between devices  186 us (73%)
  local copies, waits for them, and re-layouts  19.1 us (7%)
  matrix products  17.6 us (7%)
  between operations  14 us (5%)
  starting transfers between devices  10.2 us (4%)
  other arithmetic  8.46 us (3%)
    all_gather x4, waiting for transfers between devices, on_device(): lax.all_gather(my_piece(frozen[c * step:(c + 1) * step], copies), LINE, a...  126 us
    all_gather x1, waiting for transfers between devices, on_device(): both = lax.all_gather(my_piece(both, copies), LINE, axis=0, tiled=True)  38.5 us
    ppermute x9, waiting for transfers between devices, passed_along(): return lax.ppermute(x, axis, [(i, (i + by) % size) for i in range(size)])  21 us
    ppermute x9, starting transfers between devices, passed_along(): return lax.ppermute(x, axis, [(i, (i + by) % size) for i in range(size)])  10 us
    dot_general x4, matrix products, on_device(): jnp.einsum('tk,dk->td', grad_rows, weights[c], preferred_element_type=jnp...  9.74 us
  transfers between devices with their start and end apart: 14, of which 11 were waited for; matrix products, arithmetic and copies ran while one was open for 15% of the time, Pallas kernels for 0%

profile of v1, /device:TPU:0, one launch (start us, length us, event | category | flops | bytes accessed | tf_op | source)
XLA Modules:
  0.0 255.6 jit_solution(16316380510552314799)
XLA Ops:
  7.2 1.6 fusion.86
  8.9 2.6 %fusion.94 = (bf16[1,256,1024]{2,1,0:T(8,128)(2,1)}, bf16[1,256,1024]{2,1,0:T(8,128)(2,1)S(1)}, bf16[1,256,1024]{2,1,0:T(8,128)(2,1)S(1)}, bf16[1,256,1024]{2,1,0:T(8,128)(2,1)S(1)}) fusion(bf16[1,1024,1024]{2,1,0:T(8,128)(2,1)} %param.11), kind=kLoop, calls=%fused_computation.93 | loop fusion | bytes 4194304 | tf_op jit(solution)/shard_map/slice | solution.py:57
  13.9 38.5 %all-gather.10.cloned.1.call-done = bf16[128,5120]{1,0:T(8,128)(2,1)} async-done(((bf16[8,5120]{1,0:T(8,128)(2,1)}), bf16[128,5120]{1,0:T(8,128)(2,1)}) %all-gather.10.cloned.1.call-update) | async-done | bytes 1310736 | tf_op jit(solution)/shard_map/all_gather | solution.py:52
  52.4 1.2 fusion.73
  54.1 2.1 convolution_convert_fusion.1
  56.2 1.1 fusion.76
  57.6 1.6 constant_dynamic-slice_fusion.6
  59.8 2.5 fusion.93
  63.6 3.3 %collective-permute-start.7 = (bf16[32,2560]{1,0:T(8,128)(2,1)}, bf16[32,2560]{1,0:T(8,128)(2,1)S(1)}, u32[]{:S(2)}, u32[]{:S(2)}) collective-permute-start(bf16[32,2560]{1,0:T(8,128)(2,1)} %get-tuple-element.14), channel_id=1, source_target_pairs={{0,12},{4,0},{8,4},{12,8},{1,13},{5,1},{9,5},{13,9},{2,14},{6,2},{... | collective-permute-start | bytes 491528 | tf_op jit(solution)/shard_map/ppermute | solution.py:13
  66.9 2.3 slice.53
  69.2 1.6 copy.17
  70.8 4.0 %collective-permute-done.5 = bf16[32,2560]{1,0:T(8,128)(2,1)S(1)} collective-permute-done((bf16[32,2560]{1,0:T(8,128)(2,1)}, bf16[32,2560]{1,0:T(8,128)(2,1)S(1)}, u32[]{:S(2)}, u32[]{:S(2)}) %collective-permute-start.5) | collective-permute-done | bytes 163872 | tf_op jit(solution)/shard_map/ppermute | solution.py:13
  74.8 1.4 collective-permute-done.7
  76.3 7.6 %collective-permute-done.6 = bf16[32,2560]{1,0:T(8,128)(2,1)S(1)} collective-permute-done((bf16[32,2560]{1,0:T(8,128)(2,1)}, bf16[32,2560]{1,0:T(8,128)(2,1)S(1)}, u32[]{:S(2)}, u32[]{:S(2)}) %collective-permute-start.6) | collective-permute-done | bytes 163872 | tf_op jit(solution)/shard_map/ppermute | solution.py:13
  87.1 14.4 %all-gather.18.cloned.1.call-done = bf16[1,1024,1024]{2,1,0:T(8,128)(2,1)} async-done(((bf16[1,64,1024]{2,1,0:T(8,128)(2,1)}), bf16[1,1024,1024]{2,1,0:T(8,128)(2,1)}) %all-gather.18.cloned.1.call-update) | async-done | bytes 2097168 | tf_op jit(solution)/shard_map/all_gather | solution.py:56
  101.5 2.4 fusion.60
  105.0 1.5 collective-permute-start.3
  106.5 37.5 %all-gather.16.cloned.1.call-done = bf16[1,1024,1024]{2,1,0:T(8,128)(2,1)} async-done(((bf16[1,64,1024]{2,1,0:T(8,128)(2,1)}), bf16[1,1024,1024]{2,1,0:T(8,128)(2,1)}) %all-gather.16.cloned.1.call-update) | async-done | bytes 2097168 | tf_op jit(solution)/shard_map/all_gather | solution.py:56
  143.9 2.4 fusion.51
  147.4 1.5 collective-permute-start.2
  148.9 37.3 %all-gather.14.cloned.1.call-done = bf16[1,1024,1024]{2,1,0:T(8,128)(2,1)} async-done(((bf16[1,64,1024]{2,1,0:T(8,128)(2,1)}), bf16[1,1024,1024]{2,1,0:T(8,128)(2,1)}) %all-gather.14.cloned.1.call-update) | async-done | bytes 2097168 | tf_op jit(solution)/shard_map/all_gather | solution.py:56
  186.1 2.4 fusion.42
  189.6 1.5 collective-permute-start.1
  191.1 37.3 %all-gather.12.cloned.1.call-done = bf16[1,1024,1024]{2,1,0:T(8,128)(2,1)} async-done(((bf16[1,64,1024]{2,1,0:T(8,128)(2,1)}), bf16[1,1024,1024]{2,1,0:T(8,128)(2,1)}) %all-gather.12.cloned.1.call-update) | async-done | bytes 2097168 | tf_op jit(solution)/shard_map/all_gather | solution.py:56
  228.4 2.4 fusion.33
  231.8 1.5 collective-permute-start
  234.3 1.3 stack_reshape.14
  235.8 6.9 %collective-permute-done = bf16[176,1024]{1,0:T(8,128)(2,1)} collective-permute-done((bf16[176,1024]{1,0:T(8,128)(2,1)}, bf16[176,1024]{1,0:T(8,128)(2,1)}, u32[]{:S(2)}, u32[]{:S(2)}) %collective-permute-start) | collective-permute-done | bytes 360480 | tf_op jit(solution)/shard_map/ppermute | solution.py:13
  242.7 1.3 stack_reshape.12
  243.9 1.3 pad_maximum_fusion
  245.3 1.9 copy.18
  247.2 1.9 reshape.43
  (49 shorter events, 13.5 us)
Async XLA Ops:
  7.2 46.5 %copy-start = (bf16[1,176,4096]{2,1,0:T(8,128)(2,1)S(1)}, bf16[1,176,4096]{2,1,0:T(8,128)(2,1)}, u32[]{:S(2)}) copy-start(bf16[1,176,4096]{2,1,0:T(8,128)(2,1)} %param.7) | copy-start | bytes 4325380
  7.2 45.2 %all-gather.10.cloned.1.call-start = ((), (), s32[]{:S(2)}) async-start(), calls=%async_computation | async-start | bytes 1392640 | tf_op jit(solution)/shard_map/all_gather | solution.py:52
  8.8 92.7 %all-gather.18.cloned.1.call-start = ((), (), s32[]{:S(2)}) async-start(), calls=%async_computation.4 | async-start | bytes 2228224 | tf_op jit(solution)/shard_map/all_gather | solution.py:56
  8.9 4.9 %copy-start.4 = (s32[1,176,1]{1,2,0:T(1,128)S(1)}, s32[1,176,1]{1,2,0:T(1,128)}, u32[]{:S(2)}) copy-start(s32[1,176,1]{1,2,0:T(1,128)} %param.9) | copy-start | bytes 2116
  8.9 4.9 %copy-start.5 = (s32[8]{0:T(128)S(1)}, s32[8]{0:T(128)}, u32[]{:S(2)}) copy-start(s32[8]{0:T(128)} %param.10) | copy-start | bytes 100
  8.9 43.5 %copy-start.1 = (bf16[1,176,1024]{2,1,0:T(8,128)(2,1)S(1)}, bf16[1,176,1024]{2,1,0:T(8,128)(2,1)}, u32[]{:S(2)}) copy-start(bf16[1,176,1024]{2,1,0:T(8,128)(2,1)} %param.8) | copy-start | bytes 1081348
  12.2 131.7 %all-gather.16.cloned.1.call-start = ((), (), s32[]{:S(2)}) async-start(), calls=%async_computation.3 | async-start | bytes 2228224 | tf_op jit(solution)/shard_map/all_gather | solution.py:56
  12.9 173.2 %all-gather.14.cloned.1.call-start = ((), (), s32[]{:S(2)}) async-start(), calls=%async_computation.2 | async-start | bytes 2228224 | tf_op jit(solution)/shard_map/all_gather | solution.py:56
  13.7 214.7 %all-gather.12.cloned.1.call-start = ((), (), s32[]{:S(2)}) async-start(), calls=%async_computation.1 | async-start | bytes 2228224 | tf_op jit(solution)/shard_map/all_gather | solution.py:56
  57.4 2.4 collective-permute-start.4
  63.1 11.8 %collective-permute-start.5 = (bf16[32,2560]{1,0:T(8,128)(2,1)}, bf16[32,2560]{1,0:T(8,128)(2,1)S(1)}, u32[]{:S(2)}, u32[]{:S(2)}) collective-permute-start(bf16[32,2560]{1,0:T(8,128)(2,1)} %get-tuple-element.13), channel_id=1, source_target_pairs={{0,4},{4,8},{8,12},{12,0},{1,5},{5,9},{9,13},{13,1},{2,6},{6,10},{... | collective-permute-start | bytes 491528 | tf_op jit(solution)/shard_map/ppermute | solution.py:13
  63.6 12.6 %collective-permute-start.7 = (bf16[32,2560]{1,0:T(8,128)(2,1)}, bf16[32,2560]{1,0:T(8,128)(2,1)S(1)}, u32[]{:S(2)}, u32[]{:S(2)}) collective-permute-start(bf16[32,2560]{1,0:T(8,128)(2,1)} %get-tuple-element.14), channel_id=1, source_target_pairs={{0,12},{4,0},{8,4},{12,8},{1,13},{5,1},{9,5},{13,9},{2,14},{6,2},{... | collective-permute-start | bytes 491528 | tf_op jit(solution)/shard_map/ppermute | solution.py:13
  66.9 17.0 %collective-permute-start.6 = (bf16[32,2560]{1,0:T(8,128)(2,1)}, bf16[32,2560]{1,0:T(8,128)(2,1)S(1)}, u32[]{:S(2)}, u32[]{:S(2)}) collective-permute-start(bf16[32,2560]{1,0:T(8,128)(2,1)} %get-tuple-element.15), channel_id=1, source_target_pairs={{0,8},{4,12},{8,0},{12,4},{1,9},{5,13},{9,1},{13,5},{2,10},{6,14},... | collective-permute-start | bytes 491528 | tf_op jit(solution)/shard_map/ppermute | solution.py:13
  85.0 1.5 collective-permute-start.8
  87.1 16.9 %copy-start.3 = (bf16[128,4,1,256]{0,3,2,1:T(8,128)(2,1)S(1)}, bf16[128,4,1,256]{0,3,2,1:T(8,128)(2,1)}, u32[]{:S(2)}) copy-start(bf16[128,4,1,256]{0,3,2,1:T(8,128)(2,1)} %get-tuple-element.10) | copy-start | bytes 786436
  105.0 41.4 %copy-start.2 = (bf16[128,4,1,256]{0,3,2,1:T(8,128)(2,1)S(1)}, bf16[128,4,1,256]{0,3,2,1:T(8,128)(2,1)}, u32[]{:S(2)}) copy-start(bf16[128,4,1,256]{0,3,2,1:T(8,128)(2,1)} %get-tuple-element.11) | copy-start | bytes 786436
  105.0 129.0 %collective-permute-start.3 = (bf16[176,1024]{1,0:T(8,128)(2,1)}, bf16[176,1024]{1,0:T(8,128)(2,1)S(1)}, u32[]{:S(2)}, u32[]{:S(2)}) collective-permute-start(bf16[176,1024]{1,0:T(8,128)(2,1)} %fusion.26), channel_id=1, source_target_pairs={{0,2},{2,0},{1,3},{3,1},{4,6},{6,4},{5,7},{7,5},{8,10},{10,8},{9,1... | collective-permute-start | bytes 1081352 | tf_op jit(solution)/shard_map/ppermute | solution.py:13
  147.4 86.9 %collective-permute-start.2 = (bf16[176,1024]{1,0:T(8,128)(2,1)}, bf16[176,1024]{1,0:T(8,128)(2,1)}, u32[]{:S(2)}, u32[]{:S(2)}) collective-permute-start(bf16[176,1024]{1,0:T(8,128)(2,1)} %fusion.22), channel_id=1, source_target_pairs={{0,2},{2,0},{1,3},{3,1},{4,6},{6,4},{5,7},{7,5},{8,10},{10,8},{9,1... | collective-permute-start | bytes 1081352 | tf_op jit(solution)/shard_map/ppermute | solution.py:13
  189.6 45.9 %collective-permute-start.1 = (bf16[176,1024]{1,0:T(8,128)(2,1)}, bf16[176,1024]{1,0:T(8,128)(2,1)S(1)}, u32[]{:S(2)}, u32[]{:S(2)}) collective-permute-start(bf16[176,1024]{1,0:T(8,128)(2,1)} %fusion.18), channel_id=1, source_target_pairs={{0,2},{2,0},{1,3},{3,1},{4,6},{6,4},{5,7},{7,5},{8,10},{10,8},{9,1... | collective-permute-start | bytes 1081352 | tf_op jit(solution)/shard_map/ppermute | solution.py:13
  231.8 10.9 %collective-permute-start = (bf16[176,1024]{1,0:T(8,128)(2,1)}, bf16[176,1024]{1,0:T(8,128)(2,1)}, u32[]{:S(2)}, u32[]{:S(2)}) collective-permute-start(bf16[176,1024]{1,0:T(8,128)(2,1)} %fusion.14), channel_id=1, source_target_pairs={{0,2},{2,0},{1,3},{3,1},{4,6},{6,4},{5,7},{7,5},{8,10},{10,8},{9,1... | collective-permute-start | bytes 1081352 | tf_op jit(solution)/shard_map/ppermute | solution.py:13
Sparse Core Ops, SparseCore 0:
  10.9 41.4 all-gather.9
  54.6 46.9 all-gather.17
  103.7 40.1 all-gather.15
  145.9 40.1 all-gather.13
  188.2 40.1 all-gather.11

commit v2 on v1

v2 whole, which is shorter than its diff:
```python
import itertools
import jax
import jax.numpy as jnp
from jax import lax
from jax.sharding import PartitionSpec as P

ADAPTER_SCALE = 2.0
AXES = ("groups", "adapter", "segment", "replica")
LANES = 128
F32 = jnp.float32
BF16 = jnp.bfloat16


def moved(x, to):
    sizes = [lax.axis_size(a) for a in AXES]
    number = {at: i for i, at in enumerate(itertools.product(*map(range, sizes)))}
    pairs = []
    for at, i in number.items():
        target = to(*at)
        if target is not None:
            pairs.append((i, number[tuple(t % s for t, s in zip(target, sizes))]))
    return lax.ppermute(x, AXES, pairs)


def on_device(
    saved_layer_input,
    value_output_gradient,
    token_adapter_index,
    adapter_slot_index,
    frozen_value_weight,
    adapter_down_weight,
    adapter_up_weight,
):
    inputs = saved_layer_input[0]
    grad_rows = value_output_gradient[0]
    row_ids = token_adapter_index[0, :, 0]
    tokens, width = inputs.shape
    value_width = grad_rows.shape[1]
    adapters = adapter_slot_index.shape[0]
    groups, holders, replicas = (lax.axis_size(a) for a in ("groups", "adapter", "replica"))
    group, here, core = (lax.axis_index(a) for a in ("groups", "adapter", "replica"))
    slots, rank = adapter_down_weight.shape[1:3]
    own_slots = slots // replicas
    frozen = frozen_value_weight[0]
    shard = frozen.shape[0]
    copies = groups * replicas
    piece = shard // copies
    peers = [(dg, dr) for dg in range(groups) for dr in range(replicas)]

    both = jnp.concatenate([adapter_down_weight[0], adapter_up_weight[0]], axis=2)
    rows = own_slots * rank
    own = lax.dynamic_slice_in_dim(both, core * own_slots, own_slots, axis=0).reshape(rows, -1)
    held = [own]
    for k in range(1, holders):
        held.append(moved(own, lambda g, z, s, r: (g, z + k, s, r)))
    held = jnp.concatenate(held, axis=0)
    maps = [held]
    for dr in range(1, replicas):
        maps.append(moved(held, lambda g, z, s, r: (g, z, s, r + dr)))
    maps = jnp.concatenate(maps, axis=0)
    down, up = maps[:, :width], maps[:, width:]
    row_slot = jnp.concatenate(
        [
            ((here - k) % holders) * slots
            + ((core - dr) % replicas) * own_slots
            + jnp.arange(rows, dtype=jnp.int32) // rank
            for dr in range(replicas)
            for k in range(holders)
        ]
    )

    slot_range = jnp.arange(adapters, dtype=jnp.int32)
    slot_row = jnp.sum(
        jnp.where(row_ids[:, None] == slot_range[None, :], adapter_slot_index[None, :], 0), axis=1
    )
    tagged = jnp.concatenate(
        [grad_rows, jnp.broadcast_to(slot_row[:, None], (tokens, LANES)).astype(BF16)], axis=1
    )
    by_peer = {(0, 0): tagged}
    for dg in range(groups):
        if dg:
            by_peer[dg, 0] = moved(tagged, lambda g, z, s, r: (g - dg, z, s, r))
        for dr in range(1, replicas):
            by_peer[dg, dr] = moved(by_peer[dg, 0], lambda g, z, s, r: (g, z, s, r - dr))
    tagged = jnp.concatenate([by_peer[p] for p in peers], axis=0)
    grads_all = tagged[:, :value_width]
    slots_all = tagged[:, value_width].astype(jnp.int32)

    quarter = group * replicas + core
    mine = lax.dynamic_slice_in_dim(frozen, quarter * piece, piece, axis=0)
    ups, downs = [mine], [mine]
    for k in range(1, holders):
        ups.append(
            moved(
                ups[-1],
                lambda g, z, s, r: (g, z + 1, s, r) if k - 1 <= z < holders - 1 else None,
            )
        )
        downs.append(
            moved(
                downs[-1],
                lambda g, z, s, r: (g, z - 1, s, r) if 0 < z <= holders - k else None,
            )
        )

    keep = slots_all[:, None] == row_slot[None, :]
    proj_grad = jnp.einsum("tk,rk->tr", grads_all, up, preferred_element_type=F32)
    sel_all = jnp.where(keep, proj_grad, 0.0).astype(BF16)
    proj_in = jnp.einsum("td,rd->tr", inputs, down, preferred_element_type=F32)
    in_sel = jnp.where(keep[:tokens], proj_in, 0.0).astype(BF16)
    grad_sel = sel_all[:tokens]
    part = jnp.concatenate(
        [
            jnp.einsum("tr,td->rd", grad_sel, inputs, preferred_element_type=F32),
            jnp.einsum("tr,tk->rk", in_sel, grad_rows, preferred_element_type=F32),
        ],
        axis=1,
    ).astype(BF16)

    part = part.reshape(replicas, holders, rows, width + value_width)
    chip = part[0].astype(F32)
    for dr in range(1, replicas):
        chip = chip + moved(part[dr], lambda g, z, s, r: (g, z, s, r - dr)).astype(F32)
    chip_out = chip.astype(BF16)
    total = chip[0]
    for k in range(1, holders):
        total = total + moved(chip_out[k], lambda g, z, s, r: (g, z - k, s, r)).astype(F32)
    total = (ADAPTER_SCALE * total).astype(BF16)
    summed = jnp.zeros((slots, rank, width + value_width), BF16)
    for dr in range(replicas):
        got = moved(total, lambda g, z, s, r: (g, z, s, r + dr)) if dr else total
        summed = lax.dynamic_update_slice_in_dim(
            summed,
            got.reshape(own_slots, rank, -1),
            ((core - dr) % replicas) * own_slots,
            axis=0,
        )
    down_grad = summed[None, :, :, :width]
    up_grad = summed[None, :, :, width:]

    batches = [([(mine, here, None)], lambda z: True)]
    for k in range(1, holders):
        has = lambda z, k=k: z >= k or z <= holders - 1 - k
        from_below = here >= k
        from_above = here <= holders - 1 - k
        if 2 * k <= holders - 1:
            blocks = [(ups[k], here - k, from_below), (downs[k], here + k, from_above)]
        else:
            blocks = [
                (
                    jnp.where(from_below, ups[k], downs[k]),
                    jnp.where(from_below, here - k, here + k),
                    from_below | from_above,
                )
            ]
        if k == 1:
            batches[0][0].extend(blocks)
        else:
            batches.append((blocks, has))

    passed = jnp.zeros((tokens, width), BF16)
    for blocks, has in batches:
        weight = jnp.concatenate([b for b, _, _ in blocks], axis=0)
        columns = jnp.concatenate(
            [
                lax.dynamic_slice_in_dim(
                    down, jnp.clip(at, 0, holders - 1) * shard + quarter * piece, piece, axis=1
                )
                for _, at, _ in blocks
            ],
            axis=1,
        )
        base = jnp.einsum("tk,dk->td", grads_all, weight, preferred_element_type=F32).astype(BF16)
        lora = (
            ADAPTER_SCALE * jnp.einsum("tr,rd->td", sel_all, columns, preferred_element_type=F32)
        ).astype(BF16)
        out = (base.astype(F32) + lora.astype(F32)).astype(BF16)
        for i, (dg, dr) in enumerate(peers):
            got = moved(
                out[i * tokens : (i + 1) * tokens],
                lambda g, z, s, r: (g + dg, z, s - 1, r + dr) if has(z) else None,
            )
            source = ((group - dg) % groups) * replicas + (core - dr) % replicas
            for j, (_, at, valid) in enumerate(blocks):
                place = jnp.clip(at, 0, holders - 1) * shard + source * piece
                block = got[:, j * piece : (j + 1) * piece]
                if valid is not None:
                    old = lax.dynamic_slice_in_dim(passed, place, piece, axis=1)
                    block = jnp.where(valid, block, old)
                passed = lax.dynamic_update_slice_in_dim(passed, block, place, axis=1)
    return passed[None], down_grad, up_grad


def solution(mesh):
    placed = (
        P("segment", ("groups", "adapter", "replica"), None),
        P("segment", ("groups", "adapter", "replica"), None),
        P("segment", ("groups", "adapter", "replica"), None),
        P("groups"),
        P("segment", "adapter", None),
        P("segment", "adapter", None, None),
        P("segment", "adapter", None, None),
    )
    return jax.shard_map(
        on_device,
        mesh=mesh,
        in_specs=placed,
        out_specs=(
            P("segment", ("groups", "adapter", "replica"), None),
            P(("groups", "segment"), "adapter", None, None),
            P(("groups", "segment"), "adapter", None, None),
        ),
        check_vma=False,
    )
```

time: 256 us -> 125 us (0.49)
  waiting for transfers between devices: 186 us -> 35.4 us
  starting transfers between devices: 10.2 us -> 57.8 us
  between operations: 14 us -> 1.44 us
  local copies, waits for them, and re-layouts: 19.1 us -> 10.3 us
  matrix products: 17.6 us -> 12.3 us
    all_gather x5 -> x0, waiting for transfers between devices: 165 us -> none  [the longest x4 126 us: on_device(): lax.all_gather(my_piece(frozen[c * step:(c + 1) * step], copies), LINE, a...]
    ppermute x9 -> x30, starting transfers between devices: 10 us -> 57.8 us  [moved(): return lax.ppermute(x, AXES, pairs)]
    ppermute x9 -> x30, waiting for transfers between devices: 21 us -> 35.4 us  [moved(): return lax.ppermute(x, AXES, pairs)]
    slice x5 -> x4, local copies, waits for them, and re-layouts: 8 us -> 1.29 us  [the longest x1 1.16 us: on_device(): down, up = (maps[:, :width], maps[:, width:])]
    unnamed x12 -> x22, local copies, waits for them, and re-layouts: 0.04 us -> 5.99 us
    dot_general x11 -> x9, matrix products: 17.6 us -> 12.3 us  [the longest x3 4.74 us: on_device(): jnp.einsum('tk,dk->td', grads_all, weight, preferred_element_type=F32)]
    another operation x5 -> x0, local copies, waits for them, and re-layouts: 4.87 us -> none  [on_device(): passed = jnp.stack(passed, axis=2).reshape(1, -1, width)]
    convert_element_type x2 -> x1, other arithmetic: 3.56 us -> 0.01 us  [on_device(): jnp.broadcast_to(slot_row[:, None], (tokens, LANES)).astype(BF16)]
  transfers between devices with their start and end apart: 14 -> 30, of which waited for: 11 -> 13; matrix products, arithmetic and copies ran while one was open for 15% -> 19% of each run, Pallas kernels for 0% -> 0%
where the time goes in v2:
time: 125 us; the launch traced here: 124 us
  starting transfers between devices  57.8 us (46%)
  waiting for transfers between devices  35.4 us (28%)
  matrix products  12.3 us (10%)
  local copies, waits for them, and re-layouts  10.3 us (8%)
  other arithmetic  6.84 us (5%)
  between operations  1.44 us (1%)
    ppermute x30, starting transfers between devices, moved(): return lax.ppermute(x, AXES, pairs)  57.8 us
    ppermute x30, waiting for transfers between devices, moved(): return lax.ppermute(x, AXES, pairs)  35.4 us
    unnamed x22, local copies, waits for them, and re-layouts  5.99 us
    dot_general x3, matrix products, on_device(): jnp.einsum('tk,dk->td', grads_all, weight, preferred_element_type=F32)  4.74 us
    dot_general x1, matrix products, on_device(): jnp.einsum('tr,tk->rk', in_sel, grad_rows, preferred_element_type=F32)  2.58 us
    dot_general x3, matrix products, on_device(): jnp.einsum('tr,rd->td', sel_all, columns, preferred_element_type=F32)  2.57 us
  transfers between devices with their start and end apart: 30, of which 13 were waited for; matrix products, arithmetic and copies ran while one was open for 19% of the time, Pallas kernels for 0%

profile of v2, /device:TPU:0, one launch (start us, length us, event | category | flops | bytes accessed | tf_op | source)
XLA Modules:
  0.0 124.0 jit_solution(17704598408046195607)
XLA Ops:
  1.7 1.8 %pad_maximum_fusion.3 = bf16[176,1152]{1,0:T(8,128)(2,1)} fusion(bf16[176,128]{1,0:T(8,128)(2,1)S(1)} %broadcast_in_dim.50, bf16[176,1024]{1,0:T(8,128)(2,1)} %bitcast.69), kind=kLoop, calls=%fused_computation.49 | loop fusion | flops 811008 | bytes 811008 | tf_op jit(solution)/shard_map/concatenate | solution.py:76
  3.4 3.0 %collective-permute-start.1 = (bf16[176,1152]{1,0:T(8,128)(2,1)}, bf16[176,1152]{1,0:T(8,128)(2,1)S(1)}, u32[]{:S(2)}, u32[]{:S(2)}) collective-permute-start(bf16[176,1152]{1,0:T(8,128)(2,1)} %pad_maximum_fusion.3), channel_id=1, source_target_pairs={{0,16},{1,17},{2,18},{3,19},{4,20},{5,21},{6,22},{7,23},{8,24},{9,... | collective-permute-start | bytes 1216520 | tf_op jit(solution)/shard_map/ppermute | solution.py:22
  6.4 1.7 %constant_dynamic-update-slice_fusion.4 = (bf16[128,5120]{1,0:T(8,128)(2,1)}, bf16[16,5120]{1,0:T(8,128)(2,1)}) fusion(s32[]{:T(128)S(6)} %select_n.347, bf16[2,16,1024]{2,1,0:T(8,128)(2,1)} %bitcast.75, bf16[2,16,4096]{2,1,0:T(8,128)(2,1)} %bitcast.74), kind=kLoop, calls=%fused_computation.112 | loop fusion | flops 327679 | bytes 655364
  8.1 1.6 %collective-permute-start.5 = (bf16[16,5120]{1,0:T(8,128)(2,1)}, bf16[16,5120]{1,0:T(8,128)(2,1)}, u32[]{:S(2)}, u32[]{:S(2)}) collective-permute-start(bf16[16,5120]{1,0:T(8,128)(2,1)} %get-tuple-element.6), channel_id=1, source_target_pairs={{0,4},{1,5},{2,6},{3,7},{4,8},{5,9},{6,10},{7,11},{8,12},{9,13},{1... | collective-permute-start | bytes 491528 | tf_op jit(solution)/shard_map/ppermute | solution.py:22
  9.7 2.6 %collective-permute-start.6 = (bf16[16,5120]{1,0:T(8,128)(2,1)}, bf16[16,5120]{1,0:T(8,128)(2,1)}, u32[]{:S(2)}, u32[]{:S(2)}) collective-permute-start(bf16[16,5120]{1,0:T(8,128)(2,1)} %get-tuple-element.6), channel_id=1, source_target_pairs={{0,8},{1,9},{2,10},{3,11},{4,12},{5,13},{6,14},{7,15},{8,0},{9,1},... | collective-permute-start | bytes 491528 | tf_op jit(solution)/shard_map/ppermute | solution.py:22
  14.0 3.3 %collective-permute-done.5 = bf16[16,5120]{1,0:T(8,128)(2,1)} collective-permute-done((bf16[16,5120]{1,0:T(8,128)(2,1)}, bf16[16,5120]{1,0:T(8,128)(2,1)}, u32[]{:S(2)}, u32[]{:S(2)}) %collective-permute-start.5) | collective-permute-done | bytes 163872 | tf_op jit(solution)/shard_map/ppermute | solution.py:22
  17.3 8.2 %collective-permute-start.3 = (bf16[256,1024]{1,0:T(8,128)(2,1)S(1)}, bf16[256,1024]{1,0:T(8,128)(2,1)}, u32[]{:S(2)}, u32[]{:S(2)}) collective-permute-start(bf16[256,1024]{1,0:T(8,128)(2,1)S(1)} %dynamic-slice_bitcast_fusion), channel_id=1, source_target_pairs={{0,4},{1,5},{2,6},{3,7},{4,8},{5,9},{6,10},{7,11},{8,12},{9,13},{1... | collective-permute-start | bytes 1572872 | tf_op jit(solution)/shard_map/ppermute | solution.py:22
  28.0 1.6 %constant_dynamic-update-slice_fusion.3 = bf16[128,5120]{1,0:T(8,128)(2,1)} fusion(bf16[128,5120]{1,0:T(8,128)(2,1)} %get-tuple-element.5, bf16[16,5120]{1,0:T(8,128)(2,1)} %collective-permute-done.5), kind=kLoop, calls=%fused_computation.111 | loop fusion | bytes 327680
  29.5 1.6 %constant_dynamic-update-slice_fusion.2 = bf16[128,5120]{1,0:T(8,128)(2,1)} fusion(bf16[128,5120]{1,0:T(8,128)(2,1)} %constant_dynamic-update-slice_fusion.3, bf16[16,5120]{1,0:T(8,128)(2,1)} %collective-permute-done.6), kind=kLoop, calls=%fused_computation.110 | loop fusion | bytes 327680
  33.8 6.3 %collective-permute-done.4 = bf16[256,1024]{1,0:T(8,128)(2,1)} collective-permute-done((bf16[256,1024]{1,0:T(8,128)(2,1)S(1)}, bf16[256,1024]{1,0:T(8,128)(2,1)}, u32[]{:S(2)}, u32[]{:S(2)}) %collective-permute-start.4) | collective-permute-done | bytes 524320 | tf_op jit(solution)/shard_map/ppermute | solution.py:22
  41.9 1.7 %copy-done.2 = bf16[128,5120]{1,0:T(8,128)(2,1)S(1)} copy-done((bf16[128,5120]{1,0:T(8,128)(2,1)S(1)}, bf16[128,5120]{1,0:T(8,128)(2,1)}, u32[]{:S(2)}) %copy-start.2) | copy-done | bytes 1310744
  45.6 2.6 %convolution_convert_fusion.3 = bf16[128,1024]{1,0:T(8,128)(2,1)S(1)} fusion(bf16[1,176,4096]{2,1,0:T(8,128)(2,1)} %param.7, pred[704,128]{1,0:T(8,128)(4,1)S(1)} %broadcast_compare_fusion, bf16[1,176,1024]{2,1,0:T(8,128)(2,1)S(1)} %copy-done.1, bf16[128,5120]{1,0:T(8,128)(2,1)} %copy-done.3), kind=kOutput, calls=%fused_computation.31 | convolution fusion | flops 230862848 | bytes 3135488 | tf_op jit(solution)/shard_map/tr,tk->rk/dot_general | solution.py:115
  48.2 1.8 %convolution_convert_fusion = bf16[128,4096]{1,0:T(8,128)(2,1)S(1)} fusion(bf16[1,176,4096]{2,1,0:T(8,128)(2,1)} %param.7, bf16[704,128]{1,0:T(8,128)(2,1)S(1)} %fusion.24), kind=kOutput, calls=%fused_computation | convolution fusion | flops 185073664 | bytes 2535424 | tf_op jit(solution)/shard_map/tr,td->rd/dot_general | solution.py:114
  51.8 2.5 %add_convert_fusion = bf16[704,768]{1,0:T(8,128)(2,1)S(1)} fusion(bf16[704,768]{1,0:T(8,128)(2,1)S(1)} %multiply_convert_fusion, bf16[256,1024]{1,0:T(8,128)(2,1)} %collective-permute-done.4, bf16[256,1024]{1,0:T(8,128)(2,1)} %collective-permute-done.3, bf16[256,1024]{1,0:T(8,128)(2,1)S(1)} %copy-done.8, bf16[704,1152]{1,0:T(8,128)(2,1)S(1)} %copy-done.5), kind=kOutput, calls=%fused_computation.1 | convolution fusion | flops 1114718208 | bytes 5177344 | tf_op jit(solution)/shard_map/tk,dk->td/dot_general | solution.py:173
  54.4 1.6 %collective-permute-start.9 = (bf16[176,768]{1,0:T(8,128)(2,1)S(1)}, bf16[176,768]{1,0:T(8,128)(2,1)S(1)}, u32[]{:S(2)}, u32[]{:S(2)}) collective-permute-start(bf16[176,768]{1,0:T(8,128)(2,1)S(1)} %get-tuple-element.14), channel_id=1, source_target_pairs={{0,2},{1,3},{2,0},{3,1},{4,6},{5,7},{6,4},{7,5},{8,10},{9,11},{10,... | collective-permute-start | bytes 811016 | tf_op jit(solution)/shard_map/ppermute | solution.py:22
  61.1 1.6 %fusion.22 = bf16[704,256]{1,0:T(8,128)(2,1)S(1)} fusion(f32[704,256]{1,0:T(8,128)S(1)} %fusion.15, bf16[704,1152]{1,0:T(8,128)(2,1)S(1)} %copy-done.5, bf16[256,1024]{1,0:T(8,128)(2,1)} %collective-permute-done.13, bf16[256,1024]{1,0:T(8,128)(2,1)} %collective-permute-done.14, pred[]{:T(512)S(6)} %ge.10), kind=kOutput, calls=%fused_computation.29 | convolution fusion | flops 370081792 | bytes 3571713 | tf_op jit(solution)/shard_map/tk,dk->td/dot_general | solution.py:173
  65.5 3.1 %collective-permute-done.10 = bf16[176,768]{1,0:T(8,128)(2,1)S(1)} collective-permute-done((bf16[176,768]{1,0:T(8,128)(2,1)S(1)}, bf16[176,768]{1,0:T(8,128)(2,1)S(1)}, u32[]{:S(2)}, u32[]{:S(2)}) %collective-permute-start.10) | collective-permute-done | bytes 270368 | tf_op jit(solution)/shard_map/ppermute | solution.py:22
  68.5 2.2 %collective-permute-start.16 = (bf16[176,256]{1,0:T(8,128)(2,1)S(1)}, bf16[176,256]{1,0:T(8,128)(2,1)S(1)}, u32[]{:S(2)}, u32[]{:S(2)}) collective-permute-start(bf16[176,256]{1,0:T(8,128)(2,1)S(1)} %get-tuple-element.27), channel_id=1, source_target_pairs={{0,3},{1,2},{2,1},{3,0},{4,7},{5,6},{6,5},{7,4},{8,11},{9,10},{10,... | collective-permute-start | bytes 270344 | tf_op jit(solution)/shard_map/ppermute | solution.py:22
  70.8 4.4 %collective-permute-done.11 = bf16[176,768]{1,0:T(8,128)(2,1)S(1)} collective-permute-done((bf16[176,768]{1,0:T(8,128)(2,1)S(1)}, bf16[176,768]{1,0:T(8,128)(2,1)S(1)}, u32[]{:S(2)}, u32[]{:S(2)}) %collective-permute-start.11) | collective-permute-done | bytes 270368 | tf_op jit(solution)/shard_map/ppermute | solution.py:22
  75.3 2.4 %collective-permute-start.17 = (bf16[176,256]{1,0:T(8,128)(2,1)S(1)}, bf16[176,256]{1,0:T(8,128)(2,1)S(1)}, u32[]{:S(2)}, u32[]{:S(2)}) collective-permute-start(bf16[176,256]{1,0:T(8,128)(2,1)S(1)} %get-tuple-element.26), channel_id=1, source_target_pairs={{0,18},{1,19},{2,16},{3,17},{4,22},{5,23},{6,20},{7,21},{8,26},{9,... | collective-permute-start | bytes 270344 | tf_op jit(solution)/shard_map/ppermute | solution.py:22
  77.8 2.3 %collective-permute-done.12 = bf16[176,768]{1,0:T(8,128)(2,1)S(1)} collective-permute-done((bf16[176,768]{1,0:T(8,128)(2,1)S(1)}, bf16[176,768]{1,0:T(8,128)(2,1)S(1)}, u32[]{:S(2)}, u32[]{:S(2)}) %collective-permute-start.12) | collective-permute-done | bytes 270368 | tf_op jit(solution)/shard_map/ppermute | solution.py:22
  80.1 2.8 %collective-permute-start.18 = (bf16[176,256]{1,0:T(8,128)(2,1)S(1)}, bf16[176,256]{1,0:T(8,128)(2,1)S(1)}, u32[]{:S(2)}, u32[]{:S(2)}) collective-permute-start(bf16[176,256]{1,0:T(8,128)(2,1)S(1)} %get-tuple-element.25), channel_id=1, source_target_pairs={{0,19},{1,18},{2,17},{3,16},{4,23},{5,22},{6,21},{7,20},{8,27},{9,... | collective-permute-start | bytes 270344 | tf_op jit(solution)/shard_map/ppermute | solution.py:22
  87.9 1.9 %collective-permute-start.26 = (bf16[16,5120]{1,0:T(8,128)(2,1)S(1)}, bf16[16,5120]{1,0:T(8,128)(2,1)S(1)}, u32[]{:S(2)}, u32[]{:S(2)}) collective-permute-start(bf16[16,5120]{1,0:T(8,128)(2,1)S(1)} %get-tuple-element.18), channel_id=1, source_target_pairs={{0,12},{1,13},{2,14},{3,15},{4,0},{5,1},{6,2},{7,3},{8,4},{9,5},{1... | collective-permute-start | bytes 491528 | tf_op jit(solution)/shard_map/ppermute | solution.py:22
  89.8 3.8 %collective-permute-start.27 = (bf16[16,5120]{1,0:T(8,128)(2,1)S(1)}, bf16[16,5120]{1,0:T(8,128)(2,1)S(1)}, u32[]{:S(2)}, u32[]{:S(2)}) collective-permute-start(bf16[16,5120]{1,0:T(8,128)(2,1)S(1)} %get-tuple-element.20), channel_id=1, source_target_pairs={{0,8},{1,9},{2,10},{3,11},{4,12},{5,13},{6,14},{7,15},{8,0},{9,1},... | collective-permute-start | bytes 491528 | tf_op jit(solution)/shard_map/ppermute | solution.py:22
  93.6 1.9 %collective-permute-start.28 = (bf16[16,5120]{1,0:T(8,128)(2,1)S(1)}, bf16[16,5120]{1,0:T(8,128)(2,1)S(1)}, u32[]{:S(2)}, u32[]{:S(2)}) collective-permute-start(bf16[16,5120]{1,0:T(8,128)(2,1)S(1)} %get-tuple-element.19), channel_id=1, source_target_pairs={{0,4},{1,5},{2,6},{3,7},{4,8},{5,9},{6,10},{7,11},{8,12},{9,13},{1... | collective-permute-start | bytes 491528 | tf_op jit(solution)/shard_map/ppermute | solution.py:22
  95.5 6.9 %collective-permute-done.20 = bf16[256,1024]{1,0:T(8,128)(2,1)S(1)} collective-permute-done((bf16[256,1024]{1,0:T(8,128)(2,1)}, bf16[256,1024]{1,0:T(8,128)(2,1)S(1)}, u32[]{:S(2)}, u32[]{:S(2)}) %collective-permute-start.20) | collective-permute-done | bytes 524320 | tf_op jit(solution)/shard_map/ppermute | solution.py:22
  103.1 3.1 %collective-permute-start.21 = (bf16[176,256]{1,0:T(8,128)(2,1)S(1)}, bf16[176,256]{1,0:T(8,128)(2,1)S(1)}, u32[]{:S(2)}, u32[]{:S(2)}) collective-permute-start(bf16[176,256]{1,0:T(8,128)(2,1)S(1)} %get-tuple-element.24), channel_id=1, source_target_pairs={{0,2},{1,3},{2,0},{3,1},{12,14},{13,15},{14,12},{15,13},{16,18},{1... | collective-permute-start | bytes 270344 | tf_op jit(solution)/shard_map/ppermute | solution.py:22
  106.1 3.4 %collective-permute-start.22 = (bf16[176,256]{1,0:T(8,128)(2,1)S(1)}, bf16[176,256]{1,0:T(8,128)(2,1)S(1)}, u32[]{:S(2)}, u32[]{:S(2)}) collective-permute-start(bf16[176,256]{1,0:T(8,128)(2,1)S(1)} %get-tuple-element.23), channel_id=1, source_target_pairs={{0,3},{1,2},{2,1},{3,0},{12,15},{13,14},{14,13},{15,12},{16,19},{1... | collective-permute-start | bytes 270344 | tf_op jit(solution)/shard_map/ppermute | solution.py:22
  109.6 2.1 %collective-permute-done.26 = bf16[16,5120]{1,0:T(8,128)(2,1)S(1)} collective-permute-done((bf16[16,5120]{1,0:T(8,128)(2,1)S(1)}, bf16[16,5120]{1,0:T(8,128)(2,1)S(1)}, u32[]{:S(2)}, u32[]{:S(2)}) %collective-permute-start.26) | collective-permute-done | bytes 163872 | tf_op jit(solution)/shard_map/ppermute | solution.py:22
  111.7 3.3 %collective-permute-start.23 = (bf16[176,256]{1,0:T(8,128)(2,1)S(1)}, bf16[176,256]{1,0:T(8,128)(2,1)S(1)}, u32[]{:S(2)}, u32[]{:S(2)}) collective-permute-start(bf16[176,256]{1,0:T(8,128)(2,1)S(1)} %get-tuple-element.22), channel_id=1, source_target_pairs={{0,18},{1,19},{2,16},{3,17},{12,30},{13,31},{14,28},{15,29},{16,2}... | collective-permute-start | bytes 270344 | tf_op jit(solution)/shard_map/ppermute | solution.py:22
  115.0 3.2 %collective-permute-start.24 = (bf16[176,256]{1,0:T(8,128)(2,1)S(1)}, bf16[176,256]{1,0:T(8,128)(2,1)S(1)}, u32[]{:S(2)}, u32[]{:S(2)}) collective-permute-start(bf16[176,256]{1,0:T(8,128)(2,1)S(1)} %get-tuple-element.21), channel_id=1, source_target_pairs={{0,19},{1,18},{2,17},{3,16},{12,31},{13,30},{14,29},{15,28},{16,3}... | collective-permute-start | bytes 270344 | tf_op jit(solution)/shard_map/ppermute | solution.py:22
  119.6 2.8 %collective-permute-done.24 = bf16[176,256]{1,0:T(8,128)(2,1)S(1)} collective-permute-done((bf16[176,256]{1,0:T(8,128)(2,1)S(1)}, bf16[176,256]{1,0:T(8,128)(2,1)S(1)}, u32[]{:S(2)}, u32[]{:S(2)}) %collective-permute-start.24) | collective-permute-done | bytes 90144 | tf_op jit(solution)/shard_map/ppermute | solution.py:22
  (109 shorter events, 29.5 us)
Async XLA Ops:
  3.4 27.7 %collective-permute-start.1 = (bf16[176,1152]{1,0:T(8,128)(2,1)}, bf16[176,1152]{1,0:T(8,128)(2,1)S(1)}, u32[]{:S(2)}, u32[]{:S(2)}) collective-permute-start(bf16[176,1152]{1,0:T(8,128)(2,1)} %pad_maximum_fusion.3), channel_id=1, source_target_pairs={{0,16},{1,17},{2,18},{3,19},{4,20},{5,21},{6,22},{7,23},{8,24},{9,... | collective-permute-start | bytes 1216520 | tf_op jit(solution)/shard_map/ppermute | solution.py:22
  6.4 34.9 %collective-permute-start = (bf16[176,1152]{1,0:T(8,128)(2,1)}, bf16[176,1152]{1,0:T(8,128)(2,1)S(1)}, u32[]{:S(2)}, u32[]{:S(2)}) collective-permute-start(bf16[176,1152]{1,0:T(8,128)(2,1)} %pad_maximum_fusion.3), channel_id=1, source_target_pairs={{0,1},{1,0},{2,3},{3,2},{4,5},{5,4},{6,7},{7,6},{8,9},{9,8},{10,11... | collective-permute-start | bytes 1216520 | tf_op jit(solution)/shard_map/ppermute | solution.py:22
  8.1 9.2 %collective-permute-start.5 = (bf16[16,5120]{1,0:T(8,128)(2,1)}, bf16[16,5120]{1,0:T(8,128)(2,1)}, u32[]{:S(2)}, u32[]{:S(2)}) collective-permute-start(bf16[16,5120]{1,0:T(8,128)(2,1)} %get-tuple-element.6), channel_id=1, source_target_pairs={{0,4},{1,5},{2,6},{3,7},{4,8},{5,9},{6,10},{7,11},{8,12},{9,13},{1... | collective-permute-start | bytes 491528 | tf_op jit(solution)/shard_map/ppermute | solution.py:22
  9.7 15.8 %collective-permute-start.6 = (bf16[16,5120]{1,0:T(8,128)(2,1)}, bf16[16,5120]{1,0:T(8,128)(2,1)}, u32[]{:S(2)}, u32[]{:S(2)}) collective-permute-start(bf16[16,5120]{1,0:T(8,128)(2,1)} %get-tuple-element.6), channel_id=1, source_target_pairs={{0,8},{1,9},{2,10},{3,11},{4,12},{5,13},{6,14},{7,15},{8,0},{9,1},... | collective-permute-start | bytes 491528 | tf_op jit(solution)/shard_map/ppermute | solution.py:22
  12.2 14.5 %collective-permute-start.7 = (bf16[16,5120]{1,0:T(8,128)(2,1)}, bf16[16,5120]{1,0:T(8,128)(2,1)S(1)}, u32[]{:S(2)}, u32[]{:S(2)}) collective-permute-start(bf16[16,5120]{1,0:T(8,128)(2,1)} %get-tuple-element.6), channel_id=1, source_target_pairs={{0,12},{1,13},{2,14},{3,15},{4,0},{5,1},{6,2},{7,3},{8,4},{9,5},{1... | collective-permute-start | bytes 491528 | tf_op jit(solution)/shard_map/ppermute | solution.py:22
  14.0 27.4 %copy-start.1 = (bf16[1,176,1024]{2,1,0:T(8,128)(2,1)S(1)}, bf16[1,176,1024]{2,1,0:T(8,128)(2,1)}, u32[]{:S(2)}) copy-start(bf16[1,176,1024]{2,1,0:T(8,128)(2,1)} %param.8) | copy-start | bytes 1081348
  14.0 27.6 %copy-start.7 = (bf16[256,1024]{1,0:T(8,128)(2,1)}, bf16[256,1024]{1,0:T(8,128)(2,1)S(1)}, u32[]{:S(2)}) copy-start(bf16[256,1024]{1,0:T(8,128)(2,1)S(1)} %dynamic-slice_bitcast_fusion) | copy-start | bytes 1572868
  17.3 15.0 %collective-permute-start.3 = (bf16[256,1024]{1,0:T(8,128)(2,1)S(1)}, bf16[256,1024]{1,0:T(8,128)(2,1)}, u32[]{:S(2)}, u32[]{:S(2)}) collective-permute-start(bf16[256,1024]{1,0:T(8,128)(2,1)S(1)} %dynamic-slice_bitcast_fusion), channel_id=1, source_target_pairs={{0,4},{1,5},{2,6},{3,7},{4,8},{5,9},{6,10},{7,11},{8,12},{9,13},{1... | collective-permute-start | bytes 1572872 | tf_op jit(solution)/shard_map/ppermute | solution.py:22
  25.5 14.6 %collective-permute-start.4 = (bf16[256,1024]{1,0:T(8,128)(2,1)S(1)}, bf16[256,1024]{1,0:T(8,128)(2,1)}, u32[]{:S(2)}, u32[]{:S(2)}) collective-permute-start(bf16[256,1024]{1,0:T(8,128)(2,1)S(1)} %dynamic-slice_bitcast_fusion), channel_id=1, source_target_pairs={{4,0},{5,1},{6,2},{7,3},{8,4},{9,5},{10,6},{11,7},{12,8},{13,9},{1... | collective-permute-start | bytes 1572872 | tf_op jit(solution)/shard_map/ppermute | solution.py:22
  27.9 14.1 %collective-permute-start.8 = (bf16[64,5120]{1,0:T(8,128)(2,1)S(1)}, bf16[64,5120]{1,0:T(8,128)(2,1)S(1)}, u32[]{:S(2)}, u32[]{:S(2)}) collective-permute-start(bf16[64,5120]{1,0:T(8,128)(2,1)S(1)} %pad_maximum_fusion.2), channel_id=1, source_target_pairs={{0,1},{1,0},{2,3},{3,2},{4,5},{5,4},{6,7},{7,6},{8,9},{9,8},{10,11... | collective-permute-start | bytes 1966088 | tf_op jit(solution)/shard_map/ppermute | solution.py:22
  31.1 10.2 %collective-permute-start.2 = (bf16[176,1152]{1,0:T(8,128)(2,1)S(1)}, bf16[176,1152]{1,0:T(8,128)(2,1)S(1)}, u32[]{:S(2)}, u32[]{:S(2)}) collective-permute-start(bf16[176,1152]{1,0:T(8,128)(2,1)S(1)} %collective-permute-done.1), channel_id=1, source_target_pairs={{0,1},{1,0},{2,3},{3,2},{4,5},{5,4},{6,7},{7,6},{8,9},{9,8},{10,11... | collective-permute-start | bytes 1216520 | tf_op jit(solution)/shard_map/ppermute | solution.py:22
  32.3 26.0 %collective-permute-start.13 = (bf16[256,1024]{1,0:T(8,128)(2,1)}, bf16[256,1024]{1,0:T(8,128)(2,1)}, u32[]{:S(2)}, u32[]{:S(2)}) collective-permute-start(bf16[256,1024]{1,0:T(8,128)(2,1)} %collective-permute-done.3), channel_id=1, source_target_pairs={{4,8},{5,9},{6,10},{7,11},{8,12},{9,13},{10,14},{11,15},{20,24},{2... | collective-permute-start | bytes 1572872 | tf_op jit(solution)/shard_map/ppermute | solution.py:22
  40.1 19.8 %collective-permute-start.14 = (bf16[256,1024]{1,0:T(8,128)(2,1)}, bf16[256,1024]{1,0:T(8,128)(2,1)}, u32[]{:S(2)}, u32[]{:S(2)}) collective-permute-start(bf16[256,1024]{1,0:T(8,128)(2,1)} %collective-permute-done.4), channel_id=1, source_target_pairs={{4,0},{5,1},{6,2},{7,3},{8,4},{9,5},{10,6},{11,7},{20,16},{21,17},... | collective-permute-start | bytes 1572872 | tf_op jit(solution)/shard_map/ppermute | solution.py:22
  50.1 37.5 %collective-permute-start.25 = (bf16[4,16,5120]{2,1,0:T(8,128)(2,1)S(1)}, bf16[4,16,5120]{2,1,0:T(8,128)(2,1)S(1)}, u32[]{:S(2)}, u32[]{:S(2)}) collective-permute-start(bf16[4,16,5120]{2,1,0:T(8,128)(2,1)S(1)} %bitcast.73), channel_id=1, source_target_pairs={{0,1},{1,0},{2,3},{3,2},{4,5},{5,4},{6,7},{7,6},{8,9},{9,8},{10,11... | collective-permute-start | bytes 1966088 | tf_op jit(solution)/shard_map/ppermute | solution.py:22
  54.4 9.4 %collective-permute-start.9 = (bf16[176,768]{1,0:T(8,128)(2,1)S(1)}, bf16[176,768]{1,0:T(8,128)(2,1)S(1)}, u32[]{:S(2)}, u32[]{:S(2)}) collective-permute-start(bf16[176,768]{1,0:T(8,128)(2,1)S(1)} %get-tuple-element.14), channel_id=1, source_target_pairs={{0,2},{1,3},{2,0},{3,1},{4,6},{5,7},{6,4},{7,5},{8,10},{9,11},{10,... | collective-permute-start | bytes 811016 | tf_op jit(solution)/shard_map/ppermute | solution.py:22
  55.9 12.6 %collective-permute-start.10 = (bf16[176,768]{1,0:T(8,128)(2,1)S(1)}, bf16[176,768]{1,0:T(8,128)(2,1)S(1)}, u32[]{:S(2)}, u32[]{:S(2)}) collective-permute-start(bf16[176,768]{1,0:T(8,128)(2,1)S(1)} %get-tuple-element.13), channel_id=1, source_target_pairs={{0,3},{1,2},{2,1},{3,0},{4,7},{5,6},{6,5},{7,4},{8,11},{9,10},{10,... | collective-permute-start | bytes 811016 | tf_op jit(solution)/shard_map/ppermute | solution.py:22
  58.3 17.0 %collective-permute-start.11 = (bf16[176,768]{1,0:T(8,128)(2,1)S(1)}, bf16[176,768]{1,0:T(8,128)(2,1)S(1)}, u32[]{:S(2)}, u32[]{:S(2)}) collective-permute-start(bf16[176,768]{1,0:T(8,128)(2,1)S(1)} %get-tuple-element.12), channel_id=1, source_target_pairs={{0,18},{1,19},{2,16},{3,17},{4,22},{5,23},{6,20},{7,21},{8,26},{9,... | collective-permute-start | bytes 811016 | tf_op jit(solution)/shard_map/ppermute | solution.py:22
  59.8 20.3 %collective-permute-start.12 = (bf16[176,768]{1,0:T(8,128)(2,1)S(1)}, bf16[176,768]{1,0:T(8,128)(2,1)S(1)}, u32[]{:S(2)}, u32[]{:S(2)}) collective-permute-start(bf16[176,768]{1,0:T(8,128)(2,1)S(1)} %get-tuple-element.11), channel_id=1, source_target_pairs={{0,19},{1,18},{2,17},{3,16},{4,23},{5,22},{6,21},{7,20},{8,27},{9,... | collective-permute-start | bytes 811016 | tf_op jit(solution)/shard_map/ppermute | solution.py:22
  63.7 19.3 %collective-permute-start.15 = (bf16[176,256]{1,0:T(8,128)(2,1)S(1)}, bf16[176,256]{1,0:T(8,128)(2,1)S(1)}, u32[]{:S(2)}, u32[]{:S(2)}) collective-permute-start(bf16[176,256]{1,0:T(8,128)(2,1)S(1)} %get-tuple-element.28), channel_id=1, source_target_pairs={{0,2},{1,3},{2,0},{3,1},{4,6},{5,7},{6,4},{7,5},{8,10},{9,11},{10,... | collective-permute-start | bytes 270344 | tf_op jit(solution)/shard_map/ppermute | solution.py:22
  68.5 15.4 %collective-permute-start.16 = (bf16[176,256]{1,0:T(8,128)(2,1)S(1)}, bf16[176,256]{1,0:T(8,128)(2,1)S(1)}, u32[]{:S(2)}, u32[]{:S(2)}) collective-permute-start(bf16[176,256]{1,0:T(8,128)(2,1)S(1)} %get-tuple-element.27), channel_id=1, source_target_pairs={{0,3},{1,2},{2,1},{3,0},{4,7},{5,6},{6,5},{7,4},{8,11},{9,10},{10,... | collective-permute-start | bytes 270344 | tf_op jit(solution)/shard_map/ppermute | solution.py:22
  75.3 11.6 %collective-permute-start.17 = (bf16[176,256]{1,0:T(8,128)(2,1)S(1)}, bf16[176,256]{1,0:T(8,128)(2,1)S(1)}, u32[]{:S(2)}, u32[]{:S(2)}) collective-permute-start(bf16[176,256]{1,0:T(8,128)(2,1)S(1)} %get-tuple-element.26), channel_id=1, source_target_pairs={{0,18},{1,19},{2,16},{3,17},{4,22},{5,23},{6,20},{7,21},{8,26},{9,... | collective-permute-start | bytes 270344 | tf_op jit(solution)/shard_map/ppermute | solution.py:22
  80.1 7.5 %collective-permute-start.18 = (bf16[176,256]{1,0:T(8,128)(2,1)S(1)}, bf16[176,256]{1,0:T(8,128)(2,1)S(1)}, u32[]{:S(2)}, u32[]{:S(2)}) collective-permute-start(bf16[176,256]{1,0:T(8,128)(2,1)S(1)} %get-tuple-element.25), channel_id=1, source_target_pairs={{0,19},{1,18},{2,17},{3,16},{4,23},{5,22},{6,21},{7,20},{8,27},{9,... | collective-permute-start | bytes 270344 | tf_op jit(solution)/shard_map/ppermute | solution.py:22
  83.1 12.5 %collective-permute-start.19 = (bf16[256,1024]{1,0:T(8,128)(2,1)}, bf16[256,1024]{1,0:T(8,128)(2,1)S(1)}, u32[]{:S(2)}, u32[]{:S(2)}) collective-permute-start(bf16[256,1024]{1,0:T(8,128)(2,1)} %collective-permute-done.13), channel_id=1, source_target_pairs={{8,12},{9,13},{10,14},{11,15},{24,28},{25,29},{26,30},{27,31}} | collective-permute-start | bytes 1572872 | tf_op jit(solution)/shard_map/ppermute | solution.py:22
  84.0 18.4 %collective-permute-start.20 = (bf16[256,1024]{1,0:T(8,128)(2,1)}, bf16[256,1024]{1,0:T(8,128)(2,1)S(1)}, u32[]{:S(2)}, u32[]{:S(2)}) collective-permute-start(bf16[256,1024]{1,0:T(8,128)(2,1)} %collective-permute-done.14), channel_id=1, source_target_pairs={{4,0},{5,1},{6,2},{7,3},{20,16},{21,17},{22,18},{23,19}} | collective-permute-start | bytes 1572872 | tf_op jit(solution)/shard_map/ppermute | solution.py:22
  87.9 23.8 %collective-permute-start.26 = (bf16[16,5120]{1,0:T(8,128)(2,1)S(1)}, bf16[16,5120]{1,0:T(8,128)(2,1)S(1)}, u32[]{:S(2)}, u32[]{:S(2)}) collective-permute-start(bf16[16,5120]{1,0:T(8,128)(2,1)S(1)} %get-tuple-element.18), channel_id=1, source_target_pairs={{0,12},{1,13},{2,14},{3,15},{4,0},{5,1},{6,2},{7,3},{8,4},{9,5},{1... | collective-permute-start | bytes 491528 | tf_op jit(solution)/shard_map/ppermute | solution.py:22
  89.8 25.2 %collective-permute-start.27 = (bf16[16,5120]{1,0:T(8,128)(2,1)S(1)}, bf16[16,5120]{1,0:T(8,128)(2,1)S(1)}, u32[]{:S(2)}, u32[]{:S(2)}) collective-permute-start(bf16[16,5120]{1,0:T(8,128)(2,1)S(1)} %get-tuple-element.20), channel_id=1, source_target_pairs={{0,8},{1,9},{2,10},{3,11},{4,12},{5,13},{6,14},{7,15},{8,0},{9,1},... | collective-permute-start | bytes 491528 | tf_op jit(solution)/shard_map/ppermute | solution.py:22
  93.6 24.6 %collective-permute-start.28 = (bf16[16,5120]{1,0:T(8,128)(2,1)S(1)}, bf16[16,5120]{1,0:T(8,128)(2,1)S(1)}, u32[]{:S(2)}, u32[]{:S(2)}) collective-permute-start(bf16[16,5120]{1,0:T(8,128)(2,1)S(1)} %get-tuple-element.19), channel_id=1, source_target_pairs={{0,4},{1,5},{2,6},{3,7},{4,8},{5,9},{6,10},{7,11},{8,12},{9,13},{1... | collective-permute-start | bytes 491528 | tf_op jit(solution)/shard_map/ppermute | solution.py:22
  103.1 15.7 %collective-permute-start.21 = (bf16[176,256]{1,0:T(8,128)(2,1)S(1)}, bf16[176,256]{1,0:T(8,128)(2,1)S(1)}, u32[]{:S(2)}, u32[]{:S(2)}) collective-permute-start(bf16[176,256]{1,0:T(8,128)(2,1)S(1)} %get-tuple-element.24), channel_id=1, source_target_pairs={{0,2},{1,3},{2,0},{3,1},{12,14},{13,15},{14,12},{15,13},{16,18},{1... | collective-permute-start | bytes 270344 | tf_op jit(solution)/shard_map/ppermute | solution.py:22
  106.1 12.7 %collective-permute-start.22 = (bf16[176,256]{1,0:T(8,128)(2,1)S(1)}, bf16[176,256]{1,0:T(8,128)(2,1)S(1)}, u32[]{:S(2)}, u32[]{:S(2)}) collective-permute-start(bf16[176,256]{1,0:T(8,128)(2,1)S(1)} %get-tuple-element.23), channel_id=1, source_target_pairs={{0,3},{1,2},{2,1},{3,0},{12,15},{13,14},{14,13},{15,12},{16,19},{1... | collective-permute-start | bytes 270344 | tf_op jit(solution)/shard_map/ppermute | solution.py:22
  111.7 7.7 %collective-permute-start.23 = (bf16[176,256]{1,0:T(8,128)(2,1)S(1)}, bf16[176,256]{1,0:T(8,128)(2,1)S(1)}, u32[]{:S(2)}, u32[]{:S(2)}) collective-permute-start(bf16[176,256]{1,0:T(8,128)(2,1)S(1)} %get-tuple-element.22), channel_id=1, source_target_pairs={{0,18},{1,19},{2,16},{3,17},{12,30},{13,31},{14,28},{15,29},{16,2}... | collective-permute-start | bytes 270344 | tf_op jit(solution)/shard_map/ppermute | solution.py:22
  115.0 7.4 %collective-permute-start.24 = (bf16[176,256]{1,0:T(8,128)(2,1)S(1)}, bf16[176,256]{1,0:T(8,128)(2,1)S(1)}, u32[]{:S(2)}, u32[]{:S(2)}) collective-permute-start(bf16[176,256]{1,0:T(8,128)(2,1)S(1)} %get-tuple-element.21), channel_id=1, source_target_pairs={{0,19},{1,18},{2,17},{3,16},{12,31},{13,30},{14,29},{15,28},{16,3}... | collective-permute-start | bytes 270344 | tf_op jit(solution)/shard_map/ppermute | solution.py:22
  118.3 4.1 %collective-permute-start.29 = (bf16[16,5120]{1,0:T(8,128)(2,1)S(1)}, bf16[16,5120]{1,0:T(8,128)(2,1)S(1)}, u32[]{:S(2)}, u32[]{:S(2)}) collective-permute-start(bf16[16,5120]{1,0:T(8,128)(2,1)S(1)} %get-tuple-element.4), channel_id=1, source_target_pairs={{0,1},{1,0},{2,3},{3,2},{4,5},{5,4},{6,7},{7,6},{8,9},{9,8},{10,11... | collective-permute-start | bytes 491528 | tf_op jit(solution)/shard_map/ppermute | solution.py:22
  (7 other events, 24.3 us)

commit v3 on v2

--- a/solution.py
+++ b/solution.py
@@ -50,10 +50,7 @@
     both = jnp.concatenate([adapter_down_weight[0], adapter_up_weight[0]], axis=2)
     rows = own_slots * rank
     own = lax.dynamic_slice_in_dim(both, core * own_slots, own_slots, axis=0).reshape(rows, -1)
-    held = [own]
-    for k in range(1, holders):
-        held.append(moved(own, lambda g, z, s, r: (g, z + k, s, r)))
-    held = jnp.concatenate(held, axis=0)
+    held = lax.all_gather(own, "adapter", axis=0, tiled=True)
     maps = [held]
     for dr in range(1, replicas):
         maps.append(moved(held, lambda g, z, s, r: (g, z, s, r + dr)))
@@ -61,7 +58,7 @@
     down, up = maps[:, :width], maps[:, width:]
     row_slot = jnp.concatenate(
         [
-            ((here - k) % holders) * slots
+            k * slots
             + ((core - dr) % replicas) * own_slots
             + jnp.arange(rows, dtype=jnp.int32) // rank
             for dr in range(replicas)
@@ -87,21 +84,17 @@
     slots_all = tagged[:, value_width].astype(jnp.int32)
 
     quarter = group * replicas + core
-    mine = lax.dynamic_slice_in_dim(frozen, quarter * piece, piece, axis=0)
-    ups, downs = [mine], [mine]
-    for k in range(1, holders):
-        ups.append(
-            moved(
-                ups[-1],
-                lambda g, z, s, r: (g, z + 1, s, r) if k - 1 <= z < holders - 1 else None,
-            )
+    chunks = 2 if piece % (2 * LANES) == 0 else 1
+    step = piece // chunks
+    weights = [
+        lax.all_gather(
+            lax.dynamic_slice_in_dim(frozen, quarter * piece + c * step, step, axis=0),
+            "adapter",
+            axis=0,
+            tiled=True,
         )
-        downs.append(
-            moved(
-                downs[-1],
-                lambda g, z, s, r: (g, z - 1, s, r) if 0 < z <= holders - k else None,
-            )
-        )
+        for c in range(chunks)
+    ]
 
     keep = slots_all[:, None] == row_slot[None, :]
     proj_grad = jnp.einsum("tk,rk->tr", grads_all, up, preferred_element_type=F32)
@@ -122,9 +115,10 @@
     for dr in range(1, replicas):
         chip = chip + moved(part[dr], lambda g, z, s, r: (g, z, s, r - dr)).astype(F32)
     chip_out = chip.astype(BF16)
-    total = chip[0]
+    total = lax.dynamic_index_in_dim(chip, here, 0, keepdims=False)
     for k in range(1, holders):
-        total = total + moved(chip_out[k], lambda g, z, s, r: (g, z - k, s, r)).astype(F32)
+        block = lax.dynamic_index_in_dim(chip_out, (here + k) % holders, 0, keepdims=False)
+        total = total + moved(block, lambda g, z, s, r: (g, z + k, s, r)).astype(F32)
     total = (ADAPTER_SCALE * total).astype(BF16)
     summed = jnp.zeros((slots, rank, width + value_width), BF16)
     for dr in range(replicas):
@@ -138,56 +132,35 @@
     down_grad = summed[None, :, :, :width]
     up_grad = summed[None, :, :, width:]
 
-    batches = [([(mine, here, None)], lambda z: True)]
-    for k in range(1, holders):
-        has = lambda z, k=k: z >= k or z <= holders - 1 - k
-        from_below = here >= k
-        from_above = here <= holders - 1 - k
-        if 2 * k <= holders - 1:
-            blocks = [(ups[k], here - k, from_below), (downs[k], here + k, from_above)]
-        else:
-            blocks = [
-                (
-                    jnp.where(from_below, ups[k], downs[k]),
-                    jnp.where(from_below, here - k, here + k),
-                    from_below | from_above,
-                )
-            ]
-        if k == 1:
-            batches[0][0].extend(blocks)
-        else:
-            batches.append((blocks, has))
-
     passed = jnp.zeros((tokens, width), BF16)
-    for blocks, has in batches:
-        weight = jnp.concatenate([b for b, _, _ in blocks], axis=0)
+    for c in range(chunks):
         columns = jnp.concatenate(
             [
                 lax.dynamic_slice_in_dim(
-                    down, jnp.clip(at, 0, holders - 1) * shard + quarter * piece, piece, axis=1
+                    down, k * shard + quarter * piece + c * step, step, axis=1
                 )
-                for _, at, _ in blocks
+                for k in range(holders)
             ],
             axis=1,
         )
-        base = jnp.einsum("tk,dk->td", grads_all, weight, preferred_element_type=F32).astype(BF16)
+        base = jnp.einsum("tk,dk->td", grads_all, weights[c], preferred_element_type=F32)
         lora = (
             ADAPTER_SCALE * jnp.einsum("tr,rd->td", sel_all, columns, preferred_element_type=F32)
         ).astype(BF16)
-        out = (base.astype(F32) + lora.astype(F32)).astype(BF16)
+        out = (base.astype(BF16).astype(F32) + lora.astype(F32)).astype(BF16)
         for i, (dg, dr) in enumerate(peers):
             got = moved(
                 out[i * tokens : (i + 1) * tokens],
-                lambda g, z, s, r: (g + dg, z, s - 1, r + dr) if has(z) else None,
+                lambda g, z, s, r: (g + dg, z, s - 1, r + dr),
             )
             source = ((group - dg) % groups) * replicas + (core - dr) % replicas
-            for j, (_, at, valid) in enumerate(blocks):
-                place = jnp.clip(at, 0, holders - 1) * shard + source * piece
-                block = got[:, j * piece : (j + 1) * piece]
-                if valid is not None:
-                    old = lax.dynamic_slice_in_dim(passed, place, piece, axis=1)
-                    block = jnp.where(valid, block, old)
-                passed = lax.dynamic_update_slice_in_dim(passed, block, place, axis=1)
+            for k in range(holders):
+                passed = lax.dynamic_update_slice_in_dim(
+                    passed,
+                    got[:, k * step : (k + 1) * step],
+                    k * shard + source * piece + c * step,
+                    axis=1,
+                )
     return passed[None], down_grad, up_grad
 
 

time: 125 us -> 139 us (1.11)
  starting transfers between devices: 57.8 us -> 18.2 us
  blocking collectives: 0 us -> 24.4 us
  waiting for transfers between devices: 35.4 us -> 52.4 us
  between operations: 1.44 us -> 14.9 us
  local copies, waits for them, and re-layouts: 10.3 us -> 7.02 us
  other arithmetic: 6.84 us -> 9.99 us
    ppermute x30 -> x17, starting transfers between devices: 57.8 us -> 18.1 us  [moved(): return lax.ppermute(x, AXES, pairs)]
    all_gather x0 -> x1, blocking collectives: none -> 24.4 us  [on_device(): held = lax.all_gather(own, 'adapter', axis=0, tiled=True)]
    all_gather x0 -> x2, waiting for transfers between devices: none -> 22.9 us  [on_device(): lax.all_gather(lax.dynamic_slice_in_dim(frozen, quarter * piece + c * ste...]
    ppermute x30 -> x17, waiting for transfers between devices: 35.4 us -> 29.5 us  [moved(): return lax.ppermute(x, AXES, pairs)]
    unnamed x22, local copies, waits for them, and re-layouts: 5.99 us -> 1.76 us
    concatenate x1, other arithmetic: 0.15 us -> 2.41 us  [on_device(): tagged = jnp.concatenate([by_peer[p] for p in peers], axis=0)]
    unnamed x1 -> x0, other arithmetic: 1.67 us -> none
    eq x2, other arithmetic: 0.34 us -> 1.81 us  [on_device(): keep = slots_all[:, None] == row_slot[None, :]]
  transfers between devices with their start and end apart: 30 -> 19, of which waited for: 13 -> 7; matrix products, arithmetic and copies ran while one was open for 19% -> 17% of each run, Pallas kernels for 0% -> 0%
where the time goes in v3:
time: 139 us
  waiting for transfers between devices  52.4 us (38%)
  blocking collectives  24.4 us (18%)
  starting transfers between devices  18.2 us (13%)
  between operations  14.9 us (11%)
  matrix products  12 us (9%)
  other arithmetic  9.99 us (7%)
  local copies, waits for them, and re-layouts  7.02 us (5%)
    ppermute x17, waiting for transfers between devices, moved(): return lax.ppermute(x, AXES, pairs)  29.5 us
    all_gather x1, blocking collectives, on_device(): held = lax.all_gather(own, 'adapter', axis=0, tiled=True)  24.4 us
    all_gather x2, waiting for transfers between devices, on_device(): lax.all_gather(lax.dynamic_slice_in_dim(frozen, quarter * piece + c * ste...  22.9 us
    ppermute x17, starting transfers between devices, moved(): return lax.ppermute(x, AXES, pairs)  18.1 us
    dot_general x2, matrix products, on_device(): jnp.einsum('tk,dk->td', grads_all, weights[c], preferred_element_type=F32)  5.42 us
  transfers between devices with their start and end apart: 19, of which 7 were waited for; matrix products, arithmetic and copies ran while one was open for 17% of the time, Pallas kernels for 0%

profile of v3, /device:TPU:0, one launch (start us, length us, event | category | flops | bytes accessed | tf_op | source)
XLA Modules:
  0.0 138.9 jit_solution(9863267679936318709)
XLA Ops:
  7.3 2.0 %constant_dynamic-slice_fusion = (bf16[1,128,1024]{2,1,0:T(8,128)(2,1)}, bf16[1,128,1024]{2,1,0:T(8,128)(2,1)}) fusion(bf16[1,1024,1024]{2,1,0:T(8,128)(2,1)} %param.11, s32[]{:T(128)S(6)} %select_n.291, s32[]{:T(128)S(6)} %select_n.263), kind=kLoop, calls=%fused_computation.156 | loop fusion | bytes 1048584 | tf_op jit(solution)/shard_map/dynamic_slice | solution.py:91
  9.3 0.8 select_reduce_fusion
  10.2 0.8 pad_maximum_fusion.5
  11.0 3.0 %collective-permute-start.1 = (bf16[176,1152]{1,0:T(8,128)(2,1)}, bf16[176,1152]{1,0:T(8,128)(2,1)S(1)}, u32[]{:S(2)}, u32[]{:S(2)}) collective-permute-start(bf16[176,1152]{1,0:T(8,128)(2,1)} %pad_maximum_fusion.5), channel_id=1, source_target_pairs={{0,16},{1,17},{2,18},{3,19},{4,20},{5,21},{6,22},{7,23},{8,24},{9,... | collective-permute-start | bytes 1216520 | tf_op jit(solution)/shard_map/ppermute | solution.py:22
  14.0 24.4 %all-gather.1 = bf16[1,64,5120]{2,1,0:T(8,128)(2,1)S(1)} all-gather(bf16[1,16,5120]{2,1,0:T(8,128)(2,1)S(1)} %fusion.30), channel_id=3, replica_groups=mesh['groups'=2,'adapter'=4,'segment'=2,'replica'=2] {'adapter'}, dimensions={1}, use_global_device_ids=true | all-gather | bytes 819200 | tf_op jit(solution)/shard_map/all_gather | solution.py:53
  39.5 1.7 %collective-permute-done.2 = bf16[176,1152]{1,0:T(8,128)(2,1)} collective-permute-done((bf16[176,1152]{1,0:T(8,128)(2,1)S(1)}, bf16[176,1152]{1,0:T(8,128)(2,1)}, u32[]{:S(2)}, u32[]{:S(2)}) %collective-permute-start.2) | collective-permute-done | bytes 405536 | tf_op jit(solution)/shard_map/ppermute | solution.py:22
  41.2 1.0 convert_reduce_fusion
  42.2 0.8 broadcast_compare_fusion
  43.0 2.4 %pad_maximum_fusion.1 = bf16[704,1152]{1,0:T(8,128)(2,1)} fusion(bf16[176,1152]{1,0:T(8,128)(2,1)} %collective-permute-done.2, bf16[176,1152]{1,0:T(8,128)(2,1)S(1)} %collective-permute-done.1, bf16[176,1152]{1,0:T(8,128)(2,1)} %collective-permute-done, bf16[176,128]{1,0:T(8,128)(2,1)S(1)} %copy-done.6, bf16[176,1024]{1,0:T(8,128)(2,1)S(1)} %bitcast.199), kind=kLoop, calls=%fused_computation.18 | loop fusion | flops 8110080 | bytes 3244032 | tf_op jit(solution)/shard_map/concatenate | solution.py:82
  45.4 0.8 copy-done.2
  46.3 1.9 %fusion.5 = bf16[704,128]{1,0:T(8,128)(2,1)S(1)} fusion(bf16[704,1152]{1,0:T(8,128)(2,1)} %pad_maximum_fusion.1, bf16[64,5120]{1,0:T(8,128)(2,1)S(1)} %collective-permute-done.3, bf16[64,5120]{1,0:T(8,128)(2,1)S(1)} %bitcast.193, s32[128]{0:T(128)S(1)} %concatenate.27, s32[704]{0:T(1024)S(1)} %convert_reduce_fusion), kind=kOutput, calls=%fused_computation.35 | convolution fusion | flops 185344000 | bytes 2936064 | tf_op jit(solution)/shard_map/tk,rk->tr/dot_general | solution.py:100
  49.3 2.7 %convolution_convert_fusion.3 = bf16[128,1024]{1,0:T(8,128)(2,1)} fusion(bf16[1,176,4096]{2,1,0:T(8,128)(2,1)S(1)} %copy-done, bf16[64,5120]{1,0:T(8,128)(2,1)} %copy-done.2, bf16[64,5120]{1,0:T(8,128)(2,1)S(1)} %bitcast.194, pred[704,128]{1,0:T(8,128)(4,1)} %broadcast_compare_fusion, bf16[1,176,1024]{2,1,0:T(8,128)(2,1)S(1)} %copy-done.1), kind=kOutput, calls=%fused_computation.33 | convolution fusion | flops 232960000 | bytes 3397632 | tf_op jit(solution)/shard_map/tr,tk->rk/dot_general | solution.py:108
  52.0 1.1 fusion.22
  54.4 1.2 fusion.3
  55.6 1.2 convert_add_fusion
  56.8 0.8 dynamic-slice_bitcast_fusion.2
  57.6 1.6 %collective-permute-start.13 = (bf16[16,5120]{1,0:T(8,128)(2,1)}, bf16[16,5120]{1,0:T(8,128)(2,1)}, u32[]{:S(2)}, u32[]{:S(2)}) collective-permute-start(bf16[16,5120]{1,0:T(8,128)(2,1)} %get-tuple-element.27), channel_id=1, source_target_pairs={{0,4},{1,5},{2,6},{3,7},{4,8},{5,9},{6,10},{7,11},{8,12},{9,13},{1... | collective-permute-start | bytes 491528 | tf_op jit(solution)/shard_map/ppermute | solution.py:22
  59.2 2.6 %collective-permute-start.15 = (bf16[16,5120]{1,0:T(8,128)(2,1)}, bf16[16,5120]{1,0:T(8,128)(2,1)}, u32[]{:S(2)}, u32[]{:S(2)}) collective-permute-start(bf16[16,5120]{1,0:T(8,128)(2,1)} %get-tuple-element.28), channel_id=1, source_target_pairs={{0,12},{1,13},{2,14},{3,15},{4,0},{5,1},{6,2},{7,3},{8,4},{9,5},{1... | collective-permute-start | bytes 491528 | tf_op jit(solution)/shard_map/ppermute | solution.py:22
  62.3 2.6 %add_convert_fusion = bf16[704,512]{1,0:T(8,128)(2,1)S(1)} fusion(bf16[704,512]{1,0:T(8,128)(2,1)S(1)} %fusion.4, bf16[704,1152]{1,0:T(8,128)(2,1)} %pad_maximum_fusion.1, bf16[1,512,1024]{2,1,0:T(8,128)(2,1)} %all-gather.8.cloned.1.call-done), kind=kOutput, calls=%fused_computation.24 | convolution fusion | flops 739999744 | bytes 3932160 | tf_op jit(solution)/shard_map/tk,dk->td/dot_general | solution.py:146
  65.1 2.1 %collective-permute-start.10 = (bf16[176,512]{1,0:T(8,128)(2,1)S(1)}, bf16[176,512]{1,0:T(8,128)(2,1)S(1)}, u32[]{:S(2)}, u32[]{:S(2)}) collective-permute-start(bf16[176,512]{1,0:T(8,128)(2,1)S(1)} %get-tuple-element.20), channel_id=1, source_target_pairs={{0,18},{1,19},{2,16},{3,17},{4,22},{5,23},{6,20},{7,21},{8,26},{9,... | collective-permute-start | bytes 540680 | tf_op jit(solution)/shard_map/ppermute | solution.py:22
  67.2 22.9 %all-gather.6.cloned.1.call-done = bf16[1,512,1024]{2,1,0:T(8,128)(2,1)} async-done(((bf16[1,128,1024]{2,1,0:T(8,128)(2,1)}), bf16[1,512,1024]{2,1,0:T(8,128)(2,1)}) %all-gather.6.cloned.1.call-update) | async-done | bytes 1048592 | tf_op jit(solution)/shard_map/all_gather | solution.py:90
  90.1 2.8 %add_convert_fusion.1 = bf16[704,512]{1,0:T(8,128)(2,1)S(1)} fusion(bf16[704,512]{1,0:T(8,128)(2,1)} %fusion.3, bf16[704,1152]{1,0:T(8,128)(2,1)} %pad_maximum_fusion.1, bf16[1,512,1024]{2,1,0:T(8,128)(2,1)} %all-gather.6.cloned.1.call-done), kind=kOutput, calls=%fused_computation.25 | convolution fusion | flops 739999744 | bytes 3932160 | tf_op jit(solution)/shard_map/tk,dk->td/dot_general | solution.py:146
  93.5 1.1 collective-permute-start.8
  94.7 0.9 collective-permute-start.4
  95.6 1.3 bitcast_dynamic-update-slice_fusion.1
  96.9 10.7 %collective-permute-done.4 = bf16[176,512]{1,0:T(8,128)(2,1)S(1)} collective-permute-done((bf16[176,512]{1,0:T(8,128)(2,1)S(1)}, bf16[176,512]{1,0:T(8,128)(2,1)S(1)}, u32[]{:S(2)}, u32[]{:S(2)}) %collective-permute-start.4) | collective-permute-done | bytes 180256 | tf_op jit(solution)/shard_map/ppermute | solution.py:22
  108.4 5.9 %collective-permute-done.5 = bf16[176,512]{1,0:T(8,128)(2,1)S(1)} collective-permute-done((bf16[176,512]{1,0:T(8,128)(2,1)S(1)}, bf16[176,512]{1,0:T(8,128)(2,1)S(1)}, u32[]{:S(2)}, u32[]{:S(2)}) %collective-permute-start.5) | collective-permute-done | bytes 180256 | tf_op jit(solution)/shard_map/ppermute | solution.py:22
  114.3 2.7 %collective-permute-start.6 = (bf16[176,512]{1,0:T(8,128)(2,1)S(1)}, bf16[176,512]{1,0:T(8,128)(2,1)S(1)}, u32[]{:S(2)}, u32[]{:S(2)}) collective-permute-start(bf16[176,512]{1,0:T(8,128)(2,1)S(1)} %get-tuple-element.24), channel_id=1, source_target_pairs={{0,18},{1,19},{2,16},{3,17},{4,22},{5,23},{6,20},{7,21},{8,26},{9,... | collective-permute-start | bytes 540680 | tf_op jit(solution)/shard_map/ppermute | solution.py:22
  117.1 4.7 %collective-permute-done.6 = bf16[176,512]{1,0:T(8,128)(2,1)S(1)} collective-permute-done((bf16[176,512]{1,0:T(8,128)(2,1)S(1)}, bf16[176,512]{1,0:T(8,128)(2,1)S(1)}, u32[]{:S(2)}, u32[]{:S(2)}) %collective-permute-start.6) | collective-permute-done | bytes 180256 | tf_op jit(solution)/shard_map/ppermute | solution.py:22
  121.8 1.5 %collective-permute-start.7 = (bf16[176,512]{1,0:T(8,128)(2,1)S(1)}, bf16[176,512]{1,0:T(8,128)(2,1)S(1)}, u32[]{:S(2)}, u32[]{:S(2)}) collective-permute-start(bf16[176,512]{1,0:T(8,128)(2,1)S(1)} %get-tuple-element.23), channel_id=1, source_target_pairs={{0,19},{1,18},{2,17},{3,16},{4,23},{5,22},{6,21},{7,20},{8,27},{9,... | collective-permute-start | bytes 540680 | tf_op jit(solution)/shard_map/ppermute | solution.py:22
  123.4 5.8 %collective-permute-done.7 = bf16[176,512]{1,0:T(8,128)(2,1)S(1)} collective-permute-done((bf16[176,512]{1,0:T(8,128)(2,1)S(1)}, bf16[176,512]{1,0:T(8,128)(2,1)S(1)}, u32[]{:S(2)}, u32[]{:S(2)}) %collective-permute-start.7) | collective-permute-done | bytes 180256 | tf_op jit(solution)/shard_map/ppermute | solution.py:22
  131.3 0.7 slice_bitcast_fusion
  (97 shorter events, 7.5 us)
Async XLA Ops:
  7.2 41.7 %copy-start = (bf16[1,176,4096]{2,1,0:T(8,128)(2,1)S(1)}, bf16[1,176,4096]{2,1,0:T(8,128)(2,1)}, u32[]{:S(2)}) copy-start(bf16[1,176,4096]{2,1,0:T(8,128)(2,1)} %param.7) | copy-start | bytes 4325380
  7.2 3.0 %copy-start.1 = (bf16[1,176,1024]{2,1,0:T(8,128)(2,1)S(1)}, bf16[1,176,1024]{2,1,0:T(8,128)(2,1)}, u32[]{:S(2)}) copy-start(bf16[1,176,1024]{2,1,0:T(8,128)(2,1)} %param.8) | copy-start | bytes 1081348
  7.2 6.8 %copy-start.8 = (bf16[1,2,16,1024]{3,2,1,0:T(8,128)(2,1)S(1)}, bf16[1,2,16,1024]{3,2,1,0:T(8,128)(2,1)}, u32[]{:S(2)}) copy-start(bf16[1,2,16,1024]{3,2,1,0:T(8,128)(2,1)} %param.13) | copy-start | bytes 196612
  7.2 6.8 %copy-start.7 = (bf16[1,2,16,4096]{3,2,1,0:T(8,128)(2,1)S(1)}, bf16[1,2,16,4096]{3,2,1,0:T(8,128)(2,1)}, u32[]{:S(2)}) copy-start(bf16[1,2,16,4096]{3,2,1,0:T(8,128)(2,1)} %param.12) | copy-start | bytes 786436
  7.2 55.1 %all-gather.8.cloned.1.call-start = ((), (), s32[]{:S(2)}) async-start(), calls=%async_computation.1 | async-start | bytes 1310720 | tf_op jit(solution)/shard_map/all_gather | solution.py:90
  9.3 80.8 %all-gather.6.cloned.1.call-start = ((), (), s32[]{:S(2)}) async-start(), calls=%async_computation | async-start | bytes 1310720 | tf_op jit(solution)/shard_map/all_gather | solution.py:90
  10.2 3.8 %copy-start.5 = (bf16[176,128]{1,0:T(8,128)(2,1)}, bf16[176,128]{1,0:T(8,128)(2,1)S(1)}, u32[]{:S(2)}) copy-start(bf16[176,128]{1,0:T(8,128)(2,1)S(1)} %broadcast_in_dim.110) | copy-start | bytes 135172
  11.0 27.8 %collective-permute-start.1 = (bf16[176,1152]{1,0:T(8,128)(2,1)}, bf16[176,1152]{1,0:T(8,128)(2,1)S(1)}, u32[]{:S(2)}, u32[]{:S(2)}) collective-permute-start(bf16[176,1152]{1,0:T(8,128)(2,1)} %pad_maximum_fusion.5), channel_id=1, source_target_pairs={{0,16},{1,17},{2,18},{3,19},{4,20},{5,21},{6,22},{7,23},{8,24},{9,... | collective-permute-start | bytes 1216520 | tf_op jit(solution)/shard_map/ppermute | solution.py:22
  14.0 25.5 %collective-permute-start = (bf16[176,1152]{1,0:T(8,128)(2,1)}, bf16[176,1152]{1,0:T(8,128)(2,1)}, u32[]{:S(2)}, u32[]{:S(2)}) collective-permute-start(bf16[176,1152]{1,0:T(8,128)(2,1)} %pad_maximum_fusion.5), channel_id=1, source_target_pairs={{0,1},{1,0},{2,3},{3,2},{4,5},{5,4},{6,7},{7,6},{8,9},{9,8},{10,11... | collective-permute-start | bytes 1216520 | tf_op jit(solution)/shard_map/ppermute | solution.py:22
  38.4 7.0 %collective-permute-start.3 = (bf16[64,5120]{1,0:T(8,128)(2,1)S(1)}, bf16[64,5120]{1,0:T(8,128)(2,1)S(1)}, u32[]{:S(2)}, u32[]{:S(2)}) collective-permute-start(bf16[64,5120]{1,0:T(8,128)(2,1)S(1)} %bitcast.192), channel_id=1, source_target_pairs={{0,1},{1,0},{2,3},{3,2},{4,5},{5,4},{6,7},{7,6},{8,9},{9,8},{10,11... | collective-permute-start | bytes 1966088 | tf_op jit(solution)/shard_map/ppermute | solution.py:22
  38.8 2.4 %collective-permute-start.2 = (bf16[176,1152]{1,0:T(8,128)(2,1)S(1)}, bf16[176,1152]{1,0:T(8,128)(2,1)}, u32[]{:S(2)}, u32[]{:S(2)}) collective-permute-start(bf16[176,1152]{1,0:T(8,128)(2,1)S(1)} %collective-permute-done.1), channel_id=1, source_target_pairs={{0,1},{1,0},{2,3},{3,2},{4,5},{5,4},{6,7},{7,6},{8,9},{9,8},{10,11... | collective-permute-start | bytes 1216520 | tf_op jit(solution)/shard_map/ppermute | solution.py:22
  39.5 3.6 %copy-start.6 = (bf16[176,128]{1,0:T(8,128)(2,1)S(1)}, bf16[176,128]{1,0:T(8,128)(2,1)}, u32[]{:S(2)}) copy-start(bf16[176,128]{1,0:T(8,128)(2,1)} %copy-done.5) | copy-start | bytes 135172
  45.4 0.8 copy-start.2
  48.2 0.7 copy-start.9
  52.0 1.3 copy-start.3
  53.1 0.9 copy-start.10
  53.1 2.5 %collective-permute-start.12 = (bf16[4,16,5120]{2,1,0:T(8,128)(2,1)S(1)}, bf16[4,16,5120]{2,1,0:T(8,128)(2,1)S(1)}, u32[]{:S(2)}, u32[]{:S(2)}) collective-permute-start(bf16[4,16,5120]{2,1,0:T(8,128)(2,1)S(1)} %bitcast.201), channel_id=1, source_target_pairs={{0,1},{1,0},{2,3},{3,2},{4,5},{5,4},{6,7},{7,6},{8,9},{9,8},{10,11... | collective-permute-start | bytes 1966088 | tf_op jit(solution)/shard_map/ppermute | solution.py:22
  57.6 35.3 %collective-permute-start.13 = (bf16[16,5120]{1,0:T(8,128)(2,1)}, bf16[16,5120]{1,0:T(8,128)(2,1)}, u32[]{:S(2)}, u32[]{:S(2)}) collective-permute-start(bf16[16,5120]{1,0:T(8,128)(2,1)} %get-tuple-element.27), channel_id=1, source_target_pairs={{0,4},{1,5},{2,6},{3,7},{4,8},{5,9},{6,10},{7,11},{8,12},{9,13},{1... | collective-permute-start | bytes 491528 | tf_op jit(solution)/shard_map/ppermute | solution.py:22
  59.2 34.3 %collective-permute-start.15 = (bf16[16,5120]{1,0:T(8,128)(2,1)}, bf16[16,5120]{1,0:T(8,128)(2,1)}, u32[]{:S(2)}, u32[]{:S(2)}) collective-permute-start(bf16[16,5120]{1,0:T(8,128)(2,1)} %get-tuple-element.28), channel_id=1, source_target_pairs={{0,12},{1,13},{2,14},{3,15},{4,0},{5,1},{6,2},{7,3},{8,4},{9,5},{1... | collective-permute-start | bytes 491528 | tf_op jit(solution)/shard_map/ppermute | solution.py:22
  61.8 32.9 %collective-permute-start.14 = (bf16[16,5120]{1,0:T(8,128)(2,1)S(1)}, bf16[16,5120]{1,0:T(8,128)(2,1)}, u32[]{:S(2)}, u32[]{:S(2)}) collective-permute-start(bf16[16,5120]{1,0:T(8,128)(2,1)S(1)} %get-tuple-element.29), channel_id=1, source_target_pairs={{0,8},{1,9},{2,10},{3,11},{4,12},{5,13},{6,14},{7,15},{8,0},{9,1},... | collective-permute-start | bytes 491528 | tf_op jit(solution)/shard_map/ppermute | solution.py:22
  65.0 64.8 %collective-permute-start.11 = (bf16[176,512]{1,0:T(8,128)(2,1)S(1)}, bf16[176,512]{1,0:T(8,128)(2,1)S(1)}, u32[]{:S(2)}, u32[]{:S(2)}) collective-permute-start(bf16[176,512]{1,0:T(8,128)(2,1)S(1)} %get-tuple-element.19), channel_id=1, source_target_pairs={{0,19},{1,18},{2,17},{3,16},{4,23},{5,22},{6,21},{7,20},{8,27},{9,... | collective-permute-start | bytes 540680 | tf_op jit(solution)/shard_map/ppermute | solution.py:22
  65.1 64.6 %collective-permute-start.10 = (bf16[176,512]{1,0:T(8,128)(2,1)S(1)}, bf16[176,512]{1,0:T(8,128)(2,1)S(1)}, u32[]{:S(2)}, u32[]{:S(2)}) collective-permute-start(bf16[176,512]{1,0:T(8,128)(2,1)S(1)} %get-tuple-element.20), channel_id=1, source_target_pairs={{0,18},{1,19},{2,16},{3,17},{4,22},{5,23},{6,20},{7,21},{8,26},{9,... | collective-permute-start | bytes 540680 | tf_op jit(solution)/shard_map/ppermute | solution.py:22
  92.9 36.7 %collective-permute-start.9 = (bf16[176,512]{1,0:T(8,128)(2,1)S(1)}, bf16[176,512]{1,0:T(8,128)(2,1)S(1)}, u32[]{:S(2)}, u32[]{:S(2)}) collective-permute-start(bf16[176,512]{1,0:T(8,128)(2,1)S(1)} %get-tuple-element.21), channel_id=1, source_target_pairs={{0,3},{1,2},{2,1},{3,0},{4,7},{5,6},{6,5},{7,4},{8,11},{9,10},{10,... | collective-permute-start | bytes 540680 | tf_op jit(solution)/shard_map/ppermute | solution.py:22
  93.5 36.0 %collective-permute-start.8 = (bf16[176,512]{1,0:T(8,128)(2,1)S(1)}, bf16[176,512]{1,0:T(8,128)(2,1)S(1)}, u32[]{:S(2)}, u32[]{:S(2)}) collective-permute-start(bf16[176,512]{1,0:T(8,128)(2,1)S(1)} %get-tuple-element.22), channel_id=1, source_target_pairs={{0,2},{1,3},{2,0},{3,1},{4,6},{5,7},{6,4},{7,5},{8,10},{9,11},{10,... | collective-permute-start | bytes 540680 | tf_op jit(solution)/shard_map/ppermute | solution.py:22
  94.7 12.9 %collective-permute-start.4 = (bf16[176,512]{1,0:T(8,128)(2,1)S(1)}, bf16[176,512]{1,0:T(8,128)(2,1)S(1)}, u32[]{:S(2)}, u32[]{:S(2)}) collective-permute-start(bf16[176,512]{1,0:T(8,128)(2,1)S(1)} %get-tuple-element.26), channel_id=1, source_target_pairs={{0,2},{1,3},{2,0},{3,1},{4,6},{5,7},{6,4},{7,5},{8,10},{9,11},{10,... | collective-permute-start | bytes 540680 | tf_op jit(solution)/shard_map/ppermute | solution.py:22
  107.6 6.7 %collective-permute-start.5 = (bf16[176,512]{1,0:T(8,128)(2,1)S(1)}, bf16[176,512]{1,0:T(8,128)(2,1)S(1)}, u32[]{:S(2)}, u32[]{:S(2)}) collective-permute-start(bf16[176,512]{1,0:T(8,128)(2,1)S(1)} %get-tuple-element.25), channel_id=1, source_target_pairs={{0,3},{1,2},{2,1},{3,0},{4,7},{5,6},{6,5},{7,4},{8,11},{9,10},{10,... | collective-permute-start | bytes 540680 | tf_op jit(solution)/shard_map/ppermute | solution.py:22
  114.3 7.5 %collective-permute-start.6 = (bf16[176,512]{1,0:T(8,128)(2,1)S(1)}, bf16[176,512]{1,0:T(8,128)(2,1)S(1)}, u32[]{:S(2)}, u32[]{:S(2)}) collective-permute-start(bf16[176,512]{1,0:T(8,128)(2,1)S(1)} %get-tuple-element.24), channel_id=1, source_target_pairs={{0,18},{1,19},{2,16},{3,17},{4,22},{5,23},{6,20},{7,21},{8,26},{9,... | collective-permute-start | bytes 540680 | tf_op jit(solution)/shard_map/ppermute | solution.py:22
  121.8 7.5 %collective-permute-start.7 = (bf16[176,512]{1,0:T(8,128)(2,1)S(1)}, bf16[176,512]{1,0:T(8,128)(2,1)S(1)}, u32[]{:S(2)}, u32[]{:S(2)}) collective-permute-start(bf16[176,512]{1,0:T(8,128)(2,1)S(1)} %get-tuple-element.23), channel_id=1, source_target_pairs={{0,19},{1,18},{2,17},{3,16},{4,23},{5,22},{6,21},{7,20},{8,27},{9,... | collective-permute-start | bytes 540680 | tf_op jit(solution)/shard_map/ppermute | solution.py:22
  129.3 1.4 %collective-permute-start.16 = (bf16[16,5120]{1,0:T(8,128)(2,1)S(1)}, bf16[16,5120]{1,0:T(8,128)(2,1)S(1)}, u32[]{:S(2)}, u32[]{:S(2)}) collective-permute-start(bf16[16,5120]{1,0:T(8,128)(2,1)S(1)} %get-tuple-element.4), channel_id=1, source_target_pairs={{0,1},{1,0},{2,3},{3,2},{4,5},{5,4},{6,7},{7,6},{8,9},{9,8},{10,11... | collective-permute-start | bytes 491528 | tf_op jit(solution)/shard_map/ppermute | solution.py:22
  130.0 2.1 %copy-start.4 = (bf16[1,176,4096]{2,1,0:T(8,128)(2,1)}, bf16[1,176,4096]{2,1,0:T(8,128)(2,1)S(1)}, u32[]{:S(2)}) copy-start(bf16[1,176,4096]{2,1,0:T(8,128)(2,1)S(1)} %fusion.47) | copy-start | bytes 4325380
Sparse Core Ops, SparseCore 0:
  10.2 36.9 all-gather.7
  48.7 41.2 all-gather.5

commit v4 on v3

v4 whole, which is shorter than its diff:
```python
import functools
import itertools
import jax
import jax.numpy as jnp
from jax import lax
from jax.experimental import pallas as pl
from jax.experimental.pallas import tpu as pltpu
from jax.sharding import PartitionSpec as P

ADAPTER_SCALE = 2.0
AXES = ("groups", "adapter", "segment", "replica")
LANES = 128
F32 = jnp.float32
BF16 = jnp.bfloat16
VMEM = 32 * 1024 * 1024


def moved(x, to):
    sizes = [lax.axis_size(a) for a in AXES]
    number = {at: i for i, at in enumerate(itertools.product(*map(range, sizes)))}
    pairs = [
        (i, number[tuple(t % s for t, s in zip(to(*at), sizes))]) for at, i in number.items()
    ]
    return lax.ppermute(x, AXES, pairs)


def after(x, *others):
    return lax.optimization_barrier((x, *others))[0]


def rows_by_rows(a, b):
    return lax.dot_general(a, b, (((1,), (1,)), ((), ())), preferred_element_type=F32)


def columns_by_columns(a, b):
    return lax.dot_general(a, b, (((0,), (0,)), ((), ())), preferred_element_type=F32)


def call(kernel, out_shape, flops, operands, scratch=()):
    moved_bytes = sum(x.size * x.dtype.itemsize for x in (*operands, *out_shape))
    return pl.pallas_call(
        kernel,
        out_shape=out_shape,
        scratch_shapes=list(scratch),
        compiler_params=pltpu.CompilerParams(vmem_limit_bytes=VMEM),
        cost_estimate=pl.CostEstimate(flops=flops, bytes_accessed=moved_bytes, transcendentals=0),
    )(*operands)


def adapter_kernel(sizes, *refs):
    tokens, width, value_width, groups, holders, replicas, shard = sizes
    x_ref, slot_ref = refs[0], refs[1]
    g_refs = refs[2 : 2 + groups]
    map_refs = refs[2 + groups : 2 + groups + groups * replicas]
    outs = refs[2 + groups + groups * replicas :]
    sel_ref, own_ref = outs[0], outs[1]
    other_refs = outs[2 : 1 + replicas]
    column_refs = outs[1 + replicas : 1 + replicas + holders]
    down, up = outs[1 + replicas + holders :]
    group, here = lax.axis_index("groups"), lax.axis_index("adapter")
    rows = own_ref.shape[0]
    wide, narrow = width // groups, value_width // groups
    for dr in range(replicas):
        for dg in range(groups):
            ref = map_refs[dr * groups + dg]
            at = lax.rem(group + groups - dg, groups)
            down[pl.ds(dr * rows, rows), pl.ds(pl.multiple_of(at * wide, wide), wide)] = ref[
                :, :wide
            ]
            up[pl.ds(dr * rows, rows), pl.ds(pl.multiple_of(at * narrow, narrow), narrow)] = ref[
                :, wide:
            ]
    half = shard // groups
    for k in range(holders):
        at = lax.rem(here + holders - k, holders) * shard + group * half
        column_refs[k][...] = down[:, pl.ds(pl.multiple_of(at, half), half)]
    slots = slot_ref[...]
    for dg in range(groups):
        keep = g_refs[dg][:, value_width:].astype(F32)[:, :1] == slots
        proj_grad = rows_by_rows(g_refs[dg][:, :value_width], up[...])
        sel_ref[pl.ds(dg * tokens, tokens), :] = jnp.where(keep, proj_grad, 0.0).astype(BF16)
    keep = g_refs[0][:, value_width:].astype(F32)[:, :1] == slots
    in_sel = jnp.where(keep, rows_by_rows(x_ref[...], down[...]), 0.0).astype(BF16)
    grad_sel = sel_ref[pl.ds(0, tokens), :]
    step = 1024
    for at in range(0, width + value_width, step):
        if at < width:
            part = columns_by_columns(grad_sel, x_ref[:, at : at + step])
        else:
            part = columns_by_columns(in_sel, g_refs[0][:, at - width : at - width + step])
        own_ref[:, at : at + step] = part[:rows]
        for dr in range(1, replicas):
            other_refs[dr - 1][:, at : at + step] = part[dr * rows : (dr + 1) * rows].astype(BF16)


def frozen_kernel(sizes, pieces, *refs):
    tokens, value_width, groups, replicas = sizes
    g_refs, sel_ref, refs = refs[:groups], refs[groups], refs[groups + 1 :]
    out_refs = refs[-groups:]
    core = lax.axis_index("replica")
    used, start = 0, 0
    for count in pieces:
        columns, blocks = refs[used], refs[used + 1 : used + 1 + count]
        used += 1 + count
        wide = blocks[0].shape[0]
        for j, block in enumerate(blocks):
            at = 0 if count == 1 else lax.rem(core + replicas - j, replicas) * wide
            for dg in range(groups):
                base = rows_by_rows(g_refs[dg][:, :value_width], block[...]).astype(BF16)
                lora = jnp.dot(
                    sel_ref[pl.ds(dg * tokens, tokens), :],
                    columns[:, pl.ds(pl.multiple_of(at, wide), wide)],
                    preferred_element_type=F32,
                )
                lora = (ADAPTER_SCALE * lora).astype(BF16)
                out_refs[dg][:, pl.ds(pl.multiple_of(start + at, wide), wide)] = (
                    base.astype(F32) + lora.astype(F32)
                ).astype(BF16)
        start += columns.shape[1]


def chip_kernel(*refs):
    own_ref, came_refs, out_refs = refs[0], refs[1], refs[2:]
    rows = out_refs[0].shape[0]
    for k, out in enumerate(out_refs):
        total = own_ref[pl.ds(k * rows, rows), :] + came_refs[pl.ds(k * rows, rows), :].astype(F32)
        out[...] = total.astype(out.dtype)


def total_kernel(*refs):
    total = refs[0][...]
    for ref in refs[1:-1]:
        total = total + ref[...].astype(F32)
    refs[-1][...] = (ADAPTER_SCALE * total).astype(BF16)


def spread_kernel(width, replicas, *refs):
    core = lax.axis_index("replica")
    down_ref, up_ref = refs[replicas:]
    slots = down_ref.shape[0] // replicas
    rank = down_ref.shape[1]
    for dr in range(replicas):
        at = lax.rem(core + replicas - dr, replicas) * slots
        for j in range(slots):
            down_ref[at + j] = refs[dr][j * rank : (j + 1) * rank, :width]
            up_ref[at + j] = refs[dr][j * rank : (j + 1) * rank, width:]


def on_device(
    saved_layer_input,
    value_output_gradient,
    token_adapter_index,
    adapter_slot_index,
    frozen_value_weight,
    adapter_down_weight,
    adapter_up_weight,
):
    inputs = saved_layer_input[0]
    grad_rows = value_output_gradient[0]
    row_ids = token_adapter_index[0, :, 0]
    tokens, width = inputs.shape
    value_width = grad_rows.shape[1]
    adapters = adapter_slot_index.shape[0]
    groups, holders, replicas = (lax.axis_size(a) for a in ("groups", "adapter", "replica"))
    group, here, core = (lax.axis_index(a) for a in ("groups", "adapter", "replica"))
    slots, rank = adapter_down_weight.shape[1:3]
    own_slots = slots // replicas
    rows = own_slots * rank
    frozen = frozen_value_weight[0]
    shard = frozen.shape[0]
    half = shard // groups
    piece = half // replicas
    cols = width + value_width

    wide, narrow = width // groups, value_width // groups
    own = jnp.concatenate(
        [
            lax.dynamic_slice(
                adapter_down_weight[0], (core * own_slots, 0, group * wide), (own_slots, rank, wide)
            ).reshape(rows, wide),
            lax.dynamic_slice(
                adapter_up_weight[0],
                (core * own_slots, 0, group * narrow),
                (own_slots, rank, narrow),
            ).reshape(rows, narrow),
        ],
        axis=1,
    )
    held = [own]
    for k in range(1, holders):
        held.append(moved(own, lambda g, z, s, r: (g, z + k, s, r)))
    held = jnp.concatenate(held, axis=0)
    maps = [held]
    for dg in range(1, groups):
        maps.append(moved(held, lambda g, z, s, r: (g + dg, z, s, r)))
    for dr in range(1, replicas):
        maps += [moved(m, lambda g, z, s, r: (g, z, s, r + dr)) for m in maps[:groups]]
    row_slot = jnp.concatenate(
        [
            ((here - k) % holders) * slots
            + ((core - dr) % replicas) * own_slots
            + jnp.arange(rows, dtype=jnp.int32) // rank
            for dr in range(replicas)
            for k in range(holders)
        ]
    ).astype(F32)[None]

    slot_range = jnp.arange(adapters, dtype=jnp.int32)
    slot_row = jnp.sum(
        jnp.where(row_ids[:, None] == slot_range[None, :], adapter_slot_index[None, :], 0), axis=1
    )
    tagged = jnp.concatenate(
        [grad_rows, jnp.broadcast_to(slot_row[:, None], (tokens, LANES)).astype(BF16)], axis=1
    )
    grads = [tagged]
    for dg in range(1, groups):
        grads.append(moved(tagged, lambda g, z, s, r: (g - dg, z, s, r)))

    mine = lax.dynamic_slice_in_dim(frozen, group * half, half, axis=0)
    ring = [lax.dynamic_slice_in_dim(mine, core * piece, piece, axis=0)]
    blocks = [[mine]]
    for k in range(1, holders):
        ring.append(moved(ring[-1], lambda g, z, s, r: (g, z + 1, s, r)))
        pieces = [ring[k]] + [
            moved(ring[k], lambda g, z, s, r: (g, z, s, r + dr)) for dr in range(1, replicas)
        ]
        if piece % LANES:
            whole = jnp.zeros((half, value_width), BF16)
            for dr in range(replicas):
                at = ((core - dr) % replicas) * piece
                whole = lax.dynamic_update_slice_in_dim(whole, pieces[dr], at, axis=0)
            pieces = [whole]
        blocks.append(pieces)

    sizes = (tokens, width, value_width, groups, holders, replicas, shard)
    kept = replicas * holders * rows
    outs = call(
        functools.partial(adapter_kernel, sizes),
        [jax.ShapeDtypeStruct((groups * tokens, kept), BF16)]
        + [jax.ShapeDtypeStruct((holders * rows, cols), F32)]
        + [jax.ShapeDtypeStruct((holders * rows, cols), BF16)] * (replicas - 1)
        + [jax.ShapeDtypeStruct((kept, half), BF16)] * holders,
        4 * tokens * kept * cols,
        (inputs, row_slot, *grads, *maps),
        [pltpu.VMEM((kept, width), BF16), pltpu.VMEM((kept, value_width), BF16)],
    )
    sel, part, others, columns = outs[0], outs[1], outs[2 : 1 + replicas], outs[1 + replicas :]

    for dr in range(1, replicas - 1):
        part = part + moved(others[dr - 1], lambda g, z, s, r: (g, z, s, r - dr)).astype(F32)
    dr = replicas - 1
    came = moved(others[dr - 1], lambda g, z, s, r: (g, z, s, r - dr))
    chip = call(
        chip_kernel,
        [jax.ShapeDtypeStruct((rows, cols), F32)]
        + [jax.ShapeDtypeStruct((rows, cols), BF16)] * (holders - 1),
        holders * rows * cols,
        (part, came),
    )
    sums = [chip[0]] + [
        moved(chip[k], lambda g, z, s, r: (g, z - k, s, r)) for k in range(1, holders)
    ]
    total = call(
        total_kernel, [jax.ShapeDtypeStruct((rows, cols), BF16)], holders * rows * cols, sums
    )[0]
    totals = [total] + [
        moved(total, lambda g, z, s, r: (g, z, s, r + dr)) for dr in range(1, replicas)
    ]
    down_grad, up_grad = call(
        functools.partial(spread_kernel, width, replicas),
        [
            jax.ShapeDtypeStruct((slots, rank, width), BF16),
            jax.ShapeDtypeStruct((slots, rank, value_width), BF16),
        ],
        0,
        totals,
    )

    batches = [list(range(min(2, holders)))] + [[k] for k in range(2, holders)]
    passed = jnp.zeros((tokens, width), BF16)
    before = ()
    for batch in batches:
        operands = [*grads, sel]
        for k in batch:
            operands += [columns[k], *blocks[k]]
        out = call(
            functools.partial(
                frozen_kernel,
                (tokens, value_width, groups, replicas),
                [len(blocks[k]) for k in batch],
            ),
            [jax.ShapeDtypeStruct((tokens, half * len(batch)), BF16)] * groups,
            2 * groups * tokens * half * len(batch) * (value_width + kept),
            operands,
        )
        got = []
        for dg in range(groups):
            mail = after(out[dg], *before) if before else out[dg]
            got.append(moved(mail, lambda g, z, s, r: (g + dg, z, s - 1, r)))
        before = got
        for dg in range(groups):
            source = (group - dg) % groups
            for j, k in enumerate(batch):
                passed = lax.dynamic_update_slice_in_dim(
                    passed,
                    got[dg][:, j * half : (j + 1) * half],
                    ((here - k) % holders) * shard + source * half,
                    axis=1,
                )
    return passed[None], down_grad[None], up_grad[None]


def solution(mesh):
    placed = (
        P("segment", ("groups", "adapter", "replica"), None),
        P("segment", ("groups", "adapter", "replica"), None),
        P("segment", ("groups", "adapter", "replica"), None),
        P("groups"),
        P("segment", "adapter", None),
        P("segment", "adapter", None, None),
        P("segment", "adapter", None, None),
    )
    return jax.shard_map(
        on_device,
        mesh=mesh,
        in_specs=placed,
        out_specs=(
            P("segment", ("groups", "adapter", "replica"), None),
            P(("groups", "segment"), "adapter", None, None),
            P(("groups", "segment"), "adapter", None, None),
        ),
        check_vma=False,
    )
```

time: 139 us -> 119 us (0.86)
  blocking collectives: 24.4 us -> 0 us
  starting transfers between devices: 18.2 us -> 37.2 us
  between operations: 14.9 us -> 0.83 us
  Pallas kernels: 0 us -> 13 us
  matrix products: 12 us -> 0 us
  other arithmetic: 9.99 us -> 0.88 us
  waiting for transfers between devices: 52.4 us -> 56.4 us
  local copies, waits for them, and re-layouts: 7.02 us -> 10.5 us
    ppermute x17 -> x24, waiting for transfers between devices: 29.5 us -> 56.4 us  [moved(): return lax.ppermute(x, AXES, pairs)]
    all_gather x1 -> x0, blocking collectives: 24.4 us -> none  [on_device(): held = lax.all_gather(own, 'adapter', axis=0, tiled=True)]
    all_gather x2 -> x0, waiting for transfers between devices: 22.9 us -> none  [on_device(): lax.all_gather(lax.dynamic_slice_in_dim(frozen, quarter * piece + c * ste...]
    ppermute x17 -> x24, starting transfers between devices: 18.1 us -> 37.2 us  [moved(): return lax.ppermute(x, AXES, pairs)]
    pallas_call x0 -> x7, Pallas kernels: none -> 13 us  [call(): pl.pallas_call(kernel, out_shape=out_shape, scratch_shapes=list(scratch),...]
    dot_general x7 -> x0, matrix products: 12 us -> none  [the longest x2 5.42 us: on_device(): jnp.einsum('tk,dk->td', grads_all, weights[c], preferred_element_type=F32)]
    concatenate x5 -> x6, other arithmetic: 4.05 us -> 0.05 us  [the longest x1 0.03 us: on_device(): held = jnp.concatenate(held, axis=0)]
    unnamed x22 -> x16, local copies, waits for them, and re-layouts: 1.76 us -> 5.5 us
  transfers between devices with their start and end apart: 19 -> 24, of which waited for: 7 -> 14; matrix products, arithmetic and copies ran while one was open for 17% -> 3% of each run, Pallas kernels for 0% -> 11%
where the time goes in v4:
time: 119 us
  waiting for transfers between devices  56.4 us (47%)
  starting transfers between devices  37.2 us (31%)
  Pallas kernels  13 us (11%)
  local copies, waits for them, and re-layouts  10.5 us (9%)
    ppermute x24, waiting for transfers between devices, moved(): return lax.ppermute(x, AXES, pairs)  56.4 us
    ppermute x24, starting transfers between devices, moved(): return lax.ppermute(x, AXES, pairs)  37.2 us
    pallas_call x7, Pallas kernels, call(): pl.pallas_call(kernel, out_shape=out_shape, scratch_shapes=list(scratch),...  13 us
    unnamed x16, local copies, waits for them, and re-layouts  5.5 us
  transfers between devices with their start and end apart: 24, of which 14 were waited for; matrix products, arithmetic and copies ran while one was open for 3% of the time, Pallas kernels for 11%

profile of v4, /device:TPU:0, one launch (start us, length us, event | category | flops | bytes accessed | tf_op | source)
XLA Modules:
  0.0 118.8 jit_solution(12475386029959437882)
XLA Ops:
  2.4 3.1 %collective-permute-start.1 = (bf16[16,2560]{1,0:T(8,128)(2,1)S(1)}, bf16[16,2560]{1,0:T(8,128)(2,1)S(1)}, u32[]{:S(2)}, u32[]{:S(2)}) collective-permute-start(bf16[16,2560]{1,0:T(8,128)(2,1)S(1)} %pad_maximum_fusion.2), channel_id=1, source_target_pairs={{0,4},{1,5},{2,6},{3,7},{4,8},{5,9},{6,10},{7,11},{8,12},{9,13},{1... | collective-permute-start | bytes 245768 | tf_op jit(solution)/shard_map/ppermute | solution.py:24
  5.5 2.6 %collective-permute-start.2 = (bf16[16,2560]{1,0:T(8,128)(2,1)S(1)}, bf16[16,2560]{1,0:T(8,128)(2,1)S(1)}, u32[]{:S(2)}, u32[]{:S(2)}) collective-permute-start(bf16[16,2560]{1,0:T(8,128)(2,1)S(1)} %pad_maximum_fusion.2), channel_id=1, source_target_pairs={{0,8},{1,9},{2,10},{3,11},{4,12},{5,13},{6,14},{7,15},{8,0},{9,1},... | collective-permute-start | bytes 245768 | tf_op jit(solution)/shard_map/ppermute | solution.py:24
  8.1 1.3 %collective-permute-start.3 = (bf16[16,2560]{1,0:T(8,128)(2,1)S(1)}, bf16[16,2560]{1,0:T(8,128)(2,1)S(1)}, u32[]{:S(2)}, u32[]{:S(2)}) collective-permute-start(bf16[16,2560]{1,0:T(8,128)(2,1)S(1)} %pad_maximum_fusion.2), channel_id=1, source_target_pairs={{0,12},{1,13},{2,14},{3,15},{4,0},{5,1},{6,2},{7,3},{8,4},{9,5},{1... | collective-permute-start | bytes 245768 | tf_op jit(solution)/shard_map/ppermute | solution.py:24
  11.8 1.7 %collective-permute-done.2 = bf16[16,2560]{1,0:T(8,128)(2,1)S(1)} collective-permute-done((bf16[16,2560]{1,0:T(8,128)(2,1)S(1)}, bf16[16,2560]{1,0:T(8,128)(2,1)S(1)}, u32[]{:S(2)}, u32[]{:S(2)}) %collective-permute-start.2) | collective-permute-done | bytes 81952 | tf_op jit(solution)/shard_map/ppermute | solution.py:24
  13.8 1.6 %collective-permute-start.4 = (bf16[64,2560]{1,0:T(8,128)(2,1)S(1)}, bf16[64,2560]{1,0:T(8,128)(2,1)}, u32[]{:S(2)}, u32[]{:S(2)}) collective-permute-start(bf16[64,2560]{1,0:T(8,128)(2,1)S(1)} %pad_maximum_fusion.1.refs_4_), channel_id=1, source_target_pairs={{0,16},{1,17},{2,18},{3,19},{4,20},{5,21},{6,22},{7,23},{8,24},{9,... | collective-permute-start | bytes 983048 | tf_op jit(solution)/shard_map/ppermute | solution.py:24
  16.1 8.5 %collective-permute-done.4.refs_5_ = bf16[64,2560]{1,0:T(8,128)(2,1)} collective-permute-done((bf16[64,2560]{1,0:T(8,128)(2,1)S(1)}, bf16[64,2560]{1,0:T(8,128)(2,1)}, u32[]{:S(2)}, u32[]{:S(2)}) %collective-permute-start.4) | collective-permute-done | bytes 327712 | tf_op jit(solution)/shard_map/ppermute | solution.py:24
  25.5 6.4 %collective-permute-done.refs_3_.refs_1_ = bf16[176,1152]{1,0:T(8,128)(2,1)S(1)} collective-permute-done((bf16[176,1152]{1,0:T(8,128)(2,1)S(1)}, bf16[176,1152]{1,0:T(8,128)(2,1)S(1)}, u32[]{:S(2)}, u32[]{:S(2)}) %collective-permute-start) | collective-permute-done | bytes 405536 | tf_op jit(solution)/shard_map/ppermute | solution.py:24
  31.9 1.4 %copy-done.1 = bf16[1,176,4096]{2,1,0:T(8,128)(2,1)S(1)} copy-done((bf16[1,176,4096]{2,1,0:T(8,128)(2,1)S(1)}, bf16[1,176,4096]{2,1,0:T(8,128)(2,1)}, u32[]{:S(2)}) %copy-start.1) | copy-done | bytes 1441816
  33.2 3.5 %shard_map.94 = (bf16[352,128]{1,0:T(8,128)(2,1)S(1)}, f32[64,5120]{1,0:T(8,128)S(1)}, bf16[64,5120]{1,0:T(8,128)(2,1)}, bf16[128,512]{1,0:T(8,128)(2,1)S(1)}, b...) custom-call(bf16[176,4096]{1,0:T(8,128)(2,1)S(1)} %bitcast.53, ...), custom_call_target="tpu_custom_call" | custom-call | flops 461373440 | bytes 6144512 | tf_op jit(solution)/shard_map/pallas_call | solution.py:41
  38.5 13.6 %collective-permute-start.11 = (bf16[256,1024]{1,0:T(8,128)(2,1)}, bf16[256,1024]{1,0:T(8,128)(2,1)}, u32[]{:S(2)}, u32[]{:S(2)}) collective-permute-start(bf16[256,1024]{1,0:T(8,128)(2,1)} %collective-permute-done.7.refs_6_), channel_id=1, source_target_pairs={{0,4},{1,5},{2,6},{3,7},{4,8},{5,9},{6,10},{7,11},{8,12},{9,13},{1... | collective-permute-start | bytes 1572872 | tf_op jit(solution)/shard_map/ppermute | solution.py:24
  52.1 3.6 %shard_map.95 = (bf16[176,1024]{1,0:T(8,128)(2,1)}, bf16[176,1024]{1,0:T(8,128)(2,1)S(1)}) custom-call(bf16[176,1152]{1,0:T(8,128)(2,1)S(1)} %pad_maximum_fusion.refs_2_.refs_0_, bf16[176,1152]{1,0:T(8,128)(2,1)S(1)} %collective-permute-done.refs_3_.refs_1_, bf16[352,128]{1,0:T(8,128)(2,1)S(1)} %get-tuple-element.26.refs_2_, ...), custom_call_target="tpu_custom_call" | custom-call | flops 830472192 | bytes 3981312 | tf_op jit(solution)/shard_map/pallas_call | solution.py:41
  55.7 1.4 %collective-permute-start.9 = (bf16[176,1024]{1,0:T(8,128)(2,1)}, bf16[176,1024]{1,0:T(8,128)(2,1)}, u32[]{:S(2)}, u32[]{:S(2)}) collective-permute-start(bf16[176,1024]{1,0:T(8,128)(2,1)} %get-tuple-element.29), channel_id=1, source_target_pairs={{0,2},{1,3},{2,0},{3,1},{4,6},{5,7},{6,4},{7,5},{8,10},{9,11},{10,... | collective-permute-start | bytes 1081352 | tf_op jit(solution)/shard_map/ppermute | solution.py:24
  57.1 7.1 %collective-permute-done.11.refs_4_ = bf16[256,1024]{1,0:T(8,128)(2,1)} collective-permute-done((bf16[256,1024]{1,0:T(8,128)(2,1)}, bf16[256,1024]{1,0:T(8,128)(2,1)}, u32[]{:S(2)}, u32[]{:S(2)}) %collective-permute-start.11) | collective-permute-done | bytes 524320 | tf_op jit(solution)/shard_map/ppermute | solution.py:24
  64.2 2.5 %collective-permute-start.15 = (bf16[256,1024]{1,0:T(8,128)(2,1)}, bf16[256,1024]{1,0:T(8,128)(2,1)}, u32[]{:S(2)}, u32[]{:S(2)}) collective-permute-start(bf16[256,1024]{1,0:T(8,128)(2,1)} %collective-permute-done.11.refs_4_), channel_id=1, source_target_pairs={{0,4},{1,5},{2,6},{3,7},{4,8},{5,9},{6,10},{7,11},{8,12},{9,13},{1... | collective-permute-start | bytes 1572872 | tf_op jit(solution)/shard_map/ppermute | solution.py:24
  66.7 2.3 %collective-permute-start.10 = (bf16[176,1024]{1,0:T(8,128)(2,1)S(1)}, bf16[176,1024]{1,0:T(8,128)(2,1)S(1)}, u32[]{:S(2)}, u32[]{:S(2)}) collective-permute-start(bf16[176,1024]{1,0:T(8,128)(2,1)S(1)} %get-tuple-element.30), channel_id=1, source_target_pairs={{0,18},{1,19},{2,16},{3,17},{4,22},{5,23},{6,20},{7,21},{8,26},{9,... | collective-permute-start | bytes 1081352 | tf_op jit(solution)/shard_map/ppermute | solution.py:24
  69.1 1.3 %copy-done.3 = f32[64,5120]{1,0:T(8,128)S(1)} copy-done((f32[64,5120]{1,0:T(8,128)S(1)}, f32[64,5120]{1,0:T(8,128)}, u32[]{:S(2)}) %copy-start.3) | copy-done | bytes 1310744
  70.4 1.2 %shard_map.98 = (f32[16,5120]{1,0:T(8,128)S(1)}, bf16[16,5120]{1,0:T(8,128)(2,1)S(1)}, bf16[16,5120]{1,0:T(8,128)(2,1)S(1)}, bf16[16,5120]{1,0:T(8,128)(2,1)S(1)}) custom-call(f32[64,5120]{1,0:T(8,128)S(1)} %copy-done.3, bf16[64,5120]{1,0:T(8,128)(2,1)} %collective-permute-done.19.refs_1_), custom_call_target="tpu_custom_call" | custom-call | flops 327680 | bytes 2785280 | tf_op jit(solution)/shard_map/pallas_call | solution.py:41
  71.6 1.4 %collective-permute-start.20 = (bf16[16,5120]{1,0:T(8,128)(2,1)S(1)}, bf16[16,5120]{1,0:T(8,128)(2,1)S(1)}, u32[]{:S(2)}, u32[]{:S(2)}) collective-permute-start(bf16[16,5120]{1,0:T(8,128)(2,1)S(1)} %get-tuple-element.44), channel_id=1, source_target_pairs={{0,12},{1,13},{2,14},{3,15},{4,0},{5,1},{6,2},{7,3},{8,4},{9,5},{1... | collective-permute-start | bytes 491528 | tf_op jit(solution)/shard_map/ppermute | solution.py:24
  75.5 1.9 %collective-permute-done.10 = bf16[176,1024]{1,0:T(8,128)(2,1)S(1)} collective-permute-done((bf16[176,1024]{1,0:T(8,128)(2,1)S(1)}, bf16[176,1024]{1,0:T(8,128)(2,1)S(1)}, u32[]{:S(2)}, u32[]{:S(2)}) %collective-permute-start.10) | collective-permute-done | bytes 360480 | tf_op jit(solution)/shard_map/ppermute | solution.py:24
  77.9 3.4 %collective-permute-done.15.refs_4_ = bf16[256,1024]{1,0:T(8,128)(2,1)} collective-permute-done((bf16[256,1024]{1,0:T(8,128)(2,1)}, bf16[256,1024]{1,0:T(8,128)(2,1)}, u32[]{:S(2)}, u32[]{:S(2)}) %collective-permute-start.15) | collective-permute-done | bytes 524320 | tf_op jit(solution)/shard_map/ppermute | solution.py:24
  81.2 2.1 %collective-permute-done.20.refs_1_ = bf16[16,5120]{1,0:T(8,128)(2,1)S(1)} collective-permute-done((bf16[16,5120]{1,0:T(8,128)(2,1)S(1)}, bf16[16,5120]{1,0:T(8,128)(2,1)S(1)}, u32[]{:S(2)}, u32[]{:S(2)}) %collective-permute-start.20) | collective-permute-done | bytes 163872 | tf_op jit(solution)/shard_map/ppermute | solution.py:24
  83.3 10.5 %collective-permute-done.21.refs_2_ = bf16[16,5120]{1,0:T(8,128)(2,1)S(1)} collective-permute-done((bf16[16,5120]{1,0:T(8,128)(2,1)S(1)}, bf16[16,5120]{1,0:T(8,128)(2,1)S(1)}, u32[]{:S(2)}, u32[]{:S(2)}) %collective-permute-start.21) | collective-permute-done | bytes 163872 | tf_op jit(solution)/shard_map/ppermute | solution.py:24
  94.1 1.9 %shard_map.96 = (bf16[176,512]{1,0:T(8,128)(2,1)S(1)}, bf16[176,512]{1,0:T(8,128)(2,1)S(1)}) custom-call(bf16[176,1152]{1,0:T(8,128)(2,1)S(1)} %pad_maximum_fusion.refs_2_.refs_0_, bf16[176,1152]{1,0:T(8,128)(2,1)S(1)} %collective-permute-done.refs_3_.refs_1_, bf16[352,128]{1,0:T(8,128)(2,1)S(1)} %get-tuple-element.26.refs_2_, ...), custom_call_target="tpu_custom_call" | custom-call | flops 415236096 | bytes 2441216 | tf_op jit(solution)/shard_map/pallas_call | solution.py:41
  96.0 1.5 %collective-permute-start.13 = (bf16[176,512]{1,0:T(8,128)(2,1)S(1)}, bf16[176,512]{1,0:T(8,128)(2,1)S(1)}, u32[]{:S(2)}, u32[]{:S(2)}) collective-permute-start(bf16[176,512]{1,0:T(8,128)(2,1)S(1)} %get-tuple-element.33), channel_id=1, source_target_pairs={{0,2},{1,3},{2,0},{3,1},{4,6},{5,7},{6,4},{7,5},{8,10},{9,11},{10,... | collective-permute-start | bytes 540680 | tf_op jit(solution)/shard_map/ppermute | solution.py:24
  97.5 1.6 %collective-permute-start.14 = (bf16[176,512]{1,0:T(8,128)(2,1)S(1)}, bf16[176,512]{1,0:T(8,128)(2,1)S(1)}, u32[]{:S(2)}, u32[]{:S(2)}) collective-permute-start(bf16[176,512]{1,0:T(8,128)(2,1)S(1)} %get-tuple-element.35), channel_id=1, source_target_pairs={{0,18},{1,19},{2,16},{3,17},{4,22},{5,23},{6,20},{7,21},{8,26},{9,... | collective-permute-start | bytes 540680 | tf_op jit(solution)/shard_map/ppermute | solution.py:24
  99.8 3.6 %collective-permute-done.13 = bf16[176,512]{1,0:T(8,128)(2,1)S(1)} collective-permute-done((bf16[176,512]{1,0:T(8,128)(2,1)S(1)}, bf16[176,512]{1,0:T(8,128)(2,1)S(1)}, u32[]{:S(2)}, u32[]{:S(2)}) %collective-permute-start.13) | collective-permute-done | bytes 180256 | tf_op jit(solution)/shard_map/ppermute | solution.py:24
  103.4 1.9 %shard_map.97 = (bf16[176,512]{1,0:T(8,128)(2,1)S(1)}, bf16[176,512]{1,0:T(8,128)(2,1)S(1)}) custom-call(bf16[176,1152]{1,0:T(8,128)(2,1)S(1)} %pad_maximum_fusion.refs_2_.refs_0_, bf16[176,1152]{1,0:T(8,128)(2,1)S(1)} %collective-permute-done.refs_3_.refs_1_, bf16[352,128]{1,0:T(8,128)(2,1)S(1)} %get-tuple-element.26.refs_2_, ...), custom_call_target="tpu_custom_call" | custom-call | flops 415236096 | bytes 2441216 | tf_op jit(solution)/shard_map/pallas_call | solution.py:41
  105.4 2.3 %collective-permute-done.14 = bf16[176,512]{1,0:T(8,128)(2,1)S(1)} collective-permute-done((bf16[176,512]{1,0:T(8,128)(2,1)S(1)}, bf16[176,512]{1,0:T(8,128)(2,1)S(1)}, u32[]{:S(2)}, u32[]{:S(2)}) %collective-permute-start.14) | collective-permute-done | bytes 180256 | tf_op jit(solution)/shard_map/ppermute | solution.py:24
  107.7 1.5 %collective-permute-start.17 = (bf16[176,512]{1,0:T(8,128)(2,1)S(1)}, bf16[176,512]{1,0:T(8,128)(2,1)S(1)}, u32[]{:S(2)}, u32[]{:S(2)}) collective-permute-start(bf16[176,512]{1,0:T(8,128)(2,1)S(1)} %get-tuple-element.38), channel_id=1, source_target_pairs={{0,2},{1,3},{2,0},{3,1},{4,6},{5,7},{6,4},{7,5},{8,10},{9,11},{10,... | collective-permute-start | bytes 540680 | tf_op jit(solution)/shard_map/ppermute | solution.py:24
  109.8 5.3 %collective-permute-done.17 = bf16[176,512]{1,0:T(8,128)(2,1)S(1)} collective-permute-done((bf16[176,512]{1,0:T(8,128)(2,1)S(1)}, bf16[176,512]{1,0:T(8,128)(2,1)S(1)}, u32[]{:S(2)}, u32[]{:S(2)}) %collective-permute-start.17) | collective-permute-done | bytes 180256 | tf_op jit(solution)/shard_map/ppermute | solution.py:24
  115.2 2.5 %collective-permute-done.18 = bf16[176,512]{1,0:T(8,128)(2,1)S(1)} collective-permute-done((bf16[176,512]{1,0:T(8,128)(2,1)S(1)}, bf16[176,512]{1,0:T(8,128)(2,1)S(1)}, u32[]{:S(2)}, u32[]{:S(2)}) %collective-permute-start.18) | collective-permute-done | bytes 180256 | tf_op jit(solution)/shard_map/ppermute | solution.py:24
  117.7 1.1 copy-done.6
  (64 shorter events, 12.5 us)
Async XLA Ops:
  0.6 8.8 %copy-start = (bf16[1,1024,1024]{2,1,0:T(8,128)(2,1)S(1)}, bf16[1,1024,1024]{2,1,0:T(8,128)(2,1)}, u32[]{:S(2)}) copy-start(bf16[1,1024,1024]{2,1,0:T(8,128)(2,1)} %param.11) | copy-start | bytes 6291460
  0.6 14.8 %copy-start.7 = (bf16[1,176,1024]{2,1,0:T(8,128)(2,1)S(1)}, bf16[1,176,1024]{2,1,0:T(8,128)(2,1)}, u32[]{:S(2)}) copy-start(bf16[1,176,1024]{2,1,0:T(8,128)(2,1)} %param.8) | copy-start | bytes 1081348
  2.4 9.4 %collective-permute-start.1 = (bf16[16,2560]{1,0:T(8,128)(2,1)S(1)}, bf16[16,2560]{1,0:T(8,128)(2,1)S(1)}, u32[]{:S(2)}, u32[]{:S(2)}) collective-permute-start(bf16[16,2560]{1,0:T(8,128)(2,1)S(1)} %pad_maximum_fusion.2), channel_id=1, source_target_pairs={{0,4},{1,5},{2,6},{3,7},{4,8},{5,9},{6,10},{7,11},{8,12},{9,13},{1... | collective-permute-start | bytes 245768 | tf_op jit(solution)/shard_map/ppermute | solution.py:24
  5.5 8.1 %collective-permute-start.2 = (bf16[16,2560]{1,0:T(8,128)(2,1)S(1)}, bf16[16,2560]{1,0:T(8,128)(2,1)S(1)}, u32[]{:S(2)}, u32[]{:S(2)}) collective-permute-start(bf16[16,2560]{1,0:T(8,128)(2,1)S(1)} %pad_maximum_fusion.2), channel_id=1, source_target_pairs={{0,8},{1,9},{2,10},{3,11},{4,12},{5,13},{6,14},{7,15},{8,0},{9,1},... | collective-permute-start | bytes 245768 | tf_op jit(solution)/shard_map/ppermute | solution.py:24
  8.1 5.7 %collective-permute-start.3 = (bf16[16,2560]{1,0:T(8,128)(2,1)S(1)}, bf16[16,2560]{1,0:T(8,128)(2,1)S(1)}, u32[]{:S(2)}, u32[]{:S(2)}) collective-permute-start(bf16[16,2560]{1,0:T(8,128)(2,1)S(1)} %pad_maximum_fusion.2), channel_id=1, source_target_pairs={{0,12},{1,13},{2,14},{3,15},{4,0},{5,1},{6,2},{7,3},{8,4},{9,5},{1... | collective-permute-start | bytes 245768 | tf_op jit(solution)/shard_map/ppermute | solution.py:24
  10.3 15.0 %collective-permute-start.7 = (bf16[256,1024]{1,0:T(8,128)(2,1)}, bf16[256,1024]{1,0:T(8,128)(2,1)}, u32[]{:S(2)}, u32[]{:S(2)}) collective-permute-start(bf16[256,1024]{1,0:T(8,128)(2,1)} %dynamic-slice_bitcast_fusion.1), channel_id=1, source_target_pairs={{0,4},{1,5},{2,6},{3,7},{4,8},{5,9},{6,10},{7,11},{8,12},{9,13},{1... | collective-permute-start | bytes 1572872 | tf_op jit(solution)/shard_map/ppermute | solution.py:24
  13.8 10.8 %collective-permute-start.4 = (bf16[64,2560]{1,0:T(8,128)(2,1)S(1)}, bf16[64,2560]{1,0:T(8,128)(2,1)}, u32[]{:S(2)}, u32[]{:S(2)}) collective-permute-start(bf16[64,2560]{1,0:T(8,128)(2,1)S(1)} %pad_maximum_fusion.1.refs_4_), channel_id=1, source_target_pairs={{0,16},{1,17},{2,18},{3,19},{4,20},{5,21},{6,22},{7,23},{8,24},{9,... | collective-permute-start | bytes 983048 | tf_op jit(solution)/shard_map/ppermute | solution.py:24
  15.5 16.4 %collective-permute-start = (bf16[176,1152]{1,0:T(8,128)(2,1)S(1)}, bf16[176,1152]{1,0:T(8,128)(2,1)S(1)}, u32[]{:S(2)}, u32[]{:S(2)}) collective-permute-start(bf16[176,1152]{1,0:T(8,128)(2,1)S(1)} %pad_maximum_fusion.refs_2_.refs_0_), channel_id=1, source_target_pairs={{0,16},{1,17},{2,18},{3,19},{4,20},{5,21},{6,22},{7,23},{8,24},{9,... | collective-permute-start | bytes 1216520 | tf_op jit(solution)/shard_map/ppermute | solution.py:24
  16.1 15.8 %collective-permute-start.5 = (bf16[64,2560]{1,0:T(8,128)(2,1)S(1)}, bf16[64,2560]{1,0:T(8,128)(2,1)}, u32[]{:S(2)}, u32[]{:S(2)}) collective-permute-start(bf16[64,2560]{1,0:T(8,128)(2,1)S(1)} %pad_maximum_fusion.1.refs_4_), channel_id=1, source_target_pairs={{0,1},{1,0},{2,3},{3,2},{4,5},{5,4},{6,7},{7,6},{8,9},{9,8},{10,11... | collective-permute-start | bytes 983048 | tf_op jit(solution)/shard_map/ppermute | solution.py:24
  24.6 7.3 %collective-permute-start.6 = (bf16[64,2560]{1,0:T(8,128)(2,1)}, bf16[64,2560]{1,0:T(8,128)(2,1)}, u32[]{:S(2)}, u32[]{:S(2)}) collective-permute-start(bf16[64,2560]{1,0:T(8,128)(2,1)} %collective-permute-done.4.refs_5_), channel_id=1, source_target_pairs={{0,1},{1,0},{2,3},{3,2},{4,5},{5,4},{6,7},{7,6},{8,9},{9,8},{10,11... | collective-permute-start | bytes 983048 | tf_op jit(solution)/shard_map/ppermute | solution.py:24
  25.4 26.7 %collective-permute-start.8 = (bf16[256,1024]{1,0:T(8,128)(2,1)}, bf16[256,1024]{1,0:T(8,128)(2,1)}, u32[]{:S(2)}, u32[]{:S(2)}) collective-permute-start(bf16[256,1024]{1,0:T(8,128)(2,1)} %collective-permute-done.7.refs_6_), channel_id=1, source_target_pairs={{0,1},{1,0},{2,3},{3,2},{4,5},{5,4},{6,7},{7,6},{8,9},{9,8},{10,11... | collective-permute-start | bytes 1572872 | tf_op jit(solution)/shard_map/ppermute | solution.py:24
  31.9 1.4 %copy-start.1 = (bf16[1,176,4096]{2,1,0:T(8,128)(2,1)S(1)}, bf16[1,176,4096]{2,1,0:T(8,128)(2,1)}, u32[]{:S(2)}) copy-start(bf16[1,176,4096]{2,1,0:T(8,128)(2,1)} %param.7) | copy-start | bytes 4325380
  36.8 1.1 copy-start.2
  37.8 0.7 copy-start.4
  38.5 30.6 %collective-permute-start.19 = (bf16[64,5120]{1,0:T(8,128)(2,1)}, bf16[64,5120]{1,0:T(8,128)(2,1)}, u32[]{:S(2)}, u32[]{:S(2)}) collective-permute-start(bf16[64,5120]{1,0:T(8,128)(2,1)} %get-tuple-element.42), channel_id=1, source_target_pairs={{0,1},{1,0},{2,3},{3,2},{4,5},{5,4},{6,7},{7,6},{8,9},{9,8},{10,11... | collective-permute-start | bytes 1966088 | tf_op jit(solution)/shard_map/ppermute | solution.py:24
  38.5 25.7 %collective-permute-start.11 = (bf16[256,1024]{1,0:T(8,128)(2,1)}, bf16[256,1024]{1,0:T(8,128)(2,1)}, u32[]{:S(2)}, u32[]{:S(2)}) collective-permute-start(bf16[256,1024]{1,0:T(8,128)(2,1)} %collective-permute-done.7.refs_6_), channel_id=1, source_target_pairs={{0,4},{1,5},{2,6},{3,7},{4,8},{5,9},{6,10},{7,11},{8,12},{9,13},{1... | collective-permute-start | bytes 1572872 | tf_op jit(solution)/shard_map/ppermute | solution.py:24
  55.7 17.3 %collective-permute-start.9 = (bf16[176,1024]{1,0:T(8,128)(2,1)}, bf16[176,1024]{1,0:T(8,128)(2,1)}, u32[]{:S(2)}, u32[]{:S(2)}) collective-permute-start(bf16[176,1024]{1,0:T(8,128)(2,1)} %get-tuple-element.29), channel_id=1, source_target_pairs={{0,2},{1,3},{2,0},{3,1},{4,6},{5,7},{6,4},{7,5},{8,10},{9,11},{10,... | collective-permute-start | bytes 1081352 | tf_op jit(solution)/shard_map/ppermute | solution.py:24
  64.2 17.0 %collective-permute-start.15 = (bf16[256,1024]{1,0:T(8,128)(2,1)}, bf16[256,1024]{1,0:T(8,128)(2,1)}, u32[]{:S(2)}, u32[]{:S(2)}) collective-permute-start(bf16[256,1024]{1,0:T(8,128)(2,1)} %collective-permute-done.11.refs_4_), channel_id=1, source_target_pairs={{0,4},{1,5},{2,6},{3,7},{4,8},{5,9},{6,10},{7,11},{8,12},{9,13},{1... | collective-permute-start | bytes 1572872 | tf_op jit(solution)/shard_map/ppermute | solution.py:24
  66.7 10.7 %collective-permute-start.10 = (bf16[176,1024]{1,0:T(8,128)(2,1)S(1)}, bf16[176,1024]{1,0:T(8,128)(2,1)S(1)}, u32[]{:S(2)}, u32[]{:S(2)}) collective-permute-start(bf16[176,1024]{1,0:T(8,128)(2,1)S(1)} %get-tuple-element.30), channel_id=1, source_target_pairs={{0,18},{1,19},{2,16},{3,17},{4,22},{5,23},{6,20},{7,21},{8,26},{9,... | collective-permute-start | bytes 1081352 | tf_op jit(solution)/shard_map/ppermute | solution.py:24
  69.1 25.0 %collective-permute-start.12 = (bf16[256,1024]{1,0:T(8,128)(2,1)}, bf16[256,1024]{1,0:T(8,128)(2,1)S(1)}, u32[]{:S(2)}, u32[]{:S(2)}) collective-permute-start(bf16[256,1024]{1,0:T(8,128)(2,1)} %collective-permute-done.11.refs_4_), channel_id=1, source_target_pairs={{0,1},{1,0},{2,3},{3,2},{4,5},{5,4},{6,7},{7,6},{8,9},{9,8},{10,11... | collective-permute-start | bytes 1572872 | tf_op jit(solution)/shard_map/ppermute | solution.py:24
  69.1 1.3 %copy-start.3 = (f32[64,5120]{1,0:T(8,128)S(1)}, f32[64,5120]{1,0:T(8,128)}, u32[]{:S(2)}) copy-start(f32[64,5120]{1,0:T(8,128)} %copy-done.2) | copy-start | bytes 3932164
  71.6 11.7 %collective-permute-start.20 = (bf16[16,5120]{1,0:T(8,128)(2,1)S(1)}, bf16[16,5120]{1,0:T(8,128)(2,1)S(1)}, u32[]{:S(2)}, u32[]{:S(2)}) collective-permute-start(bf16[16,5120]{1,0:T(8,128)(2,1)S(1)} %get-tuple-element.44), channel_id=1, source_target_pairs={{0,12},{1,13},{2,14},{3,15},{4,0},{5,1},{6,2},{7,3},{8,4},{9,5},{1... | collective-permute-start | bytes 491528 | tf_op jit(solution)/shard_map/ppermute | solution.py:24
  73.0 21.1 %copy-start.5 = (bf16[128,512]{1,0:T(8,128)(2,1)S(1)}, bf16[128,512]{1,0:T(8,128)(2,1)}, u32[]{:S(2)}) copy-start(bf16[128,512]{1,0:T(8,128)(2,1)} %copy-done.4) | copy-start | bytes 393220
  73.0 20.8 %collective-permute-start.21 = (bf16[16,5120]{1,0:T(8,128)(2,1)S(1)}, bf16[16,5120]{1,0:T(8,128)(2,1)S(1)}, u32[]{:S(2)}, u32[]{:S(2)}) collective-permute-start(bf16[16,5120]{1,0:T(8,128)(2,1)S(1)} %get-tuple-element.45), channel_id=1, source_target_pairs={{0,8},{1,9},{2,10},{3,11},{4,12},{5,13},{6,14},{7,15},{8,0},{9,1},... | collective-permute-start | bytes 491528 | tf_op jit(solution)/shard_map/ppermute | solution.py:24
  77.4 16.5 %collective-permute-start.22 = (bf16[16,5120]{1,0:T(8,128)(2,1)S(1)}, bf16[16,5120]{1,0:T(8,128)(2,1)S(1)}, u32[]{:S(2)}, u32[]{:S(2)}) collective-permute-start(bf16[16,5120]{1,0:T(8,128)(2,1)S(1)} %get-tuple-element.46), channel_id=1, source_target_pairs={{0,4},{1,5},{2,6},{3,7},{4,8},{5,9},{6,10},{7,11},{8,12},{9,13},{1... | collective-permute-start | bytes 491528 | tf_op jit(solution)/shard_map/ppermute | solution.py:24
  81.2 22.2 %collective-permute-start.16 = (bf16[256,1024]{1,0:T(8,128)(2,1)}, bf16[256,1024]{1,0:T(8,128)(2,1)S(1)}, u32[]{:S(2)}, u32[]{:S(2)}) collective-permute-start(bf16[256,1024]{1,0:T(8,128)(2,1)} %collective-permute-done.15.refs_4_), channel_id=1, source_target_pairs={{0,1},{1,0},{2,3},{3,2},{4,5},{5,4},{6,7},{7,6},{8,9},{9,8},{10,11... | collective-permute-start | bytes 1572872 | tf_op jit(solution)/shard_map/ppermute | solution.py:24
  93.9 5.1 %collective-permute-start.23 = (bf16[16,5120]{1,0:T(8,128)(2,1)S(1)}, bf16[16,5120]{1,0:T(8,128)(2,1)S(1)}, u32[]{:S(2)}, u32[]{:S(2)}) collective-permute-start(bf16[16,5120]{1,0:T(8,128)(2,1)S(1)} %shard_map.99.refs_0_), channel_id=1, source_target_pairs={{0,1},{1,0},{2,3},{3,2},{4,5},{5,4},{6,7},{7,6},{8,9},{9,8},{10,11... | collective-permute-start | bytes 491528 | tf_op jit(solution)/shard_map/ppermute | solution.py:24
  96.0 7.4 %collective-permute-start.13 = (bf16[176,512]{1,0:T(8,128)(2,1)S(1)}, bf16[176,512]{1,0:T(8,128)(2,1)S(1)}, u32[]{:S(2)}, u32[]{:S(2)}) collective-permute-start(bf16[176,512]{1,0:T(8,128)(2,1)S(1)} %get-tuple-element.33), channel_id=1, source_target_pairs={{0,2},{1,3},{2,0},{3,1},{4,6},{5,7},{6,4},{7,5},{8,10},{9,11},{10,... | collective-permute-start | bytes 540680 | tf_op jit(solution)/shard_map/ppermute | solution.py:24
  97.5 10.2 %collective-permute-start.14 = (bf16[176,512]{1,0:T(8,128)(2,1)S(1)}, bf16[176,512]{1,0:T(8,128)(2,1)S(1)}, u32[]{:S(2)}, u32[]{:S(2)}) collective-permute-start(bf16[176,512]{1,0:T(8,128)(2,1)S(1)} %get-tuple-element.35), channel_id=1, source_target_pairs={{0,18},{1,19},{2,16},{3,17},{4,22},{5,23},{6,20},{7,21},{8,26},{9,... | collective-permute-start | bytes 540680 | tf_op jit(solution)/shard_map/ppermute | solution.py:24
  107.7 7.5 %collective-permute-start.17 = (bf16[176,512]{1,0:T(8,128)(2,1)S(1)}, bf16[176,512]{1,0:T(8,128)(2,1)S(1)}, u32[]{:S(2)}, u32[]{:S(2)}) collective-permute-start(bf16[176,512]{1,0:T(8,128)(2,1)S(1)} %get-tuple-element.38), channel_id=1, source_target_pairs={{0,2},{1,3},{2,0},{3,1},{4,6},{5,7},{6,4},{7,5},{8,10},{9,11},{10,... | collective-permute-start | bytes 540680 | tf_op jit(solution)/shard_map/ppermute | solution.py:24
  109.2 8.5 %collective-permute-start.18 = (bf16[176,512]{1,0:T(8,128)(2,1)S(1)}, bf16[176,512]{1,0:T(8,128)(2,1)S(1)}, u32[]{:S(2)}, u32[]{:S(2)}) collective-permute-start(bf16[176,512]{1,0:T(8,128)(2,1)S(1)} %get-tuple-element.40), channel_id=1, source_target_pairs={{0,18},{1,19},{2,16},{3,17},{4,22},{5,23},{6,20},{7,21},{8,26},{9,... | collective-permute-start | bytes 540680 | tf_op jit(solution)/shard_map/ppermute | solution.py:24
  117.7 1.1 copy-start.6

commit v5 on v4

v5 whole, which is shorter than its diff:
```python
import functools
import itertools
import jax
import jax.numpy as jnp
from jax import lax
from jax.experimental import pallas as pl
from jax.experimental.pallas import tpu as pltpu
from jax.sharding import PartitionSpec as P

ADAPTER_SCALE = 2.0
AXES = ("groups", "adapter", "segment", "replica")
LANES = 128
F32 = jnp.float32
BF16 = jnp.bfloat16
MIB = 1024 * 1024


def moved(x, to):
    sizes = [lax.axis_size(a) for a in AXES]
    number = {at: i for i, at in enumerate(itertools.product(*map(range, sizes)))}
    pairs = [
        (i, number[tuple(t % s for t, s in zip(to(*at), sizes))]) for at, i in number.items()
    ]
    return lax.ppermute(x, AXES, pairs)


def after(x, *others):
    return lax.optimization_barrier((x, *others))[0]


def rows_by_rows(a, b):
    return lax.dot_general(a, b, (((1,), (1,)), ((), ())), preferred_element_type=F32)


def columns_by_columns(a, b):
    return lax.dot_general(a, b, (((0,), (0,)), ((), ())), preferred_element_type=F32)


def call(kernel, out_shape, operands, scratch=()):
    held = sum(x.size * x.dtype.itemsize for x in (*operands, *out_shape, *scratch))
    return pl.pallas_call(
        kernel,
        out_shape=out_shape,
        scratch_shapes=[pltpu.VMEM(x.shape, x.dtype) for x in scratch],
        compiler_params=pltpu.CompilerParams(vmem_limit_bytes=2 * held + 4 * MIB),
        cost_estimate=pl.CostEstimate(flops=1000, bytes_accessed=1000, transcendentals=0),
    )(*operands)


def slots_of(tagged_ref):
    return tagged_ref[:, -LANES:].astype(F32)[:, :1]


def tag_kernel(g_ref, name_ref, slot_ref, out_ref):
    out_ref[:, :-LANES] = g_ref[...]
    tokens, adapters = g_ref.shape[0], slot_ref.shape[1]
    named = name_ref[...] == lax.broadcasted_iota(jnp.int32, (tokens, adapters), 1)
    slot = jnp.sum(jnp.where(named, slot_ref[...], 0).astype(F32), axis=1, keepdims=True)
    out_ref[:, -LANES:] = jnp.broadcast_to(slot, (tokens, LANES)).astype(BF16)


def own_kernel(sizes, down_ref, up_ref, out_ref):
    groups, holders, shard = sizes
    half = shard // groups
    rank = down_ref.shape[1]
    slots = out_ref.shape[0] // rank
    first = lax.axis_index("replica") * slots
    for j in range(slots):
        to = pl.ds(j * rank, rank)
        for z in range(holders):
            at = pl.multiple_of(z * shard + lax.axis_index("groups") * half, half)
            out_ref[to, z * half : (z + 1) * half] = down_ref[first + j, :, pl.ds(at, half)]
        out_ref[to, holders * half :] = up_ref[first + j]


def adapter_kernel(sizes, *refs):
    groups, holders, replicas, shard = sizes
    x_ref, g_ref, slot_ref, sel_ref = refs[:4]
    map_refs, refs = refs[4 : 4 + groups * replicas], refs[4 + groups * replicas :]
    own_ref, other_refs, down = refs[0], refs[1:-1], refs[-1]
    group = lax.axis_index("groups")
    tokens, width = x_ref.shape
    rows, cols = own_ref.shape
    half = shard // groups
    for dg in range(groups):
        first = lax.rem(group + groups - dg, groups) * half
        for dr in range(replicas):
            for z in range(holders):
                at = pl.multiple_of(first + z * shard, half)
                down[pl.ds(dr * rows, rows), pl.ds(at, half)] = map_refs[dg * replicas + dr][
                    :, z * half : (z + 1) * half
                ]
    keep = slots_of(g_ref) == slot_ref[...]
    in_sel = jnp.where(keep, rows_by_rows(x_ref[...], down[...]), 0.0).astype(BF16)
    grad_sel = sel_ref[pl.ds(0, tokens), :]
    step, split = 1024, cols // 2
    for at in range(0, cols, step):
        if at < width:
            part = columns_by_columns(grad_sel, x_ref[:, at : at + step])
        else:
            part = columns_by_columns(in_sel, g_ref[:, at - width : at - width + step])
        own_ref[:, at : at + step] = part[:rows]
        for dr in range(1, replicas):
            sent = part[dr * rows : (dr + 1) * rows].astype(BF16)
            for j in range(0, step, LANES):
                ref, to = other_refs[2 * dr - 2 + (at + j) // split], (at + j) % split
                ref[:, to : to + LANES] = sent[:, j : j + LANES]


def frozen_kernel(sizes, k, count, *refs):
    tokens, groups, holders, replicas = sizes
    g_refs, refs = refs[:groups], refs[groups:]
    down_refs, refs = refs[:replicas], refs[replicas:]
    core, here = lax.axis_index("replica"), lax.axis_index("adapter")
    if k == 0:
        slot_ref, up_refs, refs = refs[0], refs[1 : 1 + replicas], refs[1 + replicas :]
        sel_ref = refs[-1]
        out_refs = refs[-1 - groups : -1]
        rows = up_refs[0].shape[0]
        for dg in range(groups):
            for dr in range(replicas):
                keep = slots_of(g_refs[dg]) == slot_ref[:, dr * rows : (dr + 1) * rows]
                proj_grad = rows_by_rows(g_refs[dg][:, :-LANES], up_refs[dr][...])
                sel_ref[pl.ds(dg * tokens, tokens), dr * rows : (dr + 1) * rows] = jnp.where(
                    keep, proj_grad, 0.0
                ).astype(BF16)
    else:
        sel_ref, refs = refs[0], refs[1:]
        out_refs = refs[-groups:]
    rows = down_refs[0].shape[0]
    half = down_refs[0].shape[1] // holders
    shard_at = lax.rem(here + holders - k, holders) * half
    for j, block in enumerate(refs[:count]):
        wide = block.shape[0]
        at = 0 if count == 1 else lax.rem(core + replicas - j, replicas) * wide
        columns = pl.ds(pl.multiple_of(shard_at + at, wide), wide)
        for dg in range(groups):
            base = rows_by_rows(g_refs[dg][:, :-LANES], block[...]).astype(BF16)
            lora = 0.0
            for dr in range(replicas):
                lora = lora + jnp.dot(
                    sel_ref[pl.ds(dg * tokens, tokens), dr * rows : (dr + 1) * rows],
                    down_refs[dr][:, columns],
                    preferred_element_type=F32,
                )
            lora = (ADAPTER_SCALE * lora).astype(BF16)
            out_refs[dg][:, pl.ds(at if count == 1 else pl.multiple_of(at, wide), wide)] = (
                base.astype(F32) + lora.astype(F32)
            ).astype(BF16)


def place_kernel(sizes, *refs):
    groups, holders, shard, half = sizes
    group, here = lax.axis_index("groups"), lax.axis_index("adapter")
    out_ref = refs[-1]
    for k in range(holders):
        for dg in range(groups):
            source = lax.rem(group + groups - dg, groups)
            at = lax.rem(here + holders - k, holders) * shard + source * half
            out_ref[:, pl.ds(pl.multiple_of(at, half), half)] = refs[k * groups + dg][...]


def chip_kernel(replicas, *refs):
    own_ref, came_refs, out_refs = refs[0], refs[1 : 2 * replicas - 1], refs[2 * replicas - 1 :]
    rows = out_refs[0].shape[0]
    split = came_refs[0].shape[1]
    for k, out in enumerate(out_refs):
        for j in range(2):
            at = pl.ds(k * rows, rows), pl.ds(j * split, split)
            total = own_ref[at]
            for ref in came_refs[j::2]:
                total = total + ref[pl.ds(k * rows, rows), :].astype(F32)
            out[:, pl.ds(j * split, split)] = total.astype(out.dtype)


def total_kernel(*refs):
    total = refs[0][...]
    for ref in refs[1:-1]:
        total = total + ref[...].astype(F32)
    refs[-1][...] = (ADAPTER_SCALE * total).astype(BF16)


def spread_kernel(width, replicas, *refs):
    core = lax.axis_index("replica")
    down_ref, up_ref = refs[replicas:]
    slots = down_ref.shape[0] // replicas
    rank = down_ref.shape[1]
    for dr in range(replicas):
        at = lax.rem(core + replicas - dr, replicas) * slots
        for j in range(slots):
            down_ref[at + j] = refs[dr][j * rank : (j + 1) * rank, :width]
            up_ref[at + j] = refs[dr][j * rank : (j + 1) * rank, width:]


def on_device(
    saved_layer_input,
    value_output_gradient,
    token_adapter_index,
    adapter_slot_index,
    frozen_value_weight,
    adapter_down_weight,
    adapter_up_weight,
):
    inputs = saved_layer_input[0]
    grad_rows = value_output_gradient[0]
    tokens, width = inputs.shape
    value_width = grad_rows.shape[1]
    groups, holders, replicas = (lax.axis_size(a) for a in ("groups", "adapter", "replica"))
    group, here, core = (lax.axis_index(a) for a in ("groups", "adapter", "replica"))
    slots, rank = adapter_down_weight.shape[1:3]
    own_slots = slots // replicas
    rows = own_slots * rank
    frozen = frozen_value_weight[0]
    shard = frozen.shape[0]
    half = shard // groups
    piece = half // replicas
    cols = width + value_width

    tagged = call(
        tag_kernel,
        [jax.ShapeDtypeStruct((tokens, value_width + LANES), BF16)],
        (grad_rows, token_adapter_index[0], adapter_slot_index[None]),
    )[0]
    grads = [tagged] + [
        moved(tagged, lambda g, z, s, r: (g - dg, z, s, r)) for dg in range(1, groups)
    ]

    own = call(
        functools.partial(own_kernel, (groups, holders, shard)),
        [jax.ShapeDtypeStruct((rows, holders * half + value_width), BF16)],
        (adapter_down_weight[0], adapter_up_weight[0]),
    )[0]
    held = [own]
    for k in range(1, holders):
        held.append(moved(own, lambda g, z, s, r: (g, z + k, s, r)))
    held, grads = lax.optimization_barrier((held, grads))
    ups = [jnp.concatenate([x[:, holders * half :] for x in held], axis=0)]
    downs = [jnp.concatenate([x[:, : holders * half] for x in held], axis=0)]
    for dr in range(1, replicas):
        ups.append(moved(ups[0], lambda g, z, s, r: (g, z, s, r + dr)))
        downs.append(moved(downs[0], lambda g, z, s, r: (g, z, s, r + dr)))
    others = [moved(downs[0], lambda g, z, s, r: (g + dg, z, s, r)) for dg in range(1, groups)]
    row_slot = jnp.concatenate(
        [
            ((here - k) % holders) * slots
            + ((core - dr) % replicas) * own_slots
            + jnp.arange(rows, dtype=jnp.int32) // rank
            for dr in range(replicas)
            for k in range(holders)
        ]
    ).astype(F32)[None]

    mine = lax.dynamic_slice_in_dim(frozen, group * half, half, axis=0)
    ring = [lax.dynamic_slice_in_dim(mine, core * piece, piece, axis=0)]
    def pieces_of(k, *before):
        if k == 0:
            return [mine]
        block = after(ring[k], *before) if before else ring[k]
        pieces = [block] + [
            moved(block, lambda g, z, s, r: (g, z, s, r + dr)) for dr in range(1, replicas)
        ]
        if piece % LANES:
            whole = jnp.zeros((half, value_width), BF16)
            for dr in range(replicas):
                at = ((core - dr) % replicas) * piece
                whole = lax.dynamic_update_slice_in_dim(whole, pieces[dr], at, axis=0)
            pieces = [whole]
        return pieces

    kept = replicas * holders * rows

    def adapter_sums(sel):
        maps = list(downs)
        for other in others:
            maps.append(after(other, sel))
            for dr in range(1, replicas):
                maps.append(moved(maps[-dr], lambda g, z, s, r: (g, z, s, r + dr)))
        gradients = call(
            functools.partial(adapter_kernel, (groups, holders, replicas, shard)),
            [jax.ShapeDtypeStruct((holders * rows, cols), F32)]
            + [jax.ShapeDtypeStruct((holders * rows, cols // 2), BF16)] * (2 * replicas - 2),
            (inputs, tagged, row_slot, sel, *maps),
            [jax.ShapeDtypeStruct((kept, width), BF16)],
        )
        part, sent = gradients[0], gradients[1:]
        came = [
            moved(sent[2 * dr - 2 + j], lambda g, z, s, r: (g, z, s, r - dr))
            for dr in range(1, replicas)
            for j in range(2)
        ]
        chip = call(
            functools.partial(chip_kernel, replicas),
            [jax.ShapeDtypeStruct((rows, cols), F32)]
            + [jax.ShapeDtypeStruct((rows, cols), BF16)] * (holders - 1),
            (part, *came),
        )
        return part, chip

    arrived, outs = [], []
    for k in range(holders):
        if k:
            last = ring[-1]
            if k == 2:
                last = after(last, downs[0])
            elif k > 2:
                last = after(last, *outs[k - 2], part)
            ring.append(moved(last, lambda g, z, s, r: (g, z + 1, s, r)))
        gate = [*arrived[k - 2], *outs[k - 1]] if k > 1 else []
        blocks = pieces_of(k, *gate, *(chip[:1] if k > 2 else ()))
        out = call(
            functools.partial(frozen_kernel, (tokens, groups, holders, replicas), k, len(blocks)),
            [jax.ShapeDtypeStruct((tokens, half), BF16)] * groups
            + [jax.ShapeDtypeStruct((groups * tokens, kept), BF16)] * (k == 0),
            [*grads, *downs, *([sel] if k else [row_slot, *ups]), *blocks],
        )
        if k == 0:
            sel = out[groups]
            part, chip = adapter_sums(sel)
        outs.append(list(out[:groups]))
        mails = outs[-1]
        if k > 2:
            mails = [after(mail, *arrived[-1]) for mail in mails]
        arrived.append(
            [moved(mails[dg], lambda g, z, s, r: (g + dg, z, s - 1, r)) for dg in range(groups)]
        )
    passed = call(
        functools.partial(place_kernel, (groups, holders, shard, half)),
        [jax.ShapeDtypeStruct((tokens, width), BF16)],
        [x for got in arrived for x in got],
    )[0]

    sums = [chip[0]] + [
        moved(after(chip[k], ring[-1]), lambda g, z, s, r: (g, z - k, s, r))
        for k in range(1, holders)
    ]
    total = call(total_kernel, [jax.ShapeDtypeStruct((rows, cols), BF16)], sums)[0]
    totals = [total] + [
        moved(total, lambda g, z, s, r: (g, z, s, r + dr)) for dr in range(1, replicas)
    ]
    down_grad, up_grad = call(
        functools.partial(spread_kernel, width, replicas),
        [
            jax.ShapeDtypeStruct((slots, rank, width), BF16),
            jax.ShapeDtypeStruct((slots, rank, value_width), BF16),
        ],
        totals,
    )

    return passed[None], down_grad[None], up_grad[None]


def solution(mesh):
    placed = (
        P("segment", ("groups", "adapter", "replica"), None),
        P("segment", ("groups", "adapter", "replica"), None),
        P("segment", ("groups", "adapter", "replica"), None),
        P("groups"),
        P("segment", "adapter", None),
        P("segment", "adapter", None, None),
        P("segment", "adapter", None, None),
    )
    return jax.shard_map(
        on_device,
        mesh=mesh,
        in_specs=placed,
        out_specs=(
            P("segment", ("groups", "adapter", "replica"), None),
            P(("groups", "segment"), "adapter", None, None),
            P(("groups", "segment"), "adapter", None, None),
        ),
        check_vma=False,
    )
```

time: 119 us -> 88.2 us (0.74)
  waiting for transfers between devices: 56.4 us -> 37.7 us
  starting transfers between devices: 37.2 us -> 27.6 us
  Pallas kernels: 13 us -> 11.3 us
  local copies, waits for them, and re-layouts: 10.5 us -> 8.98 us
    ppermute x24 -> x28, waiting for transfers between devices: 56.4 us -> 37.7 us  [moved(): return lax.ppermute(x, AXES, pairs)]
    ppermute x24 -> x28, starting transfers between devices: 37.2 us -> 27.6 us  [moved(): return lax.ppermute(x, AXES, pairs)]
    slice x0 -> x8, local copies, waits for them, and re-layouts: none -> 2.31 us  [the longest x4 2.28 us: on_device(): ups = [jnp.concatenate([x[:, holders * half:] for x in held], axis=0)]]
    dynamic_update_slice x8 -> x0, local copies, waits for them, and re-layouts: 1.98 us -> none  [on_device(): lax.dynamic_update_slice_in_dim(passed, got[dg][:, j * half:(j + 1) * hal...]
    unnamed x16 -> x18, local copies, waits for them, and re-layouts: 5.5 us -> 3.6 us
    reshape x2 -> x0, local copies, waits for them, and re-layouts: 1.72 us -> none  [on_device(): own = jnp.concatenate([lax.dynamic_slice(adapter_down_weight[0], (core *...]
    pallas_call x7 -> x11, Pallas kernels: 13 us -> 11.3 us  [call(): pl.pallas_call(kernel, out_shape=out_shape, scratch_shapes=[pltpu.VMEM(x....]
    concatenate x1, local copies, waits for them, and re-layouts: 0.1 us -> 1.3 us  [on_device(): jnp.concatenate([(here - k) % holders * slots + (core - dr) % replicas *...]
  transfers between devices with their start and end apart: 24 -> 28, of which waited for: 14 -> 12; matrix products, arithmetic and copies ran while one was open for 3% -> 8% of each run, Pallas kernels for 11% -> 12%
where the time goes in v5:
time: 88.2 us; the launch traced here: 87.7 us
  waiting for transfers between devices  37.7 us (43%)
  starting transfers between devices  27.6 us (31%)
  Pallas kernels  11.3 us (13%)
  local copies, waits for them, and re-layouts  8.98 us (10%)
  other arithmetic  1.2 us (1%)
  between operations  0.91 us (1%)
    ppermute x28, waiting for transfers between devices, moved(): return lax.ppermute(x, AXES, pairs)  37.7 us
    ppermute x28, starting transfers between devices, moved(): return lax.ppermute(x, AXES, pairs)  27.6 us
    pallas_call x11, Pallas kernels, call(): pl.pallas_call(kernel, out_shape=out_shape, scratch_shapes=[pltpu.VMEM(x....  11.3 us
    unnamed x18, local copies, waits for them, and re-layouts  3.6 us
    slice x4, local copies, waits for them, and re-layouts, on_device(): ups = [jnp.concatenate([x[:, holders * half:] for x in held], axis=0)]  2.28 us
  transfers between devices with their start and end apart: 28, of which 12 were waited for; matrix products, arithmetic and copies ran while one was open for 8% of the time, Pallas kernels for 12%

profile of v5, /device:TPU:0, one launch (start us, length us, event | category | flops | bytes accessed | tf_op | source)
XLA Modules:
  0.0 87.7 jit_solution(15182101591041852732)
XLA Ops:
  0.7 1.1 %copy-done.3 = bf16[1,2,16,4096]{3,2,1,0:T(8,128)(2,1)S(1)} copy-done((bf16[1,2,16,4096]{3,2,1,0:T(8,128)(2,1)S(1)}, bf16[1,2,16,4096]{3,2,1,0:T(8,128)(2,1)}, u32[]{:S(2)}) %copy-start.3) | copy-done | bytes 262168
  2.6 3.1 %collective-permute-start = (bf16[16,3072]{1,0:T(8,128)(2,1)S(1)}, bf16[16,3072]{1,0:T(8,128)(2,1)S(1)}, u32[]{:S(2)}, u32[]{:S(2)}) collective-permute-start(bf16[16,3072]{1,0:T(8,128)(2,1)S(1)} %shard_map.94), channel_id=1, source_target_pairs={{0,4},{1,5},{2,6},{3,7},{4,8},{5,9},{6,10},{7,11},{8,12},{9,13},{1... | collective-permute-start | bytes 294920 | tf_op jit(solution)/shard_map/ppermute | solution.py:24
  5.7 2.6 %collective-permute-start.1 = (bf16[16,3072]{1,0:T(8,128)(2,1)S(1)}, bf16[16,3072]{1,0:T(8,128)(2,1)S(1)}, u32[]{:S(2)}, u32[]{:S(2)}) collective-permute-start(bf16[16,3072]{1,0:T(8,128)(2,1)S(1)} %shard_map.94), channel_id=1, source_target_pairs={{0,8},{1,9},{2,10},{3,11},{4,12},{5,13},{6,14},{7,15},{8,0},{9,1},... | collective-permute-start | bytes 294920 | tf_op jit(solution)/shard_map/ppermute | solution.py:24
  8.3 1.3 %collective-permute-start.2 = (bf16[16,3072]{1,0:T(8,128)(2,1)S(1)}, bf16[16,3072]{1,0:T(8,128)(2,1)S(1)}, u32[]{:S(2)}, u32[]{:S(2)}) collective-permute-start(bf16[16,3072]{1,0:T(8,128)(2,1)S(1)} %shard_map.94), channel_id=1, source_target_pairs={{0,12},{1,13},{2,14},{3,15},{4,0},{5,1},{6,2},{7,3},{8,4},{9,5},{1... | collective-permute-start | bytes 294920 | tf_op jit(solution)/shard_map/ppermute | solution.py:24
  12.2 1.6 %collective-permute-start.3 = (bf16[176,1152]{1,0:T(8,128)(2,1)S(1)}, bf16[176,1152]{1,0:T(8,128)(2,1)S(1)}, u32[]{:S(2)}, u32[]{:S(2)}) collective-permute-start(bf16[176,1152]{1,0:T(8,128)(2,1)S(1)} %shard_map.95.refs_0_.refs_1_), channel_id=1, source_target_pairs={{0,16},{1,17},{2,18},{3,19},{4,20},{5,21},{6,22},{7,23},{8,24},{9,... | collective-permute-start | bytes 1216520 | tf_op jit(solution)/shard_map/ppermute | solution.py:24
  15.5 7.1 %collective-permute-done.3.refs_1_ = bf16[176,1152]{1,0:T(8,128)(2,1)S(1)} collective-permute-done((bf16[176,1152]{1,0:T(8,128)(2,1)S(1)}, bf16[176,1152]{1,0:T(8,128)(2,1)S(1)}, u32[]{:S(2)}, u32[]{:S(2)}) %collective-permute-start.3) | collective-permute-done | bytes 405536 | tf_op jit(solution)/shard_map/ppermute | solution.py:24
  22.7 1.6 %collective-permute-start.16 = (bf16[64,2048]{1,0:T(8,128)(2,1)S(1)}, bf16[64,2048]{1,0:T(8,128)(2,1)}, u32[]{:S(2)}, u32[]{:S(2)}) collective-permute-start(bf16[64,2048]{1,0:T(8,128)(2,1)S(1)} %pad_maximum_fusion.refs_2_.refs_4_), channel_id=1, source_target_pairs={{0,16},{1,17},{2,18},{3,19},{4,20},{5,21},{6,22},{7,23},{8,24},{9,... | collective-permute-start | bytes 786440 | tf_op jit(solution)/shard_map/ppermute | solution.py:24
  24.3 5.1 %collective-permute-done.8.refs_5_ = bf16[256,1024]{1,0:T(8,128)(2,1)} collective-permute-done((bf16[256,1024]{1,0:T(8,128)(2,1)}, bf16[256,1024]{1,0:T(8,128)(2,1)}, u32[]{:S(2)}, u32[]{:S(2)}) %collective-permute-start.8) | collective-permute-done | bytes 524320 | tf_op jit(solution)/shard_map/ppermute | solution.py:24
  29.9 1.3 %concatenate.41 = s32[1,128]{1,0:T(1,128)} concatenate(s32[1,16]{1,0:T(1,128)} %get-tuple-element.78, s32[1,16]{1,0:T(1,128)} %get-tuple-element.77, s32[1,16]{1,0:T(1,128)S(1)} %get-tuple-element.76, s32[1,16]{1,0:T(1,128)S(1)} %get-tuple-element.75, s32[1,16]{1,0:T(1,128)S(1)} %get-tuple-element.74, s32[1,16]{1,0:T(1,128)S(1)} %get-tuple-element.73, ...), dimensions={1} | concatenate | bytes 1024 | tf_op jit(solution)/shard_map/concatenate | solution.py:243
  35.7 1.5 %shard_map.96 = (bf16[176,512]{1,0:T(8,128)(2,1)S(1)}, bf16[176,512]{1,0:T(8,128)(2,1)S(1)}, bf16[352,128]{1,0:T(8,128)(2,1)S(1)}) custom-call(bf16[176,1152]{1,0:T(8,128)(2,1)S(1)} %shard_map.95.refs_0_.refs_1_, bf16[176,1152]{1,0:T(8,128)(2,1)S(1)} %collective-permute-done.3.refs_1_, bf16[64,2048]{1,0:T(8,128)(2,1)S(1)} %pad_maximum_fusion.refs_2_.refs_4_, ...), custom_call_target="tpu_custom_call" | custom-call | flops 1000 | bytes 1000 | tf_op jit(solution)/shard_map/pallas_call | solution.py:41
  37.7 1.5 %collective-permute-start.6 = (bf16[176,512]{1,0:T(8,128)(2,1)S(1)}, bf16[176,512]{1,0:T(8,128)(2,1)S(1)}, u32[]{:S(2)}, u32[]{:S(2)}) collective-permute-start(bf16[176,512]{1,0:T(8,128)(2,1)S(1)} %get-tuple-element.43), channel_id=1, source_target_pairs={{0,2},{1,3},{2,0},{3,1},{4,6},{5,7},{6,4},{7,5},{8,10},{9,11},{10,... | collective-permute-start | bytes 540680 | tf_op jit(solution)/shard_map/ppermute | solution.py:24
  39.6 2.2 %shard_map.99 = (f32[64,5120]{1,0:T(8,128)S(1)}, bf16[64,2560]{1,0:T(8,128)(2,1)S(1)}, bf16[64,2560]{1,0:T(8,128)(2,1)S(1)}) custom-call(bf16[176,4096]{1,0:T(8,128)(2,1)S(1)} %bitcast.29, bf16[176,1152]{1,0:T(8,128)(2,1)S(1)} %shard_map.95.refs_0_.refs_1_, f32[1,128]{1,0:T(1,128)S(1)} %convert_element_type.10.refs_4_.refs_2_, ...), custom_call_target="tpu_custom_call" | custom-call | flops 1000 | bytes 1000 | tf_op jit(solution)/shard_map/pallas_call | solution.py:41
  41.9 2.2 %shard_map.97 = (bf16[176,512]{1,0:T(8,128)(2,1)S(1)}, bf16[176,512]{1,0:T(8,128)(2,1)S(1)}) custom-call(bf16[176,1152]{1,0:T(8,128)(2,1)S(1)} %shard_map.95.refs_0_.refs_1_, bf16[176,1152]{1,0:T(8,128)(2,1)S(1)} %collective-permute-done.3.refs_1_, bf16[64,2048]{1,0:T(8,128)(2,1)S(1)} %pad_maximum_fusion.refs_2_.refs_4_, ...), custom_call_target="tpu_custom_call" | custom-call | flops 1000 | bytes 1000 | tf_op jit(solution)/shard_map/pallas_call | solution.py:41
  45.1 3.0 %collective-permute-done.7.refs_1_ = bf16[176,512]{1,0:T(8,128)(2,1)S(1)} collective-permute-done((bf16[176,512]{1,0:T(8,128)(2,1)S(1)}, bf16[176,512]{1,0:T(8,128)(2,1)S(1)}, u32[]{:S(2)}, u32[]{:S(2)}) %collective-permute-start.7) | collective-permute-done | bytes 180256 | tf_op jit(solution)/shard_map/ppermute | solution.py:24
  48.1 1.1 %collective-permute-start.18 = (bf16[256,1024]{1,0:T(8,128)(2,1)}, bf16[256,1024]{1,0:T(8,128)(2,1)S(1)}, u32[]{:S(2)}, u32[]{:S(2)}) collective-permute-start(bf16[256,1024]{1,0:T(8,128)(2,1)} %collective-permute-done.12.refs_5_), channel_id=1, source_target_pairs={{0,4},{1,5},{2,6},{3,7},{4,8},{5,9},{6,10},{7,11},{8,12},{9,13},{1... | collective-permute-start | bytes 1572872 | tf_op jit(solution)/shard_map/ppermute | solution.py:24
  49.7 1.5 %collective-permute-start.10 = (bf16[176,512]{1,0:T(8,128)(2,1)S(1)}, bf16[176,512]{1,0:T(8,128)(2,1)S(1)}, u32[]{:S(2)}, u32[]{:S(2)}) collective-permute-start(bf16[176,512]{1,0:T(8,128)(2,1)S(1)} %get-tuple-element.46), channel_id=1, source_target_pairs={{0,2},{1,3},{2,0},{3,1},{4,6},{5,7},{6,4},{7,5},{8,10},{9,11},{10,... | collective-permute-start | bytes 540680 | tf_op jit(solution)/shard_map/ppermute | solution.py:24
  51.2 1.7 %collective-permute-start.11 = (bf16[176,512]{1,0:T(8,128)(2,1)S(1)}, bf16[176,512]{1,0:T(8,128)(2,1)S(1)}, u32[]{:S(2)}, u32[]{:S(2)}) collective-permute-start(bf16[176,512]{1,0:T(8,128)(2,1)S(1)} %get-tuple-element.47), channel_id=1, source_target_pairs={{0,18},{1,19},{2,16},{3,17},{4,22},{5,23},{6,20},{7,21},{8,26},{9,... | collective-permute-start | bytes 540680 | tf_op jit(solution)/shard_map/ppermute | solution.py:24
  53.0 2.1 %shard_map.98 = (bf16[176,512]{1,0:T(8,128)(2,1)S(1)}, bf16[176,512]{1,0:T(8,128)(2,1)S(1)}) custom-call(bf16[176,1152]{1,0:T(8,128)(2,1)S(1)} %shard_map.95.refs_0_.refs_1_, bf16[176,1152]{1,0:T(8,128)(2,1)S(1)} %collective-permute-done.3.refs_1_, bf16[64,2048]{1,0:T(8,128)(2,1)S(1)} %pad_maximum_fusion.refs_2_.refs_4_, ...), custom_call_target="tpu_custom_call" | custom-call | flops 1000 | bytes 1000 | tf_op jit(solution)/shard_map/pallas_call | solution.py:41
  55.1 2.0 %collective-permute-done.10.refs_2_ = bf16[176,512]{1,0:T(8,128)(2,1)S(1)} collective-permute-done((bf16[176,512]{1,0:T(8,128)(2,1)S(1)}, bf16[176,512]{1,0:T(8,128)(2,1)S(1)}, u32[]{:S(2)}, u32[]{:S(2)}) %collective-permute-start.10) | collective-permute-done | bytes 180256 | tf_op jit(solution)/shard_map/ppermute | solution.py:24
  57.1 3.3 %collective-permute-done.11.refs_3_ = bf16[176,512]{1,0:T(8,128)(2,1)S(1)} collective-permute-done((bf16[176,512]{1,0:T(8,128)(2,1)S(1)}, bf16[176,512]{1,0:T(8,128)(2,1)S(1)}, u32[]{:S(2)}, u32[]{:S(2)}) %collective-permute-start.11) | collective-permute-done | bytes 180256 | tf_op jit(solution)/shard_map/ppermute | solution.py:24
  60.4 4.3 %collective-permute-done.18.refs_5_ = bf16[256,1024]{1,0:T(8,128)(2,1)S(1)} collective-permute-done((bf16[256,1024]{1,0:T(8,128)(2,1)}, bf16[256,1024]{1,0:T(8,128)(2,1)S(1)}, u32[]{:S(2)}, u32[]{:S(2)}) %collective-permute-start.18) | collective-permute-done | bytes 524320 | tf_op jit(solution)/shard_map/ppermute | solution.py:24
  64.7 1.5 %collective-permute-start.14 = (bf16[176,512]{1,0:T(8,128)(2,1)S(1)}, bf16[176,512]{1,0:T(8,128)(2,1)S(1)}, u32[]{:S(2)}, u32[]{:S(2)}) collective-permute-start(bf16[176,512]{1,0:T(8,128)(2,1)S(1)} %get-tuple-element.50), channel_id=1, source_target_pairs={{0,2},{1,3},{2,0},{3,1},{4,6},{5,7},{6,4},{7,5},{8,10},{9,11},{10,... | collective-permute-start | bytes 540680 | tf_op jit(solution)/shard_map/ppermute | solution.py:24
  66.2 1.5 %collective-permute-start.15 = (bf16[176,512]{1,0:T(8,128)(2,1)S(1)}, bf16[176,512]{1,0:T(8,128)(2,1)S(1)}, u32[]{:S(2)}, u32[]{:S(2)}) collective-permute-start(bf16[176,512]{1,0:T(8,128)(2,1)S(1)} %get-tuple-element.51), channel_id=1, source_target_pairs={{0,18},{1,19},{2,16},{3,17},{4,22},{5,23},{6,20},{7,21},{8,26},{9,... | collective-permute-start | bytes 540680 | tf_op jit(solution)/shard_map/ppermute | solution.py:24
  67.7 2.3 %collective-permute-start.25 = (bf16[16,5120]{1,0:T(8,128)(2,1)S(1)}, bf16[16,5120]{1,0:T(8,128)(2,1)S(1)}, u32[]{:S(2)}, u32[]{:S(2)}) collective-permute-start(bf16[16,5120]{1,0:T(8,128)(2,1)S(1)} %get-tuple-element.66), channel_id=1, source_target_pairs={{0,8},{1,9},{2,10},{3,11},{4,12},{5,13},{6,14},{7,15},{8,0},{9,1},... | collective-permute-start | bytes 491528 | tf_op jit(solution)/shard_map/ppermute | solution.py:24
  70.0 1.5 %collective-permute-start.24 = (bf16[16,5120]{1,0:T(8,128)(2,1)S(1)}, bf16[16,5120]{1,0:T(8,128)(2,1)S(1)}, u32[]{:S(2)}, u32[]{:S(2)}) collective-permute-start(bf16[16,5120]{1,0:T(8,128)(2,1)S(1)} %get-tuple-element.64), channel_id=1, source_target_pairs={{0,12},{1,13},{2,14},{3,15},{4,0},{5,1},{6,2},{7,3},{8,4},{9,5},{1... | collective-permute-start | bytes 491528 | tf_op jit(solution)/shard_map/ppermute | solution.py:24
  71.5 1.0 %shard_map.101 = (bf16[176,512]{1,0:T(8,128)(2,1)S(1)}, bf16[176,512]{1,0:T(8,128)(2,1)S(1)}) custom-call(bf16[176,1152]{1,0:T(8,128)(2,1)S(1)} %shard_map.95.refs_0_.refs_1_, bf16[176,1152]{1,0:T(8,128)(2,1)S(1)} %collective-permute-done.3.refs_1_, bf16[64,2048]{1,0:T(8,128)(2,1)S(1)} %pad_maximum_fusion.refs_2_.refs_4_, ...), custom_call_target="tpu_custom_call" | custom-call | flops 1000 | bytes 1000 | tf_op jit(solution)/shard_map/pallas_call | solution.py:41
  72.5 3.9 %collective-permute-done.15.refs_5_ = bf16[176,512]{1,0:T(8,128)(2,1)S(1)} collective-permute-done((bf16[176,512]{1,0:T(8,128)(2,1)S(1)}, bf16[176,512]{1,0:T(8,128)(2,1)S(1)}, u32[]{:S(2)}, u32[]{:S(2)}) %collective-permute-start.15) | collective-permute-done | bytes 180256 | tf_op jit(solution)/shard_map/ppermute | solution.py:24
  76.5 1.4 %collective-permute-start.23 = (bf16[176,512]{1,0:T(8,128)(2,1)S(1)}, bf16[176,512]{1,0:T(8,128)(2,1)S(1)}, u32[]{:S(2)}, u32[]{:S(2)}) collective-permute-start(bf16[176,512]{1,0:T(8,128)(2,1)S(1)} %get-tuple-element.62), channel_id=1, source_target_pairs={{0,18},{1,19},{2,16},{3,17},{4,22},{5,23},{6,20},{7,21},{8,26},{9,... | collective-permute-start | bytes 540680 | tf_op jit(solution)/shard_map/ppermute | solution.py:24
  78.5 4.2 %collective-permute-done.25.refs_2_ = bf16[16,5120]{1,0:T(8,128)(2,1)S(1)} collective-permute-done((bf16[16,5120]{1,0:T(8,128)(2,1)S(1)}, bf16[16,5120]{1,0:T(8,128)(2,1)S(1)}, u32[]{:S(2)}, u32[]{:S(2)}) %collective-permute-start.25) | collective-permute-done | bytes 163872 | tf_op jit(solution)/shard_map/ppermute | solution.py:24
  82.9 1.4 %collective-permute-done.27.refs_1_ = bf16[16,5120]{1,0:T(8,128)(2,1)S(1)} collective-permute-done((bf16[16,5120]{1,0:T(8,128)(2,1)S(1)}, bf16[16,5120]{1,0:T(8,128)(2,1)S(1)}, u32[]{:S(2)}, u32[]{:S(2)}) %collective-permute-start.27) | collective-permute-done | bytes 163872 | tf_op jit(solution)/shard_map/ppermute | solution.py:24
  85.0 1.5 %collective-permute-done.22.refs_6_ = bf16[176,512]{1,0:T(8,128)(2,1)S(1)} collective-permute-done((bf16[176,512]{1,0:T(8,128)(2,1)S(1)}, bf16[176,512]{1,0:T(8,128)(2,1)S(1)}, u32[]{:S(2)}, u32[]{:S(2)}) %collective-permute-start.22) | collective-permute-done | bytes 180256 | tf_op jit(solution)/shard_map/ppermute | solution.py:24
  86.5 1.2 %shard_map.102 = bf16[176,4096]{1,0:T(8,128)(2,1)} custom-call(bf16[176,512]{1,0:T(8,128)(2,1)S(1)} %collective-permute-done.6.refs_0_, bf16[176,512]{1,0:T(8,128)(2,1)S(1)} %collective-permute-done.7.refs_1_, bf16[176,512]{1,0:T(8,128)(2,1)S(1)} %collective-permute-done.10.refs_2_, bf16[176,512]{1,0:T(8,128)(2,1)S(1)} %collective-permute-done.11.refs_3_, ...), custom_call_target="tpu_custom_call" | custom-call | flops 1000 | bytes 1000 | tf_op jit(solution)/shard_map/pallas_call | solution.py:41
  (72 shorter events, 14.2 us)
Async XLA Ops:
  0.6 13.2 %copy-start = (bf16[1,1024,1024]{2,1,0:T(8,128)(2,1)S(1)}, bf16[1,1024,1024]{2,1,0:T(8,128)(2,1)}, u32[]{:S(2)}) copy-start(bf16[1,1024,1024]{2,1,0:T(8,128)(2,1)} %param.11) | copy-start | bytes 6291460
  2.6 12.8 %collective-permute-start = (bf16[16,3072]{1,0:T(8,128)(2,1)S(1)}, bf16[16,3072]{1,0:T(8,128)(2,1)S(1)}, u32[]{:S(2)}, u32[]{:S(2)}) collective-permute-start(bf16[16,3072]{1,0:T(8,128)(2,1)S(1)} %shard_map.94), channel_id=1, source_target_pairs={{0,4},{1,5},{2,6},{3,7},{4,8},{5,9},{6,10},{7,11},{8,12},{9,13},{1... | collective-permute-start | bytes 294920 | tf_op jit(solution)/shard_map/ppermute | solution.py:24
  5.7 9.8 %collective-permute-start.1 = (bf16[16,3072]{1,0:T(8,128)(2,1)S(1)}, bf16[16,3072]{1,0:T(8,128)(2,1)S(1)}, u32[]{:S(2)}, u32[]{:S(2)}) collective-permute-start(bf16[16,3072]{1,0:T(8,128)(2,1)S(1)} %shard_map.94), channel_id=1, source_target_pairs={{0,8},{1,9},{2,10},{3,11},{4,12},{5,13},{6,14},{7,15},{8,0},{9,1},... | collective-permute-start | bytes 294920 | tf_op jit(solution)/shard_map/ppermute | solution.py:24
  8.3 7.2 %collective-permute-start.2 = (bf16[16,3072]{1,0:T(8,128)(2,1)S(1)}, bf16[16,3072]{1,0:T(8,128)(2,1)S(1)}, u32[]{:S(2)}, u32[]{:S(2)}) collective-permute-start(bf16[16,3072]{1,0:T(8,128)(2,1)S(1)} %shard_map.94), channel_id=1, source_target_pairs={{0,12},{1,13},{2,14},{3,15},{4,0},{5,1},{6,2},{7,3},{8,4},{9,5},{1... | collective-permute-start | bytes 294920 | tf_op jit(solution)/shard_map/ppermute | solution.py:24
  12.2 10.3 %collective-permute-start.3 = (bf16[176,1152]{1,0:T(8,128)(2,1)S(1)}, bf16[176,1152]{1,0:T(8,128)(2,1)S(1)}, u32[]{:S(2)}, u32[]{:S(2)}) collective-permute-start(bf16[176,1152]{1,0:T(8,128)(2,1)S(1)} %shard_map.95.refs_0_.refs_1_), channel_id=1, source_target_pairs={{0,16},{1,17},{2,18},{3,19},{4,20},{5,21},{6,22},{7,23},{8,24},{9,... | collective-permute-start | bytes 1216520 | tf_op jit(solution)/shard_map/ppermute | solution.py:24
  14.7 14.7 %collective-permute-start.8 = (bf16[256,1024]{1,0:T(8,128)(2,1)}, bf16[256,1024]{1,0:T(8,128)(2,1)}, u32[]{:S(2)}, u32[]{:S(2)}) collective-permute-start(bf16[256,1024]{1,0:T(8,128)(2,1)} %dynamic-slice_bitcast_fusion.1), channel_id=1, source_target_pairs={{0,4},{1,5},{2,6},{3,7},{4,8},{5,9},{6,10},{7,11},{8,12},{9,13},{1... | collective-permute-start | bytes 1572872 | tf_op jit(solution)/shard_map/ppermute | solution.py:24
  15.4 7.2 %copy-start.6 = (bf16[16,3072]{1,0:T(8,128)(2,1)}, bf16[16,3072]{1,0:T(8,128)(2,1)S(1)}, u32[]{:S(2)}) copy-start(bf16[16,3072]{1,0:T(8,128)(2,1)S(1)} %collective-permute-done) | copy-start | bytes 294916
  15.5 7.1 %copy-start.7 = (bf16[16,3072]{1,0:T(8,128)(2,1)}, bf16[16,3072]{1,0:T(8,128)(2,1)S(1)}, u32[]{:S(2)}) copy-start(bf16[16,3072]{1,0:T(8,128)(2,1)S(1)} %collective-permute-done.1) | copy-start | bytes 294916
  15.5 7.1 %copy-start.8 = (bf16[16,3072]{1,0:T(8,128)(2,1)}, bf16[16,3072]{1,0:T(8,128)(2,1)S(1)}, u32[]{:S(2)}) copy-start(bf16[16,3072]{1,0:T(8,128)(2,1)S(1)} %collective-permute-done.2) | copy-start | bytes 294916
  22.7 13.1 %collective-permute-start.4 = (bf16[64,2048]{1,0:T(8,128)(2,1)S(1)}, bf16[64,2048]{1,0:T(8,128)(2,1)S(1)}, u32[]{:S(2)}, u32[]{:S(2)}) collective-permute-start(bf16[64,2048]{1,0:T(8,128)(2,1)S(1)} %pad_maximum_fusion.refs_2_.refs_4_), channel_id=1, source_target_pairs={{0,1},{1,0},{2,3},{3,2},{4,5},{5,4},{6,7},{7,6},{8,9},{9,8},{10,11... | collective-permute-start | bytes 786440 | tf_op jit(solution)/shard_map/ppermute | solution.py:24
  22.7 14.5 %collective-permute-start.16 = (bf16[64,2048]{1,0:T(8,128)(2,1)S(1)}, bf16[64,2048]{1,0:T(8,128)(2,1)}, u32[]{:S(2)}, u32[]{:S(2)}) collective-permute-start(bf16[64,2048]{1,0:T(8,128)(2,1)S(1)} %pad_maximum_fusion.refs_2_.refs_4_), channel_id=1, source_target_pairs={{0,16},{1,17},{2,18},{3,19},{4,20},{5,21},{6,22},{7,23},{8,24},{9,... | collective-permute-start | bytes 786440 | tf_op jit(solution)/shard_map/ppermute | solution.py:24
  29.4 18.7 %collective-permute-start.12 = (bf16[256,1024]{1,0:T(8,128)(2,1)}, bf16[256,1024]{1,0:T(8,128)(2,1)}, u32[]{:S(2)}, u32[]{:S(2)}) collective-permute-start(bf16[256,1024]{1,0:T(8,128)(2,1)} %collective-permute-done.8.refs_5_), channel_id=1, source_target_pairs={{0,4},{1,5},{2,6},{3,7},{4,8},{5,9},{6,10},{7,11},{8,12},{9,13},{1... | collective-permute-start | bytes 1572872 | tf_op jit(solution)/shard_map/ppermute | solution.py:24
  29.4 12.5 %collective-permute-start.9 = (bf16[256,1024]{1,0:T(8,128)(2,1)}, bf16[256,1024]{1,0:T(8,128)(2,1)}, u32[]{:S(2)}, u32[]{:S(2)}) collective-permute-start(bf16[256,1024]{1,0:T(8,128)(2,1)} %collective-permute-done.8.refs_5_), channel_id=1, source_target_pairs={{0,1},{1,0},{2,3},{3,2},{4,5},{5,4},{6,7},{7,6},{8,9},{9,8},{10,11... | collective-permute-start | bytes 1572872 | tf_op jit(solution)/shard_map/ppermute | solution.py:24
  34.2 1.6 %collective-permute-start.5 = (bf16[64,1024]{1,0:T(8,128)(2,1)S(1)}, bf16[64,1024]{1,0:T(8,128)(2,1)S(1)}, u32[]{:S(2)}, u32[]{:S(2)}) collective-permute-start(bf16[64,1024]{1,0:T(8,128)(2,1)S(1)} %pad_maximum_fusion.1.refs_5_), channel_id=1, source_target_pairs={{0,1},{1,0},{2,3},{3,2},{4,5},{5,4},{6,7},{7,6},{8,9},{9,8},{10,11... | collective-permute-start | bytes 393224 | tf_op jit(solution)/shard_map/ppermute | solution.py:24
  37.2 2.4 %collective-permute-start.17 = (bf16[64,2048]{1,0:T(8,128)(2,1)}, bf16[64,2048]{1,0:T(8,128)(2,1)S(1)}, u32[]{:S(2)}, u32[]{:S(2)}) collective-permute-start(bf16[64,2048]{1,0:T(8,128)(2,1)} %collective-permute-done.16.refs_6_), channel_id=1, source_target_pairs={{0,1},{1,0},{2,3},{3,2},{4,5},{5,4},{6,7},{7,6},{8,9},{9,8},{10,11... | collective-permute-start | bytes 786440 | tf_op jit(solution)/shard_map/ppermute | solution.py:24
  37.7 7.4 %collective-permute-start.6 = (bf16[176,512]{1,0:T(8,128)(2,1)S(1)}, bf16[176,512]{1,0:T(8,128)(2,1)S(1)}, u32[]{:S(2)}, u32[]{:S(2)}) collective-permute-start(bf16[176,512]{1,0:T(8,128)(2,1)S(1)} %get-tuple-element.43), channel_id=1, source_target_pairs={{0,2},{1,3},{2,0},{3,1},{4,6},{5,7},{6,4},{7,5},{8,10},{9,11},{10,... | collective-permute-start | bytes 540680 | tf_op jit(solution)/shard_map/ppermute | solution.py:24
  39.1 8.9 %collective-permute-start.7 = (bf16[176,512]{1,0:T(8,128)(2,1)S(1)}, bf16[176,512]{1,0:T(8,128)(2,1)S(1)}, u32[]{:S(2)}, u32[]{:S(2)}) collective-permute-start(bf16[176,512]{1,0:T(8,128)(2,1)S(1)} %get-tuple-element.44), channel_id=1, source_target_pairs={{0,18},{1,19},{2,16},{3,17},{4,22},{5,23},{6,20},{7,21},{8,26},{9,... | collective-permute-start | bytes 540680 | tf_op jit(solution)/shard_map/ppermute | solution.py:24
  48.1 4.9 %collective-permute-start.13 = (bf16[256,1024]{1,0:T(8,128)(2,1)}, bf16[256,1024]{1,0:T(8,128)(2,1)S(1)}, u32[]{:S(2)}, u32[]{:S(2)}) collective-permute-start(bf16[256,1024]{1,0:T(8,128)(2,1)} %collective-permute-done.12.refs_5_), channel_id=1, source_target_pairs={{0,1},{1,0},{2,3},{3,2},{4,5},{5,4},{6,7},{7,6},{8,9},{9,8},{10,11... | collective-permute-start | bytes 1572872 | tf_op jit(solution)/shard_map/ppermute | solution.py:24
  48.1 16.6 %collective-permute-start.18 = (bf16[256,1024]{1,0:T(8,128)(2,1)}, bf16[256,1024]{1,0:T(8,128)(2,1)S(1)}, u32[]{:S(2)}, u32[]{:S(2)}) collective-permute-start(bf16[256,1024]{1,0:T(8,128)(2,1)} %collective-permute-done.12.refs_5_), channel_id=1, source_target_pairs={{0,4},{1,5},{2,6},{3,7},{4,8},{5,9},{6,10},{7,11},{8,12},{9,13},{1... | collective-permute-start | bytes 1572872 | tf_op jit(solution)/shard_map/ppermute | solution.py:24
  49.2 2.0 %collective-permute-start.19 = (bf16[64,2560]{1,0:T(8,128)(2,1)S(1)}, bf16[64,2560]{1,0:T(8,128)(2,1)S(1)}, u32[]{:S(2)}, u32[]{:S(2)}) collective-permute-start(bf16[64,2560]{1,0:T(8,128)(2,1)S(1)} %get-tuple-element.55), channel_id=1, source_target_pairs={{0,1},{1,0},{2,3},{3,2},{4,5},{5,4},{6,7},{7,6},{8,9},{9,8},{10,11... | collective-permute-start | bytes 983048 | tf_op jit(solution)/shard_map/ppermute | solution.py:24
  49.4 3.5 %collective-permute-start.20 = (bf16[64,2560]{1,0:T(8,128)(2,1)S(1)}, bf16[64,2560]{1,0:T(8,128)(2,1)S(1)}, u32[]{:S(2)}, u32[]{:S(2)}) collective-permute-start(bf16[64,2560]{1,0:T(8,128)(2,1)S(1)} %get-tuple-element.56), channel_id=1, source_target_pairs={{0,1},{1,0},{2,3},{3,2},{4,5},{5,4},{6,7},{7,6},{8,9},{9,8},{10,11... | collective-permute-start | bytes 983048 | tf_op jit(solution)/shard_map/ppermute | solution.py:24
  49.7 7.4 %collective-permute-start.10 = (bf16[176,512]{1,0:T(8,128)(2,1)S(1)}, bf16[176,512]{1,0:T(8,128)(2,1)S(1)}, u32[]{:S(2)}, u32[]{:S(2)}) collective-permute-start(bf16[176,512]{1,0:T(8,128)(2,1)S(1)} %get-tuple-element.46), channel_id=1, source_target_pairs={{0,2},{1,3},{2,0},{3,1},{4,6},{5,7},{6,4},{7,5},{8,10},{9,11},{10,... | collective-permute-start | bytes 540680 | tf_op jit(solution)/shard_map/ppermute | solution.py:24
  51.2 9.2 %collective-permute-start.11 = (bf16[176,512]{1,0:T(8,128)(2,1)S(1)}, bf16[176,512]{1,0:T(8,128)(2,1)S(1)}, u32[]{:S(2)}, u32[]{:S(2)}) collective-permute-start(bf16[176,512]{1,0:T(8,128)(2,1)S(1)} %get-tuple-element.47), channel_id=1, source_target_pairs={{0,18},{1,19},{2,16},{3,17},{4,22},{5,23},{6,20},{7,21},{8,26},{9,... | collective-permute-start | bytes 540680 | tf_op jit(solution)/shard_map/ppermute | solution.py:24
  64.7 5.3 %collective-permute-start.21 = (bf16[256,1024]{1,0:T(8,128)(2,1)S(1)}, bf16[256,1024]{1,0:T(8,128)(2,1)S(1)}, u32[]{:S(2)}, u32[]{:S(2)}) collective-permute-start(bf16[256,1024]{1,0:T(8,128)(2,1)S(1)} %collective-permute-done.18.refs_5_), channel_id=1, source_target_pairs={{0,1},{1,0},{2,3},{3,2},{4,5},{5,4},{6,7},{7,6},{8,9},{9,8},{10,11... | collective-permute-start | bytes 1572872 | tf_op jit(solution)/shard_map/ppermute | solution.py:24
  64.7 7.8 %collective-permute-start.14 = (bf16[176,512]{1,0:T(8,128)(2,1)S(1)}, bf16[176,512]{1,0:T(8,128)(2,1)S(1)}, u32[]{:S(2)}, u32[]{:S(2)}) collective-permute-start(bf16[176,512]{1,0:T(8,128)(2,1)S(1)} %get-tuple-element.50), channel_id=1, source_target_pairs={{0,2},{1,3},{2,0},{3,1},{4,6},{5,7},{6,4},{7,5},{8,10},{9,11},{10,... | collective-permute-start | bytes 540680 | tf_op jit(solution)/shard_map/ppermute | solution.py:24
  66.2 10.3 %collective-permute-start.15 = (bf16[176,512]{1,0:T(8,128)(2,1)S(1)}, bf16[176,512]{1,0:T(8,128)(2,1)S(1)}, u32[]{:S(2)}, u32[]{:S(2)}) collective-permute-start(bf16[176,512]{1,0:T(8,128)(2,1)S(1)} %get-tuple-element.51), channel_id=1, source_target_pairs={{0,18},{1,19},{2,16},{3,17},{4,22},{5,23},{6,20},{7,21},{8,26},{9,... | collective-permute-start | bytes 540680 | tf_op jit(solution)/shard_map/ppermute | solution.py:24
  67.7 10.8 %collective-permute-start.26 = (bf16[16,5120]{1,0:T(8,128)(2,1)S(1)}, bf16[16,5120]{1,0:T(8,128)(2,1)S(1)}, u32[]{:S(2)}, u32[]{:S(2)}) collective-permute-start(bf16[16,5120]{1,0:T(8,128)(2,1)S(1)} %get-tuple-element.68), channel_id=1, source_target_pairs={{0,4},{1,5},{2,6},{3,7},{4,8},{5,9},{6,10},{7,11},{8,12},{9,13},{1... | collective-permute-start | bytes 491528 | tf_op jit(solution)/shard_map/ppermute | solution.py:24
  67.7 15.0 %collective-permute-start.25 = (bf16[16,5120]{1,0:T(8,128)(2,1)S(1)}, bf16[16,5120]{1,0:T(8,128)(2,1)S(1)}, u32[]{:S(2)}, u32[]{:S(2)}) collective-permute-start(bf16[16,5120]{1,0:T(8,128)(2,1)S(1)} %get-tuple-element.66), channel_id=1, source_target_pairs={{0,8},{1,9},{2,10},{3,11},{4,12},{5,13},{6,14},{7,15},{8,0},{9,1},... | collective-permute-start | bytes 491528 | tf_op jit(solution)/shard_map/ppermute | solution.py:24
  70.0 12.7 %collective-permute-start.24 = (bf16[16,5120]{1,0:T(8,128)(2,1)S(1)}, bf16[16,5120]{1,0:T(8,128)(2,1)S(1)}, u32[]{:S(2)}, u32[]{:S(2)}) collective-permute-start(bf16[16,5120]{1,0:T(8,128)(2,1)S(1)} %get-tuple-element.64), channel_id=1, source_target_pairs={{0,12},{1,13},{2,14},{3,15},{4,0},{5,1},{6,2},{7,3},{8,4},{9,5},{1... | collective-permute-start | bytes 491528 | tf_op jit(solution)/shard_map/ppermute | solution.py:24
  76.5 8.5 %collective-permute-start.23 = (bf16[176,512]{1,0:T(8,128)(2,1)S(1)}, bf16[176,512]{1,0:T(8,128)(2,1)S(1)}, u32[]{:S(2)}, u32[]{:S(2)}) collective-permute-start(bf16[176,512]{1,0:T(8,128)(2,1)S(1)} %get-tuple-element.62), channel_id=1, source_target_pairs={{0,18},{1,19},{2,16},{3,17},{4,22},{5,23},{6,20},{7,21},{8,26},{9,... | collective-permute-start | bytes 540680 | tf_op jit(solution)/shard_map/ppermute | solution.py:24
  77.9 8.6 %collective-permute-start.22 = (bf16[176,512]{1,0:T(8,128)(2,1)S(1)}, bf16[176,512]{1,0:T(8,128)(2,1)S(1)}, u32[]{:S(2)}, u32[]{:S(2)}) collective-permute-start(bf16[176,512]{1,0:T(8,128)(2,1)S(1)} %get-tuple-element.60), channel_id=1, source_target_pairs={{0,2},{1,3},{2,0},{3,1},{4,6},{5,7},{6,4},{7,5},{8,10},{9,11},{10,... | collective-permute-start | bytes 540680 | tf_op jit(solution)/shard_map/ppermute | solution.py:24
  82.8 1.5 %collective-permute-start.27 = (bf16[16,5120]{1,0:T(8,128)(2,1)S(1)}, bf16[16,5120]{1,0:T(8,128)(2,1)S(1)}, u32[]{:S(2)}, u32[]{:S(2)}) collective-permute-start(bf16[16,5120]{1,0:T(8,128)(2,1)S(1)} %shard_map.103.refs_0_), channel_id=1, source_target_pairs={{0,1},{1,0},{2,3},{3,2},{4,5},{5,4},{6,7},{7,6},{8,9},{9,8},{10,11... | collective-permute-start | bytes 491528 | tf_op jit(solution)/shard_map/ppermute | solution.py:24
  (5 other events, 9.1 us)

commit v6 on v5

--- a/solution.py
+++ b/solution.py
@@ -36,11 +36,13 @@
     return lax.dot_general(a, b, (((0,), (0,)), ((), ())), preferred_element_type=F32)
 
 
-def call(kernel, out_shape, operands, scratch=()):
+def call(kernel, out_shape, operands, scratch=(), scalars=0):
     held = sum(x.size * x.dtype.itemsize for x in (*operands, *out_shape, *scratch))
     return pl.pallas_call(
         kernel,
         out_shape=out_shape,
+        in_specs=[pl.BlockSpec(memory_space=pltpu.VMEM)] * (len(operands) - scalars)
+        + [pl.BlockSpec(memory_space=pltpu.SMEM)] * scalars,
         scratch_shapes=[pltpu.VMEM(x.shape, x.dtype) for x in scratch],
         compiler_params=pltpu.CompilerParams(vmem_limit_bytes=2 * held + 4 * MIB),
         cost_estimate=pl.CostEstimate(flops=1000, bytes_accessed=1000, transcendentals=0),
@@ -51,12 +53,37 @@
     return tagged_ref[:, -LANES:].astype(F32)[:, :1]
 
 
+def row_slots(holders, replicas, slots, rank, dr):
+    here, core = lax.axis_index("adapter"), lax.axis_index("replica")
+    own_slots = slots // replicas
+    lane = lax.broadcasted_iota(jnp.int32, (1, holders * own_slots * rank), 1)
+    slot = jnp.zeros_like(lane)
+    for k in range(holders):
+        for j in range(own_slots):
+            start = (k * own_slots + j) * rank
+            value = lax.rem(here + holders - k, holders) * slots
+            value = value + lax.rem(core + replicas - dr, replicas) * own_slots + j
+            slot = jnp.where((lane >= start) & (lane < start + rank), value, slot)
+    return slot.astype(F32)
+
+
 def tag_kernel(g_ref, name_ref, slot_ref, out_ref):
     out_ref[:, :-LANES] = g_ref[...]
-    tokens, adapters = g_ref.shape[0], slot_ref.shape[1]
-    named = name_ref[...] == lax.broadcasted_iota(jnp.int32, (tokens, adapters), 1)
-    slot = jnp.sum(jnp.where(named, slot_ref[...], 0).astype(F32), axis=1, keepdims=True)
-    out_ref[:, -LANES:] = jnp.broadcast_to(slot, (tokens, LANES)).astype(BF16)
+    names = name_ref[...]
+    slot = jnp.zeros_like(names)
+    for j in range(slot_ref.shape[0]):
+        slot = jnp.where(names == j, slot_ref[j], slot)
+    ones = jnp.ones((1, LANES), F32)
+    out_ref[:, -LANES:] = columns_by_columns(slot.astype(F32), ones).astype(BF16)
+
+
+def join_kernel(*refs):
+    down_ref, up_ref = refs[-2:]
+    wide = down_ref.shape[1]
+    for k, ref in enumerate(refs[:-2]):
+        rows = ref.shape[0]
+        down_ref[k * rows : (k + 1) * rows] = ref[:, :wide]
+        up_ref[k * rows : (k + 1) * rows] = ref[:, wide:]
 
 
 def own_kernel(sizes, down_ref, up_ref, out_ref):
@@ -74,9 +101,9 @@
 
 
 def adapter_kernel(sizes, *refs):
-    groups, holders, replicas, shard = sizes
-    x_ref, g_ref, slot_ref, sel_ref = refs[:4]
-    map_refs, refs = refs[4 : 4 + groups * replicas], refs[4 + groups * replicas :]
+    groups, holders, replicas, shard, slots, rank = sizes
+    x_ref, g_ref, sel_ref = refs[:3]
+    map_refs, refs = refs[3 : 3 + groups * replicas], refs[3 + groups * replicas :]
     own_ref, other_refs, down = refs[0], refs[1:-1], refs[-1]
     group = lax.axis_index("groups")
     tokens, width = x_ref.shape
@@ -90,7 +117,8 @@
                 down[pl.ds(dr * rows, rows), pl.ds(at, half)] = map_refs[dg * replicas + dr][
                     :, z * half : (z + 1) * half
                 ]
-    keep = slots_of(g_ref) == slot_ref[...]
+    row_slot = [row_slots(holders, replicas, slots, rank, dr) for dr in range(replicas)]
+    keep = slots_of(g_ref) == jnp.concatenate(row_slot, axis=1)
     in_sel = jnp.where(keep, rows_by_rows(x_ref[...], down[...]), 0.0).astype(BF16)
     grad_sel = sel_ref[pl.ds(0, tokens), :]
     step, split = 1024, cols // 2
@@ -108,18 +136,18 @@
 
 
 def frozen_kernel(sizes, k, count, *refs):
-    tokens, groups, holders, replicas = sizes
+    tokens, groups, holders, replicas, slots, rank = sizes
     g_refs, refs = refs[:groups], refs[groups:]
     down_refs, refs = refs[:replicas], refs[replicas:]
     core, here = lax.axis_index("replica"), lax.axis_index("adapter")
     if k == 0:
-        slot_ref, up_refs, refs = refs[0], refs[1 : 1 + replicas], refs[1 + replicas :]
+        up_refs, refs = refs[:replicas], refs[replicas:]
         sel_ref = refs[-1]
         out_refs = refs[-1 - groups : -1]
         rows = up_refs[0].shape[0]
         for dg in range(groups):
             for dr in range(replicas):
-                keep = slots_of(g_refs[dg]) == slot_ref[:, dr * rows : (dr + 1) * rows]
+                keep = slots_of(g_refs[dg]) == row_slots(holders, replicas, slots, rank, dr)
                 proj_grad = rows_by_rows(g_refs[dg][:, :-LANES], up_refs[dr][...])
                 sel_ref[pl.ds(dg * tokens, tokens), dr * rows : (dr + 1) * rows] = jnp.where(
                     keep, proj_grad, 0.0
@@ -131,6 +159,8 @@
     half = down_refs[0].shape[1] // holders
     shard_at = lax.rem(here + holders - k, holders) * half
     for j, block in enumerate(refs[:count]):
+        if k == 0:
+            block = block.at[pl.ds(pl.multiple_of(lax.axis_index("groups") * half, half), half)]
         wide = block.shape[0]
         at = 0 if count == 1 else lax.rem(core + replicas - j, replicas) * wide
         columns = pl.ds(pl.multiple_of(shard_at + at, wide), wide)
@@ -219,7 +249,8 @@
     tagged = call(
         tag_kernel,
         [jax.ShapeDtypeStruct((tokens, value_width + LANES), BF16)],
-        (grad_rows, token_adapter_index[0], adapter_slot_index[None]),
+        (grad_rows, token_adapter_index[0, :, 0][None], adapter_slot_index),
+        scalars=1,
     )[0]
     grads = [tagged] + [
         moved(tagged, lambda g, z, s, r: (g - dg, z, s, r)) for dg in range(1, groups)
@@ -233,28 +264,26 @@
     held = [own]
     for k in range(1, holders):
         held.append(moved(own, lambda g, z, s, r: (g, z + k, s, r)))
-    held, grads = lax.optimization_barrier((held, grads))
-    ups = [jnp.concatenate([x[:, holders * half :] for x in held], axis=0)]
-    downs = [jnp.concatenate([x[:, : holders * half] for x in held], axis=0)]
+
+    ring = [lax.dynamic_slice_in_dim(frozen, (group * replicas + core) * piece, piece, axis=0)]
+    ring.append(moved(ring[0], lambda g, z, s, r: (g, z + 1, s, r)))
+    held, grads, ring = lax.optimization_barrier((held, grads, ring))
+    joined = call(
+        join_kernel,
+        [
+            jax.ShapeDtypeStruct((holders * rows, holders * half), BF16),
+            jax.ShapeDtypeStruct((holders * rows, value_width), BF16),
+        ],
+        held,
+    )
+    downs, ups = [joined[0]], [joined[1]]
     for dr in range(1, replicas):
         ups.append(moved(ups[0], lambda g, z, s, r: (g, z, s, r + dr)))
         downs.append(moved(downs[0], lambda g, z, s, r: (g, z, s, r + dr)))
     others = [moved(downs[0], lambda g, z, s, r: (g + dg, z, s, r)) for dg in range(1, groups)]
-    row_slot = jnp.concatenate(
-        [
-            ((here - k) % holders) * slots
-            + ((core - dr) % replicas) * own_slots
-            + jnp.arange(rows, dtype=jnp.int32) // rank
-            for dr in range(replicas)
-            for k in range(holders)
-        ]
-    ).astype(F32)[None]
-
-    mine = lax.dynamic_slice_in_dim(frozen, group * half, half, axis=0)
-    ring = [lax.dynamic_slice_in_dim(mine, core * piece, piece, axis=0)]
     def pieces_of(k, *before):
         if k == 0:
-            return [mine]
+            return [frozen]
         block = after(ring[k], *before) if before else ring[k]
         pieces = [block] + [
             moved(block, lambda g, z, s, r: (g, z, s, r + dr)) for dr in range(1, replicas)
@@ -276,10 +305,10 @@
             for dr in range(1, replicas):
                 maps.append(moved(maps[-dr], lambda g, z, s, r: (g, z, s, r + dr)))
         gradients = call(
-            functools.partial(adapter_kernel, (groups, holders, replicas, shard)),
+            functools.partial(adapter_kernel, (groups, holders, replicas, shard, slots, rank)),
             [jax.ShapeDtypeStruct((holders * rows, cols), F32)]
             + [jax.ShapeDtypeStruct((holders * rows, cols // 2), BF16)] * (2 * replicas - 2),
-            (inputs, tagged, row_slot, sel, *maps),
+            (inputs, tagged, sel, *maps),
             [jax.ShapeDtypeStruct((kept, width), BF16)],
         )
         part, sent = gradients[0], gradients[1:]
@@ -298,20 +327,21 @@
 
     arrived, outs = [], []
     for k in range(holders):
-        if k:
+        if k > 1:
             last = ring[-1]
-            if k == 2:
-                last = after(last, downs[0])
-            elif k > 2:
+            if k > 2:
                 last = after(last, *outs[k - 2], part)
             ring.append(moved(last, lambda g, z, s, r: (g, z + 1, s, r)))
         gate = [*arrived[k - 2], *outs[k - 1]] if k > 1 else []
         blocks = pieces_of(k, *gate, *(chip[:1] if k > 2 else ()))
+        tokens_in = [after(tagged, part), *grads[1:]] if k == 1 else grads
         out = call(
-            functools.partial(frozen_kernel, (tokens, groups, holders, replicas), k, len(blocks)),
+            functools.partial(
+                frozen_kernel, (tokens, groups, holders, replicas, slots, rank), k, len(blocks)
+            ),
             [jax.ShapeDtypeStruct((tokens, half), BF16)] * groups
             + [jax.ShapeDtypeStruct((groups * tokens, kept), BF16)] * (k == 0),
-            [*grads, *downs, *([sel] if k else [row_slot, *ups]), *blocks],
+            [*tokens_in, *downs, *([sel] if k else ups), *blocks],
         )
         if k == 0:
             sel = out[groups]

time: 88.2 us -> 85.4 us (0.968)
  starting transfers between devices: 27.6 us -> 32.1 us
  local copies, waits for them, and re-layouts: 8.98 us -> 5.34 us
  Pallas kernels: 11.3 us -> 8.79 us
  other arithmetic: 1.2 us -> 0 us
    ppermute x28, starting transfers between devices: 27.6 us -> 32.1 us  [moved(): return lax.ppermute(x, AXES, pairs)]
    pallas_call x11 -> x12, Pallas kernels: 11.3 us -> 8.79 us  [call(): pl.pallas_call(kernel, out_shape=out_shape, in_specs=[pl.BlockSpec(memory...]
    slice x8 -> x0, local copies, waits for them, and re-layouts: 2.31 us -> none  [the longest x4 2.28 us: on_device(): ups = [jnp.concatenate([x[:, holders * half:] for x in held], axis=0)]]
    concatenate x1 -> x0, local copies, waits for them, and re-layouts: 1.3 us -> none  [on_device(): jnp.concatenate([(here - k) % holders * slots + (core - dr) % replicas *...]
    unnamed x18 -> x14, local copies, waits for them, and re-layouts: 3.6 us -> 4.11 us
  transfers between devices with their start and end apart: 28 -> 28, of which waited for: 12 -> 14; matrix products, arithmetic and copies ran while one was open for 8% -> 0% of each run, Pallas kernels for 12% -> 9%
where the time goes in v6:
time: 85.4 us; the launch traced here: 85.2 us
  waiting for transfers between devices  38.1 us (45%)
  starting transfers between devices  32.1 us (38%)
  Pallas kernels  8.79 us (10%)
  local copies, waits for them, and re-layouts  5.34 us (6%)
    ppermute x28, waiting for transfers between devices, moved(): return lax.ppermute(x, AXES, pairs)  38.1 us
    ppermute x28, starting transfers between devices, moved(): return lax.ppermute(x, AXES, pairs)  32.1 us
    pallas_call x12, Pallas kernels, call(): pl.pallas_call(kernel, out_shape=out_shape, in_specs=[pl.BlockSpec(memory...  8.79 us
    unnamed x14, local copies, waits for them, and re-layouts  4.11 us
  transfers between devices with their start and end apart: 28, of which 14 were waited for; matrix products, arithmetic and copies ran while one was open for 0% of the time, Pallas kernels for 9%

profile of v6, /device:TPU:0, one launch (start us, length us, event | category | flops | bytes accessed | tf_op | source)
XLA Modules:
  0.0 85.2 jit_solution(1138087525546186154)
XLA Ops:
  0.6 1.2 %dynamic-slice_bitcast_fusion = bf16[256,1024]{1,0:T(8,128)(2,1)S(1)} fusion(bf16[1,1024,1024]{2,1,0:T(8,128)(2,1)} %param.11, s32[]{:T(128)S(6)} %select_n.3), kind=kLoop, calls=%fused_computation | loop fusion | bytes 1048580 | tf_op jit(solution)/shard_map/dynamic_slice | solution.py:268
  1.9 3.1 %collective-permute-start.4 = (bf16[256,1024]{1,0:T(8,128)(2,1)S(1)}, bf16[256,1024]{1,0:T(8,128)(2,1)S(1)}, u32[]{:S(2)}, u32[]{:S(2)}) collective-permute-start(bf16[256,1024]{1,0:T(8,128)(2,1)S(1)} %dynamic-slice_bitcast_fusion), channel_id=1, source_target_pairs={{0,4},{1,5},{2,6},{3,7},{4,8},{5,9},{6,10},{7,11},{8,12},{9,13},{1... | collective-permute-start | bytes 1572872 | tf_op jit(solution)/shard_map/ppermute | solution.py:24
  8.0 1.6 %collective-permute-start.3 = (bf16[176,1152]{1,0:T(8,128)(2,1)S(1)}, bf16[176,1152]{1,0:T(8,128)(2,1)S(1)}, u32[]{:S(2)}, u32[]{:S(2)}) collective-permute-start(bf16[176,1152]{1,0:T(8,128)(2,1)S(1)} %shard_map.95.refs_0_.refs_1_), channel_id=1, source_target_pairs={{0,16},{1,17},{2,18},{3,19},{4,20},{5,21},{6,22},{7,23},{8,24},{9,... | collective-permute-start | bytes 1216520 | tf_op jit(solution)/shard_map/ppermute | solution.py:24
  11.4 1.6 %collective-permute-start = (bf16[16,3072]{1,0:T(8,128)(2,1)S(1)}, bf16[16,3072]{1,0:T(8,128)(2,1)S(1)}, u32[]{:S(2)}, u32[]{:S(2)}) collective-permute-start(bf16[16,3072]{1,0:T(8,128)(2,1)S(1)} %shard_map.94.refs_0_), channel_id=1, source_target_pairs={{0,4},{1,5},{2,6},{3,7},{4,8},{5,9},{6,10},{7,11},{8,12},{9,13},{1... | collective-permute-start | bytes 294920 | tf_op jit(solution)/shard_map/ppermute | solution.py:24
  13.1 1.2 %collective-permute-start.1 = (bf16[16,3072]{1,0:T(8,128)(2,1)S(1)}, bf16[16,3072]{1,0:T(8,128)(2,1)S(1)}, u32[]{:S(2)}, u32[]{:S(2)}) collective-permute-start(bf16[16,3072]{1,0:T(8,128)(2,1)S(1)} %shard_map.94.refs_0_), channel_id=1, source_target_pairs={{0,8},{1,9},{2,10},{3,11},{4,12},{5,13},{6,14},{7,15},{8,0},{9,1},... | collective-permute-start | bytes 294920 | tf_op jit(solution)/shard_map/ppermute | solution.py:24
  14.3 2.7 %collective-permute-start.2 = (bf16[16,3072]{1,0:T(8,128)(2,1)S(1)}, bf16[16,3072]{1,0:T(8,128)(2,1)S(1)}, u32[]{:S(2)}, u32[]{:S(2)}) collective-permute-start(bf16[16,3072]{1,0:T(8,128)(2,1)S(1)} %shard_map.94.refs_0_), channel_id=1, source_target_pairs={{0,12},{1,13},{2,14},{3,15},{4,0},{5,1},{6,2},{7,3},{8,4},{9,5},{1... | collective-permute-start | bytes 294920 | tf_op jit(solution)/shard_map/ppermute | solution.py:24
  17.0 5.0 %collective-permute-done.refs_1_ = bf16[16,3072]{1,0:T(8,128)(2,1)S(1)} collective-permute-done((bf16[16,3072]{1,0:T(8,128)(2,1)S(1)}, bf16[16,3072]{1,0:T(8,128)(2,1)S(1)}, u32[]{:S(2)}, u32[]{:S(2)}) %collective-permute-start) | collective-permute-done | bytes 98336 | tf_op jit(solution)/shard_map/ppermute | solution.py:24
  22.0 3.4 %collective-permute-done.1.refs_2_ = bf16[16,3072]{1,0:T(8,128)(2,1)S(1)} collective-permute-done((bf16[16,3072]{1,0:T(8,128)(2,1)S(1)}, bf16[16,3072]{1,0:T(8,128)(2,1)S(1)}, u32[]{:S(2)}, u32[]{:S(2)}) %collective-permute-start.1) | collective-permute-done | bytes 98336 | tf_op jit(solution)/shard_map/ppermute | solution.py:24
  25.5 1.6 %collective-permute-start.9 = (bf16[64,2048]{1,0:T(8,128)(2,1)S(1)}, bf16[64,2048]{1,0:T(8,128)(2,1)S(1)}, u32[]{:S(2)}, u32[]{:S(2)}) collective-permute-start(bf16[64,2048]{1,0:T(8,128)(2,1)S(1)} %get-tuple-element.46.refs_2_.refs_3_), channel_id=1, source_target_pairs={{0,16},{1,17},{2,18},{3,19},{4,20},{5,21},{6,22},{7,23},{8,24},{9,... | collective-permute-start | bytes 786440 | tf_op jit(solution)/shard_map/ppermute | solution.py:24
  27.2 2.6 %collective-permute-start.14 = (bf16[256,1024]{1,0:T(8,128)(2,1)S(1)}, bf16[256,1024]{1,0:T(8,128)(2,1)S(1)}, u32[]{:S(2)}, u32[]{:S(2)}) collective-permute-start(bf16[256,1024]{1,0:T(8,128)(2,1)S(1)} %collective-permute-done.4.refs_5_), channel_id=1, source_target_pairs={{0,4},{1,5},{2,6},{3,7},{4,8},{5,9},{6,10},{7,11},{8,12},{9,13},{1... | collective-permute-start | bytes 1572872 | tf_op jit(solution)/shard_map/ppermute | solution.py:24
  29.9 1.3 %collective-permute-done.6.refs_5_ = bf16[64,1024]{1,0:T(8,128)(2,1)S(1)} collective-permute-done((bf16[64,1024]{1,0:T(8,128)(2,1)S(1)}, bf16[64,1024]{1,0:T(8,128)(2,1)S(1)}, u32[]{:S(2)}, u32[]{:S(2)}) %collective-permute-start.6) | collective-permute-done | bytes 131104 | tf_op jit(solution)/shard_map/ppermute | solution.py:24
  31.2 1.5 %shard_map.97 = (bf16[176,512]{1,0:T(8,128)(2,1)S(1)}, bf16[176,512]{1,0:T(8,128)(2,1)S(1)}, bf16[352,128]{1,0:T(8,128)(2,1)S(1)}) custom-call(bf16[176,1152]{1,0:T(8,128)(2,1)S(1)} %shard_map.95.refs_0_.refs_1_, bf16[176,1152]{1,0:T(8,128)(2,1)S(1)} %collective-permute-done.3.refs_1_, bf16[64,2048]{1,0:T(8,128)(2,1)S(1)} %get-tuple-element.46.refs_2_.refs_3_, ...), custom_call_target="tpu_custom_call" | custom-call | flops 1000 | bytes 1000 | tf_op jit(solution)/shard_map/pallas_call | solution.py:41
  32.6 1.6 %collective-permute-done.9.refs_5_ = bf16[64,2048]{1,0:T(8,128)(2,1)S(1)} collective-permute-done((bf16[64,2048]{1,0:T(8,128)(2,1)S(1)}, bf16[64,2048]{1,0:T(8,128)(2,1)S(1)}, u32[]{:S(2)}, u32[]{:S(2)}) %collective-permute-start.9) | collective-permute-done | bytes 262176 | tf_op jit(solution)/shard_map/ppermute | solution.py:24
  34.2 1.5 %collective-permute-start.7 = (bf16[176,512]{1,0:T(8,128)(2,1)S(1)}, bf16[176,512]{1,0:T(8,128)(2,1)S(1)}, u32[]{:S(2)}, u32[]{:S(2)}) collective-permute-start(bf16[176,512]{1,0:T(8,128)(2,1)S(1)} %get-tuple-element.48), channel_id=1, source_target_pairs={{0,2},{1,3},{2,0},{3,1},{4,6},{5,7},{6,4},{7,5},{8,10},{9,11},{10,... | collective-permute-start | bytes 540680 | tf_op jit(solution)/shard_map/ppermute | solution.py:24
  35.7 1.5 %collective-permute-start.8 = (bf16[176,512]{1,0:T(8,128)(2,1)S(1)}, bf16[176,512]{1,0:T(8,128)(2,1)S(1)}, u32[]{:S(2)}, u32[]{:S(2)}) collective-permute-start(bf16[176,512]{1,0:T(8,128)(2,1)S(1)} %get-tuple-element.49), channel_id=1, source_target_pairs={{0,18},{1,19},{2,16},{3,17},{4,22},{5,23},{6,20},{7,21},{8,26},{9,... | collective-permute-start | bytes 540680 | tf_op jit(solution)/shard_map/ppermute | solution.py:24
  37.2 1.3 %shard_map.98 = (f32[64,5120]{1,0:T(8,128)S(1)}, bf16[64,2560]{1,0:T(8,128)(2,1)S(1)}, bf16[64,2560]{1,0:T(8,128)(2,1)S(1)}) custom-call(bf16[176,4096]{1,0:T(8,128)(2,1)S(1)} %bitcast.12, bf16[176,1152]{1,0:T(8,128)(2,1)S(1)} %shard_map.95.refs_0_.refs_1_, bf16[352,128]{1,0:T(8,128)(2,1)S(1)} %get-tuple-element.50.refs_2_.refs_4_, ...), custom_call_target="tpu_custom_call" | custom-call | flops 1000 | bytes 1000 | tf_op jit(solution)/shard_map/pallas_call | solution.py:41
  39.5 2.0 %collective-permute-done.7.refs_0_ = bf16[176,512]{1,0:T(8,128)(2,1)S(1)} collective-permute-done((bf16[176,512]{1,0:T(8,128)(2,1)S(1)}, bf16[176,512]{1,0:T(8,128)(2,1)S(1)}, u32[]{:S(2)}, u32[]{:S(2)}) %collective-permute-start.7) | collective-permute-done | bytes 180256 | tf_op jit(solution)/shard_map/ppermute | solution.py:24
  41.6 4.4 %collective-permute-done.8.refs_1_ = bf16[176,512]{1,0:T(8,128)(2,1)S(1)} collective-permute-done((bf16[176,512]{1,0:T(8,128)(2,1)S(1)}, bf16[176,512]{1,0:T(8,128)(2,1)S(1)}, u32[]{:S(2)}, u32[]{:S(2)}) %collective-permute-start.8) | collective-permute-done | bytes 180256 | tf_op jit(solution)/shard_map/ppermute | solution.py:24
  46.0 2.6 %collective-permute-start.18 = (bf16[256,1024]{1,0:T(8,128)(2,1)S(1)}, bf16[256,1024]{1,0:T(8,128)(2,1)S(1)}, u32[]{:S(2)}, u32[]{:S(2)}) collective-permute-start(bf16[256,1024]{1,0:T(8,128)(2,1)S(1)} %collective-permute-done.14.refs_5_), channel_id=1, source_target_pairs={{0,4},{1,5},{2,6},{3,7},{4,8},{5,9},{6,10},{7,11},{8,12},{9,13},{1... | collective-permute-start | bytes 1572872 | tf_op jit(solution)/shard_map/ppermute | solution.py:24
  49.1 1.5 %collective-permute-start.12 = (bf16[176,512]{1,0:T(8,128)(2,1)S(1)}, bf16[176,512]{1,0:T(8,128)(2,1)S(1)}, u32[]{:S(2)}, u32[]{:S(2)}) collective-permute-start(bf16[176,512]{1,0:T(8,128)(2,1)S(1)} %get-tuple-element.55), channel_id=1, source_target_pairs={{0,2},{1,3},{2,0},{3,1},{4,6},{5,7},{6,4},{7,5},{8,10},{9,11},{10,... | collective-permute-start | bytes 540680 | tf_op jit(solution)/shard_map/ppermute | solution.py:24
  52.8 3.6 %collective-permute-done.12.refs_2_ = bf16[176,512]{1,0:T(8,128)(2,1)S(1)} collective-permute-done((bf16[176,512]{1,0:T(8,128)(2,1)S(1)}, bf16[176,512]{1,0:T(8,128)(2,1)S(1)}, u32[]{:S(2)}, u32[]{:S(2)}) %collective-permute-start.12) | collective-permute-done | bytes 180256 | tf_op jit(solution)/shard_map/ppermute | solution.py:24
  56.5 3.1 %collective-permute-done.13.refs_3_ = bf16[176,512]{1,0:T(8,128)(2,1)S(1)} collective-permute-done((bf16[176,512]{1,0:T(8,128)(2,1)S(1)}, bf16[176,512]{1,0:T(8,128)(2,1)S(1)}, u32[]{:S(2)}, u32[]{:S(2)}) %collective-permute-start.13) | collective-permute-done | bytes 180256 | tf_op jit(solution)/shard_map/ppermute | solution.py:24
  59.6 2.6 %collective-permute-done.18.refs_5_ = bf16[256,1024]{1,0:T(8,128)(2,1)S(1)} collective-permute-done((bf16[256,1024]{1,0:T(8,128)(2,1)S(1)}, bf16[256,1024]{1,0:T(8,128)(2,1)S(1)}, u32[]{:S(2)}, u32[]{:S(2)}) %collective-permute-start.18) | collective-permute-done | bytes 524320 | tf_op jit(solution)/shard_map/ppermute | solution.py:24
  62.2 1.5 %collective-permute-start.16 = (bf16[176,512]{1,0:T(8,128)(2,1)S(1)}, bf16[176,512]{1,0:T(8,128)(2,1)S(1)}, u32[]{:S(2)}, u32[]{:S(2)}) collective-permute-start(bf16[176,512]{1,0:T(8,128)(2,1)S(1)} %get-tuple-element.58), channel_id=1, source_target_pairs={{0,2},{1,3},{2,0},{3,1},{4,6},{5,7},{6,4},{7,5},{8,10},{9,11},{10,... | collective-permute-start | bytes 540680 | tf_op jit(solution)/shard_map/ppermute | solution.py:24
  64.9 1.6 %collective-permute-start.25 = (bf16[16,5120]{1,0:T(8,128)(2,1)S(1)}, bf16[16,5120]{1,0:T(8,128)(2,1)S(1)}, u32[]{:S(2)}, u32[]{:S(2)}) collective-permute-start(bf16[16,5120]{1,0:T(8,128)(2,1)S(1)} %get-tuple-element.72), channel_id=1, source_target_pairs={{0,8},{1,9},{2,10},{3,11},{4,12},{5,13},{6,14},{7,15},{8,0},{9,1},... | collective-permute-start | bytes 491528 | tf_op jit(solution)/shard_map/ppermute | solution.py:24
  66.5 1.5 %collective-permute-start.24 = (bf16[16,5120]{1,0:T(8,128)(2,1)S(1)}, bf16[16,5120]{1,0:T(8,128)(2,1)S(1)}, u32[]{:S(2)}, u32[]{:S(2)}) collective-permute-start(bf16[16,5120]{1,0:T(8,128)(2,1)S(1)} %get-tuple-element.70), channel_id=1, source_target_pairs={{0,12},{1,13},{2,14},{3,15},{4,0},{5,1},{6,2},{7,3},{8,4},{9,5},{1... | collective-permute-start | bytes 491528 | tf_op jit(solution)/shard_map/ppermute | solution.py:24
  69.5 3.4 %collective-permute-done.17.refs_5_ = bf16[176,512]{1,0:T(8,128)(2,1)S(1)} collective-permute-done((bf16[176,512]{1,0:T(8,128)(2,1)S(1)}, bf16[176,512]{1,0:T(8,128)(2,1)S(1)}, u32[]{:S(2)}, u32[]{:S(2)}) %collective-permute-start.17) | collective-permute-done | bytes 180256 | tf_op jit(solution)/shard_map/ppermute | solution.py:24
  73.0 2.4 %collective-permute-start.23 = (bf16[176,512]{1,0:T(8,128)(2,1)S(1)}, bf16[176,512]{1,0:T(8,128)(2,1)S(1)}, u32[]{:S(2)}, u32[]{:S(2)}) collective-permute-start(bf16[176,512]{1,0:T(8,128)(2,1)S(1)} %get-tuple-element.68), channel_id=1, source_target_pairs={{0,18},{1,19},{2,16},{3,17},{4,22},{5,23},{6,20},{7,21},{8,26},{9,... | collective-permute-start | bytes 540680 | tf_op jit(solution)/shard_map/ppermute | solution.py:24
  75.9 3.3 %collective-permute-done.25.refs_2_ = bf16[16,5120]{1,0:T(8,128)(2,1)S(1)} collective-permute-done((bf16[16,5120]{1,0:T(8,128)(2,1)S(1)}, bf16[16,5120]{1,0:T(8,128)(2,1)S(1)}, u32[]{:S(2)}, u32[]{:S(2)}) %collective-permute-start.25) | collective-permute-done | bytes 163872 | tf_op jit(solution)/shard_map/ppermute | solution.py:24
  79.4 1.4 %collective-permute-done.27.refs_1_ = bf16[16,5120]{1,0:T(8,128)(2,1)S(1)} collective-permute-done((bf16[16,5120]{1,0:T(8,128)(2,1)S(1)}, bf16[16,5120]{1,0:T(8,128)(2,1)S(1)}, u32[]{:S(2)}, u32[]{:S(2)}) %collective-permute-start.27) | collective-permute-done | bytes 163872 | tf_op jit(solution)/shard_map/ppermute | solution.py:24
  81.5 2.4 %collective-permute-done.22.refs_6_ = bf16[176,512]{1,0:T(8,128)(2,1)S(1)} collective-permute-done((bf16[176,512]{1,0:T(8,128)(2,1)S(1)}, bf16[176,512]{1,0:T(8,128)(2,1)S(1)}, u32[]{:S(2)}, u32[]{:S(2)}) %collective-permute-start.22) | collective-permute-done | bytes 180256 | tf_op jit(solution)/shard_map/ppermute | solution.py:24
  84.0 1.2 %shard_map.103 = bf16[176,4096]{1,0:T(8,128)(2,1)} custom-call(bf16[176,512]{1,0:T(8,128)(2,1)S(1)} %collective-permute-done.7.refs_0_, bf16[176,512]{1,0:T(8,128)(2,1)S(1)} %collective-permute-done.8.refs_1_, bf16[176,512]{1,0:T(8,128)(2,1)S(1)} %collective-permute-done.12.refs_2_, bf16[176,512]{1,0:T(8,128)(2,1)S(1)} %collective-permute-done.13.refs_3_, ...), custom_call_target="tpu_custom_call" | custom-call | flops 1000 | bytes 1000 | tf_op jit(solution)/shard_map/pallas_call | solution.py:41
  (51 shorter events, 13.2 us)
Async XLA Ops:
  0.6 30.5 %copy-start = (bf16[1,1024,1024]{2,1,0:T(8,128)(2,1)S(1)}, bf16[1,1024,1024]{2,1,0:T(8,128)(2,1)}, u32[]{:S(2)}) copy-start(bf16[1,1024,1024]{2,1,0:T(8,128)(2,1)} %param.11) | copy-start | bytes 6291460
  1.9 23.5 %collective-permute-start.4 = (bf16[256,1024]{1,0:T(8,128)(2,1)S(1)}, bf16[256,1024]{1,0:T(8,128)(2,1)S(1)}, u32[]{:S(2)}, u32[]{:S(2)}) collective-permute-start(bf16[256,1024]{1,0:T(8,128)(2,1)S(1)} %dynamic-slice_bitcast_fusion), channel_id=1, source_target_pairs={{0,4},{1,5},{2,6},{3,7},{4,8},{5,9},{6,10},{7,11},{8,12},{9,13},{1... | collective-permute-start | bytes 1572872 | tf_op jit(solution)/shard_map/ppermute | solution.py:24
  5.0 1.0 %copy-start.2 = (bf16[1,176,1024]{2,1,0:T(8,128)(2,1)S(1)}, bf16[1,176,1024]{2,1,0:T(8,128)(2,1)}, u32[]{:S(2)}) copy-start(bf16[1,176,1024]{2,1,0:T(8,128)(2,1)} %param.8) | copy-start | bytes 1081348
  8.0 17.3 %collective-permute-start.3 = (bf16[176,1152]{1,0:T(8,128)(2,1)S(1)}, bf16[176,1152]{1,0:T(8,128)(2,1)S(1)}, u32[]{:S(2)}, u32[]{:S(2)}) collective-permute-start(bf16[176,1152]{1,0:T(8,128)(2,1)S(1)} %shard_map.95.refs_0_.refs_1_), channel_id=1, source_target_pairs={{0,16},{1,17},{2,18},{3,19},{4,20},{5,21},{6,22},{7,23},{8,24},{9,... | collective-permute-start | bytes 1216520 | tf_op jit(solution)/shard_map/ppermute | solution.py:24
  9.6 0.9 %copy-start.3 = (bf16[1,2,16,4096]{3,2,1,0:T(8,128)(2,1)S(1)}, bf16[1,2,16,4096]{3,2,1,0:T(8,128)(2,1)}, u32[]{:S(2)}) copy-start(bf16[1,2,16,4096]{3,2,1,0:T(8,128)(2,1)} %param.12) | copy-start | bytes 786436
  11.4 10.5 %collective-permute-start = (bf16[16,3072]{1,0:T(8,128)(2,1)S(1)}, bf16[16,3072]{1,0:T(8,128)(2,1)S(1)}, u32[]{:S(2)}, u32[]{:S(2)}) collective-permute-start(bf16[16,3072]{1,0:T(8,128)(2,1)S(1)} %shard_map.94.refs_0_), channel_id=1, source_target_pairs={{0,4},{1,5},{2,6},{3,7},{4,8},{5,9},{6,10},{7,11},{8,12},{9,13},{1... | collective-permute-start | bytes 294920 | tf_op jit(solution)/shard_map/ppermute | solution.py:24
  13.1 12.3 %collective-permute-start.1 = (bf16[16,3072]{1,0:T(8,128)(2,1)S(1)}, bf16[16,3072]{1,0:T(8,128)(2,1)S(1)}, u32[]{:S(2)}, u32[]{:S(2)}) collective-permute-start(bf16[16,3072]{1,0:T(8,128)(2,1)S(1)} %shard_map.94.refs_0_), channel_id=1, source_target_pairs={{0,8},{1,9},{2,10},{3,11},{4,12},{5,13},{6,14},{7,15},{8,0},{9,1},... | collective-permute-start | bytes 294920 | tf_op jit(solution)/shard_map/ppermute | solution.py:24
  14.3 11.1 %collective-permute-start.2 = (bf16[16,3072]{1,0:T(8,128)(2,1)S(1)}, bf16[16,3072]{1,0:T(8,128)(2,1)S(1)}, u32[]{:S(2)}, u32[]{:S(2)}) collective-permute-start(bf16[16,3072]{1,0:T(8,128)(2,1)S(1)} %shard_map.94.refs_0_), channel_id=1, source_target_pairs={{0,12},{1,13},{2,14},{3,15},{4,0},{5,1},{6,2},{7,3},{8,4},{9,5},{1... | collective-permute-start | bytes 294920 | tf_op jit(solution)/shard_map/ppermute | solution.py:24
  25.4 5.7 %collective-permute-start.5 = (bf16[64,2048]{1,0:T(8,128)(2,1)S(1)}, bf16[64,2048]{1,0:T(8,128)(2,1)S(1)}, u32[]{:S(2)}, u32[]{:S(2)}) collective-permute-start(bf16[64,2048]{1,0:T(8,128)(2,1)S(1)} %get-tuple-element.46.refs_2_.refs_3_), channel_id=1, source_target_pairs={{0,1},{1,0},{2,3},{3,2},{4,5},{5,4},{6,7},{7,6},{8,9},{9,8},{10,11... | collective-permute-start | bytes 786440 | tf_op jit(solution)/shard_map/ppermute | solution.py:24
  25.5 8.7 %collective-permute-start.9 = (bf16[64,2048]{1,0:T(8,128)(2,1)S(1)}, bf16[64,2048]{1,0:T(8,128)(2,1)S(1)}, u32[]{:S(2)}, u32[]{:S(2)}) collective-permute-start(bf16[64,2048]{1,0:T(8,128)(2,1)S(1)} %get-tuple-element.46.refs_2_.refs_3_), channel_id=1, source_target_pairs={{0,16},{1,17},{2,18},{3,19},{4,20},{5,21},{6,22},{7,23},{8,24},{9,... | collective-permute-start | bytes 786440 | tf_op jit(solution)/shard_map/ppermute | solution.py:24
  27.1 11.4 %collective-permute-start.11 = (bf16[256,1024]{1,0:T(8,128)(2,1)S(1)}, bf16[256,1024]{1,0:T(8,128)(2,1)S(1)}, u32[]{:S(2)}, u32[]{:S(2)}) collective-permute-start(bf16[256,1024]{1,0:T(8,128)(2,1)S(1)} %collective-permute-done.4.refs_5_), channel_id=1, source_target_pairs={{0,1},{1,0},{2,3},{3,2},{4,5},{5,4},{6,7},{7,6},{8,9},{9,8},{10,11... | collective-permute-start | bytes 1572872 | tf_op jit(solution)/shard_map/ppermute | solution.py:24
  27.2 18.8 %collective-permute-start.14 = (bf16[256,1024]{1,0:T(8,128)(2,1)S(1)}, bf16[256,1024]{1,0:T(8,128)(2,1)S(1)}, u32[]{:S(2)}, u32[]{:S(2)}) collective-permute-start(bf16[256,1024]{1,0:T(8,128)(2,1)S(1)} %collective-permute-done.4.refs_5_), channel_id=1, source_target_pairs={{0,4},{1,5},{2,6},{3,7},{4,8},{5,9},{6,10},{7,11},{8,12},{9,13},{1... | collective-permute-start | bytes 1572872 | tf_op jit(solution)/shard_map/ppermute | solution.py:24
  29.8 1.3 %collective-permute-start.6 = (bf16[64,1024]{1,0:T(8,128)(2,1)S(1)}, bf16[64,1024]{1,0:T(8,128)(2,1)S(1)}, u32[]{:S(2)}, u32[]{:S(2)}) collective-permute-start(bf16[64,1024]{1,0:T(8,128)(2,1)S(1)} %get-tuple-element.47.refs_4_), channel_id=1, source_target_pairs={{0,1},{1,0},{2,3},{3,2},{4,5},{5,4},{6,7},{7,6},{8,9},{9,8},{10,11... | collective-permute-start | bytes 393224 | tf_op jit(solution)/shard_map/ppermute | solution.py:24
  31.2 6.0 %copy-start.1 = (bf16[1,176,4096]{2,1,0:T(8,128)(2,1)S(1)}, bf16[1,176,4096]{2,1,0:T(8,128)(2,1)}, u32[]{:S(2)}) copy-start(bf16[1,176,4096]{2,1,0:T(8,128)(2,1)} %param.7) | copy-start | bytes 4325380
  34.2 3.0 %collective-permute-start.10 = (bf16[64,2048]{1,0:T(8,128)(2,1)S(1)}, bf16[64,2048]{1,0:T(8,128)(2,1)S(1)}, u32[]{:S(2)}, u32[]{:S(2)}) collective-permute-start(bf16[64,2048]{1,0:T(8,128)(2,1)S(1)} %collective-permute-done.9.refs_5_), channel_id=1, source_target_pairs={{0,1},{1,0},{2,3},{3,2},{4,5},{5,4},{6,7},{7,6},{8,9},{9,8},{10,11... | collective-permute-start | bytes 786440 | tf_op jit(solution)/shard_map/ppermute | solution.py:24
  34.2 7.3 %collective-permute-start.7 = (bf16[176,512]{1,0:T(8,128)(2,1)S(1)}, bf16[176,512]{1,0:T(8,128)(2,1)S(1)}, u32[]{:S(2)}, u32[]{:S(2)}) collective-permute-start(bf16[176,512]{1,0:T(8,128)(2,1)S(1)} %get-tuple-element.48), channel_id=1, source_target_pairs={{0,2},{1,3},{2,0},{3,1},{4,6},{5,7},{6,4},{7,5},{8,10},{9,11},{10,... | collective-permute-start | bytes 540680 | tf_op jit(solution)/shard_map/ppermute | solution.py:24
  35.7 10.3 %collective-permute-start.8 = (bf16[176,512]{1,0:T(8,128)(2,1)S(1)}, bf16[176,512]{1,0:T(8,128)(2,1)S(1)}, u32[]{:S(2)}, u32[]{:S(2)}) collective-permute-start(bf16[176,512]{1,0:T(8,128)(2,1)S(1)} %get-tuple-element.49), channel_id=1, source_target_pairs={{0,18},{1,19},{2,16},{3,17},{4,22},{5,23},{6,20},{7,21},{8,26},{9,... | collective-permute-start | bytes 540680 | tf_op jit(solution)/shard_map/ppermute | solution.py:24
  46.0 5.8 %collective-permute-start.15 = (bf16[256,1024]{1,0:T(8,128)(2,1)S(1)}, bf16[256,1024]{1,0:T(8,128)(2,1)S(1)}, u32[]{:S(2)}, u32[]{:S(2)}) collective-permute-start(bf16[256,1024]{1,0:T(8,128)(2,1)S(1)} %collective-permute-done.14.refs_5_), channel_id=1, source_target_pairs={{0,1},{1,0},{2,3},{3,2},{4,5},{5,4},{6,7},{7,6},{8,9},{9,8},{10,11... | collective-permute-start | bytes 1572872 | tf_op jit(solution)/shard_map/ppermute | solution.py:24
  46.0 16.2 %collective-permute-start.18 = (bf16[256,1024]{1,0:T(8,128)(2,1)S(1)}, bf16[256,1024]{1,0:T(8,128)(2,1)S(1)}, u32[]{:S(2)}, u32[]{:S(2)}) collective-permute-start(bf16[256,1024]{1,0:T(8,128)(2,1)S(1)} %collective-permute-done.14.refs_5_), channel_id=1, source_target_pairs={{0,4},{1,5},{2,6},{3,7},{4,8},{5,9},{6,10},{7,11},{8,12},{9,13},{1... | collective-permute-start | bytes 1572872 | tf_op jit(solution)/shard_map/ppermute | solution.py:24
  48.6 2.0 %collective-permute-start.19 = (bf16[64,2560]{1,0:T(8,128)(2,1)S(1)}, bf16[64,2560]{1,0:T(8,128)(2,1)S(1)}, u32[]{:S(2)}, u32[]{:S(2)}) collective-permute-start(bf16[64,2560]{1,0:T(8,128)(2,1)S(1)} %get-tuple-element.61), channel_id=1, source_target_pairs={{0,1},{1,0},{2,3},{3,2},{4,5},{5,4},{6,7},{7,6},{8,9},{9,8},{10,11... | collective-permute-start | bytes 983048 | tf_op jit(solution)/shard_map/ppermute | solution.py:24
  48.8 2.8 %collective-permute-start.20 = (bf16[64,2560]{1,0:T(8,128)(2,1)S(1)}, bf16[64,2560]{1,0:T(8,128)(2,1)S(1)}, u32[]{:S(2)}, u32[]{:S(2)}) collective-permute-start(bf16[64,2560]{1,0:T(8,128)(2,1)S(1)} %get-tuple-element.62), channel_id=1, source_target_pairs={{0,1},{1,0},{2,3},{3,2},{4,5},{5,4},{6,7},{7,6},{8,9},{9,8},{10,11... | collective-permute-start | bytes 983048 | tf_op jit(solution)/shard_map/ppermute | solution.py:24
  49.1 7.4 %collective-permute-start.12 = (bf16[176,512]{1,0:T(8,128)(2,1)S(1)}, bf16[176,512]{1,0:T(8,128)(2,1)S(1)}, u32[]{:S(2)}, u32[]{:S(2)}) collective-permute-start(bf16[176,512]{1,0:T(8,128)(2,1)S(1)} %get-tuple-element.55), channel_id=1, source_target_pairs={{0,2},{1,3},{2,0},{3,1},{4,6},{5,7},{6,4},{7,5},{8,10},{9,11},{10,... | collective-permute-start | bytes 540680 | tf_op jit(solution)/shard_map/ppermute | solution.py:24
  50.6 9.0 %collective-permute-start.13 = (bf16[176,512]{1,0:T(8,128)(2,1)S(1)}, bf16[176,512]{1,0:T(8,128)(2,1)S(1)}, u32[]{:S(2)}, u32[]{:S(2)}) collective-permute-start(bf16[176,512]{1,0:T(8,128)(2,1)S(1)} %get-tuple-element.56), channel_id=1, source_target_pairs={{0,18},{1,19},{2,16},{3,17},{4,22},{5,23},{6,20},{7,21},{8,26},{9,... | collective-permute-start | bytes 540680 | tf_op jit(solution)/shard_map/ppermute | solution.py:24
  62.2 4.3 %collective-permute-start.21 = (bf16[256,1024]{1,0:T(8,128)(2,1)S(1)}, bf16[256,1024]{1,0:T(8,128)(2,1)S(1)}, u32[]{:S(2)}, u32[]{:S(2)}) collective-permute-start(bf16[256,1024]{1,0:T(8,128)(2,1)S(1)} %collective-permute-done.18.refs_5_), channel_id=1, source_target_pairs={{0,1},{1,0},{2,3},{3,2},{4,5},{5,4},{6,7},{7,6},{8,9},{9,8},{10,11... | collective-permute-start | bytes 1572872 | tf_op jit(solution)/shard_map/ppermute | solution.py:24
  62.2 7.3 %collective-permute-start.16 = (bf16[176,512]{1,0:T(8,128)(2,1)S(1)}, bf16[176,512]{1,0:T(8,128)(2,1)S(1)}, u32[]{:S(2)}, u32[]{:S(2)}) collective-permute-start(bf16[176,512]{1,0:T(8,128)(2,1)S(1)} %get-tuple-element.58), channel_id=1, source_target_pairs={{0,2},{1,3},{2,0},{3,1},{4,6},{5,7},{6,4},{7,5},{8,10},{9,11},{10,... | collective-permute-start | bytes 540680 | tf_op jit(solution)/shard_map/ppermute | solution.py:24
  63.7 9.3 %collective-permute-start.17 = (bf16[176,512]{1,0:T(8,128)(2,1)S(1)}, bf16[176,512]{1,0:T(8,128)(2,1)S(1)}, u32[]{:S(2)}, u32[]{:S(2)}) collective-permute-start(bf16[176,512]{1,0:T(8,128)(2,1)S(1)} %get-tuple-element.59), channel_id=1, source_target_pairs={{0,18},{1,19},{2,16},{3,17},{4,22},{5,23},{6,20},{7,21},{8,26},{9,... | collective-permute-start | bytes 540680 | tf_op jit(solution)/shard_map/ppermute | solution.py:24
  64.2 11.8 %collective-permute-start.26 = (bf16[16,5120]{1,0:T(8,128)(2,1)S(1)}, bf16[16,5120]{1,0:T(8,128)(2,1)S(1)}, u32[]{:S(2)}, u32[]{:S(2)}) collective-permute-start(bf16[16,5120]{1,0:T(8,128)(2,1)S(1)} %get-tuple-element.74), channel_id=1, source_target_pairs={{0,4},{1,5},{2,6},{3,7},{4,8},{5,9},{6,10},{7,11},{8,12},{9,13},{1... | collective-permute-start | bytes 491528 | tf_op jit(solution)/shard_map/ppermute | solution.py:24
  64.9 14.3 %collective-permute-start.25 = (bf16[16,5120]{1,0:T(8,128)(2,1)S(1)}, bf16[16,5120]{1,0:T(8,128)(2,1)S(1)}, u32[]{:S(2)}, u32[]{:S(2)}) collective-permute-start(bf16[16,5120]{1,0:T(8,128)(2,1)S(1)} %get-tuple-element.72), channel_id=1, source_target_pairs={{0,8},{1,9},{2,10},{3,11},{4,12},{5,13},{6,14},{7,15},{8,0},{9,1},... | collective-permute-start | bytes 491528 | tf_op jit(solution)/shard_map/ppermute | solution.py:24
  66.5 12.7 %collective-permute-start.24 = (bf16[16,5120]{1,0:T(8,128)(2,1)S(1)}, bf16[16,5120]{1,0:T(8,128)(2,1)S(1)}, u32[]{:S(2)}, u32[]{:S(2)}) collective-permute-start(bf16[16,5120]{1,0:T(8,128)(2,1)S(1)} %get-tuple-element.70), channel_id=1, source_target_pairs={{0,12},{1,13},{2,14},{3,15},{4,0},{5,1},{6,2},{7,3},{8,4},{9,5},{1... | collective-permute-start | bytes 491528 | tf_op jit(solution)/shard_map/ppermute | solution.py:24
  73.0 8.6 %collective-permute-start.23 = (bf16[176,512]{1,0:T(8,128)(2,1)S(1)}, bf16[176,512]{1,0:T(8,128)(2,1)S(1)}, u32[]{:S(2)}, u32[]{:S(2)}) collective-permute-start(bf16[176,512]{1,0:T(8,128)(2,1)S(1)} %get-tuple-element.68), channel_id=1, source_target_pairs={{0,18},{1,19},{2,16},{3,17},{4,22},{5,23},{6,20},{7,21},{8,26},{9,... | collective-permute-start | bytes 540680 | tf_op jit(solution)/shard_map/ppermute | solution.py:24
  75.4 8.6 %collective-permute-start.22 = (bf16[176,512]{1,0:T(8,128)(2,1)S(1)}, bf16[176,512]{1,0:T(8,128)(2,1)S(1)}, u32[]{:S(2)}, u32[]{:S(2)}) collective-permute-start(bf16[176,512]{1,0:T(8,128)(2,1)S(1)} %get-tuple-element.66), channel_id=1, source_target_pairs={{0,2},{1,3},{2,0},{3,1},{4,6},{5,7},{6,4},{7,5},{8,10},{9,11},{10,... | collective-permute-start | bytes 540680 | tf_op jit(solution)/shard_map/ppermute | solution.py:24
  79.3 1.5 %collective-permute-start.27 = (bf16[16,5120]{1,0:T(8,128)(2,1)S(1)}, bf16[16,5120]{1,0:T(8,128)(2,1)S(1)}, u32[]{:S(2)}, u32[]{:S(2)}) collective-permute-start(bf16[16,5120]{1,0:T(8,128)(2,1)S(1)} %shard_map.104.refs_0_), channel_id=1, source_target_pairs={{0,1},{1,0},{2,3},{3,2},{4,5},{5,4},{6,7},{7,6},{8,9},{9,8},{10,11... | collective-permute-start | bytes 491528 | tf_op jit(solution)/shard_map/ppermute | solution.py:24
  (3 other events, 2.2 us)

commit v7 on v6

--- a/solution.py
+++ b/solution.py
@@ -261,13 +261,13 @@
         [jax.ShapeDtypeStruct((rows, holders * half + value_width), BF16)],
         (adapter_down_weight[0], adapter_up_weight[0]),
     )[0]
+    ring = [lax.dynamic_slice_in_dim(frozen, (group * replicas + core) * piece, piece, axis=0)]
+    own, ring[0] = lax.optimization_barrier((own, ring[0]))
     held = [own]
     for k in range(1, holders):
         held.append(moved(own, lambda g, z, s, r: (g, z + k, s, r)))
-
-    ring = [lax.dynamic_slice_in_dim(frozen, (group * replicas + core) * piece, piece, axis=0)]
-    ring.append(moved(ring[0], lambda g, z, s, r: (g, z + 1, s, r)))
-    held, grads, ring = lax.optimization_barrier((held, grads, ring))
+    held, grads = lax.optimization_barrier((held, grads))
+    ring.append(moved(after(ring[0], held[1]), lambda g, z, s, r: (g, z + 1, s, r)))
     joined = call(
         join_kernel,
         [
@@ -325,15 +325,18 @@
         )
         return part, chip
 
-    arrived, outs = [], []
+    arrived, outs, sel = [], [], None
     for k in range(holders):
-        if k > 1:
-            last = ring[-1]
-            if k > 2:
-                last = after(last, *outs[k - 2], part)
+        for j in range(len(ring), min(k + 2, holders) if k > 1 else k + 1):
+            last = after(ring[-1], *(outs[j - 2] if j > 2 else []), part if j > 2 else sel)
             ring.append(moved(last, lambda g, z, s, r: (g, z + 1, s, r)))
-        gate = [*arrived[k - 2], *outs[k - 1]] if k > 1 else []
-        blocks = pieces_of(k, *gate, *(chip[:1] if k > 2 else ()))
+        if k < 2:
+            gate = [sel] * k
+        elif k == 2:
+            gate = [*arrived[0], *outs[1]]
+        else:
+            gate = [*arrived[k - 2], *arrived[k - 1], chip[0]]
+        blocks = pieces_of(k, *gate)
         tokens_in = [after(tagged, part), *grads[1:]] if k == 1 else grads
         out = call(
             functools.partial(

time: 85.4 us -> 91.6 us (1.073); the launches traced: 85.2 us -> 90 us
  waiting for transfers between devices: 38.1 us -> 46.4 us
  starting transfers between devices: 32.1 us -> 28.8 us
    ppermute x28, waiting for transfers between devices: 38.1 us -> 46.4 us  [moved(): return lax.ppermute(x, AXES, pairs)]
    ppermute x28, starting transfers between devices: 32.1 us -> 28.8 us  [moved(): return lax.ppermute(x, AXES, pairs)]
  transfers between devices with their start and end apart: 28 -> 28, of which waited for: 14 -> 14; matrix products, arithmetic and copies ran while one was open for 0% -> 1% of each run, Pallas kernels for 9% -> 8%
where the time goes in v7:
time: 91.6 us; the launch traced here: 90 us
  waiting for transfers between devices  46.4 us (51%)
  starting transfers between devices  28.8 us (31%)
  Pallas kernels  8.76 us (10%)
  local copies, waits for them, and re-layouts  5.34 us (6%)
    ppermute x28, waiting for transfers between devices, moved(): return lax.ppermute(x, AXES, pairs)  46.4 us
    ppermute x28, starting transfers between devices, moved(): return lax.ppermute(x, AXES, pairs)  28.8 us
    pallas_call x12, Pallas kernels, call(): pl.pallas_call(kernel, out_shape=out_shape, in_specs=[pl.BlockSpec(memory...  8.76 us
    unnamed x14, local copies, waits for them, and re-layouts  4.26 us
  transfers between devices with their start and end apart: 28, of which 14 were waited for; matrix products, arithmetic and copies ran while one was open for 1% of the time, Pallas kernels for 8%

profile of v7, /device:TPU:0, one launch (start us, length us, event | category | flops | bytes accessed | tf_op | source)
XLA Modules:
  0.0 90.0 jit_solution(11910472036530945897)
XLA Ops:
  0.7 1.1 %copy-done.2 = bf16[1,176,1024]{2,1,0:T(8,128)(2,1)S(1)} copy-done((bf16[1,176,1024]{2,1,0:T(8,128)(2,1)S(1)}, bf16[1,176,1024]{2,1,0:T(8,128)(2,1)}, u32[]{:S(2)}) %copy-start.2) | copy-done | bytes 360472
  3.9 3.0 %collective-permute-start.3 = (bf16[176,1152]{1,0:T(8,128)(2,1)S(1)}, bf16[176,1152]{1,0:T(8,128)(2,1)S(1)}, u32[]{:S(2)}, u32[]{:S(2)}) collective-permute-start(bf16[176,1152]{1,0:T(8,128)(2,1)S(1)} %shard_map.95.refs_0_.refs_1_), channel_id=1, source_target_pairs={{0,16},{1,17},{2,18},{3,19},{4,20},{5,21},{6,22},{7,23},{8,24},{9,... | collective-permute-start | bytes 1216520 | tf_op jit(solution)/shard_map/ppermute | solution.py:24
  6.9 0.9 %copy-done.3 = bf16[1,2,16,4096]{3,2,1,0:T(8,128)(2,1)S(1)} copy-done((bf16[1,2,16,4096]{3,2,1,0:T(8,128)(2,1)S(1)}, bf16[1,2,16,4096]{3,2,1,0:T(8,128)(2,1)}, u32[]{:S(2)}) %copy-start.3) | copy-done | bytes 262168
  8.7 1.1 %dynamic-slice_bitcast_fusion = bf16[256,1024]{1,0:T(8,128)(2,1)S(1)} fusion(bf16[1,1024,1024]{2,1,0:T(8,128)(2,1)} %param.11, s32[]{:T(128)S(6)} %select_n.3), kind=kLoop, calls=%fused_computation | loop fusion | bytes 1048580 | tf_op jit(solution)/shard_map/dynamic_slice | solution.py:264
  9.8 1.6 %collective-permute-start = (bf16[16,3072]{1,0:T(8,128)(2,1)S(1)}, bf16[16,3072]{1,0:T(8,128)(2,1)S(1)}, u32[]{:S(2)}, u32[]{:S(2)}) collective-permute-start(bf16[16,3072]{1,0:T(8,128)(2,1)S(1)} %shard_map.94.refs_0_), channel_id=1, source_target_pairs={{0,4},{1,5},{2,6},{3,7},{4,8},{5,9},{6,10},{7,11},{8,12},{9,13},{1... | collective-permute-start | bytes 294920 | tf_op jit(solution)/shard_map/ppermute | solution.py:24
  11.4 2.6 %collective-permute-start.1 = (bf16[16,3072]{1,0:T(8,128)(2,1)S(1)}, bf16[16,3072]{1,0:T(8,128)(2,1)S(1)}, u32[]{:S(2)}, u32[]{:S(2)}) collective-permute-start(bf16[16,3072]{1,0:T(8,128)(2,1)S(1)} %shard_map.94.refs_0_), channel_id=1, source_target_pairs={{0,8},{1,9},{2,10},{3,11},{4,12},{5,13},{6,14},{7,15},{8,0},{9,1},... | collective-permute-start | bytes 294920 | tf_op jit(solution)/shard_map/ppermute | solution.py:24
  14.0 1.3 %collective-permute-start.2 = (bf16[16,3072]{1,0:T(8,128)(2,1)S(1)}, bf16[16,3072]{1,0:T(8,128)(2,1)S(1)}, u32[]{:S(2)}, u32[]{:S(2)}) collective-permute-start(bf16[16,3072]{1,0:T(8,128)(2,1)S(1)} %shard_map.94.refs_0_), channel_id=1, source_target_pairs={{0,12},{1,13},{2,14},{3,15},{4,0},{5,1},{6,2},{7,3},{8,4},{9,5},{1... | collective-permute-start | bytes 294920 | tf_op jit(solution)/shard_map/ppermute | solution.py:24
  15.4 2.0 %collective-permute-done.refs_1_ = bf16[16,3072]{1,0:T(8,128)(2,1)S(1)} collective-permute-done((bf16[16,3072]{1,0:T(8,128)(2,1)S(1)}, bf16[16,3072]{1,0:T(8,128)(2,1)S(1)}, u32[]{:S(2)}, u32[]{:S(2)}) %collective-permute-start) | collective-permute-done | bytes 98336 | tf_op jit(solution)/shard_map/ppermute | solution.py:24
  17.3 3.2 %collective-permute-done.1.refs_2_ = bf16[16,3072]{1,0:T(8,128)(2,1)S(1)} collective-permute-done((bf16[16,3072]{1,0:T(8,128)(2,1)S(1)}, bf16[16,3072]{1,0:T(8,128)(2,1)S(1)}, u32[]{:S(2)}, u32[]{:S(2)}) %collective-permute-start.1) | collective-permute-done | bytes 98336 | tf_op jit(solution)/shard_map/ppermute | solution.py:24
  20.5 2.4 %collective-permute-start.10 = (bf16[256,1024]{1,0:T(8,128)(2,1)S(1)}, bf16[256,1024]{1,0:T(8,128)(2,1)S(1)}, u32[]{:S(2)}, u32[]{:S(2)}) collective-permute-start(bf16[256,1024]{1,0:T(8,128)(2,1)S(1)} %dynamic-slice_bitcast_fusion), channel_id=1, source_target_pairs={{0,4},{1,5},{2,6},{3,7},{4,8},{5,9},{6,10},{7,11},{8,12},{9,13},{1... | collective-permute-start | bytes 1572872 | tf_op jit(solution)/shard_map/ppermute | solution.py:24
  24.7 1.5 %shard_map.97 = (bf16[176,512]{1,0:T(8,128)(2,1)S(1)}, bf16[176,512]{1,0:T(8,128)(2,1)S(1)}, bf16[352,128]{1,0:T(8,128)(2,1)S(1)}) custom-call(bf16[176,1152]{1,0:T(8,128)(2,1)S(1)} %shard_map.95.refs_0_.refs_1_, bf16[176,1152]{1,0:T(8,128)(2,1)S(1)} %collective-permute-done.3.refs_1_, bf16[64,2048]{1,0:T(8,128)(2,1)S(1)} %get-tuple-element.50.refs_2_.refs_3_, ...), custom_call_target="tpu_custom_call" | custom-call | flops 1000 | bytes 1000 | tf_op jit(solution)/shard_map/pallas_call | solution.py:41
  26.2 9.5 %collective-permute-done.10.refs_5_ = bf16[256,1024]{1,0:T(8,128)(2,1)S(1)} collective-permute-done((bf16[256,1024]{1,0:T(8,128)(2,1)S(1)}, bf16[256,1024]{1,0:T(8,128)(2,1)S(1)}, u32[]{:S(2)}, u32[]{:S(2)}) %collective-permute-start.10) | collective-permute-done | bytes 524320 | tf_op jit(solution)/shard_map/ppermute | solution.py:24
  36.8 1.5 %collective-permute-start.6 = (bf16[176,512]{1,0:T(8,128)(2,1)S(1)}, bf16[176,512]{1,0:T(8,128)(2,1)S(1)}, u32[]{:S(2)}, u32[]{:S(2)}) collective-permute-start(bf16[176,512]{1,0:T(8,128)(2,1)S(1)} %get-tuple-element.52), channel_id=1, source_target_pairs={{0,2},{1,3},{2,0},{3,1},{4,6},{5,7},{6,4},{7,5},{8,10},{9,11},{10,... | collective-permute-start | bytes 540680 | tf_op jit(solution)/shard_map/ppermute | solution.py:24
  39.0 1.3 %shard_map.98 = (f32[64,5120]{1,0:T(8,128)S(1)}, bf16[64,2560]{1,0:T(8,128)(2,1)S(1)}, bf16[64,2560]{1,0:T(8,128)(2,1)S(1)}) custom-call(bf16[176,4096]{1,0:T(8,128)(2,1)S(1)} %bitcast.12, bf16[176,1152]{1,0:T(8,128)(2,1)S(1)} %shard_map.95.refs_0_.refs_1_, bf16[352,128]{1,0:T(8,128)(2,1)S(1)} %get-tuple-element.54.refs_2_.refs_4_, ...), custom_call_target="tpu_custom_call" | custom-call | flops 1000 | bytes 1000 | tf_op jit(solution)/shard_map/pallas_call | solution.py:41
  40.3 1.0 %shard_map.99 = (bf16[176,512]{1,0:T(8,128)(2,1)S(1)}, bf16[176,512]{1,0:T(8,128)(2,1)S(1)}) custom-call(bf16[176,1152]{1,0:T(8,128)(2,1)S(1)} %shard_map.95.refs_0_.refs_1_, bf16[176,1152]{1,0:T(8,128)(2,1)S(1)} %collective-permute-done.3.refs_1_, bf16[64,2048]{1,0:T(8,128)(2,1)S(1)} %get-tuple-element.50.refs_2_.refs_3_, ...), custom_call_target="tpu_custom_call" | custom-call | flops 1000 | bytes 1000 | tf_op jit(solution)/shard_map/pallas_call | solution.py:41
  41.3 2.9 %collective-permute-done.6.refs_0_ = bf16[176,512]{1,0:T(8,128)(2,1)S(1)} collective-permute-done((bf16[176,512]{1,0:T(8,128)(2,1)S(1)}, bf16[176,512]{1,0:T(8,128)(2,1)S(1)}, u32[]{:S(2)}, u32[]{:S(2)}) %collective-permute-start.6) | collective-permute-done | bytes 180256 | tf_op jit(solution)/shard_map/ppermute | solution.py:24
  44.1 3.4 %collective-permute-done.7.refs_1_ = bf16[176,512]{1,0:T(8,128)(2,1)S(1)} collective-permute-done((bf16[176,512]{1,0:T(8,128)(2,1)S(1)}, bf16[176,512]{1,0:T(8,128)(2,1)S(1)}, u32[]{:S(2)}, u32[]{:S(2)}) %collective-permute-start.7) | collective-permute-done | bytes 180256 | tf_op jit(solution)/shard_map/ppermute | solution.py:24
  47.5 4.2 %collective-permute-done.14.refs_5_ = bf16[256,1024]{1,0:T(8,128)(2,1)S(1)} collective-permute-done((bf16[256,1024]{1,0:T(8,128)(2,1)S(1)}, bf16[256,1024]{1,0:T(8,128)(2,1)S(1)}, u32[]{:S(2)}, u32[]{:S(2)}) %collective-permute-start.14) | collective-permute-done | bytes 524320 | tf_op jit(solution)/shard_map/ppermute | solution.py:24
  52.3 1.5 %collective-permute-start.12 = (bf16[176,512]{1,0:T(8,128)(2,1)S(1)}, bf16[176,512]{1,0:T(8,128)(2,1)S(1)}, u32[]{:S(2)}, u32[]{:S(2)}) collective-permute-start(bf16[176,512]{1,0:T(8,128)(2,1)S(1)} %get-tuple-element.61), channel_id=1, source_target_pairs={{0,2},{1,3},{2,0},{3,1},{4,6},{5,7},{6,4},{7,5},{8,10},{9,11},{10,... | collective-permute-start | bytes 540680 | tf_op jit(solution)/shard_map/ppermute | solution.py:24
  53.8 1.3 %collective-permute-start.13 = (bf16[176,512]{1,0:T(8,128)(2,1)S(1)}, bf16[176,512]{1,0:T(8,128)(2,1)S(1)}, u32[]{:S(2)}, u32[]{:S(2)}) collective-permute-start(bf16[176,512]{1,0:T(8,128)(2,1)S(1)} %get-tuple-element.62), channel_id=1, source_target_pairs={{0,18},{1,19},{2,16},{3,17},{4,22},{5,23},{6,20},{7,21},{8,26},{9,... | collective-permute-start | bytes 540680 | tf_op jit(solution)/shard_map/ppermute | solution.py:24
  55.1 1.0 %shard_map.100 = (bf16[176,512]{1,0:T(8,128)(2,1)S(1)}, bf16[176,512]{1,0:T(8,128)(2,1)S(1)}) custom-call(bf16[176,1152]{1,0:T(8,128)(2,1)S(1)} %shard_map.95.refs_0_.refs_1_, bf16[176,1152]{1,0:T(8,128)(2,1)S(1)} %collective-permute-done.3.refs_1_, bf16[64,2048]{1,0:T(8,128)(2,1)S(1)} %get-tuple-element.50.refs_2_.refs_3_, ...), custom_call_target="tpu_custom_call" | custom-call | flops 1000 | bytes 1000 | tf_op jit(solution)/shard_map/pallas_call | solution.py:41
  57.0 2.2 %collective-permute-start.17 = (bf16[176,512]{1,0:T(8,128)(2,1)S(1)}, bf16[176,512]{1,0:T(8,128)(2,1)S(1)}, u32[]{:S(2)}, u32[]{:S(2)}) collective-permute-start(bf16[176,512]{1,0:T(8,128)(2,1)S(1)} %get-tuple-element.65), channel_id=1, source_target_pairs={{0,18},{1,19},{2,16},{3,17},{4,22},{5,23},{6,20},{7,21},{8,26},{9,... | collective-permute-start | bytes 540680 | tf_op jit(solution)/shard_map/ppermute | solution.py:24
  59.7 4.0 %collective-permute-done.13.refs_3_ = bf16[176,512]{1,0:T(8,128)(2,1)S(1)} collective-permute-done((bf16[176,512]{1,0:T(8,128)(2,1)S(1)}, bf16[176,512]{1,0:T(8,128)(2,1)S(1)}, u32[]{:S(2)}, u32[]{:S(2)}) %collective-permute-start.13) | collective-permute-done | bytes 180256 | tf_op jit(solution)/shard_map/ppermute | solution.py:24
  63.7 4.2 %collective-permute-done.18.refs_5_ = bf16[256,1024]{1,0:T(8,128)(2,1)S(1)} collective-permute-done((bf16[256,1024]{1,0:T(8,128)(2,1)S(1)}, bf16[256,1024]{1,0:T(8,128)(2,1)S(1)}, u32[]{:S(2)}, u32[]{:S(2)}) %collective-permute-start.18) | collective-permute-done | bytes 524320 | tf_op jit(solution)/shard_map/ppermute | solution.py:24
  67.9 3.1 %collective-permute-done.17.refs_5_ = bf16[176,512]{1,0:T(8,128)(2,1)S(1)} collective-permute-done((bf16[176,512]{1,0:T(8,128)(2,1)S(1)}, bf16[176,512]{1,0:T(8,128)(2,1)S(1)}, u32[]{:S(2)}, u32[]{:S(2)}) %collective-permute-start.17) | collective-permute-done | bytes 180256 | tf_op jit(solution)/shard_map/ppermute | solution.py:24
  71.0 4.1 %collective-permute-start.25 = (bf16[16,5120]{1,0:T(8,128)(2,1)S(1)}, bf16[16,5120]{1,0:T(8,128)(2,1)S(1)}, u32[]{:S(2)}, u32[]{:S(2)}) collective-permute-start(bf16[16,5120]{1,0:T(8,128)(2,1)S(1)} %get-tuple-element.78), channel_id=1, source_target_pairs={{0,8},{1,9},{2,10},{3,11},{4,12},{5,13},{6,14},{7,15},{8,0},{9,1},... | collective-permute-start | bytes 491528 | tf_op jit(solution)/shard_map/ppermute | solution.py:24
  75.2 1.0 %shard_map.102 = (bf16[176,512]{1,0:T(8,128)(2,1)S(1)}, bf16[176,512]{1,0:T(8,128)(2,1)S(1)}) custom-call(bf16[176,1152]{1,0:T(8,128)(2,1)S(1)} %shard_map.95.refs_0_.refs_1_, bf16[176,1152]{1,0:T(8,128)(2,1)S(1)} %collective-permute-done.3.refs_1_, bf16[64,2048]{1,0:T(8,128)(2,1)S(1)} %get-tuple-element.50.refs_2_.refs_3_, ...), custom_call_target="tpu_custom_call" | custom-call | flops 1000 | bytes 1000 | tf_op jit(solution)/shard_map/pallas_call | solution.py:41
  76.2 2.3 %collective-permute-start.23 = (bf16[176,512]{1,0:T(8,128)(2,1)S(1)}, bf16[176,512]{1,0:T(8,128)(2,1)S(1)}, u32[]{:S(2)}, u32[]{:S(2)}) collective-permute-start(bf16[176,512]{1,0:T(8,128)(2,1)S(1)} %get-tuple-element.74), channel_id=1, source_target_pairs={{0,18},{1,19},{2,16},{3,17},{4,22},{5,23},{6,20},{7,21},{8,26},{9,... | collective-permute-start | bytes 540680 | tf_op jit(solution)/shard_map/ppermute | solution.py:24
  79.0 1.0 %collective-permute-done.26.refs_3_ = bf16[16,5120]{1,0:T(8,128)(2,1)S(1)} collective-permute-done((bf16[16,5120]{1,0:T(8,128)(2,1)S(1)}, bf16[16,5120]{1,0:T(8,128)(2,1)S(1)}, u32[]{:S(2)}, u32[]{:S(2)}) %collective-permute-start.26) | collective-permute-done | bytes 163872 | tf_op jit(solution)/shard_map/ppermute | solution.py:24
  79.9 6.6 %collective-permute-done.25.refs_2_ = bf16[16,5120]{1,0:T(8,128)(2,1)S(1)} collective-permute-done((bf16[16,5120]{1,0:T(8,128)(2,1)S(1)}, bf16[16,5120]{1,0:T(8,128)(2,1)S(1)}, u32[]{:S(2)}, u32[]{:S(2)}) %collective-permute-start.25) | collective-permute-done | bytes 163872 | tf_op jit(solution)/shard_map/ppermute | solution.py:24
  86.7 1.4 %collective-permute-done.27.refs_1_ = bf16[16,5120]{1,0:T(8,128)(2,1)S(1)} collective-permute-done((bf16[16,5120]{1,0:T(8,128)(2,1)S(1)}, bf16[16,5120]{1,0:T(8,128)(2,1)S(1)}, u32[]{:S(2)}, u32[]{:S(2)}) %collective-permute-start.27) | collective-permute-done | bytes 163872 | tf_op jit(solution)/shard_map/ppermute | solution.py:24
  88.8 1.2 %shard_map.103 = bf16[176,4096]{1,0:T(8,128)(2,1)} custom-call(bf16[176,512]{1,0:T(8,128)(2,1)S(1)} %collective-permute-done.6.refs_0_, bf16[176,512]{1,0:T(8,128)(2,1)S(1)} %collective-permute-done.7.refs_1_, bf16[176,512]{1,0:T(8,128)(2,1)S(1)} %collective-permute-done.12.refs_2_, bf16[176,512]{1,0:T(8,128)(2,1)S(1)} %collective-permute-done.13.refs_3_, ...), custom_call_target="tpu_custom_call" | custom-call | flops 1000 | bytes 1000 | tf_op jit(solution)/shard_map/pallas_call | solution.py:41
  (51 shorter events, 9.9 us)
Async XLA Ops:
  0.6 24.1 %copy-start = (bf16[1,1024,1024]{2,1,0:T(8,128)(2,1)S(1)}, bf16[1,1024,1024]{2,1,0:T(8,128)(2,1)}, u32[]{:S(2)}) copy-start(bf16[1,1024,1024]{2,1,0:T(8,128)(2,1)} %param.11) | copy-start | bytes 6291460
  0.6 1.1 %copy-start.2 = (bf16[1,176,1024]{2,1,0:T(8,128)(2,1)S(1)}, bf16[1,176,1024]{2,1,0:T(8,128)(2,1)}, u32[]{:S(2)}) copy-start(bf16[1,176,1024]{2,1,0:T(8,128)(2,1)} %param.8) | copy-start | bytes 1081348
  3.9 16.6 %collective-permute-start.3 = (bf16[176,1152]{1,0:T(8,128)(2,1)S(1)}, bf16[176,1152]{1,0:T(8,128)(2,1)S(1)}, u32[]{:S(2)}, u32[]{:S(2)}) collective-permute-start(bf16[176,1152]{1,0:T(8,128)(2,1)S(1)} %shard_map.95.refs_0_.refs_1_), channel_id=1, source_target_pairs={{0,16},{1,17},{2,18},{3,19},{4,20},{5,21},{6,22},{7,23},{8,24},{9,... | collective-permute-start | bytes 1216520 | tf_op jit(solution)/shard_map/ppermute | solution.py:24
  6.9 0.9 %copy-start.3 = (bf16[1,2,16,4096]{3,2,1,0:T(8,128)(2,1)S(1)}, bf16[1,2,16,4096]{3,2,1,0:T(8,128)(2,1)}, u32[]{:S(2)}) copy-start(bf16[1,2,16,4096]{3,2,1,0:T(8,128)(2,1)} %param.12) | copy-start | bytes 786436
  9.8 7.5 %collective-permute-start = (bf16[16,3072]{1,0:T(8,128)(2,1)S(1)}, bf16[16,3072]{1,0:T(8,128)(2,1)S(1)}, u32[]{:S(2)}, u32[]{:S(2)}) collective-permute-start(bf16[16,3072]{1,0:T(8,128)(2,1)S(1)} %shard_map.94.refs_0_), channel_id=1, source_target_pairs={{0,4},{1,5},{2,6},{3,7},{4,8},{5,9},{6,10},{7,11},{8,12},{9,13},{1... | collective-permute-start | bytes 294920 | tf_op jit(solution)/shard_map/ppermute | solution.py:24
  11.4 9.0 %collective-permute-start.1 = (bf16[16,3072]{1,0:T(8,128)(2,1)S(1)}, bf16[16,3072]{1,0:T(8,128)(2,1)S(1)}, u32[]{:S(2)}, u32[]{:S(2)}) collective-permute-start(bf16[16,3072]{1,0:T(8,128)(2,1)S(1)} %shard_map.94.refs_0_), channel_id=1, source_target_pairs={{0,8},{1,9},{2,10},{3,11},{4,12},{5,13},{6,14},{7,15},{8,0},{9,1},... | collective-permute-start | bytes 294920 | tf_op jit(solution)/shard_map/ppermute | solution.py:24
  14.0 6.5 %collective-permute-start.2 = (bf16[16,3072]{1,0:T(8,128)(2,1)S(1)}, bf16[16,3072]{1,0:T(8,128)(2,1)S(1)}, u32[]{:S(2)}, u32[]{:S(2)}) collective-permute-start(bf16[16,3072]{1,0:T(8,128)(2,1)S(1)} %shard_map.94.refs_0_), channel_id=1, source_target_pairs={{0,12},{1,13},{2,14},{3,15},{4,0},{5,1},{6,2},{7,3},{8,4},{9,5},{1... | collective-permute-start | bytes 294920 | tf_op jit(solution)/shard_map/ppermute | solution.py:24
  20.5 15.2 %collective-permute-start.10 = (bf16[256,1024]{1,0:T(8,128)(2,1)S(1)}, bf16[256,1024]{1,0:T(8,128)(2,1)S(1)}, u32[]{:S(2)}, u32[]{:S(2)}) collective-permute-start(bf16[256,1024]{1,0:T(8,128)(2,1)S(1)} %dynamic-slice_bitcast_fusion), channel_id=1, source_target_pairs={{0,4},{1,5},{2,6},{3,7},{4,8},{5,9},{6,10},{7,11},{8,12},{9,13},{1... | collective-permute-start | bytes 1572872 | tf_op jit(solution)/shard_map/ppermute | solution.py:24
  22.9 1.8 %collective-permute-start.4 = (bf16[64,2048]{1,0:T(8,128)(2,1)S(1)}, bf16[64,2048]{1,0:T(8,128)(2,1)S(1)}, u32[]{:S(2)}, u32[]{:S(2)}) collective-permute-start(bf16[64,2048]{1,0:T(8,128)(2,1)S(1)} %get-tuple-element.50.refs_2_.refs_3_), channel_id=1, source_target_pairs={{0,1},{1,0},{2,3},{3,2},{4,5},{5,4},{6,7},{7,6},{8,9},{9,8},{10,11... | collective-permute-start | bytes 786440 | tf_op jit(solution)/shard_map/ppermute | solution.py:24
  23.0 1.7 %collective-permute-start.5 = (bf16[64,1024]{1,0:T(8,128)(2,1)S(1)}, bf16[64,1024]{1,0:T(8,128)(2,1)S(1)}, u32[]{:S(2)}, u32[]{:S(2)}) collective-permute-start(bf16[64,1024]{1,0:T(8,128)(2,1)S(1)} %get-tuple-element.51.refs_4_), channel_id=1, source_target_pairs={{0,1},{1,0},{2,3},{3,2},{4,5},{5,4},{6,7},{7,6},{8,9},{9,8},{10,11... | collective-permute-start | bytes 393224 | tf_op jit(solution)/shard_map/ppermute | solution.py:24
  23.5 13.0 %collective-permute-start.8 = (bf16[64,2048]{1,0:T(8,128)(2,1)S(1)}, bf16[64,2048]{1,0:T(8,128)(2,1)S(1)}, u32[]{:S(2)}, u32[]{:S(2)}) collective-permute-start(bf16[64,2048]{1,0:T(8,128)(2,1)S(1)} %get-tuple-element.50.refs_2_.refs_3_), channel_id=1, source_target_pairs={{0,16},{1,17},{2,18},{3,19},{4,20},{5,21},{6,22},{7,23},{8,24},{9,... | collective-permute-start | bytes 786440 | tf_op jit(solution)/shard_map/ppermute | solution.py:24
  24.7 14.3 %copy-start.1 = (bf16[1,176,4096]{2,1,0:T(8,128)(2,1)S(1)}, bf16[1,176,4096]{2,1,0:T(8,128)(2,1)}, u32[]{:S(2)}) copy-start(bf16[1,176,4096]{2,1,0:T(8,128)(2,1)} %param.7) | copy-start | bytes 4325380
  35.6 4.6 %collective-permute-start.11 = (bf16[256,1024]{1,0:T(8,128)(2,1)S(1)}, bf16[256,1024]{1,0:T(8,128)(2,1)S(1)}, u32[]{:S(2)}, u32[]{:S(2)}) collective-permute-start(bf16[256,1024]{1,0:T(8,128)(2,1)S(1)} %collective-permute-done.10.refs_5_), channel_id=1, source_target_pairs={{0,1},{1,0},{2,3},{3,2},{4,5},{5,4},{6,7},{7,6},{8,9},{9,8},{10,11... | collective-permute-start | bytes 1572872 | tf_op jit(solution)/shard_map/ppermute | solution.py:24
  35.7 16.1 %collective-permute-start.14 = (bf16[256,1024]{1,0:T(8,128)(2,1)S(1)}, bf16[256,1024]{1,0:T(8,128)(2,1)S(1)}, u32[]{:S(2)}, u32[]{:S(2)}) collective-permute-start(bf16[256,1024]{1,0:T(8,128)(2,1)S(1)} %collective-permute-done.10.refs_5_), channel_id=1, source_target_pairs={{0,4},{1,5},{2,6},{3,7},{4,8},{5,9},{6,10},{7,11},{8,12},{9,13},{1... | collective-permute-start | bytes 1572872 | tf_op jit(solution)/shard_map/ppermute | solution.py:24
  36.5 2.4 %collective-permute-start.9 = (bf16[64,2048]{1,0:T(8,128)(2,1)S(1)}, bf16[64,2048]{1,0:T(8,128)(2,1)S(1)}, u32[]{:S(2)}, u32[]{:S(2)}) collective-permute-start(bf16[64,2048]{1,0:T(8,128)(2,1)S(1)} %collective-permute-done.8.refs_5_), channel_id=1, source_target_pairs={{0,1},{1,0},{2,3},{3,2},{4,5},{5,4},{6,7},{7,6},{8,9},{9,8},{10,11... | collective-permute-start | bytes 786440 | tf_op jit(solution)/shard_map/ppermute | solution.py:24
  36.8 7.4 %collective-permute-start.6 = (bf16[176,512]{1,0:T(8,128)(2,1)S(1)}, bf16[176,512]{1,0:T(8,128)(2,1)S(1)}, u32[]{:S(2)}, u32[]{:S(2)}) collective-permute-start(bf16[176,512]{1,0:T(8,128)(2,1)S(1)} %get-tuple-element.52), channel_id=1, source_target_pairs={{0,2},{1,3},{2,0},{3,1},{4,6},{5,7},{6,4},{7,5},{8,10},{9,11},{10,... | collective-permute-start | bytes 540680 | tf_op jit(solution)/shard_map/ppermute | solution.py:24
  38.2 9.3 %collective-permute-start.7 = (bf16[176,512]{1,0:T(8,128)(2,1)S(1)}, bf16[176,512]{1,0:T(8,128)(2,1)S(1)}, u32[]{:S(2)}, u32[]{:S(2)}) collective-permute-start(bf16[176,512]{1,0:T(8,128)(2,1)S(1)} %get-tuple-element.53), channel_id=1, source_target_pairs={{0,18},{1,19},{2,16},{3,17},{4,22},{5,23},{6,20},{7,21},{8,26},{9,... | collective-permute-start | bytes 540680 | tf_op jit(solution)/shard_map/ppermute | solution.py:24
  51.8 2.0 %collective-permute-start.15 = (bf16[256,1024]{1,0:T(8,128)(2,1)S(1)}, bf16[256,1024]{1,0:T(8,128)(2,1)S(1)}, u32[]{:S(2)}, u32[]{:S(2)}) collective-permute-start(bf16[256,1024]{1,0:T(8,128)(2,1)S(1)} %collective-permute-done.14.refs_5_), channel_id=1, source_target_pairs={{0,1},{1,0},{2,3},{3,2},{4,5},{5,4},{6,7},{7,6},{8,9},{9,8},{10,11... | collective-permute-start | bytes 1572872 | tf_op jit(solution)/shard_map/ppermute | solution.py:24
  51.8 16.1 %collective-permute-start.18 = (bf16[256,1024]{1,0:T(8,128)(2,1)S(1)}, bf16[256,1024]{1,0:T(8,128)(2,1)S(1)}, u32[]{:S(2)}, u32[]{:S(2)}) collective-permute-start(bf16[256,1024]{1,0:T(8,128)(2,1)S(1)} %collective-permute-done.14.refs_5_), channel_id=1, source_target_pairs={{0,4},{1,5},{2,6},{3,7},{4,8},{5,9},{6,10},{7,11},{8,12},{9,13},{1... | collective-permute-start | bytes 1572872 | tf_op jit(solution)/shard_map/ppermute | solution.py:24
  51.8 4.4 %collective-permute-start.19 = (bf16[64,2560]{1,0:T(8,128)(2,1)S(1)}, bf16[64,2560]{1,0:T(8,128)(2,1)S(1)}, u32[]{:S(2)}, u32[]{:S(2)}) collective-permute-start(bf16[64,2560]{1,0:T(8,128)(2,1)S(1)} %get-tuple-element.67), channel_id=1, source_target_pairs={{0,1},{1,0},{2,3},{3,2},{4,5},{5,4},{6,7},{7,6},{8,9},{9,8},{10,11... | collective-permute-start | bytes 983048 | tf_op jit(solution)/shard_map/ppermute | solution.py:24
  52.3 4.7 %collective-permute-start.20 = (bf16[64,2560]{1,0:T(8,128)(2,1)S(1)}, bf16[64,2560]{1,0:T(8,128)(2,1)S(1)}, u32[]{:S(2)}, u32[]{:S(2)}) collective-permute-start(bf16[64,2560]{1,0:T(8,128)(2,1)S(1)} %get-tuple-element.68), channel_id=1, source_target_pairs={{0,1},{1,0},{2,3},{3,2},{4,5},{5,4},{6,7},{7,6},{8,9},{9,8},{10,11... | collective-permute-start | bytes 983048 | tf_op jit(solution)/shard_map/ppermute | solution.py:24
  52.3 7.3 %collective-permute-start.12 = (bf16[176,512]{1,0:T(8,128)(2,1)S(1)}, bf16[176,512]{1,0:T(8,128)(2,1)S(1)}, u32[]{:S(2)}, u32[]{:S(2)}) collective-permute-start(bf16[176,512]{1,0:T(8,128)(2,1)S(1)} %get-tuple-element.61), channel_id=1, source_target_pairs={{0,2},{1,3},{2,0},{3,1},{4,6},{5,7},{6,4},{7,5},{8,10},{9,11},{10,... | collective-permute-start | bytes 540680 | tf_op jit(solution)/shard_map/ppermute | solution.py:24
  53.8 9.9 %collective-permute-start.13 = (bf16[176,512]{1,0:T(8,128)(2,1)S(1)}, bf16[176,512]{1,0:T(8,128)(2,1)S(1)}, u32[]{:S(2)}, u32[]{:S(2)}) collective-permute-start(bf16[176,512]{1,0:T(8,128)(2,1)S(1)} %get-tuple-element.62), channel_id=1, source_target_pairs={{0,18},{1,19},{2,16},{3,17},{4,22},{5,23},{6,20},{7,21},{8,26},{9,... | collective-permute-start | bytes 540680 | tf_op jit(solution)/shard_map/ppermute | solution.py:24
  56.2 11.8 %collective-permute-start.16 = (bf16[176,512]{1,0:T(8,128)(2,1)S(1)}, bf16[176,512]{1,0:T(8,128)(2,1)S(1)}, u32[]{:S(2)}, u32[]{:S(2)}) collective-permute-start(bf16[176,512]{1,0:T(8,128)(2,1)S(1)} %get-tuple-element.64), channel_id=1, source_target_pairs={{0,2},{1,3},{2,0},{3,1},{4,6},{5,7},{6,4},{7,5},{8,10},{9,11},{10,... | collective-permute-start | bytes 540680 | tf_op jit(solution)/shard_map/ppermute | solution.py:24
  57.0 14.0 %collective-permute-start.17 = (bf16[176,512]{1,0:T(8,128)(2,1)S(1)}, bf16[176,512]{1,0:T(8,128)(2,1)S(1)}, u32[]{:S(2)}, u32[]{:S(2)}) collective-permute-start(bf16[176,512]{1,0:T(8,128)(2,1)S(1)} %get-tuple-element.65), channel_id=1, source_target_pairs={{0,18},{1,19},{2,16},{3,17},{4,22},{5,23},{6,20},{7,21},{8,26},{9,... | collective-permute-start | bytes 540680 | tf_op jit(solution)/shard_map/ppermute | solution.py:24
  71.0 4.1 %collective-permute-start.21 = (bf16[256,1024]{1,0:T(8,128)(2,1)S(1)}, bf16[256,1024]{1,0:T(8,128)(2,1)S(1)}, u32[]{:S(2)}, u32[]{:S(2)}) collective-permute-start(bf16[256,1024]{1,0:T(8,128)(2,1)S(1)} %collective-permute-done.18.refs_5_), channel_id=1, source_target_pairs={{0,1},{1,0},{2,3},{3,2},{4,5},{5,4},{6,7},{7,6},{8,9},{9,8},{10,11... | collective-permute-start | bytes 1572872 | tf_op jit(solution)/shard_map/ppermute | solution.py:24
  71.0 8.9 %collective-permute-start.26 = (bf16[16,5120]{1,0:T(8,128)(2,1)S(1)}, bf16[16,5120]{1,0:T(8,128)(2,1)S(1)}, u32[]{:S(2)}, u32[]{:S(2)}) collective-permute-start(bf16[16,5120]{1,0:T(8,128)(2,1)S(1)} %get-tuple-element.80), channel_id=1, source_target_pairs={{0,4},{1,5},{2,6},{3,7},{4,8},{5,9},{6,10},{7,11},{8,12},{9,13},{1... | collective-permute-start | bytes 491528 | tf_op jit(solution)/shard_map/ppermute | solution.py:24
  71.0 15.5 %collective-permute-start.25 = (bf16[16,5120]{1,0:T(8,128)(2,1)S(1)}, bf16[16,5120]{1,0:T(8,128)(2,1)S(1)}, u32[]{:S(2)}, u32[]{:S(2)}) collective-permute-start(bf16[16,5120]{1,0:T(8,128)(2,1)S(1)} %get-tuple-element.78), channel_id=1, source_target_pairs={{0,8},{1,9},{2,10},{3,11},{4,12},{5,13},{6,14},{7,15},{8,0},{9,1},... | collective-permute-start | bytes 491528 | tf_op jit(solution)/shard_map/ppermute | solution.py:24
  75.1 11.4 %collective-permute-start.24 = (bf16[16,5120]{1,0:T(8,128)(2,1)S(1)}, bf16[16,5120]{1,0:T(8,128)(2,1)S(1)}, u32[]{:S(2)}, u32[]{:S(2)}) collective-permute-start(bf16[16,5120]{1,0:T(8,128)(2,1)S(1)} %get-tuple-element.76), channel_id=1, source_target_pairs={{0,12},{1,13},{2,14},{3,15},{4,0},{5,1},{6,2},{7,3},{8,4},{9,5},{1... | collective-permute-start | bytes 491528 | tf_op jit(solution)/shard_map/ppermute | solution.py:24
  76.2 12.7 %collective-permute-start.23 = (bf16[176,512]{1,0:T(8,128)(2,1)S(1)}, bf16[176,512]{1,0:T(8,128)(2,1)S(1)}, u32[]{:S(2)}, u32[]{:S(2)}) collective-permute-start(bf16[176,512]{1,0:T(8,128)(2,1)S(1)} %get-tuple-element.74), channel_id=1, source_target_pairs={{0,18},{1,19},{2,16},{3,17},{4,22},{5,23},{6,20},{7,21},{8,26},{9,... | collective-permute-start | bytes 540680 | tf_op jit(solution)/shard_map/ppermute | solution.py:24
  78.4 10.4 %collective-permute-start.22 = (bf16[176,512]{1,0:T(8,128)(2,1)S(1)}, bf16[176,512]{1,0:T(8,128)(2,1)S(1)}, u32[]{:S(2)}, u32[]{:S(2)}) collective-permute-start(bf16[176,512]{1,0:T(8,128)(2,1)S(1)} %get-tuple-element.72), channel_id=1, source_target_pairs={{0,2},{1,3},{2,0},{3,1},{4,6},{5,7},{6,4},{7,5},{8,10},{9,11},{10,... | collective-permute-start | bytes 540680 | tf_op jit(solution)/shard_map/ppermute | solution.py:24
  86.6 1.5 %collective-permute-start.27 = (bf16[16,5120]{1,0:T(8,128)(2,1)S(1)}, bf16[16,5120]{1,0:T(8,128)(2,1)S(1)}, u32[]{:S(2)}, u32[]{:S(2)}) collective-permute-start(bf16[16,5120]{1,0:T(8,128)(2,1)S(1)} %shard_map.104.refs_0_), channel_id=1, source_target_pairs={{0,1},{1,0},{2,3},{3,2},{4,5},{5,4},{6,7},{7,6},{8,9},{9,8},{10,11... | collective-permute-start | bytes 491528 | tf_op jit(solution)/shard_map/ppermute | solution.py:24
  (3 other events, 2.2 us)

commit v8 on v6

--- a/solution.py
+++ b/solution.py
@@ -246,6 +246,16 @@
     piece = half // replicas
     cols = width + value_width
 
+    own = call(
+        functools.partial(own_kernel, (groups, holders, shard)),
+        [jax.ShapeDtypeStruct((rows, holders * half + value_width), BF16)],
+        (adapter_down_weight[0], adapter_up_weight[0]),
+    )[0]
+    ring = [lax.dynamic_slice_in_dim(frozen, (group * replicas + core) * piece, piece, axis=0)]
+    held = [own]
+    for k in range(1, holders):
+        held.append(moved(own, lambda g, z, s, r: (g, z + k, s, r)))
+    ring.append(moved(ring[0], lambda g, z, s, r: (g, z + 1, s, r)))
     tagged = call(
         tag_kernel,
         [jax.ShapeDtypeStruct((tokens, value_width + LANES), BF16)],
@@ -253,21 +263,10 @@
         scalars=1,
     )[0]
     grads = [tagged] + [
-        moved(tagged, lambda g, z, s, r: (g - dg, z, s, r)) for dg in range(1, groups)
+        moved(after(tagged, held[-1]), lambda g, z, s, r: (g - dg, z, s, r))
+        for dg in range(1, groups)
     ]
 
-    own = call(
-        functools.partial(own_kernel, (groups, holders, shard)),
-        [jax.ShapeDtypeStruct((rows, holders * half + value_width), BF16)],
-        (adapter_down_weight[0], adapter_up_weight[0]),
-    )[0]
-    held = [own]
-    for k in range(1, holders):
-        held.append(moved(own, lambda g, z, s, r: (g, z + k, s, r)))
-
-    ring = [lax.dynamic_slice_in_dim(frozen, (group * replicas + core) * piece, piece, axis=0)]
-    ring.append(moved(ring[0], lambda g, z, s, r: (g, z + 1, s, r)))
-    held, grads, ring = lax.optimization_barrier((held, grads, ring))
     joined = call(
         join_kernel,
         [
@@ -327,10 +326,8 @@
 
     arrived, outs = [], []
     for k in range(holders):
-        if k > 1:
-            last = ring[-1]
-            if k > 2:
-                last = after(last, *outs[k - 2], part)
+        for j in range(len(ring), min(k + 2, holders) if k > 1 else k + 1):
+            last = after(ring[-1], *outs[j - 2], part) if j > 2 else ring[-1]
             ring.append(moved(last, lambda g, z, s, r: (g, z + 1, s, r)))
         gate = [*arrived[k - 2], *outs[k - 1]] if k > 1 else []
         blocks = pieces_of(k, *gate, *(chip[:1] if k > 2 else ()))

time: 85.4 us -> 90 us (1.054)
  waiting for transfers between devices: 38.1 us -> 47.2 us
  starting transfers between devices: 32.1 us -> 27.7 us
    ppermute x28, waiting for transfers between devices: 38.1 us -> 47.2 us  [moved(): return lax.ppermute(x, AXES, pairs)]
    ppermute x28, starting transfers between devices: 32.1 us -> 27.7 us  [moved(): return lax.ppermute(x, AXES, pairs)]
  transfers between devices with their start and end apart: 28 -> 28, of which waited for: 14 -> 15; matrix products, arithmetic and copies ran while one was open for 0% -> 0% of each run, Pallas kernels for 9% -> 8%
where the time goes in v8:
time: 90 us; the launch traced here: 89.8 us
  waiting for transfers between devices  47.2 us (52%)
  starting transfers between devices  27.7 us (31%)
  Pallas kernels  8.77 us (10%)
  local copies, waits for them, and re-layouts  5.34 us (6%)
    ppermute x28, waiting for transfers between devices, moved(): return lax.ppermute(x, AXES, pairs)  47.2 us
    ppermute x28, starting transfers between devices, moved(): return lax.ppermute(x, AXES, pairs)  27.7 us
    pallas_call x12, Pallas kernels, call(): pl.pallas_call(kernel, out_shape=out_shape, in_specs=[pl.BlockSpec(memory...  8.77 us
    unnamed x14, local copies, waits for them, and re-layouts  4.11 us
  transfers between devices with their start and end apart: 28, of which 15 were waited for; matrix products, arithmetic and copies ran while one was open for 0% of the time, Pallas kernels for 8%

profile of v8, /device:TPU:0, one launch (start us, length us, event | category | flops | bytes accessed | tf_op | source)
XLA Modules:
  0.0 89.8 jit_solution(13503592021378498409)
XLA Ops:
  0.6 1.2 %dynamic-slice_bitcast_fusion = bf16[256,1024]{1,0:T(8,128)(2,1)S(1)} fusion(bf16[1,1024,1024]{2,1,0:T(8,128)(2,1)} %param.11, s32[]{:T(128)S(6)} %select_n.3), kind=kLoop, calls=%fused_computation | loop fusion | bytes 1048580 | tf_op jit(solution)/shard_map/dynamic_slice | solution.py:254
  1.9 3.1 %collective-permute-start.10 = (bf16[256,1024]{1,0:T(8,128)(2,1)S(1)}, bf16[256,1024]{1,0:T(8,128)(2,1)S(1)}, u32[]{:S(2)}, u32[]{:S(2)}) collective-permute-start(bf16[256,1024]{1,0:T(8,128)(2,1)S(1)} %dynamic-slice_bitcast_fusion), channel_id=1, source_target_pairs={{0,4},{1,5},{2,6},{3,7},{4,8},{5,9},{6,10},{7,11},{8,12},{9,13},{1... | collective-permute-start | bytes 1572872 | tf_op jit(solution)/shard_map/ppermute | solution.py:24
  6.8 2.1 %collective-permute-start = (bf16[16,3072]{1,0:T(8,128)(2,1)S(1)}, bf16[16,3072]{1,0:T(8,128)(2,1)S(1)}, u32[]{:S(2)}, u32[]{:S(2)}) collective-permute-start(bf16[16,3072]{1,0:T(8,128)(2,1)S(1)} %shard_map.95.refs_0_), channel_id=1, source_target_pairs={{0,12},{1,13},{2,14},{3,15},{4,0},{5,1},{6,2},{7,3},{8,4},{9,5},{1... | collective-permute-start | bytes 294920 | tf_op jit(solution)/shard_map/ppermute | solution.py:24
  8.9 2.6 %collective-permute-start.3 = (bf16[16,3072]{1,0:T(8,128)(2,1)S(1)}, bf16[16,3072]{1,0:T(8,128)(2,1)S(1)}, u32[]{:S(2)}, u32[]{:S(2)}) collective-permute-start(bf16[16,3072]{1,0:T(8,128)(2,1)S(1)} %shard_map.95.refs_0_), channel_id=1, source_target_pairs={{0,8},{1,9},{2,10},{3,11},{4,12},{5,13},{6,14},{7,15},{8,0},{9,1},... | collective-permute-start | bytes 294920 | tf_op jit(solution)/shard_map/ppermute | solution.py:24
  14.5 7.2 %collective-permute-done.refs_3_ = bf16[16,3072]{1,0:T(8,128)(2,1)S(1)} collective-permute-done((bf16[16,3072]{1,0:T(8,128)(2,1)S(1)}, bf16[16,3072]{1,0:T(8,128)(2,1)S(1)}, u32[]{:S(2)}, u32[]{:S(2)}) %collective-permute-start) | collective-permute-done | bytes 98336 | tf_op jit(solution)/shard_map/ppermute | solution.py:24
  21.7 1.9 %collective-permute-start.1 = (bf16[176,1152]{1,0:T(8,128)(2,1)S(1)}, bf16[176,1152]{1,0:T(8,128)(2,1)S(1)}, u32[]{:S(2)}, u32[]{:S(2)}) collective-permute-start(bf16[176,1152]{1,0:T(8,128)(2,1)S(1)} %shard_map.94.refs_0_.refs_1_), channel_id=1, source_target_pairs={{0,16},{1,17},{2,18},{3,19},{4,20},{5,21},{6,22},{7,23},{8,24},{9,... | collective-permute-start | bytes 1216520 | tf_op jit(solution)/shard_map/ppermute | solution.py:24
  24.1 3.2 %collective-permute-done.3.refs_2_ = bf16[16,3072]{1,0:T(8,128)(2,1)S(1)} collective-permute-done((bf16[16,3072]{1,0:T(8,128)(2,1)S(1)}, bf16[16,3072]{1,0:T(8,128)(2,1)S(1)}, u32[]{:S(2)}, u32[]{:S(2)}) %collective-permute-start.3) | collective-permute-done | bytes 98336 | tf_op jit(solution)/shard_map/ppermute | solution.py:24
  27.9 1.5 %collective-permute-start.8 = (bf16[64,2048]{1,0:T(8,128)(2,1)S(1)}, bf16[64,2048]{1,0:T(8,128)(2,1)S(1)}, u32[]{:S(2)}, u32[]{:S(2)}) collective-permute-start(bf16[64,2048]{1,0:T(8,128)(2,1)S(1)} %get-tuple-element.35.refs_2_.refs_3_), channel_id=1, source_target_pairs={{0,16},{1,17},{2,18},{3,19},{4,20},{5,21},{6,22},{7,23},{8,24},{9,... | collective-permute-start | bytes 786440 | tf_op jit(solution)/shard_map/ppermute | solution.py:24
  29.5 4.4 %collective-permute-done.1.refs_1_ = bf16[176,1152]{1,0:T(8,128)(2,1)S(1)} collective-permute-done((bf16[176,1152]{1,0:T(8,128)(2,1)S(1)}, bf16[176,1152]{1,0:T(8,128)(2,1)S(1)}, u32[]{:S(2)}, u32[]{:S(2)}) %collective-permute-start.1) | collective-permute-done | bytes 405536 | tf_op jit(solution)/shard_map/ppermute | solution.py:24
  34.0 1.5 %shard_map.97 = (bf16[176,512]{1,0:T(8,128)(2,1)S(1)}, bf16[176,512]{1,0:T(8,128)(2,1)S(1)}, bf16[352,128]{1,0:T(8,128)(2,1)S(1)}) custom-call(bf16[176,1152]{1,0:T(8,128)(2,1)S(1)} %shard_map.94.refs_0_.refs_1_, bf16[176,1152]{1,0:T(8,128)(2,1)S(1)} %collective-permute-done.1.refs_1_, bf16[64,2048]{1,0:T(8,128)(2,1)S(1)} %get-tuple-element.35.refs_2_.refs_3_, ...), custom_call_target="tpu_custom_call" | custom-call | flops 1000 | bytes 1000 | tf_op jit(solution)/shard_map/pallas_call | solution.py:41
  35.4 3.2 %collective-permute-done.8.refs_5_ = bf16[64,2048]{1,0:T(8,128)(2,1)S(1)} collective-permute-done((bf16[64,2048]{1,0:T(8,128)(2,1)S(1)}, bf16[64,2048]{1,0:T(8,128)(2,1)S(1)}, u32[]{:S(2)}, u32[]{:S(2)}) %collective-permute-start.8) | collective-permute-done | bytes 262176 | tf_op jit(solution)/shard_map/ppermute | solution.py:24
  38.6 1.7 %collective-permute-start.6 = (bf16[176,512]{1,0:T(8,128)(2,1)S(1)}, bf16[176,512]{1,0:T(8,128)(2,1)S(1)}, u32[]{:S(2)}, u32[]{:S(2)}) collective-permute-start(bf16[176,512]{1,0:T(8,128)(2,1)S(1)} %get-tuple-element.37), channel_id=1, source_target_pairs={{0,2},{1,3},{2,0},{3,1},{4,6},{5,7},{6,4},{7,5},{8,10},{9,11},{10,... | collective-permute-start | bytes 540680 | tf_op jit(solution)/shard_map/ppermute | solution.py:24
  40.4 1.5 %collective-permute-start.7 = (bf16[176,512]{1,0:T(8,128)(2,1)S(1)}, bf16[176,512]{1,0:T(8,128)(2,1)S(1)}, u32[]{:S(2)}, u32[]{:S(2)}) collective-permute-start(bf16[176,512]{1,0:T(8,128)(2,1)S(1)} %get-tuple-element.38), channel_id=1, source_target_pairs={{0,18},{1,19},{2,16},{3,17},{4,22},{5,23},{6,20},{7,21},{8,26},{9,... | collective-permute-start | bytes 540680 | tf_op jit(solution)/shard_map/ppermute | solution.py:24
  41.9 1.3 %shard_map.98 = (f32[64,5120]{1,0:T(8,128)S(1)}, bf16[64,2560]{1,0:T(8,128)(2,1)S(1)}, bf16[64,2560]{1,0:T(8,128)(2,1)S(1)}) custom-call(bf16[176,4096]{1,0:T(8,128)(2,1)S(1)} %bitcast.12, bf16[176,1152]{1,0:T(8,128)(2,1)S(1)} %shard_map.94.refs_0_.refs_1_, bf16[352,128]{1,0:T(8,128)(2,1)S(1)} %get-tuple-element.39.refs_2_.refs_4_, ...), custom_call_target="tpu_custom_call" | custom-call | flops 1000 | bytes 1000 | tf_op jit(solution)/shard_map/pallas_call | solution.py:41
  43.2 1.0 %shard_map.99 = (bf16[176,512]{1,0:T(8,128)(2,1)S(1)}, bf16[176,512]{1,0:T(8,128)(2,1)S(1)}) custom-call(bf16[176,1152]{1,0:T(8,128)(2,1)S(1)} %shard_map.94.refs_0_.refs_1_, bf16[176,1152]{1,0:T(8,128)(2,1)S(1)} %collective-permute-done.1.refs_1_, bf16[64,2048]{1,0:T(8,128)(2,1)S(1)} %get-tuple-element.35.refs_2_.refs_3_, ...), custom_call_target="tpu_custom_call" | custom-call | flops 1000 | bytes 1000 | tf_op jit(solution)/shard_map/pallas_call | solution.py:41
  44.2 1.8 %collective-permute-done.6.refs_0_ = bf16[176,512]{1,0:T(8,128)(2,1)S(1)} collective-permute-done((bf16[176,512]{1,0:T(8,128)(2,1)S(1)}, bf16[176,512]{1,0:T(8,128)(2,1)S(1)}, u32[]{:S(2)}, u32[]{:S(2)}) %collective-permute-start.6) | collective-permute-done | bytes 180256 | tf_op jit(solution)/shard_map/ppermute | solution.py:24
  46.0 4.7 %collective-permute-done.7.refs_1_ = bf16[176,512]{1,0:T(8,128)(2,1)S(1)} collective-permute-done((bf16[176,512]{1,0:T(8,128)(2,1)S(1)}, bf16[176,512]{1,0:T(8,128)(2,1)S(1)}, u32[]{:S(2)}, u32[]{:S(2)}) %collective-permute-start.7) | collective-permute-done | bytes 180256 | tf_op jit(solution)/shard_map/ppermute | solution.py:24
  51.7 1.5 %collective-permute-start.12 = (bf16[176,512]{1,0:T(8,128)(2,1)S(1)}, bf16[176,512]{1,0:T(8,128)(2,1)S(1)}, u32[]{:S(2)}, u32[]{:S(2)}) collective-permute-start(bf16[176,512]{1,0:T(8,128)(2,1)S(1)} %get-tuple-element.43), channel_id=1, source_target_pairs={{0,2},{1,3},{2,0},{3,1},{4,6},{5,7},{6,4},{7,5},{8,10},{9,11},{10,... | collective-permute-start | bytes 540680 | tf_op jit(solution)/shard_map/ppermute | solution.py:24
  53.2 1.2 %collective-permute-start.13 = (bf16[176,512]{1,0:T(8,128)(2,1)S(1)}, bf16[176,512]{1,0:T(8,128)(2,1)S(1)}, u32[]{:S(2)}, u32[]{:S(2)}) collective-permute-start(bf16[176,512]{1,0:T(8,128)(2,1)S(1)} %get-tuple-element.44), channel_id=1, source_target_pairs={{0,18},{1,19},{2,16},{3,17},{4,22},{5,23},{6,20},{7,21},{8,26},{9,... | collective-permute-start | bytes 540680 | tf_op jit(solution)/shard_map/ppermute | solution.py:24
  54.6 1.0 %shard_map.100 = (bf16[176,512]{1,0:T(8,128)(2,1)S(1)}, bf16[176,512]{1,0:T(8,128)(2,1)S(1)}) custom-call(bf16[176,1152]{1,0:T(8,128)(2,1)S(1)} %shard_map.94.refs_0_.refs_1_, bf16[176,1152]{1,0:T(8,128)(2,1)S(1)} %collective-permute-done.1.refs_1_, bf16[64,2048]{1,0:T(8,128)(2,1)S(1)} %get-tuple-element.35.refs_2_.refs_3_, ...), custom_call_target="tpu_custom_call" | custom-call | flops 1000 | bytes 1000 | tf_op jit(solution)/shard_map/pallas_call | solution.py:41
  55.7 3.4 %collective-permute-done.12.refs_2_ = bf16[176,512]{1,0:T(8,128)(2,1)S(1)} collective-permute-done((bf16[176,512]{1,0:T(8,128)(2,1)S(1)}, bf16[176,512]{1,0:T(8,128)(2,1)S(1)}, u32[]{:S(2)}, u32[]{:S(2)}) %collective-permute-start.12) | collective-permute-done | bytes 180256 | tf_op jit(solution)/shard_map/ppermute | solution.py:24
  59.1 2.9 %collective-permute-done.13.refs_3_ = bf16[176,512]{1,0:T(8,128)(2,1)S(1)} collective-permute-done((bf16[176,512]{1,0:T(8,128)(2,1)S(1)}, bf16[176,512]{1,0:T(8,128)(2,1)S(1)}, u32[]{:S(2)}, u32[]{:S(2)}) %collective-permute-start.13) | collective-permute-done | bytes 180256 | tf_op jit(solution)/shard_map/ppermute | solution.py:24
  62.0 4.8 %collective-permute-done.18.refs_5_ = bf16[256,1024]{1,0:T(8,128)(2,1)S(1)} collective-permute-done((bf16[256,1024]{1,0:T(8,128)(2,1)S(1)}, bf16[256,1024]{1,0:T(8,128)(2,1)S(1)}, u32[]{:S(2)}, u32[]{:S(2)}) %collective-permute-start.18) | collective-permute-done | bytes 524320 | tf_op jit(solution)/shard_map/ppermute | solution.py:24
  66.8 1.5 %collective-permute-start.16 = (bf16[176,512]{1,0:T(8,128)(2,1)S(1)}, bf16[176,512]{1,0:T(8,128)(2,1)S(1)}, u32[]{:S(2)}, u32[]{:S(2)}) collective-permute-start(bf16[176,512]{1,0:T(8,128)(2,1)S(1)} %get-tuple-element.46), channel_id=1, source_target_pairs={{0,2},{1,3},{2,0},{3,1},{4,6},{5,7},{6,4},{7,5},{8,10},{9,11},{10,... | collective-permute-start | bytes 540680 | tf_op jit(solution)/shard_map/ppermute | solution.py:24
  69.0 3.3 %collective-permute-start.24 = (bf16[16,5120]{1,0:T(8,128)(2,1)S(1)}, bf16[16,5120]{1,0:T(8,128)(2,1)S(1)}, u32[]{:S(2)}, u32[]{:S(2)}) collective-permute-start(bf16[16,5120]{1,0:T(8,128)(2,1)S(1)} %get-tuple-element.58), channel_id=1, source_target_pairs={{0,12},{1,13},{2,14},{3,15},{4,0},{5,1},{6,2},{7,3},{8,4},{9,5},{1... | collective-permute-start | bytes 491528 | tf_op jit(solution)/shard_map/ppermute | solution.py:24
  72.4 1.0 %shard_map.102 = (bf16[176,512]{1,0:T(8,128)(2,1)S(1)}, bf16[176,512]{1,0:T(8,128)(2,1)S(1)}) custom-call(bf16[176,1152]{1,0:T(8,128)(2,1)S(1)} %shard_map.94.refs_0_.refs_1_, bf16[176,1152]{1,0:T(8,128)(2,1)S(1)} %collective-permute-done.1.refs_1_, bf16[64,2048]{1,0:T(8,128)(2,1)S(1)} %get-tuple-element.35.refs_2_.refs_3_, ...), custom_call_target="tpu_custom_call" | custom-call | flops 1000 | bytes 1000 | tf_op jit(solution)/shard_map/pallas_call | solution.py:41
  74.1 3.2 %collective-permute-done.17.refs_5_ = bf16[176,512]{1,0:T(8,128)(2,1)S(1)} collective-permute-done((bf16[176,512]{1,0:T(8,128)(2,1)S(1)}, bf16[176,512]{1,0:T(8,128)(2,1)S(1)}, u32[]{:S(2)}, u32[]{:S(2)}) %collective-permute-start.17) | collective-permute-done | bytes 180256 | tf_op jit(solution)/shard_map/ppermute | solution.py:24
  77.3 2.7 %collective-permute-start.23 = (bf16[176,512]{1,0:T(8,128)(2,1)S(1)}, bf16[176,512]{1,0:T(8,128)(2,1)S(1)}, u32[]{:S(2)}, u32[]{:S(2)}) collective-permute-start(bf16[176,512]{1,0:T(8,128)(2,1)S(1)} %get-tuple-element.56), channel_id=1, source_target_pairs={{0,18},{1,19},{2,16},{3,17},{4,22},{5,23},{6,20},{7,21},{8,26},{9,... | collective-permute-start | bytes 540680 | tf_op jit(solution)/shard_map/ppermute | solution.py:24
  80.5 3.0 %collective-permute-done.25.refs_2_ = bf16[16,5120]{1,0:T(8,128)(2,1)S(1)} collective-permute-done((bf16[16,5120]{1,0:T(8,128)(2,1)S(1)}, bf16[16,5120]{1,0:T(8,128)(2,1)S(1)}, u32[]{:S(2)}, u32[]{:S(2)}) %collective-permute-start.25) | collective-permute-done | bytes 163872 | tf_op jit(solution)/shard_map/ppermute | solution.py:24
  83.7 1.4 %collective-permute-done.27.refs_1_ = bf16[16,5120]{1,0:T(8,128)(2,1)S(1)} collective-permute-done((bf16[16,5120]{1,0:T(8,128)(2,1)S(1)}, bf16[16,5120]{1,0:T(8,128)(2,1)S(1)}, u32[]{:S(2)}, u32[]{:S(2)}) %collective-permute-start.27) | collective-permute-done | bytes 163872 | tf_op jit(solution)/shard_map/ppermute | solution.py:24
  85.9 2.7 %collective-permute-done.22.refs_6_ = bf16[176,512]{1,0:T(8,128)(2,1)S(1)} collective-permute-done((bf16[176,512]{1,0:T(8,128)(2,1)S(1)}, bf16[176,512]{1,0:T(8,128)(2,1)S(1)}, u32[]{:S(2)}, u32[]{:S(2)}) %collective-permute-start.22) | collective-permute-done | bytes 180256 | tf_op jit(solution)/shard_map/ppermute | solution.py:24
  88.6 1.2 %shard_map.103 = bf16[176,4096]{1,0:T(8,128)(2,1)} custom-call(bf16[176,512]{1,0:T(8,128)(2,1)S(1)} %collective-permute-done.6.refs_0_, bf16[176,512]{1,0:T(8,128)(2,1)S(1)} %collective-permute-done.7.refs_1_, bf16[176,512]{1,0:T(8,128)(2,1)S(1)} %collective-permute-done.12.refs_2_, bf16[176,512]{1,0:T(8,128)(2,1)S(1)} %collective-permute-done.13.refs_3_, ...), custom_call_target="tpu_custom_call" | custom-call | flops 1000 | bytes 1000 | tf_op jit(solution)/shard_map/pallas_call | solution.py:41
  (51 shorter events, 10.2 us)
Async XLA Ops:
  0.6 33.3 %copy-start = (bf16[1,1024,1024]{2,1,0:T(8,128)(2,1)S(1)}, bf16[1,1024,1024]{2,1,0:T(8,128)(2,1)}, u32[]{:S(2)}) copy-start(bf16[1,1024,1024]{2,1,0:T(8,128)(2,1)} %param.11) | copy-start | bytes 6291460
  1.9 27.6 %collective-permute-start.10 = (bf16[256,1024]{1,0:T(8,128)(2,1)S(1)}, bf16[256,1024]{1,0:T(8,128)(2,1)S(1)}, u32[]{:S(2)}, u32[]{:S(2)}) collective-permute-start(bf16[256,1024]{1,0:T(8,128)(2,1)S(1)} %dynamic-slice_bitcast_fusion), channel_id=1, source_target_pairs={{0,4},{1,5},{2,6},{3,7},{4,8},{5,9},{6,10},{7,11},{8,12},{9,13},{1... | collective-permute-start | bytes 1572872 | tf_op jit(solution)/shard_map/ppermute | solution.py:24
  5.0 0.9 %copy-start.3 = (bf16[1,2,16,4096]{3,2,1,0:T(8,128)(2,1)S(1)}, bf16[1,2,16,4096]{3,2,1,0:T(8,128)(2,1)}, u32[]{:S(2)}) copy-start(bf16[1,2,16,4096]{3,2,1,0:T(8,128)(2,1)} %param.12) | copy-start | bytes 786436
  6.8 15.0 %collective-permute-start = (bf16[16,3072]{1,0:T(8,128)(2,1)S(1)}, bf16[16,3072]{1,0:T(8,128)(2,1)S(1)}, u32[]{:S(2)}, u32[]{:S(2)}) collective-permute-start(bf16[16,3072]{1,0:T(8,128)(2,1)S(1)} %shard_map.95.refs_0_), channel_id=1, source_target_pairs={{0,12},{1,13},{2,14},{3,15},{4,0},{5,1},{6,2},{7,3},{8,4},{9,5},{1... | collective-permute-start | bytes 294920 | tf_op jit(solution)/shard_map/ppermute | solution.py:24
  8.8 15.2 %collective-permute-start.2 = (bf16[16,3072]{1,0:T(8,128)(2,1)S(1)}, bf16[16,3072]{1,0:T(8,128)(2,1)S(1)}, u32[]{:S(2)}, u32[]{:S(2)}) collective-permute-start(bf16[16,3072]{1,0:T(8,128)(2,1)S(1)} %shard_map.95.refs_0_), channel_id=1, source_target_pairs={{0,4},{1,5},{2,6},{3,7},{4,8},{5,9},{6,10},{7,11},{8,12},{9,13},{1... | collective-permute-start | bytes 294920 | tf_op jit(solution)/shard_map/ppermute | solution.py:24
  8.9 18.5 %collective-permute-start.3 = (bf16[16,3072]{1,0:T(8,128)(2,1)S(1)}, bf16[16,3072]{1,0:T(8,128)(2,1)S(1)}, u32[]{:S(2)}, u32[]{:S(2)}) collective-permute-start(bf16[16,3072]{1,0:T(8,128)(2,1)S(1)} %shard_map.95.refs_0_), channel_id=1, source_target_pairs={{0,8},{1,9},{2,10},{3,11},{4,12},{5,13},{6,14},{7,15},{8,0},{9,1},... | collective-permute-start | bytes 294920 | tf_op jit(solution)/shard_map/ppermute | solution.py:24
  11.4 1.0 %copy-start.2 = (bf16[1,176,1024]{2,1,0:T(8,128)(2,1)S(1)}, bf16[1,176,1024]{2,1,0:T(8,128)(2,1)}, u32[]{:S(2)}) copy-start(bf16[1,176,1024]{2,1,0:T(8,128)(2,1)} %param.8) | copy-start | bytes 1081348
  21.7 12.2 %collective-permute-start.1 = (bf16[176,1152]{1,0:T(8,128)(2,1)S(1)}, bf16[176,1152]{1,0:T(8,128)(2,1)S(1)}, u32[]{:S(2)}, u32[]{:S(2)}) collective-permute-start(bf16[176,1152]{1,0:T(8,128)(2,1)S(1)} %shard_map.94.refs_0_.refs_1_), channel_id=1, source_target_pairs={{0,16},{1,17},{2,18},{3,19},{4,20},{5,21},{6,22},{7,23},{8,24},{9,... | collective-permute-start | bytes 1216520 | tf_op jit(solution)/shard_map/ppermute | solution.py:24
  27.4 2.1 %collective-permute-start.5 = (bf16[64,1024]{1,0:T(8,128)(2,1)S(1)}, bf16[64,1024]{1,0:T(8,128)(2,1)S(1)}, u32[]{:S(2)}, u32[]{:S(2)}) collective-permute-start(bf16[64,1024]{1,0:T(8,128)(2,1)S(1)} %get-tuple-element.36.refs_4_), channel_id=1, source_target_pairs={{0,1},{1,0},{2,3},{3,2},{4,5},{5,4},{6,7},{7,6},{8,9},{9,8},{10,11... | collective-permute-start | bytes 393224 | tf_op jit(solution)/shard_map/ppermute | solution.py:24
  27.4 2.1 %collective-permute-start.4 = (bf16[64,2048]{1,0:T(8,128)(2,1)S(1)}, bf16[64,2048]{1,0:T(8,128)(2,1)S(1)}, u32[]{:S(2)}, u32[]{:S(2)}) collective-permute-start(bf16[64,2048]{1,0:T(8,128)(2,1)S(1)} %get-tuple-element.35.refs_2_.refs_3_), channel_id=1, source_target_pairs={{0,1},{1,0},{2,3},{3,2},{4,5},{5,4},{6,7},{7,6},{8,9},{9,8},{10,11... | collective-permute-start | bytes 786440 | tf_op jit(solution)/shard_map/ppermute | solution.py:24
  27.9 10.7 %collective-permute-start.8 = (bf16[64,2048]{1,0:T(8,128)(2,1)S(1)}, bf16[64,2048]{1,0:T(8,128)(2,1)S(1)}, u32[]{:S(2)}, u32[]{:S(2)}) collective-permute-start(bf16[64,2048]{1,0:T(8,128)(2,1)S(1)} %get-tuple-element.35.refs_2_.refs_3_), channel_id=1, source_target_pairs={{0,16},{1,17},{2,18},{3,19},{4,20},{5,21},{6,22},{7,23},{8,24},{9,... | collective-permute-start | bytes 786440 | tf_op jit(solution)/shard_map/ppermute | solution.py:24
  29.5 13.7 %collective-permute-start.11 = (bf16[256,1024]{1,0:T(8,128)(2,1)S(1)}, bf16[256,1024]{1,0:T(8,128)(2,1)S(1)}, u32[]{:S(2)}, u32[]{:S(2)}) collective-permute-start(bf16[256,1024]{1,0:T(8,128)(2,1)S(1)} %collective-permute-done.10.refs_5_), channel_id=1, source_target_pairs={{0,1},{1,0},{2,3},{3,2},{4,5},{5,4},{6,7},{7,6},{8,9},{9,8},{10,11... | collective-permute-start | bytes 1572872 | tf_op jit(solution)/shard_map/ppermute | solution.py:24
  29.5 21.2 %collective-permute-start.14 = (bf16[256,1024]{1,0:T(8,128)(2,1)S(1)}, bf16[256,1024]{1,0:T(8,128)(2,1)S(1)}, u32[]{:S(2)}, u32[]{:S(2)}) collective-permute-start(bf16[256,1024]{1,0:T(8,128)(2,1)S(1)} %collective-permute-done.10.refs_5_), channel_id=1, source_target_pairs={{0,4},{1,5},{2,6},{3,7},{4,8},{5,9},{6,10},{7,11},{8,12},{9,13},{1... | collective-permute-start | bytes 1572872 | tf_op jit(solution)/shard_map/ppermute | solution.py:24
  34.0 7.9 %copy-start.1 = (bf16[1,176,4096]{2,1,0:T(8,128)(2,1)S(1)}, bf16[1,176,4096]{2,1,0:T(8,128)(2,1)}, u32[]{:S(2)}) copy-start(bf16[1,176,4096]{2,1,0:T(8,128)(2,1)} %param.7) | copy-start | bytes 4325380
  38.6 3.2 %collective-permute-start.9 = (bf16[64,2048]{1,0:T(8,128)(2,1)S(1)}, bf16[64,2048]{1,0:T(8,128)(2,1)S(1)}, u32[]{:S(2)}, u32[]{:S(2)}) collective-permute-start(bf16[64,2048]{1,0:T(8,128)(2,1)S(1)} %collective-permute-done.8.refs_5_), channel_id=1, source_target_pairs={{0,1},{1,0},{2,3},{3,2},{4,5},{5,4},{6,7},{7,6},{8,9},{9,8},{10,11... | collective-permute-start | bytes 786440 | tf_op jit(solution)/shard_map/ppermute | solution.py:24
  38.6 7.3 %collective-permute-start.6 = (bf16[176,512]{1,0:T(8,128)(2,1)S(1)}, bf16[176,512]{1,0:T(8,128)(2,1)S(1)}, u32[]{:S(2)}, u32[]{:S(2)}) collective-permute-start(bf16[176,512]{1,0:T(8,128)(2,1)S(1)} %get-tuple-element.37), channel_id=1, source_target_pairs={{0,2},{1,3},{2,0},{3,1},{4,6},{5,7},{6,4},{7,5},{8,10},{9,11},{10,... | collective-permute-start | bytes 540680 | tf_op jit(solution)/shard_map/ppermute | solution.py:24
  40.4 10.3 %collective-permute-start.7 = (bf16[176,512]{1,0:T(8,128)(2,1)S(1)}, bf16[176,512]{1,0:T(8,128)(2,1)S(1)}, u32[]{:S(2)}, u32[]{:S(2)}) collective-permute-start(bf16[176,512]{1,0:T(8,128)(2,1)S(1)} %get-tuple-element.38), channel_id=1, source_target_pairs={{0,18},{1,19},{2,16},{3,17},{4,22},{5,23},{6,20},{7,21},{8,26},{9,... | collective-permute-start | bytes 540680 | tf_op jit(solution)/shard_map/ppermute | solution.py:24
  50.6 4.0 %collective-permute-start.15 = (bf16[256,1024]{1,0:T(8,128)(2,1)S(1)}, bf16[256,1024]{1,0:T(8,128)(2,1)S(1)}, u32[]{:S(2)}, u32[]{:S(2)}) collective-permute-start(bf16[256,1024]{1,0:T(8,128)(2,1)S(1)} %collective-permute-done.14.refs_5_), channel_id=1, source_target_pairs={{0,1},{1,0},{2,3},{3,2},{4,5},{5,4},{6,7},{7,6},{8,9},{9,8},{10,11... | collective-permute-start | bytes 1572872 | tf_op jit(solution)/shard_map/ppermute | solution.py:24
  50.6 16.1 %collective-permute-start.18 = (bf16[256,1024]{1,0:T(8,128)(2,1)S(1)}, bf16[256,1024]{1,0:T(8,128)(2,1)S(1)}, u32[]{:S(2)}, u32[]{:S(2)}) collective-permute-start(bf16[256,1024]{1,0:T(8,128)(2,1)S(1)} %collective-permute-done.14.refs_5_), channel_id=1, source_target_pairs={{0,4},{1,5},{2,6},{3,7},{4,8},{5,9},{6,10},{7,11},{8,12},{9,13},{1... | collective-permute-start | bytes 1572872 | tf_op jit(solution)/shard_map/ppermute | solution.py:24
  51.2 2.0 %collective-permute-start.19 = (bf16[64,2560]{1,0:T(8,128)(2,1)S(1)}, bf16[64,2560]{1,0:T(8,128)(2,1)S(1)}, u32[]{:S(2)}, u32[]{:S(2)}) collective-permute-start(bf16[64,2560]{1,0:T(8,128)(2,1)S(1)} %get-tuple-element.49), channel_id=1, source_target_pairs={{0,1},{1,0},{2,3},{3,2},{4,5},{5,4},{6,7},{7,6},{8,9},{9,8},{10,11... | collective-permute-start | bytes 983048 | tf_op jit(solution)/shard_map/ppermute | solution.py:24
  51.4 3.0 %collective-permute-start.20 = (bf16[64,2560]{1,0:T(8,128)(2,1)S(1)}, bf16[64,2560]{1,0:T(8,128)(2,1)S(1)}, u32[]{:S(2)}, u32[]{:S(2)}) collective-permute-start(bf16[64,2560]{1,0:T(8,128)(2,1)S(1)} %get-tuple-element.50), channel_id=1, source_target_pairs={{0,1},{1,0},{2,3},{3,2},{4,5},{5,4},{6,7},{7,6},{8,9},{9,8},{10,11... | collective-permute-start | bytes 983048 | tf_op jit(solution)/shard_map/ppermute | solution.py:24
  51.7 7.4 %collective-permute-start.12 = (bf16[176,512]{1,0:T(8,128)(2,1)S(1)}, bf16[176,512]{1,0:T(8,128)(2,1)S(1)}, u32[]{:S(2)}, u32[]{:S(2)}) collective-permute-start(bf16[176,512]{1,0:T(8,128)(2,1)S(1)} %get-tuple-element.43), channel_id=1, source_target_pairs={{0,2},{1,3},{2,0},{3,1},{4,6},{5,7},{6,4},{7,5},{8,10},{9,11},{10,... | collective-permute-start | bytes 540680 | tf_op jit(solution)/shard_map/ppermute | solution.py:24
  53.2 8.8 %collective-permute-start.13 = (bf16[176,512]{1,0:T(8,128)(2,1)S(1)}, bf16[176,512]{1,0:T(8,128)(2,1)S(1)}, u32[]{:S(2)}, u32[]{:S(2)}) collective-permute-start(bf16[176,512]{1,0:T(8,128)(2,1)S(1)} %get-tuple-element.44), channel_id=1, source_target_pairs={{0,18},{1,19},{2,16},{3,17},{4,22},{5,23},{6,20},{7,21},{8,26},{9,... | collective-permute-start | bytes 540680 | tf_op jit(solution)/shard_map/ppermute | solution.py:24
  66.8 2.2 %collective-permute-start.21 = (bf16[256,1024]{1,0:T(8,128)(2,1)S(1)}, bf16[256,1024]{1,0:T(8,128)(2,1)S(1)}, u32[]{:S(2)}, u32[]{:S(2)}) collective-permute-start(bf16[256,1024]{1,0:T(8,128)(2,1)S(1)} %collective-permute-done.18.refs_5_), channel_id=1, source_target_pairs={{0,1},{1,0},{2,3},{3,2},{4,5},{5,4},{6,7},{7,6},{8,9},{9,8},{10,11... | collective-permute-start | bytes 1572872 | tf_op jit(solution)/shard_map/ppermute | solution.py:24
  66.8 7.3 %collective-permute-start.16 = (bf16[176,512]{1,0:T(8,128)(2,1)S(1)}, bf16[176,512]{1,0:T(8,128)(2,1)S(1)}, u32[]{:S(2)}, u32[]{:S(2)}) collective-permute-start(bf16[176,512]{1,0:T(8,128)(2,1)S(1)} %get-tuple-element.46), channel_id=1, source_target_pairs={{0,2},{1,3},{2,0},{3,1},{4,6},{5,7},{6,4},{7,5},{8,10},{9,11},{10,... | collective-permute-start | bytes 540680 | tf_op jit(solution)/shard_map/ppermute | solution.py:24
  68.3 9.1 %collective-permute-start.17 = (bf16[176,512]{1,0:T(8,128)(2,1)S(1)}, bf16[176,512]{1,0:T(8,128)(2,1)S(1)}, u32[]{:S(2)}, u32[]{:S(2)}) collective-permute-start(bf16[176,512]{1,0:T(8,128)(2,1)S(1)} %get-tuple-element.47), channel_id=1, source_target_pairs={{0,18},{1,19},{2,16},{3,17},{4,22},{5,23},{6,20},{7,21},{8,26},{9,... | collective-permute-start | bytes 540680 | tf_op jit(solution)/shard_map/ppermute | solution.py:24
  68.5 12.0 %collective-permute-start.26 = (bf16[16,5120]{1,0:T(8,128)(2,1)S(1)}, bf16[16,5120]{1,0:T(8,128)(2,1)S(1)}, u32[]{:S(2)}, u32[]{:S(2)}) collective-permute-start(bf16[16,5120]{1,0:T(8,128)(2,1)S(1)} %get-tuple-element.62), channel_id=1, source_target_pairs={{0,4},{1,5},{2,6},{3,7},{4,8},{5,9},{6,10},{7,11},{8,12},{9,13},{1... | collective-permute-start | bytes 491528 | tf_op jit(solution)/shard_map/ppermute | solution.py:24
  68.5 15.0 %collective-permute-start.25 = (bf16[16,5120]{1,0:T(8,128)(2,1)S(1)}, bf16[16,5120]{1,0:T(8,128)(2,1)S(1)}, u32[]{:S(2)}, u32[]{:S(2)}) collective-permute-start(bf16[16,5120]{1,0:T(8,128)(2,1)S(1)} %get-tuple-element.60), channel_id=1, source_target_pairs={{0,8},{1,9},{2,10},{3,11},{4,12},{5,13},{6,14},{7,15},{8,0},{9,1},... | collective-permute-start | bytes 491528 | tf_op jit(solution)/shard_map/ppermute | solution.py:24
  69.0 14.5 %collective-permute-start.24 = (bf16[16,5120]{1,0:T(8,128)(2,1)S(1)}, bf16[16,5120]{1,0:T(8,128)(2,1)S(1)}, u32[]{:S(2)}, u32[]{:S(2)}) collective-permute-start(bf16[16,5120]{1,0:T(8,128)(2,1)S(1)} %get-tuple-element.58), channel_id=1, source_target_pairs={{0,12},{1,13},{2,14},{3,15},{4,0},{5,1},{6,2},{7,3},{8,4},{9,5},{1... | collective-permute-start | bytes 491528 | tf_op jit(solution)/shard_map/ppermute | solution.py:24
  77.3 8.5 %collective-permute-start.23 = (bf16[176,512]{1,0:T(8,128)(2,1)S(1)}, bf16[176,512]{1,0:T(8,128)(2,1)S(1)}, u32[]{:S(2)}, u32[]{:S(2)}) collective-permute-start(bf16[176,512]{1,0:T(8,128)(2,1)S(1)} %get-tuple-element.56), channel_id=1, source_target_pairs={{0,18},{1,19},{2,16},{3,17},{4,22},{5,23},{6,20},{7,21},{8,26},{9,... | collective-permute-start | bytes 540680 | tf_op jit(solution)/shard_map/ppermute | solution.py:24
  80.0 8.6 %collective-permute-start.22 = (bf16[176,512]{1,0:T(8,128)(2,1)S(1)}, bf16[176,512]{1,0:T(8,128)(2,1)S(1)}, u32[]{:S(2)}, u32[]{:S(2)}) collective-permute-start(bf16[176,512]{1,0:T(8,128)(2,1)S(1)} %get-tuple-element.54), channel_id=1, source_target_pairs={{0,2},{1,3},{2,0},{3,1},{4,6},{5,7},{6,4},{7,5},{8,10},{9,11},{10,... | collective-permute-start | bytes 540680 | tf_op jit(solution)/shard_map/ppermute | solution.py:24
  83.7 1.5 %collective-permute-start.27 = (bf16[16,5120]{1,0:T(8,128)(2,1)S(1)}, bf16[16,5120]{1,0:T(8,128)(2,1)S(1)}, u32[]{:S(2)}, u32[]{:S(2)}) collective-permute-start(bf16[16,5120]{1,0:T(8,128)(2,1)S(1)} %shard_map.104.refs_0_), channel_id=1, source_target_pairs={{0,1},{1,0},{2,3},{3,2},{4,5},{5,4},{6,7},{7,6},{8,9},{9,8},{10,11... | collective-permute-start | bytes 491528 | tf_op jit(solution)/shard_map/ppermute | solution.py:24
  (3 other events, 2.2 us)

commit v9 on v6

--- a/solution.py
+++ b/solution.py
@@ -18,9 +18,11 @@
 def moved(x, to):
     sizes = [lax.axis_size(a) for a in AXES]
     number = {at: i for i, at in enumerate(itertools.product(*map(range, sizes)))}
-    pairs = [
-        (i, number[tuple(t % s for t, s in zip(to(*at), sizes))]) for at, i in number.items()
-    ]
+    pairs = []
+    for at, i in number.items():
+        target = to(*at)
+        if target is not None:
+            pairs.append((i, number[tuple(t % s for t, s in zip(target, sizes))]))
     return lax.ppermute(x, AXES, pairs)
 
 
@@ -34,6 +36,18 @@
 
 def columns_by_columns(a, b):
     return lax.dot_general(a, b, (((0,), (0,)), ((), ())), preferred_element_type=F32)
+
+
+def inner(z):
+    return (z == 1) | (z == 2)
+
+
+def shard_of(k, here, holders):
+    if holders != 4:
+        return lax.rem(here + holders - k, holders)
+    if k < 2:
+        return here ^ k
+    return here ^ jnp.where(inner(here), 5 - k, k)
 
 
 def call(kernel, out_shape, operands, scratch=(), scalars=0):
@@ -61,7 +75,7 @@
     for k in range(holders):
         for j in range(own_slots):
             start = (k * own_slots + j) * rank
-            value = lax.rem(here + holders - k, holders) * slots
+            value = (here ^ k) * slots
             value = value + lax.rem(core + replicas - dr, replicas) * own_slots + j
             slot = jnp.where((lane >= start) & (lane < start + rank), value, slot)
     return slot.astype(F32)
@@ -75,6 +89,19 @@
         slot = jnp.where(names == j, slot_ref[j], slot)
     ones = jnp.ones((1, LANES), F32)
     out_ref[:, -LANES:] = columns_by_columns(slot.astype(F32), ones).astype(BF16)
+
+
+def pick_kernel(here_ref, there_ref, out_ref, *part_refs):
+    rows = part_refs[0].shape[0]
+
+    def put(ref):
+        out_ref[...] = ref[...]
+        for j, part_ref in enumerate(part_refs):
+            part_ref[...] = ref[j * rows : (j + 1) * rows]
+
+    at_inner = inner(lax.axis_index("adapter"))
+    pl.when(at_inner)(lambda: put(here_ref))
+    pl.when(jnp.logical_not(at_inner))(lambda: put(there_ref))
 
 
 def join_kernel(*refs):
@@ -135,7 +162,7 @@
                 ref[:, to : to + LANES] = sent[:, j : j + LANES]
 
 
-def frozen_kernel(sizes, k, count, *refs):
+def frozen_kernel(sizes, k, spec, *refs):
     tokens, groups, holders, replicas, slots, rank = sizes
     g_refs, refs = refs[:groups], refs[groups:]
     down_refs, refs = refs[:replicas], refs[replicas:]
@@ -157,12 +184,14 @@
         out_refs = refs[-groups:]
     rows = down_refs[0].shape[0]
     half = down_refs[0].shape[1] // holders
-    shard_at = lax.rem(here + holders - k, holders) * half
-    for j, block in enumerate(refs[:count]):
+    shard_at = shard_of(k, here, holders) * half
+    for (dr, offset), block in zip(spec, refs):
         if k == 0:
             block = block.at[pl.ds(pl.multiple_of(lax.axis_index("groups") * half, half), half)]
         wide = block.shape[0]
-        at = 0 if count == 1 else lax.rem(core + replicas - j, replicas) * wide
+        at = 0
+        if wide < half:
+            at = lax.rem(core + replicas - dr, replicas) * (half // replicas) + offset
         columns = pl.ds(pl.multiple_of(shard_at + at, wide), wide)
         for dg in range(groups):
             base = rows_by_rows(g_refs[dg][:, :-LANES], block[...]).astype(BF16)
@@ -174,7 +203,7 @@
                     preferred_element_type=F32,
                 )
             lora = (ADAPTER_SCALE * lora).astype(BF16)
-            out_refs[dg][:, pl.ds(at if count == 1 else pl.multiple_of(at, wide), wide)] = (
+            out_refs[dg][:, pl.ds(pl.multiple_of(at, wide) if wide < half else 0, wide)] = (
                 base.astype(F32) + lora.astype(F32)
             ).astype(BF16)
 
@@ -186,7 +215,7 @@
     for k in range(holders):
         for dg in range(groups):
             source = lax.rem(group + groups - dg, groups)
-            at = lax.rem(here + holders - k, holders) * shard + source * half
+            at = shard_of(k, here, holders) * shard + source * half
             out_ref[:, pl.ds(pl.multiple_of(at, half), half)] = refs[k * groups + dg][...]
 
 
@@ -263,11 +292,22 @@
     )[0]
     held = [own]
     for k in range(1, holders):
-        held.append(moved(own, lambda g, z, s, r: (g, z + k, s, r)))
+        held.append(moved(own, lambda g, z, s, r: (g, z ^ k, s, r)))
 
     ring = [lax.dynamic_slice_in_dim(frozen, (group * replicas + core) * piece, piece, axis=0)]
-    ring.append(moved(ring[0], lambda g, z, s, r: (g, z + 1, s, r)))
-    held, grads, ring = lax.optimization_barrier((held, grads, ring))
+    line = holders == 4
+    if line:
+        swap = lambda g, z, s, r: (g, 3 - z, s, r) if inner(z) else None
+        outward = lambda g, z, s, r: (g, z ^ 1, s, r) if inner(z) else None
+        near = moved(ring[0], lambda g, z, s, r: (g, z ^ 1, s, r))
+        across = moved(ring[0], swap)
+        held, grads, near, across = lax.optimization_barrier((held, grads, near, across))
+        ring.append(near)
+        far = moved(near, swap)
+        passed_on = moved(across, outward)
+    else:
+        ring.append(moved(ring[0], lambda g, z, s, r: (g, z + 1, s, r)))
+        held, grads, ring = lax.optimization_barrier((held, grads, ring))
     joined = call(
         join_kernel,
         [
@@ -283,18 +323,30 @@
     others = [moved(downs[0], lambda g, z, s, r: (g + dg, z, s, r)) for dg in range(1, groups)]
     def pieces_of(k, *before):
         if k == 0:
-            return [frozen]
-        block = after(ring[k], *before) if before else ring[k]
-        pieces = [block] + [
-            moved(block, lambda g, z, s, r: (g, z, s, r + dr)) for dr in range(1, replicas)
-        ]
+            return [(0, 0)], [frozen]
+        if isinstance(ring[k], list):
+            whole, *parts = [after(x, *before) if before else x for x in ring[k]]
+        else:
+            whole = after(ring[k], *before) if before else ring[k]
+            parts = [whole]
+        spec, pieces = [(0, 0)], [whole]
+        for dr in range(1, replicas):
+            for j, part in enumerate(parts):
+                spec.append((dr, j * part.shape[0]))
+                pieces.append(moved(part, lambda g, z, s, r: (g, z, s, r + dr)))
         if piece % LANES:
             whole = jnp.zeros((half, value_width), BF16)
-            for dr in range(replicas):
-                at = ((core - dr) % replicas) * piece
-                whole = lax.dynamic_update_slice_in_dim(whole, pieces[dr], at, axis=0)
-            pieces = [whole]
-        return pieces
+            for (dr, offset), part in zip(spec, pieces):
+                at = ((core - dr) % replicas) * piece + offset
+                whole = lax.dynamic_update_slice_in_dim(whole, part, at, axis=0)
+            spec, pieces = [(0, 0)], [whole]
+        return spec, pieces
+
+    def picked(at_inner, at_end):
+        count = 2 if piece % (2 * LANES) == 0 else 1
+        shapes = [piece] + [piece // count] * count
+        shapes = [jax.ShapeDtypeStruct((n, value_width), BF16) for n in shapes]
+        return list(call(pick_kernel, shapes, (at_inner, at_end)))
 
     kept = replicas * holders * rows
 
@@ -327,17 +379,21 @@
 
     arrived, outs = [], []
     for k in range(holders):
-        if k > 1:
-            last = ring[-1]
-            if k > 2:
-                last = after(last, *outs[k - 2], part)
-            ring.append(moved(last, lambda g, z, s, r: (g, z + 1, s, r)))
+        if line and k == 2:
+            far = after(far, *outs[1], part)
+            last = moved(far, outward)
+            ring.append(picked(across, passed_on))
+            ring.append(picked(far, last))
+        elif not line and k > 1:
+            last = after(ring[-1], *outs[k - 2], part) if k > 2 else ring[-1]
+            last = moved(last, lambda g, z, s, r: (g, z + 1, s, r))
+            ring.append(last)
         gate = [*arrived[k - 2], *outs[k - 1]] if k > 1 else []
-        blocks = pieces_of(k, *gate, *(chip[:1] if k > 2 else ()))
+        spec, blocks = pieces_of(k, *gate, *(chip[:1] if k > 2 else ()))
         tokens_in = [after(tagged, part), *grads[1:]] if k == 1 else grads
         out = call(
             functools.partial(
-                frozen_kernel, (tokens, groups, holders, replicas, slots, rank), k, len(blocks)
+                frozen_kernel, (tokens, groups, holders, replicas, slots, rank), k, spec
             ),
             [jax.ShapeDtypeStruct((tokens, half), BF16)] * groups
             + [jax.ShapeDtypeStruct((groups * tokens, kept), BF16)] * (k == 0),
@@ -360,7 +416,7 @@
     )[0]
 
     sums = [chip[0]] + [
-        moved(after(chip[k], ring[-1]), lambda g, z, s, r: (g, z - k, s, r))
+        moved(after(chip[k], last), lambda g, z, s, r: (g, z ^ k, s, r))
         for k in range(1, holders)
     ]
     total = call(total_kernel, [jax.ShapeDtypeStruct((rows, cols), BF16)], sums)[0]

time: 85.4 us -> 85.5 us (level)
  waiting for transfers between devices: 38.1 us -> 34.1 us
  starting transfers between devices: 32.1 us -> 35.6 us
    ppermute x28 -> x32, waiting for transfers between devices: 38.1 us -> 34.1 us  [moved(): return lax.ppermute(x, AXES, pairs)]
    ppermute x28 -> x32, starting transfers between devices: 32.1 us -> 35.6 us  [moved(): return lax.ppermute(x, AXES, pairs)]
    pallas_call x12 -> x14, Pallas kernels: 8.79 us -> 9.24 us  [call(): pl.pallas_call(kernel, out_shape=out_shape, in_specs=[pl.BlockSpec(memory...]
  transfers between devices with their start and end apart: 28 -> 32, of which waited for: 14 -> 11; matrix products, arithmetic and copies ran while one was open for 0% -> 0% of each run, Pallas kernels for 9% -> 9%
where the time goes in v9:
time: 85.5 us; the launch traced here: 85.2 us
  starting transfers between devices  35.6 us (42%)
  waiting for transfers between devices  34.1 us (40%)
  Pallas kernels  9.24 us (11%)
  local copies, waits for them, and re-layouts  5.34 us (6%)
  between operations  0.91 us (1%)
    ppermute x32, starting transfers between devices, moved(): return lax.ppermute(x, AXES, pairs)  35.6 us
    ppermute x32, waiting for transfers between devices, moved(): return lax.ppermute(x, AXES, pairs)  34.1 us
    pallas_call x14, Pallas kernels, call(): pl.pallas_call(kernel, out_shape=out_shape, in_specs=[pl.BlockSpec(memory...  9.24 us
    unnamed x14, local copies, waits for them, and re-layouts  4.11 us
  transfers between devices with their start and end apart: 32, of which 11 were waited for; matrix products, arithmetic and copies ran while one was open for 0% of the time, Pallas kernels for 9%

profile of v9, /device:TPU:0, one launch (start us, length us, event | category | flops | bytes accessed | tf_op | source)
XLA Modules:
  0.0 85.2 jit_solution(15141857117429899837)
XLA Ops:
  0.6 1.2 %dynamic-slice_bitcast_fusion = bf16[256,1024]{1,0:T(8,128)(2,1)S(1)} fusion(bf16[1,1024,1024]{2,1,0:T(8,128)(2,1)} %param.11, s32[]{:T(128)S(6)} %select_n.3), kind=kLoop, calls=%fused_computation | loop fusion | bytes 1048580 | tf_op jit(solution)/shard_map/dynamic_slice | solution.py:297
  1.9 3.1 %collective-permute-start.4 = (bf16[256,1024]{1,0:T(8,128)(2,1)S(1)}, bf16[256,1024]{1,0:T(8,128)(2,1)S(1)}, u32[]{:S(2)}, u32[]{:S(2)}) collective-permute-start(bf16[256,1024]{1,0:T(8,128)(2,1)S(1)} %dynamic-slice_bitcast_fusion), channel_id=1, source_target_pairs={{0,4},{1,5},{2,6},{3,7},{4,0},{5,1},{6,2},{7,3},{8,12},{9,13},{10,... | collective-permute-start | bytes 1572872 | tf_op jit(solution)/shard_map/ppermute | solution.py:26
  5.7 1.0 %copy-done.2 = bf16[1,176,1024]{2,1,0:T(8,128)(2,1)S(1)} copy-done((bf16[1,176,1024]{2,1,0:T(8,128)(2,1)S(1)}, bf16[1,176,1024]{2,1,0:T(8,128)(2,1)}, u32[]{:S(2)}) %copy-start.2) | copy-done | bytes 360472
  8.8 1.6 %collective-permute-start.3 = (bf16[176,1152]{1,0:T(8,128)(2,1)S(1)}, bf16[176,1152]{1,0:T(8,128)(2,1)S(1)}, u32[]{:S(2)}, u32[]{:S(2)}) collective-permute-start(bf16[176,1152]{1,0:T(8,128)(2,1)S(1)} %shard_map.95.refs_0_.refs_1_), channel_id=1, source_target_pairs={{0,16},{1,17},{2,18},{3,19},{4,20},{5,21},{6,22},{7,23},{8,24},{9,... | collective-permute-start | bytes 1216520 | tf_op jit(solution)/shard_map/ppermute | solution.py:26
  10.3 0.9 %copy-done.3 = bf16[1,2,16,4096]{3,2,1,0:T(8,128)(2,1)S(1)} copy-done((bf16[1,2,16,4096]{3,2,1,0:T(8,128)(2,1)S(1)}, bf16[1,2,16,4096]{3,2,1,0:T(8,128)(2,1)}, u32[]{:S(2)}) %copy-start.3) | copy-done | bytes 262168
  12.1 4.4 %collective-permute-start = (bf16[16,3072]{1,0:T(8,128)(2,1)S(1)}, bf16[16,3072]{1,0:T(8,128)(2,1)S(1)}, u32[]{:S(2)}, u32[]{:S(2)}) collective-permute-start(bf16[16,3072]{1,0:T(8,128)(2,1)S(1)} %shard_map.94.refs_0_), channel_id=1, source_target_pairs={{0,4},{1,5},{2,6},{3,7},{4,0},{5,1},{6,2},{7,3},{8,12},{9,13},{10,... | collective-permute-start | bytes 294920 | tf_op jit(solution)/shard_map/ppermute | solution.py:26
  16.6 2.7 %collective-permute-done.refs_1_ = bf16[16,3072]{1,0:T(8,128)(2,1)S(1)} collective-permute-done((bf16[16,3072]{1,0:T(8,128)(2,1)S(1)}, bf16[16,3072]{1,0:T(8,128)(2,1)S(1)}, u32[]{:S(2)}, u32[]{:S(2)}) %collective-permute-start) | collective-permute-done | bytes 98336 | tf_op jit(solution)/shard_map/ppermute | solution.py:26
  19.3 3.5 %collective-permute-start.2 = (bf16[16,3072]{1,0:T(8,128)(2,1)S(1)}, bf16[16,3072]{1,0:T(8,128)(2,1)S(1)}, u32[]{:S(2)}, u32[]{:S(2)}) collective-permute-start(bf16[16,3072]{1,0:T(8,128)(2,1)S(1)} %shard_map.94.refs_0_), channel_id=1, source_target_pairs={{0,12},{1,13},{2,14},{3,15},{4,8},{5,9},{6,10},{7,11},{8,4},{9,5},... | collective-permute-start | bytes 294920 | tf_op jit(solution)/shard_map/ppermute | solution.py:26
  22.8 5.7 %collective-permute-done.1.refs_2_ = bf16[16,3072]{1,0:T(8,128)(2,1)S(1)} collective-permute-done((bf16[16,3072]{1,0:T(8,128)(2,1)S(1)}, bf16[16,3072]{1,0:T(8,128)(2,1)S(1)}, u32[]{:S(2)}, u32[]{:S(2)}) %collective-permute-start.1) | collective-permute-done | bytes 98336 | tf_op jit(solution)/shard_map/ppermute | solution.py:26
  28.6 1.6 %collective-permute-start.10 = (bf16[64,2048]{1,0:T(8,128)(2,1)S(1)}, bf16[64,2048]{1,0:T(8,128)(2,1)S(1)}, u32[]{:S(2)}, u32[]{:S(2)}) collective-permute-start(bf16[64,2048]{1,0:T(8,128)(2,1)S(1)} %get-tuple-element.57.refs_2_.refs_3_), channel_id=1, source_target_pairs={{0,16},{1,17},{2,18},{3,19},{4,20},{5,21},{6,22},{7,23},{8,24},{9,... | collective-permute-start | bytes 786440 | tf_op jit(solution)/shard_map/ppermute | solution.py:26
  31.5 1.3 %collective-permute-start.15 = (bf16[256,1024]{1,0:T(8,128)(2,1)S(1)}, bf16[256,1024]{1,0:T(8,128)(2,1)S(1)}, u32[]{:S(2)}, u32[]{:S(2)}) collective-permute-start(bf16[256,1024]{1,0:T(8,128)(2,1)S(1)} %collective-permute-done.5.here_ref), channel_id=1, source_target_pairs={{4,0},{5,1},{6,2},{7,3},{8,12},{9,13},{10,14},{11,15},{20,16},{21,... | collective-permute-start | bytes 1572872 | tf_op jit(solution)/shard_map/ppermute | solution.py:26
  32.9 1.5 %shard_map.97 = (bf16[176,512]{1,0:T(8,128)(2,1)S(1)}, bf16[176,512]{1,0:T(8,128)(2,1)S(1)}, bf16[352,128]{1,0:T(8,128)(2,1)S(1)}) custom-call(bf16[176,1152]{1,0:T(8,128)(2,1)S(1)} %shard_map.95.refs_0_.refs_1_, bf16[176,1152]{1,0:T(8,128)(2,1)S(1)} %collective-permute-done.3.refs_1_, bf16[64,2048]{1,0:T(8,128)(2,1)S(1)} %get-tuple-element.57.refs_2_.refs_3_, ...), custom_call_target="tpu_custom_call" | custom-call | flops 1000 | bytes 1000 | tf_op jit(solution)/shard_map/pallas_call | solution.py:55
  34.3 3.0 %collective-permute-done.10.refs_5_ = bf16[64,2048]{1,0:T(8,128)(2,1)S(1)} collective-permute-done((bf16[64,2048]{1,0:T(8,128)(2,1)S(1)}, bf16[64,2048]{1,0:T(8,128)(2,1)S(1)}, u32[]{:S(2)}, u32[]{:S(2)}) %collective-permute-start.10) | collective-permute-done | bytes 262176 | tf_op jit(solution)/shard_map/ppermute | solution.py:26
  37.3 1.5 %collective-permute-start.8 = (bf16[176,512]{1,0:T(8,128)(2,1)S(1)}, bf16[176,512]{1,0:T(8,128)(2,1)S(1)}, u32[]{:S(2)}, u32[]{:S(2)}) collective-permute-start(bf16[176,512]{1,0:T(8,128)(2,1)S(1)} %get-tuple-element.59), channel_id=1, source_target_pairs={{0,2},{1,3},{2,0},{3,1},{4,6},{5,7},{6,4},{7,5},{8,10},{9,11},{10,... | collective-permute-start | bytes 540680 | tf_op jit(solution)/shard_map/ppermute | solution.py:26
  38.9 2.4 %collective-permute-start.9 = (bf16[176,512]{1,0:T(8,128)(2,1)S(1)}, bf16[176,512]{1,0:T(8,128)(2,1)S(1)}, u32[]{:S(2)}, u32[]{:S(2)}) collective-permute-start(bf16[176,512]{1,0:T(8,128)(2,1)S(1)} %get-tuple-element.60), channel_id=1, source_target_pairs={{0,18},{1,19},{2,16},{3,17},{4,22},{5,23},{6,20},{7,21},{8,26},{9,... | collective-permute-start | bytes 540680 | tf_op jit(solution)/shard_map/ppermute | solution.py:26
  41.3 1.3 %shard_map.98 = (f32[64,5120]{1,0:T(8,128)S(1)}, bf16[64,2560]{1,0:T(8,128)(2,1)S(1)}, bf16[64,2560]{1,0:T(8,128)(2,1)S(1)}) custom-call(bf16[176,4096]{1,0:T(8,128)(2,1)S(1)} %bitcast.12, bf16[176,1152]{1,0:T(8,128)(2,1)S(1)} %shard_map.95.refs_0_.refs_1_, bf16[352,128]{1,0:T(8,128)(2,1)S(1)} %get-tuple-element.61.refs_2_.refs_4_, ...), custom_call_target="tpu_custom_call" | custom-call | flops 1000 | bytes 1000 | tf_op jit(solution)/shard_map/pallas_call | solution.py:55
  42.6 1.0 %shard_map.99 = (bf16[176,512]{1,0:T(8,128)(2,1)S(1)}, bf16[176,512]{1,0:T(8,128)(2,1)S(1)}) custom-call(bf16[176,1152]{1,0:T(8,128)(2,1)S(1)} %shard_map.95.refs_0_.refs_1_, bf16[176,1152]{1,0:T(8,128)(2,1)S(1)} %collective-permute-done.3.refs_1_, bf16[64,2048]{1,0:T(8,128)(2,1)S(1)} %get-tuple-element.57.refs_2_.refs_3_, ...), custom_call_target="tpu_custom_call" | custom-call | flops 1000 | bytes 1000 | tf_op jit(solution)/shard_map/pallas_call | solution.py:55
  43.6 1.3 %collective-permute-start.21 = (bf16[256,1024]{1,0:T(8,128)(2,1)S(1)}, bf16[256,1024]{1,0:T(8,128)(2,1)S(1)}, u32[]{:S(2)}, u32[]{:S(2)}) collective-permute-start(bf16[256,1024]{1,0:T(8,128)(2,1)S(1)} %collective-permute-done.20.here_ref), channel_id=1, source_target_pairs={{4,0},{5,1},{6,2},{7,3},{8,12},{9,13},{10,14},{11,15},{20,16},{21,... | collective-permute-start | bytes 1572872 | tf_op jit(solution)/shard_map/ppermute | solution.py:26
  44.9 4.3 %collective-permute-done.15.there_ref = bf16[256,1024]{1,0:T(8,128)(2,1)S(1)} collective-permute-done((bf16[256,1024]{1,0:T(8,128)(2,1)S(1)}, bf16[256,1024]{1,0:T(8,128)(2,1)S(1)}, u32[]{:S(2)}, u32[]{:S(2)}) %collective-permute-start.15) | collective-permute-done | bytes 524320 | tf_op jit(solution)/shard_map/ppermute | solution.py:26
  50.9 1.5 %collective-permute-start.13 = (bf16[176,512]{1,0:T(8,128)(2,1)S(1)}, bf16[176,512]{1,0:T(8,128)(2,1)S(1)}, u32[]{:S(2)}, u32[]{:S(2)}) collective-permute-start(bf16[176,512]{1,0:T(8,128)(2,1)S(1)} %get-tuple-element.66), channel_id=1, source_target_pairs={{0,2},{1,3},{2,0},{3,1},{4,6},{5,7},{6,4},{7,5},{8,10},{9,11},{10,... | collective-permute-start | bytes 540680 | tf_op jit(solution)/shard_map/ppermute | solution.py:26
  52.9 1.2 %shard_map.101 = (bf16[176,512]{1,0:T(8,128)(2,1)S(1)}, bf16[176,512]{1,0:T(8,128)(2,1)S(1)}) custom-call(bf16[176,1152]{1,0:T(8,128)(2,1)S(1)} %shard_map.95.refs_0_.refs_1_, bf16[176,1152]{1,0:T(8,128)(2,1)S(1)} %collective-permute-done.3.refs_1_, bf16[64,2048]{1,0:T(8,128)(2,1)S(1)} %get-tuple-element.57.refs_2_.refs_3_, ...), custom_call_target="tpu_custom_call" | custom-call | flops 1000 | bytes 1000 | tf_op jit(solution)/shard_map/pallas_call | solution.py:55
  54.2 6.6 %collective-permute-done.21.there_ref = bf16[256,1024]{1,0:T(8,128)(2,1)S(1)} collective-permute-done((bf16[256,1024]{1,0:T(8,128)(2,1)S(1)}, bf16[256,1024]{1,0:T(8,128)(2,1)S(1)}, u32[]{:S(2)}, u32[]{:S(2)}) %collective-permute-start.21) | collective-permute-done | bytes 524320 | tf_op jit(solution)/shard_map/ppermute | solution.py:26
  61.8 1.5 %collective-permute-start.18 = (bf16[176,512]{1,0:T(8,128)(2,1)S(1)}, bf16[176,512]{1,0:T(8,128)(2,1)S(1)}, u32[]{:S(2)}, u32[]{:S(2)}) collective-permute-start(bf16[176,512]{1,0:T(8,128)(2,1)S(1)} %get-tuple-element.75), channel_id=1, source_target_pairs={{0,2},{1,3},{2,0},{3,1},{4,6},{5,7},{6,4},{7,5},{8,10},{9,11},{10,... | collective-permute-start | bytes 540680 | tf_op jit(solution)/shard_map/ppermute | solution.py:26
  63.3 1.5 %collective-permute-start.19 = (bf16[176,512]{1,0:T(8,128)(2,1)S(1)}, bf16[176,512]{1,0:T(8,128)(2,1)S(1)}, u32[]{:S(2)}, u32[]{:S(2)}) collective-permute-start(bf16[176,512]{1,0:T(8,128)(2,1)S(1)} %get-tuple-element.76), channel_id=1, source_target_pairs={{0,18},{1,19},{2,16},{3,17},{4,22},{5,23},{6,20},{7,21},{8,26},{9,... | collective-permute-start | bytes 540680 | tf_op jit(solution)/shard_map/ppermute | solution.py:26
  64.8 2.4 %collective-permute-start.30 = (bf16[16,5120]{1,0:T(8,128)(2,1)S(1)}, bf16[16,5120]{1,0:T(8,128)(2,1)S(1)}, u32[]{:S(2)}, u32[]{:S(2)}) collective-permute-start(bf16[16,5120]{1,0:T(8,128)(2,1)S(1)} %get-tuple-element.96), channel_id=1, source_target_pairs={{0,12},{1,13},{2,14},{3,15},{4,8},{5,9},{6,10},{7,11},{8,4},{9,5},... | collective-permute-start | bytes 491528 | tf_op jit(solution)/shard_map/ppermute | solution.py:26
  67.6 1.6 %collective-permute-start.28 = (bf16[16,5120]{1,0:T(8,128)(2,1)S(1)}, bf16[16,5120]{1,0:T(8,128)(2,1)S(1)}, u32[]{:S(2)}, u32[]{:S(2)}) collective-permute-start(bf16[16,5120]{1,0:T(8,128)(2,1)S(1)} %get-tuple-element.92), channel_id=1, source_target_pairs={{0,4},{1,5},{2,6},{3,7},{4,0},{5,1},{6,2},{7,3},{8,12},{9,13},{10,... | collective-permute-start | bytes 491528 | tf_op jit(solution)/shard_map/ppermute | solution.py:26
  69.2 1.2 %shard_map.104 = (bf16[176,512]{1,0:T(8,128)(2,1)S(1)}, bf16[176,512]{1,0:T(8,128)(2,1)S(1)}) custom-call(bf16[176,1152]{1,0:T(8,128)(2,1)S(1)} %shard_map.95.refs_0_.refs_1_, bf16[176,1152]{1,0:T(8,128)(2,1)S(1)} %collective-permute-done.3.refs_1_, bf16[64,2048]{1,0:T(8,128)(2,1)S(1)} %get-tuple-element.57.refs_2_.refs_3_, ...), custom_call_target="tpu_custom_call" | custom-call | flops 1000 | bytes 1000 | tf_op jit(solution)/shard_map/pallas_call | solution.py:55
  70.4 2.7 %collective-permute-done.19.refs_5_ = bf16[176,512]{1,0:T(8,128)(2,1)S(1)} collective-permute-done((bf16[176,512]{1,0:T(8,128)(2,1)S(1)}, bf16[176,512]{1,0:T(8,128)(2,1)S(1)}, u32[]{:S(2)}, u32[]{:S(2)}) %collective-permute-start.19) | collective-permute-done | bytes 180256 | tf_op jit(solution)/shard_map/ppermute | solution.py:26
  73.1 1.4 %collective-permute-start.27 = (bf16[176,512]{1,0:T(8,128)(2,1)S(1)}, bf16[176,512]{1,0:T(8,128)(2,1)S(1)}, u32[]{:S(2)}, u32[]{:S(2)}) collective-permute-start(bf16[176,512]{1,0:T(8,128)(2,1)S(1)} %get-tuple-element.90), channel_id=1, source_target_pairs={{0,18},{1,19},{2,16},{3,17},{4,22},{5,23},{6,20},{7,21},{8,26},{9,... | collective-permute-start | bytes 540680 | tf_op jit(solution)/shard_map/ppermute | solution.py:26
  75.1 6.6 %collective-permute-done.29.refs_2_ = bf16[16,5120]{1,0:T(8,128)(2,1)S(1)} collective-permute-done((bf16[16,5120]{1,0:T(8,128)(2,1)S(1)}, bf16[16,5120]{1,0:T(8,128)(2,1)S(1)}, u32[]{:S(2)}, u32[]{:S(2)}) %collective-permute-start.29) | collective-permute-done | bytes 163872 | tf_op jit(solution)/shard_map/ppermute | solution.py:26
  81.8 1.4 %collective-permute-done.31.refs_1_ = bf16[16,5120]{1,0:T(8,128)(2,1)S(1)} collective-permute-done((bf16[16,5120]{1,0:T(8,128)(2,1)S(1)}, bf16[16,5120]{1,0:T(8,128)(2,1)S(1)}, u32[]{:S(2)}, u32[]{:S(2)}) %collective-permute-start.31) | collective-permute-done | bytes 163872 | tf_op jit(solution)/shard_map/ppermute | solution.py:26
  84.0 1.2 %shard_map.105 = bf16[176,4096]{1,0:T(8,128)(2,1)} custom-call(bf16[176,512]{1,0:T(8,128)(2,1)S(1)} %collective-permute-done.8.refs_0_, bf16[176,512]{1,0:T(8,128)(2,1)S(1)} %collective-permute-done.9.refs_1_, bf16[176,512]{1,0:T(8,128)(2,1)S(1)} %collective-permute-done.13.refs_2_, bf16[176,512]{1,0:T(8,128)(2,1)S(1)} %collective-permute-done.14.refs_3_, ...), custom_call_target="tpu_custom_call" | custom-call | flops 1000 | bytes 1000 | tf_op jit(solution)/shard_map/pallas_call | solution.py:55
  (61 shorter events, 10.3 us)
Async XLA Ops:
  1.9 26.6 %collective-permute-start.4 = (bf16[256,1024]{1,0:T(8,128)(2,1)S(1)}, bf16[256,1024]{1,0:T(8,128)(2,1)S(1)}, u32[]{:S(2)}, u32[]{:S(2)}) collective-permute-start(bf16[256,1024]{1,0:T(8,128)(2,1)S(1)} %dynamic-slice_bitcast_fusion), channel_id=1, source_target_pairs={{0,4},{1,5},{2,6},{3,7},{4,0},{5,1},{6,2},{7,3},{8,12},{9,13},{10,... | collective-permute-start | bytes 1572872 | tf_op jit(solution)/shard_map/ppermute | solution.py:26
  5.0 23.5 %collective-permute-start.5 = (bf16[256,1024]{1,0:T(8,128)(2,1)S(1)}, bf16[256,1024]{1,0:T(8,128)(2,1)S(1)}, u32[]{:S(2)}, u32[]{:S(2)}) collective-permute-start(bf16[256,1024]{1,0:T(8,128)(2,1)S(1)} %dynamic-slice_bitcast_fusion), channel_id=1, source_target_pairs={{4,8},{5,9},{6,10},{7,11},{8,4},{9,5},{10,6},{11,7},{20,24},{21,25... | collective-permute-start | bytes 1572872 | tf_op jit(solution)/shard_map/ppermute | solution.py:26
  8.8 19.7 %collective-permute-start.3 = (bf16[176,1152]{1,0:T(8,128)(2,1)S(1)}, bf16[176,1152]{1,0:T(8,128)(2,1)S(1)}, u32[]{:S(2)}, u32[]{:S(2)}) collective-permute-start(bf16[176,1152]{1,0:T(8,128)(2,1)S(1)} %shard_map.95.refs_0_.refs_1_), channel_id=1, source_target_pairs={{0,16},{1,17},{2,18},{3,19},{4,20},{5,21},{6,22},{7,23},{8,24},{9,... | collective-permute-start | bytes 1216520 | tf_op jit(solution)/shard_map/ppermute | solution.py:26
  12.1 7.2 %collective-permute-start = (bf16[16,3072]{1,0:T(8,128)(2,1)S(1)}, bf16[16,3072]{1,0:T(8,128)(2,1)S(1)}, u32[]{:S(2)}, u32[]{:S(2)}) collective-permute-start(bf16[16,3072]{1,0:T(8,128)(2,1)S(1)} %shard_map.94.refs_0_), channel_id=1, source_target_pairs={{0,4},{1,5},{2,6},{3,7},{4,0},{5,1},{6,2},{7,3},{8,12},{9,13},{10,... | collective-permute-start | bytes 294920 | tf_op jit(solution)/shard_map/ppermute | solution.py:26
  16.6 11.9 %collective-permute-start.1 = (bf16[16,3072]{1,0:T(8,128)(2,1)S(1)}, bf16[16,3072]{1,0:T(8,128)(2,1)S(1)}, u32[]{:S(2)}, u32[]{:S(2)}) collective-permute-start(bf16[16,3072]{1,0:T(8,128)(2,1)S(1)} %shard_map.94.refs_0_), channel_id=1, source_target_pairs={{0,8},{1,9},{2,10},{3,11},{4,12},{5,13},{6,14},{7,15},{8,0},{9,1},... | collective-permute-start | bytes 294920 | tf_op jit(solution)/shard_map/ppermute | solution.py:26
  19.3 9.2 %collective-permute-start.2 = (bf16[16,3072]{1,0:T(8,128)(2,1)S(1)}, bf16[16,3072]{1,0:T(8,128)(2,1)S(1)}, u32[]{:S(2)}, u32[]{:S(2)}) collective-permute-start(bf16[16,3072]{1,0:T(8,128)(2,1)S(1)} %shard_map.94.refs_0_), channel_id=1, source_target_pairs={{0,12},{1,13},{2,14},{3,15},{4,8},{5,9},{6,10},{7,11},{8,4},{9,5},... | collective-permute-start | bytes 294920 | tf_op jit(solution)/shard_map/ppermute | solution.py:26
  28.5 4.3 %collective-permute-start.6 = (bf16[64,2048]{1,0:T(8,128)(2,1)S(1)}, bf16[64,2048]{1,0:T(8,128)(2,1)S(1)}, u32[]{:S(2)}, u32[]{:S(2)}) collective-permute-start(bf16[64,2048]{1,0:T(8,128)(2,1)S(1)} %get-tuple-element.57.refs_2_.refs_3_), channel_id=1, source_target_pairs={{0,1},{1,0},{2,3},{3,2},{4,5},{5,4},{6,7},{7,6},{8,9},{9,8},{10,11... | collective-permute-start | bytes 786440 | tf_op jit(solution)/shard_map/ppermute | solution.py:26
  28.6 8.7 %collective-permute-start.10 = (bf16[64,2048]{1,0:T(8,128)(2,1)S(1)}, bf16[64,2048]{1,0:T(8,128)(2,1)S(1)}, u32[]{:S(2)}, u32[]{:S(2)}) collective-permute-start(bf16[64,2048]{1,0:T(8,128)(2,1)S(1)} %get-tuple-element.57.refs_2_.refs_3_), channel_id=1, source_target_pairs={{0,16},{1,17},{2,18},{3,19},{4,20},{5,21},{6,22},{7,23},{8,24},{9,... | collective-permute-start | bytes 786440 | tf_op jit(solution)/shard_map/ppermute | solution.py:26
  30.2 1.3 %collective-permute-start.7 = (bf16[64,1024]{1,0:T(8,128)(2,1)S(1)}, bf16[64,1024]{1,0:T(8,128)(2,1)S(1)}, u32[]{:S(2)}, u32[]{:S(2)}) collective-permute-start(bf16[64,1024]{1,0:T(8,128)(2,1)S(1)} %get-tuple-element.58.refs_4_), channel_id=1, source_target_pairs={{0,1},{1,0},{2,3},{3,2},{4,5},{5,4},{6,7},{7,6},{8,9},{9,8},{10,11... | collective-permute-start | bytes 393224 | tf_op jit(solution)/shard_map/ppermute | solution.py:26
  30.3 12.2 %collective-permute-start.12 = (bf16[256,1024]{1,0:T(8,128)(2,1)S(1)}, bf16[256,1024]{1,0:T(8,128)(2,1)S(1)}, u32[]{:S(2)}, u32[]{:S(2)}) collective-permute-start(bf16[256,1024]{1,0:T(8,128)(2,1)S(1)} %collective-permute-done.4.refs_5_), channel_id=1, source_target_pairs={{0,1},{1,0},{2,3},{3,2},{4,5},{5,4},{6,7},{7,6},{8,9},{9,8},{10,11... | collective-permute-start | bytes 1572872 | tf_op jit(solution)/shard_map/ppermute | solution.py:26
  30.7 12.9 %collective-permute-start.20 = (bf16[256,1024]{1,0:T(8,128)(2,1)S(1)}, bf16[256,1024]{1,0:T(8,128)(2,1)S(1)}, u32[]{:S(2)}, u32[]{:S(2)}) collective-permute-start(bf16[256,1024]{1,0:T(8,128)(2,1)S(1)} %collective-permute-done.4.refs_5_), channel_id=1, source_target_pairs={{4,8},{5,9},{6,10},{7,11},{8,4},{9,5},{10,6},{11,7},{20,24},{21,25... | collective-permute-start | bytes 1572872 | tf_op jit(solution)/shard_map/ppermute | solution.py:26
  31.5 17.7 %collective-permute-start.15 = (bf16[256,1024]{1,0:T(8,128)(2,1)S(1)}, bf16[256,1024]{1,0:T(8,128)(2,1)S(1)}, u32[]{:S(2)}, u32[]{:S(2)}) collective-permute-start(bf16[256,1024]{1,0:T(8,128)(2,1)S(1)} %collective-permute-done.5.here_ref), channel_id=1, source_target_pairs={{4,0},{5,1},{6,2},{7,3},{8,12},{9,13},{10,14},{11,15},{20,16},{21,... | collective-permute-start | bytes 1572872 | tf_op jit(solution)/shard_map/ppermute | solution.py:26
  37.3 1.5 %collective-permute-start.11 = (bf16[64,2048]{1,0:T(8,128)(2,1)S(1)}, bf16[64,2048]{1,0:T(8,128)(2,1)S(1)}, u32[]{:S(2)}, u32[]{:S(2)}) collective-permute-start(bf16[64,2048]{1,0:T(8,128)(2,1)S(1)} %collective-permute-done.10.refs_5_), channel_id=1, source_target_pairs={{0,1},{1,0},{2,3},{3,2},{4,5},{5,4},{6,7},{7,6},{8,9},{9,8},{10,11... | collective-permute-start | bytes 786440 | tf_op jit(solution)/shard_map/ppermute | solution.py:26
  37.3 11.9 %collective-permute-start.8 = (bf16[176,512]{1,0:T(8,128)(2,1)S(1)}, bf16[176,512]{1,0:T(8,128)(2,1)S(1)}, u32[]{:S(2)}, u32[]{:S(2)}) collective-permute-start(bf16[176,512]{1,0:T(8,128)(2,1)S(1)} %get-tuple-element.59), channel_id=1, source_target_pairs={{0,2},{1,3},{2,0},{3,1},{4,6},{5,7},{6,4},{7,5},{8,10},{9,11},{10,... | collective-permute-start | bytes 540680 | tf_op jit(solution)/shard_map/ppermute | solution.py:26
  38.9 10.4 %collective-permute-start.9 = (bf16[176,512]{1,0:T(8,128)(2,1)S(1)}, bf16[176,512]{1,0:T(8,128)(2,1)S(1)}, u32[]{:S(2)}, u32[]{:S(2)}) collective-permute-start(bf16[176,512]{1,0:T(8,128)(2,1)S(1)} %get-tuple-element.60), channel_id=1, source_target_pairs={{0,18},{1,19},{2,16},{3,17},{4,22},{5,23},{6,20},{7,21},{8,26},{9,... | collective-permute-start | bytes 540680 | tf_op jit(solution)/shard_map/ppermute | solution.py:26
  43.6 17.2 %collective-permute-start.21 = (bf16[256,1024]{1,0:T(8,128)(2,1)S(1)}, bf16[256,1024]{1,0:T(8,128)(2,1)S(1)}, u32[]{:S(2)}, u32[]{:S(2)}) collective-permute-start(bf16[256,1024]{1,0:T(8,128)(2,1)S(1)} %collective-permute-done.20.here_ref), channel_id=1, source_target_pairs={{4,0},{5,1},{6,2},{7,3},{8,12},{9,13},{10,14},{11,15},{20,16},{21,... | collective-permute-start | bytes 1572872 | tf_op jit(solution)/shard_map/ppermute | solution.py:26
  49.3 1.6 %collective-permute-start.17 = (bf16[128,1024]{1,0:T(8,128)(2,1)S(1)}, bf16[128,1024]{1,0:T(8,128)(2,1)S(1)}, u32[]{:S(2)}, u32[]{:S(2)}) collective-permute-start(bf16[128,1024]{1,0:T(8,128)(2,1)S(1)} %get-tuple-element.74), channel_id=1, source_target_pairs={{0,1},{1,0},{2,3},{3,2},{4,5},{5,4},{6,7},{7,6},{8,9},{9,8},{10,11... | collective-permute-start | bytes 786440 | tf_op jit(solution)/shard_map/ppermute | solution.py:26
  49.4 3.0 %collective-permute-start.16 = (bf16[128,1024]{1,0:T(8,128)(2,1)S(1)}, bf16[128,1024]{1,0:T(8,128)(2,1)S(1)}, u32[]{:S(2)}, u32[]{:S(2)}) collective-permute-start(bf16[128,1024]{1,0:T(8,128)(2,1)S(1)} %get-tuple-element.72), channel_id=1, source_target_pairs={{0,1},{1,0},{2,3},{3,2},{4,5},{5,4},{6,7},{7,6},{8,9},{9,8},{10,11... | collective-permute-start | bytes 786440 | tf_op jit(solution)/shard_map/ppermute | solution.py:26
  49.9 4.2 %collective-permute-start.22 = (bf16[64,2560]{1,0:T(8,128)(2,1)S(1)}, bf16[64,2560]{1,0:T(8,128)(2,1)S(1)}, u32[]{:S(2)}, u32[]{:S(2)}) collective-permute-start(bf16[64,2560]{1,0:T(8,128)(2,1)S(1)} %get-tuple-element.79), channel_id=1, source_target_pairs={{0,1},{1,0},{2,3},{3,2},{4,5},{5,4},{6,7},{7,6},{8,9},{9,8},{10,11... | collective-permute-start | bytes 983048 | tf_op jit(solution)/shard_map/ppermute | solution.py:26
  49.9 4.1 %collective-permute-start.23 = (bf16[64,2560]{1,0:T(8,128)(2,1)S(1)}, bf16[64,2560]{1,0:T(8,128)(2,1)S(1)}, u32[]{:S(2)}, u32[]{:S(2)}) collective-permute-start(bf16[64,2560]{1,0:T(8,128)(2,1)S(1)} %get-tuple-element.80), channel_id=1, source_target_pairs={{0,1},{1,0},{2,3},{3,2},{4,5},{5,4},{6,7},{7,6},{8,9},{9,8},{10,11... | collective-permute-start | bytes 983048 | tf_op jit(solution)/shard_map/ppermute | solution.py:26
  50.9 10.0 %collective-permute-start.13 = (bf16[176,512]{1,0:T(8,128)(2,1)S(1)}, bf16[176,512]{1,0:T(8,128)(2,1)S(1)}, u32[]{:S(2)}, u32[]{:S(2)}) collective-permute-start(bf16[176,512]{1,0:T(8,128)(2,1)S(1)} %get-tuple-element.66), channel_id=1, source_target_pairs={{0,2},{1,3},{2,0},{3,1},{4,6},{5,7},{6,4},{7,5},{8,10},{9,11},{10,... | collective-permute-start | bytes 540680 | tf_op jit(solution)/shard_map/ppermute | solution.py:26
  52.4 8.9 %collective-permute-start.14 = (bf16[176,512]{1,0:T(8,128)(2,1)S(1)}, bf16[176,512]{1,0:T(8,128)(2,1)S(1)}, u32[]{:S(2)}, u32[]{:S(2)}) collective-permute-start(bf16[176,512]{1,0:T(8,128)(2,1)S(1)} %get-tuple-element.67), channel_id=1, source_target_pairs={{0,18},{1,19},{2,16},{3,17},{4,22},{5,23},{6,20},{7,21},{8,26},{9,... | collective-permute-start | bytes 540680 | tf_op jit(solution)/shard_map/ppermute | solution.py:26
  61.3 5.9 %collective-permute-start.25 = (bf16[128,1024]{1,0:T(8,128)(2,1)S(1)}, bf16[128,1024]{1,0:T(8,128)(2,1)S(1)}, u32[]{:S(2)}, u32[]{:S(2)}) collective-permute-start(bf16[128,1024]{1,0:T(8,128)(2,1)S(1)} %get-tuple-element.86), channel_id=1, source_target_pairs={{0,1},{1,0},{2,3},{3,2},{4,5},{5,4},{6,7},{7,6},{8,9},{9,8},{10,11... | collective-permute-start | bytes 786440 | tf_op jit(solution)/shard_map/ppermute | solution.py:26
  61.3 6.3 %collective-permute-start.24 = (bf16[128,1024]{1,0:T(8,128)(2,1)S(1)}, bf16[128,1024]{1,0:T(8,128)(2,1)S(1)}, u32[]{:S(2)}, u32[]{:S(2)}) collective-permute-start(bf16[128,1024]{1,0:T(8,128)(2,1)S(1)} %get-tuple-element.84), channel_id=1, source_target_pairs={{0,1},{1,0},{2,3},{3,2},{4,5},{5,4},{6,7},{7,6},{8,9},{9,8},{10,11... | collective-permute-start | bytes 786440 | tf_op jit(solution)/shard_map/ppermute | solution.py:26
  61.8 8.6 %collective-permute-start.18 = (bf16[176,512]{1,0:T(8,128)(2,1)S(1)}, bf16[176,512]{1,0:T(8,128)(2,1)S(1)}, u32[]{:S(2)}, u32[]{:S(2)}) collective-permute-start(bf16[176,512]{1,0:T(8,128)(2,1)S(1)} %get-tuple-element.75), channel_id=1, source_target_pairs={{0,2},{1,3},{2,0},{3,1},{4,6},{5,7},{6,4},{7,5},{8,10},{9,11},{10,... | collective-permute-start | bytes 540680 | tf_op jit(solution)/shard_map/ppermute | solution.py:26
  63.3 9.8 %collective-permute-start.19 = (bf16[176,512]{1,0:T(8,128)(2,1)S(1)}, bf16[176,512]{1,0:T(8,128)(2,1)S(1)}, u32[]{:S(2)}, u32[]{:S(2)}) collective-permute-start(bf16[176,512]{1,0:T(8,128)(2,1)S(1)} %get-tuple-element.76), channel_id=1, source_target_pairs={{0,18},{1,19},{2,16},{3,17},{4,22},{5,23},{6,20},{7,21},{8,26},{9,... | collective-permute-start | bytes 540680 | tf_op jit(solution)/shard_map/ppermute | solution.py:26
  64.8 10.3 %collective-permute-start.30 = (bf16[16,5120]{1,0:T(8,128)(2,1)S(1)}, bf16[16,5120]{1,0:T(8,128)(2,1)S(1)}, u32[]{:S(2)}, u32[]{:S(2)}) collective-permute-start(bf16[16,5120]{1,0:T(8,128)(2,1)S(1)} %get-tuple-element.96), channel_id=1, source_target_pairs={{0,12},{1,13},{2,14},{3,15},{4,8},{5,9},{6,10},{7,11},{8,4},{9,5},... | collective-permute-start | bytes 491528 | tf_op jit(solution)/shard_map/ppermute | solution.py:26
  67.2 14.5 %collective-permute-start.29 = (bf16[16,5120]{1,0:T(8,128)(2,1)S(1)}, bf16[16,5120]{1,0:T(8,128)(2,1)S(1)}, u32[]{:S(2)}, u32[]{:S(2)}) collective-permute-start(bf16[16,5120]{1,0:T(8,128)(2,1)S(1)} %get-tuple-element.94), channel_id=1, source_target_pairs={{0,8},{1,9},{2,10},{3,11},{4,12},{5,13},{6,14},{7,15},{8,0},{9,1},... | collective-permute-start | bytes 491528 | tf_op jit(solution)/shard_map/ppermute | solution.py:26
  67.6 14.1 %collective-permute-start.28 = (bf16[16,5120]{1,0:T(8,128)(2,1)S(1)}, bf16[16,5120]{1,0:T(8,128)(2,1)S(1)}, u32[]{:S(2)}, u32[]{:S(2)}) collective-permute-start(bf16[16,5120]{1,0:T(8,128)(2,1)S(1)} %get-tuple-element.92), channel_id=1, source_target_pairs={{0,4},{1,5},{2,6},{3,7},{4,0},{5,1},{6,2},{7,3},{8,12},{9,13},{10,... | collective-permute-start | bytes 491528 | tf_op jit(solution)/shard_map/ppermute | solution.py:26
  73.1 10.9 %collective-permute-start.27 = (bf16[176,512]{1,0:T(8,128)(2,1)S(1)}, bf16[176,512]{1,0:T(8,128)(2,1)S(1)}, u32[]{:S(2)}, u32[]{:S(2)}) collective-permute-start(bf16[176,512]{1,0:T(8,128)(2,1)S(1)} %get-tuple-element.90), channel_id=1, source_target_pairs={{0,18},{1,19},{2,16},{3,17},{4,22},{5,23},{6,20},{7,21},{8,26},{9,... | collective-permute-start | bytes 540680 | tf_op jit(solution)/shard_map/ppermute | solution.py:26
  74.5 9.5 %collective-permute-start.26 = (bf16[176,512]{1,0:T(8,128)(2,1)S(1)}, bf16[176,512]{1,0:T(8,128)(2,1)S(1)}, u32[]{:S(2)}, u32[]{:S(2)}) collective-permute-start(bf16[176,512]{1,0:T(8,128)(2,1)S(1)} %get-tuple-element.88), channel_id=1, source_target_pairs={{0,2},{1,3},{2,0},{3,1},{4,6},{5,7},{6,4},{7,5},{8,10},{9,11},{10,... | collective-permute-start | bytes 540680 | tf_op jit(solution)/shard_map/ppermute | solution.py:26
  81.8 1.5 %collective-permute-start.31 = (bf16[16,5120]{1,0:T(8,128)(2,1)S(1)}, bf16[16,5120]{1,0:T(8,128)(2,1)S(1)}, u32[]{:S(2)}, u32[]{:S(2)}) collective-permute-start(bf16[16,5120]{1,0:T(8,128)(2,1)S(1)} %shard_map.106.refs_0_), channel_id=1, source_target_pairs={{0,1},{1,0},{2,3},{3,2},{4,5},{5,4},{6,7},{7,6},{8,9},{9,8},{10,11... | collective-permute-start | bytes 491528 | tf_op jit(solution)/shard_map/ppermute | solution.py:26
  (7 other events, 44.8 us)

commit v10 on v6

--- a/solution.py
+++ b/solution.py
@@ -10,6 +10,7 @@
 ADAPTER_SCALE = 2.0
 AXES = ("groups", "adapter", "segment", "replica")
 LANES = 128
+SPARE = 256
 F32 = jnp.float32
 BF16 = jnp.bfloat16
 MIB = 1024 * 1024
@@ -18,9 +19,11 @@
 def moved(x, to):
     sizes = [lax.axis_size(a) for a in AXES]
     number = {at: i for i, at in enumerate(itertools.product(*map(range, sizes)))}
-    pairs = [
-        (i, number[tuple(t % s for t, s in zip(to(*at), sizes))]) for at, i in number.items()
-    ]
+    pairs = []
+    for at, i in number.items():
+        target = to(*at)
+        if target is not None:
+            pairs.append((i, number[tuple(t % s for t, s in zip(target, sizes))]))
     return lax.ppermute(x, AXES, pairs)
 
 
@@ -49,10 +52,6 @@
     )(*operands)
 
 
-def slots_of(tagged_ref):
-    return tagged_ref[:, -LANES:].astype(F32)[:, :1]
-
-
 def row_slots(holders, replicas, slots, rank, dr):
     here, core = lax.axis_index("adapter"), lax.axis_index("replica")
     own_slots = slots // replicas
@@ -61,29 +60,28 @@
     for k in range(holders):
         for j in range(own_slots):
             start = (k * own_slots + j) * rank
-            value = lax.rem(here + holders - k, holders) * slots
+            value = (here ^ k) * slots
             value = value + lax.rem(core + replicas - dr, replicas) * own_slots + j
             slot = jnp.where((lane >= start) & (lane < start + rank), value, slot)
     return slot.astype(F32)
 
 
-def tag_kernel(g_ref, name_ref, slot_ref, out_ref):
-    out_ref[:, :-LANES] = g_ref[...]
+def name_kernel(name_ref, slot_ref, out_ref):
     names = name_ref[...]
     slot = jnp.zeros_like(names)
     for j in range(slot_ref.shape[0]):
         slot = jnp.where(names == j, slot_ref[j], slot)
-    ones = jnp.ones((1, LANES), F32)
-    out_ref[:, -LANES:] = columns_by_columns(slot.astype(F32), ones).astype(BF16)
+    ones = jnp.ones((1, out_ref.shape[1]), F32)
+    out_ref[...] = columns_by_columns(slot.astype(F32), ones).astype(BF16)
 
 
 def join_kernel(*refs):
-    down_ref, up_ref = refs[-2:]
-    wide = down_ref.shape[1]
+    both_ref, down_ref = refs[-2:]
+    both_ref[:, -SPARE:] = jnp.zeros((both_ref.shape[0], SPARE), BF16)
     for k, ref in enumerate(refs[:-2]):
         rows = ref.shape[0]
-        down_ref[k * rows : (k + 1) * rows] = ref[:, :wide]
-        up_ref[k * rows : (k + 1) * rows] = ref[:, wide:]
+        both_ref[k * rows : (k + 1) * rows, :-SPARE] = ref[...]
+        down_ref[k * rows : (k + 1) * rows] = ref[:, : down_ref.shape[1]]
 
 
 def own_kernel(sizes, down_ref, up_ref, out_ref):
@@ -102,8 +100,8 @@
 
 def adapter_kernel(sizes, *refs):
     groups, holders, replicas, shard, slots, rank = sizes
-    x_ref, g_ref, sel_ref = refs[:3]
-    map_refs, refs = refs[3 : 3 + groups * replicas], refs[3 + groups * replicas :]
+    x_ref, g_ref, named_ref, sel_ref = refs[:4]
+    map_refs, refs = refs[4 : 4 + groups * replicas], refs[4 + groups * replicas :]
     own_ref, other_refs, down = refs[0], refs[1:-1], refs[-1]
     group = lax.axis_index("groups")
     tokens, width = x_ref.shape
@@ -118,7 +116,7 @@
                     :, z * half : (z + 1) * half
                 ]
     row_slot = [row_slots(holders, replicas, slots, rank, dr) for dr in range(replicas)]
-    keep = slots_of(g_ref) == jnp.concatenate(row_slot, axis=1)
+    keep = named_ref[...].astype(F32)[:, :1] == jnp.concatenate(row_slot, axis=1)
     in_sel = jnp.where(keep, rows_by_rows(x_ref[...], down[...]), 0.0).astype(BF16)
     grad_sel = sel_ref[pl.ds(0, tokens), :]
     step, split = 1024, cols // 2
@@ -138,25 +136,26 @@
 def frozen_kernel(sizes, k, count, *refs):
     tokens, groups, holders, replicas, slots, rank = sizes
     g_refs, refs = refs[:groups], refs[groups:]
-    down_refs, refs = refs[:replicas], refs[replicas:]
+    map_refs, refs = refs[:replicas], refs[replicas:]
     core, here = lax.axis_index("replica"), lax.axis_index("adapter")
+    rows = map_refs[0].shape[0]
+    wide = map_refs[0].shape[1] - g_refs[0].shape[1] - SPARE
+    half = wide // holders
     if k == 0:
-        up_refs, refs = refs[:replicas], refs[replicas:]
+        named_refs, refs = refs[:groups], refs[groups:]
         sel_ref = refs[-1]
         out_refs = refs[-1 - groups : -1]
-        rows = up_refs[0].shape[0]
         for dg in range(groups):
+            names = named_refs[dg][...].astype(F32)[:, :1]
             for dr in range(replicas):
-                keep = slots_of(g_refs[dg]) == row_slots(holders, replicas, slots, rank, dr)
-                proj_grad = rows_by_rows(g_refs[dg][:, :-LANES], up_refs[dr][...])
+                keep = names == row_slots(holders, replicas, slots, rank, dr)
+                proj_grad = rows_by_rows(g_refs[dg][...], map_refs[dr][:, wide:-SPARE])
                 sel_ref[pl.ds(dg * tokens, tokens), dr * rows : (dr + 1) * rows] = jnp.where(
                     keep, proj_grad, 0.0
                 ).astype(BF16)
     else:
         sel_ref, refs = refs[0], refs[1:]
         out_refs = refs[-groups:]
-    rows = down_refs[0].shape[0]
-    half = down_refs[0].shape[1] // holders
     shard_at = lax.rem(here + holders - k, holders) * half
     for j, block in enumerate(refs[:count]):
         if k == 0:
@@ -165,12 +164,12 @@
         at = 0 if count == 1 else lax.rem(core + replicas - j, replicas) * wide
         columns = pl.ds(pl.multiple_of(shard_at + at, wide), wide)
         for dg in range(groups):
-            base = rows_by_rows(g_refs[dg][:, :-LANES], block[...]).astype(BF16)
+            base = rows_by_rows(g_refs[dg][...], block[...]).astype(BF16)
             lora = 0.0
             for dr in range(replicas):
                 lora = lora + jnp.dot(
                     sel_ref[pl.ds(dg * tokens, tokens), dr * rows : (dr + 1) * rows],
-                    down_refs[dr][:, columns],
+                    map_refs[dr][:, columns],
                     preferred_element_type=F32,
                 )
             lora = (ADAPTER_SCALE * lora).astype(BF16)
@@ -246,15 +245,16 @@
     piece = half // replicas
     cols = width + value_width
 
-    tagged = call(
-        tag_kernel,
-        [jax.ShapeDtypeStruct((tokens, value_width + LANES), BF16)],
-        (grad_rows, token_adapter_index[0, :, 0][None], adapter_slot_index),
+    own_named = call(
+        name_kernel,
+        [jax.ShapeDtypeStruct((tokens, 3 * LANES), BF16)],
+        (token_adapter_index[0, :, 0][None], adapter_slot_index),
         scalars=1,
     )[0]
-    grads = [tagged] + [
-        moved(tagged, lambda g, z, s, r: (g - dg, z, s, r)) for dg in range(1, groups)
-    ]
+    grads, named = [grad_rows], [own_named]
+    for dg in range(1, groups):
+        grads.append(moved(grad_rows, lambda g, z, s, r: (g - dg, z, s, r)))
+        named.append(moved(own_named, lambda g, z, s, r: (g - dg, z, s, r)))
 
     own = call(
         functools.partial(own_kernel, (groups, holders, shard)),
@@ -263,24 +263,23 @@
     )[0]
     held = [own]
     for k in range(1, holders):
-        held.append(moved(own, lambda g, z, s, r: (g, z + k, s, r)))
+        held.append(moved(own, lambda g, z, s, r: (g, z ^ k, s, r)))
 
     ring = [lax.dynamic_slice_in_dim(frozen, (group * replicas + core) * piece, piece, axis=0)]
     ring.append(moved(ring[0], lambda g, z, s, r: (g, z + 1, s, r)))
-    held, grads, ring = lax.optimization_barrier((held, grads, ring))
-    joined = call(
+    held, grads, named = lax.optimization_barrier((held, grads, named))
+    both, downs = call(
         join_kernel,
         [
+            jax.ShapeDtypeStruct((holders * rows, holders * half + value_width + SPARE), BF16),
             jax.ShapeDtypeStruct((holders * rows, holders * half), BF16),
-            jax.ShapeDtypeStruct((holders * rows, value_width), BF16),
         ],
         held,
     )
-    downs, ups = [joined[0]], [joined[1]]
-    for dr in range(1, replicas):
-        ups.append(moved(ups[0], lambda g, z, s, r: (g, z, s, r + dr)))
-        downs.append(moved(downs[0], lambda g, z, s, r: (g, z, s, r + dr)))
-    others = [moved(downs[0], lambda g, z, s, r: (g + dg, z, s, r)) for dg in range(1, groups)]
+    both = [both] + [
+        moved(both, lambda g, z, s, r: (g, z, s, r + dr)) for dr in range(1, replicas)
+    ]
+    others = [moved(downs, lambda g, z, s, r: (g + dg, z, s, r)) for dg in range(1, groups)]
     def pieces_of(k, *before):
         if k == 0:
             return [frozen]
@@ -298,8 +297,8 @@
 
     kept = replicas * holders * rows
 
-    def adapter_sums(sel):
-        maps = list(downs)
+    def adapter_sums(sel, *before):
+        maps = list(both)
         for other in others:
             maps.append(after(other, sel))
             for dr in range(1, replicas):
@@ -308,12 +307,12 @@
             functools.partial(adapter_kernel, (groups, holders, replicas, shard, slots, rank)),
             [jax.ShapeDtypeStruct((holders * rows, cols), F32)]
             + [jax.ShapeDtypeStruct((holders * rows, cols // 2), BF16)] * (2 * replicas - 2),
-            (inputs, tagged, sel, *maps),
+            (inputs, grad_rows, named[0], sel, *maps),
             [jax.ShapeDtypeStruct((kept, width), BF16)],
         )
         part, sent = gradients[0], gradients[1:]
         came = [
-            moved(sent[2 * dr - 2 + j], lambda g, z, s, r: (g, z, s, r - dr))
+            moved(after(sent[2 * dr - 2 + j], *before), lambda g, z, s, r: (g, z, s, r - dr))
             for dr in range(1, replicas)
             for j in range(2)
         ]
@@ -325,27 +324,24 @@
         )
         return part, chip
 
-    arrived, outs = [], []
+    arrived, outs, sel = [], [], None
     for k in range(holders):
         if k > 1:
-            last = ring[-1]
-            if k > 2:
-                last = after(last, *outs[k - 2], part)
+            last = after(ring[-1], *outs[k - 2], part) if k > 2 else after(ring[-1], sel)
             ring.append(moved(last, lambda g, z, s, r: (g, z + 1, s, r)))
-        gate = [*arrived[k - 2], *outs[k - 1]] if k > 1 else []
-        blocks = pieces_of(k, *gate, *(chip[:1] if k > 2 else ()))
-        tokens_in = [after(tagged, part), *grads[1:]] if k == 1 else grads
+        gate = outs[k - 1] if k > 1 else [sel] * k
+        blocks = pieces_of(k, *gate, *([*arrived[k - 2], chip[0]] if k > 2 else ()))
+        tokens_in = [after(grad_rows, part), *grads[1:]] if k == 1 else grads
         out = call(
             functools.partial(
                 frozen_kernel, (tokens, groups, holders, replicas, slots, rank), k, len(blocks)
             ),
             [jax.ShapeDtypeStruct((tokens, half), BF16)] * groups
             + [jax.ShapeDtypeStruct((groups * tokens, kept), BF16)] * (k == 0),
-            [*tokens_in, *downs, *([sel] if k else ups), *blocks],
+            [*tokens_in, *both, *([sel] if k else named), *blocks],
         )
         if k == 0:
             sel = out[groups]
-            part, chip = adapter_sums(sel)
         outs.append(list(out[:groups]))
         mails = outs[-1]
         if k > 2:
@@ -353,6 +349,8 @@
         arrived.append(
             [moved(mails[dg], lambda g, z, s, r: (g + dg, z, s - 1, r)) for dg in range(groups)]
         )
+        if k == 0:
+            part, chip = adapter_sums(sel, *arrived[0])
     passed = call(
         functools.partial(place_kernel, (groups, holders, shard, half)),
         [jax.ShapeDtypeStruct((tokens, width), BF16)],
@@ -360,7 +358,7 @@
     )[0]
 
     sums = [chip[0]] + [
-        moved(after(chip[k], ring[-1]), lambda g, z, s, r: (g, z - k, s, r))
+        moved(after(chip[k], ring[-1]), lambda g, z, s, r: (g, z ^ k, s, r))
         for k in range(1, holders)
     ]
     total = call(total_kernel, [jax.ShapeDtypeStruct((rows, cols), BF16)], sums)[0]

time: 85.4 us -> 89.1 us (1.043)
  waiting for transfers between devices: 38.1 us -> 48.2 us
  starting transfers between devices: 32.1 us -> 25.2 us
    ppermute x28, waiting for transfers between devices: 38.1 us -> 48.2 us  [moved(): return lax.ppermute(x, AXES, pairs)]
    ppermute x28, starting transfers between devices: 32.1 us -> 25.2 us  [moved(): return lax.ppermute(x, AXES, pairs)]
  transfers between devices with their start and end apart: 28 -> 28, of which waited for: 14 -> 15; matrix products, arithmetic and copies ran while one was open for 0% -> 1% of each run, Pallas kernels for 9% -> 9%
where the time goes in v10:
time: 89.1 us; the launch traced here: 88.8 us
  waiting for transfers between devices  48.2 us (54%)
  starting transfers between devices  25.2 us (28%)
  Pallas kernels  8.81 us (10%)
  local copies, waits for them, and re-layouts  5.8 us (7%)
    ppermute x28, waiting for transfers between devices, moved(): return lax.ppermute(x, AXES, pairs)  48.2 us
    ppermute x28, starting transfers between devices, moved(): return lax.ppermute(x, AXES, pairs)  25.2 us
    pallas_call x12, Pallas kernels, call(): pl.pallas_call(kernel, out_shape=out_shape, in_specs=[pl.BlockSpec(memory...  8.81 us
    unnamed x14, local copies, waits for them, and re-layouts  4.72 us
  transfers between devices with their start and end apart: 28, of which 15 were waited for; matrix products, arithmetic and copies ran while one was open for 1% of the time, Pallas kernels for 9%

profile of v10, /device:TPU:0, one launch (start us, length us, event | category | flops | bytes accessed | tf_op | source)
XLA Modules:
  0.0 88.8 jit_solution(1869969513063603483)
XLA Ops:
  0.6 3.0 %collective-permute-start.3 = (bf16[176,1024]{1,0:T(8,128)(2,1)}, bf16[176,1024]{1,0:T(8,128)(2,1)S(1)}, u32[]{:S(2)}, u32[]{:S(2)}) collective-permute-start(bf16[176,1024]{1,0:T(8,128)(2,1)} %bitcast.11), channel_id=1, source_target_pairs={{0,16},{1,17},{2,18},{3,19},{4,20},{5,21},{6,22},{7,23},{8,24},{9,... | collective-permute-start | bytes 1081352 | tf_op jit(solution)/shard_map/ppermute | solution.py:27
  3.7 0.9 %copy-done.3 = bf16[1,2,16,4096]{3,2,1,0:T(8,128)(2,1)S(1)} copy-done((bf16[1,2,16,4096]{3,2,1,0:T(8,128)(2,1)S(1)}, bf16[1,2,16,4096]{3,2,1,0:T(8,128)(2,1)}, u32[]{:S(2)}) %copy-start.3) | copy-done | bytes 262168
  4.6 0.8 copy-done.4
  5.5 1.6 %collective-permute-start = (bf16[16,3072]{1,0:T(8,128)(2,1)S(1)}, bf16[16,3072]{1,0:T(8,128)(2,1)S(1)}, u32[]{:S(2)}, u32[]{:S(2)}) collective-permute-start(bf16[16,3072]{1,0:T(8,128)(2,1)S(1)} %shard_map.94.refs_0_), channel_id=1, source_target_pairs={{0,4},{1,5},{2,6},{3,7},{4,0},{5,1},{6,2},{7,3},{8,12},{9,13},{10,... | collective-permute-start | bytes 294920 | tf_op jit(solution)/shard_map/ppermute | solution.py:27
  7.1 2.6 %collective-permute-start.1 = (bf16[16,3072]{1,0:T(8,128)(2,1)S(1)}, bf16[16,3072]{1,0:T(8,128)(2,1)S(1)}, u32[]{:S(2)}, u32[]{:S(2)}) collective-permute-start(bf16[16,3072]{1,0:T(8,128)(2,1)S(1)} %shard_map.94.refs_0_), channel_id=1, source_target_pairs={{0,8},{1,9},{2,10},{3,11},{4,12},{5,13},{6,14},{7,15},{8,0},{9,1},... | collective-permute-start | bytes 294920 | tf_op jit(solution)/shard_map/ppermute | solution.py:27
  12.4 1.1 %dynamic-slice_bitcast_fusion = bf16[256,1024]{1,0:T(8,128)(2,1)S(1)} fusion(bf16[1,1024,1024]{2,1,0:T(8,128)(2,1)} %param.11, s32[]{:T(128)S(6)} %select_n.3), kind=kLoop, calls=%fused_computation | loop fusion | bytes 1048580 | tf_op jit(solution)/shard_map/dynamic_slice | solution.py:268
  13.5 0.9 %collective-permute-start.10 = (bf16[256,1024]{1,0:T(8,128)(2,1)S(1)}, bf16[256,1024]{1,0:T(8,128)(2,1)S(1)}, u32[]{:S(2)}, u32[]{:S(2)}) collective-permute-start(bf16[256,1024]{1,0:T(8,128)(2,1)S(1)} %dynamic-slice_bitcast_fusion), channel_id=1, source_target_pairs={{0,4},{1,5},{2,6},{3,7},{4,8},{5,9},{6,10},{7,11},{8,12},{9,13},{1... | collective-permute-start | bytes 1572872 | tf_op jit(solution)/shard_map/ppermute | solution.py:27
  14.5 14.0 %collective-permute-done.1.refs_2_ = bf16[16,3072]{1,0:T(8,128)(2,1)S(1)} collective-permute-done((bf16[16,3072]{1,0:T(8,128)(2,1)S(1)}, bf16[16,3072]{1,0:T(8,128)(2,1)S(1)}, u32[]{:S(2)}, u32[]{:S(2)}) %collective-permute-start.1) | collective-permute-done | bytes 98336 | tf_op jit(solution)/shard_map/ppermute | solution.py:27
  28.7 1.7 %collective-permute-done.5.refs_3_.refs_5_ = bf16[64,3328]{1,0:T(8,128)(2,1)S(1)} collective-permute-done((bf16[64,3328]{1,0:T(8,128)(2,1)S(1)}, bf16[64,3328]{1,0:T(8,128)(2,1)S(1)}, u32[]{:S(2)}, u32[]{:S(2)}) %collective-permute-start.5) | collective-permute-done | bytes 426016 | tf_op jit(solution)/shard_map/ppermute | solution.py:27
  30.4 1.6 %copy-done.1 = bf16[1,1024,1024]{2,1,0:T(8,128)(2,1)S(1)} copy-done((bf16[1,1024,1024]{2,1,0:T(8,128)(2,1)S(1)}, bf16[1,1024,1024]{2,1,0:T(8,128)(2,1)}, u32[]{:S(2)}) %copy-start.1) | copy-done | bytes 2097176
  32.0 1.5 %shard_map.97 = (bf16[176,512]{1,0:T(8,128)(2,1)S(1)}, bf16[176,512]{1,0:T(8,128)(2,1)S(1)}, bf16[352,128]{1,0:T(8,128)(2,1)S(1)}) custom-call(bf16[176,1024]{1,0:T(8,128)(2,1)S(1)} %bitcast.12, bf16[176,1024]{1,0:T(8,128)(2,1)S(1)} %collective-permute-done.3.refs_1_, bf16[64,3328]{1,0:T(8,128)(2,1)S(1)} %get-tuple-element.50.refs_2_.refs_4_, ...), custom_call_target="tpu_custom_call" | custom-call | flops 1000 | bytes 1000 | tf_op jit(solution)/shard_map/pallas_call | solution.py:44
  33.7 1.6 %collective-permute-start.14 = (bf16[256,1024]{1,0:T(8,128)(2,1)S(1)}, bf16[256,1024]{1,0:T(8,128)(2,1)S(1)}, u32[]{:S(2)}, u32[]{:S(2)}) collective-permute-start(bf16[256,1024]{1,0:T(8,128)(2,1)S(1)} %collective-permute-done.10.refs_5_), channel_id=1, source_target_pairs={{0,4},{1,5},{2,6},{3,7},{4,8},{5,9},{6,10},{7,11},{8,12},{9,13},{1... | collective-permute-start | bytes 1572872 | tf_op jit(solution)/shard_map/ppermute | solution.py:27
  35.3 2.1 %collective-permute-done.8.refs_6_ = bf16[64,2048]{1,0:T(8,128)(2,1)S(1)} collective-permute-done((bf16[64,2048]{1,0:T(8,128)(2,1)S(1)}, bf16[64,2048]{1,0:T(8,128)(2,1)S(1)}, u32[]{:S(2)}, u32[]{:S(2)}) %collective-permute-start.8) | collective-permute-done | bytes 262176 | tf_op jit(solution)/shard_map/ppermute | solution.py:27
  37.4 1.5 %collective-permute-start.6 = (bf16[176,512]{1,0:T(8,128)(2,1)S(1)}, bf16[176,512]{1,0:T(8,128)(2,1)S(1)}, u32[]{:S(2)}, u32[]{:S(2)}) collective-permute-start(bf16[176,512]{1,0:T(8,128)(2,1)S(1)} %get-tuple-element.53), channel_id=1, source_target_pairs={{0,2},{1,3},{2,0},{3,1},{4,6},{5,7},{6,4},{7,5},{8,10},{9,11},{10,... | collective-permute-start | bytes 540680 | tf_op jit(solution)/shard_map/ppermute | solution.py:27
  39.1 1.3 %shard_map.98 = (f32[64,5120]{1,0:T(8,128)S(1)}, bf16[64,2560]{1,0:T(8,128)(2,1)S(1)}, bf16[64,2560]{1,0:T(8,128)(2,1)S(1)}) custom-call(bf16[176,4096]{1,0:T(8,128)(2,1)S(1)} %bitcast.18, bf16[176,1024]{1,0:T(8,128)(2,1)S(1)} %bitcast.13, bf16[176,384]{1,0:T(8,128)(2,1)S(1)} %shard_map.95.refs_4_.refs_2_, ...), custom_call_target="tpu_custom_call" | custom-call | flops 1000 | bytes 1000 | tf_op jit(solution)/shard_map/pallas_call | solution.py:44
  40.4 1.0 %shard_map.99 = (bf16[176,512]{1,0:T(8,128)(2,1)S(1)}, bf16[176,512]{1,0:T(8,128)(2,1)S(1)}) custom-call(bf16[176,1024]{1,0:T(8,128)(2,1)S(1)} %bitcast.14, bf16[176,1024]{1,0:T(8,128)(2,1)S(1)} %collective-permute-done.3.refs_1_, bf16[64,3328]{1,0:T(8,128)(2,1)S(1)} %get-tuple-element.50.refs_2_.refs_4_, ...), custom_call_target="tpu_custom_call" | custom-call | flops 1000 | bytes 1000 | tf_op jit(solution)/shard_map/pallas_call | solution.py:44
  41.4 8.3 %collective-permute-done.14.refs_5_ = bf16[256,1024]{1,0:T(8,128)(2,1)S(1)} collective-permute-done((bf16[256,1024]{1,0:T(8,128)(2,1)S(1)}, bf16[256,1024]{1,0:T(8,128)(2,1)S(1)}, u32[]{:S(2)}, u32[]{:S(2)}) %collective-permute-start.14) | collective-permute-done | bytes 524320 | tf_op jit(solution)/shard_map/ppermute | solution.py:27
  50.4 1.5 %collective-permute-start.12 = (bf16[176,512]{1,0:T(8,128)(2,1)S(1)}, bf16[176,512]{1,0:T(8,128)(2,1)S(1)}, u32[]{:S(2)}, u32[]{:S(2)}) collective-permute-start(bf16[176,512]{1,0:T(8,128)(2,1)S(1)} %get-tuple-element.61), channel_id=1, source_target_pairs={{0,2},{1,3},{2,0},{3,1},{4,6},{5,7},{6,4},{7,5},{8,10},{9,11},{10,... | collective-permute-start | bytes 540680 | tf_op jit(solution)/shard_map/ppermute | solution.py:27
  52.1 1.3 %collective-permute-start.13 = (bf16[176,512]{1,0:T(8,128)(2,1)S(1)}, bf16[176,512]{1,0:T(8,128)(2,1)S(1)}, u32[]{:S(2)}, u32[]{:S(2)}) collective-permute-start(bf16[176,512]{1,0:T(8,128)(2,1)S(1)} %get-tuple-element.62), channel_id=1, source_target_pairs={{0,18},{1,19},{2,16},{3,17},{4,22},{5,23},{6,20},{7,21},{8,26},{9,... | collective-permute-start | bytes 540680 | tf_op jit(solution)/shard_map/ppermute | solution.py:27
  53.5 1.0 %shard_map.100 = (bf16[176,512]{1,0:T(8,128)(2,1)S(1)}, bf16[176,512]{1,0:T(8,128)(2,1)S(1)}) custom-call(bf16[176,1024]{1,0:T(8,128)(2,1)S(1)} %bitcast.15, bf16[176,1024]{1,0:T(8,128)(2,1)S(1)} %collective-permute-done.3.refs_1_, bf16[64,3328]{1,0:T(8,128)(2,1)S(1)} %get-tuple-element.50.refs_2_.refs_4_, ...), custom_call_target="tpu_custom_call" | custom-call | flops 1000 | bytes 1000 | tf_op jit(solution)/shard_map/pallas_call | solution.py:44
  54.5 3.2 %collective-permute-done.12.refs_2_ = bf16[176,512]{1,0:T(8,128)(2,1)S(1)} collective-permute-done((bf16[176,512]{1,0:T(8,128)(2,1)S(1)}, bf16[176,512]{1,0:T(8,128)(2,1)S(1)}, u32[]{:S(2)}, u32[]{:S(2)}) %collective-permute-start.12) | collective-permute-done | bytes 180256 | tf_op jit(solution)/shard_map/ppermute | solution.py:27
  57.7 3.2 %collective-permute-done.13.refs_3_ = bf16[176,512]{1,0:T(8,128)(2,1)S(1)} collective-permute-done((bf16[176,512]{1,0:T(8,128)(2,1)S(1)}, bf16[176,512]{1,0:T(8,128)(2,1)S(1)}, u32[]{:S(2)}, u32[]{:S(2)}) %collective-permute-start.13) | collective-permute-done | bytes 180256 | tf_op jit(solution)/shard_map/ppermute | solution.py:27
  60.9 4.9 %collective-permute-done.18.refs_5_ = bf16[256,1024]{1,0:T(8,128)(2,1)S(1)} collective-permute-done((bf16[256,1024]{1,0:T(8,128)(2,1)S(1)}, bf16[256,1024]{1,0:T(8,128)(2,1)S(1)}, u32[]{:S(2)}, u32[]{:S(2)}) %collective-permute-start.18) | collective-permute-done | bytes 524320 | tf_op jit(solution)/shard_map/ppermute | solution.py:27
  65.8 1.5 %collective-permute-start.16 = (bf16[176,512]{1,0:T(8,128)(2,1)S(1)}, bf16[176,512]{1,0:T(8,128)(2,1)S(1)}, u32[]{:S(2)}, u32[]{:S(2)}) collective-permute-start(bf16[176,512]{1,0:T(8,128)(2,1)S(1)} %get-tuple-element.64), channel_id=1, source_target_pairs={{0,2},{1,3},{2,0},{3,1},{4,6},{5,7},{6,4},{7,5},{8,10},{9,11},{10,... | collective-permute-start | bytes 540680 | tf_op jit(solution)/shard_map/ppermute | solution.py:27
  67.7 4.3 %collective-permute-start.24 = (bf16[16,5120]{1,0:T(8,128)(2,1)S(1)}, bf16[16,5120]{1,0:T(8,128)(2,1)S(1)}, u32[]{:S(2)}, u32[]{:S(2)}) collective-permute-start(bf16[16,5120]{1,0:T(8,128)(2,1)S(1)} %get-tuple-element.78), channel_id=1, source_target_pairs={{0,4},{1,5},{2,6},{3,7},{4,0},{5,1},{6,2},{7,3},{8,12},{9,13},{10,... | collective-permute-start | bytes 491528 | tf_op jit(solution)/shard_map/ppermute | solution.py:27
  72.0 1.0 %shard_map.102 = (bf16[176,512]{1,0:T(8,128)(2,1)S(1)}, bf16[176,512]{1,0:T(8,128)(2,1)S(1)}) custom-call(bf16[176,1024]{1,0:T(8,128)(2,1)S(1)} %bitcast.16, bf16[176,1024]{1,0:T(8,128)(2,1)S(1)} %collective-permute-done.3.refs_1_, bf16[64,3328]{1,0:T(8,128)(2,1)S(1)} %get-tuple-element.50.refs_2_.refs_4_, ...), custom_call_target="tpu_custom_call" | custom-call | flops 1000 | bytes 1000 | tf_op jit(solution)/shard_map/pallas_call | solution.py:44
  73.2 3.2 %collective-permute-done.17.refs_5_ = bf16[176,512]{1,0:T(8,128)(2,1)S(1)} collective-permute-done((bf16[176,512]{1,0:T(8,128)(2,1)S(1)}, bf16[176,512]{1,0:T(8,128)(2,1)S(1)}, u32[]{:S(2)}, u32[]{:S(2)}) %collective-permute-start.17) | collective-permute-done | bytes 180256 | tf_op jit(solution)/shard_map/ppermute | solution.py:27
  76.4 2.6 %collective-permute-start.23 = (bf16[176,512]{1,0:T(8,128)(2,1)S(1)}, bf16[176,512]{1,0:T(8,128)(2,1)S(1)}, u32[]{:S(2)}, u32[]{:S(2)}) collective-permute-start(bf16[176,512]{1,0:T(8,128)(2,1)S(1)} %get-tuple-element.76), channel_id=1, source_target_pairs={{0,18},{1,19},{2,16},{3,17},{4,22},{5,23},{6,20},{7,21},{8,26},{9,... | collective-permute-start | bytes 540680 | tf_op jit(solution)/shard_map/ppermute | solution.py:27
  79.6 2.6 %collective-permute-done.25.refs_2_ = bf16[16,5120]{1,0:T(8,128)(2,1)S(1)} collective-permute-done((bf16[16,5120]{1,0:T(8,128)(2,1)S(1)}, bf16[16,5120]{1,0:T(8,128)(2,1)S(1)}, u32[]{:S(2)}, u32[]{:S(2)}) %collective-permute-start.25) | collective-permute-done | bytes 163872 | tf_op jit(solution)/shard_map/ppermute | solution.py:27
  82.3 1.4 %collective-permute-done.27.refs_1_ = bf16[16,5120]{1,0:T(8,128)(2,1)S(1)} collective-permute-done((bf16[16,5120]{1,0:T(8,128)(2,1)S(1)}, bf16[16,5120]{1,0:T(8,128)(2,1)S(1)}, u32[]{:S(2)}, u32[]{:S(2)}) %collective-permute-start.27) | collective-permute-done | bytes 163872 | tf_op jit(solution)/shard_map/ppermute | solution.py:27
  84.8 2.8 %collective-permute-done.22.refs_6_ = bf16[176,512]{1,0:T(8,128)(2,1)S(1)} collective-permute-done((bf16[176,512]{1,0:T(8,128)(2,1)S(1)}, bf16[176,512]{1,0:T(8,128)(2,1)S(1)}, u32[]{:S(2)}, u32[]{:S(2)}) %collective-permute-start.22) | collective-permute-done | bytes 180256 | tf_op jit(solution)/shard_map/ppermute | solution.py:27
  87.6 1.2 %shard_map.103 = bf16[176,4096]{1,0:T(8,128)(2,1)} custom-call(bf16[176,512]{1,0:T(8,128)(2,1)S(1)} %collective-permute-done.6.refs_0_, bf16[176,512]{1,0:T(8,128)(2,1)S(1)} %collective-permute-done.7.refs_1_, bf16[176,512]{1,0:T(8,128)(2,1)S(1)} %collective-permute-done.12.refs_2_, bf16[176,512]{1,0:T(8,128)(2,1)S(1)} %collective-permute-done.13.refs_3_, ...), custom_call_target="tpu_custom_call" | custom-call | flops 1000 | bytes 1000 | tf_op jit(solution)/shard_map/pallas_call | solution.py:44
  (51 shorter events, 6.7 us)
Async XLA Ops:
  0.6 29.8 %copy-start = (bf16[1,176,1024]{2,1,0:T(8,128)(2,1)S(1)}, bf16[1,176,1024]{2,1,0:T(8,128)(2,1)}, u32[]{:S(2)}) copy-start(bf16[1,176,1024]{2,1,0:T(8,128)(2,1)} %param.8) | copy-start | bytes 1081348
  0.6 27.9 %collective-permute-start.3 = (bf16[176,1024]{1,0:T(8,128)(2,1)}, bf16[176,1024]{1,0:T(8,128)(2,1)S(1)}, u32[]{:S(2)}, u32[]{:S(2)}) collective-permute-start(bf16[176,1024]{1,0:T(8,128)(2,1)} %bitcast.11), channel_id=1, source_target_pairs={{0,16},{1,17},{2,18},{3,19},{4,20},{5,21},{6,22},{7,23},{8,24},{9,... | collective-permute-start | bytes 1081352 | tf_op jit(solution)/shard_map/ppermute | solution.py:27
  3.7 0.9 %copy-start.3 = (bf16[1,2,16,4096]{3,2,1,0:T(8,128)(2,1)S(1)}, bf16[1,2,16,4096]{3,2,1,0:T(8,128)(2,1)}, u32[]{:S(2)}) copy-start(bf16[1,2,16,4096]{3,2,1,0:T(8,128)(2,1)} %param.12) | copy-start | bytes 786436
  5.5 8.0 %collective-permute-start = (bf16[16,3072]{1,0:T(8,128)(2,1)S(1)}, bf16[16,3072]{1,0:T(8,128)(2,1)S(1)}, u32[]{:S(2)}, u32[]{:S(2)}) collective-permute-start(bf16[16,3072]{1,0:T(8,128)(2,1)S(1)} %shard_map.94.refs_0_), channel_id=1, source_target_pairs={{0,4},{1,5},{2,6},{3,7},{4,0},{5,1},{6,2},{7,3},{8,12},{9,13},{10,... | collective-permute-start | bytes 294920 | tf_op jit(solution)/shard_map/ppermute | solution.py:27
  7.1 21.4 %collective-permute-start.1 = (bf16[16,3072]{1,0:T(8,128)(2,1)S(1)}, bf16[16,3072]{1,0:T(8,128)(2,1)S(1)}, u32[]{:S(2)}, u32[]{:S(2)}) collective-permute-start(bf16[16,3072]{1,0:T(8,128)(2,1)S(1)} %shard_map.94.refs_0_), channel_id=1, source_target_pairs={{0,8},{1,9},{2,10},{3,11},{4,12},{5,13},{6,14},{7,15},{8,0},{9,1},... | collective-permute-start | bytes 294920 | tf_op jit(solution)/shard_map/ppermute | solution.py:27
  9.7 18.8 %collective-permute-start.2 = (bf16[16,3072]{1,0:T(8,128)(2,1)S(1)}, bf16[16,3072]{1,0:T(8,128)(2,1)S(1)}, u32[]{:S(2)}, u32[]{:S(2)}) collective-permute-start(bf16[16,3072]{1,0:T(8,128)(2,1)S(1)} %shard_map.94.refs_0_), channel_id=1, source_target_pairs={{0,12},{1,13},{2,14},{3,15},{4,8},{5,9},{6,10},{7,11},{8,4},{9,5},... | collective-permute-start | bytes 294920 | tf_op jit(solution)/shard_map/ppermute | solution.py:27
  12.1 16.4 %collective-permute-start.4 = (bf16[176,384]{1,0:T(8,128)(2,1)S(1)}, bf16[176,384]{1,0:T(8,128)(2,1)S(1)}, u32[]{:S(2)}, u32[]{:S(2)}) collective-permute-start(bf16[176,384]{1,0:T(8,128)(2,1)S(1)} %shard_map.95.refs_4_.refs_2_), channel_id=1, source_target_pairs={{0,16},{1,17},{2,18},{3,19},{4,20},{5,21},{6,22},{7,23},{8,24},{9,... | collective-permute-start | bytes 405512 | tf_op jit(solution)/shard_map/ppermute | solution.py:27
  13.5 20.0 %collective-permute-start.10 = (bf16[256,1024]{1,0:T(8,128)(2,1)S(1)}, bf16[256,1024]{1,0:T(8,128)(2,1)S(1)}, u32[]{:S(2)}, u32[]{:S(2)}) collective-permute-start(bf16[256,1024]{1,0:T(8,128)(2,1)S(1)} %dynamic-slice_bitcast_fusion), channel_id=1, source_target_pairs={{0,4},{1,5},{2,6},{3,7},{4,8},{5,9},{6,10},{7,11},{8,12},{9,13},{1... | collective-permute-start | bytes 1572872 | tf_op jit(solution)/shard_map/ppermute | solution.py:27
  28.6 1.8 %collective-permute-start.5 = (bf16[64,3328]{1,0:T(8,128)(2,1)S(1)}, bf16[64,3328]{1,0:T(8,128)(2,1)S(1)}, u32[]{:S(2)}, u32[]{:S(2)}) collective-permute-start(bf16[64,3328]{1,0:T(8,128)(2,1)S(1)} %get-tuple-element.50.refs_2_.refs_4_), channel_id=1, source_target_pairs={{0,1},{1,0},{2,3},{3,2},{4,5},{5,4},{6,7},{7,6},{8,9},{9,8},{10,11... | collective-permute-start | bytes 1277960 | tf_op jit(solution)/shard_map/ppermute | solution.py:27
  28.6 8.7 %collective-permute-start.8 = (bf16[64,2048]{1,0:T(8,128)(2,1)S(1)}, bf16[64,2048]{1,0:T(8,128)(2,1)S(1)}, u32[]{:S(2)}, u32[]{:S(2)}) collective-permute-start(bf16[64,2048]{1,0:T(8,128)(2,1)S(1)} %get-tuple-element.56), channel_id=1, source_target_pairs={{0,16},{1,17},{2,18},{3,19},{4,20},{5,21},{6,22},{7,23},{8,24},{9,... | collective-permute-start | bytes 786440 | tf_op jit(solution)/shard_map/ppermute | solution.py:27
  30.4 1.6 %copy-start.1 = (bf16[1,1024,1024]{2,1,0:T(8,128)(2,1)S(1)}, bf16[1,1024,1024]{2,1,0:T(8,128)(2,1)}, u32[]{:S(2)}) copy-start(bf16[1,1024,1024]{2,1,0:T(8,128)(2,1)} %param.11) | copy-start | bytes 6291460
  32.0 7.1 %copy-start.2 = (bf16[1,176,4096]{2,1,0:T(8,128)(2,1)S(1)}, bf16[1,176,4096]{2,1,0:T(8,128)(2,1)}, u32[]{:S(2)}) copy-start(bf16[1,176,4096]{2,1,0:T(8,128)(2,1)} %param.7) | copy-start | bytes 4325380
  33.5 6.9 %collective-permute-start.11 = (bf16[256,1024]{1,0:T(8,128)(2,1)S(1)}, bf16[256,1024]{1,0:T(8,128)(2,1)S(1)}, u32[]{:S(2)}, u32[]{:S(2)}) collective-permute-start(bf16[256,1024]{1,0:T(8,128)(2,1)S(1)} %collective-permute-done.10.refs_5_), channel_id=1, source_target_pairs={{0,1},{1,0},{2,3},{3,2},{4,5},{5,4},{6,7},{7,6},{8,9},{9,8},{10,11... | collective-permute-start | bytes 1572872 | tf_op jit(solution)/shard_map/ppermute | solution.py:27
  33.7 16.0 %collective-permute-start.14 = (bf16[256,1024]{1,0:T(8,128)(2,1)S(1)}, bf16[256,1024]{1,0:T(8,128)(2,1)S(1)}, u32[]{:S(2)}, u32[]{:S(2)}) collective-permute-start(bf16[256,1024]{1,0:T(8,128)(2,1)S(1)} %collective-permute-done.10.refs_5_), channel_id=1, source_target_pairs={{0,4},{1,5},{2,6},{3,7},{4,8},{5,9},{6,10},{7,11},{8,12},{9,13},{1... | collective-permute-start | bytes 1572872 | tf_op jit(solution)/shard_map/ppermute | solution.py:27
  37.4 1.7 %collective-permute-start.9 = (bf16[64,2048]{1,0:T(8,128)(2,1)S(1)}, bf16[64,2048]{1,0:T(8,128)(2,1)S(1)}, u32[]{:S(2)}, u32[]{:S(2)}) collective-permute-start(bf16[64,2048]{1,0:T(8,128)(2,1)S(1)} %collective-permute-done.8.refs_6_), channel_id=1, source_target_pairs={{0,1},{1,0},{2,3},{3,2},{4,5},{5,4},{6,7},{7,6},{8,9},{9,8},{10,11... | collective-permute-start | bytes 786440 | tf_op jit(solution)/shard_map/ppermute | solution.py:27
  37.4 12.3 %collective-permute-start.6 = (bf16[176,512]{1,0:T(8,128)(2,1)S(1)}, bf16[176,512]{1,0:T(8,128)(2,1)S(1)}, u32[]{:S(2)}, u32[]{:S(2)}) collective-permute-start(bf16[176,512]{1,0:T(8,128)(2,1)S(1)} %get-tuple-element.53), channel_id=1, source_target_pairs={{0,2},{1,3},{2,0},{3,1},{4,6},{5,7},{6,4},{7,5},{8,10},{9,11},{10,... | collective-permute-start | bytes 540680 | tf_op jit(solution)/shard_map/ppermute | solution.py:27
  38.9 10.8 %collective-permute-start.7 = (bf16[176,512]{1,0:T(8,128)(2,1)S(1)}, bf16[176,512]{1,0:T(8,128)(2,1)S(1)}, u32[]{:S(2)}, u32[]{:S(2)}) collective-permute-start(bf16[176,512]{1,0:T(8,128)(2,1)S(1)} %get-tuple-element.54), channel_id=1, source_target_pairs={{0,18},{1,19},{2,16},{3,17},{4,22},{5,23},{6,20},{7,21},{8,26},{9,... | collective-permute-start | bytes 540680 | tf_op jit(solution)/shard_map/ppermute | solution.py:27
  49.7 3.8 %collective-permute-start.15 = (bf16[256,1024]{1,0:T(8,128)(2,1)S(1)}, bf16[256,1024]{1,0:T(8,128)(2,1)S(1)}, u32[]{:S(2)}, u32[]{:S(2)}) collective-permute-start(bf16[256,1024]{1,0:T(8,128)(2,1)S(1)} %collective-permute-done.14.refs_5_), channel_id=1, source_target_pairs={{0,1},{1,0},{2,3},{3,2},{4,5},{5,4},{6,7},{7,6},{8,9},{9,8},{10,11... | collective-permute-start | bytes 1572872 | tf_op jit(solution)/shard_map/ppermute | solution.py:27
  49.7 16.1 %collective-permute-start.18 = (bf16[256,1024]{1,0:T(8,128)(2,1)S(1)}, bf16[256,1024]{1,0:T(8,128)(2,1)S(1)}, u32[]{:S(2)}, u32[]{:S(2)}) collective-permute-start(bf16[256,1024]{1,0:T(8,128)(2,1)S(1)} %collective-permute-done.14.refs_5_), channel_id=1, source_target_pairs={{0,4},{1,5},{2,6},{3,7},{4,8},{5,9},{6,10},{7,11},{8,12},{9,13},{1... | collective-permute-start | bytes 1572872 | tf_op jit(solution)/shard_map/ppermute | solution.py:27
  49.7 2.4 %collective-permute-start.20 = (bf16[64,2560]{1,0:T(8,128)(2,1)S(1)}, bf16[64,2560]{1,0:T(8,128)(2,1)S(1)}, u32[]{:S(2)}, u32[]{:S(2)}) collective-permute-start(bf16[64,2560]{1,0:T(8,128)(2,1)S(1)} %get-tuple-element.70), channel_id=1, source_target_pairs={{0,1},{1,0},{2,3},{3,2},{4,5},{5,4},{6,7},{7,6},{8,9},{9,8},{10,11... | collective-permute-start | bytes 983048 | tf_op jit(solution)/shard_map/ppermute | solution.py:27
  50.3 3.1 %collective-permute-start.19 = (bf16[64,2560]{1,0:T(8,128)(2,1)S(1)}, bf16[64,2560]{1,0:T(8,128)(2,1)S(1)}, u32[]{:S(2)}, u32[]{:S(2)}) collective-permute-start(bf16[64,2560]{1,0:T(8,128)(2,1)S(1)} %get-tuple-element.68), channel_id=1, source_target_pairs={{0,1},{1,0},{2,3},{3,2},{4,5},{5,4},{6,7},{7,6},{8,9},{9,8},{10,11... | collective-permute-start | bytes 983048 | tf_op jit(solution)/shard_map/ppermute | solution.py:27
  50.4 7.4 %collective-permute-start.12 = (bf16[176,512]{1,0:T(8,128)(2,1)S(1)}, bf16[176,512]{1,0:T(8,128)(2,1)S(1)}, u32[]{:S(2)}, u32[]{:S(2)}) collective-permute-start(bf16[176,512]{1,0:T(8,128)(2,1)S(1)} %get-tuple-element.61), channel_id=1, source_target_pairs={{0,2},{1,3},{2,0},{3,1},{4,6},{5,7},{6,4},{7,5},{8,10},{9,11},{10,... | collective-permute-start | bytes 540680 | tf_op jit(solution)/shard_map/ppermute | solution.py:27
  52.1 8.8 %collective-permute-start.13 = (bf16[176,512]{1,0:T(8,128)(2,1)S(1)}, bf16[176,512]{1,0:T(8,128)(2,1)S(1)}, u32[]{:S(2)}, u32[]{:S(2)}) collective-permute-start(bf16[176,512]{1,0:T(8,128)(2,1)S(1)} %get-tuple-element.62), channel_id=1, source_target_pairs={{0,18},{1,19},{2,16},{3,17},{4,22},{5,23},{6,20},{7,21},{8,26},{9,... | collective-permute-start | bytes 540680 | tf_op jit(solution)/shard_map/ppermute | solution.py:27
  65.8 1.9 %collective-permute-start.21 = (bf16[256,1024]{1,0:T(8,128)(2,1)S(1)}, bf16[256,1024]{1,0:T(8,128)(2,1)S(1)}, u32[]{:S(2)}, u32[]{:S(2)}) collective-permute-start(bf16[256,1024]{1,0:T(8,128)(2,1)S(1)} %collective-permute-done.18.refs_5_), channel_id=1, source_target_pairs={{0,1},{1,0},{2,3},{3,2},{4,5},{5,4},{6,7},{7,6},{8,9},{9,8},{10,11... | collective-permute-start | bytes 1572872 | tf_op jit(solution)/shard_map/ppermute | solution.py:27
  65.8 7.3 %collective-permute-start.16 = (bf16[176,512]{1,0:T(8,128)(2,1)S(1)}, bf16[176,512]{1,0:T(8,128)(2,1)S(1)}, u32[]{:S(2)}, u32[]{:S(2)}) collective-permute-start(bf16[176,512]{1,0:T(8,128)(2,1)S(1)} %get-tuple-element.64), channel_id=1, source_target_pairs={{0,2},{1,3},{2,0},{3,1},{4,6},{5,7},{6,4},{7,5},{8,10},{9,11},{10,... | collective-permute-start | bytes 540680 | tf_op jit(solution)/shard_map/ppermute | solution.py:27
  67.3 9.1 %collective-permute-start.17 = (bf16[176,512]{1,0:T(8,128)(2,1)S(1)}, bf16[176,512]{1,0:T(8,128)(2,1)S(1)}, u32[]{:S(2)}, u32[]{:S(2)}) collective-permute-start(bf16[176,512]{1,0:T(8,128)(2,1)S(1)} %get-tuple-element.65), channel_id=1, source_target_pairs={{0,18},{1,19},{2,16},{3,17},{4,22},{5,23},{6,20},{7,21},{8,26},{9,... | collective-permute-start | bytes 540680 | tf_op jit(solution)/shard_map/ppermute | solution.py:27
  67.6 12.0 %collective-permute-start.26 = (bf16[16,5120]{1,0:T(8,128)(2,1)S(1)}, bf16[16,5120]{1,0:T(8,128)(2,1)S(1)}, u32[]{:S(2)}, u32[]{:S(2)}) collective-permute-start(bf16[16,5120]{1,0:T(8,128)(2,1)S(1)} %get-tuple-element.82), channel_id=1, source_target_pairs={{0,12},{1,13},{2,14},{3,15},{4,8},{5,9},{6,10},{7,11},{8,4},{9,5},... | collective-permute-start | bytes 491528 | tf_op jit(solution)/shard_map/ppermute | solution.py:27
  67.6 14.5 %collective-permute-start.25 = (bf16[16,5120]{1,0:T(8,128)(2,1)S(1)}, bf16[16,5120]{1,0:T(8,128)(2,1)S(1)}, u32[]{:S(2)}, u32[]{:S(2)}) collective-permute-start(bf16[16,5120]{1,0:T(8,128)(2,1)S(1)} %get-tuple-element.80), channel_id=1, source_target_pairs={{0,8},{1,9},{2,10},{3,11},{4,12},{5,13},{6,14},{7,15},{8,0},{9,1},... | collective-permute-start | bytes 491528 | tf_op jit(solution)/shard_map/ppermute | solution.py:27
  67.7 14.4 %collective-permute-start.24 = (bf16[16,5120]{1,0:T(8,128)(2,1)S(1)}, bf16[16,5120]{1,0:T(8,128)(2,1)S(1)}, u32[]{:S(2)}, u32[]{:S(2)}) collective-permute-start(bf16[16,5120]{1,0:T(8,128)(2,1)S(1)} %get-tuple-element.78), channel_id=1, source_target_pairs={{0,4},{1,5},{2,6},{3,7},{4,0},{5,1},{6,2},{7,3},{8,12},{9,13},{10,... | collective-permute-start | bytes 491528 | tf_op jit(solution)/shard_map/ppermute | solution.py:27
  76.4 8.4 %collective-permute-start.23 = (bf16[176,512]{1,0:T(8,128)(2,1)S(1)}, bf16[176,512]{1,0:T(8,128)(2,1)S(1)}, u32[]{:S(2)}, u32[]{:S(2)}) collective-permute-start(bf16[176,512]{1,0:T(8,128)(2,1)S(1)} %get-tuple-element.76), channel_id=1, source_target_pairs={{0,18},{1,19},{2,16},{3,17},{4,22},{5,23},{6,20},{7,21},{8,26},{9,... | collective-permute-start | bytes 540680 | tf_op jit(solution)/shard_map/ppermute | solution.py:27
  79.0 8.6 %collective-permute-start.22 = (bf16[176,512]{1,0:T(8,128)(2,1)S(1)}, bf16[176,512]{1,0:T(8,128)(2,1)S(1)}, u32[]{:S(2)}, u32[]{:S(2)}) collective-permute-start(bf16[176,512]{1,0:T(8,128)(2,1)S(1)} %get-tuple-element.74), channel_id=1, source_target_pairs={{0,2},{1,3},{2,0},{3,1},{4,6},{5,7},{6,4},{7,5},{8,10},{9,11},{10,... | collective-permute-start | bytes 540680 | tf_op jit(solution)/shard_map/ppermute | solution.py:27
  82.3 1.5 %collective-permute-start.27 = (bf16[16,5120]{1,0:T(8,128)(2,1)S(1)}, bf16[16,5120]{1,0:T(8,128)(2,1)S(1)}, u32[]{:S(2)}, u32[]{:S(2)}) collective-permute-start(bf16[16,5120]{1,0:T(8,128)(2,1)S(1)} %shard_map.104.refs_0_), channel_id=1, source_target_pairs={{0,1},{1,0},{2,3},{3,2},{4,5},{5,4},{6,7},{7,6},{8,9},{9,8},{10,11... | collective-permute-start | bytes 491528 | tf_op jit(solution)/shard_map/ppermute | solution.py:27
  (3 other events, 2.2 us)

commit v11 on v10

--- a/solution.py
+++ b/solution.py
@@ -37,6 +37,18 @@
 
 def columns_by_columns(a, b):
     return lax.dot_general(a, b, (((0,), (0,)), ((), ())), preferred_element_type=F32)
+
+
+def inner(z):
+    return (z == 1) | (z == 2)
+
+
+def shard_of(k, here, holders):
+    if holders != 4:
+        return lax.rem(here + holders - k, holders)
+    if k < 2:
+        return here ^ k
+    return here ^ jnp.where(inner(here), 5 - k, k)
 
 
 def call(kernel, out_shape, operands, scratch=(), scalars=0):
@@ -133,49 +145,86 @@
                 ref[:, to : to + LANES] = sent[:, j : j + LANES]
 
 
-def frozen_kernel(sizes, k, count, *refs):
+def ranks_kept(sizes, g_ref, names, map_refs, wide):
+    holders, replicas, slots, rank = sizes
+    kept = []
+    for dr in range(replicas):
+        keep = names == row_slots(holders, replicas, slots, rank, dr)
+        proj_grad = rows_by_rows(g_ref[...], map_refs[dr][:, wide:-SPARE])
+        kept.append(jnp.where(keep, proj_grad, 0.0).astype(BF16))
+    return jnp.concatenate(kept, axis=1)
+
+
+def frozen_kernel(sizes, k, spec, guests, *refs):
     tokens, groups, holders, replicas, slots, rank = sizes
     g_refs, refs = refs[:groups], refs[groups:]
     map_refs, refs = refs[:replicas], refs[replicas:]
     core, here = lax.axis_index("replica"), lax.axis_index("adapter")
     rows = map_refs[0].shape[0]
-    wide = map_refs[0].shape[1] - g_refs[0].shape[1] - SPARE
+    value_width = g_refs[0].shape[1]
+    wide = map_refs[0].shape[1] - value_width - SPARE
     half = wide // holders
+    ranks = (holders, replicas, slots, rank)
     if k == 0:
-        named_refs, refs = refs[:groups], refs[groups:]
-        sel_ref = refs[-1]
-        out_refs = refs[-1 - groups : -1]
+        named_refs, refs, sel_ref = refs[:groups], refs[groups:-1], refs[-1]
         for dg in range(groups):
             names = named_refs[dg][...].astype(F32)[:, :1]
-            for dr in range(replicas):
-                keep = names == row_slots(holders, replicas, slots, rank, dr)
-                proj_grad = rows_by_rows(g_refs[dg][...], map_refs[dr][:, wide:-SPARE])
-                sel_ref[pl.ds(dg * tokens, tokens), dr * rows : (dr + 1) * rows] = jnp.where(
-                    keep, proj_grad, 0.0
-                ).astype(BF16)
+            sel_ref[pl.ds(dg * tokens, tokens), :] = ranks_kept(
+                ranks, g_refs[dg], names, map_refs, wide
+            )
     else:
         sel_ref, refs = refs[0], refs[1:]
-        out_refs = refs[-groups:]
-    shard_at = lax.rem(here + holders - k, holders) * half
-    for j, block in enumerate(refs[:count]):
+    sets = [(g_refs[dg], sel_ref[pl.ds(dg * tokens, tokens), :]) for dg in range(groups)]
+    if guests:
+        guest_ref, refs = refs[0], refs[1:]
+        for dg in range(groups):
+            at = pl.ds(dg * tokens, tokens)
+            names = guest_ref[at, value_width:].astype(F32)[:, :1]
+            g_ref = guest_ref.at[at, pl.ds(0, value_width)]
+            sets.append((g_ref, ranks_kept(ranks, g_ref, names, map_refs, wide)))
+    out_refs = list(refs[len(spec) : len(spec) + groups])
+    if guests:
+        out_refs += [refs[-1].at[pl.ds(dg * tokens, tokens)] for dg in range(groups)]
+    shard_at = shard_of(k, here, holders) * half
+    for (dr, offset), block in zip(spec, refs):
         if k == 0:
             block = block.at[pl.ds(pl.multiple_of(lax.axis_index("groups") * half, half), half)]
-        wide = block.shape[0]
-        at = 0 if count == 1 else lax.rem(core + replicas - j, replicas) * wide
-        columns = pl.ds(pl.multiple_of(shard_at + at, wide), wide)
-        for dg in range(groups):
-            base = rows_by_rows(g_refs[dg][...], block[...]).astype(BF16)
+        size = block.shape[0]
+        at = 0
+        if size < half:
+            at = lax.rem(core + replicas - dr, replicas) * (half // replicas) + offset
+        columns = pl.ds(pl.multiple_of(shard_at + at, size), size)
+        for (g_ref, sel), out_ref in zip(sets, out_refs):
+            base = rows_by_rows(g_ref[...], block[...]).astype(BF16)
             lora = 0.0
-            for dr in range(replicas):
+            for j in range(replicas):
                 lora = lora + jnp.dot(
-                    sel_ref[pl.ds(dg * tokens, tokens), dr * rows : (dr + 1) * rows],
-                    map_refs[dr][:, columns],
+                    sel[:, j * rows : (j + 1) * rows],
+                    map_refs[j][:, columns],
                     preferred_element_type=F32,
                 )
             lora = (ADAPTER_SCALE * lora).astype(BF16)
-            out_refs[dg][:, pl.ds(at if count == 1 else pl.multiple_of(at, wide), wide)] = (
+            out_ref[:, pl.ds(pl.multiple_of(at, size) if size < half else 0, size)] = (
                 base.astype(F32) + lora.astype(F32)
             ).astype(BF16)
+
+
+def guest_kernel(groups, *refs):
+    out_ref = refs[-1]
+    tokens, value_width = refs[0].shape
+    for dg in range(groups):
+        at = pl.ds(dg * tokens, tokens)
+        out_ref[at, :value_width] = refs[dg][...]
+        out_ref[at, value_width:] = refs[groups + dg][:, :LANES]
+
+
+def pick_kernel(here_ref, there_ref, out_ref):
+    def put(ref):
+        out_ref[...] = ref[...]
+
+    at_inner = inner(lax.axis_index("adapter"))
+    pl.when(at_inner)(lambda: put(here_ref))
+    pl.when(jnp.logical_not(at_inner))(lambda: put(there_ref))
 
 
 def place_kernel(sizes, *refs):
@@ -185,21 +234,29 @@
     for k in range(holders):
         for dg in range(groups):
             source = lax.rem(group + groups - dg, groups)
-            at = lax.rem(here + holders - k, holders) * shard + source * half
+            at = shard_of(k, here, holders) * shard + source * half
             out_ref[:, pl.ds(pl.multiple_of(at, half), half)] = refs[k * groups + dg][...]
 
 
 def chip_kernel(replicas, *refs):
     own_ref, came_refs, out_refs = refs[0], refs[1 : 2 * replicas - 1], refs[2 * replicas - 1 :]
-    rows = out_refs[0].shape[0]
     split = came_refs[0].shape[1]
-    for k, out in enumerate(out_refs):
+    start = 0
+    for out in out_refs:
+        rows = out.shape[0]
         for j in range(2):
-            at = pl.ds(k * rows, rows), pl.ds(j * split, split)
+            at = pl.ds(start, rows), pl.ds(j * split, split)
             total = own_ref[at]
             for ref in came_refs[j::2]:
-                total = total + ref[pl.ds(k * rows, rows), :].astype(F32)
+                total = total + ref[pl.ds(start, rows), :].astype(F32)
             out[:, pl.ds(j * split, split)] = total.astype(out.dtype)
+        start += rows
+
+
+def fold_kernel(own_ref, came_ref, keep_ref, send_ref):
+    rows = keep_ref.shape[0]
+    keep_ref[...] = own_ref[:rows] + came_ref[:rows].astype(F32)
+    send_ref[...] = (own_ref[rows:] + came_ref[rows:].astype(F32)).astype(BF16)
 
 
 def total_kernel(*refs):
@@ -266,7 +323,6 @@
         held.append(moved(own, lambda g, z, s, r: (g, z ^ k, s, r)))
 
     ring = [lax.dynamic_slice_in_dim(frozen, (group * replicas + core) * piece, piece, axis=0)]
-    ring.append(moved(ring[0], lambda g, z, s, r: (g, z + 1, s, r)))
     held, grads, named = lax.optimization_barrier((held, grads, named))
     both, downs = call(
         join_kernel,
@@ -280,20 +336,34 @@
         moved(both, lambda g, z, s, r: (g, z, s, r + dr)) for dr in range(1, replicas)
     ]
     others = [moved(downs, lambda g, z, s, r: (g + dg, z, s, r)) for dg in range(1, groups)]
+    line = holders == 4
+    swap = lambda g, z, s, r: (g, 3 - z, s, r) if inner(z) else None
+    outward = lambda g, z, s, r: (g, z ^ 1, s, r) if inner(z) else None
+    inward = lambda g, z, s, r: None if inner(z) else (g, z ^ 1, s, r)
+    onward = lambda g, z, s, r: (g, z + 1, s, r)
+    first = after(ring[0], both[0])
+    if line:
+        near = moved(first, lambda g, z, s, r: (g, z ^ 1, s, r))
+        across = moved(first, swap)
+        ring.append(near)
+    else:
+        ring.append(moved(first, onward))
+
     def pieces_of(k, *before):
         if k == 0:
-            return [frozen]
+            return [(0, 0)], [frozen]
         block = after(ring[k], *before) if before else ring[k]
         pieces = [block] + [
             moved(block, lambda g, z, s, r: (g, z, s, r + dr)) for dr in range(1, replicas)
         ]
+        spec = [(dr, 0) for dr in range(replicas)]
         if piece % LANES:
             whole = jnp.zeros((half, value_width), BF16)
-            for dr in range(replicas):
-                at = ((core - dr) % replicas) * piece
-                whole = lax.dynamic_update_slice_in_dim(whole, pieces[dr], at, axis=0)
-            pieces = [whole]
-        return pieces
+            for (dr, offset), part in zip(spec, pieces):
+                at = ((core - dr) % replicas) * piece + offset
+                whole = lax.dynamic_update_slice_in_dim(whole, part, at, axis=0)
+            spec, pieces = [(0, 0)], [whole]
+        return spec, pieces
 
     kept = replicas * holders * rows
 
@@ -318,32 +388,54 @@
         ]
         chip = call(
             functools.partial(chip_kernel, replicas),
-            [jax.ShapeDtypeStruct((rows, cols), F32)]
-            + [jax.ShapeDtypeStruct((rows, cols), BF16)] * (holders - 1),
+            [
+                jax.ShapeDtypeStruct((holders // 2 * rows, cols), F32),
+                jax.ShapeDtypeStruct((holders // 2 * rows, cols), BF16),
+            ],
             (part, *came),
         )
         return part, chip
 
     arrived, outs, sel = [], [], None
     for k in range(holders):
-        if k > 1:
+        if line and k == 2:
+            near, across = lax.optimization_barrier((near, across, part, *arrived[0]))[:2]
+            last = moved(near, swap)
+            guests = call(
+                functools.partial(guest_kernel, groups),
+                [jax.ShapeDtypeStruct((groups * tokens, value_width + LANES), BF16)],
+                (*grads, *named),
+            )[0]
+            guests = moved(after(guests, near), inward)
+            passed_on = moved(across, outward)
+            last, passed_on, guests = lax.optimization_barrier(
+                (last, passed_on, guests, *arrived[1], chip[0])
+            )[:3]
+            shape = jax.ShapeDtypeStruct(passed_on.shape, BF16)
+            ring += [call(pick_kernel, [shape], (across, passed_on))[0], last]
+        elif k > 1 and not line:
             last = after(ring[-1], *outs[k - 2], part) if k > 2 else after(ring[-1], sel)
-            ring.append(moved(last, lambda g, z, s, r: (g, z + 1, s, r)))
-        gate = outs[k - 1] if k > 1 else [sel] * k
-        blocks = pieces_of(k, *gate, *([*arrived[k - 2], chip[0]] if k > 2 else ()))
-        tokens_in = [after(grad_rows, part), *grads[1:]] if k == 1 else grads
+            last = moved(last, onward)
+            ring.append(last)
+        gate = [] if k == 0 else arrived[0] if k == 1 else outs[k - 1] if k == 2 or not line else []
+        spec, blocks = pieces_of(k, *gate, *([*arrived[k - 2], chip[0]] if k > 2 and not line else ()))
+        hosts = line and k == 3
         out = call(
             functools.partial(
-                frozen_kernel, (tokens, groups, holders, replicas, slots, rank), k, len(blocks)
+                frozen_kernel, (tokens, groups, holders, replicas, slots, rank), k, spec, hosts
             ),
             [jax.ShapeDtypeStruct((tokens, half), BF16)] * groups
-            + [jax.ShapeDtypeStruct((groups * tokens, kept), BF16)] * (k == 0),
-            [*tokens_in, *both, *([sel] if k else named), *blocks],
+            + [jax.ShapeDtypeStruct((groups * tokens, kept), BF16)] * (k == 0)
+            + [jax.ShapeDtypeStruct((groups * tokens, half), BF16)] * hosts,
+            [*grads, *both, *([sel] if k else named), *([guests] if hosts else []), *blocks],
         )
         if k == 0:
             sel = out[groups]
         outs.append(list(out[:groups]))
         mails = outs[-1]
+        if hosts:
+            back = moved(out[groups], outward).reshape(groups, tokens, half)
+            mails = [jnp.where(inner(here), mails[dg], back[dg]) for dg in range(groups)]
         if k > 2:
             mails = [after(mail, *arrived[-1]) for mail in mails]
         arrived.append(
@@ -357,11 +449,20 @@
         [x for got in arrived for x in got],
     )[0]
 
-    sums = [chip[0]] + [
-        moved(after(chip[k], ring[-1]), lambda g, z, s, r: (g, z ^ k, s, r))
-        for k in range(1, holders)
-    ]
-    total = call(total_kernel, [jax.ShapeDtypeStruct((rows, cols), BF16)], sums)[0]
+    keep, send, by = chip[0], after(chip[1], last), holders // 2
+    while by > 1:
+        came = moved(send, lambda g, z, s, r: (g, z ^ by, s, r))
+        by //= 2
+        keep, send = call(
+            fold_kernel,
+            [
+                jax.ShapeDtypeStruct((by * rows, cols), F32),
+                jax.ShapeDtypeStruct((by * rows, cols), BF16),
+            ],
+            (keep, came),
+        )
+    came = moved(after(send, *arrived[-2]), lambda g, z, s, r: (g, z ^ 1, s, r))
+    total = call(total_kernel, [jax.ShapeDtypeStruct((rows, cols), BF16)], (keep, came))[0]
     totals = [total] + [
         moved(total, lambda g, z, s, r: (g, z, s, r + dr)) for dr in range(1, replicas)
     ]

time: 89.1 us -> 99.4 us (1.12)
  starting transfers between devices: 25.2 us -> 35.5 us
  waiting for transfers between devices: 48.2 us -> 45.1 us
  Pallas kernels: 8.81 us -> 10.6 us
  other arithmetic: 0 us -> 1.05 us
    ppermute x28 -> x30, starting transfers between devices: 25.2 us -> 35.5 us  [moved(): return lax.ppermute(x, AXES, pairs)]
    ppermute x28 -> x30, waiting for transfers between devices: 48.2 us -> 45.1 us  [moved(): return lax.ppermute(x, AXES, pairs)]
    pallas_call x12 -> x15, Pallas kernels: 8.81 us -> 10.6 us  [call(): pl.pallas_call(kernel, out_shape=out_shape, in_specs=[pl.BlockSpec(memory...]
    select_n x0 -> x1, other arithmetic: none -> 1.05 us  [on_device(): jnp.where(inner(here), mails[dg], back[dg])]
  transfers between devices with their start and end apart: 28 -> 30, of which waited for: 15 -> 15; matrix products, arithmetic and copies ran while one was open for 1% -> 2% of each run, Pallas kernels for 9% -> 9%
where the time goes in v11:
time: 99.4 us; the launch traced here: 99.1 us
  waiting for transfers between devices  45.1 us (45%)
  starting transfers between devices  35.5 us (36%)
  Pallas kernels  10.6 us (11%)
  local copies, waits for them, and re-layouts  5.8 us (6%)
  other arithmetic  1.05 us (1%)
    ppermute x30, waiting for transfers between devices, moved(): return lax.ppermute(x, AXES, pairs)  45.1 us
    ppermute x30, starting transfers between devices, moved(): return lax.ppermute(x, AXES, pairs)  35.5 us
    pallas_call x15, Pallas kernels, call(): pl.pallas_call(kernel, out_shape=out_shape, in_specs=[pl.BlockSpec(memory...  10.6 us
    unnamed x14, local copies, waits for them, and re-layouts  4.72 us
  transfers between devices with their start and end apart: 30, of which 15 were waited for; matrix products, arithmetic and copies ran while one was open for 2% of the time, Pallas kernels for 9%

profile of v11, /device:TPU:0, one launch (start us, length us, event | category | flops | bytes accessed | tf_op | source)
XLA Modules:
  0.0 99.1 jit_solution(3312439126270616251)
XLA Ops:
  0.6 3.0 %collective-permute-start.3 = (bf16[176,1024]{1,0:T(8,128)(2,1)}, bf16[176,1024]{1,0:T(8,128)(2,1)S(1)}, u32[]{:S(2)}, u32[]{:S(2)}) collective-permute-start(bf16[176,1024]{1,0:T(8,128)(2,1)} %bitcast.11), channel_id=1, source_target_pairs={{0,16},{1,17},{2,18},{3,19},{4,20},{5,21},{6,22},{7,23},{8,24},{9,... | collective-permute-start | bytes 1081352 | tf_op jit(solution)/shard_map/ppermute | solution.py:27
  7.7 2.1 %collective-permute-start = (bf16[16,3072]{1,0:T(8,128)(2,1)S(1)}, bf16[16,3072]{1,0:T(8,128)(2,1)S(1)}, u32[]{:S(2)}, u32[]{:S(2)}) collective-permute-start(bf16[16,3072]{1,0:T(8,128)(2,1)S(1)} %shard_map.94.refs_0_), channel_id=1, source_target_pairs={{0,4},{1,5},{2,6},{3,7},{4,0},{5,1},{6,2},{7,3},{8,12},{9,13},{10,... | collective-permute-start | bytes 294920 | tf_op jit(solution)/shard_map/ppermute | solution.py:27
  9.8 2.6 %collective-permute-start.1 = (bf16[16,3072]{1,0:T(8,128)(2,1)S(1)}, bf16[16,3072]{1,0:T(8,128)(2,1)S(1)}, u32[]{:S(2)}, u32[]{:S(2)}) collective-permute-start(bf16[16,3072]{1,0:T(8,128)(2,1)S(1)} %shard_map.94.refs_0_), channel_id=1, source_target_pairs={{0,8},{1,9},{2,10},{3,11},{4,12},{5,13},{6,14},{7,15},{8,0},{9,1},... | collective-permute-start | bytes 294920 | tf_op jit(solution)/shard_map/ppermute | solution.py:27
  13.4 6.3 %collective-permute-done.1.refs_2_ = bf16[16,3072]{1,0:T(8,128)(2,1)S(1)} collective-permute-done((bf16[16,3072]{1,0:T(8,128)(2,1)S(1)}, bf16[16,3072]{1,0:T(8,128)(2,1)S(1)}, u32[]{:S(2)}, u32[]{:S(2)}) %collective-permute-start.1) | collective-permute-done | bytes 98336 | tf_op jit(solution)/shard_map/ppermute | solution.py:27
  20.9 1.7 %collective-permute-start.8 = (bf16[256,1024]{1,0:T(8,128)(2,1)S(1)}, bf16[256,1024]{1,0:T(8,128)(2,1)S(1)}, u32[]{:S(2)}, u32[]{:S(2)}) collective-permute-start(bf16[256,1024]{1,0:T(8,128)(2,1)S(1)} %dynamic-slice_bitcast_fusion), channel_id=1, source_target_pairs={{0,4},{1,5},{2,6},{3,7},{4,0},{5,1},{6,2},{7,3},{8,12},{9,13},{10,... | collective-permute-start | bytes 1572872 | tf_op jit(solution)/shard_map/ppermute | solution.py:27
  22.6 1.5 %collective-permute-start.13 = (bf16[64,2048]{1,0:T(8,128)(2,1)S(1)}, bf16[64,2048]{1,0:T(8,128)(2,1)S(1)}, u32[]{:S(2)}, u32[]{:S(2)}) collective-permute-start(bf16[64,2048]{1,0:T(8,128)(2,1)S(1)} %get-tuple-element.64), channel_id=1, source_target_pairs={{0,16},{1,17},{2,18},{3,19},{4,20},{5,21},{6,22},{7,23},{8,24},{9,... | collective-permute-start | bytes 786440 | tf_op jit(solution)/shard_map/ppermute | solution.py:27
  24.8 1.6 %copy-done.1 = bf16[1,1024,1024]{2,1,0:T(8,128)(2,1)S(1)} copy-done((bf16[1,1024,1024]{2,1,0:T(8,128)(2,1)S(1)}, bf16[1,1024,1024]{2,1,0:T(8,128)(2,1)}, u32[]{:S(2)}) %copy-start.1) | copy-done | bytes 2097176
  26.4 1.5 %shard_map.97 = (bf16[176,512]{1,0:T(8,128)(2,1)S(1)}, bf16[176,512]{1,0:T(8,128)(2,1)S(1)}, bf16[352,128]{1,0:T(8,128)(2,1)S(1)}) custom-call(bf16[176,1024]{1,0:T(8,128)(2,1)S(1)} %bitcast.12, bf16[176,1024]{1,0:T(8,128)(2,1)S(1)} %collective-permute-done.3.refs_1_, bf16[64,3328]{1,0:T(8,128)(2,1)S(1)} %get-tuple-element.54.refs_2_.refs_4_, ...), custom_call_target="tpu_custom_call" | custom-call | flops 1000 | bytes 1000 | tf_op jit(solution)/shard_map/pallas_call | solution.py:56
  27.9 1.6 %collective-permute-start.6 = (bf16[176,512]{1,0:T(8,128)(2,1)S(1)}, bf16[176,512]{1,0:T(8,128)(2,1)S(1)}, u32[]{:S(2)}, u32[]{:S(2)}) collective-permute-start(bf16[176,512]{1,0:T(8,128)(2,1)S(1)} %get-tuple-element.57), channel_id=1, source_target_pairs={{0,2},{1,3},{2,0},{3,1},{4,6},{5,7},{6,4},{7,5},{8,10},{9,11},{10,... | collective-permute-start | bytes 540680 | tf_op jit(solution)/shard_map/ppermute | solution.py:27
  31.0 4.3 %collective-permute-done.8.refs_5_ = bf16[256,1024]{1,0:T(8,128)(2,1)S(1)} collective-permute-done((bf16[256,1024]{1,0:T(8,128)(2,1)S(1)}, bf16[256,1024]{1,0:T(8,128)(2,1)S(1)}, u32[]{:S(2)}, u32[]{:S(2)}) %collective-permute-start.8) | collective-permute-done | bytes 524320 | tf_op jit(solution)/shard_map/ppermute | solution.py:27
  35.4 2.8 %collective-permute-done.7.refs_1_ = bf16[176,512]{1,0:T(8,128)(2,1)S(1)} collective-permute-done((bf16[176,512]{1,0:T(8,128)(2,1)S(1)}, bf16[176,512]{1,0:T(8,128)(2,1)S(1)}, u32[]{:S(2)}, u32[]{:S(2)}) %collective-permute-start.7) | collective-permute-done | bytes 180256 | tf_op jit(solution)/shard_map/ppermute | solution.py:27
  38.2 1.3 %shard_map.99 = (f32[64,5120]{1,0:T(8,128)S(1)}, bf16[64,2560]{1,0:T(8,128)(2,1)S(1)}, bf16[64,2560]{1,0:T(8,128)(2,1)S(1)}) custom-call(bf16[176,4096]{1,0:T(8,128)(2,1)S(1)} %bitcast.19, bf16[176,1024]{1,0:T(8,128)(2,1)S(1)} %bitcast.14, bf16[176,384]{1,0:T(8,128)(2,1)S(1)} %shard_map.95.refs_4_.refs_2_, ...), custom_call_target="tpu_custom_call" | custom-call | flops 1000 | bytes 1000 | tf_op jit(solution)/shard_map/pallas_call | solution.py:56
  39.6 4.9 %collective-permute-start.17 = (bf16[352,1152]{1,0:T(8,128)(2,1)S(1)}, bf16[352,1152]{1,0:T(8,128)(2,1)S(1)}, u32[]{:S(2)}, u32[]{:S(2)}) collective-permute-start(bf16[352,1152]{1,0:T(8,128)(2,1)S(1)} %shard_map.100), channel_id=1, source_target_pairs={{0,4},{1,5},{2,6},{3,7},{12,8},{13,9},{14,10},{15,11},{16,20},{17,... | collective-permute-start | bytes 2433032 | tf_op jit(solution)/shard_map/ppermute | solution.py:27
  45.1 1.3 %collective-permute-start.16 = (bf16[256,1024]{1,0:T(8,128)(2,1)S(1)}, bf16[256,1024]{1,0:T(8,128)(2,1)S(1)}, u32[]{:S(2)}, u32[]{:S(2)}) collective-permute-start(bf16[256,1024]{1,0:T(8,128)(2,1)S(1)} %collective-permute-done.12.here_ref), channel_id=1, source_target_pairs={{4,0},{5,1},{6,2},{7,3},{8,12},{9,13},{10,14},{11,15},{20,16},{21,... | collective-permute-start | bytes 1572872 | tf_op jit(solution)/shard_map/ppermute | solution.py:27
  48.1 1.5 %collective-permute-start.10 = (bf16[176,512]{1,0:T(8,128)(2,1)S(1)}, bf16[176,512]{1,0:T(8,128)(2,1)S(1)}, u32[]{:S(2)}, u32[]{:S(2)}) collective-permute-start(bf16[176,512]{1,0:T(8,128)(2,1)S(1)} %get-tuple-element.62), channel_id=1, source_target_pairs={{0,2},{1,3},{2,0},{3,1},{4,6},{5,7},{6,4},{7,5},{8,10},{9,11},{10,... | collective-permute-start | bytes 540680 | tf_op jit(solution)/shard_map/ppermute | solution.py:27
  49.6 1.5 %collective-permute-start.11 = (bf16[176,512]{1,0:T(8,128)(2,1)S(1)}, bf16[176,512]{1,0:T(8,128)(2,1)S(1)}, u32[]{:S(2)}, u32[]{:S(2)}) collective-permute-start(bf16[176,512]{1,0:T(8,128)(2,1)S(1)} %get-tuple-element.63), channel_id=1, source_target_pairs={{0,18},{1,19},{2,16},{3,17},{4,22},{5,23},{6,20},{7,21},{8,26},{9,... | collective-permute-start | bytes 540680 | tf_op jit(solution)/shard_map/ppermute | solution.py:27
  51.3 9.8 %collective-permute-done.16.there_ref = bf16[256,1024]{1,0:T(8,128)(2,1)S(1)} collective-permute-done((bf16[256,1024]{1,0:T(8,128)(2,1)S(1)}, bf16[256,1024]{1,0:T(8,128)(2,1)S(1)}, u32[]{:S(2)}, u32[]{:S(2)}) %collective-permute-start.16) | collective-permute-done | bytes 524320 | tf_op jit(solution)/shard_map/ppermute | solution.py:27
  61.1 1.3 %collective-permute-done.17.refs_5_ = bf16[352,1152]{1,0:T(8,128)(2,1)S(1)} collective-permute-done((bf16[352,1152]{1,0:T(8,128)(2,1)S(1)}, bf16[352,1152]{1,0:T(8,128)(2,1)S(1)}, u32[]{:S(2)}, u32[]{:S(2)}) %collective-permute-start.17) | collective-permute-done | bytes 811040 | tf_op jit(solution)/shard_map/ppermute | solution.py:27
  63.0 1.3 %collective-permute-done.23.refs_7_ = bf16[256,1024]{1,0:T(8,128)(2,1)S(1)} collective-permute-done((bf16[256,1024]{1,0:T(8,128)(2,1)S(1)}, bf16[256,1024]{1,0:T(8,128)(2,1)S(1)}, u32[]{:S(2)}, u32[]{:S(2)}) %collective-permute-start.23) | collective-permute-done | bytes 524320 | tf_op jit(solution)/shard_map/ppermute | solution.py:27
  64.3 2.1 %shard_map.104 = (bf16[176,512]{1,0:T(8,128)(2,1)S(1)}, bf16[176,512]{1,0:T(8,128)(2,1)S(1)}, bf16[352,512]{1,0:T(8,128)(2,1)S(1)}) custom-call(bf16[176,1024]{1,0:T(8,128)(2,1)S(1)} %bitcast.16, bf16[176,1024]{1,0:T(8,128)(2,1)S(1)} %collective-permute-done.3.refs_1_, bf16[64,3328]{1,0:T(8,128)(2,1)S(1)} %get-tuple-element.54.refs_2_.refs_4_, ...), custom_call_target="tpu_custom_call" | custom-call | flops 1000 | bytes 1000 | tf_op jit(solution)/shard_map/pallas_call | solution.py:56
  66.3 1.3 %collective-permute-start.24 = (bf16[352,512]{1,0:T(8,128)(2,1)S(1)}, bf16[352,512]{1,0:T(8,128)(2,1)}, u32[]{:S(2)}, u32[]{:S(2)}) collective-permute-start(bf16[352,512]{1,0:T(8,128)(2,1)S(1)} %get-tuple-element.82), channel_id=1, source_target_pairs={{4,0},{5,1},{6,2},{7,3},{8,12},{9,13},{10,14},{11,15},{20,16},{21,... | collective-permute-start | bytes 1081352 | tf_op jit(solution)/shard_map/ppermute | solution.py:27
  67.6 3.2 %collective-permute-start.27 = (bf16[32,5120]{1,0:T(8,128)(2,1)S(1)}, bf16[32,5120]{1,0:T(8,128)(2,1)S(1)}, u32[]{:S(2)}, u32[]{:S(2)}) collective-permute-start(bf16[32,5120]{1,0:T(8,128)(2,1)S(1)} %get-tuple-element.87), channel_id=1, source_target_pairs={{0,8},{1,9},{2,10},{3,11},{4,12},{5,13},{6,14},{7,15},{8,0},{9,1},... | collective-permute-start | bytes 983048 | tf_op jit(solution)/shard_map/ppermute | solution.py:27
  70.9 1.7 %shard_map.103 = (bf16[176,512]{1,0:T(8,128)(2,1)}, bf16[176,512]{1,0:T(8,128)(2,1)}) custom-call(bf16[176,1024]{1,0:T(8,128)(2,1)S(1)} %bitcast.17, bf16[176,1024]{1,0:T(8,128)(2,1)S(1)} %collective-permute-done.3.refs_1_, bf16[64,3328]{1,0:T(8,128)(2,1)S(1)} %get-tuple-element.54.refs_2_.refs_4_, ...), custom_call_target="tpu_custom_call" | custom-call | flops 1000 | bytes 1000 | tf_op jit(solution)/shard_map/pallas_call | solution.py:56
  72.6 1.5 %collective-permute-start.21 = (bf16[176,512]{1,0:T(8,128)(2,1)}, bf16[176,512]{1,0:T(8,128)(2,1)S(1)}, u32[]{:S(2)}, u32[]{:S(2)}) collective-permute-start(bf16[176,512]{1,0:T(8,128)(2,1)} %get-tuple-element.77), channel_id=1, source_target_pairs={{0,2},{1,3},{2,0},{3,1},{4,6},{5,7},{6,4},{7,5},{8,10},{9,11},{10,... | collective-permute-start | bytes 540680 | tf_op jit(solution)/shard_map/ppermute | solution.py:27
  74.1 1.5 %collective-permute-start.22 = (bf16[176,512]{1,0:T(8,128)(2,1)}, bf16[176,512]{1,0:T(8,128)(2,1)S(1)}, u32[]{:S(2)}, u32[]{:S(2)}) collective-permute-start(bf16[176,512]{1,0:T(8,128)(2,1)} %get-tuple-element.78), channel_id=1, source_target_pairs={{0,18},{1,19},{2,16},{3,17},{4,22},{5,23},{6,20},{7,21},{8,26},{9,... | collective-permute-start | bytes 540680 | tf_op jit(solution)/shard_map/ppermute | solution.py:27
  75.6 10.3 %collective-permute-done.27.came_ref = bf16[32,5120]{1,0:T(8,128)(2,1)S(1)} collective-permute-done((bf16[32,5120]{1,0:T(8,128)(2,1)S(1)}, bf16[32,5120]{1,0:T(8,128)(2,1)S(1)}, u32[]{:S(2)}, u32[]{:S(2)}) %collective-permute-start.27) | collective-permute-done | bytes 327712 | tf_op jit(solution)/shard_map/ppermute | solution.py:27
  87.1 2.5 %collective-permute-start.26 = (bf16[176,512]{1,0:T(8,128)(2,1)S(1)}, bf16[176,512]{1,0:T(8,128)(2,1)S(1)}, u32[]{:S(2)}, u32[]{:S(2)}) collective-permute-start(bf16[176,512]{1,0:T(8,128)(2,1)S(1)} %get-tuple-element.85), channel_id=1, source_target_pairs={{0,18},{1,19},{2,16},{3,17},{4,22},{5,23},{6,20},{7,21},{8,26},{9,... | collective-permute-start | bytes 540680 | tf_op jit(solution)/shard_map/ppermute | solution.py:27
  90.1 1.4 %collective-permute-done.28.refs_1_ = bf16[16,5120]{1,0:T(8,128)(2,1)S(1)} collective-permute-done((bf16[16,5120]{1,0:T(8,128)(2,1)S(1)}, bf16[16,5120]{1,0:T(8,128)(2,1)S(1)}, u32[]{:S(2)}, u32[]{:S(2)}) %collective-permute-start.28) | collective-permute-done | bytes 163872 | tf_op jit(solution)/shard_map/ppermute | solution.py:27
  91.6 1.4 %collective-permute-done.29.refs_1_ = bf16[16,5120]{1,0:T(8,128)(2,1)S(1)} collective-permute-done((bf16[16,5120]{1,0:T(8,128)(2,1)S(1)}, bf16[16,5120]{1,0:T(8,128)(2,1)S(1)}, u32[]{:S(2)}, u32[]{:S(2)}) %collective-permute-start.29) | collective-permute-done | bytes 163872 | tf_op jit(solution)/shard_map/ppermute | solution.py:27
  93.8 1.7 %collective-permute-done.26.refs_7_ = bf16[176,512]{1,0:T(8,128)(2,1)S(1)} collective-permute-done((bf16[176,512]{1,0:T(8,128)(2,1)S(1)}, bf16[176,512]{1,0:T(8,128)(2,1)S(1)}, u32[]{:S(2)}, u32[]{:S(2)}) %collective-permute-start.26) | collective-permute-done | bytes 180256 | tf_op jit(solution)/shard_map/ppermute | solution.py:27
  95.5 2.3 %collective-permute-done.25.refs_6_ = bf16[176,512]{1,0:T(8,128)(2,1)S(1)} collective-permute-done((bf16[176,512]{1,0:T(8,128)(2,1)S(1)}, bf16[176,512]{1,0:T(8,128)(2,1)S(1)}, u32[]{:S(2)}, u32[]{:S(2)}) %collective-permute-start.25) | collective-permute-done | bytes 180256 | tf_op jit(solution)/shard_map/ppermute | solution.py:27
  97.8 1.2 %shard_map.105 = bf16[176,4096]{1,0:T(8,128)(2,1)} custom-call(bf16[176,512]{1,0:T(8,128)(2,1)S(1)} %collective-permute-done.6.refs_0_, bf16[176,512]{1,0:T(8,128)(2,1)S(1)} %collective-permute-done.7.refs_1_, bf16[176,512]{1,0:T(8,128)(2,1)S(1)} %collective-permute-done.10.refs_2_, bf16[176,512]{1,0:T(8,128)(2,1)S(1)} %collective-permute-done.11.refs_3_, ...), custom_call_target="tpu_custom_call" | custom-call | flops 1000 | bytes 1000 | tf_op jit(solution)/shard_map/pallas_call | solution.py:56
  (59 shorter events, 14.4 us)
Async XLA Ops:
  0.6 24.2 %copy-start = (bf16[1,176,1024]{2,1,0:T(8,128)(2,1)S(1)}, bf16[1,176,1024]{2,1,0:T(8,128)(2,1)}, u32[]{:S(2)}) copy-start(bf16[1,176,1024]{2,1,0:T(8,128)(2,1)} %param.8) | copy-start | bytes 1081348
  0.6 19.1 %collective-permute-start.3 = (bf16[176,1024]{1,0:T(8,128)(2,1)}, bf16[176,1024]{1,0:T(8,128)(2,1)S(1)}, u32[]{:S(2)}, u32[]{:S(2)}) collective-permute-start(bf16[176,1024]{1,0:T(8,128)(2,1)} %bitcast.11), channel_id=1, source_target_pairs={{0,16},{1,17},{2,18},{3,19},{4,20},{5,21},{6,22},{7,23},{8,24},{9,... | collective-permute-start | bytes 1081352 | tf_op jit(solution)/shard_map/ppermute | solution.py:27
  5.8 13.9 %collective-permute-start.4 = (bf16[176,384]{1,0:T(8,128)(2,1)S(1)}, bf16[176,384]{1,0:T(8,128)(2,1)S(1)}, u32[]{:S(2)}, u32[]{:S(2)}) collective-permute-start(bf16[176,384]{1,0:T(8,128)(2,1)S(1)} %shard_map.95.refs_4_.refs_2_), channel_id=1, source_target_pairs={{0,16},{1,17},{2,18},{3,19},{4,20},{5,21},{6,22},{7,23},{8,24},{9,... | collective-permute-start | bytes 405512 | tf_op jit(solution)/shard_map/ppermute | solution.py:27
  7.7 5.7 %collective-permute-start = (bf16[16,3072]{1,0:T(8,128)(2,1)S(1)}, bf16[16,3072]{1,0:T(8,128)(2,1)S(1)}, u32[]{:S(2)}, u32[]{:S(2)}) collective-permute-start(bf16[16,3072]{1,0:T(8,128)(2,1)S(1)} %shard_map.94.refs_0_), channel_id=1, source_target_pairs={{0,4},{1,5},{2,6},{3,7},{4,0},{5,1},{6,2},{7,3},{8,12},{9,13},{10,... | collective-permute-start | bytes 294920 | tf_op jit(solution)/shard_map/ppermute | solution.py:27
  9.8 9.9 %collective-permute-start.1 = (bf16[16,3072]{1,0:T(8,128)(2,1)S(1)}, bf16[16,3072]{1,0:T(8,128)(2,1)S(1)}, u32[]{:S(2)}, u32[]{:S(2)}) collective-permute-start(bf16[16,3072]{1,0:T(8,128)(2,1)S(1)} %shard_map.94.refs_0_), channel_id=1, source_target_pairs={{0,8},{1,9},{2,10},{3,11},{4,12},{5,13},{6,14},{7,15},{8,0},{9,1},... | collective-permute-start | bytes 294920 | tf_op jit(solution)/shard_map/ppermute | solution.py:27
  12.4 7.3 %collective-permute-start.2 = (bf16[16,3072]{1,0:T(8,128)(2,1)S(1)}, bf16[16,3072]{1,0:T(8,128)(2,1)S(1)}, u32[]{:S(2)}, u32[]{:S(2)}) collective-permute-start(bf16[16,3072]{1,0:T(8,128)(2,1)S(1)} %shard_map.94.refs_0_), channel_id=1, source_target_pairs={{0,12},{1,13},{2,14},{3,15},{4,8},{5,9},{6,10},{7,11},{8,4},{9,5},... | collective-permute-start | bytes 294920 | tf_op jit(solution)/shard_map/ppermute | solution.py:27
  19.8 5.1 %collective-permute-start.5 = (bf16[64,3328]{1,0:T(8,128)(2,1)S(1)}, bf16[64,3328]{1,0:T(8,128)(2,1)S(1)}, u32[]{:S(2)}, u32[]{:S(2)}) collective-permute-start(bf16[64,3328]{1,0:T(8,128)(2,1)S(1)} %get-tuple-element.54.refs_2_.refs_4_), channel_id=1, source_target_pairs={{0,1},{1,0},{2,3},{3,2},{4,5},{5,4},{6,7},{7,6},{8,9},{9,8},{10,11... | collective-permute-start | bytes 1277960 | tf_op jit(solution)/shard_map/ppermute | solution.py:27
  20.9 14.4 %collective-permute-start.8 = (bf16[256,1024]{1,0:T(8,128)(2,1)S(1)}, bf16[256,1024]{1,0:T(8,128)(2,1)S(1)}, u32[]{:S(2)}, u32[]{:S(2)}) collective-permute-start(bf16[256,1024]{1,0:T(8,128)(2,1)S(1)} %dynamic-slice_bitcast_fusion), channel_id=1, source_target_pairs={{0,4},{1,5},{2,6},{3,7},{4,0},{5,1},{6,2},{7,3},{8,12},{9,13},{10,... | collective-permute-start | bytes 1572872 | tf_op jit(solution)/shard_map/ppermute | solution.py:27
  22.6 8.4 %collective-permute-start.13 = (bf16[64,2048]{1,0:T(8,128)(2,1)S(1)}, bf16[64,2048]{1,0:T(8,128)(2,1)S(1)}, u32[]{:S(2)}, u32[]{:S(2)}) collective-permute-start(bf16[64,2048]{1,0:T(8,128)(2,1)S(1)} %get-tuple-element.64), channel_id=1, source_target_pairs={{0,16},{1,17},{2,18},{3,19},{4,20},{5,21},{6,22},{7,23},{8,24},{9,... | collective-permute-start | bytes 786440 | tf_op jit(solution)/shard_map/ppermute | solution.py:27
  24.1 15.4 %collective-permute-start.12 = (bf16[256,1024]{1,0:T(8,128)(2,1)S(1)}, bf16[256,1024]{1,0:T(8,128)(2,1)S(1)}, u32[]{:S(2)}, u32[]{:S(2)}) collective-permute-start(bf16[256,1024]{1,0:T(8,128)(2,1)S(1)} %dynamic-slice_bitcast_fusion), channel_id=1, source_target_pairs={{4,8},{5,9},{6,10},{7,11},{8,4},{9,5},{10,6},{11,7},{20,24},{21,25... | collective-permute-start | bytes 1572872 | tf_op jit(solution)/shard_map/ppermute | solution.py:27
  27.9 10.4 %copy-start.2 = (bf16[1,176,4096]{2,1,0:T(8,128)(2,1)S(1)}, bf16[1,176,4096]{2,1,0:T(8,128)(2,1)}, u32[]{:S(2)}) copy-start(bf16[1,176,4096]{2,1,0:T(8,128)(2,1)} %param.7) | copy-start | bytes 4325380
  27.9 7.5 %collective-permute-start.6 = (bf16[176,512]{1,0:T(8,128)(2,1)S(1)}, bf16[176,512]{1,0:T(8,128)(2,1)S(1)}, u32[]{:S(2)}, u32[]{:S(2)}) collective-permute-start(bf16[176,512]{1,0:T(8,128)(2,1)S(1)} %get-tuple-element.57), channel_id=1, source_target_pairs={{0,2},{1,3},{2,0},{3,1},{4,6},{5,7},{6,4},{7,5},{8,10},{9,11},{10,... | collective-permute-start | bytes 540680 | tf_op jit(solution)/shard_map/ppermute | solution.py:27
  29.4 8.7 %collective-permute-start.7 = (bf16[176,512]{1,0:T(8,128)(2,1)S(1)}, bf16[176,512]{1,0:T(8,128)(2,1)S(1)}, u32[]{:S(2)}, u32[]{:S(2)}) collective-permute-start(bf16[176,512]{1,0:T(8,128)(2,1)S(1)} %get-tuple-element.58), channel_id=1, source_target_pairs={{0,18},{1,19},{2,16},{3,17},{4,22},{5,23},{6,20},{7,21},{8,26},{9,... | collective-permute-start | bytes 540680 | tf_op jit(solution)/shard_map/ppermute | solution.py:27
  31.0 7.2 %collective-permute-start.14 = (bf16[64,2048]{1,0:T(8,128)(2,1)S(1)}, bf16[64,2048]{1,0:T(8,128)(2,1)S(1)}, u32[]{:S(2)}, u32[]{:S(2)}) collective-permute-start(bf16[64,2048]{1,0:T(8,128)(2,1)S(1)} %collective-permute-done.13.refs_6_), channel_id=1, source_target_pairs={{0,1},{1,0},{2,3},{3,2},{4,5},{5,4},{6,7},{7,6},{8,9},{9,8},{10,11... | collective-permute-start | bytes 786440 | tf_op jit(solution)/shard_map/ppermute | solution.py:27
  38.2 8.6 %collective-permute-start.9 = (bf16[256,1024]{1,0:T(8,128)(2,1)S(1)}, bf16[256,1024]{1,0:T(8,128)(2,1)S(1)}, u32[]{:S(2)}, u32[]{:S(2)}) collective-permute-start(bf16[256,1024]{1,0:T(8,128)(2,1)S(1)} %collective-permute-done.8.refs_5_), channel_id=1, source_target_pairs={{0,1},{1,0},{2,3},{3,2},{4,5},{5,4},{6,7},{7,6},{8,9},{9,8},{10,11... | collective-permute-start | bytes 1572872 | tf_op jit(solution)/shard_map/ppermute | solution.py:27
  39.6 22.8 %collective-permute-start.17 = (bf16[352,1152]{1,0:T(8,128)(2,1)S(1)}, bf16[352,1152]{1,0:T(8,128)(2,1)S(1)}, u32[]{:S(2)}, u32[]{:S(2)}) collective-permute-start(bf16[352,1152]{1,0:T(8,128)(2,1)S(1)} %shard_map.100), channel_id=1, source_target_pairs={{0,4},{1,5},{2,6},{3,7},{12,8},{13,9},{14,10},{15,11},{16,20},{17,... | collective-permute-start | bytes 2433032 | tf_op jit(solution)/shard_map/ppermute | solution.py:27
  44.4 6.8 %collective-permute-start.15 = (bf16[256,1024]{1,0:T(8,128)(2,1)S(1)}, bf16[256,1024]{1,0:T(8,128)(2,1)S(1)}, u32[]{:S(2)}, u32[]{:S(2)}) collective-permute-start(bf16[256,1024]{1,0:T(8,128)(2,1)S(1)} %collective-permute-done.8.refs_5_), channel_id=1, source_target_pairs={{4,8},{5,9},{6,10},{7,11},{8,4},{9,5},{10,6},{11,7},{20,24},{21,25... | collective-permute-start | bytes 1572872 | tf_op jit(solution)/shard_map/ppermute | solution.py:27
  45.1 16.0 %collective-permute-start.16 = (bf16[256,1024]{1,0:T(8,128)(2,1)S(1)}, bf16[256,1024]{1,0:T(8,128)(2,1)S(1)}, u32[]{:S(2)}, u32[]{:S(2)}) collective-permute-start(bf16[256,1024]{1,0:T(8,128)(2,1)S(1)} %collective-permute-done.12.here_ref), channel_id=1, source_target_pairs={{4,0},{5,1},{6,2},{7,3},{8,12},{9,13},{10,14},{11,15},{20,16},{21,... | collective-permute-start | bytes 1572872 | tf_op jit(solution)/shard_map/ppermute | solution.py:27
  46.4 1.7 %collective-permute-start.19 = (bf16[64,2560]{1,0:T(8,128)(2,1)S(1)}, bf16[64,2560]{1,0:T(8,128)(2,1)S(1)}, u32[]{:S(2)}, u32[]{:S(2)}) collective-permute-start(bf16[64,2560]{1,0:T(8,128)(2,1)S(1)} %get-tuple-element.73), channel_id=1, source_target_pairs={{0,1},{1,0},{2,3},{3,2},{4,5},{5,4},{6,7},{7,6},{8,9},{9,8},{10,11... | collective-permute-start | bytes 983048 | tf_op jit(solution)/shard_map/ppermute | solution.py:27
  46.7 2.9 %collective-permute-start.18 = (bf16[64,2560]{1,0:T(8,128)(2,1)S(1)}, bf16[64,2560]{1,0:T(8,128)(2,1)S(1)}, u32[]{:S(2)}, u32[]{:S(2)}) collective-permute-start(bf16[64,2560]{1,0:T(8,128)(2,1)S(1)} %get-tuple-element.71), channel_id=1, source_target_pairs={{0,1},{1,0},{2,3},{3,2},{4,5},{5,4},{6,7},{7,6},{8,9},{9,8},{10,11... | collective-permute-start | bytes 983048 | tf_op jit(solution)/shard_map/ppermute | solution.py:27
  48.1 13.0 %collective-permute-start.10 = (bf16[176,512]{1,0:T(8,128)(2,1)S(1)}, bf16[176,512]{1,0:T(8,128)(2,1)S(1)}, u32[]{:S(2)}, u32[]{:S(2)}) collective-permute-start(bf16[176,512]{1,0:T(8,128)(2,1)S(1)} %get-tuple-element.62), channel_id=1, source_target_pairs={{0,2},{1,3},{2,0},{3,1},{4,6},{5,7},{6,4},{7,5},{8,10},{9,11},{10,... | collective-permute-start | bytes 540680 | tf_op jit(solution)/shard_map/ppermute | solution.py:27
  49.6 11.5 %collective-permute-start.11 = (bf16[176,512]{1,0:T(8,128)(2,1)S(1)}, bf16[176,512]{1,0:T(8,128)(2,1)S(1)}, u32[]{:S(2)}, u32[]{:S(2)}) collective-permute-start(bf16[176,512]{1,0:T(8,128)(2,1)S(1)} %get-tuple-element.63), channel_id=1, source_target_pairs={{0,18},{1,19},{2,16},{3,17},{4,22},{5,23},{6,20},{7,21},{8,26},{9,... | collective-permute-start | bytes 540680 | tf_op jit(solution)/shard_map/ppermute | solution.py:27
  62.4 1.9 %collective-permute-start.23 = (bf16[256,1024]{1,0:T(8,128)(2,1)S(1)}, bf16[256,1024]{1,0:T(8,128)(2,1)S(1)}, u32[]{:S(2)}, u32[]{:S(2)}) collective-permute-start(bf16[256,1024]{1,0:T(8,128)(2,1)S(1)} %collective-permute-done.15.refs_6_), channel_id=1, source_target_pairs={{0,1},{1,0},{2,3},{3,2},{4,5},{5,4},{6,7},{7,6},{8,9},{9,8},{10,11... | collective-permute-start | bytes 1572872 | tf_op jit(solution)/shard_map/ppermute | solution.py:27
  62.4 8.5 %collective-permute-start.20 = (bf16[256,1024]{1,0:T(8,128)(2,1)S(1)}, bf16[256,1024]{1,0:T(8,128)(2,1)S(1)}, u32[]{:S(2)}, u32[]{:S(2)}) collective-permute-start(bf16[256,1024]{1,0:T(8,128)(2,1)S(1)} %shard_map.102.refs_5_), channel_id=1, source_target_pairs={{0,1},{1,0},{2,3},{3,2},{4,5},{5,4},{6,7},{7,6},{8,9},{9,8},{10,11... | collective-permute-start | bytes 1572872 | tf_op jit(solution)/shard_map/ppermute | solution.py:27
  66.3 19.7 %collective-permute-start.24 = (bf16[352,512]{1,0:T(8,128)(2,1)S(1)}, bf16[352,512]{1,0:T(8,128)(2,1)}, u32[]{:S(2)}, u32[]{:S(2)}) collective-permute-start(bf16[352,512]{1,0:T(8,128)(2,1)S(1)} %get-tuple-element.82), channel_id=1, source_target_pairs={{4,0},{5,1},{6,2},{7,3},{8,12},{9,13},{10,14},{11,15},{20,16},{21,... | collective-permute-start | bytes 1081352 | tf_op jit(solution)/shard_map/ppermute | solution.py:27
  67.6 18.2 %collective-permute-start.27 = (bf16[32,5120]{1,0:T(8,128)(2,1)S(1)}, bf16[32,5120]{1,0:T(8,128)(2,1)S(1)}, u32[]{:S(2)}, u32[]{:S(2)}) collective-permute-start(bf16[32,5120]{1,0:T(8,128)(2,1)S(1)} %get-tuple-element.87), channel_id=1, source_target_pairs={{0,8},{1,9},{2,10},{3,11},{4,12},{5,13},{6,14},{7,15},{8,0},{9,1},... | collective-permute-start | bytes 983048 | tf_op jit(solution)/shard_map/ppermute | solution.py:27
  72.6 13.3 %collective-permute-start.21 = (bf16[176,512]{1,0:T(8,128)(2,1)}, bf16[176,512]{1,0:T(8,128)(2,1)S(1)}, u32[]{:S(2)}, u32[]{:S(2)}) collective-permute-start(bf16[176,512]{1,0:T(8,128)(2,1)} %get-tuple-element.77), channel_id=1, source_target_pairs={{0,2},{1,3},{2,0},{3,1},{4,6},{5,7},{6,4},{7,5},{8,10},{9,11},{10,... | collective-permute-start | bytes 540680 | tf_op jit(solution)/shard_map/ppermute | solution.py:27
  74.1 11.8 %collective-permute-start.22 = (bf16[176,512]{1,0:T(8,128)(2,1)}, bf16[176,512]{1,0:T(8,128)(2,1)S(1)}, u32[]{:S(2)}, u32[]{:S(2)}) collective-permute-start(bf16[176,512]{1,0:T(8,128)(2,1)} %get-tuple-element.78), channel_id=1, source_target_pairs={{0,18},{1,19},{2,16},{3,17},{4,22},{5,23},{6,20},{7,21},{8,26},{9,... | collective-permute-start | bytes 540680 | tf_op jit(solution)/shard_map/ppermute | solution.py:27
  85.9 5.6 %collective-permute-start.28 = (bf16[16,5120]{1,0:T(8,128)(2,1)S(1)}, bf16[16,5120]{1,0:T(8,128)(2,1)S(1)}, u32[]{:S(2)}, u32[]{:S(2)}) collective-permute-start(bf16[16,5120]{1,0:T(8,128)(2,1)S(1)} %get-tuple-element.90), channel_id=1, source_target_pairs={{0,4},{1,5},{2,6},{3,7},{4,0},{5,1},{6,2},{7,3},{8,12},{9,13},{10,... | collective-permute-start | bytes 491528 | tf_op jit(solution)/shard_map/ppermute | solution.py:27
  87.1 8.5 %collective-permute-start.26 = (bf16[176,512]{1,0:T(8,128)(2,1)S(1)}, bf16[176,512]{1,0:T(8,128)(2,1)S(1)}, u32[]{:S(2)}, u32[]{:S(2)}) collective-permute-start(bf16[176,512]{1,0:T(8,128)(2,1)S(1)} %get-tuple-element.85), channel_id=1, source_target_pairs={{0,18},{1,19},{2,16},{3,17},{4,22},{5,23},{6,20},{7,21},{8,26},{9,... | collective-permute-start | bytes 540680 | tf_op jit(solution)/shard_map/ppermute | solution.py:27
  89.6 8.3 %collective-permute-start.25 = (bf16[176,512]{1,0:T(8,128)(2,1)S(1)}, bf16[176,512]{1,0:T(8,128)(2,1)S(1)}, u32[]{:S(2)}, u32[]{:S(2)}) collective-permute-start(bf16[176,512]{1,0:T(8,128)(2,1)S(1)} %get-tuple-element.83), channel_id=1, source_target_pairs={{0,2},{1,3},{2,0},{3,1},{4,6},{5,7},{6,4},{7,5},{8,10},{9,11},{10,... | collective-permute-start | bytes 540680 | tf_op jit(solution)/shard_map/ppermute | solution.py:27
  91.6 1.5 %collective-permute-start.29 = (bf16[16,5120]{1,0:T(8,128)(2,1)S(1)}, bf16[16,5120]{1,0:T(8,128)(2,1)S(1)}, u32[]{:S(2)}, u32[]{:S(2)}) collective-permute-start(bf16[16,5120]{1,0:T(8,128)(2,1)S(1)} %shard_map.107.refs_0_), channel_id=1, source_target_pairs={{0,1},{1,0},{2,3},{3,2},{4,5},{5,4},{6,7},{7,6},{8,9},{9,8},{10,11... | collective-permute-start | bytes 491528 | tf_op jit(solution)/shard_map/ppermute | solution.py:27
  (5 other events, 4.7 us)

commit v12 on v10

--- a/solution.py
+++ b/solution.py
@@ -133,7 +133,7 @@
                 ref[:, to : to + LANES] = sent[:, j : j + LANES]
 
 
-def frozen_kernel(sizes, k, count, *refs):
+def frozen_kernel(sizes, k, spec, *refs):
     tokens, groups, holders, replicas, slots, rank = sizes
     g_refs, refs = refs[:groups], refs[groups:]
     map_refs, refs = refs[:replicas], refs[replicas:]
@@ -157,14 +157,16 @@
         sel_ref, refs = refs[0], refs[1:]
         out_refs = refs[-groups:]
     shard_at = lax.rem(here + holders - k, holders) * half
-    for j, block in enumerate(refs[:count]):
+    for (dr, offset), block in zip(spec, refs):
         if k == 0:
             block = block.at[pl.ds(pl.multiple_of(lax.axis_index("groups") * half, half), half)]
-        wide = block.shape[0]
-        at = 0 if count == 1 else lax.rem(core + replicas - j, replicas) * wide
+        wide = half if k == 0 or len(spec) == 1 else half // len(spec)
+        at = 0
+        if wide < half:
+            at = lax.rem(core + replicas - dr, replicas) * (half // replicas) + offset
         columns = pl.ds(pl.multiple_of(shard_at + at, wide), wide)
         for dg in range(groups):
-            base = rows_by_rows(g_refs[dg][...], block[...]).astype(BF16)
+            base = rows_by_rows(g_refs[dg][...], block[:wide]).astype(BF16)
             lora = 0.0
             for dr in range(replicas):
                 lora = lora + jnp.dot(
@@ -173,7 +175,7 @@
                     preferred_element_type=F32,
                 )
             lora = (ADAPTER_SCALE * lora).astype(BF16)
-            out_refs[dg][:, pl.ds(at if count == 1 else pl.multiple_of(at, wide), wide)] = (
+            out_refs[dg][:, pl.ds(pl.multiple_of(at, wide) if wide < half else 0, wide)] = (
                 base.astype(F32) + lora.astype(F32)
             ).astype(BF16)
 
@@ -251,22 +253,32 @@
         (token_adapter_index[0, :, 0][None], adapter_slot_index),
         scalars=1,
     )[0]
-    grads, named = [grad_rows], [own_named]
-    for dg in range(1, groups):
-        grads.append(moved(grad_rows, lambda g, z, s, r: (g - dg, z, s, r)))
-        named.append(moved(own_named, lambda g, z, s, r: (g - dg, z, s, r)))
-
     own = call(
         functools.partial(own_kernel, (groups, holders, shard)),
         [jax.ShapeDtypeStruct((rows, holders * half + value_width), BF16)],
         (adapter_down_weight[0], adapter_up_weight[0]),
     )[0]
+    grads, named = [grad_rows], [own_named]
+    for dg in range(1, groups):
+        grads.append(moved(grad_rows, lambda g, z, s, r: (g - dg, z, s, r)))
+        named.append(moved(own_named, lambda g, z, s, r: (g - dg, z, s, r)))
+
     held = [own]
     for k in range(1, holders):
         held.append(moved(own, lambda g, z, s, r: (g, z ^ k, s, r)))
 
+    part_rows = piece // 2
+    quarter = (group * replicas + core) * piece
+    parts = [
+        lax.dynamic_slice_in_dim(frozen, quarter + j * part_rows, part_rows + spare, axis=0)
+        for j, spare in enumerate((16, 0))
+    ]
+    own_named, parts = lax.optimization_barrier((own_named, parts))
+    held = [own]
+    for k in range(1, holders):
+        held.append(moved(own, lambda g, z, s, r: (g, z ^ k, s, r)))
+
     ring = [lax.dynamic_slice_in_dim(frozen, (group * replicas + core) * piece, piece, axis=0)]
-    ring.append(moved(ring[0], lambda g, z, s, r: (g, z + 1, s, r)))
     held, grads, named = lax.optimization_barrier((held, grads, named))
     both, downs = call(
         join_kernel,
@@ -280,20 +292,25 @@
         moved(both, lambda g, z, s, r: (g, z, s, r + dr)) for dr in range(1, replicas)
     ]
     others = [moved(downs, lambda g, z, s, r: (g + dg, z, s, r)) for dg in range(1, groups)]
+    onward = lambda g, z, s, r: (g, z + 1, s, r)
+    ring = [parts, [moved(after(x, both[0]), onward) for x in parts]]
+
     def pieces_of(k, *before):
         if k == 0:
-            return [frozen]
-        block = after(ring[k], *before) if before else ring[k]
-        pieces = [block] + [
-            moved(block, lambda g, z, s, r: (g, z, s, r + dr)) for dr in range(1, replicas)
-        ]
-        if piece % LANES:
+            return [(0, 0)], [frozen]
+        spec, pieces = [], []
+        for dr in range(replicas):
+            for j, part in enumerate(ring[k]):
+                spec.append((dr, j * part_rows))
+                mail = after(part, *before) if before else part
+                pieces.append(moved(mail, lambda g, z, s, r: (g, z, s, r + dr)) if dr else part)
+        if part_rows % LANES:
             whole = jnp.zeros((half, value_width), BF16)
-            for dr in range(replicas):
-                at = ((core - dr) % replicas) * piece
-                whole = lax.dynamic_update_slice_in_dim(whole, pieces[dr], at, axis=0)
-            pieces = [whole]
-        return pieces
+            for (dr, offset), part in zip(spec, pieces):
+                at = ((core - dr) % replicas) * piece + offset
+                whole = lax.dynamic_update_slice_in_dim(whole, part[:part_rows], at, axis=0)
+            spec, pieces = [(0, 0)], [whole]
+        return spec, pieces
 
     kept = replicas * holders * rows
 
@@ -327,14 +344,14 @@
     arrived, outs, sel = [], [], None
     for k in range(holders):
         if k > 1:
-            last = after(ring[-1], *outs[k - 2], part) if k > 2 else after(ring[-1], sel)
-            ring.append(moved(last, lambda g, z, s, r: (g, z + 1, s, r)))
-        gate = outs[k - 1] if k > 1 else [sel] * k
-        blocks = pieces_of(k, *gate, *([*arrived[k - 2], chip[0]] if k > 2 else ()))
+            gate = [part] if k > 2 else [sel]
+            ring.append([moved(after(x, *gate), onward) for x in ring[-1]])
+        gate = outs[k - 1] if k > 1 else arrived[0] if k else []
+        spec, blocks = pieces_of(k, *gate, *([*arrived[k - 2], chip[0]] if k > 2 else ()))
         tokens_in = [after(grad_rows, part), *grads[1:]] if k == 1 else grads
         out = call(
             functools.partial(
-                frozen_kernel, (tokens, groups, holders, replicas, slots, rank), k, len(blocks)
+                frozen_kernel, (tokens, groups, holders, replicas, slots, rank), k, spec
             ),
             [jax.ShapeDtypeStruct((tokens, half), BF16)] * groups
             + [jax.ShapeDtypeStruct((groups * tokens, kept), BF16)] * (k == 0),
@@ -358,7 +375,7 @@
     )[0]
 
     sums = [chip[0]] + [
-        moved(after(chip[k], ring[-1]), lambda g, z, s, r: (g, z ^ k, s, r))
+        moved(after(chip[k], *ring[-1]), lambda g, z, s, r: (g, z ^ k, s, r))
         for k in range(1, holders)
     ]
     total = call(total_kernel, [jax.ShapeDtypeStruct((rows, cols), BF16)], sums)[0]

time: 89.1 us -> 97 us (1.089)
  starting transfers between devices: 25.2 us -> 29.4 us
  waiting for transfers between devices: 48.2 us -> 50 us
    ppermute x28 -> x34, starting transfers between devices: 25.2 us -> 29.4 us  [moved(): return lax.ppermute(x, AXES, pairs)]
    ppermute x28 -> x34, waiting for transfers between devices: 48.2 us -> 50 us  [moved(): return lax.ppermute(x, AXES, pairs)]
    dynamic_slice x1 -> x2, local copies, waits for them, and re-layouts: 1.08 us -> 1.95 us  [on_device(): lax.dynamic_slice_in_dim(frozen, quarter + j * part_rows, part_rows + spa...]
  transfers between devices with their start and end apart: 28 -> 34, of which waited for: 15 -> 12; matrix products, arithmetic and copies ran while one was open for 1% -> 2% of each run, Pallas kernels for 9% -> 9%
where the time goes in v12:
time: 97 us; the launch traced here: 96.7 us
  waiting for transfers between devices  50 us (52%)
  starting transfers between devices  29.4 us (30%)
  Pallas kernels  9.74 us (10%)
  local copies, waits for them, and re-layouts  6.67 us (7%)
    ppermute x34, waiting for transfers between devices, moved(): return lax.ppermute(x, AXES, pairs)  50 us
    ppermute x34, starting transfers between devices, moved(): return lax.ppermute(x, AXES, pairs)  29.4 us
    pallas_call x12, Pallas kernels, call(): pl.pallas_call(kernel, out_shape=out_shape, in_specs=[pl.BlockSpec(memory...  9.74 us
    unnamed x14, local copies, waits for them, and re-layouts  4.72 us
    dynamic_slice x2, local copies, waits for them, and re-layouts, on_device(): lax.dynamic_slice_in_dim(frozen, quarter + j * part_rows, part_rows + spa...  1.95 us
  transfers between devices with their start and end apart: 34, of which 12 were waited for; matrix products, arithmetic and copies ran while one was open for 2% of the time, Pallas kernels for 9%

profile of v12, /device:TPU:0, one launch (start us, length us, event | category | flops | bytes accessed | tf_op | source)
XLA Modules:
  0.0 96.7 jit_solution(6278906985370813470)
XLA Ops:
  0.6 3.0 %collective-permute-start.3 = (bf16[176,1024]{1,0:T(8,128)(2,1)}, bf16[176,1024]{1,0:T(8,128)(2,1)S(1)}, u32[]{:S(2)}, u32[]{:S(2)}) collective-permute-start(bf16[176,1024]{1,0:T(8,128)(2,1)} %bitcast.13), channel_id=1, source_target_pairs={{0,16},{1,17},{2,18},{3,19},{4,20},{5,21},{6,22},{7,23},{8,24},{9,... | collective-permute-start | bytes 1081352 | tf_op jit(solution)/shard_map/ppermute | solution.py:27
  7.7 2.1 %collective-permute-start = (bf16[16,3072]{1,0:T(8,128)(2,1)S(1)}, bf16[16,3072]{1,0:T(8,128)(2,1)S(1)}, u32[]{:S(2)}, u32[]{:S(2)}) collective-permute-start(bf16[16,3072]{1,0:T(8,128)(2,1)S(1)} %shard_map.94.refs_0_), channel_id=1, source_target_pairs={{0,4},{1,5},{2,6},{3,7},{4,0},{5,1},{6,2},{7,3},{8,12},{9,13},{10,... | collective-permute-start | bytes 294920 | tf_op jit(solution)/shard_map/ppermute | solution.py:27
  9.8 2.6 %collective-permute-start.1 = (bf16[16,3072]{1,0:T(8,128)(2,1)S(1)}, bf16[16,3072]{1,0:T(8,128)(2,1)S(1)}, u32[]{:S(2)}, u32[]{:S(2)}) collective-permute-start(bf16[16,3072]{1,0:T(8,128)(2,1)S(1)} %shard_map.94.refs_0_), channel_id=1, source_target_pairs={{0,8},{1,9},{2,10},{3,11},{4,12},{5,13},{6,14},{7,15},{8,0},{9,1},... | collective-permute-start | bytes 294920 | tf_op jit(solution)/shard_map/ppermute | solution.py:27
  13.4 6.3 %collective-permute-done.1.refs_2_ = bf16[16,3072]{1,0:T(8,128)(2,1)S(1)} collective-permute-done((bf16[16,3072]{1,0:T(8,128)(2,1)S(1)}, bf16[16,3072]{1,0:T(8,128)(2,1)S(1)}, u32[]{:S(2)}, u32[]{:S(2)}) %collective-permute-start.1) | collective-permute-done | bytes 98336 | tf_op jit(solution)/shard_map/ppermute | solution.py:27
  19.8 1.0 %dynamic-slice_bitcast_fusion = bf16[144,1024]{1,0:T(8,128)(2,1)S(1)} fusion(bf16[1,1024,1024]{2,1,0:T(8,128)(2,1)} %param.11, s32[]{:T(128)S(6)} %select_n.6), kind=kLoop, calls=%fused_computation | loop fusion | bytes 589828 | tf_op jit(solution)/shard_map/dynamic_slice | solution.py:273
  20.8 1.6 %collective-permute-start.8 = (bf16[64,2048]{1,0:T(8,128)(2,1)S(1)}, bf16[64,2048]{1,0:T(8,128)(2,1)S(1)}, u32[]{:S(2)}, u32[]{:S(2)}) collective-permute-start(bf16[64,2048]{1,0:T(8,128)(2,1)S(1)} %get-tuple-element.66), channel_id=1, source_target_pairs={{0,16},{1,17},{2,18},{3,19},{4,20},{5,21},{6,22},{7,23},{8,24},{9,... | collective-permute-start | bytes 786440 | tf_op jit(solution)/shard_map/ppermute | solution.py:27
  23.4 1.7 %collective-permute-start.10 = (bf16[144,1024]{1,0:T(8,128)(2,1)S(1)}, bf16[144,1024]{1,0:T(8,128)(2,1)S(1)}, u32[]{:S(2)}, u32[]{:S(2)}) collective-permute-start(bf16[144,1024]{1,0:T(8,128)(2,1)S(1)} %dynamic-slice_bitcast_fusion), channel_id=1, source_target_pairs={{0,4},{1,5},{2,6},{3,7},{4,8},{5,9},{6,10},{7,11},{8,12},{9,13},{1... | collective-permute-start | bytes 884744 | tf_op jit(solution)/shard_map/ppermute | solution.py:27
  25.0 1.6 %collective-permute-start.11 = (bf16[128,1024]{1,0:T(8,128)(2,1)S(1)}, bf16[128,1024]{1,0:T(8,128)(2,1)S(1)}, u32[]{:S(2)}, u32[]{:S(2)}) collective-permute-start(bf16[128,1024]{1,0:T(8,128)(2,1)S(1)} %dynamic-slice_bitcast_fusion.1), channel_id=1, source_target_pairs={{0,4},{1,5},{2,6},{3,7},{4,8},{5,9},{6,10},{7,11},{8,12},{9,13},{1... | collective-permute-start | bytes 786440 | tf_op jit(solution)/shard_map/ppermute | solution.py:27
  26.6 1.6 %copy-done.1 = bf16[1,1024,1024]{2,1,0:T(8,128)(2,1)S(1)} copy-done((bf16[1,1024,1024]{2,1,0:T(8,128)(2,1)S(1)}, bf16[1,1024,1024]{2,1,0:T(8,128)(2,1)}, u32[]{:S(2)}) %copy-start.1) | copy-done | bytes 2097176
  28.2 1.5 %shard_map.97 = (bf16[176,512]{1,0:T(8,128)(2,1)S(1)}, bf16[176,512]{1,0:T(8,128)(2,1)S(1)}, bf16[352,128]{1,0:T(8,128)(2,1)S(1)}) custom-call(bf16[176,1024]{1,0:T(8,128)(2,1)S(1)} %bitcast.14, bf16[176,1024]{1,0:T(8,128)(2,1)S(1)} %collective-permute-done.3.refs_1_, bf16[64,3328]{1,0:T(8,128)(2,1)S(1)} %get-tuple-element.60.refs_2_.refs_4_, ...), custom_call_target="tpu_custom_call" | custom-call | flops 1000 | bytes 1000 | tf_op jit(solution)/shard_map/pallas_call | solution.py:44
  29.7 1.6 %collective-permute-start.6 = (bf16[176,512]{1,0:T(8,128)(2,1)S(1)}, bf16[176,512]{1,0:T(8,128)(2,1)S(1)}, u32[]{:S(2)}, u32[]{:S(2)}) collective-permute-start(bf16[176,512]{1,0:T(8,128)(2,1)S(1)} %get-tuple-element.63), channel_id=1, source_target_pairs={{0,2},{1,3},{2,0},{3,1},{4,6},{5,7},{6,4},{7,5},{8,10},{9,11},{10,... | collective-permute-start | bytes 540680 | tf_op jit(solution)/shard_map/ppermute | solution.py:27
  31.7 8.2 %collective-permute-done.11.refs_6_ = bf16[128,1024]{1,0:T(8,128)(2,1)S(1)} collective-permute-done((bf16[128,1024]{1,0:T(8,128)(2,1)S(1)}, bf16[128,1024]{1,0:T(8,128)(2,1)S(1)}, u32[]{:S(2)}, u32[]{:S(2)}) %collective-permute-start.11) | collective-permute-done | bytes 262176 | tf_op jit(solution)/shard_map/ppermute | solution.py:27
  40.6 1.4 %collective-permute-start.16 = (bf16[144,1024]{1,0:T(8,128)(2,1)S(1)}, bf16[144,1024]{1,0:T(8,128)(2,1)S(1)}, u32[]{:S(2)}, u32[]{:S(2)}) collective-permute-start(bf16[144,1024]{1,0:T(8,128)(2,1)S(1)} %collective-permute-done.10.refs_5_), channel_id=1, source_target_pairs={{0,4},{1,5},{2,6},{3,7},{4,8},{5,9},{6,10},{7,11},{8,12},{9,13},{1... | collective-permute-start | bytes 884744 | tf_op jit(solution)/shard_map/ppermute | solution.py:27
  42.0 1.3 %shard_map.98 = (f32[64,5120]{1,0:T(8,128)S(1)}, bf16[64,2560]{1,0:T(8,128)(2,1)S(1)}, bf16[64,2560]{1,0:T(8,128)(2,1)S(1)}) custom-call(bf16[176,4096]{1,0:T(8,128)(2,1)S(1)} %bitcast.20, bf16[176,1024]{1,0:T(8,128)(2,1)S(1)} %bitcast.15, bf16[176,384]{1,0:T(8,128)(2,1)S(1)} %shard_map.95.refs_4_.refs_2_, ...), custom_call_target="tpu_custom_call" | custom-call | flops 1000 | bytes 1000 | tf_op jit(solution)/shard_map/pallas_call | solution.py:44
  43.8 1.3 %shard_map.99 = (bf16[176,512]{1,0:T(8,128)(2,1)S(1)}, bf16[176,512]{1,0:T(8,128)(2,1)S(1)}) custom-call(bf16[176,1024]{1,0:T(8,128)(2,1)S(1)} %bitcast.16, bf16[176,1024]{1,0:T(8,128)(2,1)S(1)} %collective-permute-done.3.refs_1_, bf16[64,3328]{1,0:T(8,128)(2,1)S(1)} %get-tuple-element.60.refs_2_.refs_4_, ...), custom_call_target="tpu_custom_call" | custom-call | flops 1000 | bytes 1000 | tf_op jit(solution)/shard_map/pallas_call | solution.py:44
  45.2 6.3 %collective-permute-done.17.refs_6_ = bf16[128,1024]{1,0:T(8,128)(2,1)S(1)} collective-permute-done((bf16[128,1024]{1,0:T(8,128)(2,1)S(1)}, bf16[128,1024]{1,0:T(8,128)(2,1)S(1)}, u32[]{:S(2)}, u32[]{:S(2)}) %collective-permute-start.17) | collective-permute-done | bytes 262176 | tf_op jit(solution)/shard_map/ppermute | solution.py:27
  51.5 5.4 %collective-permute-done.16.refs_5_ = bf16[144,1024]{1,0:T(8,128)(2,1)S(1)} collective-permute-done((bf16[144,1024]{1,0:T(8,128)(2,1)S(1)}, bf16[144,1024]{1,0:T(8,128)(2,1)S(1)}, u32[]{:S(2)}, u32[]{:S(2)}) %collective-permute-start.16) | collective-permute-done | bytes 294944 | tf_op jit(solution)/shard_map/ppermute | solution.py:27
  57.0 1.6 %collective-permute-start.14 = (bf16[176,512]{1,0:T(8,128)(2,1)S(1)}, bf16[176,512]{1,0:T(8,128)(2,1)S(1)}, u32[]{:S(2)}, u32[]{:S(2)}) collective-permute-start(bf16[176,512]{1,0:T(8,128)(2,1)S(1)} %get-tuple-element.76), channel_id=1, source_target_pairs={{0,2},{1,3},{2,0},{3,1},{4,6},{5,7},{6,4},{7,5},{8,10},{9,11},{10,... | collective-permute-start | bytes 540680 | tf_op jit(solution)/shard_map/ppermute | solution.py:27
  58.6 1.1 %collective-permute-start.15 = (bf16[176,512]{1,0:T(8,128)(2,1)S(1)}, bf16[176,512]{1,0:T(8,128)(2,1)S(1)}, u32[]{:S(2)}, u32[]{:S(2)}) collective-permute-start(bf16[176,512]{1,0:T(8,128)(2,1)S(1)} %get-tuple-element.77), channel_id=1, source_target_pairs={{0,18},{1,19},{2,16},{3,17},{4,22},{5,23},{6,20},{7,21},{8,26},{9,... | collective-permute-start | bytes 540680 | tf_op jit(solution)/shard_map/ppermute | solution.py:27
  59.8 1.3 %shard_map.100 = (bf16[176,512]{1,0:T(8,128)(2,1)S(1)}, bf16[176,512]{1,0:T(8,128)(2,1)S(1)}) custom-call(bf16[176,1024]{1,0:T(8,128)(2,1)S(1)} %bitcast.17, bf16[176,1024]{1,0:T(8,128)(2,1)S(1)} %collective-permute-done.3.refs_1_, bf16[64,3328]{1,0:T(8,128)(2,1)S(1)} %get-tuple-element.60.refs_2_.refs_4_, ...), custom_call_target="tpu_custom_call" | custom-call | flops 1000 | bytes 1000 | tf_op jit(solution)/shard_map/pallas_call | solution.py:44
  61.1 7.4 %collective-permute-done.22.refs_5_ = bf16[144,1024]{1,0:T(8,128)(2,1)S(1)} collective-permute-done((bf16[144,1024]{1,0:T(8,128)(2,1)S(1)}, bf16[144,1024]{1,0:T(8,128)(2,1)S(1)}, u32[]{:S(2)}, u32[]{:S(2)}) %collective-permute-start.22) | collective-permute-done | bytes 294944 | tf_op jit(solution)/shard_map/ppermute | solution.py:27
  68.5 5.2 %collective-permute-done.23.refs_6_ = bf16[128,1024]{1,0:T(8,128)(2,1)S(1)} collective-permute-done((bf16[128,1024]{1,0:T(8,128)(2,1)S(1)}, bf16[128,1024]{1,0:T(8,128)(2,1)S(1)}, u32[]{:S(2)}, u32[]{:S(2)}) %collective-permute-start.23) | collective-permute-done | bytes 262176 | tf_op jit(solution)/shard_map/ppermute | solution.py:27
  73.7 1.5 %collective-permute-start.20 = (bf16[176,512]{1,0:T(8,128)(2,1)S(1)}, bf16[176,512]{1,0:T(8,128)(2,1)S(1)}, u32[]{:S(2)}, u32[]{:S(2)}) collective-permute-start(bf16[176,512]{1,0:T(8,128)(2,1)S(1)} %get-tuple-element.82), channel_id=1, source_target_pairs={{0,2},{1,3},{2,0},{3,1},{4,6},{5,7},{6,4},{7,5},{8,10},{9,11},{10,... | collective-permute-start | bytes 540680 | tf_op jit(solution)/shard_map/ppermute | solution.py:27
  75.2 1.1 %collective-permute-start.21 = (bf16[176,512]{1,0:T(8,128)(2,1)S(1)}, bf16[176,512]{1,0:T(8,128)(2,1)S(1)}, u32[]{:S(2)}, u32[]{:S(2)}) collective-permute-start(bf16[176,512]{1,0:T(8,128)(2,1)S(1)} %get-tuple-element.83), channel_id=1, source_target_pairs={{0,18},{1,19},{2,16},{3,17},{4,22},{5,23},{6,20},{7,21},{8,26},{9,... | collective-permute-start | bytes 540680 | tf_op jit(solution)/shard_map/ppermute | solution.py:27
  76.4 4.4 %collective-permute-start.30 = (bf16[16,5120]{1,0:T(8,128)(2,1)S(1)}, bf16[16,5120]{1,0:T(8,128)(2,1)S(1)}, u32[]{:S(2)}, u32[]{:S(2)}) collective-permute-start(bf16[16,5120]{1,0:T(8,128)(2,1)S(1)} %get-tuple-element.98), channel_id=1, source_target_pairs={{0,4},{1,5},{2,6},{3,7},{4,0},{5,1},{6,2},{7,3},{8,12},{9,13},{10,... | collective-permute-start | bytes 491528 | tf_op jit(solution)/shard_map/ppermute | solution.py:27
  80.7 1.3 %shard_map.102 = (bf16[176,512]{1,0:T(8,128)(2,1)S(1)}, bf16[176,512]{1,0:T(8,128)(2,1)S(1)}) custom-call(bf16[176,1024]{1,0:T(8,128)(2,1)S(1)} %bitcast.18, bf16[176,1024]{1,0:T(8,128)(2,1)S(1)} %collective-permute-done.3.refs_1_, bf16[64,3328]{1,0:T(8,128)(2,1)S(1)} %get-tuple-element.60.refs_2_.refs_4_, ...), custom_call_target="tpu_custom_call" | custom-call | flops 1000 | bytes 1000 | tf_op jit(solution)/shard_map/pallas_call | solution.py:44
  82.1 3.1 %collective-permute-done.21.refs_5_ = bf16[176,512]{1,0:T(8,128)(2,1)S(1)} collective-permute-done((bf16[176,512]{1,0:T(8,128)(2,1)S(1)}, bf16[176,512]{1,0:T(8,128)(2,1)S(1)}, u32[]{:S(2)}, u32[]{:S(2)}) %collective-permute-start.21) | collective-permute-done | bytes 180256 | tf_op jit(solution)/shard_map/ppermute | solution.py:27
  85.1 1.8 %collective-permute-start.29 = (bf16[176,512]{1,0:T(8,128)(2,1)S(1)}, bf16[176,512]{1,0:T(8,128)(2,1)S(1)}, u32[]{:S(2)}, u32[]{:S(2)}) collective-permute-start(bf16[176,512]{1,0:T(8,128)(2,1)S(1)} %get-tuple-element.96), channel_id=1, source_target_pairs={{0,18},{1,19},{2,16},{3,17},{4,22},{5,23},{6,20},{7,21},{8,26},{9,... | collective-permute-start | bytes 540680 | tf_op jit(solution)/shard_map/ppermute | solution.py:27
  87.5 3.4 %collective-permute-done.31.refs_2_ = bf16[16,5120]{1,0:T(8,128)(2,1)S(1)} collective-permute-done((bf16[16,5120]{1,0:T(8,128)(2,1)S(1)}, bf16[16,5120]{1,0:T(8,128)(2,1)S(1)}, u32[]{:S(2)}, u32[]{:S(2)}) %collective-permute-start.31) | collective-permute-done | bytes 163872 | tf_op jit(solution)/shard_map/ppermute | solution.py:27
  91.1 1.4 %collective-permute-done.33.refs_1_ = bf16[16,5120]{1,0:T(8,128)(2,1)S(1)} collective-permute-done((bf16[16,5120]{1,0:T(8,128)(2,1)S(1)}, bf16[16,5120]{1,0:T(8,128)(2,1)S(1)}, u32[]{:S(2)}, u32[]{:S(2)}) %collective-permute-start.33) | collective-permute-done | bytes 163872 | tf_op jit(solution)/shard_map/ppermute | solution.py:27
  93.5 2.0 %collective-permute-done.28.refs_6_ = bf16[176,512]{1,0:T(8,128)(2,1)S(1)} collective-permute-done((bf16[176,512]{1,0:T(8,128)(2,1)S(1)}, bf16[176,512]{1,0:T(8,128)(2,1)S(1)}, u32[]{:S(2)}, u32[]{:S(2)}) %collective-permute-start.28) | collective-permute-done | bytes 180256 | tf_op jit(solution)/shard_map/ppermute | solution.py:27
  95.5 1.2 %shard_map.103 = bf16[176,4096]{1,0:T(8,128)(2,1)} custom-call(bf16[176,512]{1,0:T(8,128)(2,1)S(1)} %collective-permute-done.6.refs_0_, bf16[176,512]{1,0:T(8,128)(2,1)S(1)} %collective-permute-done.7.refs_1_, bf16[176,512]{1,0:T(8,128)(2,1)S(1)} %collective-permute-done.14.refs_2_, bf16[176,512]{1,0:T(8,128)(2,1)S(1)} %collective-permute-done.15.refs_3_, ...), custom_call_target="tpu_custom_call" | custom-call | flops 1000 | bytes 1000 | tf_op jit(solution)/shard_map/pallas_call | solution.py:44
  (64 shorter events, 9.7 us)
Async XLA Ops:
  0.6 19.1 %collective-permute-start.3 = (bf16[176,1024]{1,0:T(8,128)(2,1)}, bf16[176,1024]{1,0:T(8,128)(2,1)S(1)}, u32[]{:S(2)}, u32[]{:S(2)}) collective-permute-start(bf16[176,1024]{1,0:T(8,128)(2,1)} %bitcast.13), channel_id=1, source_target_pairs={{0,16},{1,17},{2,18},{3,19},{4,20},{5,21},{6,22},{7,23},{8,24},{9,... | collective-permute-start | bytes 1081352 | tf_op jit(solution)/shard_map/ppermute | solution.py:27
  5.8 13.9 %collective-permute-start.4 = (bf16[176,384]{1,0:T(8,128)(2,1)S(1)}, bf16[176,384]{1,0:T(8,128)(2,1)S(1)}, u32[]{:S(2)}, u32[]{:S(2)}) collective-permute-start(bf16[176,384]{1,0:T(8,128)(2,1)S(1)} %shard_map.95.refs_4_.refs_2_), channel_id=1, source_target_pairs={{0,16},{1,17},{2,18},{3,19},{4,20},{5,21},{6,22},{7,23},{8,24},{9,... | collective-permute-start | bytes 405512 | tf_op jit(solution)/shard_map/ppermute | solution.py:27
  7.7 5.7 %collective-permute-start = (bf16[16,3072]{1,0:T(8,128)(2,1)S(1)}, bf16[16,3072]{1,0:T(8,128)(2,1)S(1)}, u32[]{:S(2)}, u32[]{:S(2)}) collective-permute-start(bf16[16,3072]{1,0:T(8,128)(2,1)S(1)} %shard_map.94.refs_0_), channel_id=1, source_target_pairs={{0,4},{1,5},{2,6},{3,7},{4,0},{5,1},{6,2},{7,3},{8,12},{9,13},{10,... | collective-permute-start | bytes 294920 | tf_op jit(solution)/shard_map/ppermute | solution.py:27
  9.8 9.9 %collective-permute-start.1 = (bf16[16,3072]{1,0:T(8,128)(2,1)S(1)}, bf16[16,3072]{1,0:T(8,128)(2,1)S(1)}, u32[]{:S(2)}, u32[]{:S(2)}) collective-permute-start(bf16[16,3072]{1,0:T(8,128)(2,1)S(1)} %shard_map.94.refs_0_), channel_id=1, source_target_pairs={{0,8},{1,9},{2,10},{3,11},{4,12},{5,13},{6,14},{7,15},{8,0},{9,1},... | collective-permute-start | bytes 294920 | tf_op jit(solution)/shard_map/ppermute | solution.py:27
  12.4 7.3 %collective-permute-start.2 = (bf16[16,3072]{1,0:T(8,128)(2,1)S(1)}, bf16[16,3072]{1,0:T(8,128)(2,1)S(1)}, u32[]{:S(2)}, u32[]{:S(2)}) collective-permute-start(bf16[16,3072]{1,0:T(8,128)(2,1)S(1)} %shard_map.94.refs_0_), channel_id=1, source_target_pairs={{0,12},{1,13},{2,14},{3,15},{4,8},{5,9},{6,10},{7,11},{8,4},{9,5},... | collective-permute-start | bytes 294920 | tf_op jit(solution)/shard_map/ppermute | solution.py:27
  19.8 6.9 %collective-permute-start.5 = (bf16[64,3328]{1,0:T(8,128)(2,1)S(1)}, bf16[64,3328]{1,0:T(8,128)(2,1)S(1)}, u32[]{:S(2)}, u32[]{:S(2)}) collective-permute-start(bf16[64,3328]{1,0:T(8,128)(2,1)S(1)} %get-tuple-element.60.refs_2_.refs_4_), channel_id=1, source_target_pairs={{0,1},{1,0},{2,3},{3,2},{4,5},{5,4},{6,7},{7,6},{8,9},{9,8},{10,11... | collective-permute-start | bytes 1277960 | tf_op jit(solution)/shard_map/ppermute | solution.py:27
  20.8 10.9 %collective-permute-start.8 = (bf16[64,2048]{1,0:T(8,128)(2,1)S(1)}, bf16[64,2048]{1,0:T(8,128)(2,1)S(1)}, u32[]{:S(2)}, u32[]{:S(2)}) collective-permute-start(bf16[64,2048]{1,0:T(8,128)(2,1)S(1)} %get-tuple-element.66), channel_id=1, source_target_pairs={{0,16},{1,17},{2,18},{3,19},{4,20},{5,21},{6,22},{7,23},{8,24},{9,... | collective-permute-start | bytes 786440 | tf_op jit(solution)/shard_map/ppermute | solution.py:27
  23.4 16.6 %collective-permute-start.10 = (bf16[144,1024]{1,0:T(8,128)(2,1)S(1)}, bf16[144,1024]{1,0:T(8,128)(2,1)S(1)}, u32[]{:S(2)}, u32[]{:S(2)}) collective-permute-start(bf16[144,1024]{1,0:T(8,128)(2,1)S(1)} %dynamic-slice_bitcast_fusion), channel_id=1, source_target_pairs={{0,4},{1,5},{2,6},{3,7},{4,8},{5,9},{6,10},{7,11},{8,12},{9,13},{1... | collective-permute-start | bytes 884744 | tf_op jit(solution)/shard_map/ppermute | solution.py:27
  25.0 14.9 %collective-permute-start.11 = (bf16[128,1024]{1,0:T(8,128)(2,1)S(1)}, bf16[128,1024]{1,0:T(8,128)(2,1)S(1)}, u32[]{:S(2)}, u32[]{:S(2)}) collective-permute-start(bf16[128,1024]{1,0:T(8,128)(2,1)S(1)} %dynamic-slice_bitcast_fusion.1), channel_id=1, source_target_pairs={{0,4},{1,5},{2,6},{3,7},{4,8},{5,9},{6,10},{7,11},{8,12},{9,13},{1... | collective-permute-start | bytes 786440 | tf_op jit(solution)/shard_map/ppermute | solution.py:27
  29.7 10.3 %collective-permute-start.6 = (bf16[176,512]{1,0:T(8,128)(2,1)S(1)}, bf16[176,512]{1,0:T(8,128)(2,1)S(1)}, u32[]{:S(2)}, u32[]{:S(2)}) collective-permute-start(bf16[176,512]{1,0:T(8,128)(2,1)S(1)} %get-tuple-element.63), channel_id=1, source_target_pairs={{0,2},{1,3},{2,0},{3,1},{4,6},{5,7},{6,4},{7,5},{8,10},{9,11},{10,... | collective-permute-start | bytes 540680 | tf_op jit(solution)/shard_map/ppermute | solution.py:27
  31.3 8.7 %collective-permute-start.7 = (bf16[176,512]{1,0:T(8,128)(2,1)S(1)}, bf16[176,512]{1,0:T(8,128)(2,1)S(1)}, u32[]{:S(2)}, u32[]{:S(2)}) collective-permute-start(bf16[176,512]{1,0:T(8,128)(2,1)S(1)} %get-tuple-element.64), channel_id=1, source_target_pairs={{0,18},{1,19},{2,16},{3,17},{4,22},{5,23},{6,20},{7,21},{8,26},{9,... | collective-permute-start | bytes 540680 | tf_op jit(solution)/shard_map/ppermute | solution.py:27
  31.7 10.2 %collective-permute-start.9 = (bf16[64,2048]{1,0:T(8,128)(2,1)S(1)}, bf16[64,2048]{1,0:T(8,128)(2,1)S(1)}, u32[]{:S(2)}, u32[]{:S(2)}) collective-permute-start(bf16[64,2048]{1,0:T(8,128)(2,1)S(1)} %collective-permute-done.8.refs_6_), channel_id=1, source_target_pairs={{0,1},{1,0},{2,3},{3,2},{4,5},{5,4},{6,7},{7,6},{8,9},{9,8},{10,11... | collective-permute-start | bytes 786440 | tf_op jit(solution)/shard_map/ppermute | solution.py:27
  40.0 3.3 %collective-permute-start.13 = (bf16[128,1024]{1,0:T(8,128)(2,1)S(1)}, bf16[128,1024]{1,0:T(8,128)(2,1)S(1)}, u32[]{:S(2)}, u32[]{:S(2)}) collective-permute-start(bf16[128,1024]{1,0:T(8,128)(2,1)S(1)} %collective-permute-done.11.refs_6_), channel_id=1, source_target_pairs={{0,1},{1,0},{2,3},{3,2},{4,5},{5,4},{6,7},{7,6},{8,9},{9,8},{10,11... | collective-permute-start | bytes 786440 | tf_op jit(solution)/shard_map/ppermute | solution.py:27
  40.0 3.8 %collective-permute-start.12 = (bf16[144,1024]{1,0:T(8,128)(2,1)S(1)}, bf16[144,1024]{1,0:T(8,128)(2,1)S(1)}, u32[]{:S(2)}, u32[]{:S(2)}) collective-permute-start(bf16[144,1024]{1,0:T(8,128)(2,1)S(1)} %collective-permute-done.10.refs_5_), channel_id=1, source_target_pairs={{0,1},{1,0},{2,3},{3,2},{4,5},{5,4},{6,7},{7,6},{8,9},{9,8},{10,11... | collective-permute-start | bytes 884744 | tf_op jit(solution)/shard_map/ppermute | solution.py:27
  40.5 11.0 %collective-permute-start.17 = (bf16[128,1024]{1,0:T(8,128)(2,1)S(1)}, bf16[128,1024]{1,0:T(8,128)(2,1)S(1)}, u32[]{:S(2)}, u32[]{:S(2)}) collective-permute-start(bf16[128,1024]{1,0:T(8,128)(2,1)S(1)} %collective-permute-done.11.refs_6_), channel_id=1, source_target_pairs={{0,4},{1,5},{2,6},{3,7},{4,8},{5,9},{6,10},{7,11},{8,12},{9,13},{1... | collective-permute-start | bytes 786440 | tf_op jit(solution)/shard_map/ppermute | solution.py:27
  40.6 16.3 %collective-permute-start.16 = (bf16[144,1024]{1,0:T(8,128)(2,1)S(1)}, bf16[144,1024]{1,0:T(8,128)(2,1)S(1)}, u32[]{:S(2)}, u32[]{:S(2)}) collective-permute-start(bf16[144,1024]{1,0:T(8,128)(2,1)S(1)} %collective-permute-done.10.refs_5_), channel_id=1, source_target_pairs={{0,4},{1,5},{2,6},{3,7},{4,8},{5,9},{6,10},{7,11},{8,12},{9,13},{1... | collective-permute-start | bytes 884744 | tf_op jit(solution)/shard_map/ppermute | solution.py:27
  43.2 13.7 %collective-permute-start.25 = (bf16[64,2560]{1,0:T(8,128)(2,1)S(1)}, bf16[64,2560]{1,0:T(8,128)(2,1)S(1)}, u32[]{:S(2)}, u32[]{:S(2)}) collective-permute-start(bf16[64,2560]{1,0:T(8,128)(2,1)S(1)} %get-tuple-element.89), channel_id=1, source_target_pairs={{0,1},{1,0},{2,3},{3,2},{4,5},{5,4},{6,7},{7,6},{8,9},{9,8},{10,11... | collective-permute-start | bytes 983048 | tf_op jit(solution)/shard_map/ppermute | solution.py:27
  43.3 13.7 %collective-permute-start.24 = (bf16[64,2560]{1,0:T(8,128)(2,1)S(1)}, bf16[64,2560]{1,0:T(8,128)(2,1)S(1)}, u32[]{:S(2)}, u32[]{:S(2)}) collective-permute-start(bf16[64,2560]{1,0:T(8,128)(2,1)S(1)} %get-tuple-element.87), channel_id=1, source_target_pairs={{0,1},{1,0},{2,3},{3,2},{4,5},{5,4},{6,7},{7,6},{8,9},{9,8},{10,11... | collective-permute-start | bytes 983048 | tf_op jit(solution)/shard_map/ppermute | solution.py:27
  51.5 7.1 %collective-permute-start.19 = (bf16[128,1024]{1,0:T(8,128)(2,1)S(1)}, bf16[128,1024]{1,0:T(8,128)(2,1)S(1)}, u32[]{:S(2)}, u32[]{:S(2)}) collective-permute-start(bf16[128,1024]{1,0:T(8,128)(2,1)S(1)} %collective-permute-done.17.refs_6_), channel_id=1, source_target_pairs={{0,1},{1,0},{2,3},{3,2},{4,5},{5,4},{6,7},{7,6},{8,9},{9,8},{10,11... | collective-permute-start | bytes 786440 | tf_op jit(solution)/shard_map/ppermute | solution.py:27
  56.9 2.9 %collective-permute-start.18 = (bf16[144,1024]{1,0:T(8,128)(2,1)S(1)}, bf16[144,1024]{1,0:T(8,128)(2,1)S(1)}, u32[]{:S(2)}, u32[]{:S(2)}) collective-permute-start(bf16[144,1024]{1,0:T(8,128)(2,1)S(1)} %collective-permute-done.16.refs_5_), channel_id=1, source_target_pairs={{0,1},{1,0},{2,3},{3,2},{4,5},{5,4},{6,7},{7,6},{8,9},{9,8},{10,11... | collective-permute-start | bytes 884744 | tf_op jit(solution)/shard_map/ppermute | solution.py:27
  56.9 11.6 %collective-permute-start.22 = (bf16[144,1024]{1,0:T(8,128)(2,1)S(1)}, bf16[144,1024]{1,0:T(8,128)(2,1)S(1)}, u32[]{:S(2)}, u32[]{:S(2)}) collective-permute-start(bf16[144,1024]{1,0:T(8,128)(2,1)S(1)} %collective-permute-done.16.refs_5_), channel_id=1, source_target_pairs={{0,4},{1,5},{2,6},{3,7},{4,8},{5,9},{6,10},{7,11},{8,12},{9,13},{1... | collective-permute-start | bytes 884744 | tf_op jit(solution)/shard_map/ppermute | solution.py:27
  56.9 16.8 %collective-permute-start.23 = (bf16[128,1024]{1,0:T(8,128)(2,1)S(1)}, bf16[128,1024]{1,0:T(8,128)(2,1)S(1)}, u32[]{:S(2)}, u32[]{:S(2)}) collective-permute-start(bf16[128,1024]{1,0:T(8,128)(2,1)S(1)} %collective-permute-done.17.refs_6_), channel_id=1, source_target_pairs={{0,4},{1,5},{2,6},{3,7},{4,8},{5,9},{6,10},{7,11},{8,12},{9,13},{1... | collective-permute-start | bytes 786440 | tf_op jit(solution)/shard_map/ppermute | solution.py:27
  57.0 11.5 %collective-permute-start.14 = (bf16[176,512]{1,0:T(8,128)(2,1)S(1)}, bf16[176,512]{1,0:T(8,128)(2,1)S(1)}, u32[]{:S(2)}, u32[]{:S(2)}) collective-permute-start(bf16[176,512]{1,0:T(8,128)(2,1)S(1)} %get-tuple-element.76), channel_id=1, source_target_pairs={{0,2},{1,3},{2,0},{3,1},{4,6},{5,7},{6,4},{7,5},{8,10},{9,11},{10,... | collective-permute-start | bytes 540680 | tf_op jit(solution)/shard_map/ppermute | solution.py:27
  58.6 10.0 %collective-permute-start.15 = (bf16[176,512]{1,0:T(8,128)(2,1)S(1)}, bf16[176,512]{1,0:T(8,128)(2,1)S(1)}, u32[]{:S(2)}, u32[]{:S(2)}) collective-permute-start(bf16[176,512]{1,0:T(8,128)(2,1)S(1)} %get-tuple-element.77), channel_id=1, source_target_pairs={{0,18},{1,19},{2,16},{3,17},{4,22},{5,23},{6,20},{7,21},{8,26},{9,... | collective-permute-start | bytes 540680 | tf_op jit(solution)/shard_map/ppermute | solution.py:27
  68.5 7.8 %collective-permute-start.26 = (bf16[144,1024]{1,0:T(8,128)(2,1)S(1)}, bf16[144,1024]{1,0:T(8,128)(2,1)S(1)}, u32[]{:S(2)}, u32[]{:S(2)}) collective-permute-start(bf16[144,1024]{1,0:T(8,128)(2,1)S(1)} %collective-permute-done.22.refs_5_), channel_id=1, source_target_pairs={{0,1},{1,0},{2,3},{3,2},{4,5},{5,4},{6,7},{7,6},{8,9},{9,8},{10,11... | collective-permute-start | bytes 884744 | tf_op jit(solution)/shard_map/ppermute | solution.py:27
  73.7 8.3 %collective-permute-start.20 = (bf16[176,512]{1,0:T(8,128)(2,1)S(1)}, bf16[176,512]{1,0:T(8,128)(2,1)S(1)}, u32[]{:S(2)}, u32[]{:S(2)}) collective-permute-start(bf16[176,512]{1,0:T(8,128)(2,1)S(1)} %get-tuple-element.82), channel_id=1, source_target_pairs={{0,2},{1,3},{2,0},{3,1},{4,6},{5,7},{6,4},{7,5},{8,10},{9,11},{10,... | collective-permute-start | bytes 540680 | tf_op jit(solution)/shard_map/ppermute | solution.py:27
  75.2 9.9 %collective-permute-start.21 = (bf16[176,512]{1,0:T(8,128)(2,1)S(1)}, bf16[176,512]{1,0:T(8,128)(2,1)S(1)}, u32[]{:S(2)}, u32[]{:S(2)}) collective-permute-start(bf16[176,512]{1,0:T(8,128)(2,1)S(1)} %get-tuple-element.83), channel_id=1, source_target_pairs={{0,18},{1,19},{2,16},{3,17},{4,22},{5,23},{6,20},{7,21},{8,26},{9,... | collective-permute-start | bytes 540680 | tf_op jit(solution)/shard_map/ppermute | solution.py:27
  76.3 11.2 %collective-permute-start.32 = (bf16[16,5120]{1,0:T(8,128)(2,1)S(1)}, bf16[16,5120]{1,0:T(8,128)(2,1)S(1)}, u32[]{:S(2)}, u32[]{:S(2)}) collective-permute-start(bf16[16,5120]{1,0:T(8,128)(2,1)S(1)} %get-tuple-element.102), channel_id=1, source_target_pairs={{0,12},{1,13},{2,14},{3,15},{4,8},{5,9},{6,10},{7,11},{8,4},{9,5},... | collective-permute-start | bytes 491528 | tf_op jit(solution)/shard_map/ppermute | solution.py:27
  76.3 14.5 %collective-permute-start.31 = (bf16[16,5120]{1,0:T(8,128)(2,1)S(1)}, bf16[16,5120]{1,0:T(8,128)(2,1)S(1)}, u32[]{:S(2)}, u32[]{:S(2)}) collective-permute-start(bf16[16,5120]{1,0:T(8,128)(2,1)S(1)} %get-tuple-element.100), channel_id=1, source_target_pairs={{0,8},{1,9},{2,10},{3,11},{4,12},{5,13},{6,14},{7,15},{8,0},{9,1},... | collective-permute-start | bytes 491528 | tf_op jit(solution)/shard_map/ppermute | solution.py:27
  76.4 14.5 %collective-permute-start.30 = (bf16[16,5120]{1,0:T(8,128)(2,1)S(1)}, bf16[16,5120]{1,0:T(8,128)(2,1)S(1)}, u32[]{:S(2)}, u32[]{:S(2)}) collective-permute-start(bf16[16,5120]{1,0:T(8,128)(2,1)S(1)} %get-tuple-element.98), channel_id=1, source_target_pairs={{0,4},{1,5},{2,6},{3,7},{4,0},{5,1},{6,2},{7,3},{8,12},{9,13},{10,... | collective-permute-start | bytes 491528 | tf_op jit(solution)/shard_map/ppermute | solution.py:27
  85.1 8.4 %collective-permute-start.29 = (bf16[176,512]{1,0:T(8,128)(2,1)S(1)}, bf16[176,512]{1,0:T(8,128)(2,1)S(1)}, u32[]{:S(2)}, u32[]{:S(2)}) collective-permute-start(bf16[176,512]{1,0:T(8,128)(2,1)S(1)} %get-tuple-element.96), channel_id=1, source_target_pairs={{0,18},{1,19},{2,16},{3,17},{4,22},{5,23},{6,20},{7,21},{8,26},{9,... | collective-permute-start | bytes 540680 | tf_op jit(solution)/shard_map/ppermute | solution.py:27
  87.0 8.6 %collective-permute-start.28 = (bf16[176,512]{1,0:T(8,128)(2,1)S(1)}, bf16[176,512]{1,0:T(8,128)(2,1)S(1)}, u32[]{:S(2)}, u32[]{:S(2)}) collective-permute-start(bf16[176,512]{1,0:T(8,128)(2,1)S(1)} %get-tuple-element.94), channel_id=1, source_target_pairs={{0,2},{1,3},{2,0},{3,1},{4,6},{5,7},{6,4},{7,5},{8,10},{9,11},{10,... | collective-permute-start | bytes 540680 | tf_op jit(solution)/shard_map/ppermute | solution.py:27
  (9 other events, 48.5 us)

commit v13 on v6

--- a/solution.py
+++ b/solution.py
@@ -135,16 +135,17 @@
                 ref[:, to : to + LANES] = sent[:, j : j + LANES]
 
 
-def frozen_kernel(sizes, k, count, *refs):
+def frozen_kernel(sizes, batch, *refs):
     tokens, groups, holders, replicas, slots, rank = sizes
     g_refs, refs = refs[:groups], refs[groups:]
     down_refs, refs = refs[:replicas], refs[replicas:]
     core, here = lax.axis_index("replica"), lax.axis_index("adapter")
-    if k == 0:
+    rows = down_refs[0].shape[0]
+    half = down_refs[0].shape[1] // holders
+    if batch[0][0] == 0:
         up_refs, refs = refs[:replicas], refs[replicas:]
         sel_ref = refs[-1]
         out_refs = refs[-1 - groups : -1]
-        rows = up_refs[0].shape[0]
         for dg in range(groups):
             for dr in range(replicas):
                 keep = slots_of(g_refs[dg]) == row_slots(holders, replicas, slots, rank, dr)
@@ -155,39 +156,45 @@
     else:
         sel_ref, refs = refs[0], refs[1:]
         out_refs = refs[-groups:]
-    rows = down_refs[0].shape[0]
-    half = down_refs[0].shape[1] // holders
-    shard_at = lax.rem(here + holders - k, holders) * half
-    for j, block in enumerate(refs[:count]):
-        if k == 0:
-            block = block.at[pl.ds(pl.multiple_of(lax.axis_index("groups") * half, half), half)]
-        wide = block.shape[0]
-        at = 0 if count == 1 else lax.rem(core + replicas - j, replicas) * wide
-        columns = pl.ds(pl.multiple_of(shard_at + at, wide), wide)
-        for dg in range(groups):
-            base = rows_by_rows(g_refs[dg][:, :-LANES], block[...]).astype(BF16)
-            lora = 0.0
-            for dr in range(replicas):
-                lora = lora + jnp.dot(
-                    sel_ref[pl.ds(dg * tokens, tokens), dr * rows : (dr + 1) * rows],
-                    down_refs[dr][:, columns],
-                    preferred_element_type=F32,
-                )
-            lora = (ADAPTER_SCALE * lora).astype(BF16)
-            out_refs[dg][:, pl.ds(at if count == 1 else pl.multiple_of(at, wide), wide)] = (
-                base.astype(F32) + lora.astype(F32)
-            ).astype(BF16)
-
-
-def place_kernel(sizes, *refs):
+    for i, (k, spec) in enumerate(batch):
+        shard_at = lax.rem(here + holders - k, holders) * half
+        for (dr, offset), block in zip(spec, refs):
+            if k == 0:
+                first = pl.multiple_of(lax.axis_index("groups") * half, half)
+                block = block.at[pl.ds(first, half)]
+            wide = block.shape[0]
+            at = 0
+            if wide < half:
+                at = lax.rem(core + replicas - dr, replicas) * (half // replicas) + offset
+            columns = pl.ds(pl.multiple_of(shard_at + at, wide), wide)
+            for dg in range(groups):
+                base = rows_by_rows(g_refs[dg][:, :-LANES], block[...]).astype(BF16)
+                lora = 0.0
+                for j in range(replicas):
+                    lora = lora + jnp.dot(
+                        sel_ref[pl.ds(dg * tokens, tokens), j * rows : (j + 1) * rows],
+                        down_refs[j][:, columns],
+                        preferred_element_type=F32,
+                    )
+                lora = (ADAPTER_SCALE * lora).astype(BF16)
+                out_refs[dg][:, pl.ds(pl.multiple_of(i * half + at, wide), wide)] = (
+                    base.astype(F32) + lora.astype(F32)
+                ).astype(BF16)
+        refs = refs[len(spec) :]
+
+
+def place_kernel(sizes, batches, *refs):
     groups, holders, shard, half = sizes
     group, here = lax.axis_index("groups"), lax.axis_index("adapter")
     out_ref = refs[-1]
-    for k in range(holders):
+    for i, batch in enumerate(batches):
         for dg in range(groups):
             source = lax.rem(group + groups - dg, groups)
-            at = lax.rem(here + holders - k, holders) * shard + source * half
-            out_ref[:, pl.ds(pl.multiple_of(at, half), half)] = refs[k * groups + dg][...]
+            for j, k in enumerate(batch):
+                at = lax.rem(here + holders - k, holders) * shard + source * half
+                out_ref[:, pl.ds(pl.multiple_of(at, half), half)] = refs[i * groups + dg][
+                    :, j * half : (j + 1) * half
+                ]
 
 
 def chip_kernel(replicas, *refs):
@@ -280,28 +287,28 @@
     for dr in range(1, replicas):
         ups.append(moved(ups[0], lambda g, z, s, r: (g, z, s, r + dr)))
         downs.append(moved(downs[0], lambda g, z, s, r: (g, z, s, r + dr)))
-    others = [moved(downs[0], lambda g, z, s, r: (g + dg, z, s, r)) for dg in range(1, groups)]
     def pieces_of(k, *before):
         if k == 0:
-            return [frozen]
+            return [(0, 0)], [frozen]
         block = after(ring[k], *before) if before else ring[k]
+        spec = [(dr, 0) for dr in range(replicas)]
         pieces = [block] + [
             moved(block, lambda g, z, s, r: (g, z, s, r + dr)) for dr in range(1, replicas)
         ]
         if piece % LANES:
             whole = jnp.zeros((half, value_width), BF16)
-            for dr in range(replicas):
-                at = ((core - dr) % replicas) * piece
-                whole = lax.dynamic_update_slice_in_dim(whole, pieces[dr], at, axis=0)
-            pieces = [whole]
-        return pieces
+            for (dr, offset), part in zip(spec, pieces):
+                at = ((core - dr) % replicas) * piece + offset
+                whole = lax.dynamic_update_slice_in_dim(whole, part, at, axis=0)
+            spec, pieces = [(0, 0)], [whole]
+        return spec, pieces
 
     kept = replicas * holders * rows
 
-    def adapter_sums(sel):
+    def adapter_sums(sel, *before):
         maps = list(downs)
-        for other in others:
-            maps.append(after(other, sel))
+        for dg in range(1, groups):
+            maps.append(moved(downs[0], lambda g, z, s, r: (g + dg, z, s, r)))
             for dr in range(1, replicas):
                 maps.append(moved(maps[-dr], lambda g, z, s, r: (g, z, s, r + dr)))
         gradients = call(
@@ -313,7 +320,7 @@
         )
         part, sent = gradients[0], gradients[1:]
         came = [
-            moved(sent[2 * dr - 2 + j], lambda g, z, s, r: (g, z, s, r - dr))
+            moved(after(sent[2 * dr - 2 + j], *before), lambda g, z, s, r: (g, z, s, r - dr))
             for dr in range(1, replicas)
             for j in range(2)
         ]
@@ -325,36 +332,38 @@
         )
         return part, chip
 
-    arrived, outs = [], []
-    for k in range(holders):
-        if k > 1:
-            last = ring[-1]
-            if k > 2:
-                last = after(last, *outs[k - 2], part)
-            ring.append(moved(last, lambda g, z, s, r: (g, z + 1, s, r)))
-        gate = [*arrived[k - 2], *outs[k - 1]] if k > 1 else []
-        blocks = pieces_of(k, *gate, *(chip[:1] if k > 2 else ()))
-        tokens_in = [after(tagged, part), *grads[1:]] if k == 1 else grads
+    batches = [list(range(min(2, holders)))] + [[k] for k in range(2, holders)]
+    arrived = []
+    for i, batch in enumerate(batches):
+        operands, specs = [], []
+        for k in batch:
+            if k > 1:
+                last = after(ring[-1], sel) if k > 2 else ring[-1]
+                ring.append(moved(last, lambda g, z, s, r: (g, z + 1, s, r)))
+            gate = arrived[0] if k == 2 else [*arrived[i - 2], chip[0]] if k > 2 else []
+            spec, blocks = pieces_of(k, *gate)
+            specs.append((k, spec))
+            operands += blocks
         out = call(
             functools.partial(
-                frozen_kernel, (tokens, groups, holders, replicas, slots, rank), k, len(blocks)
+                frozen_kernel, (tokens, groups, holders, replicas, slots, rank), specs
             ),
-            [jax.ShapeDtypeStruct((tokens, half), BF16)] * groups
-            + [jax.ShapeDtypeStruct((groups * tokens, kept), BF16)] * (k == 0),
-            [*tokens_in, *downs, *([sel] if k else ups), *blocks],
+            [jax.ShapeDtypeStruct((tokens, half * len(batch)), BF16)] * groups
+            + [jax.ShapeDtypeStruct((groups * tokens, kept), BF16)] * (i == 0),
+            [*grads, *downs, *([sel] if i else ups), *operands],
         )
-        if k == 0:
+        if i == 0:
             sel = out[groups]
-            part, chip = adapter_sums(sel)
-        outs.append(list(out[:groups]))
-        mails = outs[-1]
-        if k > 2:
+        mails = list(out[:groups])
+        if i > 1:
             mails = [after(mail, *arrived[-1]) for mail in mails]
         arrived.append(
             [moved(mails[dg], lambda g, z, s, r: (g + dg, z, s - 1, r)) for dg in range(groups)]
         )
+        if i == 0:
+            part, chip = adapter_sums(sel, *arrived[0])
     passed = call(
-        functools.partial(place_kernel, (groups, holders, shard, half)),
+        functools.partial(place_kernel, (groups, holders, shard, half), batches),
         [jax.ShapeDtypeStruct((tokens, width), BF16)],
         [x for got in arrived for x in got],
     )[0]

time: 85.4 us -> 81.3 us (0.952)
  starting transfers between devices: 32.1 us -> 26.8 us
  waiting for transfers between devices: 38.1 us -> 39.6 us
    ppermute x28 -> x26, starting transfers between devices: 32.1 us -> 26.8 us  [moved(): return lax.ppermute(x, AXES, pairs)]
    ppermute x28 -> x26, waiting for transfers between devices: 38.1 us -> 39.6 us  [moved(): return lax.ppermute(x, AXES, pairs)]
    pallas_call x12 -> x11, Pallas kernels: 8.79 us -> 8.53 us  [call(): pl.pallas_call(kernel, out_shape=out_shape, in_specs=[pl.BlockSpec(memory...]
  transfers between devices with their start and end apart: 28 -> 26, of which waited for: 14 -> 14; matrix products, arithmetic and copies ran while one was open for 0% -> 0% of each run, Pallas kernels for 9% -> 9%
where the time goes in v13:
time: 81.3 us; the launch traced here: 81.1 us
  waiting for transfers between devices  39.6 us (49%)
  starting transfers between devices  26.8 us (33%)
  Pallas kernels  8.53 us (10%)
  local copies, waits for them, and re-layouts  5.34 us (7%)
    ppermute x26, waiting for transfers between devices, moved(): return lax.ppermute(x, AXES, pairs)  39.6 us
    ppermute x26, starting transfers between devices, moved(): return lax.ppermute(x, AXES, pairs)  26.8 us
    pallas_call x11, Pallas kernels, call(): pl.pallas_call(kernel, out_shape=out_shape, in_specs=[pl.BlockSpec(memory...  8.53 us
    unnamed x14, local copies, waits for them, and re-layouts  4.12 us
  transfers between devices with their start and end apart: 26, of which 14 were waited for; matrix products, arithmetic and copies ran while one was open for 0% of the time, Pallas kernels for 9%

profile of v13, /device:TPU:0, one launch (start us, length us, event | category | flops | bytes accessed | tf_op | source)
XLA Modules:
  0.0 81.1 jit_solution(17323304214375560719)
XLA Ops:
  0.6 1.2 %dynamic-slice_bitcast_fusion = bf16[256,1024]{1,0:T(8,128)(2,1)S(1)} fusion(bf16[1,1024,1024]{2,1,0:T(8,128)(2,1)} %param.11, s32[]{:T(128)S(6)} %select_n.3), kind=kLoop, calls=%fused_computation | loop fusion | bytes 1048580 | tf_op jit(solution)/shard_map/dynamic_slice | solution.py:275
  1.9 3.1 %collective-permute-start.4 = (bf16[256,1024]{1,0:T(8,128)(2,1)S(1)}, bf16[256,1024]{1,0:T(8,128)(2,1)S(1)}, u32[]{:S(2)}, u32[]{:S(2)}) collective-permute-start(bf16[256,1024]{1,0:T(8,128)(2,1)S(1)} %dynamic-slice_bitcast_fusion), channel_id=1, source_target_pairs={{0,4},{1,5},{2,6},{3,7},{4,8},{5,9},{6,10},{7,11},{8,12},{9,13},{1... | collective-permute-start | bytes 1572872 | tf_op jit(solution)/shard_map/ppermute | solution.py:24
  5.0 1.0 %copy-done.2 = bf16[1,176,1024]{2,1,0:T(8,128)(2,1)S(1)} copy-done((bf16[1,176,1024]{2,1,0:T(8,128)(2,1)S(1)}, bf16[1,176,1024]{2,1,0:T(8,128)(2,1)}, u32[]{:S(2)}) %copy-start.2) | copy-done | bytes 360472
  8.0 1.6 %collective-permute-start.3 = (bf16[176,1152]{1,0:T(8,128)(2,1)S(1)}, bf16[176,1152]{1,0:T(8,128)(2,1)S(1)}, u32[]{:S(2)}, u32[]{:S(2)}) collective-permute-start(bf16[176,1152]{1,0:T(8,128)(2,1)S(1)} %shard_map.95.refs_0_.refs_1_), channel_id=1, source_target_pairs={{0,16},{1,17},{2,18},{3,19},{4,20},{5,21},{6,22},{7,23},{8,24},{9,... | collective-permute-start | bytes 1216520 | tf_op jit(solution)/shard_map/ppermute | solution.py:24
  11.4 1.6 %collective-permute-start = (bf16[16,3072]{1,0:T(8,128)(2,1)S(1)}, bf16[16,3072]{1,0:T(8,128)(2,1)S(1)}, u32[]{:S(2)}, u32[]{:S(2)}) collective-permute-start(bf16[16,3072]{1,0:T(8,128)(2,1)S(1)} %shard_map.94.refs_0_), channel_id=1, source_target_pairs={{0,4},{1,5},{2,6},{3,7},{4,8},{5,9},{6,10},{7,11},{8,12},{9,13},{1... | collective-permute-start | bytes 294920 | tf_op jit(solution)/shard_map/ppermute | solution.py:24
  13.1 1.2 %collective-permute-start.1 = (bf16[16,3072]{1,0:T(8,128)(2,1)S(1)}, bf16[16,3072]{1,0:T(8,128)(2,1)S(1)}, u32[]{:S(2)}, u32[]{:S(2)}) collective-permute-start(bf16[16,3072]{1,0:T(8,128)(2,1)S(1)} %shard_map.94.refs_0_), channel_id=1, source_target_pairs={{0,8},{1,9},{2,10},{3,11},{4,12},{5,13},{6,14},{7,15},{8,0},{9,1},... | collective-permute-start | bytes 294920 | tf_op jit(solution)/shard_map/ppermute | solution.py:24
  14.3 2.7 %collective-permute-start.2 = (bf16[16,3072]{1,0:T(8,128)(2,1)S(1)}, bf16[16,3072]{1,0:T(8,128)(2,1)S(1)}, u32[]{:S(2)}, u32[]{:S(2)}) collective-permute-start(bf16[16,3072]{1,0:T(8,128)(2,1)S(1)} %shard_map.94.refs_0_), channel_id=1, source_target_pairs={{0,12},{1,13},{2,14},{3,15},{4,0},{5,1},{6,2},{7,3},{8,4},{9,5},{1... | collective-permute-start | bytes 294920 | tf_op jit(solution)/shard_map/ppermute | solution.py:24
  17.0 5.0 %collective-permute-done.refs_1_ = bf16[16,3072]{1,0:T(8,128)(2,1)S(1)} collective-permute-done((bf16[16,3072]{1,0:T(8,128)(2,1)S(1)}, bf16[16,3072]{1,0:T(8,128)(2,1)S(1)}, u32[]{:S(2)}, u32[]{:S(2)}) %collective-permute-start) | collective-permute-done | bytes 98336 | tf_op jit(solution)/shard_map/ppermute | solution.py:24
  22.0 3.4 %collective-permute-done.1.refs_2_ = bf16[16,3072]{1,0:T(8,128)(2,1)S(1)} collective-permute-done((bf16[16,3072]{1,0:T(8,128)(2,1)S(1)}, bf16[16,3072]{1,0:T(8,128)(2,1)S(1)}, u32[]{:S(2)}, u32[]{:S(2)}) %collective-permute-start.1) | collective-permute-done | bytes 98336 | tf_op jit(solution)/shard_map/ppermute | solution.py:24
  25.4 2.6 %collective-permute-start.10 = (bf16[256,1024]{1,0:T(8,128)(2,1)S(1)}, bf16[256,1024]{1,0:T(8,128)(2,1)S(1)}, u32[]{:S(2)}, u32[]{:S(2)}) collective-permute-start(bf16[256,1024]{1,0:T(8,128)(2,1)S(1)} %collective-permute-done.4.refs_7_), channel_id=1, source_target_pairs={{0,4},{1,5},{2,6},{3,7},{4,8},{5,9},{6,10},{7,11},{8,12},{9,13},{1... | collective-permute-start | bytes 1572872 | tf_op jit(solution)/shard_map/ppermute | solution.py:24
  28.3 1.5 %collective-permute-start.15 = (bf16[64,2048]{1,0:T(8,128)(2,1)S(1)}, bf16[64,2048]{1,0:T(8,128)(2,1)S(1)}, u32[]{:S(2)}, u32[]{:S(2)}) collective-permute-start(bf16[64,2048]{1,0:T(8,128)(2,1)S(1)} %get-tuple-element.44.refs_2_.refs_3_), channel_id=1, source_target_pairs={{0,16},{1,17},{2,18},{3,19},{4,20},{5,21},{6,22},{7,23},{8,24},{9,... | collective-permute-start | bytes 786440 | tf_op jit(solution)/shard_map/ppermute | solution.py:24
  29.8 1.3 %collective-permute-done.6.refs_5_ = bf16[64,1024]{1,0:T(8,128)(2,1)S(1)} collective-permute-done((bf16[64,1024]{1,0:T(8,128)(2,1)S(1)}, bf16[64,1024]{1,0:T(8,128)(2,1)S(1)}, u32[]{:S(2)}, u32[]{:S(2)}) %collective-permute-start.6) | collective-permute-done | bytes 131104 | tf_op jit(solution)/shard_map/ppermute | solution.py:24
  31.2 2.2 %shard_map.97 = (bf16[176,1024]{1,0:T(8,128)(2,1)S(1)}, bf16[176,1024]{1,0:T(8,128)(2,1)S(1)}, bf16[352,128]{1,0:T(8,128)(2,1)S(1)}) custom-call(bf16[176,1152]{1,0:T(8,128)(2,1)S(1)} %shard_map.95.refs_0_.refs_1_, bf16[176,1152]{1,0:T(8,128)(2,1)S(1)} %collective-permute-done.3.refs_1_, bf16[64,2048]{1,0:T(8,128)(2,1)S(1)} %get-tuple-element.44.refs_2_.refs_3_, ...), custom_call_target="tpu_custom_call" | custom-call | flops 1000 | bytes 1000 | tf_op jit(solution)/shard_map/pallas_call | solution.py:41
  33.4 1.6 %collective-permute-start.8 = (bf16[176,1024]{1,0:T(8,128)(2,1)S(1)}, bf16[176,1024]{1,0:T(8,128)(2,1)S(1)}, u32[]{:S(2)}, u32[]{:S(2)}) collective-permute-start(bf16[176,1024]{1,0:T(8,128)(2,1)S(1)} %get-tuple-element.47), channel_id=1, source_target_pairs={{0,2},{1,3},{2,0},{3,1},{4,6},{5,7},{6,4},{7,5},{8,10},{9,11},{10,... | collective-permute-start | bytes 1081352 | tf_op jit(solution)/shard_map/ppermute | solution.py:24
  35.4 1.4 %collective-permute-done.15.refs_5_ = bf16[64,2048]{1,0:T(8,128)(2,1)S(1)} collective-permute-done((bf16[64,2048]{1,0:T(8,128)(2,1)S(1)}, bf16[64,2048]{1,0:T(8,128)(2,1)S(1)}, u32[]{:S(2)}, u32[]{:S(2)}) %collective-permute-start.15) | collective-permute-done | bytes 262176 | tf_op jit(solution)/shard_map/ppermute | solution.py:24
  36.8 4.8 %collective-permute-done.10.refs_5_ = bf16[256,1024]{1,0:T(8,128)(2,1)S(1)} collective-permute-done((bf16[256,1024]{1,0:T(8,128)(2,1)S(1)}, bf16[256,1024]{1,0:T(8,128)(2,1)S(1)}, u32[]{:S(2)}, u32[]{:S(2)}) %collective-permute-start.10) | collective-permute-done | bytes 524320 | tf_op jit(solution)/shard_map/ppermute | solution.py:24
  42.3 1.3 %shard_map.99 = (f32[64,5120]{1,0:T(8,128)S(1)}, bf16[64,2560]{1,0:T(8,128)(2,1)S(1)}, bf16[64,2560]{1,0:T(8,128)(2,1)S(1)}) custom-call(bf16[176,4096]{1,0:T(8,128)(2,1)S(1)} %bitcast.12, bf16[176,1152]{1,0:T(8,128)(2,1)S(1)} %shard_map.95.refs_0_.refs_1_, bf16[352,128]{1,0:T(8,128)(2,1)S(1)} %get-tuple-element.49.refs_4_.refs_2_, ...), custom_call_target="tpu_custom_call" | custom-call | flops 1000 | bytes 1000 | tf_op jit(solution)/shard_map/pallas_call | solution.py:41
  43.6 1.2 %collective-permute-done.8.refs_0_ = bf16[176,1024]{1,0:T(8,128)(2,1)S(1)} collective-permute-done((bf16[176,1024]{1,0:T(8,128)(2,1)S(1)}, bf16[176,1024]{1,0:T(8,128)(2,1)S(1)}, u32[]{:S(2)}, u32[]{:S(2)}) %collective-permute-start.8) | collective-permute-done | bytes 360480 | tf_op jit(solution)/shard_map/ppermute | solution.py:24
  44.7 6.9 %collective-permute-done.9.refs_1_ = bf16[176,1024]{1,0:T(8,128)(2,1)S(1)} collective-permute-done((bf16[176,1024]{1,0:T(8,128)(2,1)S(1)}, bf16[176,1024]{1,0:T(8,128)(2,1)S(1)}, u32[]{:S(2)}, u32[]{:S(2)}) %collective-permute-start.9) | collective-permute-done | bytes 360480 | tf_op jit(solution)/shard_map/ppermute | solution.py:24
  52.1 1.1 %collective-permute-done.18.refs_2_ = bf16[64,2560]{1,0:T(8,128)(2,1)S(1)} collective-permute-done((bf16[64,2560]{1,0:T(8,128)(2,1)S(1)}, bf16[64,2560]{1,0:T(8,128)(2,1)S(1)}, u32[]{:S(2)}, u32[]{:S(2)}) %collective-permute-start.18) | collective-permute-done | bytes 327712 | tf_op jit(solution)/shard_map/ppermute | solution.py:24
  53.9 3.1 %collective-permute-done.14.refs_5_ = bf16[256,1024]{1,0:T(8,128)(2,1)S(1)} collective-permute-done((bf16[256,1024]{1,0:T(8,128)(2,1)S(1)}, bf16[256,1024]{1,0:T(8,128)(2,1)S(1)}, u32[]{:S(2)}, u32[]{:S(2)}) %collective-permute-start.14) | collective-permute-done | bytes 524320 | tf_op jit(solution)/shard_map/ppermute | solution.py:24
  57.0 1.0 %shard_map.98 = (bf16[176,512]{1,0:T(8,128)(2,1)S(1)}, bf16[176,512]{1,0:T(8,128)(2,1)S(1)}) custom-call(bf16[176,1152]{1,0:T(8,128)(2,1)S(1)} %shard_map.95.refs_0_.refs_1_, bf16[176,1152]{1,0:T(8,128)(2,1)S(1)} %collective-permute-done.3.refs_1_, bf16[64,2048]{1,0:T(8,128)(2,1)S(1)} %get-tuple-element.44.refs_2_.refs_3_, ...), custom_call_target="tpu_custom_call" | custom-call | flops 1000 | bytes 1000 | tf_op jit(solution)/shard_map/pallas_call | solution.py:41
  58.0 1.6 %collective-permute-start.12 = (bf16[176,512]{1,0:T(8,128)(2,1)S(1)}, bf16[176,512]{1,0:T(8,128)(2,1)S(1)}, u32[]{:S(2)}, u32[]{:S(2)}) collective-permute-start(bf16[176,512]{1,0:T(8,128)(2,1)S(1)} %get-tuple-element.51), channel_id=1, source_target_pairs={{0,2},{1,3},{2,0},{3,1},{4,6},{5,7},{6,4},{7,5},{8,10},{9,11},{10,... | collective-permute-start | bytes 540680 | tf_op jit(solution)/shard_map/ppermute | solution.py:24
  59.5 1.5 %collective-permute-start.13 = (bf16[176,512]{1,0:T(8,128)(2,1)S(1)}, bf16[176,512]{1,0:T(8,128)(2,1)S(1)}, u32[]{:S(2)}, u32[]{:S(2)}) collective-permute-start(bf16[176,512]{1,0:T(8,128)(2,1)S(1)} %get-tuple-element.52), channel_id=1, source_target_pairs={{0,18},{1,19},{2,16},{3,17},{4,22},{5,23},{6,20},{7,21},{8,26},{9,... | collective-permute-start | bytes 540680 | tf_op jit(solution)/shard_map/ppermute | solution.py:24
  61.5 3.4 %collective-permute-start.22 = (bf16[16,5120]{1,0:T(8,128)(2,1)S(1)}, bf16[16,5120]{1,0:T(8,128)(2,1)S(1)}, u32[]{:S(2)}, u32[]{:S(2)}) collective-permute-start(bf16[16,5120]{1,0:T(8,128)(2,1)S(1)} %get-tuple-element.66), channel_id=1, source_target_pairs={{0,12},{1,13},{2,14},{3,15},{4,0},{5,1},{6,2},{7,3},{8,4},{9,5},{1... | collective-permute-start | bytes 491528 | tf_op jit(solution)/shard_map/ppermute | solution.py:24
  64.9 1.0 %shard_map.101 = (bf16[176,512]{1,0:T(8,128)(2,1)S(1)}, bf16[176,512]{1,0:T(8,128)(2,1)S(1)}) custom-call(bf16[176,1152]{1,0:T(8,128)(2,1)S(1)} %shard_map.95.refs_0_.refs_1_, bf16[176,1152]{1,0:T(8,128)(2,1)S(1)} %collective-permute-done.3.refs_1_, bf16[64,2048]{1,0:T(8,128)(2,1)S(1)} %get-tuple-element.44.refs_2_.refs_3_, ...), custom_call_target="tpu_custom_call" | custom-call | flops 1000 | bytes 1000 | tf_op jit(solution)/shard_map/pallas_call | solution.py:41
  65.9 3.9 %collective-permute-done.13.refs_3_ = bf16[176,512]{1,0:T(8,128)(2,1)S(1)} collective-permute-done((bf16[176,512]{1,0:T(8,128)(2,1)S(1)}, bf16[176,512]{1,0:T(8,128)(2,1)S(1)}, u32[]{:S(2)}, u32[]{:S(2)}) %collective-permute-start.13) | collective-permute-done | bytes 180256 | tf_op jit(solution)/shard_map/ppermute | solution.py:24
  69.8 1.4 %collective-permute-start.21 = (bf16[176,512]{1,0:T(8,128)(2,1)S(1)}, bf16[176,512]{1,0:T(8,128)(2,1)S(1)}, u32[]{:S(2)}, u32[]{:S(2)}) collective-permute-start(bf16[176,512]{1,0:T(8,128)(2,1)S(1)} %get-tuple-element.64), channel_id=1, source_target_pairs={{0,18},{1,19},{2,16},{3,17},{4,22},{5,23},{6,20},{7,21},{8,26},{9,... | collective-permute-start | bytes 540680 | tf_op jit(solution)/shard_map/ppermute | solution.py:24
  71.8 4.2 %collective-permute-done.23.refs_2_ = bf16[16,5120]{1,0:T(8,128)(2,1)S(1)} collective-permute-done((bf16[16,5120]{1,0:T(8,128)(2,1)S(1)}, bf16[16,5120]{1,0:T(8,128)(2,1)S(1)}, u32[]{:S(2)}, u32[]{:S(2)}) %collective-permute-start.23) | collective-permute-done | bytes 163872 | tf_op jit(solution)/shard_map/ppermute | solution.py:24
  76.2 1.4 %collective-permute-done.25.refs_1_ = bf16[16,5120]{1,0:T(8,128)(2,1)S(1)} collective-permute-done((bf16[16,5120]{1,0:T(8,128)(2,1)S(1)}, bf16[16,5120]{1,0:T(8,128)(2,1)S(1)}, u32[]{:S(2)}, u32[]{:S(2)}) %collective-permute-start.25) | collective-permute-done | bytes 163872 | tf_op jit(solution)/shard_map/ppermute | solution.py:24
  78.4 1.5 %collective-permute-done.20.refs_4_ = bf16[176,512]{1,0:T(8,128)(2,1)S(1)} collective-permute-done((bf16[176,512]{1,0:T(8,128)(2,1)S(1)}, bf16[176,512]{1,0:T(8,128)(2,1)S(1)}, u32[]{:S(2)}, u32[]{:S(2)}) %collective-permute-start.20) | collective-permute-done | bytes 180256 | tf_op jit(solution)/shard_map/ppermute | solution.py:24
  79.8 1.2 %shard_map.102 = bf16[176,4096]{1,0:T(8,128)(2,1)} custom-call(bf16[176,1024]{1,0:T(8,128)(2,1)S(1)} %collective-permute-done.8.refs_0_, bf16[176,1024]{1,0:T(8,128)(2,1)S(1)} %collective-permute-done.9.refs_1_, bf16[176,512]{1,0:T(8,128)(2,1)S(1)} %collective-permute-done.12.refs_2_, bf16[176,512]{1,0:T(8,128)(2,1)S(1)} %collective-permute-done.13.refs_3_, ...), custom_call_target="tpu_custom_call" | custom-call | flops 1000 | bytes 1000 | tf_op jit(solution)/shard_map/pallas_call | solution.py:41
  (46 shorter events, 8.5 us)
Async XLA Ops:
  0.6 30.5 %copy-start = (bf16[1,1024,1024]{2,1,0:T(8,128)(2,1)S(1)}, bf16[1,1024,1024]{2,1,0:T(8,128)(2,1)}, u32[]{:S(2)}) copy-start(bf16[1,1024,1024]{2,1,0:T(8,128)(2,1)} %param.11) | copy-start | bytes 6291460
  1.9 23.5 %collective-permute-start.4 = (bf16[256,1024]{1,0:T(8,128)(2,1)S(1)}, bf16[256,1024]{1,0:T(8,128)(2,1)S(1)}, u32[]{:S(2)}, u32[]{:S(2)}) collective-permute-start(bf16[256,1024]{1,0:T(8,128)(2,1)S(1)} %dynamic-slice_bitcast_fusion), channel_id=1, source_target_pairs={{0,4},{1,5},{2,6},{3,7},{4,8},{5,9},{6,10},{7,11},{8,12},{9,13},{1... | collective-permute-start | bytes 1572872 | tf_op jit(solution)/shard_map/ppermute | solution.py:24
  5.0 1.0 %copy-start.2 = (bf16[1,176,1024]{2,1,0:T(8,128)(2,1)S(1)}, bf16[1,176,1024]{2,1,0:T(8,128)(2,1)}, u32[]{:S(2)}) copy-start(bf16[1,176,1024]{2,1,0:T(8,128)(2,1)} %param.8) | copy-start | bytes 1081348
  5.9 0.7 copy-start.5
  8.0 17.3 %collective-permute-start.3 = (bf16[176,1152]{1,0:T(8,128)(2,1)S(1)}, bf16[176,1152]{1,0:T(8,128)(2,1)S(1)}, u32[]{:S(2)}, u32[]{:S(2)}) collective-permute-start(bf16[176,1152]{1,0:T(8,128)(2,1)S(1)} %shard_map.95.refs_0_.refs_1_), channel_id=1, source_target_pairs={{0,16},{1,17},{2,18},{3,19},{4,20},{5,21},{6,22},{7,23},{8,24},{9,... | collective-permute-start | bytes 1216520 | tf_op jit(solution)/shard_map/ppermute | solution.py:24
  9.6 0.9 %copy-start.3 = (bf16[1,2,16,4096]{3,2,1,0:T(8,128)(2,1)S(1)}, bf16[1,2,16,4096]{3,2,1,0:T(8,128)(2,1)}, u32[]{:S(2)}) copy-start(bf16[1,2,16,4096]{3,2,1,0:T(8,128)(2,1)} %param.12) | copy-start | bytes 786436
  10.6 0.8 %copy-start.4 = (bf16[1,2,16,1024]{3,2,1,0:T(8,128)(2,1)S(1)}, bf16[1,2,16,1024]{3,2,1,0:T(8,128)(2,1)}, u32[]{:S(2)}) copy-start(bf16[1,2,16,1024]{3,2,1,0:T(8,128)(2,1)} %param.13) | copy-start | bytes 196612
  11.4 10.5 %collective-permute-start = (bf16[16,3072]{1,0:T(8,128)(2,1)S(1)}, bf16[16,3072]{1,0:T(8,128)(2,1)S(1)}, u32[]{:S(2)}, u32[]{:S(2)}) collective-permute-start(bf16[16,3072]{1,0:T(8,128)(2,1)S(1)} %shard_map.94.refs_0_), channel_id=1, source_target_pairs={{0,4},{1,5},{2,6},{3,7},{4,8},{5,9},{6,10},{7,11},{8,12},{9,13},{1... | collective-permute-start | bytes 294920 | tf_op jit(solution)/shard_map/ppermute | solution.py:24
  13.1 12.3 %collective-permute-start.1 = (bf16[16,3072]{1,0:T(8,128)(2,1)S(1)}, bf16[16,3072]{1,0:T(8,128)(2,1)S(1)}, u32[]{:S(2)}, u32[]{:S(2)}) collective-permute-start(bf16[16,3072]{1,0:T(8,128)(2,1)S(1)} %shard_map.94.refs_0_), channel_id=1, source_target_pairs={{0,8},{1,9},{2,10},{3,11},{4,12},{5,13},{6,14},{7,15},{8,0},{9,1},... | collective-permute-start | bytes 294920 | tf_op jit(solution)/shard_map/ppermute | solution.py:24
  14.3 11.1 %collective-permute-start.2 = (bf16[16,3072]{1,0:T(8,128)(2,1)S(1)}, bf16[16,3072]{1,0:T(8,128)(2,1)S(1)}, u32[]{:S(2)}, u32[]{:S(2)}) collective-permute-start(bf16[16,3072]{1,0:T(8,128)(2,1)S(1)} %shard_map.94.refs_0_), channel_id=1, source_target_pairs={{0,12},{1,13},{2,14},{3,15},{4,0},{5,1},{6,2},{7,3},{8,4},{9,5},{1... | collective-permute-start | bytes 294920 | tf_op jit(solution)/shard_map/ppermute | solution.py:24
  25.4 5.8 %collective-permute-start.7 = (bf16[256,1024]{1,0:T(8,128)(2,1)S(1)}, bf16[256,1024]{1,0:T(8,128)(2,1)S(1)}, u32[]{:S(2)}, u32[]{:S(2)}) collective-permute-start(bf16[256,1024]{1,0:T(8,128)(2,1)S(1)} %collective-permute-done.4.refs_7_), channel_id=1, source_target_pairs={{0,1},{1,0},{2,3},{3,2},{4,5},{5,4},{6,7},{7,6},{8,9},{9,8},{10,11... | collective-permute-start | bytes 1572872 | tf_op jit(solution)/shard_map/ppermute | solution.py:24
  25.4 16.2 %collective-permute-start.10 = (bf16[256,1024]{1,0:T(8,128)(2,1)S(1)}, bf16[256,1024]{1,0:T(8,128)(2,1)S(1)}, u32[]{:S(2)}, u32[]{:S(2)}) collective-permute-start(bf16[256,1024]{1,0:T(8,128)(2,1)S(1)} %collective-permute-done.4.refs_7_), channel_id=1, source_target_pairs={{0,4},{1,5},{2,6},{3,7},{4,8},{5,9},{6,10},{7,11},{8,12},{9,13},{1... | collective-permute-start | bytes 1572872 | tf_op jit(solution)/shard_map/ppermute | solution.py:24
  28.0 3.1 %collective-permute-start.5 = (bf16[64,2048]{1,0:T(8,128)(2,1)S(1)}, bf16[64,2048]{1,0:T(8,128)(2,1)S(1)}, u32[]{:S(2)}, u32[]{:S(2)}) collective-permute-start(bf16[64,2048]{1,0:T(8,128)(2,1)S(1)} %get-tuple-element.44.refs_2_.refs_3_), channel_id=1, source_target_pairs={{0,1},{1,0},{2,3},{3,2},{4,5},{5,4},{6,7},{7,6},{8,9},{9,8},{10,11... | collective-permute-start | bytes 786440 | tf_op jit(solution)/shard_map/ppermute | solution.py:24
  28.3 8.6 %collective-permute-start.15 = (bf16[64,2048]{1,0:T(8,128)(2,1)S(1)}, bf16[64,2048]{1,0:T(8,128)(2,1)S(1)}, u32[]{:S(2)}, u32[]{:S(2)}) collective-permute-start(bf16[64,2048]{1,0:T(8,128)(2,1)S(1)} %get-tuple-element.44.refs_2_.refs_3_), channel_id=1, source_target_pairs={{0,16},{1,17},{2,18},{3,19},{4,20},{5,21},{6,22},{7,23},{8,24},{9,... | collective-permute-start | bytes 786440 | tf_op jit(solution)/shard_map/ppermute | solution.py:24
  29.8 1.3 %collective-permute-start.6 = (bf16[64,1024]{1,0:T(8,128)(2,1)S(1)}, bf16[64,1024]{1,0:T(8,128)(2,1)S(1)}, u32[]{:S(2)}, u32[]{:S(2)}) collective-permute-start(bf16[64,1024]{1,0:T(8,128)(2,1)S(1)} %get-tuple-element.45.refs_4_), channel_id=1, source_target_pairs={{0,1},{1,0},{2,3},{3,2},{4,5},{5,4},{6,7},{7,6},{8,9},{9,8},{10,11... | collective-permute-start | bytes 393224 | tf_op jit(solution)/shard_map/ppermute | solution.py:24
  31.1 11.1 %copy-start.1 = (bf16[1,176,4096]{2,1,0:T(8,128)(2,1)S(1)}, bf16[1,176,4096]{2,1,0:T(8,128)(2,1)}, u32[]{:S(2)}) copy-start(bf16[1,176,4096]{2,1,0:T(8,128)(2,1)} %param.7) | copy-start | bytes 4325380
  33.4 11.3 %collective-permute-start.8 = (bf16[176,1024]{1,0:T(8,128)(2,1)S(1)}, bf16[176,1024]{1,0:T(8,128)(2,1)S(1)}, u32[]{:S(2)}, u32[]{:S(2)}) collective-permute-start(bf16[176,1024]{1,0:T(8,128)(2,1)S(1)} %get-tuple-element.47), channel_id=1, source_target_pairs={{0,2},{1,3},{2,0},{3,1},{4,6},{5,7},{6,4},{7,5},{8,10},{9,11},{10,... | collective-permute-start | bytes 1081352 | tf_op jit(solution)/shard_map/ppermute | solution.py:24
  35.0 16.6 %collective-permute-start.9 = (bf16[176,1024]{1,0:T(8,128)(2,1)S(1)}, bf16[176,1024]{1,0:T(8,128)(2,1)S(1)}, u32[]{:S(2)}, u32[]{:S(2)}) collective-permute-start(bf16[176,1024]{1,0:T(8,128)(2,1)S(1)} %get-tuple-element.48), channel_id=1, source_target_pairs={{0,18},{1,19},{2,16},{3,17},{4,22},{5,23},{6,20},{7,21},{8,26},{9,... | collective-permute-start | bytes 1081352 | tf_op jit(solution)/shard_map/ppermute | solution.py:24
  36.8 5.5 %collective-permute-start.16 = (bf16[64,2048]{1,0:T(8,128)(2,1)S(1)}, bf16[64,2048]{1,0:T(8,128)(2,1)S(1)}, u32[]{:S(2)}, u32[]{:S(2)}) collective-permute-start(bf16[64,2048]{1,0:T(8,128)(2,1)S(1)} %collective-permute-done.15.refs_5_), channel_id=1, source_target_pairs={{0,1},{1,0},{2,3},{3,2},{4,5},{5,4},{6,7},{7,6},{8,9},{9,8},{10,11... | collective-permute-start | bytes 786440 | tf_op jit(solution)/shard_map/ppermute | solution.py:24
  41.6 15.3 %collective-permute-start.14 = (bf16[256,1024]{1,0:T(8,128)(2,1)S(1)}, bf16[256,1024]{1,0:T(8,128)(2,1)S(1)}, u32[]{:S(2)}, u32[]{:S(2)}) collective-permute-start(bf16[256,1024]{1,0:T(8,128)(2,1)S(1)} %collective-permute-done.10.refs_5_), channel_id=1, source_target_pairs={{0,4},{1,5},{2,6},{3,7},{4,8},{5,9},{6,10},{7,11},{8,12},{9,13},{1... | collective-permute-start | bytes 1572872 | tf_op jit(solution)/shard_map/ppermute | solution.py:24
  51.6 1.6 %collective-permute-start.18 = (bf16[64,2560]{1,0:T(8,128)(2,1)S(1)}, bf16[64,2560]{1,0:T(8,128)(2,1)S(1)}, u32[]{:S(2)}, u32[]{:S(2)}) collective-permute-start(bf16[64,2560]{1,0:T(8,128)(2,1)S(1)} %get-tuple-element.58), channel_id=1, source_target_pairs={{0,1},{1,0},{2,3},{3,2},{4,5},{5,4},{6,7},{7,6},{8,9},{9,8},{10,11... | collective-permute-start | bytes 983048 | tf_op jit(solution)/shard_map/ppermute | solution.py:24
  51.6 2.1 %collective-permute-start.17 = (bf16[64,2560]{1,0:T(8,128)(2,1)S(1)}, bf16[64,2560]{1,0:T(8,128)(2,1)S(1)}, u32[]{:S(2)}, u32[]{:S(2)}) collective-permute-start(bf16[64,2560]{1,0:T(8,128)(2,1)S(1)} %get-tuple-element.56), channel_id=1, source_target_pairs={{0,1},{1,0},{2,3},{3,2},{4,5},{5,4},{6,7},{7,6},{8,9},{9,8},{10,11... | collective-permute-start | bytes 983048 | tf_op jit(solution)/shard_map/ppermute | solution.py:24
  52.1 4.9 %collective-permute-start.11 = (bf16[256,1024]{1,0:T(8,128)(2,1)S(1)}, bf16[256,1024]{1,0:T(8,128)(2,1)S(1)}, u32[]{:S(2)}, u32[]{:S(2)}) collective-permute-start(bf16[256,1024]{1,0:T(8,128)(2,1)S(1)} %collective-permute-done.10.refs_5_), channel_id=1, source_target_pairs={{0,1},{1,0},{2,3},{3,2},{4,5},{5,4},{6,7},{7,6},{8,9},{9,8},{10,11... | collective-permute-start | bytes 1572872 | tf_op jit(solution)/shard_map/ppermute | solution.py:24
  57.0 4.5 %collective-permute-start.19 = (bf16[256,1024]{1,0:T(8,128)(2,1)S(1)}, bf16[256,1024]{1,0:T(8,128)(2,1)S(1)}, u32[]{:S(2)}, u32[]{:S(2)}) collective-permute-start(bf16[256,1024]{1,0:T(8,128)(2,1)S(1)} %collective-permute-done.14.refs_5_), channel_id=1, source_target_pairs={{0,1},{1,0},{2,3},{3,2},{4,5},{5,4},{6,7},{7,6},{8,9},{9,8},{10,11... | collective-permute-start | bytes 1572872 | tf_op jit(solution)/shard_map/ppermute | solution.py:24
  58.0 7.9 %collective-permute-start.12 = (bf16[176,512]{1,0:T(8,128)(2,1)S(1)}, bf16[176,512]{1,0:T(8,128)(2,1)S(1)}, u32[]{:S(2)}, u32[]{:S(2)}) collective-permute-start(bf16[176,512]{1,0:T(8,128)(2,1)S(1)} %get-tuple-element.51), channel_id=1, source_target_pairs={{0,2},{1,3},{2,0},{3,1},{4,6},{5,7},{6,4},{7,5},{8,10},{9,11},{10,... | collective-permute-start | bytes 540680 | tf_op jit(solution)/shard_map/ppermute | solution.py:24
  59.5 10.3 %collective-permute-start.13 = (bf16[176,512]{1,0:T(8,128)(2,1)S(1)}, bf16[176,512]{1,0:T(8,128)(2,1)S(1)}, u32[]{:S(2)}, u32[]{:S(2)}) collective-permute-start(bf16[176,512]{1,0:T(8,128)(2,1)S(1)} %get-tuple-element.52), channel_id=1, source_target_pairs={{0,18},{1,19},{2,16},{3,17},{4,22},{5,23},{6,20},{7,21},{8,26},{9,... | collective-permute-start | bytes 540680 | tf_op jit(solution)/shard_map/ppermute | solution.py:24
  61.0 10.8 %collective-permute-start.24 = (bf16[16,5120]{1,0:T(8,128)(2,1)S(1)}, bf16[16,5120]{1,0:T(8,128)(2,1)S(1)}, u32[]{:S(2)}, u32[]{:S(2)}) collective-permute-start(bf16[16,5120]{1,0:T(8,128)(2,1)S(1)} %get-tuple-element.70), channel_id=1, source_target_pairs={{0,4},{1,5},{2,6},{3,7},{4,8},{5,9},{6,10},{7,11},{8,12},{9,13},{1... | collective-permute-start | bytes 491528 | tf_op jit(solution)/shard_map/ppermute | solution.py:24
  61.0 15.0 %collective-permute-start.23 = (bf16[16,5120]{1,0:T(8,128)(2,1)S(1)}, bf16[16,5120]{1,0:T(8,128)(2,1)S(1)}, u32[]{:S(2)}, u32[]{:S(2)}) collective-permute-start(bf16[16,5120]{1,0:T(8,128)(2,1)S(1)} %get-tuple-element.68), channel_id=1, source_target_pairs={{0,8},{1,9},{2,10},{3,11},{4,12},{5,13},{6,14},{7,15},{8,0},{9,1},... | collective-permute-start | bytes 491528 | tf_op jit(solution)/shard_map/ppermute | solution.py:24
  61.5 14.6 %collective-permute-start.22 = (bf16[16,5120]{1,0:T(8,128)(2,1)S(1)}, bf16[16,5120]{1,0:T(8,128)(2,1)S(1)}, u32[]{:S(2)}, u32[]{:S(2)}) collective-permute-start(bf16[16,5120]{1,0:T(8,128)(2,1)S(1)} %get-tuple-element.66), channel_id=1, source_target_pairs={{0,12},{1,13},{2,14},{3,15},{4,0},{5,1},{6,2},{7,3},{8,4},{9,5},{1... | collective-permute-start | bytes 491528 | tf_op jit(solution)/shard_map/ppermute | solution.py:24
  69.8 8.5 %collective-permute-start.21 = (bf16[176,512]{1,0:T(8,128)(2,1)S(1)}, bf16[176,512]{1,0:T(8,128)(2,1)S(1)}, u32[]{:S(2)}, u32[]{:S(2)}) collective-permute-start(bf16[176,512]{1,0:T(8,128)(2,1)S(1)} %get-tuple-element.64), channel_id=1, source_target_pairs={{0,18},{1,19},{2,16},{3,17},{4,22},{5,23},{6,20},{7,21},{8,26},{9,... | collective-permute-start | bytes 540680 | tf_op jit(solution)/shard_map/ppermute | solution.py:24
  71.3 8.6 %collective-permute-start.20 = (bf16[176,512]{1,0:T(8,128)(2,1)S(1)}, bf16[176,512]{1,0:T(8,128)(2,1)S(1)}, u32[]{:S(2)}, u32[]{:S(2)}) collective-permute-start(bf16[176,512]{1,0:T(8,128)(2,1)S(1)} %get-tuple-element.62), channel_id=1, source_target_pairs={{0,2},{1,3},{2,0},{3,1},{4,6},{5,7},{6,4},{7,5},{8,10},{9,11},{10,... | collective-permute-start | bytes 540680 | tf_op jit(solution)/shard_map/ppermute | solution.py:24
  76.2 1.5 %collective-permute-start.25 = (bf16[16,5120]{1,0:T(8,128)(2,1)S(1)}, bf16[16,5120]{1,0:T(8,128)(2,1)S(1)}, u32[]{:S(2)}, u32[]{:S(2)}) collective-permute-start(bf16[16,5120]{1,0:T(8,128)(2,1)S(1)} %shard_map.103.refs_0_), channel_id=1, source_target_pairs={{0,1},{1,0},{2,3},{3,2},{4,5},{5,4},{6,7},{7,6},{8,9},{9,8},{10,11... | collective-permute-start | bytes 491528 | tf_op jit(solution)/shard_map/ppermute | solution.py:24
  (1 other events, 0.7 us)

commit v14 on v13

--- a/solution.py
+++ b/solution.py
@@ -156,6 +156,8 @@
     else:
         sel_ref, refs = refs[0], refs[1:]
         out_refs = refs[-groups:]
+        if refs[-1].shape[0] > tokens:
+            out_refs = [refs[-1].at[pl.ds(dg * tokens, tokens)] for dg in range(groups)]
     for i, (k, spec) in enumerate(batch):
         shard_at = lax.rem(here + holders - k, holders) * half
         for (dr, offset), block in zip(spec, refs):
@@ -183,6 +185,12 @@
         refs = refs[len(spec) :]
 
 
+def split_kernel(block_ref, *part_refs):
+    rows = part_refs[0].shape[0]
+    for j, ref in enumerate(part_refs):
+        ref[...] = block_ref[j * rows : (j + 1) * rows]
+
+
 def place_kernel(sizes, batches, *refs):
     groups, holders, shard, half = sizes
     group, here = lax.axis_index("groups"), lax.axis_index("adapter")
@@ -211,22 +219,29 @@
 
 
 def total_kernel(*refs):
-    total = refs[0][...]
-    for ref in refs[1:-1]:
-        total = total + ref[...].astype(F32)
-    refs[-1][...] = (ADAPTER_SCALE * total).astype(BF16)
+    half_refs, refs = refs[-2:], refs[:-2]
+    wide = half_refs[0].shape[1]
+    for j, out_ref in enumerate(half_refs):
+        at = pl.ds(j * wide, wide)
+        total = refs[0][:, at]
+        for ref in refs[1:]:
+            total = total + ref[:, at].astype(F32)
+        out_ref[...] = (ADAPTER_SCALE * total).astype(BF16)
 
 
 def spread_kernel(width, replicas, *refs):
     core = lax.axis_index("replica")
-    down_ref, up_ref = refs[replicas:]
+    down_ref, up_ref = refs[2 * replicas :]
     slots = down_ref.shape[0] // replicas
     rank = down_ref.shape[1]
+    wide = refs[0].shape[1]
     for dr in range(replicas):
         at = lax.rem(core + replicas - dr, replicas) * slots
         for j in range(slots):
-            down_ref[at + j] = refs[dr][j * rank : (j + 1) * rank, :width]
-            up_ref[at + j] = refs[dr][j * rank : (j + 1) * rank, width:]
+            rows = slice(j * rank, (j + 1) * rank)
+            down_ref[at + j, :, :wide] = refs[2 * dr][rows]
+            down_ref[at + j, :, wide:] = refs[2 * dr + 1][rows, : width - wide]
+            up_ref[at + j] = refs[2 * dr + 1][rows, width - wide :]
 
 
 def on_device(
@@ -290,11 +305,16 @@
     def pieces_of(k, *before):
         if k == 0:
             return [(0, 0)], [frozen]
-        block = after(ring[k], *before) if before else ring[k]
-        spec = [(dr, 0) for dr in range(replicas)]
-        pieces = [block] + [
-            moved(block, lambda g, z, s, r: (g, z, s, r + dr)) for dr in range(1, replicas)
-        ]
+        mails = [ring[k]]
+        if k > 1 and piece % (2 * LANES) == 0:
+            shape = jax.ShapeDtypeStruct((piece // 2, value_width), BF16)
+            mails = call(split_kernel, [shape] * 2, (ring[k],))
+        mails = [after(mail, *before) if before else mail for mail in mails]
+        spec, pieces = [(0, 0)], [ring[k]]
+        for dr in range(1, replicas):
+            for j, mail in enumerate(mails):
+                spec.append((dr, j * mail.shape[0]))
+                pieces.append(moved(mail, lambda g, z, s, r: (g, z, s, r + dr)))
         if piece % LANES:
             whole = jnp.zeros((half, value_width), BF16)
             for (dr, offset), part in zip(spec, pieces):
@@ -333,7 +353,7 @@
         return part, chip
 
     batches = [list(range(min(2, holders)))] + [[k] for k in range(2, holders)]
-    arrived = []
+    arrived, crossed = [], []
     for i, batch in enumerate(batches):
         operands, specs = [], []
         for k in batch:
@@ -348,14 +368,26 @@
             functools.partial(
                 frozen_kernel, (tokens, groups, holders, replicas, slots, rank), specs
             ),
-            [jax.ShapeDtypeStruct((tokens, half * len(batch)), BF16)] * groups
+            (
+                [jax.ShapeDtypeStruct((groups * tokens, half), BF16)]
+                if i == 1 and len(batches) > 2
+                else [jax.ShapeDtypeStruct((tokens, half * len(batch)), BF16)] * groups
+            )
             + [jax.ShapeDtypeStruct((groups * tokens, kept), BF16)] * (i == 0),
             [*grads, *downs, *([sel] if i else ups), *operands],
         )
         if i == 0:
             sel = out[groups]
         mails = list(out[:groups])
-        if i > 1:
+        if i == 1 and len(batches) > 2:
+            got = moved(out[0], lambda g, z, s, r: (g, z, s - 1, r))
+            got = [got[dg * tokens : (dg + 1) * tokens] for dg in range(groups)]
+            crossed.append(got[:1])
+            for dg in range(1, groups):
+                crossed[0].append(moved(got[dg], lambda g, z, s, r: (g + dg, z, s, r)))
+            arrived.append(crossed[0])
+            continue
+        if i > 2:
             mails = [after(mail, *arrived[-1]) for mail in mails]
         arrived.append(
             [moved(mails[dg], lambda g, z, s, r: (g + dg, z, s - 1, r)) for dg in range(groups)]
@@ -372,10 +404,10 @@
         moved(after(chip[k], ring[-1]), lambda g, z, s, r: (g, z - k, s, r))
         for k in range(1, holders)
     ]
-    total = call(total_kernel, [jax.ShapeDtypeStruct((rows, cols), BF16)], sums)[0]
-    totals = [total] + [
-        moved(total, lambda g, z, s, r: (g, z, s, r + dr)) for dr in range(1, replicas)
-    ]
+    total = call(total_kernel, [jax.ShapeDtypeStruct((rows, cols // 2), BF16)] * 2, sums)
+    totals = list(total)
+    for dr in range(1, replicas):
+        totals += [moved(x, lambda g, z, s, r: (g, z, s, r + dr)) for x in total]
     down_grad, up_grad = call(
         functools.partial(spread_kernel, width, replicas),
         [

time: 81.3 us -> 78.6 us (0.967)
  waiting for transfers between devices: 39.6 us -> 33.4 us
  starting transfers between devices: 26.8 us -> 29.8 us
    ppermute x26 -> x29, waiting for transfers between devices: 39.6 us -> 33.4 us  [moved(): return lax.ppermute(x, AXES, pairs)]
    ppermute x26 -> x29, starting transfers between devices: 26.8 us -> 29.8 us  [moved(): return lax.ppermute(x, AXES, pairs)]
    pallas_call x11 -> x13, Pallas kernels: 8.53 us -> 8.94 us  [call(): pl.pallas_call(kernel, out_shape=out_shape, in_specs=[pl.BlockSpec(memory...]
  transfers between devices with their start and end apart: 26 -> 29, of which waited for: 14 -> 13; matrix products, arithmetic and copies ran while one was open for 0% -> 0% of each run, Pallas kernels for 9% -> 10%
where the time goes in v14:
time: 78.6 us; the launch traced here: 78.3 us
  waiting for transfers between devices  33.4 us (42%)
  starting transfers between devices  29.8 us (38%)
  Pallas kernels  8.94 us (11%)
  local copies, waits for them, and re-layouts  5.37 us (7%)
  between operations  0.8 us (1%)
    ppermute x29, waiting for transfers between devices, moved(): return lax.ppermute(x, AXES, pairs)  33.4 us
    ppermute x29, starting transfers between devices, moved(): return lax.ppermute(x, AXES, pairs)  29.8 us
    pallas_call x13, Pallas kernels, call(): pl.pallas_call(kernel, out_shape=out_shape, in_specs=[pl.BlockSpec(memory...  8.94 us
    unnamed x14, local copies, waits for them, and re-layouts  4.12 us
  transfers between devices with their start and end apart: 29, of which 13 were waited for; matrix products, arithmetic and copies ran while one was open for 0% of the time, Pallas kernels for 10%

profile of v14, /device:TPU:0, one launch (start us, length us, event | category | flops | bytes accessed | tf_op | source)
XLA Modules:
  0.0 78.3 jit_solution(10503447186320892657)
XLA Ops:
  0.6 1.2 %dynamic-slice_bitcast_fusion = bf16[256,1024]{1,0:T(8,128)(2,1)S(1)} fusion(bf16[1,1024,1024]{2,1,0:T(8,128)(2,1)} %param.11, s32[]{:T(128)S(6)} %select_n.3), kind=kLoop, calls=%fused_computation | loop fusion | bytes 1048580 | tf_op jit(solution)/shard_map/dynamic_slice | solution.py:290
  1.9 3.1 %collective-permute-start.4 = (bf16[256,1024]{1,0:T(8,128)(2,1)S(1)}, bf16[256,1024]{1,0:T(8,128)(2,1)S(1)}, u32[]{:S(2)}, u32[]{:S(2)}) collective-permute-start(bf16[256,1024]{1,0:T(8,128)(2,1)S(1)} %dynamic-slice_bitcast_fusion), channel_id=1, source_target_pairs={{0,4},{1,5},{2,6},{3,7},{4,8},{5,9},{6,10},{7,11},{8,12},{9,13},{1... | collective-permute-start | bytes 1572872 | tf_op jit(solution)/shard_map/ppermute | solution.py:24
  5.0 1.0 %copy-done.2 = bf16[1,176,1024]{2,1,0:T(8,128)(2,1)S(1)} copy-done((bf16[1,176,1024]{2,1,0:T(8,128)(2,1)S(1)}, bf16[1,176,1024]{2,1,0:T(8,128)(2,1)}, u32[]{:S(2)}) %copy-start.2) | copy-done | bytes 360472
  8.0 1.6 %collective-permute-start.3 = (bf16[176,1152]{1,0:T(8,128)(2,1)S(1)}, bf16[176,1152]{1,0:T(8,128)(2,1)S(1)}, u32[]{:S(2)}, u32[]{:S(2)}) collective-permute-start(bf16[176,1152]{1,0:T(8,128)(2,1)S(1)} %shard_map.95.refs_0_.refs_1_), channel_id=1, source_target_pairs={{0,16},{1,17},{2,18},{3,19},{4,20},{5,21},{6,22},{7,23},{8,24},{9,... | collective-permute-start | bytes 1216520 | tf_op jit(solution)/shard_map/ppermute | solution.py:24
  9.6 0.9 %copy-done.3 = bf16[1,2,16,4096]{3,2,1,0:T(8,128)(2,1)S(1)} copy-done((bf16[1,2,16,4096]{3,2,1,0:T(8,128)(2,1)S(1)}, bf16[1,2,16,4096]{3,2,1,0:T(8,128)(2,1)}, u32[]{:S(2)}) %copy-start.3) | copy-done | bytes 262168
  10.6 0.8 %copy-done.4 = bf16[1,2,16,1024]{3,2,1,0:T(8,128)(2,1)S(1)} copy-done((bf16[1,2,16,1024]{3,2,1,0:T(8,128)(2,1)S(1)}, bf16[1,2,16,1024]{3,2,1,0:T(8,128)(2,1)}, u32[]{:S(2)}) %copy-start.4) | copy-done | bytes 65560
  11.4 1.6 %collective-permute-start = (bf16[16,3072]{1,0:T(8,128)(2,1)S(1)}, bf16[16,3072]{1,0:T(8,128)(2,1)S(1)}, u32[]{:S(2)}, u32[]{:S(2)}) collective-permute-start(bf16[16,3072]{1,0:T(8,128)(2,1)S(1)} %shard_map.94.refs_0_), channel_id=1, source_target_pairs={{0,4},{1,5},{2,6},{3,7},{4,8},{5,9},{6,10},{7,11},{8,12},{9,13},{1... | collective-permute-start | bytes 294920 | tf_op jit(solution)/shard_map/ppermute | solution.py:24
  13.1 1.2 %collective-permute-start.1 = (bf16[16,3072]{1,0:T(8,128)(2,1)S(1)}, bf16[16,3072]{1,0:T(8,128)(2,1)S(1)}, u32[]{:S(2)}, u32[]{:S(2)}) collective-permute-start(bf16[16,3072]{1,0:T(8,128)(2,1)S(1)} %shard_map.94.refs_0_), channel_id=1, source_target_pairs={{0,8},{1,9},{2,10},{3,11},{4,12},{5,13},{6,14},{7,15},{8,0},{9,1},... | collective-permute-start | bytes 294920 | tf_op jit(solution)/shard_map/ppermute | solution.py:24
  14.3 2.7 %collective-permute-start.2 = (bf16[16,3072]{1,0:T(8,128)(2,1)S(1)}, bf16[16,3072]{1,0:T(8,128)(2,1)S(1)}, u32[]{:S(2)}, u32[]{:S(2)}) collective-permute-start(bf16[16,3072]{1,0:T(8,128)(2,1)S(1)} %shard_map.94.refs_0_), channel_id=1, source_target_pairs={{0,12},{1,13},{2,14},{3,15},{4,0},{5,1},{6,2},{7,3},{8,4},{9,5},{1... | collective-permute-start | bytes 294920 | tf_op jit(solution)/shard_map/ppermute | solution.py:24
  17.0 5.0 %collective-permute-done.refs_1_ = bf16[16,3072]{1,0:T(8,128)(2,1)S(1)} collective-permute-done((bf16[16,3072]{1,0:T(8,128)(2,1)S(1)}, bf16[16,3072]{1,0:T(8,128)(2,1)S(1)}, u32[]{:S(2)}, u32[]{:S(2)}) %collective-permute-start) | collective-permute-done | bytes 98336 | tf_op jit(solution)/shard_map/ppermute | solution.py:24
  22.0 3.4 %collective-permute-done.1.refs_2_ = bf16[16,3072]{1,0:T(8,128)(2,1)S(1)} collective-permute-done((bf16[16,3072]{1,0:T(8,128)(2,1)S(1)}, bf16[16,3072]{1,0:T(8,128)(2,1)S(1)}, u32[]{:S(2)}, u32[]{:S(2)}) %collective-permute-start.1) | collective-permute-done | bytes 98336 | tf_op jit(solution)/shard_map/ppermute | solution.py:24
  25.4 2.6 %collective-permute-start.10 = (bf16[256,1024]{1,0:T(8,128)(2,1)S(1)}, bf16[256,1024]{1,0:T(8,128)(2,1)S(1)}, u32[]{:S(2)}, u32[]{:S(2)}) collective-permute-start(bf16[256,1024]{1,0:T(8,128)(2,1)S(1)} %collective-permute-done.4.refs_7_), channel_id=1, source_target_pairs={{0,4},{1,5},{2,6},{3,7},{4,8},{5,9},{6,10},{7,11},{8,12},{9,13},{1... | collective-permute-start | bytes 1572872 | tf_op jit(solution)/shard_map/ppermute | solution.py:24
  28.3 1.5 %collective-permute-start.16 = (bf16[64,2048]{1,0:T(8,128)(2,1)S(1)}, bf16[64,2048]{1,0:T(8,128)(2,1)S(1)}, u32[]{:S(2)}, u32[]{:S(2)}) collective-permute-start(bf16[64,2048]{1,0:T(8,128)(2,1)S(1)} %get-tuple-element.48.refs_2_.refs_3_), channel_id=1, source_target_pairs={{0,16},{1,17},{2,18},{3,19},{4,20},{5,21},{6,22},{7,23},{8,24},{9,... | collective-permute-start | bytes 786440 | tf_op jit(solution)/shard_map/ppermute | solution.py:24
  29.8 1.3 %collective-permute-done.6.refs_5_ = bf16[64,1024]{1,0:T(8,128)(2,1)S(1)} collective-permute-done((bf16[64,1024]{1,0:T(8,128)(2,1)S(1)}, bf16[64,1024]{1,0:T(8,128)(2,1)S(1)}, u32[]{:S(2)}, u32[]{:S(2)}) %collective-permute-start.6) | collective-permute-done | bytes 131104 | tf_op jit(solution)/shard_map/ppermute | solution.py:24
  31.2 2.2 %shard_map.97 = (bf16[176,1024]{1,0:T(8,128)(2,1)S(1)}, bf16[176,1024]{1,0:T(8,128)(2,1)S(1)}, bf16[352,128]{1,0:T(8,128)(2,1)S(1)}) custom-call(bf16[176,1152]{1,0:T(8,128)(2,1)S(1)} %shard_map.95.refs_0_.refs_1_, bf16[176,1152]{1,0:T(8,128)(2,1)S(1)} %collective-permute-done.3.refs_1_, bf16[64,2048]{1,0:T(8,128)(2,1)S(1)} %get-tuple-element.48.refs_2_.refs_3_, ...), custom_call_target="tpu_custom_call" | custom-call | flops 1000 | bytes 1000 | tf_op jit(solution)/shard_map/pallas_call | solution.py:41
  33.4 1.6 %collective-permute-start.8 = (bf16[176,1024]{1,0:T(8,128)(2,1)S(1)}, bf16[176,1024]{1,0:T(8,128)(2,1)S(1)}, u32[]{:S(2)}, u32[]{:S(2)}) collective-permute-start(bf16[176,1024]{1,0:T(8,128)(2,1)S(1)} %get-tuple-element.51), channel_id=1, source_target_pairs={{0,2},{1,3},{2,0},{3,1},{4,6},{5,7},{6,4},{7,5},{8,10},{9,11},{10,... | collective-permute-start | bytes 1081352 | tf_op jit(solution)/shard_map/ppermute | solution.py:24
  35.4 1.4 %collective-permute-done.16.refs_5_ = bf16[64,2048]{1,0:T(8,128)(2,1)S(1)} collective-permute-done((bf16[64,2048]{1,0:T(8,128)(2,1)S(1)}, bf16[64,2048]{1,0:T(8,128)(2,1)S(1)}, u32[]{:S(2)}, u32[]{:S(2)}) %collective-permute-start.16) | collective-permute-done | bytes 262176 | tf_op jit(solution)/shard_map/ppermute | solution.py:24
  36.8 4.8 %collective-permute-done.10.block_ref.refs_5_ = bf16[256,1024]{1,0:T(8,128)(2,1)S(1)} collective-permute-done((bf16[256,1024]{1,0:T(8,128)(2,1)S(1)}, bf16[256,1024]{1,0:T(8,128)(2,1)S(1)}, u32[]{:S(2)}, u32[]{:S(2)}) %collective-permute-start.10) | collective-permute-done | bytes 524320 | tf_op jit(solution)/shard_map/ppermute | solution.py:24
  42.3 2.4 %collective-permute-done.8.refs_0_ = bf16[176,1024]{1,0:T(8,128)(2,1)S(1)} collective-permute-done((bf16[176,1024]{1,0:T(8,128)(2,1)S(1)}, bf16[176,1024]{1,0:T(8,128)(2,1)S(1)}, u32[]{:S(2)}, u32[]{:S(2)}) %collective-permute-start.8) | collective-permute-done | bytes 360480 | tf_op jit(solution)/shard_map/ppermute | solution.py:24
  44.7 6.9 %collective-permute-done.9.refs_1_ = bf16[176,1024]{1,0:T(8,128)(2,1)S(1)} collective-permute-done((bf16[176,1024]{1,0:T(8,128)(2,1)S(1)}, bf16[176,1024]{1,0:T(8,128)(2,1)S(1)}, u32[]{:S(2)}, u32[]{:S(2)}) %collective-permute-start.9) | collective-permute-done | bytes 360480 | tf_op jit(solution)/shard_map/ppermute | solution.py:24
  52.1 1.3 %shard_map.101 = (f32[64,5120]{1,0:T(8,128)S(1)}, bf16[64,2560]{1,0:T(8,128)(2,1)S(1)}, bf16[64,2560]{1,0:T(8,128)(2,1)S(1)}) custom-call(bf16[176,4096]{1,0:T(8,128)(2,1)S(1)} %bitcast.12, bf16[176,1152]{1,0:T(8,128)(2,1)S(1)} %shard_map.95.refs_0_.refs_1_, bf16[352,128]{1,0:T(8,128)(2,1)S(1)} %get-tuple-element.53.refs_4_.refs_2_, ...), custom_call_target="tpu_custom_call" | custom-call | flops 1000 | bytes 1000 | tf_op jit(solution)/shard_map/pallas_call | solution.py:41
  54.0 1.2 %shard_map.99 = bf16[352,512]{1,0:T(8,128)(2,1)S(1)} custom-call(bf16[176,1152]{1,0:T(8,128)(2,1)S(1)} %shard_map.95.refs_0_.refs_1_, bf16[176,1152]{1,0:T(8,128)(2,1)S(1)} %collective-permute-done.3.refs_1_, bf16[64,2048]{1,0:T(8,128)(2,1)S(1)} %get-tuple-element.48.refs_2_.refs_3_, bf16[64,2048]{1,0:T(8,128)(2,1)S(1)} %collective-permute-done.5.refs_3_.refs_4_, ...), custom_call_target="tpu_custom_call" | custom-call | flops 1000 | bytes 1000 | tf_op jit(solution)/shard_map/pallas_call | solution.py:41
  55.2 1.6 %collective-permute-start.13 = (bf16[352,512]{1,0:T(8,128)(2,1)S(1)}, bf16[352,512]{1,0:T(8,128)(2,1)S(1)}, u32[]{:S(2)}, u32[]{:S(2)}) collective-permute-start(bf16[352,512]{1,0:T(8,128)(2,1)S(1)} %shard_map.99), channel_id=1, source_target_pairs={{0,2},{1,3},{2,0},{3,1},{4,6},{5,7},{6,4},{7,5},{8,10},{9,11},{10,... | collective-permute-start | bytes 1081352 | tf_op jit(solution)/shard_map/ppermute | solution.py:24
  57.8 1.7 %collective-permute-start.25 = (bf16[16,5120]{1,0:T(8,128)(2,1)S(1)}, bf16[16,5120]{1,0:T(8,128)(2,1)S(1)}, u32[]{:S(2)}, u32[]{:S(2)}) collective-permute-start(bf16[16,5120]{1,0:T(8,128)(2,1)S(1)} %get-tuple-element.74), channel_id=1, source_target_pairs={{0,8},{1,9},{2,10},{3,11},{4,12},{5,13},{6,14},{7,15},{8,0},{9,1},... | collective-permute-start | bytes 491528 | tf_op jit(solution)/shard_map/ppermute | solution.py:24
  59.5 2.7 %collective-permute-start.24 = (bf16[16,5120]{1,0:T(8,128)(2,1)S(1)}, bf16[16,5120]{1,0:T(8,128)(2,1)S(1)}, u32[]{:S(2)}, u32[]{:S(2)}) collective-permute-start(bf16[16,5120]{1,0:T(8,128)(2,1)S(1)} %get-tuple-element.72), channel_id=1, source_target_pairs={{0,12},{1,13},{2,14},{3,15},{4,0},{5,1},{6,2},{7,3},{8,4},{9,5},{1... | collective-permute-start | bytes 491528 | tf_op jit(solution)/shard_map/ppermute | solution.py:24
  62.1 1.2 %shard_map.103 = (bf16[176,512]{1,0:T(8,128)(2,1)S(1)}, bf16[176,512]{1,0:T(8,128)(2,1)S(1)}) custom-call(bf16[176,1152]{1,0:T(8,128)(2,1)S(1)} %shard_map.95.refs_0_.refs_1_, bf16[176,1152]{1,0:T(8,128)(2,1)S(1)} %collective-permute-done.3.refs_1_, bf16[64,2048]{1,0:T(8,128)(2,1)S(1)} %get-tuple-element.48.refs_2_.refs_3_, ...), custom_call_target="tpu_custom_call" | custom-call | flops 1000 | bytes 1000 | tf_op jit(solution)/shard_map/pallas_call | solution.py:41
  63.3 1.0 %collective-permute-start.22 = (bf16[176,512]{1,0:T(8,128)(2,1)S(1)}, bf16[176,512]{1,0:T(8,128)(2,1)S(1)}, u32[]{:S(2)}, u32[]{:S(2)}) collective-permute-start(bf16[176,512]{1,0:T(8,128)(2,1)S(1)} %get-tuple-element.69), channel_id=1, source_target_pairs={{0,2},{1,3},{2,0},{3,1},{4,6},{5,7},{6,4},{7,5},{8,10},{9,11},{10,... | collective-permute-start | bytes 540680 | tf_op jit(solution)/shard_map/ppermute | solution.py:24
  64.3 1.6 %collective-permute-done.13 = bf16[352,512]{1,0:T(8,128)(2,1)S(1)} collective-permute-done((bf16[352,512]{1,0:T(8,128)(2,1)S(1)}, bf16[352,512]{1,0:T(8,128)(2,1)S(1)}, u32[]{:S(2)}, u32[]{:S(2)}) %collective-permute-start.13) | collective-permute-done | bytes 360480 | tf_op jit(solution)/shard_map/ppermute | solution.py:24
  66.0 2.7 %collective-permute-start.23 = (bf16[176,512]{1,0:T(8,128)(2,1)S(1)}, bf16[176,512]{1,0:T(8,128)(2,1)S(1)}, u32[]{:S(2)}, u32[]{:S(2)}) collective-permute-start(bf16[176,512]{1,0:T(8,128)(2,1)S(1)} %get-tuple-element.70), channel_id=1, source_target_pairs={{0,18},{1,19},{2,16},{3,17},{4,22},{5,23},{6,20},{7,21},{8,26},{9,... | collective-permute-start | bytes 540680 | tf_op jit(solution)/shard_map/ppermute | solution.py:24
  69.3 3.5 %collective-permute-done.25.refs_2_ = bf16[16,5120]{1,0:T(8,128)(2,1)S(1)} collective-permute-done((bf16[16,5120]{1,0:T(8,128)(2,1)S(1)}, bf16[16,5120]{1,0:T(8,128)(2,1)S(1)}, u32[]{:S(2)}, u32[]{:S(2)}) %collective-permute-start.25) | collective-permute-done | bytes 163872 | tf_op jit(solution)/shard_map/ppermute | solution.py:24
  75.2 2.0 %collective-permute-done.14.refs_3_ = bf16[176,512]{1,0:T(8,128)(2,1)S(1)} collective-permute-done((bf16[176,512]{1,0:T(8,128)(2,1)S(1)}, bf16[176,512]{1,0:T(8,128)(2,1)S(1)}, u32[]{:S(2)}, u32[]{:S(2)}) %collective-permute-start.14) | collective-permute-done | bytes 180256 | tf_op jit(solution)/shard_map/ppermute | solution.py:24
  77.1 1.2 %shard_map.104 = bf16[176,4096]{1,0:T(8,128)(2,1)} custom-call(bf16[176,1024]{1,0:T(8,128)(2,1)S(1)} %collective-permute-done.8.refs_0_, bf16[176,1024]{1,0:T(8,128)(2,1)S(1)} %collective-permute-done.9.refs_1_, bf16[176,512]{1,0:T(8,128)(2,1)S(1)} %get-tuple-element.82.refs_2_, bf16[176,512]{1,0:T(8,128)(2,1)S(1)} %collective-permute-done.14.refs_3_, ...), custom_call_target="tpu_custom_call" | custom-call | flops 1000 | bytes 1000 | tf_op jit(solution)/shard_map/pallas_call | solution.py:41
  (55 shorter events, 8.8 us)
Async XLA Ops:
  0.6 30.5 %copy-start = (bf16[1,1024,1024]{2,1,0:T(8,128)(2,1)S(1)}, bf16[1,1024,1024]{2,1,0:T(8,128)(2,1)}, u32[]{:S(2)}) copy-start(bf16[1,1024,1024]{2,1,0:T(8,128)(2,1)} %param.11) | copy-start | bytes 6291460
  1.9 23.5 %collective-permute-start.4 = (bf16[256,1024]{1,0:T(8,128)(2,1)S(1)}, bf16[256,1024]{1,0:T(8,128)(2,1)S(1)}, u32[]{:S(2)}, u32[]{:S(2)}) collective-permute-start(bf16[256,1024]{1,0:T(8,128)(2,1)S(1)} %dynamic-slice_bitcast_fusion), channel_id=1, source_target_pairs={{0,4},{1,5},{2,6},{3,7},{4,8},{5,9},{6,10},{7,11},{8,12},{9,13},{1... | collective-permute-start | bytes 1572872 | tf_op jit(solution)/shard_map/ppermute | solution.py:24
  5.0 1.0 %copy-start.2 = (bf16[1,176,1024]{2,1,0:T(8,128)(2,1)S(1)}, bf16[1,176,1024]{2,1,0:T(8,128)(2,1)}, u32[]{:S(2)}) copy-start(bf16[1,176,1024]{2,1,0:T(8,128)(2,1)} %param.8) | copy-start | bytes 1081348
  8.0 17.3 %collective-permute-start.3 = (bf16[176,1152]{1,0:T(8,128)(2,1)S(1)}, bf16[176,1152]{1,0:T(8,128)(2,1)S(1)}, u32[]{:S(2)}, u32[]{:S(2)}) collective-permute-start(bf16[176,1152]{1,0:T(8,128)(2,1)S(1)} %shard_map.95.refs_0_.refs_1_), channel_id=1, source_target_pairs={{0,16},{1,17},{2,18},{3,19},{4,20},{5,21},{6,22},{7,23},{8,24},{9,... | collective-permute-start | bytes 1216520 | tf_op jit(solution)/shard_map/ppermute | solution.py:24
  11.4 10.5 %collective-permute-start = (bf16[16,3072]{1,0:T(8,128)(2,1)S(1)}, bf16[16,3072]{1,0:T(8,128)(2,1)S(1)}, u32[]{:S(2)}, u32[]{:S(2)}) collective-permute-start(bf16[16,3072]{1,0:T(8,128)(2,1)S(1)} %shard_map.94.refs_0_), channel_id=1, source_target_pairs={{0,4},{1,5},{2,6},{3,7},{4,8},{5,9},{6,10},{7,11},{8,12},{9,13},{1... | collective-permute-start | bytes 294920 | tf_op jit(solution)/shard_map/ppermute | solution.py:24
  13.1 12.3 %collective-permute-start.1 = (bf16[16,3072]{1,0:T(8,128)(2,1)S(1)}, bf16[16,3072]{1,0:T(8,128)(2,1)S(1)}, u32[]{:S(2)}, u32[]{:S(2)}) collective-permute-start(bf16[16,3072]{1,0:T(8,128)(2,1)S(1)} %shard_map.94.refs_0_), channel_id=1, source_target_pairs={{0,8},{1,9},{2,10},{3,11},{4,12},{5,13},{6,14},{7,15},{8,0},{9,1},... | collective-permute-start | bytes 294920 | tf_op jit(solution)/shard_map/ppermute | solution.py:24
  14.3 11.1 %collective-permute-start.2 = (bf16[16,3072]{1,0:T(8,128)(2,1)S(1)}, bf16[16,3072]{1,0:T(8,128)(2,1)S(1)}, u32[]{:S(2)}, u32[]{:S(2)}) collective-permute-start(bf16[16,3072]{1,0:T(8,128)(2,1)S(1)} %shard_map.94.refs_0_), channel_id=1, source_target_pairs={{0,12},{1,13},{2,14},{3,15},{4,0},{5,1},{6,2},{7,3},{8,4},{9,5},{1... | collective-permute-start | bytes 294920 | tf_op jit(solution)/shard_map/ppermute | solution.py:24
  25.4 5.8 %collective-permute-start.7 = (bf16[256,1024]{1,0:T(8,128)(2,1)S(1)}, bf16[256,1024]{1,0:T(8,128)(2,1)S(1)}, u32[]{:S(2)}, u32[]{:S(2)}) collective-permute-start(bf16[256,1024]{1,0:T(8,128)(2,1)S(1)} %collective-permute-done.4.refs_7_), channel_id=1, source_target_pairs={{0,1},{1,0},{2,3},{3,2},{4,5},{5,4},{6,7},{7,6},{8,9},{9,8},{10,11... | collective-permute-start | bytes 1572872 | tf_op jit(solution)/shard_map/ppermute | solution.py:24
  25.4 16.2 %collective-permute-start.10 = (bf16[256,1024]{1,0:T(8,128)(2,1)S(1)}, bf16[256,1024]{1,0:T(8,128)(2,1)S(1)}, u32[]{:S(2)}, u32[]{:S(2)}) collective-permute-start(bf16[256,1024]{1,0:T(8,128)(2,1)S(1)} %collective-permute-done.4.refs_7_), channel_id=1, source_target_pairs={{0,4},{1,5},{2,6},{3,7},{4,8},{5,9},{6,10},{7,11},{8,12},{9,13},{1... | collective-permute-start | bytes 1572872 | tf_op jit(solution)/shard_map/ppermute | solution.py:24
  28.0 3.1 %collective-permute-start.5 = (bf16[64,2048]{1,0:T(8,128)(2,1)S(1)}, bf16[64,2048]{1,0:T(8,128)(2,1)S(1)}, u32[]{:S(2)}, u32[]{:S(2)}) collective-permute-start(bf16[64,2048]{1,0:T(8,128)(2,1)S(1)} %get-tuple-element.48.refs_2_.refs_3_), channel_id=1, source_target_pairs={{0,1},{1,0},{2,3},{3,2},{4,5},{5,4},{6,7},{7,6},{8,9},{9,8},{10,11... | collective-permute-start | bytes 786440 | tf_op jit(solution)/shard_map/ppermute | solution.py:24
  28.3 8.6 %collective-permute-start.16 = (bf16[64,2048]{1,0:T(8,128)(2,1)S(1)}, bf16[64,2048]{1,0:T(8,128)(2,1)S(1)}, u32[]{:S(2)}, u32[]{:S(2)}) collective-permute-start(bf16[64,2048]{1,0:T(8,128)(2,1)S(1)} %get-tuple-element.48.refs_2_.refs_3_), channel_id=1, source_target_pairs={{0,16},{1,17},{2,18},{3,19},{4,20},{5,21},{6,22},{7,23},{8,24},{9,... | collective-permute-start | bytes 786440 | tf_op jit(solution)/shard_map/ppermute | solution.py:24
  29.8 1.3 %collective-permute-start.6 = (bf16[64,1024]{1,0:T(8,128)(2,1)S(1)}, bf16[64,1024]{1,0:T(8,128)(2,1)S(1)}, u32[]{:S(2)}, u32[]{:S(2)}) collective-permute-start(bf16[64,1024]{1,0:T(8,128)(2,1)S(1)} %get-tuple-element.49.refs_4_), channel_id=1, source_target_pairs={{0,1},{1,0},{2,3},{3,2},{4,5},{5,4},{6,7},{7,6},{8,9},{9,8},{10,11... | collective-permute-start | bytes 393224 | tf_op jit(solution)/shard_map/ppermute | solution.py:24
  31.1 21.0 %copy-start.1 = (bf16[1,176,4096]{2,1,0:T(8,128)(2,1)S(1)}, bf16[1,176,4096]{2,1,0:T(8,128)(2,1)}, u32[]{:S(2)}) copy-start(bf16[1,176,4096]{2,1,0:T(8,128)(2,1)} %param.7) | copy-start | bytes 4325380
  33.4 11.3 %collective-permute-start.8 = (bf16[176,1024]{1,0:T(8,128)(2,1)S(1)}, bf16[176,1024]{1,0:T(8,128)(2,1)S(1)}, u32[]{:S(2)}, u32[]{:S(2)}) collective-permute-start(bf16[176,1024]{1,0:T(8,128)(2,1)S(1)} %get-tuple-element.51), channel_id=1, source_target_pairs={{0,2},{1,3},{2,0},{3,1},{4,6},{5,7},{6,4},{7,5},{8,10},{9,11},{10,... | collective-permute-start | bytes 1081352 | tf_op jit(solution)/shard_map/ppermute | solution.py:24
  35.0 16.6 %collective-permute-start.9 = (bf16[176,1024]{1,0:T(8,128)(2,1)S(1)}, bf16[176,1024]{1,0:T(8,128)(2,1)S(1)}, u32[]{:S(2)}, u32[]{:S(2)}) collective-permute-start(bf16[176,1024]{1,0:T(8,128)(2,1)S(1)} %get-tuple-element.52), channel_id=1, source_target_pairs={{0,18},{1,19},{2,16},{3,17},{4,22},{5,23},{6,20},{7,21},{8,26},{9,... | collective-permute-start | bytes 1081352 | tf_op jit(solution)/shard_map/ppermute | solution.py:24
  36.8 15.3 %collective-permute-start.17 = (bf16[64,2048]{1,0:T(8,128)(2,1)S(1)}, bf16[64,2048]{1,0:T(8,128)(2,1)S(1)}, u32[]{:S(2)}, u32[]{:S(2)}) collective-permute-start(bf16[64,2048]{1,0:T(8,128)(2,1)S(1)} %collective-permute-done.16.refs_5_), channel_id=1, source_target_pairs={{0,1},{1,0},{2,3},{3,2},{4,5},{5,4},{6,7},{7,6},{8,9},{9,8},{10,11... | collective-permute-start | bytes 786440 | tf_op jit(solution)/shard_map/ppermute | solution.py:24
  41.6 15.3 %collective-permute-start.15 = (bf16[256,1024]{1,0:T(8,128)(2,1)S(1)}, bf16[256,1024]{1,0:T(8,128)(2,1)S(1)}, u32[]{:S(2)}, u32[]{:S(2)}) collective-permute-start(bf16[256,1024]{1,0:T(8,128)(2,1)S(1)} %collective-permute-done.10.block_ref.refs_5_), channel_id=1, source_target_pairs={{0,4},{1,5},{2,6},{3,7},{4,8},{5,9},{6,10},{7,11},{8,12},{9,13},{1... | collective-permute-start | bytes 1572872 | tf_op jit(solution)/shard_map/ppermute | solution.py:24
  51.6 2.4 %collective-permute-start.12 = (bf16[128,1024]{1,0:T(8,128)(2,1)S(1)}, bf16[128,1024]{1,0:T(8,128)(2,1)S(1)}, u32[]{:S(2)}, u32[]{:S(2)}) collective-permute-start(bf16[128,1024]{1,0:T(8,128)(2,1)S(1)} %get-tuple-element.57), channel_id=1, source_target_pairs={{0,1},{1,0},{2,3},{3,2},{4,5},{5,4},{6,7},{7,6},{8,9},{9,8},{10,11... | collective-permute-start | bytes 786440 | tf_op jit(solution)/shard_map/ppermute | solution.py:24
  51.6 2.4 %collective-permute-start.11 = (bf16[128,1024]{1,0:T(8,128)(2,1)S(1)}, bf16[128,1024]{1,0:T(8,128)(2,1)S(1)}, u32[]{:S(2)}, u32[]{:S(2)}) collective-permute-start(bf16[128,1024]{1,0:T(8,128)(2,1)S(1)} %get-tuple-element.55), channel_id=1, source_target_pairs={{0,1},{1,0},{2,3},{3,2},{4,5},{5,4},{6,7},{7,6},{8,9},{9,8},{10,11... | collective-permute-start | bytes 786440 | tf_op jit(solution)/shard_map/ppermute | solution.py:24
  53.4 3.6 %collective-permute-start.19 = (bf16[64,2560]{1,0:T(8,128)(2,1)S(1)}, bf16[64,2560]{1,0:T(8,128)(2,1)S(1)}, u32[]{:S(2)}, u32[]{:S(2)}) collective-permute-start(bf16[64,2560]{1,0:T(8,128)(2,1)S(1)} %get-tuple-element.64), channel_id=1, source_target_pairs={{0,1},{1,0},{2,3},{3,2},{4,5},{5,4},{6,7},{7,6},{8,9},{9,8},{10,11... | collective-permute-start | bytes 983048 | tf_op jit(solution)/shard_map/ppermute | solution.py:24
  53.5 3.5 %collective-permute-start.18 = (bf16[64,2560]{1,0:T(8,128)(2,1)S(1)}, bf16[64,2560]{1,0:T(8,128)(2,1)S(1)}, u32[]{:S(2)}, u32[]{:S(2)}) collective-permute-start(bf16[64,2560]{1,0:T(8,128)(2,1)S(1)} %get-tuple-element.62), channel_id=1, source_target_pairs={{0,1},{1,0},{2,3},{3,2},{4,5},{5,4},{6,7},{7,6},{8,9},{9,8},{10,11... | collective-permute-start | bytes 983048 | tf_op jit(solution)/shard_map/ppermute | solution.py:24
  55.2 10.8 %collective-permute-start.13 = (bf16[352,512]{1,0:T(8,128)(2,1)S(1)}, bf16[352,512]{1,0:T(8,128)(2,1)S(1)}, u32[]{:S(2)}, u32[]{:S(2)}) collective-permute-start(bf16[352,512]{1,0:T(8,128)(2,1)S(1)} %shard_map.99), channel_id=1, source_target_pairs={{0,2},{1,3},{2,0},{3,1},{4,6},{5,7},{6,4},{7,5},{8,10},{9,11},{10,... | collective-permute-start | bytes 1081352 | tf_op jit(solution)/shard_map/ppermute | solution.py:24
  57.2 2.3 %collective-permute-start.21 = (bf16[128,1024]{1,0:T(8,128)(2,1)S(1)}, bf16[128,1024]{1,0:T(8,128)(2,1)S(1)}, u32[]{:S(2)}, u32[]{:S(2)}) collective-permute-start(bf16[128,1024]{1,0:T(8,128)(2,1)S(1)} %get-tuple-element.68), channel_id=1, source_target_pairs={{0,1},{1,0},{2,3},{3,2},{4,5},{5,4},{6,7},{7,6},{8,9},{9,8},{10,11... | collective-permute-start | bytes 786440 | tf_op jit(solution)/shard_map/ppermute | solution.py:24
  57.3 4.8 %collective-permute-start.20 = (bf16[128,1024]{1,0:T(8,128)(2,1)S(1)}, bf16[128,1024]{1,0:T(8,128)(2,1)S(1)}, u32[]{:S(2)}, u32[]{:S(2)}) collective-permute-start(bf16[128,1024]{1,0:T(8,128)(2,1)S(1)} %get-tuple-element.66), channel_id=1, source_target_pairs={{0,1},{1,0},{2,3},{3,2},{4,5},{5,4},{6,7},{7,6},{8,9},{9,8},{10,11... | collective-permute-start | bytes 786440 | tf_op jit(solution)/shard_map/ppermute | solution.py:24
  57.8 10.9 %collective-permute-start.26 = (bf16[16,5120]{1,0:T(8,128)(2,1)S(1)}, bf16[16,5120]{1,0:T(8,128)(2,1)S(1)}, u32[]{:S(2)}, u32[]{:S(2)}) collective-permute-start(bf16[16,5120]{1,0:T(8,128)(2,1)S(1)} %get-tuple-element.76), channel_id=1, source_target_pairs={{0,4},{1,5},{2,6},{3,7},{4,8},{5,9},{6,10},{7,11},{8,12},{9,13},{1... | collective-permute-start | bytes 491528 | tf_op jit(solution)/shard_map/ppermute | solution.py:24
  57.8 15.0 %collective-permute-start.25 = (bf16[16,5120]{1,0:T(8,128)(2,1)S(1)}, bf16[16,5120]{1,0:T(8,128)(2,1)S(1)}, u32[]{:S(2)}, u32[]{:S(2)}) collective-permute-start(bf16[16,5120]{1,0:T(8,128)(2,1)S(1)} %get-tuple-element.74), channel_id=1, source_target_pairs={{0,8},{1,9},{2,10},{3,11},{4,12},{5,13},{6,14},{7,15},{8,0},{9,1},... | collective-permute-start | bytes 491528 | tf_op jit(solution)/shard_map/ppermute | solution.py:24
  59.5 13.4 %collective-permute-start.24 = (bf16[16,5120]{1,0:T(8,128)(2,1)S(1)}, bf16[16,5120]{1,0:T(8,128)(2,1)S(1)}, u32[]{:S(2)}, u32[]{:S(2)}) collective-permute-start(bf16[16,5120]{1,0:T(8,128)(2,1)S(1)} %get-tuple-element.72), channel_id=1, source_target_pairs={{0,12},{1,13},{2,14},{3,15},{4,0},{5,1},{6,2},{7,3},{8,4},{9,5},{1... | collective-permute-start | bytes 491528 | tf_op jit(solution)/shard_map/ppermute | solution.py:24
  63.3 11.9 %collective-permute-start.22 = (bf16[176,512]{1,0:T(8,128)(2,1)S(1)}, bf16[176,512]{1,0:T(8,128)(2,1)S(1)}, u32[]{:S(2)}, u32[]{:S(2)}) collective-permute-start(bf16[176,512]{1,0:T(8,128)(2,1)S(1)} %get-tuple-element.69), channel_id=1, source_target_pairs={{0,2},{1,3},{2,0},{3,1},{4,6},{5,7},{6,4},{7,5},{8,10},{9,11},{10,... | collective-permute-start | bytes 540680 | tf_op jit(solution)/shard_map/ppermute | solution.py:24
  66.0 9.2 %collective-permute-start.23 = (bf16[176,512]{1,0:T(8,128)(2,1)S(1)}, bf16[176,512]{1,0:T(8,128)(2,1)S(1)}, u32[]{:S(2)}, u32[]{:S(2)}) collective-permute-start(bf16[176,512]{1,0:T(8,128)(2,1)S(1)} %get-tuple-element.70), channel_id=1, source_target_pairs={{0,18},{1,19},{2,16},{3,17},{4,22},{5,23},{6,20},{7,21},{8,26},{9,... | collective-permute-start | bytes 540680 | tf_op jit(solution)/shard_map/ppermute | solution.py:24
  68.7 8.4 %collective-permute-start.14 = (bf16[176,512]{1,0:T(8,128)(2,1)S(1)}, bf16[176,512]{1,0:T(8,128)(2,1)S(1)}, u32[]{:S(2)}, u32[]{:S(2)}) collective-permute-start(bf16[176,512]{1,0:T(8,128)(2,1)S(1)} %get-tuple-element.81), channel_id=1, source_target_pairs={{0,16},{1,17},{2,18},{3,19},{4,20},{5,21},{6,22},{7,23},{8,24},{9,... | collective-permute-start | bytes 540680 | tf_op jit(solution)/shard_map/ppermute | solution.py:24
  72.9 1.3 %collective-permute-start.27 = (bf16[16,2560]{1,0:T(8,128)(2,1)S(1)}, bf16[16,2560]{1,0:T(8,128)(2,1)S(1)}, u32[]{:S(2)}, u32[]{:S(2)}) collective-permute-start(bf16[16,2560]{1,0:T(8,128)(2,1)S(1)} %get-tuple-element.77.refs_0_), channel_id=1, source_target_pairs={{0,1},{1,0},{2,3},{3,2},{4,5},{5,4},{6,7},{7,6},{8,9},{9,8},{10,11... | collective-permute-start | bytes 245768 | tf_op jit(solution)/shard_map/ppermute | solution.py:24
  73.0 1.4 %collective-permute-start.28 = (bf16[16,2560]{1,0:T(8,128)(2,1)S(1)}, bf16[16,2560]{1,0:T(8,128)(2,1)S(1)}, u32[]{:S(2)}, u32[]{:S(2)}) collective-permute-start(bf16[16,2560]{1,0:T(8,128)(2,1)S(1)} %get-tuple-element.78.refs_1_), channel_id=1, source_target_pairs={{0,1},{1,0},{2,3},{3,2},{4,5},{5,4},{6,7},{7,6},{8,9},{9,8},{10,11... | collective-permute-start | bytes 245768 | tf_op jit(solution)/shard_map/ppermute | solution.py:24
  (4 other events, 3.1 us)

commit v15 on v14

--- a/solution.py
+++ b/solution.py
@@ -84,6 +84,16 @@
         rows = ref.shape[0]
         down_ref[k * rows : (k + 1) * rows] = ref[:, :wide]
         up_ref[k * rows : (k + 1) * rows] = ref[:, wide:]
+
+
+def piece_kernel(replicas, frozen_ref, out_ref, sem):
+    rows = out_ref.shape[0]
+    at = (lax.axis_index("groups") * replicas + lax.axis_index("replica")) * rows
+    copy = pltpu.make_async_copy(
+        frozen_ref.at[pl.ds(pl.multiple_of(at, rows), rows)], out_ref, sem
+    )
+    copy.start()
+    copy.wait()
 
 
 def own_kernel(sizes, down_ref, up_ref, out_ref):
@@ -191,18 +201,15 @@
         ref[...] = block_ref[j * rows : (j + 1) * rows]
 
 
-def place_kernel(sizes, batches, *refs):
+def place_kernel(sizes, places, *refs):
     groups, holders, shard, half = sizes
     group, here = lax.axis_index("groups"), lax.axis_index("adapter")
     out_ref = refs[-1]
-    for i, batch in enumerate(batches):
-        for dg in range(groups):
-            source = lax.rem(group + groups - dg, groups)
-            for j, k in enumerate(batch):
-                at = lax.rem(here + holders - k, holders) * shard + source * half
-                out_ref[:, pl.ds(pl.multiple_of(at, half), half)] = refs[i * groups + dg][
-                    :, j * half : (j + 1) * half
-                ]
+    for ref, (batch, dg) in zip(refs, places):
+        source = lax.rem(group + groups - dg, groups)
+        for j, k in enumerate(batch):
+            at = lax.rem(here + holders - k, holders) * shard + source * half
+            out_ref[:, pl.ds(pl.multiple_of(at, half), half)] = ref[:, j * half : (j + 1) * half]
 
 
 def chip_kernel(replicas, *refs):
@@ -287,7 +294,17 @@
     for k in range(1, holders):
         held.append(moved(own, lambda g, z, s, r: (g, z + k, s, r)))
 
-    ring = [lax.dynamic_slice_in_dim(frozen, (group * replicas + core) * piece, piece, axis=0)]
+    ring = [
+        pl.pallas_call(
+            functools.partial(piece_kernel, replicas),
+            out_shape=jax.ShapeDtypeStruct((piece, value_width), BF16),
+            in_specs=[pl.BlockSpec(memory_space=pltpu.HBM)],
+            out_specs=pl.BlockSpec(memory_space=pltpu.VMEM),
+            scratch_shapes=[pltpu.SemaphoreType.DMA],
+            compiler_params=pltpu.CompilerParams(vmem_limit_bytes=4 * MIB),
+            cost_estimate=pl.CostEstimate(flops=1000, bytes_accessed=1000, transcendentals=0),
+        )(frozen)
+    ]
     ring.append(moved(ring[0], lambda g, z, s, r: (g, z + 1, s, r)))
     held, grads, ring = lax.optimization_barrier((held, grads, ring))
     joined = call(
@@ -394,10 +411,13 @@
         )
         if i == 0:
             part, chip = adapter_sums(sel, *arrived[0])
+    places = [(batch, dg) for batch in batches for dg in range(groups)]
+    parts = dict(zip([(b[0], dg) for b, dg in places], [x for got in arrived for x in got]))
+    places[-groups:] = places[-groups:][::-1]
     passed = call(
-        functools.partial(place_kernel, (groups, holders, shard, half), batches),
+        functools.partial(place_kernel, (groups, holders, shard, half), places),
         [jax.ShapeDtypeStruct((tokens, width), BF16)],
-        [x for got in arrived for x in got],
+        [parts[batch[0], dg] for batch, dg in places],
     )[0]
 
     sums = [chip[0]] + [

time: 78.6 us -> 77.7 us (0.989)
  local copies, waits for them, and re-layouts: 5.37 us -> 1.65 us
  starting transfers between devices: 29.8 us -> 31.3 us
    unnamed x14 -> x16, local copies, waits for them, and re-layouts: 4.12 us -> 1.63 us
    ppermute x29, starting transfers between devices: 29.8 us -> 31.3 us  [moved(): return lax.ppermute(x, AXES, pairs)]
    dynamic_slice x1 -> x0, local copies, waits for them, and re-layouts: 1.23 us -> none  [on_device(): lax.dynamic_slice_in_dim(frozen, (group * replicas + core) * piece, piece...]
  transfers between devices with their start and end apart: 29 -> 29, of which waited for: 13 -> 12; matrix products, arithmetic and copies ran while one was open for 0% -> 0% of each run, Pallas kernels for 10% -> 10%
where the time goes in v15:
time: 77.7 us; the launch traced here: 76.9 us
  waiting for transfers between devices  34.1 us (44%)
  starting transfers between devices  31.3 us (40%)
  Pallas kernels  9 us (12%)
  local copies, waits for them, and re-layouts  1.65 us (2%)
  between operations  0.83 us (1%)
    ppermute x29, waiting for transfers between devices, moved(): return lax.ppermute(x, AXES, pairs)  34.1 us
    ppermute x29, starting transfers between devices, moved(): return lax.ppermute(x, AXES, pairs)  31.3 us
    pallas_call x13, Pallas kernels, call(): pl.pallas_call(kernel, out_shape=out_shape, in_specs=[pl.BlockSpec(memory...  8.94 us
    unnamed x16, local copies, waits for them, and re-layouts  1.63 us
  transfers between devices with their start and end apart: 29, of which 12 were waited for; matrix products, arithmetic and copies ran while one was open for 0% of the time, Pallas kernels for 10%

profile of v15, /device:TPU:0, one launch (start us, length us, event | category | flops | bytes accessed | tf_op | source)
XLA Modules:
  0.0 76.9 jit_solution(15377325995400212757)
XLA Ops:
  0.7 1.6 %copy-done = bf16[1,1024,1024]{2,1,0:T(8,128)(2,1)S(1)} copy-done((bf16[1,1024,1024]{2,1,0:T(8,128)(2,1)S(1)}, bf16[1,1024,1024]{2,1,0:T(8,128)(2,1)}, u32[]{:S(2)}) %copy-start) | copy-done | bytes 2097176
  2.3 3.1 %collective-permute-start.4 = (bf16[256,1024]{1,0:T(8,128)(2,1)S(1)}, bf16[256,1024]{1,0:T(8,128)(2,1)S(1)}, u32[]{:S(2)}, u32[]{:S(2)}) collective-permute-start(bf16[256,1024]{1,0:T(8,128)(2,1)S(1)} %shard_map.96), channel_id=1, source_target_pairs={{0,4},{1,5},{2,6},{3,7},{4,8},{5,9},{6,10},{7,11},{8,12},{9,13},{1... | collective-permute-start | bytes 1572872 | tf_op jit(solution)/shard_map/ppermute | solution.py:24
  5.4 0.8 shard_map.95.refs_0_.refs_1_
  6.2 1.6 %collective-permute-start.3 = (bf16[176,1152]{1,0:T(8,128)(2,1)S(1)}, bf16[176,1152]{1,0:T(8,128)(2,1)S(1)}, u32[]{:S(2)}, u32[]{:S(2)}) collective-permute-start(bf16[176,1152]{1,0:T(8,128)(2,1)S(1)} %shard_map.95.refs_0_.refs_1_), channel_id=1, source_target_pairs={{0,16},{1,17},{2,18},{3,19},{4,20},{5,21},{6,22},{7,23},{8,24},{9,... | collective-permute-start | bytes 1216520 | tf_op jit(solution)/shard_map/ppermute | solution.py:24
  7.8 1.6 %collective-permute-start = (bf16[16,3072]{1,0:T(8,128)(2,1)S(1)}, bf16[16,3072]{1,0:T(8,128)(2,1)S(1)}, u32[]{:S(2)}, u32[]{:S(2)}) collective-permute-start(bf16[16,3072]{1,0:T(8,128)(2,1)S(1)} %shard_map.94.refs_0_), channel_id=1, source_target_pairs={{0,4},{1,5},{2,6},{3,7},{4,8},{5,9},{6,10},{7,11},{8,12},{9,13},{1... | collective-permute-start | bytes 294920 | tf_op jit(solution)/shard_map/ppermute | solution.py:24
  9.4 1.9 %collective-permute-start.1 = (bf16[16,3072]{1,0:T(8,128)(2,1)S(1)}, bf16[16,3072]{1,0:T(8,128)(2,1)S(1)}, u32[]{:S(2)}, u32[]{:S(2)}) collective-permute-start(bf16[16,3072]{1,0:T(8,128)(2,1)S(1)} %shard_map.94.refs_0_), channel_id=1, source_target_pairs={{0,8},{1,9},{2,10},{3,11},{4,12},{5,13},{6,14},{7,15},{8,0},{9,1},... | collective-permute-start | bytes 294920 | tf_op jit(solution)/shard_map/ppermute | solution.py:24
  11.3 2.1 %collective-permute-start.2 = (bf16[16,3072]{1,0:T(8,128)(2,1)S(1)}, bf16[16,3072]{1,0:T(8,128)(2,1)S(1)}, u32[]{:S(2)}, u32[]{:S(2)}) collective-permute-start(bf16[16,3072]{1,0:T(8,128)(2,1)S(1)} %shard_map.94.refs_0_), channel_id=1, source_target_pairs={{0,12},{1,13},{2,14},{3,15},{4,0},{5,1},{6,2},{7,3},{8,4},{9,5},{1... | collective-permute-start | bytes 294920 | tf_op jit(solution)/shard_map/ppermute | solution.py:24
  13.4 9.1 %collective-permute-done.refs_1_ = bf16[16,3072]{1,0:T(8,128)(2,1)S(1)} collective-permute-done((bf16[16,3072]{1,0:T(8,128)(2,1)S(1)}, bf16[16,3072]{1,0:T(8,128)(2,1)S(1)}, u32[]{:S(2)}, u32[]{:S(2)}) %collective-permute-start) | collective-permute-done | bytes 98336 | tf_op jit(solution)/shard_map/ppermute | solution.py:24
  22.4 3.4 %collective-permute-done.1.refs_2_ = bf16[16,3072]{1,0:T(8,128)(2,1)S(1)} collective-permute-done((bf16[16,3072]{1,0:T(8,128)(2,1)S(1)}, bf16[16,3072]{1,0:T(8,128)(2,1)S(1)}, u32[]{:S(2)}, u32[]{:S(2)}) %collective-permute-start.1) | collective-permute-done | bytes 98336 | tf_op jit(solution)/shard_map/ppermute | solution.py:24
  25.9 2.6 %collective-permute-start.10 = (bf16[256,1024]{1,0:T(8,128)(2,1)S(1)}, bf16[256,1024]{1,0:T(8,128)(2,1)S(1)}, u32[]{:S(2)}, u32[]{:S(2)}) collective-permute-start(bf16[256,1024]{1,0:T(8,128)(2,1)S(1)} %collective-permute-done.4.refs_7_), channel_id=1, source_target_pairs={{0,4},{1,5},{2,6},{3,7},{4,8},{5,9},{6,10},{7,11},{8,12},{9,13},{1... | collective-permute-start | bytes 1572872 | tf_op jit(solution)/shard_map/ppermute | solution.py:24
  28.7 1.5 %collective-permute-start.16 = (bf16[64,2048]{1,0:T(8,128)(2,1)S(1)}, bf16[64,2048]{1,0:T(8,128)(2,1)S(1)}, u32[]{:S(2)}, u32[]{:S(2)}) collective-permute-start(bf16[64,2048]{1,0:T(8,128)(2,1)S(1)} %get-tuple-element.48.refs_2_.refs_3_), channel_id=1, source_target_pairs={{0,16},{1,17},{2,18},{3,19},{4,20},{5,21},{6,22},{7,23},{8,24},{9,... | collective-permute-start | bytes 786440 | tf_op jit(solution)/shard_map/ppermute | solution.py:24
  30.3 1.3 %collective-permute-done.6.refs_5_ = bf16[64,1024]{1,0:T(8,128)(2,1)S(1)} collective-permute-done((bf16[64,1024]{1,0:T(8,128)(2,1)S(1)}, bf16[64,1024]{1,0:T(8,128)(2,1)S(1)}, u32[]{:S(2)}, u32[]{:S(2)}) %collective-permute-start.6) | collective-permute-done | bytes 131104 | tf_op jit(solution)/shard_map/ppermute | solution.py:24
  31.6 2.2 %shard_map.98 = (bf16[176,1024]{1,0:T(8,128)(2,1)S(1)}, bf16[176,1024]{1,0:T(8,128)(2,1)S(1)}, bf16[352,128]{1,0:T(8,128)(2,1)S(1)}) custom-call(bf16[176,1152]{1,0:T(8,128)(2,1)S(1)} %shard_map.95.refs_0_.refs_1_, bf16[176,1152]{1,0:T(8,128)(2,1)S(1)} %collective-permute-done.3.refs_1_, bf16[64,2048]{1,0:T(8,128)(2,1)S(1)} %get-tuple-element.48.refs_2_.refs_3_, ...), custom_call_target="tpu_custom_call" | custom-call | flops 1000 | bytes 1000 | tf_op jit(solution)/shard_map/pallas_call | solution.py:41
  33.9 1.6 %collective-permute-start.8 = (bf16[176,1024]{1,0:T(8,128)(2,1)S(1)}, bf16[176,1024]{1,0:T(8,128)(2,1)S(1)}, u32[]{:S(2)}, u32[]{:S(2)}) collective-permute-start(bf16[176,1024]{1,0:T(8,128)(2,1)S(1)} %get-tuple-element.51), channel_id=1, source_target_pairs={{0,2},{1,3},{2,0},{3,1},{4,6},{5,7},{6,4},{7,5},{8,10},{9,11},{10,... | collective-permute-start | bytes 1081352 | tf_op jit(solution)/shard_map/ppermute | solution.py:24
  35.9 1.4 %collective-permute-done.16.refs_5_ = bf16[64,2048]{1,0:T(8,128)(2,1)S(1)} collective-permute-done((bf16[64,2048]{1,0:T(8,128)(2,1)S(1)}, bf16[64,2048]{1,0:T(8,128)(2,1)S(1)}, u32[]{:S(2)}, u32[]{:S(2)}) %collective-permute-start.16) | collective-permute-done | bytes 262176 | tf_op jit(solution)/shard_map/ppermute | solution.py:24
  37.3 4.8 %collective-permute-done.10.block_ref.refs_5_ = bf16[256,1024]{1,0:T(8,128)(2,1)S(1)} collective-permute-done((bf16[256,1024]{1,0:T(8,128)(2,1)S(1)}, bf16[256,1024]{1,0:T(8,128)(2,1)S(1)}, u32[]{:S(2)}, u32[]{:S(2)}) %collective-permute-start.10) | collective-permute-done | bytes 524320 | tf_op jit(solution)/shard_map/ppermute | solution.py:24
  42.1 0.7 collective-permute-start.15
  42.8 2.4 %collective-permute-done.8.refs_0_ = bf16[176,1024]{1,0:T(8,128)(2,1)S(1)} collective-permute-done((bf16[176,1024]{1,0:T(8,128)(2,1)S(1)}, bf16[176,1024]{1,0:T(8,128)(2,1)S(1)}, u32[]{:S(2)}, u32[]{:S(2)}) %collective-permute-start.8) | collective-permute-done | bytes 360480 | tf_op jit(solution)/shard_map/ppermute | solution.py:24
  45.2 6.9 %collective-permute-done.9.refs_1_ = bf16[176,1024]{1,0:T(8,128)(2,1)S(1)} collective-permute-done((bf16[176,1024]{1,0:T(8,128)(2,1)S(1)}, bf16[176,1024]{1,0:T(8,128)(2,1)S(1)}, u32[]{:S(2)}, u32[]{:S(2)}) %collective-permute-start.9) | collective-permute-done | bytes 360480 | tf_op jit(solution)/shard_map/ppermute | solution.py:24
  52.6 1.3 %shard_map.102 = (f32[64,5120]{1,0:T(8,128)S(1)}, bf16[64,2560]{1,0:T(8,128)(2,1)S(1)}, bf16[64,2560]{1,0:T(8,128)(2,1)S(1)}) custom-call(bf16[176,4096]{1,0:T(8,128)(2,1)S(1)} %bitcast.11, bf16[176,1152]{1,0:T(8,128)(2,1)S(1)} %shard_map.95.refs_0_.refs_1_, bf16[352,128]{1,0:T(8,128)(2,1)S(1)} %get-tuple-element.53.refs_4_.refs_2_, ...), custom_call_target="tpu_custom_call" | custom-call | flops 1000 | bytes 1000 | tf_op jit(solution)/shard_map/pallas_call | solution.py:41
  54.5 1.2 %shard_map.100 = bf16[352,512]{1,0:T(8,128)(2,1)S(1)} custom-call(bf16[176,1152]{1,0:T(8,128)(2,1)S(1)} %shard_map.95.refs_0_.refs_1_, bf16[176,1152]{1,0:T(8,128)(2,1)S(1)} %collective-permute-done.3.refs_1_, bf16[64,2048]{1,0:T(8,128)(2,1)S(1)} %get-tuple-element.48.refs_2_.refs_3_, bf16[64,2048]{1,0:T(8,128)(2,1)S(1)} %collective-permute-done.5.refs_3_.refs_4_, ...), custom_call_target="tpu_custom_call" | custom-call | flops 1000 | bytes 1000 | tf_op jit(solution)/shard_map/pallas_call | solution.py:41
  55.6 1.6 %collective-permute-start.13 = (bf16[352,512]{1,0:T(8,128)(2,1)S(1)}, bf16[352,512]{1,0:T(8,128)(2,1)S(1)}, u32[]{:S(2)}, u32[]{:S(2)}) collective-permute-start(bf16[352,512]{1,0:T(8,128)(2,1)S(1)} %shard_map.100), channel_id=1, source_target_pairs={{0,2},{1,3},{2,0},{3,1},{4,6},{5,7},{6,4},{7,5},{8,10},{9,11},{10,... | collective-permute-start | bytes 1081352 | tf_op jit(solution)/shard_map/ppermute | solution.py:24
  58.3 1.6 %collective-permute-start.25 = (bf16[16,5120]{1,0:T(8,128)(2,1)S(1)}, bf16[16,5120]{1,0:T(8,128)(2,1)S(1)}, u32[]{:S(2)}, u32[]{:S(2)}) collective-permute-start(bf16[16,5120]{1,0:T(8,128)(2,1)S(1)} %get-tuple-element.74), channel_id=1, source_target_pairs={{0,8},{1,9},{2,10},{3,11},{4,12},{5,13},{6,14},{7,15},{8,0},{9,1},... | collective-permute-start | bytes 491528 | tf_op jit(solution)/shard_map/ppermute | solution.py:24
  59.9 2.7 %collective-permute-start.24 = (bf16[16,5120]{1,0:T(8,128)(2,1)S(1)}, bf16[16,5120]{1,0:T(8,128)(2,1)S(1)}, u32[]{:S(2)}, u32[]{:S(2)}) collective-permute-start(bf16[16,5120]{1,0:T(8,128)(2,1)S(1)} %get-tuple-element.72), channel_id=1, source_target_pairs={{0,12},{1,13},{2,14},{3,15},{4,0},{5,1},{6,2},{7,3},{8,4},{9,5},{1... | collective-permute-start | bytes 491528 | tf_op jit(solution)/shard_map/ppermute | solution.py:24
  62.6 1.2 %shard_map.104 = (bf16[176,512]{1,0:T(8,128)(2,1)S(1)}, bf16[176,512]{1,0:T(8,128)(2,1)S(1)}) custom-call(bf16[176,1152]{1,0:T(8,128)(2,1)S(1)} %shard_map.95.refs_0_.refs_1_, bf16[176,1152]{1,0:T(8,128)(2,1)S(1)} %collective-permute-done.3.refs_1_, bf16[64,2048]{1,0:T(8,128)(2,1)S(1)} %get-tuple-element.48.refs_2_.refs_3_, ...), custom_call_target="tpu_custom_call" | custom-call | flops 1000 | bytes 1000 | tf_op jit(solution)/shard_map/pallas_call | solution.py:41
  63.8 2.0 %collective-permute-start.22 = (bf16[176,512]{1,0:T(8,128)(2,1)S(1)}, bf16[176,512]{1,0:T(8,128)(2,1)S(1)}, u32[]{:S(2)}, u32[]{:S(2)}) collective-permute-start(bf16[176,512]{1,0:T(8,128)(2,1)S(1)} %get-tuple-element.69), channel_id=1, source_target_pairs={{0,18},{1,19},{2,16},{3,17},{4,22},{5,23},{6,20},{7,21},{8,26},{9,... | collective-permute-start | bytes 540680 | tf_op jit(solution)/shard_map/ppermute | solution.py:24
  66.1 1.5 %collective-permute-start.23 = (bf16[176,512]{1,0:T(8,128)(2,1)S(1)}, bf16[176,512]{1,0:T(8,128)(2,1)S(1)}, u32[]{:S(2)}, u32[]{:S(2)}) collective-permute-start(bf16[176,512]{1,0:T(8,128)(2,1)S(1)} %get-tuple-element.70), channel_id=1, source_target_pairs={{0,2},{1,3},{2,0},{3,1},{4,6},{5,7},{6,4},{7,5},{8,10},{9,11},{10,... | collective-permute-start | bytes 540680 | tf_op jit(solution)/shard_map/ppermute | solution.py:24
  67.6 2.3 %collective-permute-start.14 = (bf16[176,512]{1,0:T(8,128)(2,1)S(1)}, bf16[176,512]{1,0:T(8,128)(2,1)S(1)}, u32[]{:S(2)}, u32[]{:S(2)}) collective-permute-start(bf16[176,512]{1,0:T(8,128)(2,1)S(1)} %get-tuple-element.81), channel_id=1, source_target_pairs={{0,16},{1,17},{2,18},{3,19},{4,20},{5,21},{6,22},{7,23},{8,24},{9,... | collective-permute-start | bytes 540680 | tf_op jit(solution)/shard_map/ppermute | solution.py:24
  69.9 3.4 %collective-permute-done.25.refs_2_ = bf16[16,5120]{1,0:T(8,128)(2,1)S(1)} collective-permute-done((bf16[16,5120]{1,0:T(8,128)(2,1)S(1)}, bf16[16,5120]{1,0:T(8,128)(2,1)S(1)}, u32[]{:S(2)}, u32[]{:S(2)}) %collective-permute-start.25) | collective-permute-done | bytes 163872 | tf_op jit(solution)/shard_map/ppermute | solution.py:24
  74.0 0.8 collective-permute-done.27.refs_2_
  74.9 0.8 shard_map.107
  75.7 1.2 %shard_map.105 = bf16[176,4096]{1,0:T(8,128)(2,1)} custom-call(bf16[176,1024]{1,0:T(8,128)(2,1)S(1)} %collective-permute-done.8.refs_0_, bf16[176,1024]{1,0:T(8,128)(2,1)S(1)} %collective-permute-done.9.refs_1_, bf16[176,512]{1,0:T(8,128)(2,1)S(1)} %get-tuple-element.82.refs_2_, bf16[176,512]{1,0:T(8,128)(2,1)S(1)} %collective-permute-done.14.refs_3_, ...), custom_call_target="tpu_custom_call" | custom-call | flops 1000 | bytes 1000 | tf_op jit(solution)/shard_map/pallas_call | solution.py:41
  (57 shorter events, 4.3 us)
Async XLA Ops:
  2.3 5.5 %copy-start.5 = (bf16[1,2,16,1024]{3,2,1,0:T(8,128)(2,1)S(1)}, bf16[1,2,16,1024]{3,2,1,0:T(8,128)(2,1)}, u32[]{:S(2)}) copy-start(bf16[1,2,16,1024]{3,2,1,0:T(8,128)(2,1)} %param.13) | copy-start | bytes 196612
  2.3 29.3 %copy-start.1 = (bf16[1,1024,1024]{2,1,0:T(8,128)(2,1)S(1)}, bf16[1,1024,1024]{2,1,0:T(8,128)(2,1)}, u32[]{:S(2)}) copy-start(bf16[1,1024,1024]{2,1,0:T(8,128)(2,1)} %param.11) | copy-start | bytes 6291460
  2.3 23.5 %collective-permute-start.4 = (bf16[256,1024]{1,0:T(8,128)(2,1)S(1)}, bf16[256,1024]{1,0:T(8,128)(2,1)S(1)}, u32[]{:S(2)}, u32[]{:S(2)}) collective-permute-start(bf16[256,1024]{1,0:T(8,128)(2,1)S(1)} %shard_map.96), channel_id=1, source_target_pairs={{0,4},{1,5},{2,6},{3,7},{4,8},{5,9},{6,10},{7,11},{8,12},{9,13},{1... | collective-permute-start | bytes 1572872 | tf_op jit(solution)/shard_map/ppermute | solution.py:24
  6.2 19.6 %collective-permute-start.3 = (bf16[176,1152]{1,0:T(8,128)(2,1)S(1)}, bf16[176,1152]{1,0:T(8,128)(2,1)S(1)}, u32[]{:S(2)}, u32[]{:S(2)}) collective-permute-start(bf16[176,1152]{1,0:T(8,128)(2,1)S(1)} %shard_map.95.refs_0_.refs_1_), channel_id=1, source_target_pairs={{0,16},{1,17},{2,18},{3,19},{4,20},{5,21},{6,22},{7,23},{8,24},{9,... | collective-permute-start | bytes 1216520 | tf_op jit(solution)/shard_map/ppermute | solution.py:24
  7.8 14.6 %collective-permute-start = (bf16[16,3072]{1,0:T(8,128)(2,1)S(1)}, bf16[16,3072]{1,0:T(8,128)(2,1)S(1)}, u32[]{:S(2)}, u32[]{:S(2)}) collective-permute-start(bf16[16,3072]{1,0:T(8,128)(2,1)S(1)} %shard_map.94.refs_0_), channel_id=1, source_target_pairs={{0,4},{1,5},{2,6},{3,7},{4,8},{5,9},{6,10},{7,11},{8,12},{9,13},{1... | collective-permute-start | bytes 294920 | tf_op jit(solution)/shard_map/ppermute | solution.py:24
  9.4 16.4 %collective-permute-start.1 = (bf16[16,3072]{1,0:T(8,128)(2,1)S(1)}, bf16[16,3072]{1,0:T(8,128)(2,1)S(1)}, u32[]{:S(2)}, u32[]{:S(2)}) collective-permute-start(bf16[16,3072]{1,0:T(8,128)(2,1)S(1)} %shard_map.94.refs_0_), channel_id=1, source_target_pairs={{0,8},{1,9},{2,10},{3,11},{4,12},{5,13},{6,14},{7,15},{8,0},{9,1},... | collective-permute-start | bytes 294920 | tf_op jit(solution)/shard_map/ppermute | solution.py:24
  11.3 14.5 %collective-permute-start.2 = (bf16[16,3072]{1,0:T(8,128)(2,1)S(1)}, bf16[16,3072]{1,0:T(8,128)(2,1)S(1)}, u32[]{:S(2)}, u32[]{:S(2)}) collective-permute-start(bf16[16,3072]{1,0:T(8,128)(2,1)S(1)} %shard_map.94.refs_0_), channel_id=1, source_target_pairs={{0,12},{1,13},{2,14},{3,15},{4,0},{5,1},{6,2},{7,3},{8,4},{9,5},{1... | collective-permute-start | bytes 294920 | tf_op jit(solution)/shard_map/ppermute | solution.py:24
  25.8 5.8 %collective-permute-start.7 = (bf16[256,1024]{1,0:T(8,128)(2,1)S(1)}, bf16[256,1024]{1,0:T(8,128)(2,1)S(1)}, u32[]{:S(2)}, u32[]{:S(2)}) collective-permute-start(bf16[256,1024]{1,0:T(8,128)(2,1)S(1)} %collective-permute-done.4.refs_7_), channel_id=1, source_target_pairs={{0,1},{1,0},{2,3},{3,2},{4,5},{5,4},{6,7},{7,6},{8,9},{9,8},{10,11... | collective-permute-start | bytes 1572872 | tf_op jit(solution)/shard_map/ppermute | solution.py:24
  25.9 16.2 %collective-permute-start.10 = (bf16[256,1024]{1,0:T(8,128)(2,1)S(1)}, bf16[256,1024]{1,0:T(8,128)(2,1)S(1)}, u32[]{:S(2)}, u32[]{:S(2)}) collective-permute-start(bf16[256,1024]{1,0:T(8,128)(2,1)S(1)} %collective-permute-done.4.refs_7_), channel_id=1, source_target_pairs={{0,4},{1,5},{2,6},{3,7},{4,8},{5,9},{6,10},{7,11},{8,12},{9,13},{1... | collective-permute-start | bytes 1572872 | tf_op jit(solution)/shard_map/ppermute | solution.py:24
  28.5 3.1 %collective-permute-start.5 = (bf16[64,2048]{1,0:T(8,128)(2,1)S(1)}, bf16[64,2048]{1,0:T(8,128)(2,1)S(1)}, u32[]{:S(2)}, u32[]{:S(2)}) collective-permute-start(bf16[64,2048]{1,0:T(8,128)(2,1)S(1)} %get-tuple-element.48.refs_2_.refs_3_), channel_id=1, source_target_pairs={{0,1},{1,0},{2,3},{3,2},{4,5},{5,4},{6,7},{7,6},{8,9},{9,8},{10,11... | collective-permute-start | bytes 786440 | tf_op jit(solution)/shard_map/ppermute | solution.py:24
  28.7 8.6 %collective-permute-start.16 = (bf16[64,2048]{1,0:T(8,128)(2,1)S(1)}, bf16[64,2048]{1,0:T(8,128)(2,1)S(1)}, u32[]{:S(2)}, u32[]{:S(2)}) collective-permute-start(bf16[64,2048]{1,0:T(8,128)(2,1)S(1)} %get-tuple-element.48.refs_2_.refs_3_), channel_id=1, source_target_pairs={{0,16},{1,17},{2,18},{3,19},{4,20},{5,21},{6,22},{7,23},{8,24},{9,... | collective-permute-start | bytes 786440 | tf_op jit(solution)/shard_map/ppermute | solution.py:24
  30.2 1.3 %collective-permute-start.6 = (bf16[64,1024]{1,0:T(8,128)(2,1)S(1)}, bf16[64,1024]{1,0:T(8,128)(2,1)S(1)}, u32[]{:S(2)}, u32[]{:S(2)}) collective-permute-start(bf16[64,1024]{1,0:T(8,128)(2,1)S(1)} %get-tuple-element.49.refs_4_), channel_id=1, source_target_pairs={{0,1},{1,0},{2,3},{3,2},{4,5},{5,4},{6,7},{7,6},{8,9},{9,8},{10,11... | collective-permute-start | bytes 393224 | tf_op jit(solution)/shard_map/ppermute | solution.py:24
  31.6 21.0 %copy-start.2 = (bf16[1,176,4096]{2,1,0:T(8,128)(2,1)S(1)}, bf16[1,176,4096]{2,1,0:T(8,128)(2,1)}, u32[]{:S(2)}) copy-start(bf16[1,176,4096]{2,1,0:T(8,128)(2,1)} %param.7) | copy-start | bytes 4325380
  33.9 11.3 %collective-permute-start.8 = (bf16[176,1024]{1,0:T(8,128)(2,1)S(1)}, bf16[176,1024]{1,0:T(8,128)(2,1)S(1)}, u32[]{:S(2)}, u32[]{:S(2)}) collective-permute-start(bf16[176,1024]{1,0:T(8,128)(2,1)S(1)} %get-tuple-element.51), channel_id=1, source_target_pairs={{0,2},{1,3},{2,0},{3,1},{4,6},{5,7},{6,4},{7,5},{8,10},{9,11},{10,... | collective-permute-start | bytes 1081352 | tf_op jit(solution)/shard_map/ppermute | solution.py:24
  35.4 16.6 %collective-permute-start.9 = (bf16[176,1024]{1,0:T(8,128)(2,1)S(1)}, bf16[176,1024]{1,0:T(8,128)(2,1)S(1)}, u32[]{:S(2)}, u32[]{:S(2)}) collective-permute-start(bf16[176,1024]{1,0:T(8,128)(2,1)S(1)} %get-tuple-element.52), channel_id=1, source_target_pairs={{0,18},{1,19},{2,16},{3,17},{4,22},{5,23},{6,20},{7,21},{8,26},{9,... | collective-permute-start | bytes 1081352 | tf_op jit(solution)/shard_map/ppermute | solution.py:24
  37.3 15.3 %collective-permute-start.17 = (bf16[64,2048]{1,0:T(8,128)(2,1)S(1)}, bf16[64,2048]{1,0:T(8,128)(2,1)S(1)}, u32[]{:S(2)}, u32[]{:S(2)}) collective-permute-start(bf16[64,2048]{1,0:T(8,128)(2,1)S(1)} %collective-permute-done.16.refs_5_), channel_id=1, source_target_pairs={{0,1},{1,0},{2,3},{3,2},{4,5},{5,4},{6,7},{7,6},{8,9},{9,8},{10,11... | collective-permute-start | bytes 786440 | tf_op jit(solution)/shard_map/ppermute | solution.py:24
  42.1 15.3 %collective-permute-start.15 = (bf16[256,1024]{1,0:T(8,128)(2,1)S(1)}, bf16[256,1024]{1,0:T(8,128)(2,1)S(1)}, u32[]{:S(2)}, u32[]{:S(2)}) collective-permute-start(bf16[256,1024]{1,0:T(8,128)(2,1)S(1)} %collective-permute-done.10.block_ref.refs_5_), channel_id=1, source_target_pairs={{0,4},{1,5},{2,6},{3,7},{4,8},{5,9},{6,10},{7,11},{8,12},{9,13},{1... | collective-permute-start | bytes 1572872 | tf_op jit(solution)/shard_map/ppermute | solution.py:24
  52.1 2.4 %collective-permute-start.12 = (bf16[128,1024]{1,0:T(8,128)(2,1)S(1)}, bf16[128,1024]{1,0:T(8,128)(2,1)S(1)}, u32[]{:S(2)}, u32[]{:S(2)}) collective-permute-start(bf16[128,1024]{1,0:T(8,128)(2,1)S(1)} %get-tuple-element.57), channel_id=1, source_target_pairs={{0,1},{1,0},{2,3},{3,2},{4,5},{5,4},{6,7},{7,6},{8,9},{9,8},{10,11... | collective-permute-start | bytes 786440 | tf_op jit(solution)/shard_map/ppermute | solution.py:24
  52.1 2.4 %collective-permute-start.11 = (bf16[128,1024]{1,0:T(8,128)(2,1)S(1)}, bf16[128,1024]{1,0:T(8,128)(2,1)S(1)}, u32[]{:S(2)}, u32[]{:S(2)}) collective-permute-start(bf16[128,1024]{1,0:T(8,128)(2,1)S(1)} %get-tuple-element.55), channel_id=1, source_target_pairs={{0,1},{1,0},{2,3},{3,2},{4,5},{5,4},{6,7},{7,6},{8,9},{9,8},{10,11... | collective-permute-start | bytes 786440 | tf_op jit(solution)/shard_map/ppermute | solution.py:24
  53.9 3.6 %collective-permute-start.19 = (bf16[64,2560]{1,0:T(8,128)(2,1)S(1)}, bf16[64,2560]{1,0:T(8,128)(2,1)S(1)}, u32[]{:S(2)}, u32[]{:S(2)}) collective-permute-start(bf16[64,2560]{1,0:T(8,128)(2,1)S(1)} %get-tuple-element.64), channel_id=1, source_target_pairs={{0,1},{1,0},{2,3},{3,2},{4,5},{5,4},{6,7},{7,6},{8,9},{9,8},{10,11... | collective-permute-start | bytes 983048 | tf_op jit(solution)/shard_map/ppermute | solution.py:24
  54.0 3.5 %collective-permute-start.18 = (bf16[64,2560]{1,0:T(8,128)(2,1)S(1)}, bf16[64,2560]{1,0:T(8,128)(2,1)S(1)}, u32[]{:S(2)}, u32[]{:S(2)}) collective-permute-start(bf16[64,2560]{1,0:T(8,128)(2,1)S(1)} %get-tuple-element.62), channel_id=1, source_target_pairs={{0,1},{1,0},{2,3},{3,2},{4,5},{5,4},{6,7},{7,6},{8,9},{9,8},{10,11... | collective-permute-start | bytes 983048 | tf_op jit(solution)/shard_map/ppermute | solution.py:24
  55.6 10.5 %collective-permute-start.13 = (bf16[352,512]{1,0:T(8,128)(2,1)S(1)}, bf16[352,512]{1,0:T(8,128)(2,1)S(1)}, u32[]{:S(2)}, u32[]{:S(2)}) collective-permute-start(bf16[352,512]{1,0:T(8,128)(2,1)S(1)} %shard_map.100), channel_id=1, source_target_pairs={{0,2},{1,3},{2,0},{3,1},{4,6},{5,7},{6,4},{7,5},{8,10},{9,11},{10,... | collective-permute-start | bytes 1081352 | tf_op jit(solution)/shard_map/ppermute | solution.py:24
  57.7 2.3 %collective-permute-start.21 = (bf16[128,1024]{1,0:T(8,128)(2,1)S(1)}, bf16[128,1024]{1,0:T(8,128)(2,1)S(1)}, u32[]{:S(2)}, u32[]{:S(2)}) collective-permute-start(bf16[128,1024]{1,0:T(8,128)(2,1)S(1)} %get-tuple-element.68), channel_id=1, source_target_pairs={{0,1},{1,0},{2,3},{3,2},{4,5},{5,4},{6,7},{7,6},{8,9},{9,8},{10,11... | collective-permute-start | bytes 786440 | tf_op jit(solution)/shard_map/ppermute | solution.py:24
  57.7 4.8 %collective-permute-start.20 = (bf16[128,1024]{1,0:T(8,128)(2,1)S(1)}, bf16[128,1024]{1,0:T(8,128)(2,1)S(1)}, u32[]{:S(2)}, u32[]{:S(2)}) collective-permute-start(bf16[128,1024]{1,0:T(8,128)(2,1)S(1)} %get-tuple-element.66), channel_id=1, source_target_pairs={{0,1},{1,0},{2,3},{3,2},{4,5},{5,4},{6,7},{7,6},{8,9},{9,8},{10,11... | collective-permute-start | bytes 786440 | tf_op jit(solution)/shard_map/ppermute | solution.py:24
  58.2 9.4 %collective-permute-start.26 = (bf16[16,5120]{1,0:T(8,128)(2,1)S(1)}, bf16[16,5120]{1,0:T(8,128)(2,1)S(1)}, u32[]{:S(2)}, u32[]{:S(2)}) collective-permute-start(bf16[16,5120]{1,0:T(8,128)(2,1)S(1)} %get-tuple-element.76), channel_id=1, source_target_pairs={{0,4},{1,5},{2,6},{3,7},{4,8},{5,9},{6,10},{7,11},{8,12},{9,13},{1... | collective-permute-start | bytes 491528 | tf_op jit(solution)/shard_map/ppermute | solution.py:24
  58.3 15.0 %collective-permute-start.25 = (bf16[16,5120]{1,0:T(8,128)(2,1)S(1)}, bf16[16,5120]{1,0:T(8,128)(2,1)S(1)}, u32[]{:S(2)}, u32[]{:S(2)}) collective-permute-start(bf16[16,5120]{1,0:T(8,128)(2,1)S(1)} %get-tuple-element.74), channel_id=1, source_target_pairs={{0,8},{1,9},{2,10},{3,11},{4,12},{5,13},{6,14},{7,15},{8,0},{9,1},... | collective-permute-start | bytes 491528 | tf_op jit(solution)/shard_map/ppermute | solution.py:24
  59.9 13.4 %collective-permute-start.24 = (bf16[16,5120]{1,0:T(8,128)(2,1)S(1)}, bf16[16,5120]{1,0:T(8,128)(2,1)S(1)}, u32[]{:S(2)}, u32[]{:S(2)}) collective-permute-start(bf16[16,5120]{1,0:T(8,128)(2,1)S(1)} %get-tuple-element.72), channel_id=1, source_target_pairs={{0,12},{1,13},{2,14},{3,15},{4,0},{5,1},{6,2},{7,3},{8,4},{9,5},{1... | collective-permute-start | bytes 491528 | tf_op jit(solution)/shard_map/ppermute | solution.py:24
  63.8 11.9 %collective-permute-start.22 = (bf16[176,512]{1,0:T(8,128)(2,1)S(1)}, bf16[176,512]{1,0:T(8,128)(2,1)S(1)}, u32[]{:S(2)}, u32[]{:S(2)}) collective-permute-start(bf16[176,512]{1,0:T(8,128)(2,1)S(1)} %get-tuple-element.69), channel_id=1, source_target_pairs={{0,18},{1,19},{2,16},{3,17},{4,22},{5,23},{6,20},{7,21},{8,26},{9,... | collective-permute-start | bytes 540680 | tf_op jit(solution)/shard_map/ppermute | solution.py:24
  66.1 9.5 %collective-permute-start.23 = (bf16[176,512]{1,0:T(8,128)(2,1)S(1)}, bf16[176,512]{1,0:T(8,128)(2,1)S(1)}, u32[]{:S(2)}, u32[]{:S(2)}) collective-permute-start(bf16[176,512]{1,0:T(8,128)(2,1)S(1)} %get-tuple-element.70), channel_id=1, source_target_pairs={{0,2},{1,3},{2,0},{3,1},{4,6},{5,7},{6,4},{7,5},{8,10},{9,11},{10,... | collective-permute-start | bytes 540680 | tf_op jit(solution)/shard_map/ppermute | solution.py:24
  67.6 8.0 %collective-permute-start.14 = (bf16[176,512]{1,0:T(8,128)(2,1)S(1)}, bf16[176,512]{1,0:T(8,128)(2,1)S(1)}, u32[]{:S(2)}, u32[]{:S(2)}) collective-permute-start(bf16[176,512]{1,0:T(8,128)(2,1)S(1)} %get-tuple-element.81), channel_id=1, source_target_pairs={{0,16},{1,17},{2,18},{3,19},{4,20},{5,21},{6,22},{7,23},{8,24},{9,... | collective-permute-start | bytes 540680 | tf_op jit(solution)/shard_map/ppermute | solution.py:24
  73.4 1.3 %collective-permute-start.27 = (bf16[16,2560]{1,0:T(8,128)(2,1)S(1)}, bf16[16,2560]{1,0:T(8,128)(2,1)S(1)}, u32[]{:S(2)}, u32[]{:S(2)}) collective-permute-start(bf16[16,2560]{1,0:T(8,128)(2,1)S(1)} %get-tuple-element.77.refs_0_), channel_id=1, source_target_pairs={{0,1},{1,0},{2,3},{3,2},{4,5},{5,4},{6,7},{7,6},{8,9},{9,8},{10,11... | collective-permute-start | bytes 245768 | tf_op jit(solution)/shard_map/ppermute | solution.py:24
  73.5 1.4 %collective-permute-start.28 = (bf16[16,2560]{1,0:T(8,128)(2,1)S(1)}, bf16[16,2560]{1,0:T(8,128)(2,1)S(1)}, u32[]{:S(2)}, u32[]{:S(2)}) collective-permute-start(bf16[16,2560]{1,0:T(8,128)(2,1)S(1)} %get-tuple-element.78.refs_1_), channel_id=1, source_target_pairs={{0,1},{1,0},{2,3},{3,2},{4,5},{5,4},{6,7},{7,6},{8,9},{9,8},{10,11... | collective-permute-start | bytes 245768 | tf_op jit(solution)/shard_map/ppermute | solution.py:24
  (5 other events, 19.8 us)

commit v16 on v14

--- a/solution.py
+++ b/solution.py
@@ -191,18 +191,31 @@
         ref[...] = block_ref[j * rows : (j + 1) * rows]
 
 
-def place_kernel(sizes, batches, *refs):
+def column_of(sizes, k, dg):
     groups, holders, shard, half = sizes
     group, here = lax.axis_index("groups"), lax.axis_index("adapter")
-    out_ref = refs[-1]
-    for i, batch in enumerate(batches):
-        for dg in range(groups):
-            source = lax.rem(group + groups - dg, groups)
-            for j, k in enumerate(batch):
-                at = lax.rem(here + holders - k, holders) * shard + source * half
-                out_ref[:, pl.ds(pl.multiple_of(at, half), half)] = refs[i * groups + dg][
-                    :, j * half : (j + 1) * half
-                ]
+    source = lax.rem(group + groups - dg, groups)
+    at = lax.rem(here + holders - k, holders) * shard + source * half
+    return pl.ds(pl.multiple_of(at, half), half)
+
+
+def place_kernel(sizes, places, *refs):
+    half = sizes[-1]
+    for ref, (batch, dg) in zip(refs, places):
+        for j, k in enumerate(batch):
+            refs[-1][:, column_of(sizes, k, dg)] = ref[:, j * half : (j + 1) * half]
+
+
+def late_kernel(sizes, places, *refs):
+    out_ref, sems = refs[-2:]
+    copies = [
+        pltpu.make_async_copy(ref, out_ref.at[:, column_of(sizes, batch[0], dg)], sems.at[i])
+        for i, (ref, (batch, dg)) in enumerate(zip(refs, places))
+    ]
+    for copy in copies:
+        copy.start()
+    for copy in copies:
+        copy.wait()
 
 
 def chip_kernel(replicas, *refs):
@@ -382,27 +395,53 @@
         if i == 1 and len(batches) > 2:
             got = moved(out[0], lambda g, z, s, r: (g, z, s - 1, r))
             got = [got[dg * tokens : (dg + 1) * tokens] for dg in range(groups)]
-            crossed.append(got[:1])
-            for dg in range(1, groups):
-                crossed[0].append(moved(got[dg], lambda g, z, s, r: (g + dg, z, s, r)))
-            arrived.append(crossed[0])
+            early = [(batches[0], dg) for dg in range(groups)] + [(batch, 0)]
+            passed = call(
+                functools.partial(place_kernel, (groups, holders, shard, half), early),
+                [jax.ShapeDtypeStruct((tokens, width), BF16)],
+                [*arrived[0], got[0]],
+            )[0]
+            got, passed = lax.optimization_barrier((got, passed))
+            late = [
+                ((batch, dg), moved(got[dg], lambda g, z, s, r: (g + dg, z, s, r)))
+                for dg in range(1, groups)
+            ]
+            arrived.append([])
             continue
         if i > 2:
             mails = [after(mail, *arrived[-1]) for mail in mails]
         arrived.append(
             [moved(mails[dg], lambda g, z, s, r: (g + dg, z, s - 1, r)) for dg in range(groups)]
         )
+        if i > 1:
+            late += [((batch, dg), arrived[-1][dg]) for dg in reversed(range(groups))]
         if i == 0:
             part, chip = adapter_sums(sel, *arrived[0])
-    passed = call(
-        functools.partial(place_kernel, (groups, holders, shard, half), batches),
-        [jax.ShapeDtypeStruct((tokens, width), BF16)],
-        [x for got in arrived for x in got],
-    )[0]
+    sizes = (groups, holders, shard, half)
+    if len(batches) > 2:
+        passed = pl.pallas_call(
+            functools.partial(late_kernel, sizes, [place for place, _ in late]),
+            out_shape=jax.ShapeDtypeStruct((tokens, width), BF16),
+            in_specs=[pl.BlockSpec(memory_space=pltpu.VMEM)] * len(late)
+            + [pl.BlockSpec(memory_space=pl.ANY)],
+            out_specs=pl.BlockSpec(memory_space=pl.ANY),
+            input_output_aliases={len(late): 0},
+            scratch_shapes=[pltpu.SemaphoreType.DMA((len(late),))],
+            compiler_params=pltpu.CompilerParams(vmem_limit_bytes=8 * MIB),
+            cost_estimate=pl.CostEstimate(flops=1000, bytes_accessed=1000, transcendentals=0),
+        )(*[part for _, part in late], passed)
+    else:
+        passed = call(
+            functools.partial(
+                place_kernel, sizes, [(batch, dg) for batch in batches for dg in range(groups)]
+            ),
+            [jax.ShapeDtypeStruct((tokens, width), BF16)],
+            [x for got in arrived for x in got],
+        )[0]
 
     sums = [chip[0]] + [
         moved(after(chip[k], ring[-1]), lambda g, z, s, r: (g, z - k, s, r))
-        for k in range(1, holders)
+        for k in [*range(1, holders, 2), *range(2, holders, 2)]
     ]
     total = call(total_kernel, [jax.ShapeDtypeStruct((rows, cols // 2), BF16)] * 2, sums)
     totals = list(total)

time: 78.6 us -> 80.8 us (1.028)
  waiting for transfers between devices: 33.4 us -> 34.4 us
    ppermute x29, waiting for transfers between devices: 33.4 us -> 34.4 us  [moved(): return lax.ppermute(x, AXES, pairs)]
    pallas_call x0 -> x1, Pallas kernels: none -> 0.81 us  [on_device(): pl.pallas_call(functools.partial(late_kernel, sizes, [place for place, _...]
  transfers between devices with their start and end apart: 29 -> 29, of which waited for: 13 -> 12; matrix products, arithmetic and copies ran while one was open for 0% -> 0% of each run, Pallas kernels for 10% -> 11%
where the time goes in v16:
time: 80.8 us; the launch traced here: 80.5 us
  waiting for transfers between devices  34.4 us (43%)
  starting transfers between devices  30.2 us (37%)
  Pallas kernels  9.72 us (12%)
  local copies, waits for them, and re-layouts  5.37 us (7%)
    ppermute x29, waiting for transfers between devices, moved(): return lax.ppermute(x, AXES, pairs)  34.4 us
    ppermute x29, starting transfers between devices, moved(): return lax.ppermute(x, AXES, pairs)  30.2 us
    pallas_call x13, Pallas kernels, call(): pl.pallas_call(kernel, out_shape=out_shape, in_specs=[pl.BlockSpec(memory...  8.91 us
    unnamed x14, local copies, waits for them, and re-layouts  4.12 us
  transfers between devices with their start and end apart: 29, of which 12 were waited for; matrix products, arithmetic and copies ran while one was open for 0% of the time, Pallas kernels for 11%

profile of v16, /device:TPU:0, one launch (start us, length us, event | category | flops | bytes accessed | tf_op | source)
XLA Modules:
  0.0 80.5 jit_solution(6577152611579011218)
XLA Ops:
  0.6 1.2 %dynamic-slice_bitcast_fusion = bf16[256,1024]{1,0:T(8,128)(2,1)S(1)} fusion(bf16[1,1024,1024]{2,1,0:T(8,128)(2,1)} %param.11, s32[]{:T(128)S(6)} %select_n.3), kind=kLoop, calls=%fused_computation | loop fusion | bytes 1048580 | tf_op jit(solution)/shard_map/dynamic_slice | solution.py:303
  1.9 3.1 %collective-permute-start.4 = (bf16[256,1024]{1,0:T(8,128)(2,1)S(1)}, bf16[256,1024]{1,0:T(8,128)(2,1)S(1)}, u32[]{:S(2)}, u32[]{:S(2)}) collective-permute-start(bf16[256,1024]{1,0:T(8,128)(2,1)S(1)} %dynamic-slice_bitcast_fusion), channel_id=1, source_target_pairs={{0,4},{1,5},{2,6},{3,7},{4,8},{5,9},{6,10},{7,11},{8,12},{9,13},{1... | collective-permute-start | bytes 1572872 | tf_op jit(solution)/shard_map/ppermute | solution.py:24
  5.0 1.0 %copy-done.2 = bf16[1,176,1024]{2,1,0:T(8,128)(2,1)S(1)} copy-done((bf16[1,176,1024]{2,1,0:T(8,128)(2,1)S(1)}, bf16[1,176,1024]{2,1,0:T(8,128)(2,1)}, u32[]{:S(2)}) %copy-start.2) | copy-done | bytes 360472
  8.0 1.6 %collective-permute-start.3 = (bf16[176,1152]{1,0:T(8,128)(2,1)S(1)}, bf16[176,1152]{1,0:T(8,128)(2,1)S(1)}, u32[]{:S(2)}, u32[]{:S(2)}) collective-permute-start(bf16[176,1152]{1,0:T(8,128)(2,1)S(1)} %shard_map.95.refs_0_.refs_1_), channel_id=1, source_target_pairs={{0,16},{1,17},{2,18},{3,19},{4,20},{5,21},{6,22},{7,23},{8,24},{9,... | collective-permute-start | bytes 1216520 | tf_op jit(solution)/shard_map/ppermute | solution.py:24
  9.6 0.9 %copy-done.3 = bf16[1,2,16,4096]{3,2,1,0:T(8,128)(2,1)S(1)} copy-done((bf16[1,2,16,4096]{3,2,1,0:T(8,128)(2,1)S(1)}, bf16[1,2,16,4096]{3,2,1,0:T(8,128)(2,1)}, u32[]{:S(2)}) %copy-start.3) | copy-done | bytes 262168
  10.6 0.8 %copy-done.4 = bf16[1,2,16,1024]{3,2,1,0:T(8,128)(2,1)S(1)} copy-done((bf16[1,2,16,1024]{3,2,1,0:T(8,128)(2,1)S(1)}, bf16[1,2,16,1024]{3,2,1,0:T(8,128)(2,1)}, u32[]{:S(2)}) %copy-start.4) | copy-done | bytes 65560
  11.4 1.6 %collective-permute-start = (bf16[16,3072]{1,0:T(8,128)(2,1)S(1)}, bf16[16,3072]{1,0:T(8,128)(2,1)S(1)}, u32[]{:S(2)}, u32[]{:S(2)}) collective-permute-start(bf16[16,3072]{1,0:T(8,128)(2,1)S(1)} %shard_map.94.refs_0_), channel_id=1, source_target_pairs={{0,4},{1,5},{2,6},{3,7},{4,8},{5,9},{6,10},{7,11},{8,12},{9,13},{1... | collective-permute-start | bytes 294920 | tf_op jit(solution)/shard_map/ppermute | solution.py:24
  13.1 1.2 %collective-permute-start.1 = (bf16[16,3072]{1,0:T(8,128)(2,1)S(1)}, bf16[16,3072]{1,0:T(8,128)(2,1)S(1)}, u32[]{:S(2)}, u32[]{:S(2)}) collective-permute-start(bf16[16,3072]{1,0:T(8,128)(2,1)S(1)} %shard_map.94.refs_0_), channel_id=1, source_target_pairs={{0,8},{1,9},{2,10},{3,11},{4,12},{5,13},{6,14},{7,15},{8,0},{9,1},... | collective-permute-start | bytes 294920 | tf_op jit(solution)/shard_map/ppermute | solution.py:24
  14.3 2.7 %collective-permute-start.2 = (bf16[16,3072]{1,0:T(8,128)(2,1)S(1)}, bf16[16,3072]{1,0:T(8,128)(2,1)S(1)}, u32[]{:S(2)}, u32[]{:S(2)}) collective-permute-start(bf16[16,3072]{1,0:T(8,128)(2,1)S(1)} %shard_map.94.refs_0_), channel_id=1, source_target_pairs={{0,12},{1,13},{2,14},{3,15},{4,0},{5,1},{6,2},{7,3},{8,4},{9,5},{1... | collective-permute-start | bytes 294920 | tf_op jit(solution)/shard_map/ppermute | solution.py:24
  17.0 5.0 %collective-permute-done.refs_1_ = bf16[16,3072]{1,0:T(8,128)(2,1)S(1)} collective-permute-done((bf16[16,3072]{1,0:T(8,128)(2,1)S(1)}, bf16[16,3072]{1,0:T(8,128)(2,1)S(1)}, u32[]{:S(2)}, u32[]{:S(2)}) %collective-permute-start) | collective-permute-done | bytes 98336 | tf_op jit(solution)/shard_map/ppermute | solution.py:24
  22.0 3.4 %collective-permute-done.1.refs_2_ = bf16[16,3072]{1,0:T(8,128)(2,1)S(1)} collective-permute-done((bf16[16,3072]{1,0:T(8,128)(2,1)S(1)}, bf16[16,3072]{1,0:T(8,128)(2,1)S(1)}, u32[]{:S(2)}, u32[]{:S(2)}) %collective-permute-start.1) | collective-permute-done | bytes 98336 | tf_op jit(solution)/shard_map/ppermute | solution.py:24
  25.4 2.6 %collective-permute-start.8 = (bf16[256,1024]{1,0:T(8,128)(2,1)S(1)}, bf16[256,1024]{1,0:T(8,128)(2,1)S(1)}, u32[]{:S(2)}, u32[]{:S(2)}) collective-permute-start(bf16[256,1024]{1,0:T(8,128)(2,1)S(1)} %collective-permute-done.4.refs_7_), channel_id=1, source_target_pairs={{0,4},{1,5},{2,6},{3,7},{4,8},{5,9},{6,10},{7,11},{8,12},{9,13},{1... | collective-permute-start | bytes 1572872 | tf_op jit(solution)/shard_map/ppermute | solution.py:24
  28.3 1.5 %collective-permute-start.16 = (bf16[64,2048]{1,0:T(8,128)(2,1)S(1)}, bf16[64,2048]{1,0:T(8,128)(2,1)S(1)}, u32[]{:S(2)}, u32[]{:S(2)}) collective-permute-start(bf16[64,2048]{1,0:T(8,128)(2,1)S(1)} %get-tuple-element.50.refs_2_.refs_3_), channel_id=1, source_target_pairs={{0,16},{1,17},{2,18},{3,19},{4,20},{5,21},{6,22},{7,23},{8,24},{9,... | collective-permute-start | bytes 786440 | tf_op jit(solution)/shard_map/ppermute | solution.py:24
  29.8 1.3 %collective-permute-done.6.refs_5_ = bf16[64,1024]{1,0:T(8,128)(2,1)S(1)} collective-permute-done((bf16[64,1024]{1,0:T(8,128)(2,1)S(1)}, bf16[64,1024]{1,0:T(8,128)(2,1)S(1)}, u32[]{:S(2)}, u32[]{:S(2)}) %collective-permute-start.6) | collective-permute-done | bytes 131104 | tf_op jit(solution)/shard_map/ppermute | solution.py:24
  31.2 2.2 %shard_map.97 = (bf16[176,1024]{1,0:T(8,128)(2,1)S(1)}, bf16[176,1024]{1,0:T(8,128)(2,1)S(1)}, bf16[352,128]{1,0:T(8,128)(2,1)S(1)}) custom-call(bf16[176,1152]{1,0:T(8,128)(2,1)S(1)} %shard_map.95.refs_0_.refs_1_, bf16[176,1152]{1,0:T(8,128)(2,1)S(1)} %collective-permute-done.3.refs_1_, bf16[64,2048]{1,0:T(8,128)(2,1)S(1)} %get-tuple-element.50.refs_2_.refs_3_, ...), custom_call_target="tpu_custom_call" | custom-call | flops 1000 | bytes 1000 | tf_op jit(solution)/shard_map/pallas_call | solution.py:41
  33.4 1.5 %collective-permute-start.10 = (bf16[176,1024]{1,0:T(8,128)(2,1)S(1)}, bf16[176,1024]{1,0:T(8,128)(2,1)S(1)}, u32[]{:S(2)}, u32[]{:S(2)}) collective-permute-start(bf16[176,1024]{1,0:T(8,128)(2,1)S(1)} %get-tuple-element.56), channel_id=1, source_target_pairs={{0,18},{1,19},{2,16},{3,17},{4,22},{5,23},{6,20},{7,21},{8,26},{9,... | collective-permute-start | bytes 1081352 | tf_op jit(solution)/shard_map/ppermute | solution.py:24
  35.4 7.9 %collective-permute-done.16.refs_5_ = bf16[64,2048]{1,0:T(8,128)(2,1)S(1)} collective-permute-done((bf16[64,2048]{1,0:T(8,128)(2,1)S(1)}, bf16[64,2048]{1,0:T(8,128)(2,1)S(1)}, u32[]{:S(2)}, u32[]{:S(2)}) %collective-permute-start.16) | collective-permute-done | bytes 262176 | tf_op jit(solution)/shard_map/ppermute | solution.py:24
  43.4 2.3 %collective-permute-done.10.refs_1_ = bf16[176,1024]{1,0:T(8,128)(2,1)S(1)} collective-permute-done((bf16[176,1024]{1,0:T(8,128)(2,1)S(1)}, bf16[176,1024]{1,0:T(8,128)(2,1)S(1)}, u32[]{:S(2)}, u32[]{:S(2)}) %collective-permute-start.10) | collective-permute-done | bytes 360480 | tf_op jit(solution)/shard_map/ppermute | solution.py:24
  45.6 6.0 %collective-permute-done.9.refs_0_ = bf16[176,1024]{1,0:T(8,128)(2,1)S(1)} collective-permute-done((bf16[176,1024]{1,0:T(8,128)(2,1)S(1)}, bf16[176,1024]{1,0:T(8,128)(2,1)S(1)}, u32[]{:S(2)}, u32[]{:S(2)}) %collective-permute-start.9) | collective-permute-done | bytes 360480 | tf_op jit(solution)/shard_map/ppermute | solution.py:24
  52.2 1.3 %shard_map.102 = (f32[64,5120]{1,0:T(8,128)S(1)}, bf16[64,2560]{1,0:T(8,128)(2,1)S(1)}, bf16[64,2560]{1,0:T(8,128)(2,1)S(1)}) custom-call(bf16[176,4096]{1,0:T(8,128)(2,1)S(1)} %bitcast.12, bf16[176,1152]{1,0:T(8,128)(2,1)S(1)} %shard_map.95.refs_0_.refs_1_, bf16[352,128]{1,0:T(8,128)(2,1)S(1)} %get-tuple-element.53.refs_4_.refs_2_, ...), custom_call_target="tpu_custom_call" | custom-call | flops 1000 | bytes 1000 | tf_op jit(solution)/shard_map/pallas_call | solution.py:41
  54.0 1.2 %shard_map.99 = bf16[352,512]{1,0:T(8,128)(2,1)S(1)} custom-call(bf16[176,1152]{1,0:T(8,128)(2,1)S(1)} %shard_map.95.refs_0_.refs_1_, bf16[176,1152]{1,0:T(8,128)(2,1)S(1)} %collective-permute-done.3.refs_1_, bf16[64,2048]{1,0:T(8,128)(2,1)S(1)} %get-tuple-element.50.refs_2_.refs_3_, bf16[64,2048]{1,0:T(8,128)(2,1)S(1)} %collective-permute-done.5.refs_3_.refs_4_, ...), custom_call_target="tpu_custom_call" | custom-call | flops 1000 | bytes 1000 | tf_op jit(solution)/shard_map/pallas_call | solution.py:41
  55.2 1.6 %collective-permute-start.13 = (bf16[352,512]{1,0:T(8,128)(2,1)S(1)}, bf16[352,512]{1,0:T(8,128)(2,1)S(1)}, u32[]{:S(2)}, u32[]{:S(2)}) collective-permute-start(bf16[352,512]{1,0:T(8,128)(2,1)S(1)} %shard_map.99), channel_id=1, source_target_pairs={{0,2},{1,3},{2,0},{3,1},{4,6},{5,7},{6,4},{7,5},{8,10},{9,11},{10,... | collective-permute-start | bytes 1081352 | tf_op jit(solution)/shard_map/ppermute | solution.py:24
  56.8 2.7 %collective-permute-done.15.block_ref.refs_5_ = bf16[256,1024]{1,0:T(8,128)(2,1)S(1)} collective-permute-done((bf16[256,1024]{1,0:T(8,128)(2,1)S(1)}, bf16[256,1024]{1,0:T(8,128)(2,1)S(1)}, u32[]{:S(2)}, u32[]{:S(2)}) %collective-permute-start.15) | collective-permute-done | bytes 524320 | tf_op jit(solution)/shard_map/ppermute | solution.py:24
  60.4 0.9 %collective-permute-done.21.refs_7_ = bf16[128,1024]{1,0:T(8,128)(2,1)S(1)} collective-permute-done((bf16[128,1024]{1,0:T(8,128)(2,1)S(1)}, bf16[128,1024]{1,0:T(8,128)(2,1)S(1)}, u32[]{:S(2)}, u32[]{:S(2)}) %collective-permute-start.21) | collective-permute-done | bytes 262176 | tf_op jit(solution)/shard_map/ppermute | solution.py:24
  61.3 2.8 %collective-permute-start.24 = (bf16[16,5120]{1,0:T(8,128)(2,1)S(1)}, bf16[16,5120]{1,0:T(8,128)(2,1)S(1)}, u32[]{:S(2)}, u32[]{:S(2)}) collective-permute-start(bf16[16,5120]{1,0:T(8,128)(2,1)S(1)} %get-tuple-element.76), channel_id=1, source_target_pairs={{0,12},{1,13},{2,14},{3,15},{4,0},{5,1},{6,2},{7,3},{8,4},{9,5},{1... | collective-permute-start | bytes 491528 | tf_op jit(solution)/shard_map/ppermute | solution.py:24
  64.1 1.2 %shard_map.104 = (bf16[176,512]{1,0:T(8,128)(2,1)S(1)}, bf16[176,512]{1,0:T(8,128)(2,1)S(1)}) custom-call(bf16[176,1152]{1,0:T(8,128)(2,1)S(1)} %shard_map.95.refs_0_.refs_1_, bf16[176,1152]{1,0:T(8,128)(2,1)S(1)} %collective-permute-done.3.refs_1_, bf16[64,2048]{1,0:T(8,128)(2,1)S(1)} %get-tuple-element.50.refs_2_.refs_3_, ...), custom_call_target="tpu_custom_call" | custom-call | flops 1000 | bytes 1000 | tf_op jit(solution)/shard_map/pallas_call | solution.py:41
  65.3 3.6 %collective-permute-start.22 = (bf16[176,512]{1,0:T(8,128)(2,1)S(1)}, bf16[176,512]{1,0:T(8,128)(2,1)S(1)}, u32[]{:S(2)}, u32[]{:S(2)}) collective-permute-start(bf16[176,512]{1,0:T(8,128)(2,1)S(1)} %get-tuple-element.72), channel_id=1, source_target_pairs={{0,18},{1,19},{2,16},{3,17},{4,22},{5,23},{6,20},{7,21},{8,26},{9,... | collective-permute-start | bytes 540680 | tf_op jit(solution)/shard_map/ppermute | solution.py:24
  69.5 1.2 %shard_map.100.refs_3_ = bf16[176,4096]{1,0:T(8,128)(2,1)} custom-call(bf16[176,1024]{1,0:T(8,128)(2,1)S(1)} %collective-permute-done.9.refs_0_, bf16[176,1024]{1,0:T(8,128)(2,1)S(1)} %collective-permute-done.10.refs_1_, bf16[176,512]{1,0:T(8,128)(2,1)S(1)} %get-tuple-element.86.refs_2_), custom_call_target="tpu_custom_call" | custom-call | flops 1000 | bytes 1000 | tf_op jit(solution)/shard_map/pallas_call | solution.py:41
  70.6 1.8 %collective-permute-done.26.refs_3_ = bf16[16,5120]{1,0:T(8,128)(2,1)S(1)} collective-permute-done((bf16[16,5120]{1,0:T(8,128)(2,1)S(1)}, bf16[16,5120]{1,0:T(8,128)(2,1)S(1)}, u32[]{:S(2)}, u32[]{:S(2)}) %collective-permute-start.26) | collective-permute-done | bytes 163872 | tf_op jit(solution)/shard_map/ppermute | solution.py:24
  72.4 2.6 %collective-permute-start.14 = (bf16[176,512]{1,0:T(8,128)(2,1)S(1)}, bf16[176,512]{1,0:T(8,128)(2,1)S(1)}, u32[]{:S(2)}, u32[]{:S(2)}) collective-permute-start(bf16[176,512]{1,0:T(8,128)(2,1)S(1)} %get-tuple-element.60), channel_id=1, source_target_pairs={{0,16},{1,17},{2,18},{3,19},{4,20},{5,21},{6,22},{7,23},{8,24},{9,... | collective-permute-start | bytes 540680 | tf_op jit(solution)/shard_map/ppermute | solution.py:24
  77.4 2.3 %collective-permute-done.14.refs_0_ = bf16[176,512]{1,0:T(8,128)(2,1)S(1)} collective-permute-done((bf16[176,512]{1,0:T(8,128)(2,1)S(1)}, bf16[176,512]{1,0:T(8,128)(2,1)S(1)}, u32[]{:S(2)}, u32[]{:S(2)}) %collective-permute-start.14) | collective-permute-done | bytes 180256 | tf_op jit(solution)/shard_map/ppermute | solution.py:24
  79.7 0.8 %shard_map.105 = bf16[176,4096]{1,0:T(8,128)(2,1)} custom-call(bf16[176,512]{1,0:T(8,128)(2,1)S(1)} %collective-permute-done.14.refs_0_, bf16[176,512]{1,0:T(8,128)(2,1)S(1)} %collective-permute-done.22.refs_1_, bf16[176,512]{1,0:T(8,128)(2,1)S(1)} %collective-permute-done.23.refs_2_, ...), custom_call_target="tpu_custom_call", output_to_operand_aliasing={{}: (3, {})} | custom-call | flops 1000 | bytes 1000 | tf_op jit(solution)/shard_map/pallas_call | solution.py:422
  (56 shorter events, 8.0 us)
Async XLA Ops:
  0.6 30.5 %copy-start = (bf16[1,1024,1024]{2,1,0:T(8,128)(2,1)S(1)}, bf16[1,1024,1024]{2,1,0:T(8,128)(2,1)}, u32[]{:S(2)}) copy-start(bf16[1,1024,1024]{2,1,0:T(8,128)(2,1)} %param.11) | copy-start | bytes 6291460
  1.9 23.5 %collective-permute-start.4 = (bf16[256,1024]{1,0:T(8,128)(2,1)S(1)}, bf16[256,1024]{1,0:T(8,128)(2,1)S(1)}, u32[]{:S(2)}, u32[]{:S(2)}) collective-permute-start(bf16[256,1024]{1,0:T(8,128)(2,1)S(1)} %dynamic-slice_bitcast_fusion), channel_id=1, source_target_pairs={{0,4},{1,5},{2,6},{3,7},{4,8},{5,9},{6,10},{7,11},{8,12},{9,13},{1... | collective-permute-start | bytes 1572872 | tf_op jit(solution)/shard_map/ppermute | solution.py:24
  5.0 1.0 %copy-start.2 = (bf16[1,176,1024]{2,1,0:T(8,128)(2,1)S(1)}, bf16[1,176,1024]{2,1,0:T(8,128)(2,1)}, u32[]{:S(2)}) copy-start(bf16[1,176,1024]{2,1,0:T(8,128)(2,1)} %param.8) | copy-start | bytes 1081348
  8.0 17.3 %collective-permute-start.3 = (bf16[176,1152]{1,0:T(8,128)(2,1)S(1)}, bf16[176,1152]{1,0:T(8,128)(2,1)S(1)}, u32[]{:S(2)}, u32[]{:S(2)}) collective-permute-start(bf16[176,1152]{1,0:T(8,128)(2,1)S(1)} %shard_map.95.refs_0_.refs_1_), channel_id=1, source_target_pairs={{0,16},{1,17},{2,18},{3,19},{4,20},{5,21},{6,22},{7,23},{8,24},{9,... | collective-permute-start | bytes 1216520 | tf_op jit(solution)/shard_map/ppermute | solution.py:24
  11.4 10.5 %collective-permute-start = (bf16[16,3072]{1,0:T(8,128)(2,1)S(1)}, bf16[16,3072]{1,0:T(8,128)(2,1)S(1)}, u32[]{:S(2)}, u32[]{:S(2)}) collective-permute-start(bf16[16,3072]{1,0:T(8,128)(2,1)S(1)} %shard_map.94.refs_0_), channel_id=1, source_target_pairs={{0,4},{1,5},{2,6},{3,7},{4,8},{5,9},{6,10},{7,11},{8,12},{9,13},{1... | collective-permute-start | bytes 294920 | tf_op jit(solution)/shard_map/ppermute | solution.py:24
  13.1 12.3 %collective-permute-start.1 = (bf16[16,3072]{1,0:T(8,128)(2,1)S(1)}, bf16[16,3072]{1,0:T(8,128)(2,1)S(1)}, u32[]{:S(2)}, u32[]{:S(2)}) collective-permute-start(bf16[16,3072]{1,0:T(8,128)(2,1)S(1)} %shard_map.94.refs_0_), channel_id=1, source_target_pairs={{0,8},{1,9},{2,10},{3,11},{4,12},{5,13},{6,14},{7,15},{8,0},{9,1},... | collective-permute-start | bytes 294920 | tf_op jit(solution)/shard_map/ppermute | solution.py:24
  14.3 11.1 %collective-permute-start.2 = (bf16[16,3072]{1,0:T(8,128)(2,1)S(1)}, bf16[16,3072]{1,0:T(8,128)(2,1)S(1)}, u32[]{:S(2)}, u32[]{:S(2)}) collective-permute-start(bf16[16,3072]{1,0:T(8,128)(2,1)S(1)} %shard_map.94.refs_0_), channel_id=1, source_target_pairs={{0,12},{1,13},{2,14},{3,15},{4,0},{5,1},{6,2},{7,3},{8,4},{9,5},{1... | collective-permute-start | bytes 294920 | tf_op jit(solution)/shard_map/ppermute | solution.py:24
  25.4 5.8 %collective-permute-start.7 = (bf16[256,1024]{1,0:T(8,128)(2,1)S(1)}, bf16[256,1024]{1,0:T(8,128)(2,1)S(1)}, u32[]{:S(2)}, u32[]{:S(2)}) collective-permute-start(bf16[256,1024]{1,0:T(8,128)(2,1)S(1)} %collective-permute-done.4.refs_7_), channel_id=1, source_target_pairs={{0,1},{1,0},{2,3},{3,2},{4,5},{5,4},{6,7},{7,6},{8,9},{9,8},{10,11... | collective-permute-start | bytes 1572872 | tf_op jit(solution)/shard_map/ppermute | solution.py:24
  25.4 17.9 %collective-permute-start.8 = (bf16[256,1024]{1,0:T(8,128)(2,1)S(1)}, bf16[256,1024]{1,0:T(8,128)(2,1)S(1)}, u32[]{:S(2)}, u32[]{:S(2)}) collective-permute-start(bf16[256,1024]{1,0:T(8,128)(2,1)S(1)} %collective-permute-done.4.refs_7_), channel_id=1, source_target_pairs={{0,4},{1,5},{2,6},{3,7},{4,8},{5,9},{6,10},{7,11},{8,12},{9,13},{1... | collective-permute-start | bytes 1572872 | tf_op jit(solution)/shard_map/ppermute | solution.py:24
  28.0 3.1 %collective-permute-start.5 = (bf16[64,2048]{1,0:T(8,128)(2,1)S(1)}, bf16[64,2048]{1,0:T(8,128)(2,1)S(1)}, u32[]{:S(2)}, u32[]{:S(2)}) collective-permute-start(bf16[64,2048]{1,0:T(8,128)(2,1)S(1)} %get-tuple-element.50.refs_2_.refs_3_), channel_id=1, source_target_pairs={{0,1},{1,0},{2,3},{3,2},{4,5},{5,4},{6,7},{7,6},{8,9},{9,8},{10,11... | collective-permute-start | bytes 786440 | tf_op jit(solution)/shard_map/ppermute | solution.py:24
  28.3 15.0 %collective-permute-start.16 = (bf16[64,2048]{1,0:T(8,128)(2,1)S(1)}, bf16[64,2048]{1,0:T(8,128)(2,1)S(1)}, u32[]{:S(2)}, u32[]{:S(2)}) collective-permute-start(bf16[64,2048]{1,0:T(8,128)(2,1)S(1)} %get-tuple-element.50.refs_2_.refs_3_), channel_id=1, source_target_pairs={{0,16},{1,17},{2,18},{3,19},{4,20},{5,21},{6,22},{7,23},{8,24},{9,... | collective-permute-start | bytes 786440 | tf_op jit(solution)/shard_map/ppermute | solution.py:24
  29.8 1.3 %collective-permute-start.6 = (bf16[64,1024]{1,0:T(8,128)(2,1)S(1)}, bf16[64,1024]{1,0:T(8,128)(2,1)S(1)}, u32[]{:S(2)}, u32[]{:S(2)}) collective-permute-start(bf16[64,1024]{1,0:T(8,128)(2,1)S(1)} %get-tuple-element.51.refs_4_), channel_id=1, source_target_pairs={{0,1},{1,0},{2,3},{3,2},{4,5},{5,4},{6,7},{7,6},{8,9},{9,8},{10,11... | collective-permute-start | bytes 393224 | tf_op jit(solution)/shard_map/ppermute | solution.py:24
  31.1 21.0 %copy-start.1 = (bf16[1,176,4096]{2,1,0:T(8,128)(2,1)S(1)}, bf16[1,176,4096]{2,1,0:T(8,128)(2,1)}, u32[]{:S(2)}) copy-start(bf16[1,176,4096]{2,1,0:T(8,128)(2,1)} %param.7) | copy-start | bytes 4325380
  33.4 12.2 %collective-permute-start.10 = (bf16[176,1024]{1,0:T(8,128)(2,1)S(1)}, bf16[176,1024]{1,0:T(8,128)(2,1)S(1)}, u32[]{:S(2)}, u32[]{:S(2)}) collective-permute-start(bf16[176,1024]{1,0:T(8,128)(2,1)S(1)} %get-tuple-element.56), channel_id=1, source_target_pairs={{0,18},{1,19},{2,16},{3,17},{4,22},{5,23},{6,20},{7,21},{8,26},{9,... | collective-permute-start | bytes 1081352 | tf_op jit(solution)/shard_map/ppermute | solution.py:24
  34.9 16.7 %collective-permute-start.9 = (bf16[176,1024]{1,0:T(8,128)(2,1)S(1)}, bf16[176,1024]{1,0:T(8,128)(2,1)S(1)}, u32[]{:S(2)}, u32[]{:S(2)}) collective-permute-start(bf16[176,1024]{1,0:T(8,128)(2,1)S(1)} %get-tuple-element.55), channel_id=1, source_target_pairs={{0,2},{1,3},{2,0},{3,1},{4,6},{5,7},{6,4},{7,5},{8,10},{9,11},{10,... | collective-permute-start | bytes 1081352 | tf_op jit(solution)/shard_map/ppermute | solution.py:24
  43.3 8.9 %collective-permute-start.17 = (bf16[64,2048]{1,0:T(8,128)(2,1)S(1)}, bf16[64,2048]{1,0:T(8,128)(2,1)S(1)}, u32[]{:S(2)}, u32[]{:S(2)}) collective-permute-start(bf16[64,2048]{1,0:T(8,128)(2,1)S(1)} %collective-permute-done.16.refs_5_), channel_id=1, source_target_pairs={{0,1},{1,0},{2,3},{3,2},{4,5},{5,4},{6,7},{7,6},{8,9},{9,8},{10,11... | collective-permute-start | bytes 786440 | tf_op jit(solution)/shard_map/ppermute | solution.py:24
  43.3 16.1 %collective-permute-start.15 = (bf16[256,1024]{1,0:T(8,128)(2,1)S(1)}, bf16[256,1024]{1,0:T(8,128)(2,1)S(1)}, u32[]{:S(2)}, u32[]{:S(2)}) collective-permute-start(bf16[256,1024]{1,0:T(8,128)(2,1)S(1)} %collective-permute-done.8.block_ref.refs_5_), channel_id=1, source_target_pairs={{0,4},{1,5},{2,6},{3,7},{4,8},{5,9},{6,10},{7,11},{8,12},{9,13},{1... | collective-permute-start | bytes 1572872 | tf_op jit(solution)/shard_map/ppermute | solution.py:24
  51.7 2.4 %collective-permute-start.12 = (bf16[128,1024]{1,0:T(8,128)(2,1)S(1)}, bf16[128,1024]{1,0:T(8,128)(2,1)S(1)}, u32[]{:S(2)}, u32[]{:S(2)}) collective-permute-start(bf16[128,1024]{1,0:T(8,128)(2,1)S(1)} %get-tuple-element.59), channel_id=1, source_target_pairs={{0,1},{1,0},{2,3},{3,2},{4,5},{5,4},{6,7},{7,6},{8,9},{9,8},{10,11... | collective-permute-start | bytes 786440 | tf_op jit(solution)/shard_map/ppermute | solution.py:24
  51.7 2.4 %collective-permute-start.11 = (bf16[128,1024]{1,0:T(8,128)(2,1)S(1)}, bf16[128,1024]{1,0:T(8,128)(2,1)S(1)}, u32[]{:S(2)}, u32[]{:S(2)}) collective-permute-start(bf16[128,1024]{1,0:T(8,128)(2,1)S(1)} %get-tuple-element.57), channel_id=1, source_target_pairs={{0,1},{1,0},{2,3},{3,2},{4,5},{5,4},{6,7},{7,6},{8,9},{9,8},{10,11... | collective-permute-start | bytes 786440 | tf_op jit(solution)/shard_map/ppermute | solution.py:24
  53.5 6.0 %collective-permute-start.19 = (bf16[64,2560]{1,0:T(8,128)(2,1)S(1)}, bf16[64,2560]{1,0:T(8,128)(2,1)S(1)}, u32[]{:S(2)}, u32[]{:S(2)}) collective-permute-start(bf16[64,2560]{1,0:T(8,128)(2,1)S(1)} %get-tuple-element.67), channel_id=1, source_target_pairs={{0,1},{1,0},{2,3},{3,2},{4,5},{5,4},{6,7},{7,6},{8,9},{9,8},{10,11... | collective-permute-start | bytes 983048 | tf_op jit(solution)/shard_map/ppermute | solution.py:24
  53.5 6.0 %collective-permute-start.18 = (bf16[64,2560]{1,0:T(8,128)(2,1)S(1)}, bf16[64,2560]{1,0:T(8,128)(2,1)S(1)}, u32[]{:S(2)}, u32[]{:S(2)}) collective-permute-start(bf16[64,2560]{1,0:T(8,128)(2,1)S(1)} %get-tuple-element.65), channel_id=1, source_target_pairs={{0,1},{1,0},{2,3},{3,2},{4,5},{5,4},{6,7},{7,6},{8,9},{9,8},{10,11... | collective-permute-start | bytes 983048 | tf_op jit(solution)/shard_map/ppermute | solution.py:24
  55.2 13.7 %collective-permute-start.13 = (bf16[352,512]{1,0:T(8,128)(2,1)S(1)}, bf16[352,512]{1,0:T(8,128)(2,1)S(1)}, u32[]{:S(2)}, u32[]{:S(2)}) collective-permute-start(bf16[352,512]{1,0:T(8,128)(2,1)S(1)} %shard_map.99), channel_id=1, source_target_pairs={{0,2},{1,3},{2,0},{3,1},{4,6},{5,7},{6,4},{7,5},{8,10},{9,11},{10,... | collective-permute-start | bytes 1081352 | tf_op jit(solution)/shard_map/ppermute | solution.py:24
  59.7 1.6 %collective-permute-start.21 = (bf16[128,1024]{1,0:T(8,128)(2,1)S(1)}, bf16[128,1024]{1,0:T(8,128)(2,1)S(1)}, u32[]{:S(2)}, u32[]{:S(2)}) collective-permute-start(bf16[128,1024]{1,0:T(8,128)(2,1)S(1)} %get-tuple-element.71), channel_id=1, source_target_pairs={{0,1},{1,0},{2,3},{3,2},{4,5},{5,4},{6,7},{7,6},{8,9},{9,8},{10,11... | collective-permute-start | bytes 786440 | tf_op jit(solution)/shard_map/ppermute | solution.py:24
  59.8 4.3 %collective-permute-start.20 = (bf16[128,1024]{1,0:T(8,128)(2,1)S(1)}, bf16[128,1024]{1,0:T(8,128)(2,1)S(1)}, u32[]{:S(2)}, u32[]{:S(2)}) collective-permute-start(bf16[128,1024]{1,0:T(8,128)(2,1)S(1)} %get-tuple-element.69), channel_id=1, source_target_pairs={{0,1},{1,0},{2,3},{3,2},{4,5},{5,4},{6,7},{7,6},{8,9},{9,8},{10,11... | collective-permute-start | bytes 786440 | tf_op jit(solution)/shard_map/ppermute | solution.py:24
  60.3 12.2 %collective-permute-start.26 = (bf16[16,5120]{1,0:T(8,128)(2,1)S(1)}, bf16[16,5120]{1,0:T(8,128)(2,1)S(1)}, u32[]{:S(2)}, u32[]{:S(2)}) collective-permute-start(bf16[16,5120]{1,0:T(8,128)(2,1)S(1)} %get-tuple-element.80), channel_id=1, source_target_pairs={{0,8},{1,9},{2,10},{3,11},{4,12},{5,13},{6,14},{7,15},{8,0},{9,1},... | collective-permute-start | bytes 491528 | tf_op jit(solution)/shard_map/ppermute | solution.py:24
  60.3 14.8 %collective-permute-start.25 = (bf16[16,5120]{1,0:T(8,128)(2,1)S(1)}, bf16[16,5120]{1,0:T(8,128)(2,1)S(1)}, u32[]{:S(2)}, u32[]{:S(2)}) collective-permute-start(bf16[16,5120]{1,0:T(8,128)(2,1)S(1)} %get-tuple-element.78), channel_id=1, source_target_pairs={{0,4},{1,5},{2,6},{3,7},{4,8},{5,9},{6,10},{7,11},{8,12},{9,13},{1... | collective-permute-start | bytes 491528 | tf_op jit(solution)/shard_map/ppermute | solution.py:24
  61.3 13.8 %collective-permute-start.24 = (bf16[16,5120]{1,0:T(8,128)(2,1)S(1)}, bf16[16,5120]{1,0:T(8,128)(2,1)S(1)}, u32[]{:S(2)}, u32[]{:S(2)}) collective-permute-start(bf16[16,5120]{1,0:T(8,128)(2,1)S(1)} %get-tuple-element.76), channel_id=1, source_target_pairs={{0,12},{1,13},{2,14},{3,15},{4,0},{5,1},{6,2},{7,3},{8,4},{9,5},{1... | collective-permute-start | bytes 491528 | tf_op jit(solution)/shard_map/ppermute | solution.py:24
  65.3 12.1 %collective-permute-start.22 = (bf16[176,512]{1,0:T(8,128)(2,1)S(1)}, bf16[176,512]{1,0:T(8,128)(2,1)S(1)}, u32[]{:S(2)}, u32[]{:S(2)}) collective-permute-start(bf16[176,512]{1,0:T(8,128)(2,1)S(1)} %get-tuple-element.72), channel_id=1, source_target_pairs={{0,18},{1,19},{2,16},{3,17},{4,22},{5,23},{6,20},{7,21},{8,26},{9,... | collective-permute-start | bytes 540680 | tf_op jit(solution)/shard_map/ppermute | solution.py:24
  68.9 8.5 %collective-permute-start.23 = (bf16[176,512]{1,0:T(8,128)(2,1)S(1)}, bf16[176,512]{1,0:T(8,128)(2,1)S(1)}, u32[]{:S(2)}, u32[]{:S(2)}) collective-permute-start(bf16[176,512]{1,0:T(8,128)(2,1)S(1)} %get-tuple-element.73), channel_id=1, source_target_pairs={{0,2},{1,3},{2,0},{3,1},{4,6},{5,7},{6,4},{7,5},{8,10},{9,11},{10,... | collective-permute-start | bytes 540680 | tf_op jit(solution)/shard_map/ppermute | solution.py:24
  72.4 7.3 %collective-permute-start.14 = (bf16[176,512]{1,0:T(8,128)(2,1)S(1)}, bf16[176,512]{1,0:T(8,128)(2,1)S(1)}, u32[]{:S(2)}, u32[]{:S(2)}) collective-permute-start(bf16[176,512]{1,0:T(8,128)(2,1)S(1)} %get-tuple-element.60), channel_id=1, source_target_pairs={{0,16},{1,17},{2,18},{3,19},{4,20},{5,21},{6,22},{7,23},{8,24},{9,... | collective-permute-start | bytes 540680 | tf_op jit(solution)/shard_map/ppermute | solution.py:24
  75.1 1.3 %collective-permute-start.27 = (bf16[16,2560]{1,0:T(8,128)(2,1)S(1)}, bf16[16,2560]{1,0:T(8,128)(2,1)S(1)}, u32[]{:S(2)}, u32[]{:S(2)}) collective-permute-start(bf16[16,2560]{1,0:T(8,128)(2,1)S(1)} %get-tuple-element.81.refs_0_), channel_id=1, source_target_pairs={{0,1},{1,0},{2,3},{3,2},{4,5},{5,4},{6,7},{7,6},{8,9},{9,8},{10,11... | collective-permute-start | bytes 245768 | tf_op jit(solution)/shard_map/ppermute | solution.py:24
  75.2 1.4 %collective-permute-start.28 = (bf16[16,2560]{1,0:T(8,128)(2,1)S(1)}, bf16[16,2560]{1,0:T(8,128)(2,1)S(1)}, u32[]{:S(2)}, u32[]{:S(2)}) collective-permute-start(bf16[16,2560]{1,0:T(8,128)(2,1)S(1)} %get-tuple-element.82.refs_1_), channel_id=1, source_target_pairs={{0,1},{1,0},{2,3},{3,2},{4,5},{5,4},{6,7},{7,6},{8,9},{9,8},{10,11... | collective-permute-start | bytes 245768 | tf_op jit(solution)/shard_map/ppermute | solution.py:24
  (4 other events, 3.1 us)

commit v17 on v16

--- a/solution.py
+++ b/solution.py
@@ -373,7 +373,7 @@
             if k > 1:
                 last = after(ring[-1], sel) if k > 2 else ring[-1]
                 ring.append(moved(last, lambda g, z, s, r: (g, z + 1, s, r)))
-            gate = arrived[0] if k == 2 else [*arrived[i - 2], chip[0]] if k > 2 else []
+            gate = arrived[0][::-1] if k == 2 else [*arrived[i - 2], chip[0]] if k > 2 else []
             spec, blocks = pieces_of(k, *gate)
             specs.append((k, spec))
             operands += blocks
@@ -416,7 +416,7 @@
         if i > 1:
             late += [((batch, dg), arrived[-1][dg]) for dg in reversed(range(groups))]
         if i == 0:
-            part, chip = adapter_sums(sel, *arrived[0])
+            part, chip = adapter_sums(sel, *arrived[0][::-1])
     sizes = (groups, holders, shard, half)
     if len(batches) > 2:
         passed = pl.pallas_call(
@@ -441,7 +441,7 @@
 
     sums = [chip[0]] + [
         moved(after(chip[k], ring[-1]), lambda g, z, s, r: (g, z - k, s, r))
-        for k in [*range(1, holders, 2), *range(2, holders, 2)]
+        for k in range(1, holders)
     ]
     total = call(total_kernel, [jax.ShapeDtypeStruct((rows, cols // 2), BF16)] * 2, sums)
     totals = list(total)

time: 80.8 us -> 77 us (0.953)
  waiting for transfers between devices: 34.4 us -> 29 us
  starting transfers between devices: 30.2 us -> 31.2 us
    ppermute x29, waiting for transfers between devices: 34.4 us -> 29 us  [moved(): return lax.ppermute(x, AXES, pairs)]
    ppermute x29, starting transfers between devices: 30.2 us -> 31.2 us  [moved(): return lax.ppermute(x, AXES, pairs)]
  transfers between devices with their start and end apart: 29 -> 29, of which waited for: 12 -> 12; matrix products, arithmetic and copies ran while one was open for 0% -> 0% of each run, Pallas kernels for 11% -> 12%
where the time goes in v17:
time: 77 us; the launch traced here: 76 us
  starting transfers between devices  31.2 us (41%)
  waiting for transfers between devices  29 us (38%)
  Pallas kernels  9.74 us (13%)
  local copies, waits for them, and re-layouts  5.37 us (7%)
  between operations  0.8 us (1%)
    ppermute x29, starting transfers between devices, moved(): return lax.ppermute(x, AXES, pairs)  31.2 us
    ppermute x29, waiting for transfers between devices, moved(): return lax.ppermute(x, AXES, pairs)  29 us
    pallas_call x13, Pallas kernels, call(): pl.pallas_call(kernel, out_shape=out_shape, in_specs=[pl.BlockSpec(memory...  8.91 us
    unnamed x14, local copies, waits for them, and re-layouts  4.12 us
  transfers between devices with their start and end apart: 29, of which 12 were waited for; matrix products, arithmetic and copies ran while one was open for 0% of the time, Pallas kernels for 12%

profile of v17, /device:TPU:0, one launch (start us, length us, event | category | flops | bytes accessed | tf_op | source)
XLA Modules:
  0.0 76.0 jit_solution(17969604068489660307)
XLA Ops:
  0.6 1.2 %dynamic-slice_bitcast_fusion = bf16[256,1024]{1,0:T(8,128)(2,1)S(1)} fusion(bf16[1,1024,1024]{2,1,0:T(8,128)(2,1)} %param.11, s32[]{:T(128)S(6)} %select_n.3), kind=kLoop, calls=%fused_computation | loop fusion | bytes 1048580 | tf_op jit(solution)/shard_map/dynamic_slice | solution.py:303
  1.9 3.1 %collective-permute-start.4 = (bf16[256,1024]{1,0:T(8,128)(2,1)S(1)}, bf16[256,1024]{1,0:T(8,128)(2,1)S(1)}, u32[]{:S(2)}, u32[]{:S(2)}) collective-permute-start(bf16[256,1024]{1,0:T(8,128)(2,1)S(1)} %dynamic-slice_bitcast_fusion), channel_id=1, source_target_pairs={{0,4},{1,5},{2,6},{3,7},{4,8},{5,9},{6,10},{7,11},{8,12},{9,13},{1... | collective-permute-start | bytes 1572872 | tf_op jit(solution)/shard_map/ppermute | solution.py:24
  5.0 1.0 %copy-done.2 = bf16[1,176,1024]{2,1,0:T(8,128)(2,1)S(1)} copy-done((bf16[1,176,1024]{2,1,0:T(8,128)(2,1)S(1)}, bf16[1,176,1024]{2,1,0:T(8,128)(2,1)}, u32[]{:S(2)}) %copy-start.2) | copy-done | bytes 360472
  8.0 1.6 %collective-permute-start.3 = (bf16[176,1152]{1,0:T(8,128)(2,1)S(1)}, bf16[176,1152]{1,0:T(8,128)(2,1)S(1)}, u32[]{:S(2)}, u32[]{:S(2)}) collective-permute-start(bf16[176,1152]{1,0:T(8,128)(2,1)S(1)} %shard_map.95.refs_0_.refs_1_), channel_id=1, source_target_pairs={{0,16},{1,17},{2,18},{3,19},{4,20},{5,21},{6,22},{7,23},{8,24},{9,... | collective-permute-start | bytes 1216520 | tf_op jit(solution)/shard_map/ppermute | solution.py:24
  9.6 0.9 %copy-done.3 = bf16[1,2,16,4096]{3,2,1,0:T(8,128)(2,1)S(1)} copy-done((bf16[1,2,16,4096]{3,2,1,0:T(8,128)(2,1)S(1)}, bf16[1,2,16,4096]{3,2,1,0:T(8,128)(2,1)}, u32[]{:S(2)}) %copy-start.3) | copy-done | bytes 262168
  10.6 0.8 %copy-done.4 = bf16[1,2,16,1024]{3,2,1,0:T(8,128)(2,1)S(1)} copy-done((bf16[1,2,16,1024]{3,2,1,0:T(8,128)(2,1)S(1)}, bf16[1,2,16,1024]{3,2,1,0:T(8,128)(2,1)}, u32[]{:S(2)}) %copy-start.4) | copy-done | bytes 65560
  11.4 1.6 %collective-permute-start = (bf16[16,3072]{1,0:T(8,128)(2,1)S(1)}, bf16[16,3072]{1,0:T(8,128)(2,1)S(1)}, u32[]{:S(2)}, u32[]{:S(2)}) collective-permute-start(bf16[16,3072]{1,0:T(8,128)(2,1)S(1)} %shard_map.94.refs_0_), channel_id=1, source_target_pairs={{0,4},{1,5},{2,6},{3,7},{4,8},{5,9},{6,10},{7,11},{8,12},{9,13},{1... | collective-permute-start | bytes 294920 | tf_op jit(solution)/shard_map/ppermute | solution.py:24
  13.1 1.2 %collective-permute-start.1 = (bf16[16,3072]{1,0:T(8,128)(2,1)S(1)}, bf16[16,3072]{1,0:T(8,128)(2,1)S(1)}, u32[]{:S(2)}, u32[]{:S(2)}) collective-permute-start(bf16[16,3072]{1,0:T(8,128)(2,1)S(1)} %shard_map.94.refs_0_), channel_id=1, source_target_pairs={{0,8},{1,9},{2,10},{3,11},{4,12},{5,13},{6,14},{7,15},{8,0},{9,1},... | collective-permute-start | bytes 294920 | tf_op jit(solution)/shard_map/ppermute | solution.py:24
  14.3 2.7 %collective-permute-start.2 = (bf16[16,3072]{1,0:T(8,128)(2,1)S(1)}, bf16[16,3072]{1,0:T(8,128)(2,1)S(1)}, u32[]{:S(2)}, u32[]{:S(2)}) collective-permute-start(bf16[16,3072]{1,0:T(8,128)(2,1)S(1)} %shard_map.94.refs_0_), channel_id=1, source_target_pairs={{0,12},{1,13},{2,14},{3,15},{4,0},{5,1},{6,2},{7,3},{8,4},{9,5},{1... | collective-permute-start | bytes 294920 | tf_op jit(solution)/shard_map/ppermute | solution.py:24
  17.0 5.0 %collective-permute-done.refs_1_ = bf16[16,3072]{1,0:T(8,128)(2,1)S(1)} collective-permute-done((bf16[16,3072]{1,0:T(8,128)(2,1)S(1)}, bf16[16,3072]{1,0:T(8,128)(2,1)S(1)}, u32[]{:S(2)}, u32[]{:S(2)}) %collective-permute-start) | collective-permute-done | bytes 98336 | tf_op jit(solution)/shard_map/ppermute | solution.py:24
  22.0 3.4 %collective-permute-done.1.refs_2_ = bf16[16,3072]{1,0:T(8,128)(2,1)S(1)} collective-permute-done((bf16[16,3072]{1,0:T(8,128)(2,1)S(1)}, bf16[16,3072]{1,0:T(8,128)(2,1)S(1)}, u32[]{:S(2)}, u32[]{:S(2)}) %collective-permute-start.1) | collective-permute-done | bytes 98336 | tf_op jit(solution)/shard_map/ppermute | solution.py:24
  25.4 2.6 %collective-permute-start.8 = (bf16[256,1024]{1,0:T(8,128)(2,1)S(1)}, bf16[256,1024]{1,0:T(8,128)(2,1)S(1)}, u32[]{:S(2)}, u32[]{:S(2)}) collective-permute-start(bf16[256,1024]{1,0:T(8,128)(2,1)S(1)} %collective-permute-done.4.refs_7_), channel_id=1, source_target_pairs={{0,4},{1,5},{2,6},{3,7},{4,8},{5,9},{6,10},{7,11},{8,12},{9,13},{1... | collective-permute-start | bytes 1572872 | tf_op jit(solution)/shard_map/ppermute | solution.py:24
  28.3 1.5 %collective-permute-start.16 = (bf16[64,2048]{1,0:T(8,128)(2,1)S(1)}, bf16[64,2048]{1,0:T(8,128)(2,1)S(1)}, u32[]{:S(2)}, u32[]{:S(2)}) collective-permute-start(bf16[64,2048]{1,0:T(8,128)(2,1)S(1)} %get-tuple-element.50.refs_2_.refs_3_), channel_id=1, source_target_pairs={{0,16},{1,17},{2,18},{3,19},{4,20},{5,21},{6,22},{7,23},{8,24},{9,... | collective-permute-start | bytes 786440 | tf_op jit(solution)/shard_map/ppermute | solution.py:24
  29.8 1.3 %collective-permute-done.6.refs_5_ = bf16[64,1024]{1,0:T(8,128)(2,1)S(1)} collective-permute-done((bf16[64,1024]{1,0:T(8,128)(2,1)S(1)}, bf16[64,1024]{1,0:T(8,128)(2,1)S(1)}, u32[]{:S(2)}, u32[]{:S(2)}) %collective-permute-start.6) | collective-permute-done | bytes 131104 | tf_op jit(solution)/shard_map/ppermute | solution.py:24
  31.2 2.2 %shard_map.97 = (bf16[176,1024]{1,0:T(8,128)(2,1)S(1)}, bf16[176,1024]{1,0:T(8,128)(2,1)S(1)}, bf16[352,128]{1,0:T(8,128)(2,1)S(1)}) custom-call(bf16[176,1152]{1,0:T(8,128)(2,1)S(1)} %shard_map.95.refs_0_.refs_1_, bf16[176,1152]{1,0:T(8,128)(2,1)S(1)} %collective-permute-done.3.refs_1_, bf16[64,2048]{1,0:T(8,128)(2,1)S(1)} %get-tuple-element.50.refs_2_.refs_3_, ...), custom_call_target="tpu_custom_call" | custom-call | flops 1000 | bytes 1000 | tf_op jit(solution)/shard_map/pallas_call | solution.py:41
  33.4 1.6 %collective-permute-start.10 = (bf16[176,1024]{1,0:T(8,128)(2,1)S(1)}, bf16[176,1024]{1,0:T(8,128)(2,1)S(1)}, u32[]{:S(2)}, u32[]{:S(2)}) collective-permute-start(bf16[176,1024]{1,0:T(8,128)(2,1)S(1)} %get-tuple-element.56), channel_id=1, source_target_pairs={{0,2},{1,3},{2,0},{3,1},{4,6},{5,7},{6,4},{7,5},{8,10},{9,11},{10,... | collective-permute-start | bytes 1081352 | tf_op jit(solution)/shard_map/ppermute | solution.py:24
  35.4 1.4 %collective-permute-done.16.refs_5_ = bf16[64,2048]{1,0:T(8,128)(2,1)S(1)} collective-permute-done((bf16[64,2048]{1,0:T(8,128)(2,1)S(1)}, bf16[64,2048]{1,0:T(8,128)(2,1)S(1)}, u32[]{:S(2)}, u32[]{:S(2)}) %collective-permute-start.16) | collective-permute-done | bytes 262176 | tf_op jit(solution)/shard_map/ppermute | solution.py:24
  36.8 4.8 %collective-permute-done.8.block_ref.refs_5_ = bf16[256,1024]{1,0:T(8,128)(2,1)S(1)} collective-permute-done((bf16[256,1024]{1,0:T(8,128)(2,1)S(1)}, bf16[256,1024]{1,0:T(8,128)(2,1)S(1)}, u32[]{:S(2)}, u32[]{:S(2)}) %collective-permute-start.8) | collective-permute-done | bytes 524320 | tf_op jit(solution)/shard_map/ppermute | solution.py:24
  42.3 2.4 %collective-permute-done.10.refs_0_ = bf16[176,1024]{1,0:T(8,128)(2,1)S(1)} collective-permute-done((bf16[176,1024]{1,0:T(8,128)(2,1)S(1)}, bf16[176,1024]{1,0:T(8,128)(2,1)S(1)}, u32[]{:S(2)}, u32[]{:S(2)}) %collective-permute-start.10) | collective-permute-done | bytes 360480 | tf_op jit(solution)/shard_map/ppermute | solution.py:24
  44.7 6.9 %collective-permute-done.9.refs_1_ = bf16[176,1024]{1,0:T(8,128)(2,1)S(1)} collective-permute-done((bf16[176,1024]{1,0:T(8,128)(2,1)S(1)}, bf16[176,1024]{1,0:T(8,128)(2,1)S(1)}, u32[]{:S(2)}, u32[]{:S(2)}) %collective-permute-start.9) | collective-permute-done | bytes 360480 | tf_op jit(solution)/shard_map/ppermute | solution.py:24
  52.1 1.3 %shard_map.102 = (f32[64,5120]{1,0:T(8,128)S(1)}, bf16[64,2560]{1,0:T(8,128)(2,1)S(1)}, bf16[64,2560]{1,0:T(8,128)(2,1)S(1)}) custom-call(bf16[176,4096]{1,0:T(8,128)(2,1)S(1)} %bitcast.12, bf16[176,1152]{1,0:T(8,128)(2,1)S(1)} %shard_map.95.refs_0_.refs_1_, bf16[352,128]{1,0:T(8,128)(2,1)S(1)} %get-tuple-element.53.refs_4_.refs_2_, ...), custom_call_target="tpu_custom_call" | custom-call | flops 1000 | bytes 1000 | tf_op jit(solution)/shard_map/pallas_call | solution.py:41
  54.0 1.2 %shard_map.99 = bf16[352,512]{1,0:T(8,128)(2,1)S(1)} custom-call(bf16[176,1152]{1,0:T(8,128)(2,1)S(1)} %shard_map.95.refs_0_.refs_1_, bf16[176,1152]{1,0:T(8,128)(2,1)S(1)} %collective-permute-done.3.refs_1_, bf16[64,2048]{1,0:T(8,128)(2,1)S(1)} %get-tuple-element.50.refs_2_.refs_3_, bf16[64,2048]{1,0:T(8,128)(2,1)S(1)} %collective-permute-done.5.refs_3_.refs_4_, ...), custom_call_target="tpu_custom_call" | custom-call | flops 1000 | bytes 1000 | tf_op jit(solution)/shard_map/pallas_call | solution.py:41
  55.2 1.6 %collective-permute-start.13 = (bf16[352,512]{1,0:T(8,128)(2,1)S(1)}, bf16[352,512]{1,0:T(8,128)(2,1)S(1)}, u32[]{:S(2)}, u32[]{:S(2)}) collective-permute-start(bf16[352,512]{1,0:T(8,128)(2,1)S(1)} %shard_map.99), channel_id=1, source_target_pairs={{0,2},{1,3},{2,0},{3,1},{4,6},{5,7},{6,4},{7,5},{8,10},{9,11},{10,... | collective-permute-start | bytes 1081352 | tf_op jit(solution)/shard_map/ppermute | solution.py:24
  57.8 1.7 %collective-permute-start.25 = (bf16[16,5120]{1,0:T(8,128)(2,1)S(1)}, bf16[16,5120]{1,0:T(8,128)(2,1)S(1)}, u32[]{:S(2)}, u32[]{:S(2)}) collective-permute-start(bf16[16,5120]{1,0:T(8,128)(2,1)S(1)} %get-tuple-element.78), channel_id=1, source_target_pairs={{0,8},{1,9},{2,10},{3,11},{4,12},{5,13},{6,14},{7,15},{8,0},{9,1},... | collective-permute-start | bytes 491528 | tf_op jit(solution)/shard_map/ppermute | solution.py:24
  59.5 2.7 %collective-permute-start.24 = (bf16[16,5120]{1,0:T(8,128)(2,1)S(1)}, bf16[16,5120]{1,0:T(8,128)(2,1)S(1)}, u32[]{:S(2)}, u32[]{:S(2)}) collective-permute-start(bf16[16,5120]{1,0:T(8,128)(2,1)S(1)} %get-tuple-element.76), channel_id=1, source_target_pairs={{0,12},{1,13},{2,14},{3,15},{4,0},{5,1},{6,2},{7,3},{8,4},{9,5},{1... | collective-permute-start | bytes 491528 | tf_op jit(solution)/shard_map/ppermute | solution.py:24
  62.1 1.2 %shard_map.104 = (bf16[176,512]{1,0:T(8,128)(2,1)S(1)}, bf16[176,512]{1,0:T(8,128)(2,1)S(1)}) custom-call(bf16[176,1152]{1,0:T(8,128)(2,1)S(1)} %shard_map.95.refs_0_.refs_1_, bf16[176,1152]{1,0:T(8,128)(2,1)S(1)} %collective-permute-done.3.refs_1_, bf16[64,2048]{1,0:T(8,128)(2,1)S(1)} %get-tuple-element.50.refs_2_.refs_3_, ...), custom_call_target="tpu_custom_call" | custom-call | flops 1000 | bytes 1000 | tf_op jit(solution)/shard_map/pallas_call | solution.py:41
  63.3 2.0 %collective-permute-start.22 = (bf16[176,512]{1,0:T(8,128)(2,1)S(1)}, bf16[176,512]{1,0:T(8,128)(2,1)S(1)}, u32[]{:S(2)}, u32[]{:S(2)}) collective-permute-start(bf16[176,512]{1,0:T(8,128)(2,1)S(1)} %get-tuple-element.72), channel_id=1, source_target_pairs={{0,18},{1,19},{2,16},{3,17},{4,22},{5,23},{6,20},{7,21},{8,26},{9,... | collective-permute-start | bytes 540680 | tf_op jit(solution)/shard_map/ppermute | solution.py:24
  65.6 1.5 %collective-permute-start.23 = (bf16[176,512]{1,0:T(8,128)(2,1)S(1)}, bf16[176,512]{1,0:T(8,128)(2,1)S(1)}, u32[]{:S(2)}, u32[]{:S(2)}) collective-permute-start(bf16[176,512]{1,0:T(8,128)(2,1)S(1)} %get-tuple-element.73), channel_id=1, source_target_pairs={{0,2},{1,3},{2,0},{3,1},{4,6},{5,7},{6,4},{7,5},{8,10},{9,11},{10,... | collective-permute-start | bytes 540680 | tf_op jit(solution)/shard_map/ppermute | solution.py:24
  67.2 1.2 %shard_map.100.refs_3_ = bf16[176,4096]{1,0:T(8,128)(2,1)} custom-call(bf16[176,1024]{1,0:T(8,128)(2,1)S(1)} %collective-permute-done.10.refs_0_, bf16[176,1024]{1,0:T(8,128)(2,1)S(1)} %collective-permute-done.9.refs_1_, bf16[176,512]{1,0:T(8,128)(2,1)S(1)} %get-tuple-element.86.refs_2_), custom_call_target="tpu_custom_call" | custom-call | flops 1000 | bytes 1000 | tf_op jit(solution)/shard_map/pallas_call | solution.py:41
  68.3 2.2 %collective-permute-start.14 = (bf16[176,512]{1,0:T(8,128)(2,1)S(1)}, bf16[176,512]{1,0:T(8,128)(2,1)S(1)}, u32[]{:S(2)}, u32[]{:S(2)}) collective-permute-start(bf16[176,512]{1,0:T(8,128)(2,1)S(1)} %get-tuple-element.60), channel_id=1, source_target_pairs={{0,16},{1,17},{2,18},{3,19},{4,20},{5,21},{6,22},{7,23},{8,24},{9,... | collective-permute-start | bytes 540680 | tf_op jit(solution)/shard_map/ppermute | solution.py:24
  70.5 2.3 %collective-permute-done.25.refs_2_ = bf16[16,5120]{1,0:T(8,128)(2,1)S(1)} collective-permute-done((bf16[16,5120]{1,0:T(8,128)(2,1)S(1)}, bf16[16,5120]{1,0:T(8,128)(2,1)S(1)}, u32[]{:S(2)}, u32[]{:S(2)}) %collective-permute-start.25) | collective-permute-done | bytes 163872 | tf_op jit(solution)/shard_map/ppermute | solution.py:24
  75.2 0.8 %shard_map.105 = bf16[176,4096]{1,0:T(8,128)(2,1)} custom-call(bf16[176,512]{1,0:T(8,128)(2,1)S(1)} %collective-permute-done.14.refs_0_, bf16[176,512]{1,0:T(8,128)(2,1)S(1)} %collective-permute-done.22.refs_1_, bf16[176,512]{1,0:T(8,128)(2,1)S(1)} %collective-permute-done.23.refs_2_, ...), custom_call_target="tpu_custom_call", output_to_operand_aliasing={{}: (3, {})} | custom-call | flops 1000 | bytes 1000 | tf_op jit(solution)/shard_map/pallas_call | solution.py:422
  (56 shorter events, 8.5 us)
Async XLA Ops:
  0.6 30.5 %copy-start = (bf16[1,1024,1024]{2,1,0:T(8,128)(2,1)S(1)}, bf16[1,1024,1024]{2,1,0:T(8,128)(2,1)}, u32[]{:S(2)}) copy-start(bf16[1,1024,1024]{2,1,0:T(8,128)(2,1)} %param.11) | copy-start | bytes 6291460
  1.9 23.5 %collective-permute-start.4 = (bf16[256,1024]{1,0:T(8,128)(2,1)S(1)}, bf16[256,1024]{1,0:T(8,128)(2,1)S(1)}, u32[]{:S(2)}, u32[]{:S(2)}) collective-permute-start(bf16[256,1024]{1,0:T(8,128)(2,1)S(1)} %dynamic-slice_bitcast_fusion), channel_id=1, source_target_pairs={{0,4},{1,5},{2,6},{3,7},{4,8},{5,9},{6,10},{7,11},{8,12},{9,13},{1... | collective-permute-start | bytes 1572872 | tf_op jit(solution)/shard_map/ppermute | solution.py:24
  5.0 1.0 %copy-start.2 = (bf16[1,176,1024]{2,1,0:T(8,128)(2,1)S(1)}, bf16[1,176,1024]{2,1,0:T(8,128)(2,1)}, u32[]{:S(2)}) copy-start(bf16[1,176,1024]{2,1,0:T(8,128)(2,1)} %param.8) | copy-start | bytes 1081348
  8.0 17.3 %collective-permute-start.3 = (bf16[176,1152]{1,0:T(8,128)(2,1)S(1)}, bf16[176,1152]{1,0:T(8,128)(2,1)S(1)}, u32[]{:S(2)}, u32[]{:S(2)}) collective-permute-start(bf16[176,1152]{1,0:T(8,128)(2,1)S(1)} %shard_map.95.refs_0_.refs_1_), channel_id=1, source_target_pairs={{0,16},{1,17},{2,18},{3,19},{4,20},{5,21},{6,22},{7,23},{8,24},{9,... | collective-permute-start | bytes 1216520 | tf_op jit(solution)/shard_map/ppermute | solution.py:24
  11.4 10.5 %collective-permute-start = (bf16[16,3072]{1,0:T(8,128)(2,1)S(1)}, bf16[16,3072]{1,0:T(8,128)(2,1)S(1)}, u32[]{:S(2)}, u32[]{:S(2)}) collective-permute-start(bf16[16,3072]{1,0:T(8,128)(2,1)S(1)} %shard_map.94.refs_0_), channel_id=1, source_target_pairs={{0,4},{1,5},{2,6},{3,7},{4,8},{5,9},{6,10},{7,11},{8,12},{9,13},{1... | collective-permute-start | bytes 294920 | tf_op jit(solution)/shard_map/ppermute | solution.py:24
  13.1 12.3 %collective-permute-start.1 = (bf16[16,3072]{1,0:T(8,128)(2,1)S(1)}, bf16[16,3072]{1,0:T(8,128)(2,1)S(1)}, u32[]{:S(2)}, u32[]{:S(2)}) collective-permute-start(bf16[16,3072]{1,0:T(8,128)(2,1)S(1)} %shard_map.94.refs_0_), channel_id=1, source_target_pairs={{0,8},{1,9},{2,10},{3,11},{4,12},{5,13},{6,14},{7,15},{8,0},{9,1},... | collective-permute-start | bytes 294920 | tf_op jit(solution)/shard_map/ppermute | solution.py:24
  14.3 11.1 %collective-permute-start.2 = (bf16[16,3072]{1,0:T(8,128)(2,1)S(1)}, bf16[16,3072]{1,0:T(8,128)(2,1)S(1)}, u32[]{:S(2)}, u32[]{:S(2)}) collective-permute-start(bf16[16,3072]{1,0:T(8,128)(2,1)S(1)} %shard_map.94.refs_0_), channel_id=1, source_target_pairs={{0,12},{1,13},{2,14},{3,15},{4,0},{5,1},{6,2},{7,3},{8,4},{9,5},{1... | collective-permute-start | bytes 294920 | tf_op jit(solution)/shard_map/ppermute | solution.py:24
  25.4 5.8 %collective-permute-start.7 = (bf16[256,1024]{1,0:T(8,128)(2,1)S(1)}, bf16[256,1024]{1,0:T(8,128)(2,1)S(1)}, u32[]{:S(2)}, u32[]{:S(2)}) collective-permute-start(bf16[256,1024]{1,0:T(8,128)(2,1)S(1)} %collective-permute-done.4.refs_7_), channel_id=1, source_target_pairs={{0,1},{1,0},{2,3},{3,2},{4,5},{5,4},{6,7},{7,6},{8,9},{9,8},{10,11... | collective-permute-start | bytes 1572872 | tf_op jit(solution)/shard_map/ppermute | solution.py:24
  25.4 16.2 %collective-permute-start.8 = (bf16[256,1024]{1,0:T(8,128)(2,1)S(1)}, bf16[256,1024]{1,0:T(8,128)(2,1)S(1)}, u32[]{:S(2)}, u32[]{:S(2)}) collective-permute-start(bf16[256,1024]{1,0:T(8,128)(2,1)S(1)} %collective-permute-done.4.refs_7_), channel_id=1, source_target_pairs={{0,4},{1,5},{2,6},{3,7},{4,8},{5,9},{6,10},{7,11},{8,12},{9,13},{1... | collective-permute-start | bytes 1572872 | tf_op jit(solution)/shard_map/ppermute | solution.py:24
  28.0 3.1 %collective-permute-start.5 = (bf16[64,2048]{1,0:T(8,128)(2,1)S(1)}, bf16[64,2048]{1,0:T(8,128)(2,1)S(1)}, u32[]{:S(2)}, u32[]{:S(2)}) collective-permute-start(bf16[64,2048]{1,0:T(8,128)(2,1)S(1)} %get-tuple-element.50.refs_2_.refs_3_), channel_id=1, source_target_pairs={{0,1},{1,0},{2,3},{3,2},{4,5},{5,4},{6,7},{7,6},{8,9},{9,8},{10,11... | collective-permute-start | bytes 786440 | tf_op jit(solution)/shard_map/ppermute | solution.py:24
  28.3 8.6 %collective-permute-start.16 = (bf16[64,2048]{1,0:T(8,128)(2,1)S(1)}, bf16[64,2048]{1,0:T(8,128)(2,1)S(1)}, u32[]{:S(2)}, u32[]{:S(2)}) collective-permute-start(bf16[64,2048]{1,0:T(8,128)(2,1)S(1)} %get-tuple-element.50.refs_2_.refs_3_), channel_id=1, source_target_pairs={{0,16},{1,17},{2,18},{3,19},{4,20},{5,21},{6,22},{7,23},{8,24},{9,... | collective-permute-start | bytes 786440 | tf_op jit(solution)/shard_map/ppermute | solution.py:24
  29.8 1.3 %collective-permute-start.6 = (bf16[64,1024]{1,0:T(8,128)(2,1)S(1)}, bf16[64,1024]{1,0:T(8,128)(2,1)S(1)}, u32[]{:S(2)}, u32[]{:S(2)}) collective-permute-start(bf16[64,1024]{1,0:T(8,128)(2,1)S(1)} %get-tuple-element.51.refs_4_), channel_id=1, source_target_pairs={{0,1},{1,0},{2,3},{3,2},{4,5},{5,4},{6,7},{7,6},{8,9},{9,8},{10,11... | collective-permute-start | bytes 393224 | tf_op jit(solution)/shard_map/ppermute | solution.py:24
  31.1 21.0 %copy-start.1 = (bf16[1,176,4096]{2,1,0:T(8,128)(2,1)S(1)}, bf16[1,176,4096]{2,1,0:T(8,128)(2,1)}, u32[]{:S(2)}) copy-start(bf16[1,176,4096]{2,1,0:T(8,128)(2,1)} %param.7) | copy-start | bytes 4325380
  33.4 11.3 %collective-permute-start.10 = (bf16[176,1024]{1,0:T(8,128)(2,1)S(1)}, bf16[176,1024]{1,0:T(8,128)(2,1)S(1)}, u32[]{:S(2)}, u32[]{:S(2)}) collective-permute-start(bf16[176,1024]{1,0:T(8,128)(2,1)S(1)} %get-tuple-element.56), channel_id=1, source_target_pairs={{0,2},{1,3},{2,0},{3,1},{4,6},{5,7},{6,4},{7,5},{8,10},{9,11},{10,... | collective-permute-start | bytes 1081352 | tf_op jit(solution)/shard_map/ppermute | solution.py:24
  35.0 16.6 %collective-permute-start.9 = (bf16[176,1024]{1,0:T(8,128)(2,1)S(1)}, bf16[176,1024]{1,0:T(8,128)(2,1)S(1)}, u32[]{:S(2)}, u32[]{:S(2)}) collective-permute-start(bf16[176,1024]{1,0:T(8,128)(2,1)S(1)} %get-tuple-element.55), channel_id=1, source_target_pairs={{0,18},{1,19},{2,16},{3,17},{4,22},{5,23},{6,20},{7,21},{8,26},{9,... | collective-permute-start | bytes 1081352 | tf_op jit(solution)/shard_map/ppermute | solution.py:24
  36.8 15.3 %collective-permute-start.17 = (bf16[64,2048]{1,0:T(8,128)(2,1)S(1)}, bf16[64,2048]{1,0:T(8,128)(2,1)S(1)}, u32[]{:S(2)}, u32[]{:S(2)}) collective-permute-start(bf16[64,2048]{1,0:T(8,128)(2,1)S(1)} %collective-permute-done.16.refs_5_), channel_id=1, source_target_pairs={{0,1},{1,0},{2,3},{3,2},{4,5},{5,4},{6,7},{7,6},{8,9},{9,8},{10,11... | collective-permute-start | bytes 786440 | tf_op jit(solution)/shard_map/ppermute | solution.py:24
  41.6 15.3 %collective-permute-start.15 = (bf16[256,1024]{1,0:T(8,128)(2,1)S(1)}, bf16[256,1024]{1,0:T(8,128)(2,1)S(1)}, u32[]{:S(2)}, u32[]{:S(2)}) collective-permute-start(bf16[256,1024]{1,0:T(8,128)(2,1)S(1)} %collective-permute-done.8.block_ref.refs_5_), channel_id=1, source_target_pairs={{0,4},{1,5},{2,6},{3,7},{4,8},{5,9},{6,10},{7,11},{8,12},{9,13},{1... | collective-permute-start | bytes 1572872 | tf_op jit(solution)/shard_map/ppermute | solution.py:24
  51.6 2.4 %collective-permute-start.12 = (bf16[128,1024]{1,0:T(8,128)(2,1)S(1)}, bf16[128,1024]{1,0:T(8,128)(2,1)S(1)}, u32[]{:S(2)}, u32[]{:S(2)}) collective-permute-start(bf16[128,1024]{1,0:T(8,128)(2,1)S(1)} %get-tuple-element.59), channel_id=1, source_target_pairs={{0,1},{1,0},{2,3},{3,2},{4,5},{5,4},{6,7},{7,6},{8,9},{9,8},{10,11... | collective-permute-start | bytes 786440 | tf_op jit(solution)/shard_map/ppermute | solution.py:24
  51.6 2.4 %collective-permute-start.11 = (bf16[128,1024]{1,0:T(8,128)(2,1)S(1)}, bf16[128,1024]{1,0:T(8,128)(2,1)S(1)}, u32[]{:S(2)}, u32[]{:S(2)}) collective-permute-start(bf16[128,1024]{1,0:T(8,128)(2,1)S(1)} %get-tuple-element.57), channel_id=1, source_target_pairs={{0,1},{1,0},{2,3},{3,2},{4,5},{5,4},{6,7},{7,6},{8,9},{9,8},{10,11... | collective-permute-start | bytes 786440 | tf_op jit(solution)/shard_map/ppermute | solution.py:24
  53.4 3.6 %collective-permute-start.19 = (bf16[64,2560]{1,0:T(8,128)(2,1)S(1)}, bf16[64,2560]{1,0:T(8,128)(2,1)S(1)}, u32[]{:S(2)}, u32[]{:S(2)}) collective-permute-start(bf16[64,2560]{1,0:T(8,128)(2,1)S(1)} %get-tuple-element.67), channel_id=1, source_target_pairs={{0,1},{1,0},{2,3},{3,2},{4,5},{5,4},{6,7},{7,6},{8,9},{9,8},{10,11... | collective-permute-start | bytes 983048 | tf_op jit(solution)/shard_map/ppermute | solution.py:24
  53.5 3.5 %collective-permute-start.18 = (bf16[64,2560]{1,0:T(8,128)(2,1)S(1)}, bf16[64,2560]{1,0:T(8,128)(2,1)S(1)}, u32[]{:S(2)}, u32[]{:S(2)}) collective-permute-start(bf16[64,2560]{1,0:T(8,128)(2,1)S(1)} %get-tuple-element.65), channel_id=1, source_target_pairs={{0,1},{1,0},{2,3},{3,2},{4,5},{5,4},{6,7},{7,6},{8,9},{9,8},{10,11... | collective-permute-start | bytes 983048 | tf_op jit(solution)/shard_map/ppermute | solution.py:24
  55.2 10.5 %collective-permute-start.13 = (bf16[352,512]{1,0:T(8,128)(2,1)S(1)}, bf16[352,512]{1,0:T(8,128)(2,1)S(1)}, u32[]{:S(2)}, u32[]{:S(2)}) collective-permute-start(bf16[352,512]{1,0:T(8,128)(2,1)S(1)} %shard_map.99), channel_id=1, source_target_pairs={{0,2},{1,3},{2,0},{3,1},{4,6},{5,7},{6,4},{7,5},{8,10},{9,11},{10,... | collective-permute-start | bytes 1081352 | tf_op jit(solution)/shard_map/ppermute | solution.py:24
  57.2 2.3 %collective-permute-start.21 = (bf16[128,1024]{1,0:T(8,128)(2,1)S(1)}, bf16[128,1024]{1,0:T(8,128)(2,1)S(1)}, u32[]{:S(2)}, u32[]{:S(2)}) collective-permute-start(bf16[128,1024]{1,0:T(8,128)(2,1)S(1)} %get-tuple-element.71), channel_id=1, source_target_pairs={{0,1},{1,0},{2,3},{3,2},{4,5},{5,4},{6,7},{7,6},{8,9},{9,8},{10,11... | collective-permute-start | bytes 786440 | tf_op jit(solution)/shard_map/ppermute | solution.py:24
  57.3 4.8 %collective-permute-start.20 = (bf16[128,1024]{1,0:T(8,128)(2,1)S(1)}, bf16[128,1024]{1,0:T(8,128)(2,1)S(1)}, u32[]{:S(2)}, u32[]{:S(2)}) collective-permute-start(bf16[128,1024]{1,0:T(8,128)(2,1)S(1)} %get-tuple-element.69), channel_id=1, source_target_pairs={{0,1},{1,0},{2,3},{3,2},{4,5},{5,4},{6,7},{7,6},{8,9},{9,8},{10,11... | collective-permute-start | bytes 786440 | tf_op jit(solution)/shard_map/ppermute | solution.py:24
  57.8 10.6 %collective-permute-start.26 = (bf16[16,5120]{1,0:T(8,128)(2,1)S(1)}, bf16[16,5120]{1,0:T(8,128)(2,1)S(1)}, u32[]{:S(2)}, u32[]{:S(2)}) collective-permute-start(bf16[16,5120]{1,0:T(8,128)(2,1)S(1)} %get-tuple-element.80), channel_id=1, source_target_pairs={{0,4},{1,5},{2,6},{3,7},{4,8},{5,9},{6,10},{7,11},{8,12},{9,13},{1... | collective-permute-start | bytes 491528 | tf_op jit(solution)/shard_map/ppermute | solution.py:24
  57.8 15.0 %collective-permute-start.25 = (bf16[16,5120]{1,0:T(8,128)(2,1)S(1)}, bf16[16,5120]{1,0:T(8,128)(2,1)S(1)}, u32[]{:S(2)}, u32[]{:S(2)}) collective-permute-start(bf16[16,5120]{1,0:T(8,128)(2,1)S(1)} %get-tuple-element.78), channel_id=1, source_target_pairs={{0,8},{1,9},{2,10},{3,11},{4,12},{5,13},{6,14},{7,15},{8,0},{9,1},... | collective-permute-start | bytes 491528 | tf_op jit(solution)/shard_map/ppermute | solution.py:24
  59.5 13.4 %collective-permute-start.24 = (bf16[16,5120]{1,0:T(8,128)(2,1)S(1)}, bf16[16,5120]{1,0:T(8,128)(2,1)S(1)}, u32[]{:S(2)}, u32[]{:S(2)}) collective-permute-start(bf16[16,5120]{1,0:T(8,128)(2,1)S(1)} %get-tuple-element.76), channel_id=1, source_target_pairs={{0,12},{1,13},{2,14},{3,15},{4,0},{5,1},{6,2},{7,3},{8,4},{9,5},{1... | collective-permute-start | bytes 491528 | tf_op jit(solution)/shard_map/ppermute | solution.py:24
  63.3 11.9 %collective-permute-start.22 = (bf16[176,512]{1,0:T(8,128)(2,1)S(1)}, bf16[176,512]{1,0:T(8,128)(2,1)S(1)}, u32[]{:S(2)}, u32[]{:S(2)}) collective-permute-start(bf16[176,512]{1,0:T(8,128)(2,1)S(1)} %get-tuple-element.72), channel_id=1, source_target_pairs={{0,18},{1,19},{2,16},{3,17},{4,22},{5,23},{6,20},{7,21},{8,26},{9,... | collective-permute-start | bytes 540680 | tf_op jit(solution)/shard_map/ppermute | solution.py:24
  65.6 9.6 %collective-permute-start.23 = (bf16[176,512]{1,0:T(8,128)(2,1)S(1)}, bf16[176,512]{1,0:T(8,128)(2,1)S(1)}, u32[]{:S(2)}, u32[]{:S(2)}) collective-permute-start(bf16[176,512]{1,0:T(8,128)(2,1)S(1)} %get-tuple-element.73), channel_id=1, source_target_pairs={{0,2},{1,3},{2,0},{3,1},{4,6},{5,7},{6,4},{7,5},{8,10},{9,11},{10,... | collective-permute-start | bytes 540680 | tf_op jit(solution)/shard_map/ppermute | solution.py:24
  68.3 6.8 %collective-permute-start.14 = (bf16[176,512]{1,0:T(8,128)(2,1)S(1)}, bf16[176,512]{1,0:T(8,128)(2,1)S(1)}, u32[]{:S(2)}, u32[]{:S(2)}) collective-permute-start(bf16[176,512]{1,0:T(8,128)(2,1)S(1)} %get-tuple-element.60), channel_id=1, source_target_pairs={{0,16},{1,17},{2,18},{3,19},{4,20},{5,21},{6,22},{7,23},{8,24},{9,... | collective-permute-start | bytes 540680 | tf_op jit(solution)/shard_map/ppermute | solution.py:24
  72.9 1.3 %collective-permute-start.27 = (bf16[16,2560]{1,0:T(8,128)(2,1)S(1)}, bf16[16,2560]{1,0:T(8,128)(2,1)S(1)}, u32[]{:S(2)}, u32[]{:S(2)}) collective-permute-start(bf16[16,2560]{1,0:T(8,128)(2,1)S(1)} %get-tuple-element.81.refs_0_), channel_id=1, source_target_pairs={{0,1},{1,0},{2,3},{3,2},{4,5},{5,4},{6,7},{7,6},{8,9},{9,8},{10,11... | collective-permute-start | bytes 245768 | tf_op jit(solution)/shard_map/ppermute | solution.py:24
  73.0 1.4 %collective-permute-start.28 = (bf16[16,2560]{1,0:T(8,128)(2,1)S(1)}, bf16[16,2560]{1,0:T(8,128)(2,1)S(1)}, u32[]{:S(2)}, u32[]{:S(2)}) collective-permute-start(bf16[16,2560]{1,0:T(8,128)(2,1)S(1)} %get-tuple-element.82.refs_1_), channel_id=1, source_target_pairs={{0,1},{1,0},{2,3},{3,2},{4,5},{5,4},{6,7},{7,6},{8,9},{9,8},{10,11... | collective-permute-start | bytes 245768 | tf_op jit(solution)/shard_map/ppermute | solution.py:24
  (4 other events, 3.1 us)

commit v18 on v17

--- a/solution.py
+++ b/solution.py
@@ -13,6 +13,7 @@
 F32 = jnp.float32
 BF16 = jnp.bfloat16
 MIB = 1024 * 1024
+GRANT = 62 * MIB
 
 
 def moved(x, to):
@@ -84,6 +85,16 @@
         rows = ref.shape[0]
         down_ref[k * rows : (k + 1) * rows] = ref[:, :wide]
         up_ref[k * rows : (k + 1) * rows] = ref[:, wide:]
+
+
+def piece_kernel(replicas, frozen_ref, out_ref, sem):
+    rows = out_ref.shape[0]
+    at = (lax.axis_index("groups") * replicas + lax.axis_index("replica")) * rows
+    copy = pltpu.make_async_copy(
+        frozen_ref.at[pl.ds(pl.multiple_of(at, rows), rows)], out_ref, sem
+    )
+    copy.start()
+    copy.wait()
 
 
 def own_kernel(sizes, down_ref, up_ref, out_ref):
@@ -300,7 +311,17 @@
     for k in range(1, holders):
         held.append(moved(own, lambda g, z, s, r: (g, z + k, s, r)))
 
-    ring = [lax.dynamic_slice_in_dim(frozen, (group * replicas + core) * piece, piece, axis=0)]
+    ring = [
+        pl.pallas_call(
+            functools.partial(piece_kernel, replicas),
+            out_shape=jax.ShapeDtypeStruct((piece, value_width), BF16),
+            in_specs=[pl.BlockSpec(memory_space=pl.ANY)],
+            out_specs=pl.BlockSpec(memory_space=pltpu.VMEM),
+            scratch_shapes=[pltpu.SemaphoreType.DMA],
+            compiler_params=pltpu.CompilerParams(vmem_limit_bytes=GRANT),
+            cost_estimate=pl.CostEstimate(flops=1000, bytes_accessed=1000, transcendentals=0),
+        )(frozen)
+    ]
     ring.append(moved(ring[0], lambda g, z, s, r: (g, z + 1, s, r)))
     held, grads, ring = lax.optimization_barrier((held, grads, ring))
     joined = call(
@@ -447,6 +468,7 @@
     totals = list(total)
     for dr in range(1, replicas):
         totals += [moved(x, lambda g, z, s, r: (g, z, s, r + dr)) for x in total]
+    totals[0], passed = lax.optimization_barrier((totals[0], passed))
     down_grad, up_grad = call(
         functools.partial(spread_kernel, width, replicas),
         [

time: 77 us -> 79 us (1.026)
  waiting for transfers between devices: 29 us -> 33.6 us
  local copies, waits for them, and re-layouts: 5.37 us -> 1.64 us
  Pallas kernels: 9.74 us -> 11.6 us
    ppermute x29, waiting for transfers between devices: 29 us -> 33.6 us  [moved(): return lax.ppermute(x, AXES, pairs)]
    unnamed x14, local copies, waits for them, and re-layouts: 4.12 us -> 1.62 us
    pallas_call x0 -> x1, Pallas kernels: none -> 1.91 us  [on_device(): pl.pallas_call(functools.partial(piece_kernel, replicas), out_shape=jax.S...]
    dynamic_slice x1 -> x0, local copies, waits for them, and re-layouts: 1.23 us -> none  [on_device(): lax.dynamic_slice_in_dim(frozen, (group * replicas + core) * piece, piece...]
  transfers between devices with their start and end apart: 29 -> 29, of which waited for: 12 -> 10; matrix products, arithmetic and copies ran while one was open for 0% -> 0% of each run, Pallas kernels for 12% -> 11%
where the time goes in v18:
time: 79 us; the launch traced here: 78.8 us
  waiting for transfers between devices  33.6 us (43%)
  starting transfers between devices  31.1 us (39%)
  Pallas kernels  11.6 us (15%)
  local copies, waits for them, and re-layouts  1.64 us (2%)
  between operations  0.85 us (1%)
    ppermute x29, waiting for transfers between devices, moved(): return lax.ppermute(x, AXES, pairs)  33.6 us
    ppermute x29, starting transfers between devices, moved(): return lax.ppermute(x, AXES, pairs)  31.1 us
    pallas_call x13, Pallas kernels, call(): pl.pallas_call(kernel, out_shape=out_shape, in_specs=[pl.BlockSpec(memory...  8.86 us
    pallas_call x1, Pallas kernels, on_device(): pl.pallas_call(functools.partial(piece_kernel, replicas), out_shape=jax.S...  1.91 us
    unnamed x14, local copies, waits for them, and re-layouts  1.62 us
  transfers between devices with their start and end apart: 29, of which 10 were waited for; matrix products, arithmetic and copies ran while one was open for 0% of the time, Pallas kernels for 11%

profile of v18, /device:TPU:0, one launch (start us, length us, event | category | flops | bytes accessed | tf_op | source)
XLA Modules:
  0.0 78.8 jit_solution(8880928435467309748)
XLA Ops:
  0.7 1.9 %shard_map.96 = bf16[256,1024]{1,0:T(8,128)(2,1)} custom-call(bf16[1024,1024]{1,0:T(8,128)(2,1)} %bitcast.9), custom_call_target="tpu_custom_call" | custom-call | flops 1000 | bytes 1000 | tf_op jit(solution)/shard_map/pallas_call | solution.py:315
  2.6 3.1 %collective-permute-start.4 = (bf16[256,1024]{1,0:T(8,128)(2,1)}, bf16[256,1024]{1,0:T(8,128)(2,1)S(1)}, u32[]{:S(2)}, u32[]{:S(2)}) collective-permute-start(bf16[256,1024]{1,0:T(8,128)(2,1)} %shard_map.96), channel_id=1, source_target_pairs={{0,4},{1,5},{2,6},{3,7},{4,8},{5,9},{6,10},{7,11},{8,12},{9,13},{1... | collective-permute-start | bytes 1572872 | tf_op jit(solution)/shard_map/ppermute | solution.py:25
  5.7 0.8 shard_map.94.refs_0_.refs_1_
  6.5 1.6 %collective-permute-start.3 = (bf16[176,1152]{1,0:T(8,128)(2,1)S(1)}, bf16[176,1152]{1,0:T(8,128)(2,1)S(1)}, u32[]{:S(2)}, u32[]{:S(2)}) collective-permute-start(bf16[176,1152]{1,0:T(8,128)(2,1)S(1)} %shard_map.94.refs_0_.refs_1_), channel_id=1, source_target_pairs={{0,16},{1,17},{2,18},{3,19},{4,20},{5,21},{6,22},{7,23},{8,24},{9,... | collective-permute-start | bytes 1216520 | tf_op jit(solution)/shard_map/ppermute | solution.py:25
  8.1 1.6 %collective-permute-start = (bf16[16,3072]{1,0:T(8,128)(2,1)S(1)}, bf16[16,3072]{1,0:T(8,128)(2,1)S(1)}, u32[]{:S(2)}, u32[]{:S(2)}) collective-permute-start(bf16[16,3072]{1,0:T(8,128)(2,1)S(1)} %shard_map.95.refs_0_), channel_id=1, source_target_pairs={{0,4},{1,5},{2,6},{3,7},{4,8},{5,9},{6,10},{7,11},{8,12},{9,13},{1... | collective-permute-start | bytes 294920 | tf_op jit(solution)/shard_map/ppermute | solution.py:25
  9.7 1.2 %collective-permute-start.1 = (bf16[16,3072]{1,0:T(8,128)(2,1)S(1)}, bf16[16,3072]{1,0:T(8,128)(2,1)S(1)}, u32[]{:S(2)}, u32[]{:S(2)}) collective-permute-start(bf16[16,3072]{1,0:T(8,128)(2,1)S(1)} %shard_map.95.refs_0_), channel_id=1, source_target_pairs={{0,8},{1,9},{2,10},{3,11},{4,12},{5,13},{6,14},{7,15},{8,0},{9,1},... | collective-permute-start | bytes 294920 | tf_op jit(solution)/shard_map/ppermute | solution.py:25
  10.9 2.7 %collective-permute-start.2 = (bf16[16,3072]{1,0:T(8,128)(2,1)S(1)}, bf16[16,3072]{1,0:T(8,128)(2,1)S(1)}, u32[]{:S(2)}, u32[]{:S(2)}) collective-permute-start(bf16[16,3072]{1,0:T(8,128)(2,1)S(1)} %shard_map.95.refs_0_), channel_id=1, source_target_pairs={{0,12},{1,13},{2,14},{3,15},{4,0},{5,1},{6,2},{7,3},{8,4},{9,5},{1... | collective-permute-start | bytes 294920 | tf_op jit(solution)/shard_map/ppermute | solution.py:25
  13.6 9.3 %collective-permute-done.refs_1_ = bf16[16,3072]{1,0:T(8,128)(2,1)S(1)} collective-permute-done((bf16[16,3072]{1,0:T(8,128)(2,1)S(1)}, bf16[16,3072]{1,0:T(8,128)(2,1)S(1)}, u32[]{:S(2)}, u32[]{:S(2)}) %collective-permute-start) | collective-permute-done | bytes 98336 | tf_op jit(solution)/shard_map/ppermute | solution.py:25
  22.9 3.4 %collective-permute-done.1.refs_2_ = bf16[16,3072]{1,0:T(8,128)(2,1)S(1)} collective-permute-done((bf16[16,3072]{1,0:T(8,128)(2,1)S(1)}, bf16[16,3072]{1,0:T(8,128)(2,1)S(1)}, u32[]{:S(2)}, u32[]{:S(2)}) %collective-permute-start.1) | collective-permute-done | bytes 98336 | tf_op jit(solution)/shard_map/ppermute | solution.py:25
  26.4 2.6 %collective-permute-start.14 = (bf16[256,1024]{1,0:T(8,128)(2,1)S(1)}, bf16[256,1024]{1,0:T(8,128)(2,1)S(1)}, u32[]{:S(2)}, u32[]{:S(2)}) collective-permute-start(bf16[256,1024]{1,0:T(8,128)(2,1)S(1)} %collective-permute-done.4.refs_7_), channel_id=1, source_target_pairs={{0,4},{1,5},{2,6},{3,7},{4,8},{5,9},{6,10},{7,11},{8,12},{9,13},{1... | collective-permute-start | bytes 1572872 | tf_op jit(solution)/shard_map/ppermute | solution.py:25
  29.2 1.5 %collective-permute-start.8 = (bf16[64,2048]{1,0:T(8,128)(2,1)S(1)}, bf16[64,2048]{1,0:T(8,128)(2,1)S(1)}, u32[]{:S(2)}, u32[]{:S(2)}) collective-permute-start(bf16[64,2048]{1,0:T(8,128)(2,1)S(1)} %get-tuple-element.52.refs_2_.refs_3_), channel_id=1, source_target_pairs={{0,16},{1,17},{2,18},{3,19},{4,20},{5,21},{6,22},{7,23},{8,24},{9,... | collective-permute-start | bytes 786440 | tf_op jit(solution)/shard_map/ppermute | solution.py:25
  30.8 1.3 %collective-permute-done.6.refs_5_ = bf16[64,1024]{1,0:T(8,128)(2,1)S(1)} collective-permute-done((bf16[64,1024]{1,0:T(8,128)(2,1)S(1)}, bf16[64,1024]{1,0:T(8,128)(2,1)S(1)}, u32[]{:S(2)}, u32[]{:S(2)}) %collective-permute-start.6) | collective-permute-done | bytes 131104 | tf_op jit(solution)/shard_map/ppermute | solution.py:25
  32.1 1.6 %copy-done = bf16[1,1024,1024]{2,1,0:T(8,128)(2,1)S(1)} copy-done((bf16[1,1024,1024]{2,1,0:T(8,128)(2,1)S(1)}, bf16[1,1024,1024]{2,1,0:T(8,128)(2,1)}, u32[]{:S(2)}) %copy-start) | copy-done | bytes 2097176
  33.7 2.2 %shard_map.98 = (bf16[176,1024]{1,0:T(8,128)(2,1)S(1)}, bf16[176,1024]{1,0:T(8,128)(2,1)S(1)}, bf16[352,128]{1,0:T(8,128)(2,1)S(1)}) custom-call(bf16[176,1152]{1,0:T(8,128)(2,1)S(1)} %shard_map.94.refs_0_.refs_1_, bf16[176,1152]{1,0:T(8,128)(2,1)S(1)} %collective-permute-done.3.refs_1_, bf16[64,2048]{1,0:T(8,128)(2,1)S(1)} %get-tuple-element.52.refs_2_.refs_3_, ...), custom_call_target="tpu_custom_call" | custom-call | flops 1000 | bytes 1000 | tf_op jit(solution)/shard_map/pallas_call | solution.py:42
  35.9 1.5 %collective-permute-start.10 = (bf16[176,1024]{1,0:T(8,128)(2,1)S(1)}, bf16[176,1024]{1,0:T(8,128)(2,1)S(1)}, u32[]{:S(2)}, u32[]{:S(2)}) collective-permute-start(bf16[176,1024]{1,0:T(8,128)(2,1)S(1)} %get-tuple-element.58), channel_id=1, source_target_pairs={{0,18},{1,19},{2,16},{3,17},{4,22},{5,23},{6,20},{7,21},{8,26},{9,... | collective-permute-start | bytes 1081352 | tf_op jit(solution)/shard_map/ppermute | solution.py:25
  38.0 4.6 %collective-permute-done.14.block_ref.refs_5_ = bf16[256,1024]{1,0:T(8,128)(2,1)S(1)} collective-permute-done((bf16[256,1024]{1,0:T(8,128)(2,1)S(1)}, bf16[256,1024]{1,0:T(8,128)(2,1)S(1)}, u32[]{:S(2)}, u32[]{:S(2)}) %collective-permute-start.14) | collective-permute-done | bytes 524320 | tf_op jit(solution)/shard_map/ppermute | solution.py:25
  43.3 4.9 %collective-permute-done.10.refs_1_ = bf16[176,1024]{1,0:T(8,128)(2,1)S(1)} collective-permute-done((bf16[176,1024]{1,0:T(8,128)(2,1)S(1)}, bf16[176,1024]{1,0:T(8,128)(2,1)S(1)}, u32[]{:S(2)}, u32[]{:S(2)}) %collective-permute-start.10) | collective-permute-done | bytes 360480 | tf_op jit(solution)/shard_map/ppermute | solution.py:25
  48.1 6.0 %collective-permute-done.11.refs_0_ = bf16[176,1024]{1,0:T(8,128)(2,1)S(1)} collective-permute-done((bf16[176,1024]{1,0:T(8,128)(2,1)S(1)}, bf16[176,1024]{1,0:T(8,128)(2,1)S(1)}, u32[]{:S(2)}, u32[]{:S(2)}) %collective-permute-start.11) | collective-permute-done | bytes 360480 | tf_op jit(solution)/shard_map/ppermute | solution.py:25
  54.6 1.3 %shard_map.99 = (f32[64,5120]{1,0:T(8,128)S(1)}, bf16[64,2560]{1,0:T(8,128)(2,1)S(1)}, bf16[64,2560]{1,0:T(8,128)(2,1)S(1)}) custom-call(bf16[176,4096]{1,0:T(8,128)(2,1)S(1)} %bitcast.11, bf16[176,1152]{1,0:T(8,128)(2,1)S(1)} %shard_map.94.refs_0_.refs_1_, bf16[352,128]{1,0:T(8,128)(2,1)S(1)} %get-tuple-element.55.refs_2_.refs_4_, ...), custom_call_target="tpu_custom_call" | custom-call | flops 1000 | bytes 1000 | tf_op jit(solution)/shard_map/pallas_call | solution.py:42
  56.5 1.2 %shard_map.103 = bf16[352,512]{1,0:T(8,128)(2,1)S(1)} custom-call(bf16[176,1152]{1,0:T(8,128)(2,1)S(1)} %shard_map.94.refs_0_.refs_1_, bf16[176,1152]{1,0:T(8,128)(2,1)S(1)} %collective-permute-done.3.refs_1_, bf16[64,2048]{1,0:T(8,128)(2,1)S(1)} %get-tuple-element.52.refs_2_.refs_3_, bf16[64,2048]{1,0:T(8,128)(2,1)S(1)} %collective-permute-done.5.refs_3_.refs_4_, ...), custom_call_target="tpu_custom_call" | custom-call | flops 1000 | bytes 1000 | tf_op jit(solution)/shard_map/pallas_call | solution.py:42
  57.7 1.6 %collective-permute-start.21 = (bf16[352,512]{1,0:T(8,128)(2,1)S(1)}, bf16[352,512]{1,0:T(8,128)(2,1)S(1)}, u32[]{:S(2)}, u32[]{:S(2)}) collective-permute-start(bf16[352,512]{1,0:T(8,128)(2,1)S(1)} %shard_map.103), channel_id=1, source_target_pairs={{0,2},{1,3},{2,0},{3,1},{4,6},{5,7},{6,4},{7,5},{8,10},{9,11},{10,... | collective-permute-start | bytes 1081352 | tf_op jit(solution)/shard_map/ppermute | solution.py:25
  60.3 1.7 %collective-permute-start.17 = (bf16[16,5120]{1,0:T(8,128)(2,1)S(1)}, bf16[16,5120]{1,0:T(8,128)(2,1)S(1)}, u32[]{:S(2)}, u32[]{:S(2)}) collective-permute-start(bf16[16,5120]{1,0:T(8,128)(2,1)S(1)} %get-tuple-element.68), channel_id=1, source_target_pairs={{0,8},{1,9},{2,10},{3,11},{4,12},{5,13},{6,14},{7,15},{8,0},{9,1},... | collective-permute-start | bytes 491528 | tf_op jit(solution)/shard_map/ppermute | solution.py:25
  61.9 2.7 %collective-permute-start.16 = (bf16[16,5120]{1,0:T(8,128)(2,1)S(1)}, bf16[16,5120]{1,0:T(8,128)(2,1)S(1)}, u32[]{:S(2)}, u32[]{:S(2)}) collective-permute-start(bf16[16,5120]{1,0:T(8,128)(2,1)S(1)} %get-tuple-element.66), channel_id=1, source_target_pairs={{0,12},{1,13},{2,14},{3,15},{4,0},{5,1},{6,2},{7,3},{8,4},{9,5},{1... | collective-permute-start | bytes 491528 | tf_op jit(solution)/shard_map/ppermute | solution.py:25
  64.6 1.2 %shard_map.106 = (bf16[176,512]{1,0:T(8,128)(2,1)S(1)}, bf16[176,512]{1,0:T(8,128)(2,1)S(1)}) custom-call(bf16[176,1152]{1,0:T(8,128)(2,1)S(1)} %shard_map.94.refs_0_.refs_1_, bf16[176,1152]{1,0:T(8,128)(2,1)S(1)} %collective-permute-done.3.refs_1_, bf16[64,2048]{1,0:T(8,128)(2,1)S(1)} %get-tuple-element.52.refs_2_.refs_3_, ...), custom_call_target="tpu_custom_call" | custom-call | flops 1000 | bytes 1000 | tf_op jit(solution)/shard_map/pallas_call | solution.py:42
  65.8 1.5 %collective-permute-start.25 = (bf16[176,512]{1,0:T(8,128)(2,1)S(1)}, bf16[176,512]{1,0:T(8,128)(2,1)S(1)}, u32[]{:S(2)}, u32[]{:S(2)}) collective-permute-start(bf16[176,512]{1,0:T(8,128)(2,1)S(1)} %get-tuple-element.81), channel_id=1, source_target_pairs={{0,18},{1,19},{2,16},{3,17},{4,22},{5,23},{6,20},{7,21},{8,26},{9,... | collective-permute-start | bytes 540680 | tf_op jit(solution)/shard_map/ppermute | solution.py:25
  67.3 0.8 %collective-permute-done.21 = bf16[352,512]{1,0:T(8,128)(2,1)S(1)} collective-permute-done((bf16[352,512]{1,0:T(8,128)(2,1)S(1)}, bf16[352,512]{1,0:T(8,128)(2,1)S(1)}, u32[]{:S(2)}, u32[]{:S(2)}) %collective-permute-start.21) | collective-permute-done | bytes 360480 | tf_op jit(solution)/shard_map/ppermute | solution.py:25
  68.2 1.9 %collective-permute-start.26 = (bf16[176,512]{1,0:T(8,128)(2,1)S(1)}, bf16[176,512]{1,0:T(8,128)(2,1)S(1)}, u32[]{:S(2)}, u32[]{:S(2)}) collective-permute-start(bf16[176,512]{1,0:T(8,128)(2,1)S(1)} %get-tuple-element.82), channel_id=1, source_target_pairs={{0,2},{1,3},{2,0},{3,1},{4,6},{5,7},{6,4},{7,5},{8,10},{9,11},{10,... | collective-permute-start | bytes 540680 | tf_op jit(solution)/shard_map/ppermute | solution.py:25
  70.1 1.2 %shard_map.104.refs_3_ = bf16[176,4096]{1,0:T(8,128)(2,1)} custom-call(bf16[176,1024]{1,0:T(8,128)(2,1)S(1)} %collective-permute-done.11.refs_0_, bf16[176,1024]{1,0:T(8,128)(2,1)S(1)} %collective-permute-done.10.refs_1_, bf16[176,512]{1,0:T(8,128)(2,1)S(1)} %get-tuple-element.90.refs_2_), custom_call_target="tpu_custom_call" | custom-call | flops 1000 | bytes 1000 | tf_op jit(solution)/shard_map/pallas_call | solution.py:42
  71.3 2.0 %collective-permute-start.22 = (bf16[176,512]{1,0:T(8,128)(2,1)S(1)}, bf16[176,512]{1,0:T(8,128)(2,1)S(1)}, u32[]{:S(2)}, u32[]{:S(2)}) collective-permute-start(bf16[176,512]{1,0:T(8,128)(2,1)S(1)} %get-tuple-element.76), channel_id=1, source_target_pairs={{0,16},{1,17},{2,18},{3,19},{4,20},{5,21},{6,22},{7,23},{8,24},{9,... | collective-permute-start | bytes 540680 | tf_op jit(solution)/shard_map/ppermute | solution.py:25
  73.2 1.9 %collective-permute-done.17.refs_2_ = bf16[16,5120]{1,0:T(8,128)(2,1)S(1)} collective-permute-done((bf16[16,5120]{1,0:T(8,128)(2,1)S(1)}, bf16[16,5120]{1,0:T(8,128)(2,1)S(1)}, u32[]{:S(2)}, u32[]{:S(2)}) %collective-permute-start.17) | collective-permute-done | bytes 163872 | tf_op jit(solution)/shard_map/ppermute | solution.py:25
  76.3 0.8 %collective-permute-done.22.refs_0_ = bf16[176,512]{1,0:T(8,128)(2,1)S(1)} collective-permute-done((bf16[176,512]{1,0:T(8,128)(2,1)S(1)}, bf16[176,512]{1,0:T(8,128)(2,1)S(1)}, u32[]{:S(2)}, u32[]{:S(2)}) %collective-permute-start.22) | collective-permute-done | bytes 180256 | tf_op jit(solution)/shard_map/ppermute | solution.py:25
  77.2 0.8 %shard_map.107 = bf16[176,4096]{1,0:T(8,128)(2,1)} custom-call(bf16[176,512]{1,0:T(8,128)(2,1)S(1)} %collective-permute-done.22.refs_0_, bf16[176,512]{1,0:T(8,128)(2,1)S(1)} %collective-permute-done.25.refs_1_, bf16[176,512]{1,0:T(8,128)(2,1)S(1)} %collective-permute-done.26.refs_2_, ...), custom_call_target="tpu_custom_call", output_to_operand_aliasing={{}: (3, {})} | custom-call | flops 1000 | bytes 1000 | tf_op jit(solution)/shard_map/pallas_call | solution.py:443
  (56 shorter events, 5.7 us)
Async XLA Ops:
  0.7 7.4 %copy-start.3 = (bf16[1,2,16,4096]{3,2,1,0:T(8,128)(2,1)S(1)}, bf16[1,2,16,4096]{3,2,1,0:T(8,128)(2,1)}, u32[]{:S(2)}) copy-start(bf16[1,2,16,4096]{3,2,1,0:T(8,128)(2,1)} %param.12) | copy-start | bytes 786436
  0.7 7.4 %copy-start.4 = (bf16[1,2,16,1024]{3,2,1,0:T(8,128)(2,1)S(1)}, bf16[1,2,16,1024]{3,2,1,0:T(8,128)(2,1)}, u32[]{:S(2)}) copy-start(bf16[1,2,16,1024]{3,2,1,0:T(8,128)(2,1)} %param.13) | copy-start | bytes 196612
  2.6 23.7 %collective-permute-start.4 = (bf16[256,1024]{1,0:T(8,128)(2,1)}, bf16[256,1024]{1,0:T(8,128)(2,1)S(1)}, u32[]{:S(2)}, u32[]{:S(2)}) collective-permute-start(bf16[256,1024]{1,0:T(8,128)(2,1)} %shard_map.96), channel_id=1, source_target_pairs={{0,4},{1,5},{2,6},{3,7},{4,8},{5,9},{6,10},{7,11},{8,12},{9,13},{1... | collective-permute-start | bytes 1572872 | tf_op jit(solution)/shard_map/ppermute | solution.py:25
  6.5 19.8 %collective-permute-start.3 = (bf16[176,1152]{1,0:T(8,128)(2,1)S(1)}, bf16[176,1152]{1,0:T(8,128)(2,1)S(1)}, u32[]{:S(2)}, u32[]{:S(2)}) collective-permute-start(bf16[176,1152]{1,0:T(8,128)(2,1)S(1)} %shard_map.94.refs_0_.refs_1_), channel_id=1, source_target_pairs={{0,16},{1,17},{2,18},{3,19},{4,20},{5,21},{6,22},{7,23},{8,24},{9,... | collective-permute-start | bytes 1216520 | tf_op jit(solution)/shard_map/ppermute | solution.py:25
  8.1 14.8 %collective-permute-start = (bf16[16,3072]{1,0:T(8,128)(2,1)S(1)}, bf16[16,3072]{1,0:T(8,128)(2,1)S(1)}, u32[]{:S(2)}, u32[]{:S(2)}) collective-permute-start(bf16[16,3072]{1,0:T(8,128)(2,1)S(1)} %shard_map.95.refs_0_), channel_id=1, source_target_pairs={{0,4},{1,5},{2,6},{3,7},{4,8},{5,9},{6,10},{7,11},{8,12},{9,13},{1... | collective-permute-start | bytes 294920 | tf_op jit(solution)/shard_map/ppermute | solution.py:25
  9.7 16.6 %collective-permute-start.1 = (bf16[16,3072]{1,0:T(8,128)(2,1)S(1)}, bf16[16,3072]{1,0:T(8,128)(2,1)S(1)}, u32[]{:S(2)}, u32[]{:S(2)}) collective-permute-start(bf16[16,3072]{1,0:T(8,128)(2,1)S(1)} %shard_map.95.refs_0_), channel_id=1, source_target_pairs={{0,8},{1,9},{2,10},{3,11},{4,12},{5,13},{6,14},{7,15},{8,0},{9,1},... | collective-permute-start | bytes 294920 | tf_op jit(solution)/shard_map/ppermute | solution.py:25
  10.9 15.4 %collective-permute-start.2 = (bf16[16,3072]{1,0:T(8,128)(2,1)S(1)}, bf16[16,3072]{1,0:T(8,128)(2,1)S(1)}, u32[]{:S(2)}, u32[]{:S(2)}) collective-permute-start(bf16[16,3072]{1,0:T(8,128)(2,1)S(1)} %shard_map.95.refs_0_), channel_id=1, source_target_pairs={{0,12},{1,13},{2,14},{3,15},{4,0},{5,1},{6,2},{7,3},{8,4},{9,5},{1... | collective-permute-start | bytes 294920 | tf_op jit(solution)/shard_map/ppermute | solution.py:25
  26.3 5.8 %collective-permute-start.7 = (bf16[256,1024]{1,0:T(8,128)(2,1)S(1)}, bf16[256,1024]{1,0:T(8,128)(2,1)S(1)}, u32[]{:S(2)}, u32[]{:S(2)}) collective-permute-start(bf16[256,1024]{1,0:T(8,128)(2,1)S(1)} %collective-permute-done.4.refs_7_), channel_id=1, source_target_pairs={{0,1},{1,0},{2,3},{3,2},{4,5},{5,4},{6,7},{7,6},{8,9},{9,8},{10,11... | collective-permute-start | bytes 1572872 | tf_op jit(solution)/shard_map/ppermute | solution.py:25
  26.4 16.2 %collective-permute-start.14 = (bf16[256,1024]{1,0:T(8,128)(2,1)S(1)}, bf16[256,1024]{1,0:T(8,128)(2,1)S(1)}, u32[]{:S(2)}, u32[]{:S(2)}) collective-permute-start(bf16[256,1024]{1,0:T(8,128)(2,1)S(1)} %collective-permute-done.4.refs_7_), channel_id=1, source_target_pairs={{0,4},{1,5},{2,6},{3,7},{4,8},{5,9},{6,10},{7,11},{8,12},{9,13},{1... | collective-permute-start | bytes 1572872 | tf_op jit(solution)/shard_map/ppermute | solution.py:25
  29.0 3.1 %collective-permute-start.5 = (bf16[64,2048]{1,0:T(8,128)(2,1)S(1)}, bf16[64,2048]{1,0:T(8,128)(2,1)S(1)}, u32[]{:S(2)}, u32[]{:S(2)}) collective-permute-start(bf16[64,2048]{1,0:T(8,128)(2,1)S(1)} %get-tuple-element.52.refs_2_.refs_3_), channel_id=1, source_target_pairs={{0,1},{1,0},{2,3},{3,2},{4,5},{5,4},{6,7},{7,6},{8,9},{9,8},{10,11... | collective-permute-start | bytes 786440 | tf_op jit(solution)/shard_map/ppermute | solution.py:25
  29.2 8.8 %collective-permute-start.8 = (bf16[64,2048]{1,0:T(8,128)(2,1)S(1)}, bf16[64,2048]{1,0:T(8,128)(2,1)S(1)}, u32[]{:S(2)}, u32[]{:S(2)}) collective-permute-start(bf16[64,2048]{1,0:T(8,128)(2,1)S(1)} %get-tuple-element.52.refs_2_.refs_3_), channel_id=1, source_target_pairs={{0,16},{1,17},{2,18},{3,19},{4,20},{5,21},{6,22},{7,23},{8,24},{9,... | collective-permute-start | bytes 786440 | tf_op jit(solution)/shard_map/ppermute | solution.py:25
  30.7 1.3 %collective-permute-start.6 = (bf16[64,1024]{1,0:T(8,128)(2,1)S(1)}, bf16[64,1024]{1,0:T(8,128)(2,1)S(1)}, u32[]{:S(2)}, u32[]{:S(2)}) collective-permute-start(bf16[64,1024]{1,0:T(8,128)(2,1)S(1)} %get-tuple-element.53.refs_4_), channel_id=1, source_target_pairs={{0,1},{1,0},{2,3},{3,2},{4,5},{5,4},{6,7},{7,6},{8,9},{9,8},{10,11... | collective-permute-start | bytes 393224 | tf_op jit(solution)/shard_map/ppermute | solution.py:25
  33.7 21.0 %copy-start.1 = (bf16[1,176,4096]{2,1,0:T(8,128)(2,1)S(1)}, bf16[1,176,4096]{2,1,0:T(8,128)(2,1)}, u32[]{:S(2)}) copy-start(bf16[1,176,4096]{2,1,0:T(8,128)(2,1)} %param.7) | copy-start | bytes 4325380
  35.9 12.2 %collective-permute-start.10 = (bf16[176,1024]{1,0:T(8,128)(2,1)S(1)}, bf16[176,1024]{1,0:T(8,128)(2,1)S(1)}, u32[]{:S(2)}, u32[]{:S(2)}) collective-permute-start(bf16[176,1024]{1,0:T(8,128)(2,1)S(1)} %get-tuple-element.58), channel_id=1, source_target_pairs={{0,18},{1,19},{2,16},{3,17},{4,22},{5,23},{6,20},{7,21},{8,26},{9,... | collective-permute-start | bytes 1081352 | tf_op jit(solution)/shard_map/ppermute | solution.py:25
  37.4 16.7 %collective-permute-start.11 = (bf16[176,1024]{1,0:T(8,128)(2,1)S(1)}, bf16[176,1024]{1,0:T(8,128)(2,1)S(1)}, u32[]{:S(2)}, u32[]{:S(2)}) collective-permute-start(bf16[176,1024]{1,0:T(8,128)(2,1)S(1)} %get-tuple-element.59), channel_id=1, source_target_pairs={{0,2},{1,3},{2,0},{3,1},{4,6},{5,7},{6,4},{7,5},{8,10},{9,11},{10,... | collective-permute-start | bytes 1081352 | tf_op jit(solution)/shard_map/ppermute | solution.py:25
  38.0 16.7 %collective-permute-start.9 = (bf16[64,2048]{1,0:T(8,128)(2,1)S(1)}, bf16[64,2048]{1,0:T(8,128)(2,1)S(1)}, u32[]{:S(2)}, u32[]{:S(2)}) collective-permute-start(bf16[64,2048]{1,0:T(8,128)(2,1)S(1)} %collective-permute-done.8.refs_5_), channel_id=1, source_target_pairs={{0,1},{1,0},{2,3},{3,2},{4,5},{5,4},{6,7},{7,6},{8,9},{9,8},{10,11... | collective-permute-start | bytes 786440 | tf_op jit(solution)/shard_map/ppermute | solution.py:25
  42.6 16.7 %collective-permute-start.15 = (bf16[256,1024]{1,0:T(8,128)(2,1)S(1)}, bf16[256,1024]{1,0:T(8,128)(2,1)S(1)}, u32[]{:S(2)}, u32[]{:S(2)}) collective-permute-start(bf16[256,1024]{1,0:T(8,128)(2,1)S(1)} %collective-permute-done.14.block_ref.refs_5_), channel_id=1, source_target_pairs={{0,4},{1,5},{2,6},{3,7},{4,8},{5,9},{6,10},{7,11},{8,12},{9,13},{1... | collective-permute-start | bytes 1572872 | tf_op jit(solution)/shard_map/ppermute | solution.py:25
  54.1 2.4 %collective-permute-start.20 = (bf16[128,1024]{1,0:T(8,128)(2,1)S(1)}, bf16[128,1024]{1,0:T(8,128)(2,1)S(1)}, u32[]{:S(2)}, u32[]{:S(2)}) collective-permute-start(bf16[128,1024]{1,0:T(8,128)(2,1)S(1)} %get-tuple-element.75), channel_id=1, source_target_pairs={{0,1},{1,0},{2,3},{3,2},{4,5},{5,4},{6,7},{7,6},{8,9},{9,8},{10,11... | collective-permute-start | bytes 786440 | tf_op jit(solution)/shard_map/ppermute | solution.py:25
  54.1 2.4 %collective-permute-start.19 = (bf16[128,1024]{1,0:T(8,128)(2,1)S(1)}, bf16[128,1024]{1,0:T(8,128)(2,1)S(1)}, u32[]{:S(2)}, u32[]{:S(2)}) collective-permute-start(bf16[128,1024]{1,0:T(8,128)(2,1)S(1)} %get-tuple-element.73), channel_id=1, source_target_pairs={{0,1},{1,0},{2,3},{3,2},{4,5},{5,4},{6,7},{7,6},{8,9},{9,8},{10,11... | collective-permute-start | bytes 786440 | tf_op jit(solution)/shard_map/ppermute | solution.py:25
  55.9 3.4 %collective-permute-start.13 = (bf16[64,2560]{1,0:T(8,128)(2,1)S(1)}, bf16[64,2560]{1,0:T(8,128)(2,1)S(1)}, u32[]{:S(2)}, u32[]{:S(2)}) collective-permute-start(bf16[64,2560]{1,0:T(8,128)(2,1)S(1)} %get-tuple-element.62), channel_id=1, source_target_pairs={{0,1},{1,0},{2,3},{3,2},{4,5},{5,4},{6,7},{7,6},{8,9},{9,8},{10,11... | collective-permute-start | bytes 983048 | tf_op jit(solution)/shard_map/ppermute | solution.py:25
  56.0 3.3 %collective-permute-start.12 = (bf16[64,2560]{1,0:T(8,128)(2,1)S(1)}, bf16[64,2560]{1,0:T(8,128)(2,1)S(1)}, u32[]{:S(2)}, u32[]{:S(2)}) collective-permute-start(bf16[64,2560]{1,0:T(8,128)(2,1)S(1)} %get-tuple-element.60), channel_id=1, source_target_pairs={{0,1},{1,0},{2,3},{3,2},{4,5},{5,4},{6,7},{7,6},{8,9},{9,8},{10,11... | collective-permute-start | bytes 983048 | tf_op jit(solution)/shard_map/ppermute | solution.py:25
  57.7 10.5 %collective-permute-start.21 = (bf16[352,512]{1,0:T(8,128)(2,1)S(1)}, bf16[352,512]{1,0:T(8,128)(2,1)S(1)}, u32[]{:S(2)}, u32[]{:S(2)}) collective-permute-start(bf16[352,512]{1,0:T(8,128)(2,1)S(1)} %shard_map.103), channel_id=1, source_target_pairs={{0,2},{1,3},{2,0},{3,1},{4,6},{5,7},{6,4},{7,5},{8,10},{9,11},{10,... | collective-permute-start | bytes 1081352 | tf_op jit(solution)/shard_map/ppermute | solution.py:25
  59.4 2.5 %collective-permute-start.24 = (bf16[128,1024]{1,0:T(8,128)(2,1)S(1)}, bf16[128,1024]{1,0:T(8,128)(2,1)S(1)}, u32[]{:S(2)}, u32[]{:S(2)}) collective-permute-start(bf16[128,1024]{1,0:T(8,128)(2,1)S(1)} %get-tuple-element.80), channel_id=1, source_target_pairs={{0,1},{1,0},{2,3},{3,2},{4,5},{5,4},{6,7},{7,6},{8,9},{9,8},{10,11... | collective-permute-start | bytes 786440 | tf_op jit(solution)/shard_map/ppermute | solution.py:25
  59.5 5.1 %collective-permute-start.23 = (bf16[128,1024]{1,0:T(8,128)(2,1)S(1)}, bf16[128,1024]{1,0:T(8,128)(2,1)S(1)}, u32[]{:S(2)}, u32[]{:S(2)}) collective-permute-start(bf16[128,1024]{1,0:T(8,128)(2,1)S(1)} %get-tuple-element.78), channel_id=1, source_target_pairs={{0,1},{1,0},{2,3},{3,2},{4,5},{5,4},{6,7},{7,6},{8,9},{9,8},{10,11... | collective-permute-start | bytes 786440 | tf_op jit(solution)/shard_map/ppermute | solution.py:25
  60.0 11.3 %collective-permute-start.18 = (bf16[16,5120]{1,0:T(8,128)(2,1)S(1)}, bf16[16,5120]{1,0:T(8,128)(2,1)S(1)}, u32[]{:S(2)}, u32[]{:S(2)}) collective-permute-start(bf16[16,5120]{1,0:T(8,128)(2,1)S(1)} %get-tuple-element.70), channel_id=1, source_target_pairs={{0,4},{1,5},{2,6},{3,7},{4,8},{5,9},{6,10},{7,11},{8,12},{9,13},{1... | collective-permute-start | bytes 491528 | tf_op jit(solution)/shard_map/ppermute | solution.py:25
  60.3 14.9 %collective-permute-start.17 = (bf16[16,5120]{1,0:T(8,128)(2,1)S(1)}, bf16[16,5120]{1,0:T(8,128)(2,1)S(1)}, u32[]{:S(2)}, u32[]{:S(2)}) collective-permute-start(bf16[16,5120]{1,0:T(8,128)(2,1)S(1)} %get-tuple-element.68), channel_id=1, source_target_pairs={{0,8},{1,9},{2,10},{3,11},{4,12},{5,13},{6,14},{7,15},{8,0},{9,1},... | collective-permute-start | bytes 491528 | tf_op jit(solution)/shard_map/ppermute | solution.py:25
  61.9 13.2 %collective-permute-start.16 = (bf16[16,5120]{1,0:T(8,128)(2,1)S(1)}, bf16[16,5120]{1,0:T(8,128)(2,1)S(1)}, u32[]{:S(2)}, u32[]{:S(2)}) collective-permute-start(bf16[16,5120]{1,0:T(8,128)(2,1)S(1)} %get-tuple-element.66), channel_id=1, source_target_pairs={{0,12},{1,13},{2,14},{3,15},{4,0},{5,1},{6,2},{7,3},{8,4},{9,5},{1... | collective-permute-start | bytes 491528 | tf_op jit(solution)/shard_map/ppermute | solution.py:25
  65.8 10.1 %collective-permute-start.25 = (bf16[176,512]{1,0:T(8,128)(2,1)S(1)}, bf16[176,512]{1,0:T(8,128)(2,1)S(1)}, u32[]{:S(2)}, u32[]{:S(2)}) collective-permute-start(bf16[176,512]{1,0:T(8,128)(2,1)S(1)} %get-tuple-element.81), channel_id=1, source_target_pairs={{0,18},{1,19},{2,16},{3,17},{4,22},{5,23},{6,20},{7,21},{8,26},{9,... | collective-permute-start | bytes 540680 | tf_op jit(solution)/shard_map/ppermute | solution.py:25
  68.2 8.2 %collective-permute-start.26 = (bf16[176,512]{1,0:T(8,128)(2,1)S(1)}, bf16[176,512]{1,0:T(8,128)(2,1)S(1)}, u32[]{:S(2)}, u32[]{:S(2)}) collective-permute-start(bf16[176,512]{1,0:T(8,128)(2,1)S(1)} %get-tuple-element.82), channel_id=1, source_target_pairs={{0,2},{1,3},{2,0},{3,1},{4,6},{5,7},{6,4},{7,5},{8,10},{9,11},{10,... | collective-permute-start | bytes 540680 | tf_op jit(solution)/shard_map/ppermute | solution.py:25
  71.3 5.9 %collective-permute-start.22 = (bf16[176,512]{1,0:T(8,128)(2,1)S(1)}, bf16[176,512]{1,0:T(8,128)(2,1)S(1)}, u32[]{:S(2)}, u32[]{:S(2)}) collective-permute-start(bf16[176,512]{1,0:T(8,128)(2,1)S(1)} %get-tuple-element.76), channel_id=1, source_target_pairs={{0,16},{1,17},{2,18},{3,19},{4,20},{5,21},{6,22},{7,23},{8,24},{9,... | collective-permute-start | bytes 540680 | tf_op jit(solution)/shard_map/ppermute | solution.py:25
  75.3 2.7 %collective-permute-start.27 = (bf16[16,2560]{1,0:T(8,128)(2,1)S(1)}, bf16[16,2560]{1,0:T(8,128)(2,1)S(1)}, u32[]{:S(2)}, u32[]{:S(2)}) collective-permute-start(bf16[16,2560]{1,0:T(8,128)(2,1)S(1)} %get-tuple-element.85.refs_0_), channel_id=1, source_target_pairs={{0,1},{1,0},{2,3},{3,2},{4,5},{5,4},{6,7},{7,6},{8,9},{9,8},{10,11... | collective-permute-start | bytes 245768 | tf_op jit(solution)/shard_map/ppermute | solution.py:25
  75.3 2.7 %collective-permute-start.28 = (bf16[16,2560]{1,0:T(8,128)(2,1)S(1)}, bf16[16,2560]{1,0:T(8,128)(2,1)S(1)}, u32[]{:S(2)}, u32[]{:S(2)}) collective-permute-start(bf16[16,2560]{1,0:T(8,128)(2,1)S(1)} %get-tuple-element.86.refs_1_), channel_id=1, source_target_pairs={{0,1},{1,0},{2,3},{3,2},{4,5},{5,4},{6,7},{7,6},{8,9},{9,8},{10,11... | collective-permute-start | bytes 245768 | tf_op jit(solution)/shard_map/ppermute | solution.py:25
  (4 other events, 16.7 us)

commit v19 on v17

--- a/solution.py
+++ b/solution.py
@@ -298,7 +298,7 @@
     )[0]
     held = [own]
     for k in range(1, holders):
-        held.append(moved(own, lambda g, z, s, r: (g, z + k, s, r)))
+        held.append(moved(held[-1], lambda g, z, s, r: (g, z + 1, s, r)))
 
     ring = [lax.dynamic_slice_in_dim(frozen, (group * replicas + core) * piece, piece, axis=0)]
     ring.append(moved(ring[0], lambda g, z, s, r: (g, z + 1, s, r)))

time: 77 us -> 85.3 us (1.11)
  waiting for transfers between devices: 29 us -> 46 us
  starting transfers between devices: 31.2 us -> 22.3 us
    ppermute x29, waiting for transfers between devices: 29 us -> 46 us  [moved(): return lax.ppermute(x, AXES, pairs)]
    ppermute x29, starting transfers between devices: 31.2 us -> 22.3 us  [moved(): return lax.ppermute(x, AXES, pairs)]
  transfers between devices with their start and end apart: 29 -> 29, of which waited for: 12 -> 12; matrix products, arithmetic and copies ran while one was open for 0% -> 0% of each run, Pallas kernels for 12% -> 11%
where the time goes in v19:
time: 85.3 us; the launch traced here: 84.3 us
  waiting for transfers between devices  46 us (54%)
  starting transfers between devices  22.3 us (26%)
  Pallas kernels  9.75 us (11%)
  local copies, waits for them, and re-layouts  5.37 us (6%)
    ppermute x29, waiting for transfers between devices, moved(): return lax.ppermute(x, AXES, pairs)  46 us
    ppermute x29, starting transfers between devices, moved(): return lax.ppermute(x, AXES, pairs)  22.3 us
    pallas_call x13, Pallas kernels, call(): pl.pallas_call(kernel, out_shape=out_shape, in_specs=[pl.BlockSpec(memory...  8.91 us
    unnamed x14, local copies, waits for them, and re-layouts  4.12 us
  transfers between devices with their start and end apart: 29, of which 12 were waited for; matrix products, arithmetic and copies ran while one was open for 0% of the time, Pallas kernels for 11%

profile of v19, /device:TPU:0, one launch (start us, length us, event | category | flops | bytes accessed | tf_op | source)
XLA Modules:
  0.0 84.3 jit_solution(9290845621507146420)
XLA Ops:
  0.6 1.2 %dynamic-slice_bitcast_fusion = bf16[256,1024]{1,0:T(8,128)(2,1)S(1)} fusion(bf16[1,1024,1024]{2,1,0:T(8,128)(2,1)} %param.11, s32[]{:T(128)S(6)} %select_n.3), kind=kLoop, calls=%fused_computation | loop fusion | bytes 1048580 | tf_op jit(solution)/shard_map/dynamic_slice | solution.py:303
  1.9 3.1 %collective-permute-start.4 = (bf16[256,1024]{1,0:T(8,128)(2,1)S(1)}, bf16[256,1024]{1,0:T(8,128)(2,1)S(1)}, u32[]{:S(2)}, u32[]{:S(2)}) collective-permute-start(bf16[256,1024]{1,0:T(8,128)(2,1)S(1)} %dynamic-slice_bitcast_fusion), channel_id=1, source_target_pairs={{0,4},{1,5},{2,6},{3,7},{4,8},{5,9},{6,10},{7,11},{8,12},{9,13},{1... | collective-permute-start | bytes 1572872 | tf_op jit(solution)/shard_map/ppermute | solution.py:24
  5.0 1.0 %copy-done.2 = bf16[1,176,1024]{2,1,0:T(8,128)(2,1)S(1)} copy-done((bf16[1,176,1024]{2,1,0:T(8,128)(2,1)S(1)}, bf16[1,176,1024]{2,1,0:T(8,128)(2,1)}, u32[]{:S(2)}) %copy-start.2) | copy-done | bytes 360472
  7.3 0.8 shard_map.95.refs_0_.refs_1_
  8.0 1.6 %collective-permute-start.3 = (bf16[176,1152]{1,0:T(8,128)(2,1)S(1)}, bf16[176,1152]{1,0:T(8,128)(2,1)S(1)}, u32[]{:S(2)}, u32[]{:S(2)}) collective-permute-start(bf16[176,1152]{1,0:T(8,128)(2,1)S(1)} %shard_map.95.refs_0_.refs_1_), channel_id=1, source_target_pairs={{0,16},{1,17},{2,18},{3,19},{4,20},{5,21},{6,22},{7,23},{8,24},{9,... | collective-permute-start | bytes 1216520 | tf_op jit(solution)/shard_map/ppermute | solution.py:24
  9.6 0.9 %copy-done.3 = bf16[1,2,16,4096]{3,2,1,0:T(8,128)(2,1)S(1)} copy-done((bf16[1,2,16,4096]{3,2,1,0:T(8,128)(2,1)S(1)}, bf16[1,2,16,4096]{3,2,1,0:T(8,128)(2,1)}, u32[]{:S(2)}) %copy-start.3) | copy-done | bytes 262168
  10.6 0.8 copy-done.4
  11.4 1.6 %collective-permute-start = (bf16[16,3072]{1,0:T(8,128)(2,1)S(1)}, bf16[16,3072]{1,0:T(8,128)(2,1)S(1)}, u32[]{:S(2)}, u32[]{:S(2)}) collective-permute-start(bf16[16,3072]{1,0:T(8,128)(2,1)S(1)} %shard_map.94.refs_0_), channel_id=1, source_target_pairs={{0,4},{1,5},{2,6},{3,7},{4,8},{5,9},{6,10},{7,11},{8,12},{9,13},{1... | collective-permute-start | bytes 294920 | tf_op jit(solution)/shard_map/ppermute | solution.py:24
  13.1 7.9 %collective-permute-done.refs_1_ = bf16[16,3072]{1,0:T(8,128)(2,1)S(1)} collective-permute-done((bf16[16,3072]{1,0:T(8,128)(2,1)S(1)}, bf16[16,3072]{1,0:T(8,128)(2,1)S(1)}, u32[]{:S(2)}, u32[]{:S(2)}) %collective-permute-start) | collective-permute-done | bytes 98336 | tf_op jit(solution)/shard_map/ppermute | solution.py:24
  21.0 6.4 %collective-permute-done.1.refs_2_ = bf16[16,3072]{1,0:T(8,128)(2,1)S(1)} collective-permute-done((bf16[16,3072]{1,0:T(8,128)(2,1)S(1)}, bf16[16,3072]{1,0:T(8,128)(2,1)S(1)}, u32[]{:S(2)}, u32[]{:S(2)}) %collective-permute-start.1) | collective-permute-done | bytes 98336 | tf_op jit(solution)/shard_map/ppermute | solution.py:24
  27.4 6.4 %collective-permute-done.2.refs_3_ = bf16[16,3072]{1,0:T(8,128)(2,1)S(1)} collective-permute-done((bf16[16,3072]{1,0:T(8,128)(2,1)S(1)}, bf16[16,3072]{1,0:T(8,128)(2,1)S(1)}, u32[]{:S(2)}, u32[]{:S(2)}) %collective-permute-start.2) | collective-permute-done | bytes 98336 | tf_op jit(solution)/shard_map/ppermute | solution.py:24
  34.5 1.5 %collective-permute-start.16 = (bf16[64,2048]{1,0:T(8,128)(2,1)S(1)}, bf16[64,2048]{1,0:T(8,128)(2,1)S(1)}, u32[]{:S(2)}, u32[]{:S(2)}) collective-permute-start(bf16[64,2048]{1,0:T(8,128)(2,1)S(1)} %get-tuple-element.50.refs_2_.refs_3_), channel_id=1, source_target_pairs={{0,16},{1,17},{2,18},{3,19},{4,20},{5,21},{6,22},{7,23},{8,24},{9,... | collective-permute-start | bytes 786440 | tf_op jit(solution)/shard_map/ppermute | solution.py:24
  36.0 1.3 %collective-permute-done.6.refs_5_ = bf16[64,1024]{1,0:T(8,128)(2,1)S(1)} collective-permute-done((bf16[64,1024]{1,0:T(8,128)(2,1)S(1)}, bf16[64,1024]{1,0:T(8,128)(2,1)S(1)}, u32[]{:S(2)}, u32[]{:S(2)}) %collective-permute-start.6) | collective-permute-done | bytes 131104 | tf_op jit(solution)/shard_map/ppermute | solution.py:24
  37.3 2.2 %shard_map.97 = (bf16[176,1024]{1,0:T(8,128)(2,1)S(1)}, bf16[176,1024]{1,0:T(8,128)(2,1)S(1)}, bf16[352,128]{1,0:T(8,128)(2,1)S(1)}) custom-call(bf16[176,1152]{1,0:T(8,128)(2,1)S(1)} %shard_map.95.refs_0_.refs_1_, bf16[176,1152]{1,0:T(8,128)(2,1)S(1)} %collective-permute-done.3.refs_1_, bf16[64,2048]{1,0:T(8,128)(2,1)S(1)} %get-tuple-element.50.refs_2_.refs_3_, ...), custom_call_target="tpu_custom_call" | custom-call | flops 1000 | bytes 1000 | tf_op jit(solution)/shard_map/pallas_call | solution.py:41
  39.6 1.6 %collective-permute-start.10 = (bf16[176,1024]{1,0:T(8,128)(2,1)S(1)}, bf16[176,1024]{1,0:T(8,128)(2,1)S(1)}, u32[]{:S(2)}, u32[]{:S(2)}) collective-permute-start(bf16[176,1024]{1,0:T(8,128)(2,1)S(1)} %get-tuple-element.56), channel_id=1, source_target_pairs={{0,2},{1,3},{2,0},{3,1},{4,6},{5,7},{6,4},{7,5},{8,10},{9,11},{10,... | collective-permute-start | bytes 1081352 | tf_op jit(solution)/shard_map/ppermute | solution.py:24
  41.6 1.1 %collective-permute-done.16.refs_5_ = bf16[64,2048]{1,0:T(8,128)(2,1)S(1)} collective-permute-done((bf16[64,2048]{1,0:T(8,128)(2,1)S(1)}, bf16[64,2048]{1,0:T(8,128)(2,1)S(1)}, u32[]{:S(2)}, u32[]{:S(2)}) %collective-permute-start.16) | collective-permute-done | bytes 262176 | tf_op jit(solution)/shard_map/ppermute | solution.py:24
  42.7 7.2 %collective-permute-done.8.block_ref.refs_5_ = bf16[256,1024]{1,0:T(8,128)(2,1)S(1)} collective-permute-done((bf16[256,1024]{1,0:T(8,128)(2,1)S(1)}, bf16[256,1024]{1,0:T(8,128)(2,1)S(1)}, u32[]{:S(2)}, u32[]{:S(2)}) %collective-permute-start.8) | collective-permute-done | bytes 524320 | tf_op jit(solution)/shard_map/ppermute | solution.py:24
  50.0 0.9 %collective-permute-done.10.refs_0_ = bf16[176,1024]{1,0:T(8,128)(2,1)S(1)} collective-permute-done((bf16[176,1024]{1,0:T(8,128)(2,1)S(1)}, bf16[176,1024]{1,0:T(8,128)(2,1)S(1)}, u32[]{:S(2)}, u32[]{:S(2)}) %collective-permute-start.10) | collective-permute-done | bytes 360480 | tf_op jit(solution)/shard_map/ppermute | solution.py:24
  50.9 6.9 %collective-permute-done.9.refs_1_ = bf16[176,1024]{1,0:T(8,128)(2,1)S(1)} collective-permute-done((bf16[176,1024]{1,0:T(8,128)(2,1)S(1)}, bf16[176,1024]{1,0:T(8,128)(2,1)S(1)}, u32[]{:S(2)}, u32[]{:S(2)}) %collective-permute-start.9) | collective-permute-done | bytes 360480 | tf_op jit(solution)/shard_map/ppermute | solution.py:24
  58.3 1.3 %shard_map.102 = (f32[64,5120]{1,0:T(8,128)S(1)}, bf16[64,2560]{1,0:T(8,128)(2,1)S(1)}, bf16[64,2560]{1,0:T(8,128)(2,1)S(1)}) custom-call(bf16[176,4096]{1,0:T(8,128)(2,1)S(1)} %bitcast.12, bf16[176,1152]{1,0:T(8,128)(2,1)S(1)} %shard_map.95.refs_0_.refs_1_, bf16[352,128]{1,0:T(8,128)(2,1)S(1)} %get-tuple-element.53.refs_4_.refs_2_, ...), custom_call_target="tpu_custom_call" | custom-call | flops 1000 | bytes 1000 | tf_op jit(solution)/shard_map/pallas_call | solution.py:41
  60.2 1.2 %shard_map.99 = bf16[352,512]{1,0:T(8,128)(2,1)S(1)} custom-call(bf16[176,1152]{1,0:T(8,128)(2,1)S(1)} %shard_map.95.refs_0_.refs_1_, bf16[176,1152]{1,0:T(8,128)(2,1)S(1)} %collective-permute-done.3.refs_1_, bf16[64,2048]{1,0:T(8,128)(2,1)S(1)} %get-tuple-element.50.refs_2_.refs_3_, bf16[64,2048]{1,0:T(8,128)(2,1)S(1)} %collective-permute-done.5.refs_3_.refs_4_, ...), custom_call_target="tpu_custom_call" | custom-call | flops 1000 | bytes 1000 | tf_op jit(solution)/shard_map/pallas_call | solution.py:41
  61.4 1.6 %collective-permute-start.13 = (bf16[352,512]{1,0:T(8,128)(2,1)S(1)}, bf16[352,512]{1,0:T(8,128)(2,1)S(1)}, u32[]{:S(2)}, u32[]{:S(2)}) collective-permute-start(bf16[352,512]{1,0:T(8,128)(2,1)S(1)} %shard_map.99), channel_id=1, source_target_pairs={{0,2},{1,3},{2,0},{3,1},{4,6},{5,7},{6,4},{7,5},{8,10},{9,11},{10,... | collective-permute-start | bytes 1081352 | tf_op jit(solution)/shard_map/ppermute | solution.py:24
  62.9 2.4 %collective-permute-done.15.block_ref.refs_5_ = bf16[256,1024]{1,0:T(8,128)(2,1)S(1)} collective-permute-done((bf16[256,1024]{1,0:T(8,128)(2,1)S(1)}, bf16[256,1024]{1,0:T(8,128)(2,1)S(1)}, u32[]{:S(2)}, u32[]{:S(2)}) %collective-permute-start.15) | collective-permute-done | bytes 524320 | tf_op jit(solution)/shard_map/ppermute | solution.py:24
  66.1 1.7 %collective-permute-start.25 = (bf16[16,5120]{1,0:T(8,128)(2,1)S(1)}, bf16[16,5120]{1,0:T(8,128)(2,1)S(1)}, u32[]{:S(2)}, u32[]{:S(2)}) collective-permute-start(bf16[16,5120]{1,0:T(8,128)(2,1)S(1)} %get-tuple-element.78), channel_id=1, source_target_pairs={{0,8},{1,9},{2,10},{3,11},{4,12},{5,13},{6,14},{7,15},{8,0},{9,1},... | collective-permute-start | bytes 491528 | tf_op jit(solution)/shard_map/ppermute | solution.py:24
  67.8 2.1 %collective-permute-start.24 = (bf16[16,5120]{1,0:T(8,128)(2,1)S(1)}, bf16[16,5120]{1,0:T(8,128)(2,1)S(1)}, u32[]{:S(2)}, u32[]{:S(2)}) collective-permute-start(bf16[16,5120]{1,0:T(8,128)(2,1)S(1)} %get-tuple-element.76), channel_id=1, source_target_pairs={{0,12},{1,13},{2,14},{3,15},{4,0},{5,1},{6,2},{7,3},{8,4},{9,5},{1... | collective-permute-start | bytes 491528 | tf_op jit(solution)/shard_map/ppermute | solution.py:24
  69.9 1.2 %shard_map.104 = (bf16[176,512]{1,0:T(8,128)(2,1)S(1)}, bf16[176,512]{1,0:T(8,128)(2,1)S(1)}) custom-call(bf16[176,1152]{1,0:T(8,128)(2,1)S(1)} %shard_map.95.refs_0_.refs_1_, bf16[176,1152]{1,0:T(8,128)(2,1)S(1)} %collective-permute-done.3.refs_1_, bf16[64,2048]{1,0:T(8,128)(2,1)S(1)} %get-tuple-element.50.refs_2_.refs_3_, ...), custom_call_target="tpu_custom_call" | custom-call | flops 1000 | bytes 1000 | tf_op jit(solution)/shard_map/pallas_call | solution.py:41
  71.1 2.5 %collective-permute-start.22 = (bf16[176,512]{1,0:T(8,128)(2,1)S(1)}, bf16[176,512]{1,0:T(8,128)(2,1)S(1)}, u32[]{:S(2)}, u32[]{:S(2)}) collective-permute-start(bf16[176,512]{1,0:T(8,128)(2,1)S(1)} %get-tuple-element.72), channel_id=1, source_target_pairs={{0,18},{1,19},{2,16},{3,17},{4,22},{5,23},{6,20},{7,21},{8,26},{9,... | collective-permute-start | bytes 540680 | tf_op jit(solution)/shard_map/ppermute | solution.py:24
  74.2 1.2 %shard_map.100.refs_3_ = bf16[176,4096]{1,0:T(8,128)(2,1)} custom-call(bf16[176,1024]{1,0:T(8,128)(2,1)S(1)} %collective-permute-done.10.refs_0_, bf16[176,1024]{1,0:T(8,128)(2,1)S(1)} %collective-permute-done.9.refs_1_, bf16[176,512]{1,0:T(8,128)(2,1)S(1)} %get-tuple-element.86.refs_2_), custom_call_target="tpu_custom_call" | custom-call | flops 1000 | bytes 1000 | tf_op jit(solution)/shard_map/pallas_call | solution.py:41
  75.4 1.2 %collective-permute-start.14 = (bf16[176,512]{1,0:T(8,128)(2,1)S(1)}, bf16[176,512]{1,0:T(8,128)(2,1)S(1)}, u32[]{:S(2)}, u32[]{:S(2)}) collective-permute-start(bf16[176,512]{1,0:T(8,128)(2,1)S(1)} %get-tuple-element.60), channel_id=1, source_target_pairs={{0,16},{1,17},{2,18},{3,19},{4,20},{5,21},{6,22},{7,23},{8,24},{9,... | collective-permute-start | bytes 540680 | tf_op jit(solution)/shard_map/ppermute | solution.py:24
  76.6 4.5 %collective-permute-done.25.refs_2_ = bf16[16,5120]{1,0:T(8,128)(2,1)S(1)} collective-permute-done((bf16[16,5120]{1,0:T(8,128)(2,1)S(1)}, bf16[16,5120]{1,0:T(8,128)(2,1)S(1)}, u32[]{:S(2)}, u32[]{:S(2)}) %collective-permute-start.25) | collective-permute-done | bytes 163872 | tf_op jit(solution)/shard_map/ppermute | solution.py:24
  81.8 0.8 collective-permute-done.27.refs_2_
  83.5 0.8 shard_map.105
  (56 shorter events, 6.5 us)
Async XLA Ops:
  0.6 36.7 %copy-start = (bf16[1,1024,1024]{2,1,0:T(8,128)(2,1)S(1)}, bf16[1,1024,1024]{2,1,0:T(8,128)(2,1)}, u32[]{:S(2)}) copy-start(bf16[1,1024,1024]{2,1,0:T(8,128)(2,1)} %param.11) | copy-start | bytes 6291460
  1.9 32.0 %collective-permute-start.4 = (bf16[256,1024]{1,0:T(8,128)(2,1)S(1)}, bf16[256,1024]{1,0:T(8,128)(2,1)S(1)}, u32[]{:S(2)}, u32[]{:S(2)}) collective-permute-start(bf16[256,1024]{1,0:T(8,128)(2,1)S(1)} %dynamic-slice_bitcast_fusion), channel_id=1, source_target_pairs={{0,4},{1,5},{2,6},{3,7},{4,8},{5,9},{6,10},{7,11},{8,12},{9,13},{1... | collective-permute-start | bytes 1572872 | tf_op jit(solution)/shard_map/ppermute | solution.py:24
  5.0 1.0 %copy-start.2 = (bf16[1,176,1024]{2,1,0:T(8,128)(2,1)S(1)}, bf16[1,176,1024]{2,1,0:T(8,128)(2,1)}, u32[]{:S(2)}) copy-start(bf16[1,176,1024]{2,1,0:T(8,128)(2,1)} %param.8) | copy-start | bytes 1081348
  8.0 25.8 %collective-permute-start.3 = (bf16[176,1152]{1,0:T(8,128)(2,1)S(1)}, bf16[176,1152]{1,0:T(8,128)(2,1)S(1)}, u32[]{:S(2)}, u32[]{:S(2)}) collective-permute-start(bf16[176,1152]{1,0:T(8,128)(2,1)S(1)} %shard_map.95.refs_0_.refs_1_), channel_id=1, source_target_pairs={{0,16},{1,17},{2,18},{3,19},{4,20},{5,21},{6,22},{7,23},{8,24},{9,... | collective-permute-start | bytes 1216520 | tf_op jit(solution)/shard_map/ppermute | solution.py:24
  11.4 9.6 %collective-permute-start = (bf16[16,3072]{1,0:T(8,128)(2,1)S(1)}, bf16[16,3072]{1,0:T(8,128)(2,1)S(1)}, u32[]{:S(2)}, u32[]{:S(2)}) collective-permute-start(bf16[16,3072]{1,0:T(8,128)(2,1)S(1)} %shard_map.94.refs_0_), channel_id=1, source_target_pairs={{0,4},{1,5},{2,6},{3,7},{4,8},{5,9},{6,10},{7,11},{8,12},{9,13},{1... | collective-permute-start | bytes 294920 | tf_op jit(solution)/shard_map/ppermute | solution.py:24
  21.0 6.4 %collective-permute-start.1 = (bf16[16,3072]{1,0:T(8,128)(2,1)S(1)}, bf16[16,3072]{1,0:T(8,128)(2,1)S(1)}, u32[]{:S(2)}, u32[]{:S(2)}) collective-permute-start(bf16[16,3072]{1,0:T(8,128)(2,1)S(1)} %collective-permute-done.refs_1_), channel_id=1, source_target_pairs={{0,4},{1,5},{2,6},{3,7},{4,8},{5,9},{6,10},{7,11},{8,12},{9,13},{1... | collective-permute-start | bytes 294920 | tf_op jit(solution)/shard_map/ppermute | solution.py:24
  27.4 6.4 %collective-permute-start.2 = (bf16[16,3072]{1,0:T(8,128)(2,1)S(1)}, bf16[16,3072]{1,0:T(8,128)(2,1)S(1)}, u32[]{:S(2)}, u32[]{:S(2)}) collective-permute-start(bf16[16,3072]{1,0:T(8,128)(2,1)S(1)} %collective-permute-done.1.refs_2_), channel_id=1, source_target_pairs={{0,4},{1,5},{2,6},{3,7},{4,8},{5,9},{6,10},{7,11},{8,12},{9,13},{1... | collective-permute-start | bytes 294920 | tf_op jit(solution)/shard_map/ppermute | solution.py:24
  33.8 3.5 %collective-permute-start.7 = (bf16[256,1024]{1,0:T(8,128)(2,1)S(1)}, bf16[256,1024]{1,0:T(8,128)(2,1)S(1)}, u32[]{:S(2)}, u32[]{:S(2)}) collective-permute-start(bf16[256,1024]{1,0:T(8,128)(2,1)S(1)} %collective-permute-done.4.refs_7_), channel_id=1, source_target_pairs={{0,1},{1,0},{2,3},{3,2},{4,5},{5,4},{6,7},{7,6},{8,9},{9,8},{10,11... | collective-permute-start | bytes 1572872 | tf_op jit(solution)/shard_map/ppermute | solution.py:24
  33.9 16.1 %collective-permute-start.8 = (bf16[256,1024]{1,0:T(8,128)(2,1)S(1)}, bf16[256,1024]{1,0:T(8,128)(2,1)S(1)}, u32[]{:S(2)}, u32[]{:S(2)}) collective-permute-start(bf16[256,1024]{1,0:T(8,128)(2,1)S(1)} %collective-permute-done.4.refs_7_), channel_id=1, source_target_pairs={{0,4},{1,5},{2,6},{3,7},{4,8},{5,9},{6,10},{7,11},{8,12},{9,13},{1... | collective-permute-start | bytes 1572872 | tf_op jit(solution)/shard_map/ppermute | solution.py:24
  34.0 3.4 %collective-permute-start.5 = (bf16[64,2048]{1,0:T(8,128)(2,1)S(1)}, bf16[64,2048]{1,0:T(8,128)(2,1)S(1)}, u32[]{:S(2)}, u32[]{:S(2)}) collective-permute-start(bf16[64,2048]{1,0:T(8,128)(2,1)S(1)} %get-tuple-element.50.refs_2_.refs_3_), channel_id=1, source_target_pairs={{0,1},{1,0},{2,3},{3,2},{4,5},{5,4},{6,7},{7,6},{8,9},{9,8},{10,11... | collective-permute-start | bytes 786440 | tf_op jit(solution)/shard_map/ppermute | solution.py:24
  34.5 8.3 %collective-permute-start.16 = (bf16[64,2048]{1,0:T(8,128)(2,1)S(1)}, bf16[64,2048]{1,0:T(8,128)(2,1)S(1)}, u32[]{:S(2)}, u32[]{:S(2)}) collective-permute-start(bf16[64,2048]{1,0:T(8,128)(2,1)S(1)} %get-tuple-element.50.refs_2_.refs_3_), channel_id=1, source_target_pairs={{0,16},{1,17},{2,18},{3,19},{4,20},{5,21},{6,22},{7,23},{8,24},{9,... | collective-permute-start | bytes 786440 | tf_op jit(solution)/shard_map/ppermute | solution.py:24
  36.0 1.3 %collective-permute-start.6 = (bf16[64,1024]{1,0:T(8,128)(2,1)S(1)}, bf16[64,1024]{1,0:T(8,128)(2,1)S(1)}, u32[]{:S(2)}, u32[]{:S(2)}) collective-permute-start(bf16[64,1024]{1,0:T(8,128)(2,1)S(1)} %get-tuple-element.51.refs_4_), channel_id=1, source_target_pairs={{0,1},{1,0},{2,3},{3,2},{4,5},{5,4},{6,7},{7,6},{8,9},{9,8},{10,11... | collective-permute-start | bytes 393224 | tf_op jit(solution)/shard_map/ppermute | solution.py:24
  37.3 21.0 %copy-start.1 = (bf16[1,176,4096]{2,1,0:T(8,128)(2,1)S(1)}, bf16[1,176,4096]{2,1,0:T(8,128)(2,1)}, u32[]{:S(2)}) copy-start(bf16[1,176,4096]{2,1,0:T(8,128)(2,1)} %param.7) | copy-start | bytes 4325380
  39.6 11.3 %collective-permute-start.10 = (bf16[176,1024]{1,0:T(8,128)(2,1)S(1)}, bf16[176,1024]{1,0:T(8,128)(2,1)S(1)}, u32[]{:S(2)}, u32[]{:S(2)}) collective-permute-start(bf16[176,1024]{1,0:T(8,128)(2,1)S(1)} %get-tuple-element.56), channel_id=1, source_target_pairs={{0,2},{1,3},{2,0},{3,1},{4,6},{5,7},{6,4},{7,5},{8,10},{9,11},{10,... | collective-permute-start | bytes 1081352 | tf_op jit(solution)/shard_map/ppermute | solution.py:24
  41.1 16.6 %collective-permute-start.9 = (bf16[176,1024]{1,0:T(8,128)(2,1)S(1)}, bf16[176,1024]{1,0:T(8,128)(2,1)S(1)}, u32[]{:S(2)}, u32[]{:S(2)}) collective-permute-start(bf16[176,1024]{1,0:T(8,128)(2,1)S(1)} %get-tuple-element.55), channel_id=1, source_target_pairs={{0,18},{1,19},{2,16},{3,17},{4,22},{5,23},{6,20},{7,21},{8,26},{9,... | collective-permute-start | bytes 1081352 | tf_op jit(solution)/shard_map/ppermute | solution.py:24
  42.7 15.6 %collective-permute-start.17 = (bf16[64,2048]{1,0:T(8,128)(2,1)S(1)}, bf16[64,2048]{1,0:T(8,128)(2,1)S(1)}, u32[]{:S(2)}, u32[]{:S(2)}) collective-permute-start(bf16[64,2048]{1,0:T(8,128)(2,1)S(1)} %collective-permute-done.16.refs_5_), channel_id=1, source_target_pairs={{0,1},{1,0},{2,3},{3,2},{4,5},{5,4},{6,7},{7,6},{8,9},{9,8},{10,11... | collective-permute-start | bytes 786440 | tf_op jit(solution)/shard_map/ppermute | solution.py:24
  50.0 15.3 %collective-permute-start.15 = (bf16[256,1024]{1,0:T(8,128)(2,1)S(1)}, bf16[256,1024]{1,0:T(8,128)(2,1)S(1)}, u32[]{:S(2)}, u32[]{:S(2)}) collective-permute-start(bf16[256,1024]{1,0:T(8,128)(2,1)S(1)} %collective-permute-done.8.block_ref.refs_5_), channel_id=1, source_target_pairs={{0,4},{1,5},{2,6},{3,7},{4,8},{5,9},{6,10},{7,11},{8,12},{9,13},{1... | collective-permute-start | bytes 1572872 | tf_op jit(solution)/shard_map/ppermute | solution.py:24
  57.8 2.4 %collective-permute-start.12 = (bf16[128,1024]{1,0:T(8,128)(2,1)S(1)}, bf16[128,1024]{1,0:T(8,128)(2,1)S(1)}, u32[]{:S(2)}, u32[]{:S(2)}) collective-permute-start(bf16[128,1024]{1,0:T(8,128)(2,1)S(1)} %get-tuple-element.59), channel_id=1, source_target_pairs={{0,1},{1,0},{2,3},{3,2},{4,5},{5,4},{6,7},{7,6},{8,9},{9,8},{10,11... | collective-permute-start | bytes 786440 | tf_op jit(solution)/shard_map/ppermute | solution.py:24
  57.8 2.4 %collective-permute-start.11 = (bf16[128,1024]{1,0:T(8,128)(2,1)S(1)}, bf16[128,1024]{1,0:T(8,128)(2,1)S(1)}, u32[]{:S(2)}, u32[]{:S(2)}) collective-permute-start(bf16[128,1024]{1,0:T(8,128)(2,1)S(1)} %get-tuple-element.57), channel_id=1, source_target_pairs={{0,1},{1,0},{2,3},{3,2},{4,5},{5,4},{6,7},{7,6},{8,9},{9,8},{10,11... | collective-permute-start | bytes 786440 | tf_op jit(solution)/shard_map/ppermute | solution.py:24
  59.6 5.7 %collective-permute-start.19 = (bf16[64,2560]{1,0:T(8,128)(2,1)S(1)}, bf16[64,2560]{1,0:T(8,128)(2,1)S(1)}, u32[]{:S(2)}, u32[]{:S(2)}) collective-permute-start(bf16[64,2560]{1,0:T(8,128)(2,1)S(1)} %get-tuple-element.67), channel_id=1, source_target_pairs={{0,1},{1,0},{2,3},{3,2},{4,5},{5,4},{6,7},{7,6},{8,9},{9,8},{10,11... | collective-permute-start | bytes 983048 | tf_op jit(solution)/shard_map/ppermute | solution.py:24
  59.7 5.7 %collective-permute-start.18 = (bf16[64,2560]{1,0:T(8,128)(2,1)S(1)}, bf16[64,2560]{1,0:T(8,128)(2,1)S(1)}, u32[]{:S(2)}, u32[]{:S(2)}) collective-permute-start(bf16[64,2560]{1,0:T(8,128)(2,1)S(1)} %get-tuple-element.65), channel_id=1, source_target_pairs={{0,1},{1,0},{2,3},{3,2},{4,5},{5,4},{6,7},{7,6},{8,9},{9,8},{10,11... | collective-permute-start | bytes 983048 | tf_op jit(solution)/shard_map/ppermute | solution.py:24
  61.4 12.2 %collective-permute-start.13 = (bf16[352,512]{1,0:T(8,128)(2,1)S(1)}, bf16[352,512]{1,0:T(8,128)(2,1)S(1)}, u32[]{:S(2)}, u32[]{:S(2)}) collective-permute-start(bf16[352,512]{1,0:T(8,128)(2,1)S(1)} %shard_map.99), channel_id=1, source_target_pairs={{0,2},{1,3},{2,0},{3,1},{4,6},{5,7},{6,4},{7,5},{8,10},{9,11},{10,... | collective-permute-start | bytes 1081352 | tf_op jit(solution)/shard_map/ppermute | solution.py:24
  65.5 2.3 %collective-permute-start.21 = (bf16[128,1024]{1,0:T(8,128)(2,1)S(1)}, bf16[128,1024]{1,0:T(8,128)(2,1)S(1)}, u32[]{:S(2)}, u32[]{:S(2)}) collective-permute-start(bf16[128,1024]{1,0:T(8,128)(2,1)S(1)} %get-tuple-element.71), channel_id=1, source_target_pairs={{0,1},{1,0},{2,3},{3,2},{4,5},{5,4},{6,7},{7,6},{8,9},{9,8},{10,11... | collective-permute-start | bytes 786440 | tf_op jit(solution)/shard_map/ppermute | solution.py:24
  65.6 4.3 %collective-permute-start.20 = (bf16[128,1024]{1,0:T(8,128)(2,1)S(1)}, bf16[128,1024]{1,0:T(8,128)(2,1)S(1)}, u32[]{:S(2)}, u32[]{:S(2)}) collective-permute-start(bf16[128,1024]{1,0:T(8,128)(2,1)S(1)} %get-tuple-element.69), channel_id=1, source_target_pairs={{0,1},{1,0},{2,3},{3,2},{4,5},{5,4},{6,7},{7,6},{8,9},{9,8},{10,11... | collective-permute-start | bytes 786440 | tf_op jit(solution)/shard_map/ppermute | solution.py:24
  66.1 9.3 %collective-permute-start.26 = (bf16[16,5120]{1,0:T(8,128)(2,1)S(1)}, bf16[16,5120]{1,0:T(8,128)(2,1)S(1)}, u32[]{:S(2)}, u32[]{:S(2)}) collective-permute-start(bf16[16,5120]{1,0:T(8,128)(2,1)S(1)} %get-tuple-element.80), channel_id=1, source_target_pairs={{0,4},{1,5},{2,6},{3,7},{4,8},{5,9},{6,10},{7,11},{8,12},{9,13},{1... | collective-permute-start | bytes 491528 | tf_op jit(solution)/shard_map/ppermute | solution.py:24
  66.1 15.0 %collective-permute-start.25 = (bf16[16,5120]{1,0:T(8,128)(2,1)S(1)}, bf16[16,5120]{1,0:T(8,128)(2,1)S(1)}, u32[]{:S(2)}, u32[]{:S(2)}) collective-permute-start(bf16[16,5120]{1,0:T(8,128)(2,1)S(1)} %get-tuple-element.78), channel_id=1, source_target_pairs={{0,8},{1,9},{2,10},{3,11},{4,12},{5,13},{6,14},{7,15},{8,0},{9,1},... | collective-permute-start | bytes 491528 | tf_op jit(solution)/shard_map/ppermute | solution.py:24
  67.8 13.3 %collective-permute-start.24 = (bf16[16,5120]{1,0:T(8,128)(2,1)S(1)}, bf16[16,5120]{1,0:T(8,128)(2,1)S(1)}, u32[]{:S(2)}, u32[]{:S(2)}) collective-permute-start(bf16[16,5120]{1,0:T(8,128)(2,1)S(1)} %get-tuple-element.76), channel_id=1, source_target_pairs={{0,12},{1,13},{2,14},{3,15},{4,0},{5,1},{6,2},{7,3},{8,4},{9,5},{1... | collective-permute-start | bytes 491528 | tf_op jit(solution)/shard_map/ppermute | solution.py:24
  71.1 12.4 %collective-permute-start.22 = (bf16[176,512]{1,0:T(8,128)(2,1)S(1)}, bf16[176,512]{1,0:T(8,128)(2,1)S(1)}, u32[]{:S(2)}, u32[]{:S(2)}) collective-permute-start(bf16[176,512]{1,0:T(8,128)(2,1)S(1)} %get-tuple-element.72), channel_id=1, source_target_pairs={{0,18},{1,19},{2,16},{3,17},{4,22},{5,23},{6,20},{7,21},{8,26},{9,... | collective-permute-start | bytes 540680 | tf_op jit(solution)/shard_map/ppermute | solution.py:24
  73.6 9.9 %collective-permute-start.23 = (bf16[176,512]{1,0:T(8,128)(2,1)S(1)}, bf16[176,512]{1,0:T(8,128)(2,1)S(1)}, u32[]{:S(2)}, u32[]{:S(2)}) collective-permute-start(bf16[176,512]{1,0:T(8,128)(2,1)S(1)} %get-tuple-element.73), channel_id=1, source_target_pairs={{0,2},{1,3},{2,0},{3,1},{4,6},{5,7},{6,4},{7,5},{8,10},{9,11},{10,... | collective-permute-start | bytes 540680 | tf_op jit(solution)/shard_map/ppermute | solution.py:24
  75.4 8.1 %collective-permute-start.14 = (bf16[176,512]{1,0:T(8,128)(2,1)S(1)}, bf16[176,512]{1,0:T(8,128)(2,1)S(1)}, u32[]{:S(2)}, u32[]{:S(2)}) collective-permute-start(bf16[176,512]{1,0:T(8,128)(2,1)S(1)} %get-tuple-element.60), channel_id=1, source_target_pairs={{0,16},{1,17},{2,18},{3,19},{4,20},{5,21},{6,22},{7,23},{8,24},{9,... | collective-permute-start | bytes 540680 | tf_op jit(solution)/shard_map/ppermute | solution.py:24
  81.2 1.3 %collective-permute-start.27 = (bf16[16,2560]{1,0:T(8,128)(2,1)S(1)}, bf16[16,2560]{1,0:T(8,128)(2,1)S(1)}, u32[]{:S(2)}, u32[]{:S(2)}) collective-permute-start(bf16[16,2560]{1,0:T(8,128)(2,1)S(1)} %get-tuple-element.81.refs_0_), channel_id=1, source_target_pairs={{0,1},{1,0},{2,3},{3,2},{4,5},{5,4},{6,7},{7,6},{8,9},{9,8},{10,11... | collective-permute-start | bytes 245768 | tf_op jit(solution)/shard_map/ppermute | solution.py:24
  81.3 1.4 %collective-permute-start.28 = (bf16[16,2560]{1,0:T(8,128)(2,1)S(1)}, bf16[16,2560]{1,0:T(8,128)(2,1)S(1)}, u32[]{:S(2)}, u32[]{:S(2)}) collective-permute-start(bf16[16,2560]{1,0:T(8,128)(2,1)S(1)} %get-tuple-element.82.refs_1_), channel_id=1, source_target_pairs={{0,1},{1,0},{2,3},{3,2},{4,5},{5,4},{6,7},{7,6},{8,9},{9,8},{10,11... | collective-permute-start | bytes 245768 | tf_op jit(solution)/shard_map/ppermute | solution.py:24
  (4 other events, 3.1 us)

commit v20 on v17

--- a/solution.py
+++ b/solution.py
@@ -371,8 +371,12 @@
         operands, specs = [], []
         for k in batch:
             if k > 1:
-                last = after(ring[-1], sel) if k > 2 else ring[-1]
-                ring.append(moved(last, lambda g, z, s, r: (g, z + 1, s, r)))
+                if 2 < k == holders - 1:
+                    last = moved(after(ring[0], sel), lambda g, z, s, r: (g, z - 1, s, r))
+                else:
+                    last = after(ring[-1], sel) if k > 2 else ring[-1]
+                    last = moved(last, lambda g, z, s, r: (g, z + 1, s, r))
+                ring.append(last)
             gate = arrived[0][::-1] if k == 2 else [*arrived[i - 2], chip[0]] if k > 2 else []
             spec, blocks = pieces_of(k, *gate)
             specs.append((k, spec))

time: 77 us -> 77 us (level)
  waiting for transfers between devices: 29 us -> 28 us
  starting transfers between devices: 31.2 us -> 32.1 us
    ppermute x29, waiting for transfers between devices: 29 us -> 28 us  [moved(): return lax.ppermute(x, AXES, pairs)]
    ppermute x29, starting transfers between devices: 31.2 us -> 32.1 us  [moved(): return lax.ppermute(x, AXES, pairs)]
  transfers between devices with their start and end apart: 29 -> 29, of which waited for: 12 -> 11; matrix products, arithmetic and copies ran while one was open for 0% -> 0% of each run, Pallas kernels for 12% -> 12%
where the time goes in v20:
time: 77 us; the launch traced here: 76 us
  starting transfers between devices  32.1 us (42%)
  waiting for transfers between devices  28 us (36%)
  Pallas kernels  9.75 us (13%)
  local copies, waits for them, and re-layouts  5.37 us (7%)
  between operations  0.8 us (1%)
    ppermute x29, starting transfers between devices, moved(): return lax.ppermute(x, AXES, pairs)  32.1 us
    ppermute x29, waiting for transfers between devices, moved(): return lax.ppermute(x, AXES, pairs)  28 us
    pallas_call x13, Pallas kernels, call(): pl.pallas_call(kernel, out_shape=out_shape, in_specs=[pl.BlockSpec(memory...  8.92 us
    unnamed x14, local copies, waits for them, and re-layouts  4.12 us
  transfers between devices with their start and end apart: 29, of which 11 were waited for; matrix products, arithmetic and copies ran while one was open for 0% of the time, Pallas kernels for 12%

profile of v20, /device:TPU:0, one launch (start us, length us, event | category | flops | bytes accessed | tf_op | source)
XLA Modules:
  0.0 76.0 jit_solution(16869469661178903897)
XLA Ops:
  0.6 1.2 %dynamic-slice_bitcast_fusion = bf16[256,1024]{1,0:T(8,128)(2,1)S(1)} fusion(bf16[1,1024,1024]{2,1,0:T(8,128)(2,1)} %param.11, s32[]{:T(128)S(6)} %select_n.3), kind=kLoop, calls=%fused_computation | loop fusion | bytes 1048580 | tf_op jit(solution)/shard_map/dynamic_slice | solution.py:303
  1.9 3.1 %collective-permute-start.4 = (bf16[256,1024]{1,0:T(8,128)(2,1)S(1)}, bf16[256,1024]{1,0:T(8,128)(2,1)S(1)}, u32[]{:S(2)}, u32[]{:S(2)}) collective-permute-start(bf16[256,1024]{1,0:T(8,128)(2,1)S(1)} %dynamic-slice_bitcast_fusion), channel_id=1, source_target_pairs={{0,4},{1,5},{2,6},{3,7},{4,8},{5,9},{6,10},{7,11},{8,12},{9,13},{1... | collective-permute-start | bytes 1572872 | tf_op jit(solution)/shard_map/ppermute | solution.py:24
  5.0 1.0 %copy-done.2 = bf16[1,176,1024]{2,1,0:T(8,128)(2,1)S(1)} copy-done((bf16[1,176,1024]{2,1,0:T(8,128)(2,1)S(1)}, bf16[1,176,1024]{2,1,0:T(8,128)(2,1)}, u32[]{:S(2)}) %copy-start.2) | copy-done | bytes 360472
  8.0 1.6 %collective-permute-start.3 = (bf16[176,1152]{1,0:T(8,128)(2,1)S(1)}, bf16[176,1152]{1,0:T(8,128)(2,1)S(1)}, u32[]{:S(2)}, u32[]{:S(2)}) collective-permute-start(bf16[176,1152]{1,0:T(8,128)(2,1)S(1)} %shard_map.95.refs_0_.refs_1_), channel_id=1, source_target_pairs={{0,16},{1,17},{2,18},{3,19},{4,20},{5,21},{6,22},{7,23},{8,24},{9,... | collective-permute-start | bytes 1216520 | tf_op jit(solution)/shard_map/ppermute | solution.py:24
  9.6 0.9 %copy-done.3 = bf16[1,2,16,4096]{3,2,1,0:T(8,128)(2,1)S(1)} copy-done((bf16[1,2,16,4096]{3,2,1,0:T(8,128)(2,1)S(1)}, bf16[1,2,16,4096]{3,2,1,0:T(8,128)(2,1)}, u32[]{:S(2)}) %copy-start.3) | copy-done | bytes 262168
  10.6 0.8 %copy-done.4 = bf16[1,2,16,1024]{3,2,1,0:T(8,128)(2,1)S(1)} copy-done((bf16[1,2,16,1024]{3,2,1,0:T(8,128)(2,1)S(1)}, bf16[1,2,16,1024]{3,2,1,0:T(8,128)(2,1)}, u32[]{:S(2)}) %copy-start.4) | copy-done | bytes 65560
  11.4 1.6 %collective-permute-start = (bf16[16,3072]{1,0:T(8,128)(2,1)S(1)}, bf16[16,3072]{1,0:T(8,128)(2,1)S(1)}, u32[]{:S(2)}, u32[]{:S(2)}) collective-permute-start(bf16[16,3072]{1,0:T(8,128)(2,1)S(1)} %shard_map.94.refs_0_), channel_id=1, source_target_pairs={{0,4},{1,5},{2,6},{3,7},{4,8},{5,9},{6,10},{7,11},{8,12},{9,13},{1... | collective-permute-start | bytes 294920 | tf_op jit(solution)/shard_map/ppermute | solution.py:24
  13.1 1.2 %collective-permute-start.1 = (bf16[16,3072]{1,0:T(8,128)(2,1)S(1)}, bf16[16,3072]{1,0:T(8,128)(2,1)S(1)}, u32[]{:S(2)}, u32[]{:S(2)}) collective-permute-start(bf16[16,3072]{1,0:T(8,128)(2,1)S(1)} %shard_map.94.refs_0_), channel_id=1, source_target_pairs={{0,8},{1,9},{2,10},{3,11},{4,12},{5,13},{6,14},{7,15},{8,0},{9,1},... | collective-permute-start | bytes 294920 | tf_op jit(solution)/shard_map/ppermute | solution.py:24
  14.3 2.7 %collective-permute-start.2 = (bf16[16,3072]{1,0:T(8,128)(2,1)S(1)}, bf16[16,3072]{1,0:T(8,128)(2,1)S(1)}, u32[]{:S(2)}, u32[]{:S(2)}) collective-permute-start(bf16[16,3072]{1,0:T(8,128)(2,1)S(1)} %shard_map.94.refs_0_), channel_id=1, source_target_pairs={{0,12},{1,13},{2,14},{3,15},{4,0},{5,1},{6,2},{7,3},{8,4},{9,5},{1... | collective-permute-start | bytes 294920 | tf_op jit(solution)/shard_map/ppermute | solution.py:24
  17.0 5.0 %collective-permute-done.refs_1_ = bf16[16,3072]{1,0:T(8,128)(2,1)S(1)} collective-permute-done((bf16[16,3072]{1,0:T(8,128)(2,1)S(1)}, bf16[16,3072]{1,0:T(8,128)(2,1)S(1)}, u32[]{:S(2)}, u32[]{:S(2)}) %collective-permute-start) | collective-permute-done | bytes 98336 | tf_op jit(solution)/shard_map/ppermute | solution.py:24
  22.0 3.4 %collective-permute-done.1.refs_2_ = bf16[16,3072]{1,0:T(8,128)(2,1)S(1)} collective-permute-done((bf16[16,3072]{1,0:T(8,128)(2,1)S(1)}, bf16[16,3072]{1,0:T(8,128)(2,1)S(1)}, u32[]{:S(2)}, u32[]{:S(2)}) %collective-permute-start.1) | collective-permute-done | bytes 98336 | tf_op jit(solution)/shard_map/ppermute | solution.py:24
  26.0 2.5 %collective-permute-start.8 = (bf16[256,1024]{1,0:T(8,128)(2,1)S(1)}, bf16[256,1024]{1,0:T(8,128)(2,1)S(1)}, u32[]{:S(2)}, u32[]{:S(2)}) collective-permute-start(bf16[256,1024]{1,0:T(8,128)(2,1)S(1)} %collective-permute-done.4.refs_7_), channel_id=1, source_target_pairs={{0,4},{1,5},{2,6},{3,7},{4,8},{5,9},{6,10},{7,11},{8,12},{9,13},{1... | collective-permute-start | bytes 1572872 | tf_op jit(solution)/shard_map/ppermute | solution.py:24
  28.5 1.5 %collective-permute-start.16 = (bf16[64,2048]{1,0:T(8,128)(2,1)S(1)}, bf16[64,2048]{1,0:T(8,128)(2,1)S(1)}, u32[]{:S(2)}, u32[]{:S(2)}) collective-permute-start(bf16[64,2048]{1,0:T(8,128)(2,1)S(1)} %get-tuple-element.51.refs_2_.refs_3_), channel_id=1, source_target_pairs={{0,16},{1,17},{2,18},{3,19},{4,20},{5,21},{6,22},{7,23},{8,24},{9,... | collective-permute-start | bytes 786440 | tf_op jit(solution)/shard_map/ppermute | solution.py:24
  30.1 1.3 %collective-permute-done.6.refs_5_ = bf16[64,1024]{1,0:T(8,128)(2,1)S(1)} collective-permute-done((bf16[64,1024]{1,0:T(8,128)(2,1)S(1)}, bf16[64,1024]{1,0:T(8,128)(2,1)S(1)}, u32[]{:S(2)}, u32[]{:S(2)}) %collective-permute-start.6) | collective-permute-done | bytes 131104 | tf_op jit(solution)/shard_map/ppermute | solution.py:24
  31.4 2.2 %shard_map.97 = (bf16[176,1024]{1,0:T(8,128)(2,1)S(1)}, bf16[176,1024]{1,0:T(8,128)(2,1)S(1)}, bf16[352,128]{1,0:T(8,128)(2,1)S(1)}) custom-call(bf16[176,1152]{1,0:T(8,128)(2,1)S(1)} %shard_map.95.refs_0_.refs_1_, bf16[176,1152]{1,0:T(8,128)(2,1)S(1)} %collective-permute-done.3.refs_1_, bf16[64,2048]{1,0:T(8,128)(2,1)S(1)} %get-tuple-element.51.refs_2_.refs_3_, ...), custom_call_target="tpu_custom_call" | custom-call | flops 1000 | bytes 1000 | tf_op jit(solution)/shard_map/pallas_call | solution.py:41
  33.7 1.6 %collective-permute-start.10 = (bf16[176,1024]{1,0:T(8,128)(2,1)S(1)}, bf16[176,1024]{1,0:T(8,128)(2,1)S(1)}, u32[]{:S(2)}, u32[]{:S(2)}) collective-permute-start(bf16[176,1024]{1,0:T(8,128)(2,1)S(1)} %get-tuple-element.57), channel_id=1, source_target_pairs={{0,2},{1,3},{2,0},{3,1},{4,6},{5,7},{6,4},{7,5},{8,10},{9,11},{10,... | collective-permute-start | bytes 1081352 | tf_op jit(solution)/shard_map/ppermute | solution.py:24
  36.5 1.4 %collective-permute-start.15 = (bf16[256,1024]{1,0:T(8,128)(2,1)S(1)}, bf16[256,1024]{1,0:T(8,128)(2,1)S(1)}, u32[]{:S(2)}, u32[]{:S(2)}) collective-permute-start(bf16[256,1024]{1,0:T(8,128)(2,1)S(1)} %dynamic-slice_bitcast_fusion), channel_id=1, source_target_pairs={{0,12},{1,13},{2,14},{3,15},{4,0},{5,1},{6,2},{7,3},{8,4},{9,5},{1... | collective-permute-start | bytes 1572872 | tf_op jit(solution)/shard_map/ppermute | solution.py:24
  38.0 4.6 %collective-permute-done.8.block_ref.refs_5_ = bf16[256,1024]{1,0:T(8,128)(2,1)S(1)} collective-permute-done((bf16[256,1024]{1,0:T(8,128)(2,1)S(1)}, bf16[256,1024]{1,0:T(8,128)(2,1)S(1)}, u32[]{:S(2)}, u32[]{:S(2)}) %collective-permute-start.8) | collective-permute-done | bytes 524320 | tf_op jit(solution)/shard_map/ppermute | solution.py:24
  42.7 2.4 %collective-permute-done.10.refs_0_ = bf16[176,1024]{1,0:T(8,128)(2,1)S(1)} collective-permute-done((bf16[176,1024]{1,0:T(8,128)(2,1)S(1)}, bf16[176,1024]{1,0:T(8,128)(2,1)S(1)}, u32[]{:S(2)}, u32[]{:S(2)}) %collective-permute-start.10) | collective-permute-done | bytes 360480 | tf_op jit(solution)/shard_map/ppermute | solution.py:24
  45.0 6.9 %collective-permute-done.9.refs_1_ = bf16[176,1024]{1,0:T(8,128)(2,1)S(1)} collective-permute-done((bf16[176,1024]{1,0:T(8,128)(2,1)S(1)}, bf16[176,1024]{1,0:T(8,128)(2,1)S(1)}, u32[]{:S(2)}, u32[]{:S(2)}) %collective-permute-start.9) | collective-permute-done | bytes 360480 | tf_op jit(solution)/shard_map/ppermute | solution.py:24
  52.4 1.3 %shard_map.102 = (f32[64,5120]{1,0:T(8,128)S(1)}, bf16[64,2560]{1,0:T(8,128)(2,1)S(1)}, bf16[64,2560]{1,0:T(8,128)(2,1)S(1)}) custom-call(bf16[176,4096]{1,0:T(8,128)(2,1)S(1)} %bitcast.12, bf16[176,1152]{1,0:T(8,128)(2,1)S(1)} %shard_map.95.refs_0_.refs_1_, bf16[352,128]{1,0:T(8,128)(2,1)S(1)} %get-tuple-element.54.refs_4_.refs_2_, ...), custom_call_target="tpu_custom_call" | custom-call | flops 1000 | bytes 1000 | tf_op jit(solution)/shard_map/pallas_call | solution.py:41
  54.3 1.2 %shard_map.99 = bf16[352,512]{1,0:T(8,128)(2,1)S(1)} custom-call(bf16[176,1152]{1,0:T(8,128)(2,1)S(1)} %shard_map.95.refs_0_.refs_1_, bf16[176,1152]{1,0:T(8,128)(2,1)S(1)} %collective-permute-done.3.refs_1_, bf16[64,2048]{1,0:T(8,128)(2,1)S(1)} %get-tuple-element.51.refs_2_.refs_3_, bf16[64,2048]{1,0:T(8,128)(2,1)S(1)} %collective-permute-done.5.refs_3_.refs_4_, ...), custom_call_target="tpu_custom_call" | custom-call | flops 1000 | bytes 1000 | tf_op jit(solution)/shard_map/pallas_call | solution.py:41
  55.5 1.6 %collective-permute-start.13 = (bf16[352,512]{1,0:T(8,128)(2,1)S(1)}, bf16[352,512]{1,0:T(8,128)(2,1)S(1)}, u32[]{:S(2)}, u32[]{:S(2)}) collective-permute-start(bf16[352,512]{1,0:T(8,128)(2,1)S(1)} %shard_map.99), channel_id=1, source_target_pairs={{0,2},{1,3},{2,0},{3,1},{4,6},{5,7},{6,4},{7,5},{8,10},{9,11},{10,... | collective-permute-start | bytes 1081352 | tf_op jit(solution)/shard_map/ppermute | solution.py:24
  57.8 1.9 %collective-permute-start.25 = (bf16[16,5120]{1,0:T(8,128)(2,1)S(1)}, bf16[16,5120]{1,0:T(8,128)(2,1)S(1)}, u32[]{:S(2)}, u32[]{:S(2)}) collective-permute-start(bf16[16,5120]{1,0:T(8,128)(2,1)S(1)} %get-tuple-element.80), channel_id=1, source_target_pairs={{0,8},{1,9},{2,10},{3,11},{4,12},{5,13},{6,14},{7,15},{8,0},{9,1},... | collective-permute-start | bytes 491528 | tf_op jit(solution)/shard_map/ppermute | solution.py:24
  59.7 2.7 %collective-permute-start.24 = (bf16[16,5120]{1,0:T(8,128)(2,1)S(1)}, bf16[16,5120]{1,0:T(8,128)(2,1)S(1)}, u32[]{:S(2)}, u32[]{:S(2)}) collective-permute-start(bf16[16,5120]{1,0:T(8,128)(2,1)S(1)} %get-tuple-element.78), channel_id=1, source_target_pairs={{0,12},{1,13},{2,14},{3,15},{4,0},{5,1},{6,2},{7,3},{8,4},{9,5},{1... | collective-permute-start | bytes 491528 | tf_op jit(solution)/shard_map/ppermute | solution.py:24
  62.4 1.2 %shard_map.104 = (bf16[176,512]{1,0:T(8,128)(2,1)S(1)}, bf16[176,512]{1,0:T(8,128)(2,1)S(1)}) custom-call(bf16[176,1152]{1,0:T(8,128)(2,1)S(1)} %shard_map.95.refs_0_.refs_1_, bf16[176,1152]{1,0:T(8,128)(2,1)S(1)} %collective-permute-done.3.refs_1_, bf16[64,2048]{1,0:T(8,128)(2,1)S(1)} %get-tuple-element.51.refs_2_.refs_3_, ...), custom_call_target="tpu_custom_call" | custom-call | flops 1000 | bytes 1000 | tf_op jit(solution)/shard_map/pallas_call | solution.py:41
  63.6 1.6 %collective-permute-start.22 = (bf16[176,512]{1,0:T(8,128)(2,1)S(1)}, bf16[176,512]{1,0:T(8,128)(2,1)S(1)}, u32[]{:S(2)}, u32[]{:S(2)}) collective-permute-start(bf16[176,512]{1,0:T(8,128)(2,1)S(1)} %get-tuple-element.74), channel_id=1, source_target_pairs={{0,18},{1,19},{2,16},{3,17},{4,22},{5,23},{6,20},{7,21},{8,26},{9,... | collective-permute-start | bytes 540680 | tf_op jit(solution)/shard_map/ppermute | solution.py:24
  65.9 1.9 %collective-permute-start.23 = (bf16[176,512]{1,0:T(8,128)(2,1)S(1)}, bf16[176,512]{1,0:T(8,128)(2,1)S(1)}, u32[]{:S(2)}, u32[]{:S(2)}) collective-permute-start(bf16[176,512]{1,0:T(8,128)(2,1)S(1)} %get-tuple-element.75), channel_id=1, source_target_pairs={{0,2},{1,3},{2,0},{3,1},{4,6},{5,7},{6,4},{7,5},{8,10},{9,11},{10,... | collective-permute-start | bytes 540680 | tf_op jit(solution)/shard_map/ppermute | solution.py:24
  67.8 1.2 %shard_map.100.refs_3_ = bf16[176,4096]{1,0:T(8,128)(2,1)} custom-call(bf16[176,1024]{1,0:T(8,128)(2,1)S(1)} %collective-permute-done.10.refs_0_, bf16[176,1024]{1,0:T(8,128)(2,1)S(1)} %collective-permute-done.9.refs_1_, bf16[176,512]{1,0:T(8,128)(2,1)S(1)} %get-tuple-element.88.refs_2_), custom_call_target="tpu_custom_call" | custom-call | flops 1000 | bytes 1000 | tf_op jit(solution)/shard_map/pallas_call | solution.py:41
  69.0 2.0 %collective-permute-start.14 = (bf16[176,512]{1,0:T(8,128)(2,1)S(1)}, bf16[176,512]{1,0:T(8,128)(2,1)S(1)}, u32[]{:S(2)}, u32[]{:S(2)}) collective-permute-start(bf16[176,512]{1,0:T(8,128)(2,1)S(1)} %get-tuple-element.61), channel_id=1, source_target_pairs={{0,16},{1,17},{2,18},{3,19},{4,20},{5,21},{6,22},{7,23},{8,24},{9,... | collective-permute-start | bytes 540680 | tf_op jit(solution)/shard_map/ppermute | solution.py:24
  71.0 1.8 %collective-permute-done.25.refs_2_ = bf16[16,5120]{1,0:T(8,128)(2,1)S(1)} collective-permute-done((bf16[16,5120]{1,0:T(8,128)(2,1)S(1)}, bf16[16,5120]{1,0:T(8,128)(2,1)S(1)}, u32[]{:S(2)}, u32[]{:S(2)}) %collective-permute-start.25) | collective-permute-done | bytes 163872 | tf_op jit(solution)/shard_map/ppermute | solution.py:24
  75.2 0.8 %shard_map.105 = bf16[176,4096]{1,0:T(8,128)(2,1)} custom-call(bf16[176,512]{1,0:T(8,128)(2,1)S(1)} %collective-permute-done.14.refs_0_, bf16[176,512]{1,0:T(8,128)(2,1)S(1)} %collective-permute-done.22.refs_1_, bf16[176,512]{1,0:T(8,128)(2,1)S(1)} %collective-permute-done.23.refs_2_, ...), custom_call_target="tpu_custom_call", output_to_operand_aliasing={{}: (3, {})} | custom-call | flops 1000 | bytes 1000 | tf_op jit(solution)/shard_map/pallas_call | solution.py:426
  (56 shorter events, 9.2 us)
Async XLA Ops:
  0.6 30.8 %copy-start = (bf16[1,1024,1024]{2,1,0:T(8,128)(2,1)S(1)}, bf16[1,1024,1024]{2,1,0:T(8,128)(2,1)}, u32[]{:S(2)}) copy-start(bf16[1,1024,1024]{2,1,0:T(8,128)(2,1)} %param.11) | copy-start | bytes 6291460
  1.9 23.5 %collective-permute-start.4 = (bf16[256,1024]{1,0:T(8,128)(2,1)S(1)}, bf16[256,1024]{1,0:T(8,128)(2,1)S(1)}, u32[]{:S(2)}, u32[]{:S(2)}) collective-permute-start(bf16[256,1024]{1,0:T(8,128)(2,1)S(1)} %dynamic-slice_bitcast_fusion), channel_id=1, source_target_pairs={{0,4},{1,5},{2,6},{3,7},{4,8},{5,9},{6,10},{7,11},{8,12},{9,13},{1... | collective-permute-start | bytes 1572872 | tf_op jit(solution)/shard_map/ppermute | solution.py:24
  5.0 1.0 %copy-start.2 = (bf16[1,176,1024]{2,1,0:T(8,128)(2,1)S(1)}, bf16[1,176,1024]{2,1,0:T(8,128)(2,1)}, u32[]{:S(2)}) copy-start(bf16[1,176,1024]{2,1,0:T(8,128)(2,1)} %param.8) | copy-start | bytes 1081348
  8.0 17.3 %collective-permute-start.3 = (bf16[176,1152]{1,0:T(8,128)(2,1)S(1)}, bf16[176,1152]{1,0:T(8,128)(2,1)S(1)}, u32[]{:S(2)}, u32[]{:S(2)}) collective-permute-start(bf16[176,1152]{1,0:T(8,128)(2,1)S(1)} %shard_map.95.refs_0_.refs_1_), channel_id=1, source_target_pairs={{0,16},{1,17},{2,18},{3,19},{4,20},{5,21},{6,22},{7,23},{8,24},{9,... | collective-permute-start | bytes 1216520 | tf_op jit(solution)/shard_map/ppermute | solution.py:24
  11.4 10.5 %collective-permute-start = (bf16[16,3072]{1,0:T(8,128)(2,1)S(1)}, bf16[16,3072]{1,0:T(8,128)(2,1)S(1)}, u32[]{:S(2)}, u32[]{:S(2)}) collective-permute-start(bf16[16,3072]{1,0:T(8,128)(2,1)S(1)} %shard_map.94.refs_0_), channel_id=1, source_target_pairs={{0,4},{1,5},{2,6},{3,7},{4,8},{5,9},{6,10},{7,11},{8,12},{9,13},{1... | collective-permute-start | bytes 294920 | tf_op jit(solution)/shard_map/ppermute | solution.py:24
  13.1 12.3 %collective-permute-start.1 = (bf16[16,3072]{1,0:T(8,128)(2,1)S(1)}, bf16[16,3072]{1,0:T(8,128)(2,1)S(1)}, u32[]{:S(2)}, u32[]{:S(2)}) collective-permute-start(bf16[16,3072]{1,0:T(8,128)(2,1)S(1)} %shard_map.94.refs_0_), channel_id=1, source_target_pairs={{0,8},{1,9},{2,10},{3,11},{4,12},{5,13},{6,14},{7,15},{8,0},{9,1},... | collective-permute-start | bytes 294920 | tf_op jit(solution)/shard_map/ppermute | solution.py:24
  14.3 11.1 %collective-permute-start.2 = (bf16[16,3072]{1,0:T(8,128)(2,1)S(1)}, bf16[16,3072]{1,0:T(8,128)(2,1)S(1)}, u32[]{:S(2)}, u32[]{:S(2)}) collective-permute-start(bf16[16,3072]{1,0:T(8,128)(2,1)S(1)} %shard_map.94.refs_0_), channel_id=1, source_target_pairs={{0,12},{1,13},{2,14},{3,15},{4,0},{5,1},{6,2},{7,3},{8,4},{9,5},{1... | collective-permute-start | bytes 294920 | tf_op jit(solution)/shard_map/ppermute | solution.py:24
  25.4 6.1 %collective-permute-start.7 = (bf16[256,1024]{1,0:T(8,128)(2,1)S(1)}, bf16[256,1024]{1,0:T(8,128)(2,1)S(1)}, u32[]{:S(2)}, u32[]{:S(2)}) collective-permute-start(bf16[256,1024]{1,0:T(8,128)(2,1)S(1)} %collective-permute-done.4.refs_7_), channel_id=1, source_target_pairs={{0,1},{1,0},{2,3},{3,2},{4,5},{5,4},{6,7},{7,6},{8,9},{9,8},{10,11... | collective-permute-start | bytes 1572872 | tf_op jit(solution)/shard_map/ppermute | solution.py:24
  25.5 5.9 %collective-permute-start.5 = (bf16[64,2048]{1,0:T(8,128)(2,1)S(1)}, bf16[64,2048]{1,0:T(8,128)(2,1)S(1)}, u32[]{:S(2)}, u32[]{:S(2)}) collective-permute-start(bf16[64,2048]{1,0:T(8,128)(2,1)S(1)} %get-tuple-element.51.refs_2_.refs_3_), channel_id=1, source_target_pairs={{0,1},{1,0},{2,3},{3,2},{4,5},{5,4},{6,7},{7,6},{8,9},{9,8},{10,11... | collective-permute-start | bytes 786440 | tf_op jit(solution)/shard_map/ppermute | solution.py:24
  26.0 16.6 %collective-permute-start.8 = (bf16[256,1024]{1,0:T(8,128)(2,1)S(1)}, bf16[256,1024]{1,0:T(8,128)(2,1)S(1)}, u32[]{:S(2)}, u32[]{:S(2)}) collective-permute-start(bf16[256,1024]{1,0:T(8,128)(2,1)S(1)} %collective-permute-done.4.refs_7_), channel_id=1, source_target_pairs={{0,4},{1,5},{2,6},{3,7},{4,8},{5,9},{6,10},{7,11},{8,12},{9,13},{1... | collective-permute-start | bytes 1572872 | tf_op jit(solution)/shard_map/ppermute | solution.py:24
  28.5 8.0 %collective-permute-start.16 = (bf16[64,2048]{1,0:T(8,128)(2,1)S(1)}, bf16[64,2048]{1,0:T(8,128)(2,1)S(1)}, u32[]{:S(2)}, u32[]{:S(2)}) collective-permute-start(bf16[64,2048]{1,0:T(8,128)(2,1)S(1)} %get-tuple-element.51.refs_2_.refs_3_), channel_id=1, source_target_pairs={{0,16},{1,17},{2,18},{3,19},{4,20},{5,21},{6,22},{7,23},{8,24},{9,... | collective-permute-start | bytes 786440 | tf_op jit(solution)/shard_map/ppermute | solution.py:24
  30.1 1.3 %collective-permute-start.6 = (bf16[64,1024]{1,0:T(8,128)(2,1)S(1)}, bf16[64,1024]{1,0:T(8,128)(2,1)S(1)}, u32[]{:S(2)}, u32[]{:S(2)}) collective-permute-start(bf16[64,1024]{1,0:T(8,128)(2,1)S(1)} %get-tuple-element.52.refs_4_), channel_id=1, source_target_pairs={{0,1},{1,0},{2,3},{3,2},{4,5},{5,4},{6,7},{7,6},{8,9},{9,8},{10,11... | collective-permute-start | bytes 393224 | tf_op jit(solution)/shard_map/ppermute | solution.py:24
  31.4 21.0 %copy-start.1 = (bf16[1,176,4096]{2,1,0:T(8,128)(2,1)S(1)}, bf16[1,176,4096]{2,1,0:T(8,128)(2,1)}, u32[]{:S(2)}) copy-start(bf16[1,176,4096]{2,1,0:T(8,128)(2,1)} %param.7) | copy-start | bytes 4325380
  33.7 11.3 %collective-permute-start.10 = (bf16[176,1024]{1,0:T(8,128)(2,1)S(1)}, bf16[176,1024]{1,0:T(8,128)(2,1)S(1)}, u32[]{:S(2)}, u32[]{:S(2)}) collective-permute-start(bf16[176,1024]{1,0:T(8,128)(2,1)S(1)} %get-tuple-element.57), channel_id=1, source_target_pairs={{0,2},{1,3},{2,0},{3,1},{4,6},{5,7},{6,4},{7,5},{8,10},{9,11},{10,... | collective-permute-start | bytes 1081352 | tf_op jit(solution)/shard_map/ppermute | solution.py:24
  35.2 16.6 %collective-permute-start.9 = (bf16[176,1024]{1,0:T(8,128)(2,1)S(1)}, bf16[176,1024]{1,0:T(8,128)(2,1)S(1)}, u32[]{:S(2)}, u32[]{:S(2)}) collective-permute-start(bf16[176,1024]{1,0:T(8,128)(2,1)S(1)} %get-tuple-element.56), channel_id=1, source_target_pairs={{0,18},{1,19},{2,16},{3,17},{4,22},{5,23},{6,20},{7,21},{8,26},{9,... | collective-permute-start | bytes 1081352 | tf_op jit(solution)/shard_map/ppermute | solution.py:24
  36.5 15.9 %collective-permute-start.17 = (bf16[64,2048]{1,0:T(8,128)(2,1)S(1)}, bf16[64,2048]{1,0:T(8,128)(2,1)S(1)}, u32[]{:S(2)}, u32[]{:S(2)}) collective-permute-start(bf16[64,2048]{1,0:T(8,128)(2,1)S(1)} %collective-permute-done.16.refs_5_), channel_id=1, source_target_pairs={{0,1},{1,0},{2,3},{3,2},{4,5},{5,4},{6,7},{7,6},{8,9},{9,8},{10,11... | collective-permute-start | bytes 786440 | tf_op jit(solution)/shard_map/ppermute | solution.py:24
  36.5 20.5 %collective-permute-start.15 = (bf16[256,1024]{1,0:T(8,128)(2,1)S(1)}, bf16[256,1024]{1,0:T(8,128)(2,1)S(1)}, u32[]{:S(2)}, u32[]{:S(2)}) collective-permute-start(bf16[256,1024]{1,0:T(8,128)(2,1)S(1)} %dynamic-slice_bitcast_fusion), channel_id=1, source_target_pairs={{0,12},{1,13},{2,14},{3,15},{4,0},{5,1},{6,2},{7,3},{8,4},{9,5},{1... | collective-permute-start | bytes 1572872 | tf_op jit(solution)/shard_map/ppermute | solution.py:24
  51.9 2.4 %collective-permute-start.12 = (bf16[128,1024]{1,0:T(8,128)(2,1)S(1)}, bf16[128,1024]{1,0:T(8,128)(2,1)S(1)}, u32[]{:S(2)}, u32[]{:S(2)}) collective-permute-start(bf16[128,1024]{1,0:T(8,128)(2,1)S(1)} %get-tuple-element.60), channel_id=1, source_target_pairs={{0,1},{1,0},{2,3},{3,2},{4,5},{5,4},{6,7},{7,6},{8,9},{9,8},{10,11... | collective-permute-start | bytes 786440 | tf_op jit(solution)/shard_map/ppermute | solution.py:24
  51.9 2.4 %collective-permute-start.11 = (bf16[128,1024]{1,0:T(8,128)(2,1)S(1)}, bf16[128,1024]{1,0:T(8,128)(2,1)S(1)}, u32[]{:S(2)}, u32[]{:S(2)}) collective-permute-start(bf16[128,1024]{1,0:T(8,128)(2,1)S(1)} %get-tuple-element.58), channel_id=1, source_target_pairs={{0,1},{1,0},{2,3},{3,2},{4,5},{5,4},{6,7},{7,6},{8,9},{9,8},{10,11... | collective-permute-start | bytes 786440 | tf_op jit(solution)/shard_map/ppermute | solution.py:24
  53.7 3.4 %collective-permute-start.19 = (bf16[64,2560]{1,0:T(8,128)(2,1)S(1)}, bf16[64,2560]{1,0:T(8,128)(2,1)S(1)}, u32[]{:S(2)}, u32[]{:S(2)}) collective-permute-start(bf16[64,2560]{1,0:T(8,128)(2,1)S(1)} %get-tuple-element.69), channel_id=1, source_target_pairs={{0,1},{1,0},{2,3},{3,2},{4,5},{5,4},{6,7},{7,6},{8,9},{9,8},{10,11... | collective-permute-start | bytes 983048 | tf_op jit(solution)/shard_map/ppermute | solution.py:24
  53.8 3.3 %collective-permute-start.18 = (bf16[64,2560]{1,0:T(8,128)(2,1)S(1)}, bf16[64,2560]{1,0:T(8,128)(2,1)S(1)}, u32[]{:S(2)}, u32[]{:S(2)}) collective-permute-start(bf16[64,2560]{1,0:T(8,128)(2,1)S(1)} %get-tuple-element.67), channel_id=1, source_target_pairs={{0,1},{1,0},{2,3},{3,2},{4,5},{5,4},{6,7},{7,6},{8,9},{9,8},{10,11... | collective-permute-start | bytes 983048 | tf_op jit(solution)/shard_map/ppermute | solution.py:24
  55.5 10.5 %collective-permute-start.13 = (bf16[352,512]{1,0:T(8,128)(2,1)S(1)}, bf16[352,512]{1,0:T(8,128)(2,1)S(1)}, u32[]{:S(2)}, u32[]{:S(2)}) collective-permute-start(bf16[352,512]{1,0:T(8,128)(2,1)S(1)} %shard_map.99), channel_id=1, source_target_pairs={{0,2},{1,3},{2,0},{3,1},{4,6},{5,7},{6,4},{7,5},{8,10},{9,11},{10,... | collective-permute-start | bytes 1081352 | tf_op jit(solution)/shard_map/ppermute | solution.py:24
  57.2 2.5 %collective-permute-start.21 = (bf16[128,1024]{1,0:T(8,128)(2,1)S(1)}, bf16[128,1024]{1,0:T(8,128)(2,1)S(1)}, u32[]{:S(2)}, u32[]{:S(2)}) collective-permute-start(bf16[128,1024]{1,0:T(8,128)(2,1)S(1)} %get-tuple-element.73), channel_id=1, source_target_pairs={{0,1},{1,0},{2,3},{3,2},{4,5},{5,4},{6,7},{7,6},{8,9},{9,8},{10,11... | collective-permute-start | bytes 786440 | tf_op jit(solution)/shard_map/ppermute | solution.py:24
  57.3 5.1 %collective-permute-start.20 = (bf16[128,1024]{1,0:T(8,128)(2,1)S(1)}, bf16[128,1024]{1,0:T(8,128)(2,1)S(1)}, u32[]{:S(2)}, u32[]{:S(2)}) collective-permute-start(bf16[128,1024]{1,0:T(8,128)(2,1)S(1)} %get-tuple-element.71), channel_id=1, source_target_pairs={{0,1},{1,0},{2,3},{3,2},{4,5},{5,4},{6,7},{7,6},{8,9},{9,8},{10,11... | collective-permute-start | bytes 786440 | tf_op jit(solution)/shard_map/ppermute | solution.py:24
  57.8 11.2 %collective-permute-start.26 = (bf16[16,5120]{1,0:T(8,128)(2,1)S(1)}, bf16[16,5120]{1,0:T(8,128)(2,1)S(1)}, u32[]{:S(2)}, u32[]{:S(2)}) collective-permute-start(bf16[16,5120]{1,0:T(8,128)(2,1)S(1)} %get-tuple-element.82), channel_id=1, source_target_pairs={{0,4},{1,5},{2,6},{3,7},{4,8},{5,9},{6,10},{7,11},{8,12},{9,13},{1... | collective-permute-start | bytes 491528 | tf_op jit(solution)/shard_map/ppermute | solution.py:24
  57.8 15.0 %collective-permute-start.25 = (bf16[16,5120]{1,0:T(8,128)(2,1)S(1)}, bf16[16,5120]{1,0:T(8,128)(2,1)S(1)}, u32[]{:S(2)}, u32[]{:S(2)}) collective-permute-start(bf16[16,5120]{1,0:T(8,128)(2,1)S(1)} %get-tuple-element.80), channel_id=1, source_target_pairs={{0,8},{1,9},{2,10},{3,11},{4,12},{5,13},{6,14},{7,15},{8,0},{9,1},... | collective-permute-start | bytes 491528 | tf_op jit(solution)/shard_map/ppermute | solution.py:24
  59.7 13.1 %collective-permute-start.24 = (bf16[16,5120]{1,0:T(8,128)(2,1)S(1)}, bf16[16,5120]{1,0:T(8,128)(2,1)S(1)}, u32[]{:S(2)}, u32[]{:S(2)}) collective-permute-start(bf16[16,5120]{1,0:T(8,128)(2,1)S(1)} %get-tuple-element.78), channel_id=1, source_target_pairs={{0,12},{1,13},{2,14},{3,15},{4,0},{5,1},{6,2},{7,3},{8,4},{9,5},{1... | collective-permute-start | bytes 491528 | tf_op jit(solution)/shard_map/ppermute | solution.py:24
  63.6 11.6 %collective-permute-start.22 = (bf16[176,512]{1,0:T(8,128)(2,1)S(1)}, bf16[176,512]{1,0:T(8,128)(2,1)S(1)}, u32[]{:S(2)}, u32[]{:S(2)}) collective-permute-start(bf16[176,512]{1,0:T(8,128)(2,1)S(1)} %get-tuple-element.74), channel_id=1, source_target_pairs={{0,18},{1,19},{2,16},{3,17},{4,22},{5,23},{6,20},{7,21},{8,26},{9,... | collective-permute-start | bytes 540680 | tf_op jit(solution)/shard_map/ppermute | solution.py:24
  65.9 9.3 %collective-permute-start.23 = (bf16[176,512]{1,0:T(8,128)(2,1)S(1)}, bf16[176,512]{1,0:T(8,128)(2,1)S(1)}, u32[]{:S(2)}, u32[]{:S(2)}) collective-permute-start(bf16[176,512]{1,0:T(8,128)(2,1)S(1)} %get-tuple-element.75), channel_id=1, source_target_pairs={{0,2},{1,3},{2,0},{3,1},{4,6},{5,7},{6,4},{7,5},{8,10},{9,11},{10,... | collective-permute-start | bytes 540680 | tf_op jit(solution)/shard_map/ppermute | solution.py:24
  69.0 6.2 %collective-permute-start.14 = (bf16[176,512]{1,0:T(8,128)(2,1)S(1)}, bf16[176,512]{1,0:T(8,128)(2,1)S(1)}, u32[]{:S(2)}, u32[]{:S(2)}) collective-permute-start(bf16[176,512]{1,0:T(8,128)(2,1)S(1)} %get-tuple-element.61), channel_id=1, source_target_pairs={{0,16},{1,17},{2,18},{3,19},{4,20},{5,21},{6,22},{7,23},{8,24},{9,... | collective-permute-start | bytes 540680 | tf_op jit(solution)/shard_map/ppermute | solution.py:24
  72.9 1.3 %collective-permute-start.27 = (bf16[16,2560]{1,0:T(8,128)(2,1)S(1)}, bf16[16,2560]{1,0:T(8,128)(2,1)S(1)}, u32[]{:S(2)}, u32[]{:S(2)}) collective-permute-start(bf16[16,2560]{1,0:T(8,128)(2,1)S(1)} %get-tuple-element.83.refs_0_), channel_id=1, source_target_pairs={{0,1},{1,0},{2,3},{3,2},{4,5},{5,4},{6,7},{7,6},{8,9},{9,8},{10,11... | collective-permute-start | bytes 245768 | tf_op jit(solution)/shard_map/ppermute | solution.py:24
  73.0 1.4 %collective-permute-start.28 = (bf16[16,2560]{1,0:T(8,128)(2,1)S(1)}, bf16[16,2560]{1,0:T(8,128)(2,1)S(1)}, u32[]{:S(2)}, u32[]{:S(2)}) collective-permute-start(bf16[16,2560]{1,0:T(8,128)(2,1)S(1)} %get-tuple-element.84.refs_1_), channel_id=1, source_target_pairs={{0,1},{1,0},{2,3},{3,2},{4,5},{5,4},{6,7},{7,6},{8,9},{9,8},{10,11... | collective-permute-start | bytes 245768 | tf_op jit(solution)/shard_map/ppermute | solution.py:24
  (4 other events, 3.1 us)

commit v21 on v20

--- a/solution.py
+++ b/solution.py
@@ -78,12 +78,11 @@
 
 
 def join_kernel(*refs):
-    down_ref, up_ref = refs[-2:]
-    wide = down_ref.shape[1]
+    both_ref, down_ref = refs[-2:]
     for k, ref in enumerate(refs[:-2]):
         rows = ref.shape[0]
-        down_ref[k * rows : (k + 1) * rows] = ref[:, :wide]
-        up_ref[k * rows : (k + 1) * rows] = ref[:, wide:]
+        both_ref[k * rows : (k + 1) * rows] = ref[...]
+        down_ref[k * rows : (k + 1) * rows] = ref[:, : down_ref.shape[1]]
 
 
 def own_kernel(sizes, down_ref, up_ref, out_ref):
@@ -138,18 +137,18 @@
 def frozen_kernel(sizes, batch, *refs):
     tokens, groups, holders, replicas, slots, rank = sizes
     g_refs, refs = refs[:groups], refs[groups:]
-    down_refs, refs = refs[:replicas], refs[replicas:]
+    map_refs, refs = refs[:replicas], refs[replicas:]
     core, here = lax.axis_index("replica"), lax.axis_index("adapter")
-    rows = down_refs[0].shape[0]
-    half = down_refs[0].shape[1] // holders
+    rows = map_refs[0].shape[0]
+    width = map_refs[0].shape[1] - (g_refs[0].shape[1] - LANES)
+    half = width // holders
     if batch[0][0] == 0:
-        up_refs, refs = refs[:replicas], refs[replicas:]
         sel_ref = refs[-1]
         out_refs = refs[-1 - groups : -1]
         for dg in range(groups):
             for dr in range(replicas):
                 keep = slots_of(g_refs[dg]) == row_slots(holders, replicas, slots, rank, dr)
-                proj_grad = rows_by_rows(g_refs[dg][:, :-LANES], up_refs[dr][...])
+                proj_grad = rows_by_rows(g_refs[dg][:, :-LANES], map_refs[dr][:, width:])
                 sel_ref[pl.ds(dg * tokens, tokens), dr * rows : (dr + 1) * rows] = jnp.where(
                     keep, proj_grad, 0.0
                 ).astype(BF16)
@@ -175,7 +174,7 @@
                 for j in range(replicas):
                     lora = lora + jnp.dot(
                         sel_ref[pl.ds(dg * tokens, tokens), j * rows : (j + 1) * rows],
-                        down_refs[j][:, columns],
+                        map_refs[j][:, columns],
                         preferred_element_type=F32,
                     )
                 lora = (ADAPTER_SCALE * lora).astype(BF16)
@@ -303,18 +302,18 @@
     ring = [lax.dynamic_slice_in_dim(frozen, (group * replicas + core) * piece, piece, axis=0)]
     ring.append(moved(ring[0], lambda g, z, s, r: (g, z + 1, s, r)))
     held, grads, ring = lax.optimization_barrier((held, grads, ring))
-    joined = call(
+    both, downs = call(
         join_kernel,
         [
+            jax.ShapeDtypeStruct((holders * rows, holders * half + value_width), BF16),
             jax.ShapeDtypeStruct((holders * rows, holders * half), BF16),
-            jax.ShapeDtypeStruct((holders * rows, value_width), BF16),
         ],
         held,
     )
-    downs, ups = [joined[0]], [joined[1]]
-    for dr in range(1, replicas):
-        ups.append(moved(ups[0], lambda g, z, s, r: (g, z, s, r + dr)))
-        downs.append(moved(downs[0], lambda g, z, s, r: (g, z, s, r + dr)))
+    both = [both] + [
+        moved(both, lambda g, z, s, r: (g, z, s, r + dr)) for dr in range(1, replicas)
+    ]
+
     def pieces_of(k, *before):
         if k == 0:
             return [(0, 0)], [frozen]
@@ -339,9 +338,9 @@
     kept = replicas * holders * rows
 
     def adapter_sums(sel, *before):
-        maps = list(downs)
+        maps = list(both)
         for dg in range(1, groups):
-            maps.append(moved(downs[0], lambda g, z, s, r: (g + dg, z, s, r)))
+            maps.append(moved(downs, lambda g, z, s, r: (g + dg, z, s, r)))
             for dr in range(1, replicas):
                 maps.append(moved(maps[-dr], lambda g, z, s, r: (g, z, s, r + dr)))
         gradients = call(
@@ -377,10 +376,11 @@
                     last = after(ring[-1], sel) if k > 2 else ring[-1]
                     last = moved(last, lambda g, z, s, r: (g, z + 1, s, r))
                 ring.append(last)
-            gate = arrived[0][::-1] if k == 2 else [*arrived[i - 2], chip[0]] if k > 2 else []
+            gate = arrived[0] if k == 2 else [*arrived[i - 2]] if k > 2 else []
             spec, blocks = pieces_of(k, *gate)
             specs.append((k, spec))
             operands += blocks
+        tokens_in = [after(grads[0], part), *grads[1:]] if i == 1 else grads
         out = call(
             functools.partial(
                 frozen_kernel, (tokens, groups, holders, replicas, slots, rank), specs
@@ -391,7 +391,7 @@
                 else [jax.ShapeDtypeStruct((tokens, half * len(batch)), BF16)] * groups
             )
             + [jax.ShapeDtypeStruct((groups * tokens, kept), BF16)] * (i == 0),
-            [*grads, *downs, *([sel] if i else ups), *operands],
+            [*tokens_in, *both, *([sel] if i else []), *operands],
         )
         if i == 0:
             sel = out[groups]
@@ -420,7 +420,7 @@
         if i > 1:
             late += [((batch, dg), arrived[-1][dg]) for dg in reversed(range(groups))]
         if i == 0:
-            part, chip = adapter_sums(sel, *arrived[0][::-1])
+            part, chip = adapter_sums(sel, *arrived[0])
     sizes = (groups, holders, shard, half)
     if len(batches) > 2:
         passed = pl.pallas_call(

time: 77 us -> 76.8 us (level)
  the two profiles are of different devices: /device:TPU:0 before, /device:TPU:9 now
where the time goes in v21:
time: 76.8 us; the launch traced here: 76.5 us
  waiting for transfers between devices  40.9 us (53%)
  starting transfers between devices  19.6 us (26%)
  Pallas kernels  9.77 us (13%)
  local copies, waits for them, and re-layouts  5.36 us (7%)
  between operations  0.78 us (1%)
    ppermute x28, waiting for transfers between devices, moved(): return lax.ppermute(x, AXES, pairs)  40.9 us
    ppermute x28, starting transfers between devices, moved(): return lax.ppermute(x, AXES, pairs)  19.6 us
    pallas_call x13, Pallas kernels, call(): pl.pallas_call(kernel, out_shape=out_shape, in_specs=[pl.BlockSpec(memory...  8.93 us
    unnamed x14, local copies, waits for them, and re-layouts  4.11 us
  transfers between devices with their start and end apart: 28, of which 14 were waited for; matrix products, arithmetic and copies ran while one was open for 0% of the time, Pallas kernels for 12%

profile of v21, /device:TPU:9, one launch (start us, length us, event | category | flops | bytes accessed | tf_op | source)
XLA Modules:
  0.0 76.5 jit_solution(9042936212533615823)
XLA Ops:
  0.6 1.2 %dynamic-slice_bitcast_fusion = bf16[256,1024]{1,0:T(8,128)(2,1)S(1)} fusion(bf16[1,1024,1024]{2,1,0:T(8,128)(2,1)} %param.11, s32[]{:T(128)S(6)} %select_n.3), kind=kLoop, calls=%fused_computation | loop fusion | bytes 1048580 | tf_op jit(solution)/shard_map/dynamic_slice | solution.py:302
  1.9 1.3 %collective-permute-start.4 = (bf16[256,1024]{1,0:T(8,128)(2,1)S(1)}, bf16[256,1024]{1,0:T(8,128)(2,1)S(1)}, u32[]{:S(2)}, u32[]{:S(2)}) collective-permute-start(bf16[256,1024]{1,0:T(8,128)(2,1)S(1)} %dynamic-slice_bitcast_fusion), channel_id=1, source_target_pairs={{0,4},{1,5},{2,6},{3,7},{4,8},{5,9},{6,10},{7,11},{8,12},{9,13},{1... | collective-permute-start | bytes 1572872 | tf_op jit(solution)/shard_map/ppermute | solution.py:24
  3.2 1.0 %copy-done.2 = bf16[1,176,1024]{2,1,0:T(8,128)(2,1)S(1)} copy-done((bf16[1,176,1024]{2,1,0:T(8,128)(2,1)S(1)}, bf16[1,176,1024]{2,1,0:T(8,128)(2,1)}, u32[]{:S(2)}) %copy-start.2) | copy-done | bytes 360472
  6.3 1.3 %collective-permute-start.3 = (bf16[176,1152]{1,0:T(8,128)(2,1)S(1)}, bf16[176,1152]{1,0:T(8,128)(2,1)S(1)}, u32[]{:S(2)}, u32[]{:S(2)}) collective-permute-start(bf16[176,1152]{1,0:T(8,128)(2,1)S(1)} %shard_map.95.refs_0_.refs_1_), channel_id=1, source_target_pairs={{0,16},{1,17},{2,18},{3,19},{4,20},{5,21},{6,22},{7,23},{8,24},{9,... | collective-permute-start | bytes 1216520 | tf_op jit(solution)/shard_map/ppermute | solution.py:24
  7.6 0.9 %copy-done.3 = bf16[1,2,16,4096]{3,2,1,0:T(8,128)(2,1)S(1)} copy-done((bf16[1,2,16,4096]{3,2,1,0:T(8,128)(2,1)S(1)}, bf16[1,2,16,4096]{3,2,1,0:T(8,128)(2,1)}, u32[]{:S(2)}) %copy-start.3) | copy-done | bytes 262168
  8.6 0.8 %copy-done.4 = bf16[1,2,16,1024]{3,2,1,0:T(8,128)(2,1)S(1)} copy-done((bf16[1,2,16,1024]{3,2,1,0:T(8,128)(2,1)S(1)}, bf16[1,2,16,1024]{3,2,1,0:T(8,128)(2,1)}, u32[]{:S(2)}) %copy-start.4) | copy-done | bytes 65560
  9.4 1.3 %collective-permute-start = (bf16[16,3072]{1,0:T(8,128)(2,1)S(1)}, bf16[16,3072]{1,0:T(8,128)(2,1)S(1)}, u32[]{:S(2)}, u32[]{:S(2)}) collective-permute-start(bf16[16,3072]{1,0:T(8,128)(2,1)S(1)} %shard_map.94.refs_0_), channel_id=1, source_target_pairs={{0,4},{1,5},{2,6},{3,7},{4,8},{5,9},{6,10},{7,11},{8,12},{9,13},{1... | collective-permute-start | bytes 294920 | tf_op jit(solution)/shard_map/ppermute | solution.py:24
  10.8 1.0 %collective-permute-start.1 = (bf16[16,3072]{1,0:T(8,128)(2,1)S(1)}, bf16[16,3072]{1,0:T(8,128)(2,1)S(1)}, u32[]{:S(2)}, u32[]{:S(2)}) collective-permute-start(bf16[16,3072]{1,0:T(8,128)(2,1)S(1)} %shard_map.94.refs_0_), channel_id=1, source_target_pairs={{0,8},{1,9},{2,10},{3,11},{4,12},{5,13},{6,14},{7,15},{8,0},{9,1},... | collective-permute-start | bytes 294920 | tf_op jit(solution)/shard_map/ppermute | solution.py:24
  12.0 4.8 %collective-permute-done.refs_1_ = bf16[16,3072]{1,0:T(8,128)(2,1)S(1)} collective-permute-done((bf16[16,3072]{1,0:T(8,128)(2,1)S(1)}, bf16[16,3072]{1,0:T(8,128)(2,1)S(1)}, u32[]{:S(2)}, u32[]{:S(2)}) %collective-permute-start) | collective-permute-done | bytes 98336 | tf_op jit(solution)/shard_map/ppermute | solution.py:24
  16.8 5.4 %collective-permute-done.1.refs_2_ = bf16[16,3072]{1,0:T(8,128)(2,1)S(1)} collective-permute-done((bf16[16,3072]{1,0:T(8,128)(2,1)S(1)}, bf16[16,3072]{1,0:T(8,128)(2,1)S(1)}, u32[]{:S(2)}, u32[]{:S(2)}) %collective-permute-start.1) | collective-permute-done | bytes 98336 | tf_op jit(solution)/shard_map/ppermute | solution.py:24
  22.2 2.8 %collective-permute-done.2.refs_3_ = bf16[16,3072]{1,0:T(8,128)(2,1)S(1)} collective-permute-done((bf16[16,3072]{1,0:T(8,128)(2,1)S(1)}, bf16[16,3072]{1,0:T(8,128)(2,1)S(1)}, u32[]{:S(2)}, u32[]{:S(2)}) %collective-permute-start.2) | collective-permute-done | bytes 98336 | tf_op jit(solution)/shard_map/ppermute | solution.py:24
  25.8 1.9 %collective-permute-done.5.refs_3_.refs_4_ = bf16[64,3072]{1,0:T(8,128)(2,1)S(1)} collective-permute-done((bf16[64,3072]{1,0:T(8,128)(2,1)S(1)}, bf16[64,3072]{1,0:T(8,128)(2,1)S(1)}, u32[]{:S(2)}, u32[]{:S(2)}) %collective-permute-start.5) | collective-permute-done | bytes 393248 | tf_op jit(solution)/shard_map/ppermute | solution.py:24
  27.7 2.2 %shard_map.97 = (bf16[176,1024]{1,0:T(8,128)(2,1)S(1)}, bf16[176,1024]{1,0:T(8,128)(2,1)S(1)}, bf16[352,128]{1,0:T(8,128)(2,1)S(1)}) custom-call(bf16[176,1152]{1,0:T(8,128)(2,1)S(1)} %shard_map.95.refs_0_.refs_1_, bf16[176,1152]{1,0:T(8,128)(2,1)S(1)} %collective-permute-done.3.refs_1_, bf16[64,3072]{1,0:T(8,128)(2,1)S(1)} %get-tuple-element.52.refs_2_.refs_3_, ...), custom_call_target="tpu_custom_call" | custom-call | flops 1000 | bytes 1000 | tf_op jit(solution)/shard_map/pallas_call | solution.py:41
  29.9 1.3 %collective-permute-start.10 = (bf16[176,1024]{1,0:T(8,128)(2,1)S(1)}, bf16[176,1024]{1,0:T(8,128)(2,1)S(1)}, u32[]{:S(2)}, u32[]{:S(2)}) collective-permute-start(bf16[176,1024]{1,0:T(8,128)(2,1)S(1)} %get-tuple-element.59), channel_id=1, source_target_pairs={{0,2},{1,3},{2,0},{3,1},{4,6},{5,7},{6,4},{7,5},{8,10},{9,11},{10,... | collective-permute-start | bytes 1081352 | tf_op jit(solution)/shard_map/ppermute | solution.py:24
  31.2 1.2 %collective-permute-start.11 = (bf16[176,1024]{1,0:T(8,128)(2,1)S(1)}, bf16[176,1024]{1,0:T(8,128)(2,1)S(1)}, u32[]{:S(2)}, u32[]{:S(2)}) collective-permute-start(bf16[176,1024]{1,0:T(8,128)(2,1)S(1)} %get-tuple-element.60), channel_id=1, source_target_pairs={{0,18},{1,19},{2,16},{3,17},{4,22},{5,23},{6,20},{7,21},{8,26},{9,... | collective-permute-start | bytes 1081352 | tf_op jit(solution)/shard_map/ppermute | solution.py:24
  32.7 6.7 %collective-permute-done.7.refs_5_ = bf16[64,2048]{1,0:T(8,128)(2,1)S(1)} collective-permute-done((bf16[64,2048]{1,0:T(8,128)(2,1)S(1)}, bf16[64,2048]{1,0:T(8,128)(2,1)S(1)}, u32[]{:S(2)}, u32[]{:S(2)}) %collective-permute-start.7) | collective-permute-done | bytes 262176 | tf_op jit(solution)/shard_map/ppermute | solution.py:24
  39.3 2.0 %collective-permute-start.8 = (bf16[64,2048]{1,0:T(8,128)(2,1)S(1)}, bf16[64,2048]{1,0:T(8,128)(2,1)S(1)}, u32[]{:S(2)}, u32[]{:S(2)}) collective-permute-start(bf16[64,2048]{1,0:T(8,128)(2,1)S(1)} %collective-permute-done.7.refs_5_), channel_id=1, source_target_pairs={{0,1},{1,0},{2,3},{3,2},{4,5},{5,4},{6,7},{7,6},{8,9},{9,8},{10,11... | collective-permute-start | bytes 786440 | tf_op jit(solution)/shard_map/ppermute | solution.py:24
  41.4 7.0 %collective-permute-done.11.refs_1_ = bf16[176,1024]{1,0:T(8,128)(2,1)S(1)} collective-permute-done((bf16[176,1024]{1,0:T(8,128)(2,1)S(1)}, bf16[176,1024]{1,0:T(8,128)(2,1)S(1)}, u32[]{:S(2)}, u32[]{:S(2)}) %collective-permute-start.11) | collective-permute-done | bytes 360480 | tf_op jit(solution)/shard_map/ppermute | solution.py:24
  48.3 1.2 %collective-permute-start.13 = (bf16[128,1024]{1,0:T(8,128)(2,1)S(1)}, bf16[128,1024]{1,0:T(8,128)(2,1)S(1)}, u32[]{:S(2)}, u32[]{:S(2)}) collective-permute-start(bf16[128,1024]{1,0:T(8,128)(2,1)S(1)} %get-tuple-element.63), channel_id=1, source_target_pairs={{0,1},{1,0},{2,3},{3,2},{4,5},{5,4},{6,7},{7,6},{8,9},{9,8},{10,11... | collective-permute-start | bytes 786440 | tf_op jit(solution)/shard_map/ppermute | solution.py:24
  49.5 1.3 %shard_map.98 = (f32[64,5120]{1,0:T(8,128)S(1)}, bf16[64,2560]{1,0:T(8,128)(2,1)S(1)}, bf16[64,2560]{1,0:T(8,128)(2,1)S(1)}) custom-call(bf16[176,4096]{1,0:T(8,128)(2,1)S(1)} %bitcast.12, bf16[176,1152]{1,0:T(8,128)(2,1)S(1)} %shard_map.95.refs_0_.refs_1_, bf16[352,128]{1,0:T(8,128)(2,1)S(1)} %get-tuple-element.54.refs_2_.refs_4_, ...), custom_call_target="tpu_custom_call" | custom-call | flops 1000 | bytes 1000 | tf_op jit(solution)/shard_map/pallas_call | solution.py:41
  51.1 1.2 %shard_map.100 = bf16[352,512]{1,0:T(8,128)(2,1)S(1)} custom-call(bf16[176,1152]{1,0:T(8,128)(2,1)S(1)} %shard_map.95.refs_0_.refs_1_, bf16[176,1152]{1,0:T(8,128)(2,1)S(1)} %collective-permute-done.3.refs_1_, bf16[64,3072]{1,0:T(8,128)(2,1)S(1)} %get-tuple-element.52.refs_2_.refs_3_, bf16[64,3072]{1,0:T(8,128)(2,1)S(1)} %collective-permute-done.5.refs_3_.refs_4_, ...), custom_call_target="tpu_custom_call" | custom-call | flops 1000 | bytes 1000 | tf_op jit(solution)/shard_map/pallas_call | solution.py:41
  52.2 1.3 %collective-permute-start.14 = (bf16[352,512]{1,0:T(8,128)(2,1)S(1)}, bf16[352,512]{1,0:T(8,128)(2,1)S(1)}, u32[]{:S(2)}, u32[]{:S(2)}) collective-permute-start(bf16[352,512]{1,0:T(8,128)(2,1)S(1)} %shard_map.100), channel_id=1, source_target_pairs={{0,2},{1,3},{2,0},{3,1},{4,6},{5,7},{6,4},{7,5},{8,10},{9,11},{10,... | collective-permute-start | bytes 1081352 | tf_op jit(solution)/shard_map/ppermute | solution.py:24
  56.1 1.6 %collective-permute-start.24 = (bf16[16,5120]{1,0:T(8,128)(2,1)S(1)}, bf16[16,5120]{1,0:T(8,128)(2,1)S(1)}, u32[]{:S(2)}, u32[]{:S(2)}) collective-permute-start(bf16[16,5120]{1,0:T(8,128)(2,1)S(1)} %get-tuple-element.82), channel_id=1, source_target_pairs={{0,8},{1,9},{2,10},{3,11},{4,12},{5,13},{6,14},{7,15},{8,0},{9,1},... | collective-permute-start | bytes 491528 | tf_op jit(solution)/shard_map/ppermute | solution.py:24
  57.8 1.2 %collective-permute-start.23 = (bf16[16,5120]{1,0:T(8,128)(2,1)S(1)}, bf16[16,5120]{1,0:T(8,128)(2,1)S(1)}, u32[]{:S(2)}, u32[]{:S(2)}) collective-permute-start(bf16[16,5120]{1,0:T(8,128)(2,1)S(1)} %get-tuple-element.80), channel_id=1, source_target_pairs={{0,12},{1,13},{2,14},{3,15},{4,0},{5,1},{6,2},{7,3},{8,4},{9,5},{1... | collective-permute-start | bytes 491528 | tf_op jit(solution)/shard_map/ppermute | solution.py:24
  59.0 1.2 %shard_map.103 = (bf16[176,512]{1,0:T(8,128)(2,1)S(1)}, bf16[176,512]{1,0:T(8,128)(2,1)S(1)}) custom-call(bf16[176,1152]{1,0:T(8,128)(2,1)S(1)} %shard_map.95.refs_0_.refs_1_, bf16[176,1152]{1,0:T(8,128)(2,1)S(1)} %collective-permute-done.3.refs_1_, bf16[64,3072]{1,0:T(8,128)(2,1)S(1)} %get-tuple-element.52.refs_2_.refs_3_, ...), custom_call_target="tpu_custom_call" | custom-call | flops 1000 | bytes 1000 | tf_op jit(solution)/shard_map/pallas_call | solution.py:41
  60.4 1.5 %collective-permute-done.14 = bf16[352,512]{1,0:T(8,128)(2,1)S(1)} collective-permute-done((bf16[352,512]{1,0:T(8,128)(2,1)S(1)}, bf16[352,512]{1,0:T(8,128)(2,1)S(1)}, u32[]{:S(2)}, u32[]{:S(2)}) %collective-permute-start.14) | collective-permute-done | bytes 360480 | tf_op jit(solution)/shard_map/ppermute | solution.py:24
  61.9 1.2 %collective-permute-start.20 = (bf16[176,512]{1,0:T(8,128)(2,1)S(1)}, bf16[176,512]{1,0:T(8,128)(2,1)S(1)}, u32[]{:S(2)}, u32[]{:S(2)}) collective-permute-start(bf16[176,512]{1,0:T(8,128)(2,1)S(1)} %get-tuple-element.72), channel_id=1, source_target_pairs={{0,2},{1,3},{2,0},{3,1},{4,6},{5,7},{6,4},{7,5},{8,10},{9,11},{10,... | collective-permute-start | bytes 540680 | tf_op jit(solution)/shard_map/ppermute | solution.py:24
  63.2 1.2 %shard_map.101.refs_3_ = bf16[176,4096]{1,0:T(8,128)(2,1)} custom-call(bf16[176,1024]{1,0:T(8,128)(2,1)S(1)} %collective-permute-done.10.refs_0_, bf16[176,1024]{1,0:T(8,128)(2,1)S(1)} %collective-permute-done.11.refs_1_, bf16[176,512]{1,0:T(8,128)(2,1)S(1)} %get-tuple-element.90.refs_2_), custom_call_target="tpu_custom_call" | custom-call | flops 1000 | bytes 1000 | tf_op jit(solution)/shard_map/pallas_call | solution.py:41
  64.6 5.6 %collective-permute-done.24.refs_2_ = bf16[16,5120]{1,0:T(8,128)(2,1)S(1)} collective-permute-done((bf16[16,5120]{1,0:T(8,128)(2,1)S(1)}, bf16[16,5120]{1,0:T(8,128)(2,1)S(1)}, u32[]{:S(2)}, u32[]{:S(2)}) %collective-permute-start.24) | collective-permute-done | bytes 163872 | tf_op jit(solution)/shard_map/ppermute | solution.py:24
  70.1 2.8 %collective-permute-done.23.refs_1_ = bf16[16,5120]{1,0:T(8,128)(2,1)S(1)} collective-permute-done((bf16[16,5120]{1,0:T(8,128)(2,1)S(1)}, bf16[16,5120]{1,0:T(8,128)(2,1)S(1)}, u32[]{:S(2)}, u32[]{:S(2)}) %collective-permute-start.23) | collective-permute-done | bytes 163872 | tf_op jit(solution)/shard_map/ppermute | solution.py:24
  73.7 0.8 %collective-permute-done.26.refs_2_ = bf16[16,2560]{1,0:T(8,128)(2,1)S(1)} collective-permute-done((bf16[16,2560]{1,0:T(8,128)(2,1)S(1)}, bf16[16,2560]{1,0:T(8,128)(2,1)S(1)}, u32[]{:S(2)}, u32[]{:S(2)}) %collective-permute-start.26) | collective-permute-done | bytes 81952 | tf_op jit(solution)/shard_map/ppermute | solution.py:24
  75.6 0.8 %shard_map.104 = bf16[176,4096]{1,0:T(8,128)(2,1)} custom-call(bf16[176,512]{1,0:T(8,128)(2,1)S(1)} %collective-permute-done.15.refs_0_, bf16[176,512]{1,0:T(8,128)(2,1)S(1)} %collective-permute-done.19.refs_1_, bf16[176,512]{1,0:T(8,128)(2,1)S(1)} %collective-permute-done.20.refs_2_, ...), custom_call_target="tpu_custom_call", output_to_operand_aliasing={{}: (3, {})} | custom-call | flops 1000 | bytes 1000 | tf_op jit(solution)/shard_map/pallas_call | solution.py:426
  (54 shorter events, 8.6 us)
Async XLA Ops:
  0.6 27.1 %copy-start = (bf16[1,1024,1024]{2,1,0:T(8,128)(2,1)S(1)}, bf16[1,1024,1024]{2,1,0:T(8,128)(2,1)}, u32[]{:S(2)}) copy-start(bf16[1,1024,1024]{2,1,0:T(8,128)(2,1)} %param.11) | copy-start | bytes 6291460
  1.9 23.2 %collective-permute-start.4 = (bf16[256,1024]{1,0:T(8,128)(2,1)S(1)}, bf16[256,1024]{1,0:T(8,128)(2,1)S(1)}, u32[]{:S(2)}, u32[]{:S(2)}) collective-permute-start(bf16[256,1024]{1,0:T(8,128)(2,1)S(1)} %dynamic-slice_bitcast_fusion), channel_id=1, source_target_pairs={{0,4},{1,5},{2,6},{3,7},{4,8},{5,9},{6,10},{7,11},{8,12},{9,13},{1... | collective-permute-start | bytes 1572872 | tf_op jit(solution)/shard_map/ppermute | solution.py:24
  3.2 1.0 %copy-start.2 = (bf16[1,176,1024]{2,1,0:T(8,128)(2,1)S(1)}, bf16[1,176,1024]{2,1,0:T(8,128)(2,1)}, u32[]{:S(2)}) copy-start(bf16[1,176,1024]{2,1,0:T(8,128)(2,1)} %param.8) | copy-start | bytes 1081348
  6.3 18.8 %collective-permute-start.3 = (bf16[176,1152]{1,0:T(8,128)(2,1)S(1)}, bf16[176,1152]{1,0:T(8,128)(2,1)S(1)}, u32[]{:S(2)}, u32[]{:S(2)}) collective-permute-start(bf16[176,1152]{1,0:T(8,128)(2,1)S(1)} %shard_map.95.refs_0_.refs_1_), channel_id=1, source_target_pairs={{0,16},{1,17},{2,18},{3,19},{4,20},{5,21},{6,22},{7,23},{8,24},{9,... | collective-permute-start | bytes 1216520 | tf_op jit(solution)/shard_map/ppermute | solution.py:24
  7.6 0.9 %copy-start.3 = (bf16[1,2,16,4096]{3,2,1,0:T(8,128)(2,1)S(1)}, bf16[1,2,16,4096]{3,2,1,0:T(8,128)(2,1)}, u32[]{:S(2)}) copy-start(bf16[1,2,16,4096]{3,2,1,0:T(8,128)(2,1)} %param.12) | copy-start | bytes 786436
  9.4 7.4 %collective-permute-start = (bf16[16,3072]{1,0:T(8,128)(2,1)S(1)}, bf16[16,3072]{1,0:T(8,128)(2,1)S(1)}, u32[]{:S(2)}, u32[]{:S(2)}) collective-permute-start(bf16[16,3072]{1,0:T(8,128)(2,1)S(1)} %shard_map.94.refs_0_), channel_id=1, source_target_pairs={{0,4},{1,5},{2,6},{3,7},{4,8},{5,9},{6,10},{7,11},{8,12},{9,13},{1... | collective-permute-start | bytes 294920 | tf_op jit(solution)/shard_map/ppermute | solution.py:24
  10.8 11.5 %collective-permute-start.1 = (bf16[16,3072]{1,0:T(8,128)(2,1)S(1)}, bf16[16,3072]{1,0:T(8,128)(2,1)S(1)}, u32[]{:S(2)}, u32[]{:S(2)}) collective-permute-start(bf16[16,3072]{1,0:T(8,128)(2,1)S(1)} %shard_map.94.refs_0_), channel_id=1, source_target_pairs={{0,8},{1,9},{2,10},{3,11},{4,12},{5,13},{6,14},{7,15},{8,0},{9,1},... | collective-permute-start | bytes 294920 | tf_op jit(solution)/shard_map/ppermute | solution.py:24
  11.7 13.4 %collective-permute-start.2 = (bf16[16,3072]{1,0:T(8,128)(2,1)S(1)}, bf16[16,3072]{1,0:T(8,128)(2,1)S(1)}, u32[]{:S(2)}, u32[]{:S(2)}) collective-permute-start(bf16[16,3072]{1,0:T(8,128)(2,1)S(1)} %shard_map.94.refs_0_), channel_id=1, source_target_pairs={{0,12},{1,13},{2,14},{3,15},{4,0},{5,1},{6,2},{7,3},{8,4},{9,5},{1... | collective-permute-start | bytes 294920 | tf_op jit(solution)/shard_map/ppermute | solution.py:24
  25.1 2.6 %collective-permute-start.6 = (bf16[256,1024]{1,0:T(8,128)(2,1)S(1)}, bf16[256,1024]{1,0:T(8,128)(2,1)S(1)}, u32[]{:S(2)}, u32[]{:S(2)}) collective-permute-start(bf16[256,1024]{1,0:T(8,128)(2,1)S(1)} %collective-permute-done.4.refs_5_), channel_id=1, source_target_pairs={{0,1},{1,0},{2,3},{3,2},{4,5},{5,4},{6,7},{7,6},{8,9},{9,8},{10,11... | collective-permute-start | bytes 1572872 | tf_op jit(solution)/shard_map/ppermute | solution.py:24
  25.6 2.1 %collective-permute-start.5 = (bf16[64,3072]{1,0:T(8,128)(2,1)S(1)}, bf16[64,3072]{1,0:T(8,128)(2,1)S(1)}, u32[]{:S(2)}, u32[]{:S(2)}) collective-permute-start(bf16[64,3072]{1,0:T(8,128)(2,1)S(1)} %get-tuple-element.52.refs_2_.refs_3_), channel_id=1, source_target_pairs={{0,1},{1,0},{2,3},{3,2},{4,5},{5,4},{6,7},{7,6},{8,9},{9,8},{10,11... | collective-permute-start | bytes 1179656 | tf_op jit(solution)/shard_map/ppermute | solution.py:24
  25.7 15.6 %collective-permute-start.9 = (bf16[256,1024]{1,0:T(8,128)(2,1)S(1)}, bf16[256,1024]{1,0:T(8,128)(2,1)S(1)}, u32[]{:S(2)}, u32[]{:S(2)}) collective-permute-start(bf16[256,1024]{1,0:T(8,128)(2,1)S(1)} %collective-permute-done.4.refs_5_), channel_id=1, source_target_pairs={{0,4},{1,5},{2,6},{3,7},{4,8},{5,9},{6,10},{7,11},{8,12},{9,13},{1... | collective-permute-start | bytes 1572872 | tf_op jit(solution)/shard_map/ppermute | solution.py:24
  27.7 21.8 %copy-start.1 = (bf16[1,176,4096]{2,1,0:T(8,128)(2,1)S(1)}, bf16[1,176,4096]{2,1,0:T(8,128)(2,1)}, u32[]{:S(2)}) copy-start(bf16[1,176,4096]{2,1,0:T(8,128)(2,1)} %param.7) | copy-start | bytes 4325380
  29.9 11.4 %collective-permute-start.10 = (bf16[176,1024]{1,0:T(8,128)(2,1)S(1)}, bf16[176,1024]{1,0:T(8,128)(2,1)S(1)}, u32[]{:S(2)}, u32[]{:S(2)}) collective-permute-start(bf16[176,1024]{1,0:T(8,128)(2,1)S(1)} %get-tuple-element.59), channel_id=1, source_target_pairs={{0,2},{1,3},{2,0},{3,1},{4,6},{5,7},{6,4},{7,5},{8,10},{9,11},{10,... | collective-permute-start | bytes 1081352 | tf_op jit(solution)/shard_map/ppermute | solution.py:24
  31.2 17.1 %collective-permute-start.11 = (bf16[176,1024]{1,0:T(8,128)(2,1)S(1)}, bf16[176,1024]{1,0:T(8,128)(2,1)S(1)}, u32[]{:S(2)}, u32[]{:S(2)}) collective-permute-start(bf16[176,1024]{1,0:T(8,128)(2,1)S(1)} %get-tuple-element.60), channel_id=1, source_target_pairs={{0,18},{1,19},{2,16},{3,17},{4,22},{5,23},{6,20},{7,21},{8,26},{9,... | collective-permute-start | bytes 1081352 | tf_op jit(solution)/shard_map/ppermute | solution.py:24
  32.4 6.9 %collective-permute-start.7 = (bf16[64,2048]{1,0:T(8,128)(2,1)S(1)}, bf16[64,2048]{1,0:T(8,128)(2,1)S(1)}, u32[]{:S(2)}, u32[]{:S(2)}) collective-permute-start(bf16[64,2048]{1,0:T(8,128)(2,1)S(1)} %get-tuple-element.55), channel_id=1, source_target_pairs={{0,16},{1,17},{2,18},{3,19},{4,20},{5,21},{6,22},{7,23},{8,24},{9,... | collective-permute-start | bytes 786440 | tf_op jit(solution)/shard_map/ppermute | solution.py:24
  32.7 21.5 %collective-permute-start.16 = (bf16[256,1024]{1,0:T(8,128)(2,1)S(1)}, bf16[256,1024]{1,0:T(8,128)(2,1)S(1)}, u32[]{:S(2)}, u32[]{:S(2)}) collective-permute-start(bf16[256,1024]{1,0:T(8,128)(2,1)S(1)} %dynamic-slice_bitcast_fusion), channel_id=1, source_target_pairs={{0,12},{1,13},{2,14},{3,15},{4,0},{5,1},{6,2},{7,3},{8,4},{9,5},{1... | collective-permute-start | bytes 1572872 | tf_op jit(solution)/shard_map/ppermute | solution.py:24
  39.3 10.2 %collective-permute-start.8 = (bf16[64,2048]{1,0:T(8,128)(2,1)S(1)}, bf16[64,2048]{1,0:T(8,128)(2,1)S(1)}, u32[]{:S(2)}, u32[]{:S(2)}) collective-permute-start(bf16[64,2048]{1,0:T(8,128)(2,1)S(1)} %collective-permute-done.7.refs_5_), channel_id=1, source_target_pairs={{0,1},{1,0},{2,3},{3,2},{4,5},{5,4},{6,7},{7,6},{8,9},{9,8},{10,11... | collective-permute-start | bytes 786440 | tf_op jit(solution)/shard_map/ppermute | solution.py:24
  48.3 2.5 %collective-permute-start.13 = (bf16[128,1024]{1,0:T(8,128)(2,1)S(1)}, bf16[128,1024]{1,0:T(8,128)(2,1)S(1)}, u32[]{:S(2)}, u32[]{:S(2)}) collective-permute-start(bf16[128,1024]{1,0:T(8,128)(2,1)S(1)} %get-tuple-element.63), channel_id=1, source_target_pairs={{0,1},{1,0},{2,3},{3,2},{4,5},{5,4},{6,7},{7,6},{8,9},{9,8},{10,11... | collective-permute-start | bytes 786440 | tf_op jit(solution)/shard_map/ppermute | solution.py:24
  49.5 1.5 %collective-permute-start.12 = (bf16[128,1024]{1,0:T(8,128)(2,1)S(1)}, bf16[128,1024]{1,0:T(8,128)(2,1)S(1)}, u32[]{:S(2)}, u32[]{:S(2)}) collective-permute-start(bf16[128,1024]{1,0:T(8,128)(2,1)S(1)} %get-tuple-element.61), channel_id=1, source_target_pairs={{0,1},{1,0},{2,3},{3,2},{4,5},{5,4},{6,7},{7,6},{8,9},{9,8},{10,11... | collective-permute-start | bytes 786440 | tf_op jit(solution)/shard_map/ppermute | solution.py:24
  52.2 9.7 %collective-permute-start.14 = (bf16[352,512]{1,0:T(8,128)(2,1)S(1)}, bf16[352,512]{1,0:T(8,128)(2,1)S(1)}, u32[]{:S(2)}, u32[]{:S(2)}) collective-permute-start(bf16[352,512]{1,0:T(8,128)(2,1)S(1)} %shard_map.100), channel_id=1, source_target_pairs={{0,2},{1,3},{2,0},{3,1},{4,6},{5,7},{6,4},{7,5},{8,10},{9,11},{10,... | collective-permute-start | bytes 1081352 | tf_op jit(solution)/shard_map/ppermute | solution.py:24
  53.5 1.9 %collective-permute-start.22 = (bf16[64,2560]{1,0:T(8,128)(2,1)S(1)}, bf16[64,2560]{1,0:T(8,128)(2,1)S(1)}, u32[]{:S(2)}, u32[]{:S(2)}) collective-permute-start(bf16[64,2560]{1,0:T(8,128)(2,1)S(1)} %get-tuple-element.77), channel_id=1, source_target_pairs={{0,1},{1,0},{2,3},{3,2},{4,5},{5,4},{6,7},{7,6},{8,9},{9,8},{10,11... | collective-permute-start | bytes 983048 | tf_op jit(solution)/shard_map/ppermute | solution.py:24
  54.2 1.7 %collective-permute-start.21 = (bf16[64,2560]{1,0:T(8,128)(2,1)S(1)}, bf16[64,2560]{1,0:T(8,128)(2,1)S(1)}, u32[]{:S(2)}, u32[]{:S(2)}) collective-permute-start(bf16[64,2560]{1,0:T(8,128)(2,1)S(1)} %get-tuple-element.75), channel_id=1, source_target_pairs={{0,1},{1,0},{2,3},{3,2},{4,5},{5,4},{6,7},{7,6},{8,9},{9,8},{10,11... | collective-permute-start | bytes 983048 | tf_op jit(solution)/shard_map/ppermute | solution.py:24
  54.2 3.5 %collective-permute-start.18 = (bf16[128,1024]{1,0:T(8,128)(2,1)S(1)}, bf16[128,1024]{1,0:T(8,128)(2,1)S(1)}, u32[]{:S(2)}, u32[]{:S(2)}) collective-permute-start(bf16[128,1024]{1,0:T(8,128)(2,1)S(1)} %get-tuple-element.70), channel_id=1, source_target_pairs={{0,1},{1,0},{2,3},{3,2},{4,5},{5,4},{6,7},{7,6},{8,9},{9,8},{10,11... | collective-permute-start | bytes 786440 | tf_op jit(solution)/shard_map/ppermute | solution.py:24
  54.8 4.2 %collective-permute-start.17 = (bf16[128,1024]{1,0:T(8,128)(2,1)S(1)}, bf16[128,1024]{1,0:T(8,128)(2,1)S(1)}, u32[]{:S(2)}, u32[]{:S(2)}) collective-permute-start(bf16[128,1024]{1,0:T(8,128)(2,1)S(1)} %get-tuple-element.68), channel_id=1, source_target_pairs={{0,1},{1,0},{2,3},{3,2},{4,5},{5,4},{6,7},{7,6},{8,9},{9,8},{10,11... | collective-permute-start | bytes 786440 | tf_op jit(solution)/shard_map/ppermute | solution.py:24
  56.0 8.3 %collective-permute-start.25 = (bf16[16,5120]{1,0:T(8,128)(2,1)S(1)}, bf16[16,5120]{1,0:T(8,128)(2,1)S(1)}, u32[]{:S(2)}, u32[]{:S(2)}) collective-permute-start(bf16[16,5120]{1,0:T(8,128)(2,1)S(1)} %get-tuple-element.84), channel_id=1, source_target_pairs={{0,4},{1,5},{2,6},{3,7},{4,8},{5,9},{6,10},{7,11},{8,12},{9,13},{1... | collective-permute-start | bytes 491528 | tf_op jit(solution)/shard_map/ppermute | solution.py:24
  56.1 14.0 %collective-permute-start.24 = (bf16[16,5120]{1,0:T(8,128)(2,1)S(1)}, bf16[16,5120]{1,0:T(8,128)(2,1)S(1)}, u32[]{:S(2)}, u32[]{:S(2)}) collective-permute-start(bf16[16,5120]{1,0:T(8,128)(2,1)S(1)} %get-tuple-element.82), channel_id=1, source_target_pairs={{0,8},{1,9},{2,10},{3,11},{4,12},{5,13},{6,14},{7,15},{8,0},{9,1},... | collective-permute-start | bytes 491528 | tf_op jit(solution)/shard_map/ppermute | solution.py:24
  57.8 15.2 %collective-permute-start.23 = (bf16[16,5120]{1,0:T(8,128)(2,1)S(1)}, bf16[16,5120]{1,0:T(8,128)(2,1)S(1)}, u32[]{:S(2)}, u32[]{:S(2)}) collective-permute-start(bf16[16,5120]{1,0:T(8,128)(2,1)S(1)} %get-tuple-element.80), channel_id=1, source_target_pairs={{0,12},{1,13},{2,14},{3,15},{4,0},{5,1},{6,2},{7,3},{8,4},{9,5},{1... | collective-permute-start | bytes 491528 | tf_op jit(solution)/shard_map/ppermute | solution.py:24
  60.1 15.5 %collective-permute-start.19 = (bf16[176,512]{1,0:T(8,128)(2,1)S(1)}, bf16[176,512]{1,0:T(8,128)(2,1)S(1)}, u32[]{:S(2)}, u32[]{:S(2)}) collective-permute-start(bf16[176,512]{1,0:T(8,128)(2,1)S(1)} %get-tuple-element.71), channel_id=1, source_target_pairs={{0,18},{1,19},{2,16},{3,17},{4,22},{5,23},{6,20},{7,21},{8,26},{9,... | collective-permute-start | bytes 540680 | tf_op jit(solution)/shard_map/ppermute | solution.py:24
  61.9 13.7 %collective-permute-start.20 = (bf16[176,512]{1,0:T(8,128)(2,1)S(1)}, bf16[176,512]{1,0:T(8,128)(2,1)S(1)}, u32[]{:S(2)}, u32[]{:S(2)}) collective-permute-start(bf16[176,512]{1,0:T(8,128)(2,1)S(1)} %get-tuple-element.72), channel_id=1, source_target_pairs={{0,2},{1,3},{2,0},{3,1},{4,6},{5,7},{6,4},{7,5},{8,10},{9,11},{10,... | collective-permute-start | bytes 540680 | tf_op jit(solution)/shard_map/ppermute | solution.py:24
  64.3 11.3 %collective-permute-start.15 = (bf16[176,512]{1,0:T(8,128)(2,1)S(1)}, bf16[176,512]{1,0:T(8,128)(2,1)S(1)}, u32[]{:S(2)}, u32[]{:S(2)}) collective-permute-start(bf16[176,512]{1,0:T(8,128)(2,1)S(1)} %get-tuple-element.64), channel_id=1, source_target_pairs={{0,16},{1,17},{2,18},{3,19},{4,20},{5,21},{6,22},{7,23},{8,24},{9,... | collective-permute-start | bytes 540680 | tf_op jit(solution)/shard_map/ppermute | solution.py:24
  73.0 1.5 %collective-permute-start.26 = (bf16[16,2560]{1,0:T(8,128)(2,1)S(1)}, bf16[16,2560]{1,0:T(8,128)(2,1)S(1)}, u32[]{:S(2)}, u32[]{:S(2)}) collective-permute-start(bf16[16,2560]{1,0:T(8,128)(2,1)S(1)} %get-tuple-element.85.refs_0_), channel_id=1, source_target_pairs={{0,1},{1,0},{2,3},{3,2},{4,5},{5,4},{6,7},{7,6},{8,9},{9,8},{10,11... | collective-permute-start | bytes 245768 | tf_op jit(solution)/shard_map/ppermute | solution.py:24
  73.6 1.3 %collective-permute-start.27 = (bf16[16,2560]{1,0:T(8,128)(2,1)S(1)}, bf16[16,2560]{1,0:T(8,128)(2,1)S(1)}, u32[]{:S(2)}, u32[]{:S(2)}) collective-permute-start(bf16[16,2560]{1,0:T(8,128)(2,1)S(1)} %get-tuple-element.86.refs_1_), channel_id=1, source_target_pairs={{0,1},{1,0},{2,3},{3,2},{4,5},{5,4},{6,7},{7,6},{8,9},{9,8},{10,11... | collective-permute-start | bytes 245768 | tf_op jit(solution)/shard_map/ppermute | solution.py:24
  (3 other events, 2.2 us)

commit v22 on v21

--- a/solution.py
+++ b/solution.py
@@ -445,12 +445,13 @@
 
     sums = [chip[0]] + [
         moved(after(chip[k], ring[-1]), lambda g, z, s, r: (g, z - k, s, r))
-        for k in range(1, holders)
+        for k in reversed(range(1, holders))
     ]
     total = call(total_kernel, [jax.ShapeDtypeStruct((rows, cols // 2), BF16)] * 2, sums)
     totals = list(total)
     for dr in range(1, replicas):
         totals += [moved(x, lambda g, z, s, r: (g, z, s, r + dr)) for x in total]
+    totals[0], passed = lax.optimization_barrier((totals[0], passed))
     down_grad, up_grad = call(
         functools.partial(spread_kernel, width, replicas),
         [

time: 76.8 us -> 75.9 us (0.988)
  the two profiles are of different devices: /device:TPU:9 before, /device:TPU:0 now
where the time goes in v22:
time: 75.9 us; the launch traced here: 74.9 us
  starting transfers between devices  31.5 us (42%)
  waiting for transfers between devices  27.5 us (36%)
  Pallas kernels  9.73 us (13%)
  local copies, waits for them, and re-layouts  5.37 us (7%)
  between operations  0.82 us (1%)
    ppermute x28, starting transfers between devices, moved(): return lax.ppermute(x, AXES, pairs)  31.5 us
    ppermute x28, waiting for transfers between devices, moved(): return lax.ppermute(x, AXES, pairs)  27.5 us
    pallas_call x13, Pallas kernels, call(): pl.pallas_call(kernel, out_shape=out_shape, in_specs=[pl.BlockSpec(memory...  8.91 us
    unnamed x14, local copies, waits for them, and re-layouts  4.12 us
  transfers between devices with their start and end apart: 28, of which 11 were waited for; matrix products, arithmetic and copies ran while one was open for 0% of the time, Pallas kernels for 12%

profile of v22, /device:TPU:0, one launch (start us, length us, event | category | flops | bytes accessed | tf_op | source)
XLA Modules:
  0.0 74.9 jit_solution(13316756245124425595)
XLA Ops:
  0.6 1.2 %dynamic-slice_bitcast_fusion = bf16[256,1024]{1,0:T(8,128)(2,1)S(1)} fusion(bf16[1,1024,1024]{2,1,0:T(8,128)(2,1)} %param.11, s32[]{:T(128)S(6)} %select_n.3), kind=kLoop, calls=%fused_computation | loop fusion | bytes 1048580 | tf_op jit(solution)/shard_map/dynamic_slice | solution.py:302
  1.9 3.1 %collective-permute-start.4 = (bf16[256,1024]{1,0:T(8,128)(2,1)S(1)}, bf16[256,1024]{1,0:T(8,128)(2,1)S(1)}, u32[]{:S(2)}, u32[]{:S(2)}) collective-permute-start(bf16[256,1024]{1,0:T(8,128)(2,1)S(1)} %dynamic-slice_bitcast_fusion), channel_id=1, source_target_pairs={{0,4},{1,5},{2,6},{3,7},{4,8},{5,9},{6,10},{7,11},{8,12},{9,13},{1... | collective-permute-start | bytes 1572872 | tf_op jit(solution)/shard_map/ppermute | solution.py:24
  5.0 1.0 %copy-done.2 = bf16[1,176,1024]{2,1,0:T(8,128)(2,1)S(1)} copy-done((bf16[1,176,1024]{2,1,0:T(8,128)(2,1)S(1)}, bf16[1,176,1024]{2,1,0:T(8,128)(2,1)}, u32[]{:S(2)}) %copy-start.2) | copy-done | bytes 360472
  8.0 1.6 %collective-permute-start.3 = (bf16[176,1152]{1,0:T(8,128)(2,1)S(1)}, bf16[176,1152]{1,0:T(8,128)(2,1)S(1)}, u32[]{:S(2)}, u32[]{:S(2)}) collective-permute-start(bf16[176,1152]{1,0:T(8,128)(2,1)S(1)} %shard_map.94.refs_0_.refs_1_), channel_id=1, source_target_pairs={{0,16},{1,17},{2,18},{3,19},{4,20},{5,21},{6,22},{7,23},{8,24},{9,... | collective-permute-start | bytes 1216520 | tf_op jit(solution)/shard_map/ppermute | solution.py:24
  9.6 0.9 %copy-done.3 = bf16[1,2,16,4096]{3,2,1,0:T(8,128)(2,1)S(1)} copy-done((bf16[1,2,16,4096]{3,2,1,0:T(8,128)(2,1)S(1)}, bf16[1,2,16,4096]{3,2,1,0:T(8,128)(2,1)}, u32[]{:S(2)}) %copy-start.3) | copy-done | bytes 262168
  10.6 0.8 %copy-done.4 = bf16[1,2,16,1024]{3,2,1,0:T(8,128)(2,1)S(1)} copy-done((bf16[1,2,16,1024]{3,2,1,0:T(8,128)(2,1)S(1)}, bf16[1,2,16,1024]{3,2,1,0:T(8,128)(2,1)}, u32[]{:S(2)}) %copy-start.4) | copy-done | bytes 65560
  11.4 1.6 %collective-permute-start = (bf16[16,3072]{1,0:T(8,128)(2,1)S(1)}, bf16[16,3072]{1,0:T(8,128)(2,1)S(1)}, u32[]{:S(2)}, u32[]{:S(2)}) collective-permute-start(bf16[16,3072]{1,0:T(8,128)(2,1)S(1)} %shard_map.95.refs_0_), channel_id=1, source_target_pairs={{0,4},{1,5},{2,6},{3,7},{4,8},{5,9},{6,10},{7,11},{8,12},{9,13},{1... | collective-permute-start | bytes 294920 | tf_op jit(solution)/shard_map/ppermute | solution.py:24
  13.1 1.2 %collective-permute-start.1 = (bf16[16,3072]{1,0:T(8,128)(2,1)S(1)}, bf16[16,3072]{1,0:T(8,128)(2,1)S(1)}, u32[]{:S(2)}, u32[]{:S(2)}) collective-permute-start(bf16[16,3072]{1,0:T(8,128)(2,1)S(1)} %shard_map.95.refs_0_), channel_id=1, source_target_pairs={{0,8},{1,9},{2,10},{3,11},{4,12},{5,13},{6,14},{7,15},{8,0},{9,1},... | collective-permute-start | bytes 294920 | tf_op jit(solution)/shard_map/ppermute | solution.py:24
  14.3 2.7 %collective-permute-start.2 = (bf16[16,3072]{1,0:T(8,128)(2,1)S(1)}, bf16[16,3072]{1,0:T(8,128)(2,1)S(1)}, u32[]{:S(2)}, u32[]{:S(2)}) collective-permute-start(bf16[16,3072]{1,0:T(8,128)(2,1)S(1)} %shard_map.95.refs_0_), channel_id=1, source_target_pairs={{0,12},{1,13},{2,14},{3,15},{4,0},{5,1},{6,2},{7,3},{8,4},{9,5},{1... | collective-permute-start | bytes 294920 | tf_op jit(solution)/shard_map/ppermute | solution.py:24
  17.0 5.0 %collective-permute-done.refs_1_ = bf16[16,3072]{1,0:T(8,128)(2,1)S(1)} collective-permute-done((bf16[16,3072]{1,0:T(8,128)(2,1)S(1)}, bf16[16,3072]{1,0:T(8,128)(2,1)S(1)}, u32[]{:S(2)}, u32[]{:S(2)}) %collective-permute-start) | collective-permute-done | bytes 98336 | tf_op jit(solution)/shard_map/ppermute | solution.py:24
  22.0 3.4 %collective-permute-done.1.refs_2_ = bf16[16,3072]{1,0:T(8,128)(2,1)S(1)} collective-permute-done((bf16[16,3072]{1,0:T(8,128)(2,1)S(1)}, bf16[16,3072]{1,0:T(8,128)(2,1)S(1)}, u32[]{:S(2)}, u32[]{:S(2)}) %collective-permute-start.1) | collective-permute-done | bytes 98336 | tf_op jit(solution)/shard_map/ppermute | solution.py:24
  26.1 2.5 %collective-permute-start.17 = (bf16[256,1024]{1,0:T(8,128)(2,1)S(1)}, bf16[256,1024]{1,0:T(8,128)(2,1)S(1)}, u32[]{:S(2)}, u32[]{:S(2)}) collective-permute-start(bf16[256,1024]{1,0:T(8,128)(2,1)S(1)} %collective-permute-done.4.refs_5_), channel_id=1, source_target_pairs={{0,4},{1,5},{2,6},{3,7},{4,8},{5,9},{6,10},{7,11},{8,12},{9,13},{1... | collective-permute-start | bytes 1572872 | tf_op jit(solution)/shard_map/ppermute | solution.py:24
  28.6 2.2 %shard_map.97 = (bf16[176,1024]{1,0:T(8,128)(2,1)S(1)}, bf16[176,1024]{1,0:T(8,128)(2,1)S(1)}, bf16[352,128]{1,0:T(8,128)(2,1)S(1)}) custom-call(bf16[176,1152]{1,0:T(8,128)(2,1)S(1)} %shard_map.94.refs_0_.refs_1_, bf16[176,1152]{1,0:T(8,128)(2,1)S(1)} %collective-permute-done.3.refs_1_, bf16[64,3072]{1,0:T(8,128)(2,1)S(1)} %get-tuple-element.54.refs_2_.refs_3_, ...), custom_call_target="tpu_custom_call" | custom-call | flops 1000 | bytes 1000 | tf_op jit(solution)/shard_map/pallas_call | solution.py:41
  30.8 1.6 %collective-permute-start.9 = (bf16[176,1024]{1,0:T(8,128)(2,1)S(1)}, bf16[176,1024]{1,0:T(8,128)(2,1)S(1)}, u32[]{:S(2)}, u32[]{:S(2)}) collective-permute-start(bf16[176,1024]{1,0:T(8,128)(2,1)S(1)} %get-tuple-element.60), channel_id=1, source_target_pairs={{0,2},{1,3},{2,0},{3,1},{4,6},{5,7},{6,4},{7,5},{8,10},{9,11},{10,... | collective-permute-start | bytes 1081352 | tf_op jit(solution)/shard_map/ppermute | solution.py:24
  32.4 1.5 %collective-permute-start.10 = (bf16[176,1024]{1,0:T(8,128)(2,1)S(1)}, bf16[176,1024]{1,0:T(8,128)(2,1)S(1)}, u32[]{:S(2)}, u32[]{:S(2)}) collective-permute-start(bf16[176,1024]{1,0:T(8,128)(2,1)S(1)} %get-tuple-element.61), channel_id=1, source_target_pairs={{0,18},{1,19},{2,16},{3,17},{4,22},{5,23},{6,20},{7,21},{8,26},{9,... | collective-permute-start | bytes 1081352 | tf_op jit(solution)/shard_map/ppermute | solution.py:24
  34.4 2.9 %collective-permute-start.13 = (bf16[256,1024]{1,0:T(8,128)(2,1)S(1)}, bf16[256,1024]{1,0:T(8,128)(2,1)S(1)}, u32[]{:S(2)}, u32[]{:S(2)}) collective-permute-start(bf16[256,1024]{1,0:T(8,128)(2,1)S(1)} %dynamic-slice_bitcast_fusion), channel_id=1, source_target_pairs={{0,12},{1,13},{2,14},{3,15},{4,0},{5,1},{6,2},{7,3},{8,4},{9,5},{1... | collective-permute-start | bytes 1572872 | tf_op jit(solution)/shard_map/ppermute | solution.py:24
  37.3 4.6 %collective-permute-done.7.refs_5_ = bf16[64,2048]{1,0:T(8,128)(2,1)S(1)} collective-permute-done((bf16[64,2048]{1,0:T(8,128)(2,1)S(1)}, bf16[64,2048]{1,0:T(8,128)(2,1)S(1)}, u32[]{:S(2)}, u32[]{:S(2)}) %collective-permute-start.7) | collective-permute-done | bytes 262176 | tf_op jit(solution)/shard_map/ppermute | solution.py:24
  41.9 0.8 %collective-permute-done.17.block_ref.refs_5_ = bf16[256,1024]{1,0:T(8,128)(2,1)S(1)} collective-permute-done((bf16[256,1024]{1,0:T(8,128)(2,1)S(1)}, bf16[256,1024]{1,0:T(8,128)(2,1)S(1)}, u32[]{:S(2)}, u32[]{:S(2)}) %collective-permute-start.17) | collective-permute-done | bytes 524320 | tf_op jit(solution)/shard_map/ppermute | solution.py:24
  42.7 7.0 %collective-permute-done.10.refs_1_ = bf16[176,1024]{1,0:T(8,128)(2,1)S(1)} collective-permute-done((bf16[176,1024]{1,0:T(8,128)(2,1)S(1)}, bf16[176,1024]{1,0:T(8,128)(2,1)S(1)}, u32[]{:S(2)}, u32[]{:S(2)}) %collective-permute-start.10) | collective-permute-done | bytes 360480 | tf_op jit(solution)/shard_map/ppermute | solution.py:24
  50.2 1.3 %shard_map.98 = (f32[64,5120]{1,0:T(8,128)S(1)}, bf16[64,2560]{1,0:T(8,128)(2,1)S(1)}, bf16[64,2560]{1,0:T(8,128)(2,1)S(1)}) custom-call(bf16[176,4096]{1,0:T(8,128)(2,1)S(1)} %bitcast.12, bf16[176,1152]{1,0:T(8,128)(2,1)S(1)} %shard_map.94.refs_0_.refs_1_, bf16[352,128]{1,0:T(8,128)(2,1)S(1)} %get-tuple-element.56.refs_2_.refs_4_, ...), custom_call_target="tpu_custom_call" | custom-call | flops 1000 | bytes 1000 | tf_op jit(solution)/shard_map/pallas_call | solution.py:41
  51.6 1.2 %shard_map.102 = bf16[352,512]{1,0:T(8,128)(2,1)S(1)} custom-call(bf16[176,1152]{1,0:T(8,128)(2,1)S(1)} %shard_map.94.refs_0_.refs_1_, bf16[176,1152]{1,0:T(8,128)(2,1)S(1)} %collective-permute-done.3.refs_1_, bf16[64,3072]{1,0:T(8,128)(2,1)S(1)} %get-tuple-element.54.refs_2_.refs_3_, bf16[64,3072]{1,0:T(8,128)(2,1)S(1)} %collective-permute-done.5.refs_3_.refs_4_, ...), custom_call_target="tpu_custom_call" | custom-call | flops 1000 | bytes 1000 | tf_op jit(solution)/shard_map/pallas_call | solution.py:41
  52.8 1.6 %collective-permute-start.20 = (bf16[352,512]{1,0:T(8,128)(2,1)S(1)}, bf16[352,512]{1,0:T(8,128)(2,1)S(1)}, u32[]{:S(2)}, u32[]{:S(2)}) collective-permute-start(bf16[352,512]{1,0:T(8,128)(2,1)S(1)} %shard_map.102), channel_id=1, source_target_pairs={{0,2},{1,3},{2,0},{3,1},{4,6},{5,7},{6,4},{7,5},{8,10},{9,11},{10,... | collective-permute-start | bytes 1081352 | tf_op jit(solution)/shard_map/ppermute | solution.py:24
  56.6 2.2 %collective-permute-start.14 = (bf16[16,5120]{1,0:T(8,128)(2,1)S(1)}, bf16[16,5120]{1,0:T(8,128)(2,1)S(1)}, u32[]{:S(2)}, u32[]{:S(2)}) collective-permute-start(bf16[16,5120]{1,0:T(8,128)(2,1)S(1)} %get-tuple-element.69), channel_id=1, source_target_pairs={{0,4},{1,5},{2,6},{3,7},{4,8},{5,9},{6,10},{7,11},{8,12},{9,13},{1... | collective-permute-start | bytes 491528 | tf_op jit(solution)/shard_map/ppermute | solution.py:24
  58.8 1.7 %collective-permute-start.15 = (bf16[16,5120]{1,0:T(8,128)(2,1)S(1)}, bf16[16,5120]{1,0:T(8,128)(2,1)S(1)}, u32[]{:S(2)}, u32[]{:S(2)}) collective-permute-start(bf16[16,5120]{1,0:T(8,128)(2,1)S(1)} %get-tuple-element.71), channel_id=1, source_target_pairs={{0,8},{1,9},{2,10},{3,11},{4,12},{5,13},{6,14},{7,15},{8,0},{9,1},... | collective-permute-start | bytes 491528 | tf_op jit(solution)/shard_map/ppermute | solution.py:24
  60.5 0.8 %collective-permute-start.16 = (bf16[16,5120]{1,0:T(8,128)(2,1)S(1)}, bf16[16,5120]{1,0:T(8,128)(2,1)S(1)}, u32[]{:S(2)}, u32[]{:S(2)}) collective-permute-start(bf16[16,5120]{1,0:T(8,128)(2,1)S(1)} %get-tuple-element.73), channel_id=1, source_target_pairs={{0,12},{1,13},{2,14},{3,15},{4,0},{5,1},{6,2},{7,3},{8,4},{9,5},{1... | collective-permute-start | bytes 491528 | tf_op jit(solution)/shard_map/ppermute | solution.py:24
  61.2 1.2 %shard_map.105 = (bf16[176,512]{1,0:T(8,128)(2,1)S(1)}, bf16[176,512]{1,0:T(8,128)(2,1)S(1)}) custom-call(bf16[176,1152]{1,0:T(8,128)(2,1)S(1)} %shard_map.94.refs_0_.refs_1_, bf16[176,1152]{1,0:T(8,128)(2,1)S(1)} %collective-permute-done.3.refs_1_, bf16[64,3072]{1,0:T(8,128)(2,1)S(1)} %get-tuple-element.54.refs_2_.refs_3_, ...), custom_call_target="tpu_custom_call" | custom-call | flops 1000 | bytes 1000 | tf_op jit(solution)/shard_map/pallas_call | solution.py:41
  63.3 1.5 %collective-permute-start.25 = (bf16[176,512]{1,0:T(8,128)(2,1)S(1)}, bf16[176,512]{1,0:T(8,128)(2,1)S(1)}, u32[]{:S(2)}, u32[]{:S(2)}) collective-permute-start(bf16[176,512]{1,0:T(8,128)(2,1)S(1)} %get-tuple-element.86), channel_id=1, source_target_pairs={{0,2},{1,3},{2,0},{3,1},{4,6},{5,7},{6,4},{7,5},{8,10},{9,11},{10,... | collective-permute-start | bytes 540680 | tf_op jit(solution)/shard_map/ppermute | solution.py:24
  64.8 1.2 %shard_map.103.refs_3_ = bf16[176,4096]{1,0:T(8,128)(2,1)} custom-call(bf16[176,1024]{1,0:T(8,128)(2,1)S(1)} %collective-permute-done.9.refs_0_, bf16[176,1024]{1,0:T(8,128)(2,1)S(1)} %collective-permute-done.10.refs_1_, bf16[176,512]{1,0:T(8,128)(2,1)S(1)} %get-tuple-element.94.refs_2_), custom_call_target="tpu_custom_call" | custom-call | flops 1000 | bytes 1000 | tf_op jit(solution)/shard_map/pallas_call | solution.py:41
  66.0 1.2 %collective-permute-start.21 = (bf16[176,512]{1,0:T(8,128)(2,1)S(1)}, bf16[176,512]{1,0:T(8,128)(2,1)S(1)}, u32[]{:S(2)}, u32[]{:S(2)}) collective-permute-start(bf16[176,512]{1,0:T(8,128)(2,1)S(1)} %get-tuple-element.80), channel_id=1, source_target_pairs={{0,16},{1,17},{2,18},{3,19},{4,20},{5,21},{6,22},{7,23},{8,24},{9,... | collective-permute-start | bytes 540680 | tf_op jit(solution)/shard_map/ppermute | solution.py:24
  67.2 4.6 %collective-permute-done.15.refs_2_ = bf16[16,5120]{1,0:T(8,128)(2,1)S(1)} collective-permute-done((bf16[16,5120]{1,0:T(8,128)(2,1)S(1)}, bf16[16,5120]{1,0:T(8,128)(2,1)S(1)}, u32[]{:S(2)}, u32[]{:S(2)}) %collective-permute-start.15) | collective-permute-done | bytes 163872 | tf_op jit(solution)/shard_map/ppermute | solution.py:24
  72.5 0.8 %collective-permute-done.21.refs_0_ = bf16[176,512]{1,0:T(8,128)(2,1)S(1)} collective-permute-done((bf16[176,512]{1,0:T(8,128)(2,1)S(1)}, bf16[176,512]{1,0:T(8,128)(2,1)S(1)}, u32[]{:S(2)}, u32[]{:S(2)}) %collective-permute-start.21) | collective-permute-done | bytes 180256 | tf_op jit(solution)/shard_map/ppermute | solution.py:24
  73.3 0.8 %shard_map.106 = bf16[176,4096]{1,0:T(8,128)(2,1)} custom-call(bf16[176,512]{1,0:T(8,128)(2,1)S(1)} %collective-permute-done.21.refs_0_, bf16[176,512]{1,0:T(8,128)(2,1)S(1)} %collective-permute-done.24.refs_1_, bf16[176,512]{1,0:T(8,128)(2,1)S(1)} %collective-permute-done.25.refs_2_, ...), custom_call_target="tpu_custom_call", output_to_operand_aliasing={{}: (3, {})} | custom-call | flops 1000 | bytes 1000 | tf_op jit(solution)/shard_map/pallas_call | solution.py:426
  (54 shorter events, 8.5 us)
Async XLA Ops:
  0.6 27.9 %copy-start = (bf16[1,1024,1024]{2,1,0:T(8,128)(2,1)S(1)}, bf16[1,1024,1024]{2,1,0:T(8,128)(2,1)}, u32[]{:S(2)}) copy-start(bf16[1,1024,1024]{2,1,0:T(8,128)(2,1)} %param.11) | copy-start | bytes 6291460
  1.9 23.5 %collective-permute-start.4 = (bf16[256,1024]{1,0:T(8,128)(2,1)S(1)}, bf16[256,1024]{1,0:T(8,128)(2,1)S(1)}, u32[]{:S(2)}, u32[]{:S(2)}) collective-permute-start(bf16[256,1024]{1,0:T(8,128)(2,1)S(1)} %dynamic-slice_bitcast_fusion), channel_id=1, source_target_pairs={{0,4},{1,5},{2,6},{3,7},{4,8},{5,9},{6,10},{7,11},{8,12},{9,13},{1... | collective-permute-start | bytes 1572872 | tf_op jit(solution)/shard_map/ppermute | solution.py:24
  5.0 1.0 %copy-start.2 = (bf16[1,176,1024]{2,1,0:T(8,128)(2,1)S(1)}, bf16[1,176,1024]{2,1,0:T(8,128)(2,1)}, u32[]{:S(2)}) copy-start(bf16[1,176,1024]{2,1,0:T(8,128)(2,1)} %param.8) | copy-start | bytes 1081348
  8.0 17.3 %collective-permute-start.3 = (bf16[176,1152]{1,0:T(8,128)(2,1)S(1)}, bf16[176,1152]{1,0:T(8,128)(2,1)S(1)}, u32[]{:S(2)}, u32[]{:S(2)}) collective-permute-start(bf16[176,1152]{1,0:T(8,128)(2,1)S(1)} %shard_map.94.refs_0_.refs_1_), channel_id=1, source_target_pairs={{0,16},{1,17},{2,18},{3,19},{4,20},{5,21},{6,22},{7,23},{8,24},{9,... | collective-permute-start | bytes 1216520 | tf_op jit(solution)/shard_map/ppermute | solution.py:24
  9.6 0.9 %copy-start.3 = (bf16[1,2,16,4096]{3,2,1,0:T(8,128)(2,1)S(1)}, bf16[1,2,16,4096]{3,2,1,0:T(8,128)(2,1)}, u32[]{:S(2)}) copy-start(bf16[1,2,16,4096]{3,2,1,0:T(8,128)(2,1)} %param.12) | copy-start | bytes 786436
  11.4 10.5 %collective-permute-start = (bf16[16,3072]{1,0:T(8,128)(2,1)S(1)}, bf16[16,3072]{1,0:T(8,128)(2,1)S(1)}, u32[]{:S(2)}, u32[]{:S(2)}) collective-permute-start(bf16[16,3072]{1,0:T(8,128)(2,1)S(1)} %shard_map.95.refs_0_), channel_id=1, source_target_pairs={{0,4},{1,5},{2,6},{3,7},{4,8},{5,9},{6,10},{7,11},{8,12},{9,13},{1... | collective-permute-start | bytes 294920 | tf_op jit(solution)/shard_map/ppermute | solution.py:24
  13.1 12.3 %collective-permute-start.1 = (bf16[16,3072]{1,0:T(8,128)(2,1)S(1)}, bf16[16,3072]{1,0:T(8,128)(2,1)S(1)}, u32[]{:S(2)}, u32[]{:S(2)}) collective-permute-start(bf16[16,3072]{1,0:T(8,128)(2,1)S(1)} %shard_map.95.refs_0_), channel_id=1, source_target_pairs={{0,8},{1,9},{2,10},{3,11},{4,12},{5,13},{6,14},{7,15},{8,0},{9,1},... | collective-permute-start | bytes 294920 | tf_op jit(solution)/shard_map/ppermute | solution.py:24
  14.3 11.1 %collective-permute-start.2 = (bf16[16,3072]{1,0:T(8,128)(2,1)S(1)}, bf16[16,3072]{1,0:T(8,128)(2,1)S(1)}, u32[]{:S(2)}, u32[]{:S(2)}) collective-permute-start(bf16[16,3072]{1,0:T(8,128)(2,1)S(1)} %shard_map.95.refs_0_), channel_id=1, source_target_pairs={{0,12},{1,13},{2,14},{3,15},{4,0},{5,1},{6,2},{7,3},{8,4},{9,5},{1... | collective-permute-start | bytes 294920 | tf_op jit(solution)/shard_map/ppermute | solution.py:24
  25.4 3.2 %collective-permute-start.6 = (bf16[256,1024]{1,0:T(8,128)(2,1)S(1)}, bf16[256,1024]{1,0:T(8,128)(2,1)S(1)}, u32[]{:S(2)}, u32[]{:S(2)}) collective-permute-start(bf16[256,1024]{1,0:T(8,128)(2,1)S(1)} %collective-permute-done.4.refs_5_), channel_id=1, source_target_pairs={{0,1},{1,0},{2,3},{3,2},{4,5},{5,4},{6,7},{7,6},{8,9},{9,8},{10,11... | collective-permute-start | bytes 1572872 | tf_op jit(solution)/shard_map/ppermute | solution.py:24
  25.5 3.1 %collective-permute-start.5 = (bf16[64,3072]{1,0:T(8,128)(2,1)S(1)}, bf16[64,3072]{1,0:T(8,128)(2,1)S(1)}, u32[]{:S(2)}, u32[]{:S(2)}) collective-permute-start(bf16[64,3072]{1,0:T(8,128)(2,1)S(1)} %get-tuple-element.54.refs_2_.refs_3_), channel_id=1, source_target_pairs={{0,1},{1,0},{2,3},{3,2},{4,5},{5,4},{6,7},{7,6},{8,9},{9,8},{10,11... | collective-permute-start | bytes 1179656 | tf_op jit(solution)/shard_map/ppermute | solution.py:24
  26.1 16.6 %collective-permute-start.17 = (bf16[256,1024]{1,0:T(8,128)(2,1)S(1)}, bf16[256,1024]{1,0:T(8,128)(2,1)S(1)}, u32[]{:S(2)}, u32[]{:S(2)}) collective-permute-start(bf16[256,1024]{1,0:T(8,128)(2,1)S(1)} %collective-permute-done.4.refs_5_), channel_id=1, source_target_pairs={{0,4},{1,5},{2,6},{3,7},{4,8},{5,9},{6,10},{7,11},{8,12},{9,13},{1... | collective-permute-start | bytes 1572872 | tf_op jit(solution)/shard_map/ppermute | solution.py:24
  28.6 21.6 %copy-start.1 = (bf16[1,176,4096]{2,1,0:T(8,128)(2,1)S(1)}, bf16[1,176,4096]{2,1,0:T(8,128)(2,1)}, u32[]{:S(2)}) copy-start(bf16[1,176,4096]{2,1,0:T(8,128)(2,1)} %param.7) | copy-start | bytes 4325380
  30.8 11.9 %collective-permute-start.9 = (bf16[176,1024]{1,0:T(8,128)(2,1)S(1)}, bf16[176,1024]{1,0:T(8,128)(2,1)S(1)}, u32[]{:S(2)}, u32[]{:S(2)}) collective-permute-start(bf16[176,1024]{1,0:T(8,128)(2,1)S(1)} %get-tuple-element.60), channel_id=1, source_target_pairs={{0,2},{1,3},{2,0},{3,1},{4,6},{5,7},{6,4},{7,5},{8,10},{9,11},{10,... | collective-permute-start | bytes 1081352 | tf_op jit(solution)/shard_map/ppermute | solution.py:24
  32.4 17.3 %collective-permute-start.10 = (bf16[176,1024]{1,0:T(8,128)(2,1)S(1)}, bf16[176,1024]{1,0:T(8,128)(2,1)S(1)}, u32[]{:S(2)}, u32[]{:S(2)}) collective-permute-start(bf16[176,1024]{1,0:T(8,128)(2,1)S(1)} %get-tuple-element.61), channel_id=1, source_target_pairs={{0,18},{1,19},{2,16},{3,17},{4,22},{5,23},{6,20},{7,21},{8,26},{9,... | collective-permute-start | bytes 1081352 | tf_op jit(solution)/shard_map/ppermute | solution.py:24
  33.9 8.0 %collective-permute-start.7 = (bf16[64,2048]{1,0:T(8,128)(2,1)S(1)}, bf16[64,2048]{1,0:T(8,128)(2,1)S(1)}, u32[]{:S(2)}, u32[]{:S(2)}) collective-permute-start(bf16[64,2048]{1,0:T(8,128)(2,1)S(1)} %get-tuple-element.57), channel_id=1, source_target_pairs={{0,16},{1,17},{2,18},{3,19},{4,20},{5,21},{6,22},{7,23},{8,24},{9,... | collective-permute-start | bytes 786440 | tf_op jit(solution)/shard_map/ppermute | solution.py:24
  34.4 20.5 %collective-permute-start.13 = (bf16[256,1024]{1,0:T(8,128)(2,1)S(1)}, bf16[256,1024]{1,0:T(8,128)(2,1)S(1)}, u32[]{:S(2)}, u32[]{:S(2)}) collective-permute-start(bf16[256,1024]{1,0:T(8,128)(2,1)S(1)} %dynamic-slice_bitcast_fusion), channel_id=1, source_target_pairs={{0,12},{1,13},{2,14},{3,15},{4,0},{5,1},{6,2},{7,3},{8,4},{9,5},{1... | collective-permute-start | bytes 1572872 | tf_op jit(solution)/shard_map/ppermute | solution.py:24
  41.9 8.3 %collective-permute-start.8 = (bf16[64,2048]{1,0:T(8,128)(2,1)S(1)}, bf16[64,2048]{1,0:T(8,128)(2,1)S(1)}, u32[]{:S(2)}, u32[]{:S(2)}) collective-permute-start(bf16[64,2048]{1,0:T(8,128)(2,1)S(1)} %collective-permute-done.7.refs_5_), channel_id=1, source_target_pairs={{0,1},{1,0},{2,3},{3,2},{4,5},{5,4},{6,7},{7,6},{8,9},{9,8},{10,11... | collective-permute-start | bytes 786440 | tf_op jit(solution)/shard_map/ppermute | solution.py:24
  49.7 1.8 %collective-permute-start.18 = (bf16[128,1024]{1,0:T(8,128)(2,1)S(1)}, bf16[128,1024]{1,0:T(8,128)(2,1)S(1)}, u32[]{:S(2)}, u32[]{:S(2)}) collective-permute-start(bf16[128,1024]{1,0:T(8,128)(2,1)S(1)} %get-tuple-element.77), channel_id=1, source_target_pairs={{0,1},{1,0},{2,3},{3,2},{4,5},{5,4},{6,7},{7,6},{8,9},{9,8},{10,11... | collective-permute-start | bytes 786440 | tf_op jit(solution)/shard_map/ppermute | solution.py:24
  49.7 1.9 %collective-permute-start.19 = (bf16[128,1024]{1,0:T(8,128)(2,1)S(1)}, bf16[128,1024]{1,0:T(8,128)(2,1)S(1)}, u32[]{:S(2)}, u32[]{:S(2)}) collective-permute-start(bf16[128,1024]{1,0:T(8,128)(2,1)S(1)} %get-tuple-element.79), channel_id=1, source_target_pairs={{0,1},{1,0},{2,3},{3,2},{4,5},{5,4},{6,7},{7,6},{8,9},{9,8},{10,11... | collective-permute-start | bytes 786440 | tf_op jit(solution)/shard_map/ppermute | solution.py:24
  52.8 10.5 %collective-permute-start.20 = (bf16[352,512]{1,0:T(8,128)(2,1)S(1)}, bf16[352,512]{1,0:T(8,128)(2,1)S(1)}, u32[]{:S(2)}, u32[]{:S(2)}) collective-permute-start(bf16[352,512]{1,0:T(8,128)(2,1)S(1)} %shard_map.102), channel_id=1, source_target_pairs={{0,2},{1,3},{2,0},{3,1},{4,6},{5,7},{6,4},{7,5},{8,10},{9,11},{10,... | collective-permute-start | bytes 1081352 | tf_op jit(solution)/shard_map/ppermute | solution.py:24
  54.3 1.6 %collective-permute-start.11 = (bf16[64,2560]{1,0:T(8,128)(2,1)S(1)}, bf16[64,2560]{1,0:T(8,128)(2,1)S(1)}, u32[]{:S(2)}, u32[]{:S(2)}) collective-permute-start(bf16[64,2560]{1,0:T(8,128)(2,1)S(1)} %get-tuple-element.62), channel_id=1, source_target_pairs={{0,1},{1,0},{2,3},{3,2},{4,5},{5,4},{6,7},{7,6},{8,9},{9,8},{10,11... | collective-permute-start | bytes 983048 | tf_op jit(solution)/shard_map/ppermute | solution.py:24
  54.3 2.1 %collective-permute-start.12 = (bf16[64,2560]{1,0:T(8,128)(2,1)S(1)}, bf16[64,2560]{1,0:T(8,128)(2,1)S(1)}, u32[]{:S(2)}, u32[]{:S(2)}) collective-permute-start(bf16[64,2560]{1,0:T(8,128)(2,1)S(1)} %get-tuple-element.64), channel_id=1, source_target_pairs={{0,1},{1,0},{2,3},{3,2},{4,5},{5,4},{6,7},{7,6},{8,9},{9,8},{10,11... | collective-permute-start | bytes 983048 | tf_op jit(solution)/shard_map/ppermute | solution.py:24
  54.9 5.6 %collective-permute-start.22 = (bf16[128,1024]{1,0:T(8,128)(2,1)S(1)}, bf16[128,1024]{1,0:T(8,128)(2,1)S(1)}, u32[]{:S(2)}, u32[]{:S(2)}) collective-permute-start(bf16[128,1024]{1,0:T(8,128)(2,1)S(1)} %get-tuple-element.82), channel_id=1, source_target_pairs={{0,1},{1,0},{2,3},{3,2},{4,5},{5,4},{6,7},{7,6},{8,9},{9,8},{10,11... | collective-permute-start | bytes 786440 | tf_op jit(solution)/shard_map/ppermute | solution.py:24
  55.0 6.3 %collective-permute-start.23 = (bf16[128,1024]{1,0:T(8,128)(2,1)S(1)}, bf16[128,1024]{1,0:T(8,128)(2,1)S(1)}, u32[]{:S(2)}, u32[]{:S(2)}) collective-permute-start(bf16[128,1024]{1,0:T(8,128)(2,1)S(1)} %get-tuple-element.84), channel_id=1, source_target_pairs={{0,1},{1,0},{2,3},{3,2},{4,5},{5,4},{6,7},{7,6},{8,9},{9,8},{10,11... | collective-permute-start | bytes 786440 | tf_op jit(solution)/shard_map/ppermute | solution.py:24
  56.6 9.4 %collective-permute-start.14 = (bf16[16,5120]{1,0:T(8,128)(2,1)S(1)}, bf16[16,5120]{1,0:T(8,128)(2,1)S(1)}, u32[]{:S(2)}, u32[]{:S(2)}) collective-permute-start(bf16[16,5120]{1,0:T(8,128)(2,1)S(1)} %get-tuple-element.69), channel_id=1, source_target_pairs={{0,4},{1,5},{2,6},{3,7},{4,8},{5,9},{6,10},{7,11},{8,12},{9,13},{1... | collective-permute-start | bytes 491528 | tf_op jit(solution)/shard_map/ppermute | solution.py:24
  58.8 13.0 %collective-permute-start.15 = (bf16[16,5120]{1,0:T(8,128)(2,1)S(1)}, bf16[16,5120]{1,0:T(8,128)(2,1)S(1)}, u32[]{:S(2)}, u32[]{:S(2)}) collective-permute-start(bf16[16,5120]{1,0:T(8,128)(2,1)S(1)} %get-tuple-element.71), channel_id=1, source_target_pairs={{0,8},{1,9},{2,10},{3,11},{4,12},{5,13},{6,14},{7,15},{8,0},{9,1},... | collective-permute-start | bytes 491528 | tf_op jit(solution)/shard_map/ppermute | solution.py:24
  60.5 11.3 %collective-permute-start.16 = (bf16[16,5120]{1,0:T(8,128)(2,1)S(1)}, bf16[16,5120]{1,0:T(8,128)(2,1)S(1)}, u32[]{:S(2)}, u32[]{:S(2)}) collective-permute-start(bf16[16,5120]{1,0:T(8,128)(2,1)S(1)} %get-tuple-element.73), channel_id=1, source_target_pairs={{0,12},{1,13},{2,14},{3,15},{4,0},{5,1},{6,2},{7,3},{8,4},{9,5},{1... | collective-permute-start | bytes 491528 | tf_op jit(solution)/shard_map/ppermute | solution.py:24
  62.4 10.0 %collective-permute-start.24 = (bf16[176,512]{1,0:T(8,128)(2,1)S(1)}, bf16[176,512]{1,0:T(8,128)(2,1)S(1)}, u32[]{:S(2)}, u32[]{:S(2)}) collective-permute-start(bf16[176,512]{1,0:T(8,128)(2,1)S(1)} %get-tuple-element.85), channel_id=1, source_target_pairs={{0,18},{1,19},{2,16},{3,17},{4,22},{5,23},{6,20},{7,21},{8,26},{9,... | collective-permute-start | bytes 540680 | tf_op jit(solution)/shard_map/ppermute | solution.py:24
  63.3 9.2 %collective-permute-start.25 = (bf16[176,512]{1,0:T(8,128)(2,1)S(1)}, bf16[176,512]{1,0:T(8,128)(2,1)S(1)}, u32[]{:S(2)}, u32[]{:S(2)}) collective-permute-start(bf16[176,512]{1,0:T(8,128)(2,1)S(1)} %get-tuple-element.86), channel_id=1, source_target_pairs={{0,2},{1,3},{2,0},{3,1},{4,6},{5,7},{6,4},{7,5},{8,10},{9,11},{10,... | collective-permute-start | bytes 540680 | tf_op jit(solution)/shard_map/ppermute | solution.py:24
  66.0 7.3 %collective-permute-start.21 = (bf16[176,512]{1,0:T(8,128)(2,1)S(1)}, bf16[176,512]{1,0:T(8,128)(2,1)S(1)}, u32[]{:S(2)}, u32[]{:S(2)}) collective-permute-start(bf16[176,512]{1,0:T(8,128)(2,1)S(1)} %get-tuple-element.80), channel_id=1, source_target_pairs={{0,16},{1,17},{2,18},{3,19},{4,20},{5,21},{6,22},{7,23},{8,24},{9,... | collective-permute-start | bytes 540680 | tf_op jit(solution)/shard_map/ppermute | solution.py:24
  71.9 2.2 %collective-permute-start.26 = (bf16[16,2560]{1,0:T(8,128)(2,1)S(1)}, bf16[16,2560]{1,0:T(8,128)(2,1)S(1)}, u32[]{:S(2)}, u32[]{:S(2)}) collective-permute-start(bf16[16,2560]{1,0:T(8,128)(2,1)S(1)} %get-tuple-element.89.refs_0_), channel_id=1, source_target_pairs={{0,1},{1,0},{2,3},{3,2},{4,5},{5,4},{6,7},{7,6},{8,9},{9,8},{10,11... | collective-permute-start | bytes 245768 | tf_op jit(solution)/shard_map/ppermute | solution.py:24
  72.0 2.2 %collective-permute-start.27 = (bf16[16,2560]{1,0:T(8,128)(2,1)S(1)}, bf16[16,2560]{1,0:T(8,128)(2,1)S(1)}, u32[]{:S(2)}, u32[]{:S(2)}) collective-permute-start(bf16[16,2560]{1,0:T(8,128)(2,1)S(1)} %get-tuple-element.90.refs_1_), channel_id=1, source_target_pairs={{0,1},{1,0},{2,3},{3,2},{4,5},{5,4},{6,7},{7,6},{8,9},{9,8},{10,11... | collective-permute-start | bytes 245768 | tf_op jit(solution)/shard_map/ppermute | solution.py:24
  (3 other events, 2.2 us)

commit v23 on v22

--- a/solution.py
+++ b/solution.py
@@ -397,7 +397,7 @@
             sel = out[groups]
         mails = list(out[:groups])
         if i == 1 and len(batches) > 2:
-            got = moved(out[0], lambda g, z, s, r: (g, z, s - 1, r))
+            got = moved(after(out[0], chip[0]), lambda g, z, s, r: (g, z, s - 1, r))
             got = [got[dg * tokens : (dg + 1) * tokens] for dg in range(groups)]
             early = [(batches[0], dg) for dg in range(groups)] + [(batch, 0)]
             passed = call(

time: 75.9 us -> 75.5 us (level)
  starting transfers between devices: 31.5 us -> 34.2 us
  waiting for transfers between devices: 27.5 us -> 25.1 us
    ppermute x28, starting transfers between devices: 31.5 us -> 34.2 us  [moved(): return lax.ppermute(x, AXES, pairs)]
    ppermute x28, waiting for transfers between devices: 27.5 us -> 25.1 us  [moved(): return lax.ppermute(x, AXES, pairs)]
  transfers between devices with their start and end apart: 28 -> 28, of which waited for: 11 -> 10; matrix products, arithmetic and copies ran while one was open for 0% -> 0% of each run, Pallas kernels for 12% -> 12%
where the time goes in v23:
time: 75.5 us; the launch traced here: 75.2 us
  starting transfers between devices  34.2 us (45%)
  waiting for transfers between devices  25.1 us (33%)
  Pallas kernels  9.73 us (13%)
  local copies, waits for them, and re-layouts  5.37 us (7%)
  between operations  0.83 us (1%)
    ppermute x28, starting transfers between devices, moved(): return lax.ppermute(x, AXES, pairs)  34.2 us
    ppermute x28, waiting for transfers between devices, moved(): return lax.ppermute(x, AXES, pairs)  25.1 us
    pallas_call x13, Pallas kernels, call(): pl.pallas_call(kernel, out_shape=out_shape, in_specs=[pl.BlockSpec(memory...  8.92 us
    unnamed x14, local copies, waits for them, and re-layouts  4.12 us
  transfers between devices with their start and end apart: 28, of which 10 were waited for; matrix products, arithmetic and copies ran while one was open for 0% of the time, Pallas kernels for 12%

profile of v23, /device:TPU:0, one launch (start us, length us, event | category | flops | bytes accessed | tf_op | source)
XLA Modules:
  0.0 75.2 jit_solution(6889336639542408035)
XLA Ops:
  0.6 1.2 %dynamic-slice_bitcast_fusion = bf16[256,1024]{1,0:T(8,128)(2,1)S(1)} fusion(bf16[1,1024,1024]{2,1,0:T(8,128)(2,1)} %param.11, s32[]{:T(128)S(6)} %select_n.3), kind=kLoop, calls=%fused_computation | loop fusion | bytes 1048580 | tf_op jit(solution)/shard_map/dynamic_slice | solution.py:302
  1.9 3.1 %collective-permute-start.4 = (bf16[256,1024]{1,0:T(8,128)(2,1)S(1)}, bf16[256,1024]{1,0:T(8,128)(2,1)S(1)}, u32[]{:S(2)}, u32[]{:S(2)}) collective-permute-start(bf16[256,1024]{1,0:T(8,128)(2,1)S(1)} %dynamic-slice_bitcast_fusion), channel_id=1, source_target_pairs={{0,4},{1,5},{2,6},{3,7},{4,8},{5,9},{6,10},{7,11},{8,12},{9,13},{1... | collective-permute-start | bytes 1572872 | tf_op jit(solution)/shard_map/ppermute | solution.py:24
  5.0 1.0 %copy-done.2 = bf16[1,176,1024]{2,1,0:T(8,128)(2,1)S(1)} copy-done((bf16[1,176,1024]{2,1,0:T(8,128)(2,1)S(1)}, bf16[1,176,1024]{2,1,0:T(8,128)(2,1)}, u32[]{:S(2)}) %copy-start.2) | copy-done | bytes 360472
  8.0 1.6 %collective-permute-start.3 = (bf16[176,1152]{1,0:T(8,128)(2,1)S(1)}, bf16[176,1152]{1,0:T(8,128)(2,1)S(1)}, u32[]{:S(2)}, u32[]{:S(2)}) collective-permute-start(bf16[176,1152]{1,0:T(8,128)(2,1)S(1)} %shard_map.94.refs_0_.refs_1_), channel_id=1, source_target_pairs={{0,16},{1,17},{2,18},{3,19},{4,20},{5,21},{6,22},{7,23},{8,24},{9,... | collective-permute-start | bytes 1216520 | tf_op jit(solution)/shard_map/ppermute | solution.py:24
  9.6 0.9 %copy-done.3 = bf16[1,2,16,4096]{3,2,1,0:T(8,128)(2,1)S(1)} copy-done((bf16[1,2,16,4096]{3,2,1,0:T(8,128)(2,1)S(1)}, bf16[1,2,16,4096]{3,2,1,0:T(8,128)(2,1)}, u32[]{:S(2)}) %copy-start.3) | copy-done | bytes 262168
  11.4 1.6 %collective-permute-start = (bf16[16,3072]{1,0:T(8,128)(2,1)S(1)}, bf16[16,3072]{1,0:T(8,128)(2,1)S(1)}, u32[]{:S(2)}, u32[]{:S(2)}) collective-permute-start(bf16[16,3072]{1,0:T(8,128)(2,1)S(1)} %shard_map.95.refs_0_), channel_id=1, source_target_pairs={{0,4},{1,5},{2,6},{3,7},{4,8},{5,9},{6,10},{7,11},{8,12},{9,13},{1... | collective-permute-start | bytes 294920 | tf_op jit(solution)/shard_map/ppermute | solution.py:24
  13.1 1.2 %collective-permute-start.1 = (bf16[16,3072]{1,0:T(8,128)(2,1)S(1)}, bf16[16,3072]{1,0:T(8,128)(2,1)S(1)}, u32[]{:S(2)}, u32[]{:S(2)}) collective-permute-start(bf16[16,3072]{1,0:T(8,128)(2,1)S(1)} %shard_map.95.refs_0_), channel_id=1, source_target_pairs={{0,8},{1,9},{2,10},{3,11},{4,12},{5,13},{6,14},{7,15},{8,0},{9,1},... | collective-permute-start | bytes 294920 | tf_op jit(solution)/shard_map/ppermute | solution.py:24
  14.3 2.7 %collective-permute-start.2 = (bf16[16,3072]{1,0:T(8,128)(2,1)S(1)}, bf16[16,3072]{1,0:T(8,128)(2,1)S(1)}, u32[]{:S(2)}, u32[]{:S(2)}) collective-permute-start(bf16[16,3072]{1,0:T(8,128)(2,1)S(1)} %shard_map.95.refs_0_), channel_id=1, source_target_pairs={{0,12},{1,13},{2,14},{3,15},{4,0},{5,1},{6,2},{7,3},{8,4},{9,5},{1... | collective-permute-start | bytes 294920 | tf_op jit(solution)/shard_map/ppermute | solution.py:24
  17.0 5.0 %collective-permute-done.refs_1_ = bf16[16,3072]{1,0:T(8,128)(2,1)S(1)} collective-permute-done((bf16[16,3072]{1,0:T(8,128)(2,1)S(1)}, bf16[16,3072]{1,0:T(8,128)(2,1)S(1)}, u32[]{:S(2)}, u32[]{:S(2)}) %collective-permute-start) | collective-permute-done | bytes 98336 | tf_op jit(solution)/shard_map/ppermute | solution.py:24
  22.0 3.4 %collective-permute-done.1.refs_2_ = bf16[16,3072]{1,0:T(8,128)(2,1)S(1)} collective-permute-done((bf16[16,3072]{1,0:T(8,128)(2,1)S(1)}, bf16[16,3072]{1,0:T(8,128)(2,1)S(1)}, u32[]{:S(2)}, u32[]{:S(2)}) %collective-permute-start.1) | collective-permute-done | bytes 98336 | tf_op jit(solution)/shard_map/ppermute | solution.py:24
  26.1 1.5 %collective-permute-start.7 = (bf16[64,2048]{1,0:T(8,128)(2,1)S(1)}, bf16[64,2048]{1,0:T(8,128)(2,1)S(1)}, u32[]{:S(2)}, u32[]{:S(2)}) collective-permute-start(bf16[64,2048]{1,0:T(8,128)(2,1)S(1)} %get-tuple-element.58), channel_id=1, source_target_pairs={{0,16},{1,17},{2,18},{3,19},{4,20},{5,21},{6,22},{7,23},{8,24},{9,... | collective-permute-start | bytes 786440 | tf_op jit(solution)/shard_map/ppermute | solution.py:24
  27.6 2.5 %collective-permute-start.17 = (bf16[256,1024]{1,0:T(8,128)(2,1)S(1)}, bf16[256,1024]{1,0:T(8,128)(2,1)S(1)}, u32[]{:S(2)}, u32[]{:S(2)}) collective-permute-start(bf16[256,1024]{1,0:T(8,128)(2,1)S(1)} %collective-permute-done.4.refs_5_), channel_id=1, source_target_pairs={{0,4},{1,5},{2,6},{3,7},{4,8},{5,9},{6,10},{7,11},{8,12},{9,13},{1... | collective-permute-start | bytes 1572872 | tf_op jit(solution)/shard_map/ppermute | solution.py:24
  30.1 2.2 %shard_map.97 = (bf16[176,1024]{1,0:T(8,128)(2,1)S(1)}, bf16[176,1024]{1,0:T(8,128)(2,1)S(1)}, bf16[352,128]{1,0:T(8,128)(2,1)S(1)}) custom-call(bf16[176,1152]{1,0:T(8,128)(2,1)S(1)} %shard_map.94.refs_0_.refs_1_, bf16[176,1152]{1,0:T(8,128)(2,1)S(1)} %collective-permute-done.3.refs_1_, bf16[64,3072]{1,0:T(8,128)(2,1)S(1)} %get-tuple-element.55.refs_2_.refs_3_, ...), custom_call_target="tpu_custom_call" | custom-call | flops 1000 | bytes 1000 | tf_op jit(solution)/shard_map/pallas_call | solution.py:41
  32.4 1.6 %collective-permute-start.9 = (bf16[176,1024]{1,0:T(8,128)(2,1)S(1)}, bf16[176,1024]{1,0:T(8,128)(2,1)S(1)}, u32[]{:S(2)}, u32[]{:S(2)}) collective-permute-start(bf16[176,1024]{1,0:T(8,128)(2,1)S(1)} %get-tuple-element.61), channel_id=1, source_target_pairs={{0,2},{1,3},{2,0},{3,1},{4,6},{5,7},{6,4},{7,5},{8,10},{9,11},{10,... | collective-permute-start | bytes 1081352 | tf_op jit(solution)/shard_map/ppermute | solution.py:24
  34.4 3.5 %collective-permute-start.13 = (bf16[256,1024]{1,0:T(8,128)(2,1)S(1)}, bf16[256,1024]{1,0:T(8,128)(2,1)S(1)}, u32[]{:S(2)}, u32[]{:S(2)}) collective-permute-start(bf16[256,1024]{1,0:T(8,128)(2,1)S(1)} %dynamic-slice_bitcast_fusion), channel_id=1, source_target_pairs={{0,12},{1,13},{2,14},{3,15},{4,0},{5,1},{6,2},{7,3},{8,4},{9,5},{1... | collective-permute-start | bytes 1572872 | tf_op jit(solution)/shard_map/ppermute | solution.py:24
  38.0 1.3 %shard_map.98 = (f32[64,5120]{1,0:T(8,128)S(1)}, bf16[64,2560]{1,0:T(8,128)(2,1)S(1)}, bf16[64,2560]{1,0:T(8,128)(2,1)S(1)}) custom-call(bf16[176,4096]{1,0:T(8,128)(2,1)S(1)} %bitcast.12, bf16[176,1152]{1,0:T(8,128)(2,1)S(1)} %shard_map.94.refs_0_.refs_1_, bf16[352,128]{1,0:T(8,128)(2,1)S(1)} %get-tuple-element.57.refs_2_.refs_4_, ...), custom_call_target="tpu_custom_call" | custom-call | flops 1000 | bytes 1000 | tf_op jit(solution)/shard_map/pallas_call | solution.py:41
  39.3 4.5 %collective-permute-done.9.refs_0_ = bf16[176,1024]{1,0:T(8,128)(2,1)S(1)} collective-permute-done((bf16[176,1024]{1,0:T(8,128)(2,1)S(1)}, bf16[176,1024]{1,0:T(8,128)(2,1)S(1)}, u32[]{:S(2)}, u32[]{:S(2)}) %collective-permute-start.9) | collective-permute-done | bytes 360480 | tf_op jit(solution)/shard_map/ppermute | solution.py:24
  43.8 6.2 %collective-permute-done.10.refs_1_ = bf16[176,1024]{1,0:T(8,128)(2,1)S(1)} collective-permute-done((bf16[176,1024]{1,0:T(8,128)(2,1)S(1)}, bf16[176,1024]{1,0:T(8,128)(2,1)S(1)}, u32[]{:S(2)}, u32[]{:S(2)}) %collective-permute-start.10) | collective-permute-done | bytes 360480 | tf_op jit(solution)/shard_map/ppermute | solution.py:24
  51.1 1.3 %collective-permute-done.18.refs_6_ = bf16[128,1024]{1,0:T(8,128)(2,1)S(1)} collective-permute-done((bf16[128,1024]{1,0:T(8,128)(2,1)S(1)}, bf16[128,1024]{1,0:T(8,128)(2,1)S(1)}, u32[]{:S(2)}, u32[]{:S(2)}) %collective-permute-start.18) | collective-permute-done | bytes 262176 | tf_op jit(solution)/shard_map/ppermute | solution.py:24
  52.8 1.2 %shard_map.102 = bf16[352,512]{1,0:T(8,128)(2,1)S(1)} custom-call(bf16[176,1152]{1,0:T(8,128)(2,1)S(1)} %shard_map.94.refs_0_.refs_1_, bf16[176,1152]{1,0:T(8,128)(2,1)S(1)} %collective-permute-done.3.refs_1_, bf16[64,3072]{1,0:T(8,128)(2,1)S(1)} %get-tuple-element.55.refs_2_.refs_3_, bf16[64,3072]{1,0:T(8,128)(2,1)S(1)} %collective-permute-done.5.refs_3_.refs_4_, ...), custom_call_target="tpu_custom_call" | custom-call | flops 1000 | bytes 1000 | tf_op jit(solution)/shard_map/pallas_call | solution.py:41
  54.1 1.6 %collective-permute-start.20 = (bf16[352,512]{1,0:T(8,128)(2,1)S(1)}, bf16[352,512]{1,0:T(8,128)(2,1)S(1)}, u32[]{:S(2)}, u32[]{:S(2)}) collective-permute-start(bf16[352,512]{1,0:T(8,128)(2,1)S(1)} %shard_map.102), channel_id=1, source_target_pairs={{0,2},{1,3},{2,0},{3,1},{4,6},{5,7},{6,4},{7,5},{8,10},{9,11},{10,... | collective-permute-start | bytes 1081352 | tf_op jit(solution)/shard_map/ppermute | solution.py:24
  56.3 1.9 %collective-permute-start.14 = (bf16[16,5120]{1,0:T(8,128)(2,1)S(1)}, bf16[16,5120]{1,0:T(8,128)(2,1)S(1)}, u32[]{:S(2)}, u32[]{:S(2)}) collective-permute-start(bf16[16,5120]{1,0:T(8,128)(2,1)S(1)} %get-tuple-element.70), channel_id=1, source_target_pairs={{0,4},{1,5},{2,6},{3,7},{4,8},{5,9},{6,10},{7,11},{8,12},{9,13},{1... | collective-permute-start | bytes 491528 | tf_op jit(solution)/shard_map/ppermute | solution.py:24
  58.2 1.7 %collective-permute-start.15 = (bf16[16,5120]{1,0:T(8,128)(2,1)S(1)}, bf16[16,5120]{1,0:T(8,128)(2,1)S(1)}, u32[]{:S(2)}, u32[]{:S(2)}) collective-permute-start(bf16[16,5120]{1,0:T(8,128)(2,1)S(1)} %get-tuple-element.72), channel_id=1, source_target_pairs={{0,8},{1,9},{2,10},{3,11},{4,12},{5,13},{6,14},{7,15},{8,0},{9,1},... | collective-permute-start | bytes 491528 | tf_op jit(solution)/shard_map/ppermute | solution.py:24
  59.9 1.0 %collective-permute-start.16 = (bf16[16,5120]{1,0:T(8,128)(2,1)S(1)}, bf16[16,5120]{1,0:T(8,128)(2,1)S(1)}, u32[]{:S(2)}, u32[]{:S(2)}) collective-permute-start(bf16[16,5120]{1,0:T(8,128)(2,1)S(1)} %get-tuple-element.74), channel_id=1, source_target_pairs={{0,12},{1,13},{2,14},{3,15},{4,0},{5,1},{6,2},{7,3},{8,4},{9,5},{1... | collective-permute-start | bytes 491528 | tf_op jit(solution)/shard_map/ppermute | solution.py:24
  60.9 1.2 %shard_map.105 = (bf16[176,512]{1,0:T(8,128)(2,1)S(1)}, bf16[176,512]{1,0:T(8,128)(2,1)S(1)}) custom-call(bf16[176,1152]{1,0:T(8,128)(2,1)S(1)} %shard_map.94.refs_0_.refs_1_, bf16[176,1152]{1,0:T(8,128)(2,1)S(1)} %collective-permute-done.3.refs_1_, bf16[64,3072]{1,0:T(8,128)(2,1)S(1)} %get-tuple-element.55.refs_2_.refs_3_, ...), custom_call_target="tpu_custom_call" | custom-call | flops 1000 | bytes 1000 | tf_op jit(solution)/shard_map/pallas_call | solution.py:41
  62.0 1.6 %collective-permute-start.24 = (bf16[176,512]{1,0:T(8,128)(2,1)S(1)}, bf16[176,512]{1,0:T(8,128)(2,1)S(1)}, u32[]{:S(2)}, u32[]{:S(2)}) collective-permute-start(bf16[176,512]{1,0:T(8,128)(2,1)S(1)} %get-tuple-element.87), channel_id=1, source_target_pairs={{0,18},{1,19},{2,16},{3,17},{4,22},{5,23},{6,20},{7,21},{8,26},{9,... | collective-permute-start | bytes 540680 | tf_op jit(solution)/shard_map/ppermute | solution.py:24
  63.6 1.0 %collective-permute-done.20 = bf16[352,512]{1,0:T(8,128)(2,1)S(1)} collective-permute-done((bf16[352,512]{1,0:T(8,128)(2,1)S(1)}, bf16[352,512]{1,0:T(8,128)(2,1)S(1)}, u32[]{:S(2)}, u32[]{:S(2)}) %collective-permute-start.20) | collective-permute-done | bytes 360480 | tf_op jit(solution)/shard_map/ppermute | solution.py:24
  64.6 2.1 %collective-permute-start.25 = (bf16[176,512]{1,0:T(8,128)(2,1)S(1)}, bf16[176,512]{1,0:T(8,128)(2,1)S(1)}, u32[]{:S(2)}, u32[]{:S(2)}) collective-permute-start(bf16[176,512]{1,0:T(8,128)(2,1)S(1)} %get-tuple-element.88), channel_id=1, source_target_pairs={{0,2},{1,3},{2,0},{3,1},{4,6},{5,7},{6,4},{7,5},{8,10},{9,11},{10,... | collective-permute-start | bytes 540680 | tf_op jit(solution)/shard_map/ppermute | solution.py:24
  66.8 1.2 %shard_map.103.refs_3_ = bf16[176,4096]{1,0:T(8,128)(2,1)} custom-call(bf16[176,1024]{1,0:T(8,128)(2,1)S(1)} %collective-permute-done.9.refs_0_, bf16[176,1024]{1,0:T(8,128)(2,1)S(1)} %collective-permute-done.10.refs_1_, bf16[176,512]{1,0:T(8,128)(2,1)S(1)} %get-tuple-element.96.refs_2_), custom_call_target="tpu_custom_call" | custom-call | flops 1000 | bytes 1000 | tf_op jit(solution)/shard_map/pallas_call | solution.py:41
  68.0 1.7 %collective-permute-start.21 = (bf16[176,512]{1,0:T(8,128)(2,1)S(1)}, bf16[176,512]{1,0:T(8,128)(2,1)S(1)}, u32[]{:S(2)}, u32[]{:S(2)}) collective-permute-start(bf16[176,512]{1,0:T(8,128)(2,1)S(1)} %get-tuple-element.82), channel_id=1, source_target_pairs={{0,16},{1,17},{2,18},{3,19},{4,20},{5,21},{6,22},{7,23},{8,24},{9,... | collective-permute-start | bytes 540680 | tf_op jit(solution)/shard_map/ppermute | solution.py:24
  69.6 1.7 %collective-permute-done.15.refs_2_ = bf16[16,5120]{1,0:T(8,128)(2,1)S(1)} collective-permute-done((bf16[16,5120]{1,0:T(8,128)(2,1)S(1)}, bf16[16,5120]{1,0:T(8,128)(2,1)S(1)}, u32[]{:S(2)}, u32[]{:S(2)}) %collective-permute-start.15) | collective-permute-done | bytes 163872 | tf_op jit(solution)/shard_map/ppermute | solution.py:24
  72.6 1.0 %collective-permute-done.21.refs_0_ = bf16[176,512]{1,0:T(8,128)(2,1)S(1)} collective-permute-done((bf16[176,512]{1,0:T(8,128)(2,1)S(1)}, bf16[176,512]{1,0:T(8,128)(2,1)S(1)}, u32[]{:S(2)}, u32[]{:S(2)}) %collective-permute-start.21) | collective-permute-done | bytes 180256 | tf_op jit(solution)/shard_map/ppermute | solution.py:24
  (54 shorter events, 9.2 us)
Async XLA Ops:
  0.6 29.5 %copy-start = (bf16[1,1024,1024]{2,1,0:T(8,128)(2,1)S(1)}, bf16[1,1024,1024]{2,1,0:T(8,128)(2,1)}, u32[]{:S(2)}) copy-start(bf16[1,1024,1024]{2,1,0:T(8,128)(2,1)} %param.11) | copy-start | bytes 6291460
  1.9 23.5 %collective-permute-start.4 = (bf16[256,1024]{1,0:T(8,128)(2,1)S(1)}, bf16[256,1024]{1,0:T(8,128)(2,1)S(1)}, u32[]{:S(2)}, u32[]{:S(2)}) collective-permute-start(bf16[256,1024]{1,0:T(8,128)(2,1)S(1)} %dynamic-slice_bitcast_fusion), channel_id=1, source_target_pairs={{0,4},{1,5},{2,6},{3,7},{4,8},{5,9},{6,10},{7,11},{8,12},{9,13},{1... | collective-permute-start | bytes 1572872 | tf_op jit(solution)/shard_map/ppermute | solution.py:24
  5.0 1.0 %copy-start.2 = (bf16[1,176,1024]{2,1,0:T(8,128)(2,1)S(1)}, bf16[1,176,1024]{2,1,0:T(8,128)(2,1)}, u32[]{:S(2)}) copy-start(bf16[1,176,1024]{2,1,0:T(8,128)(2,1)} %param.8) | copy-start | bytes 1081348
  8.0 17.3 %collective-permute-start.3 = (bf16[176,1152]{1,0:T(8,128)(2,1)S(1)}, bf16[176,1152]{1,0:T(8,128)(2,1)S(1)}, u32[]{:S(2)}, u32[]{:S(2)}) collective-permute-start(bf16[176,1152]{1,0:T(8,128)(2,1)S(1)} %shard_map.94.refs_0_.refs_1_), channel_id=1, source_target_pairs={{0,16},{1,17},{2,18},{3,19},{4,20},{5,21},{6,22},{7,23},{8,24},{9,... | collective-permute-start | bytes 1216520 | tf_op jit(solution)/shard_map/ppermute | solution.py:24
  9.6 0.9 %copy-start.3 = (bf16[1,2,16,4096]{3,2,1,0:T(8,128)(2,1)S(1)}, bf16[1,2,16,4096]{3,2,1,0:T(8,128)(2,1)}, u32[]{:S(2)}) copy-start(bf16[1,2,16,4096]{3,2,1,0:T(8,128)(2,1)} %param.12) | copy-start | bytes 786436
  11.4 10.5 %collective-permute-start = (bf16[16,3072]{1,0:T(8,128)(2,1)S(1)}, bf16[16,3072]{1,0:T(8,128)(2,1)S(1)}, u32[]{:S(2)}, u32[]{:S(2)}) collective-permute-start(bf16[16,3072]{1,0:T(8,128)(2,1)S(1)} %shard_map.95.refs_0_), channel_id=1, source_target_pairs={{0,4},{1,5},{2,6},{3,7},{4,8},{5,9},{6,10},{7,11},{8,12},{9,13},{1... | collective-permute-start | bytes 294920 | tf_op jit(solution)/shard_map/ppermute | solution.py:24
  13.1 12.3 %collective-permute-start.1 = (bf16[16,3072]{1,0:T(8,128)(2,1)S(1)}, bf16[16,3072]{1,0:T(8,128)(2,1)S(1)}, u32[]{:S(2)}, u32[]{:S(2)}) collective-permute-start(bf16[16,3072]{1,0:T(8,128)(2,1)S(1)} %shard_map.95.refs_0_), channel_id=1, source_target_pairs={{0,8},{1,9},{2,10},{3,11},{4,12},{5,13},{6,14},{7,15},{8,0},{9,1},... | collective-permute-start | bytes 294920 | tf_op jit(solution)/shard_map/ppermute | solution.py:24
  14.3 11.1 %collective-permute-start.2 = (bf16[16,3072]{1,0:T(8,128)(2,1)S(1)}, bf16[16,3072]{1,0:T(8,128)(2,1)S(1)}, u32[]{:S(2)}, u32[]{:S(2)}) collective-permute-start(bf16[16,3072]{1,0:T(8,128)(2,1)S(1)} %shard_map.95.refs_0_), channel_id=1, source_target_pairs={{0,12},{1,13},{2,14},{3,15},{4,0},{5,1},{6,2},{7,3},{8,4},{9,5},{1... | collective-permute-start | bytes 294920 | tf_op jit(solution)/shard_map/ppermute | solution.py:24
  25.4 4.7 %collective-permute-start.6 = (bf16[256,1024]{1,0:T(8,128)(2,1)S(1)}, bf16[256,1024]{1,0:T(8,128)(2,1)S(1)}, u32[]{:S(2)}, u32[]{:S(2)}) collective-permute-start(bf16[256,1024]{1,0:T(8,128)(2,1)S(1)} %collective-permute-done.4.refs_5_), channel_id=1, source_target_pairs={{0,1},{1,0},{2,3},{3,2},{4,5},{5,4},{6,7},{7,6},{8,9},{9,8},{10,11... | collective-permute-start | bytes 1572872 | tf_op jit(solution)/shard_map/ppermute | solution.py:24
  25.5 4.6 %collective-permute-start.5 = (bf16[64,3072]{1,0:T(8,128)(2,1)S(1)}, bf16[64,3072]{1,0:T(8,128)(2,1)S(1)}, u32[]{:S(2)}, u32[]{:S(2)}) collective-permute-start(bf16[64,3072]{1,0:T(8,128)(2,1)S(1)} %get-tuple-element.55.refs_2_.refs_3_), channel_id=1, source_target_pairs={{0,1},{1,0},{2,3},{3,2},{4,5},{5,4},{6,7},{7,6},{8,9},{9,8},{10,11... | collective-permute-start | bytes 1179656 | tf_op jit(solution)/shard_map/ppermute | solution.py:24
  26.1 8.3 %collective-permute-start.7 = (bf16[64,2048]{1,0:T(8,128)(2,1)S(1)}, bf16[64,2048]{1,0:T(8,128)(2,1)S(1)}, u32[]{:S(2)}, u32[]{:S(2)}) collective-permute-start(bf16[64,2048]{1,0:T(8,128)(2,1)S(1)} %get-tuple-element.58), channel_id=1, source_target_pairs={{0,16},{1,17},{2,18},{3,19},{4,20},{5,21},{6,22},{7,23},{8,24},{9,... | collective-permute-start | bytes 786440 | tf_op jit(solution)/shard_map/ppermute | solution.py:24
  27.6 22.9 %collective-permute-start.17 = (bf16[256,1024]{1,0:T(8,128)(2,1)S(1)}, bf16[256,1024]{1,0:T(8,128)(2,1)S(1)}, u32[]{:S(2)}, u32[]{:S(2)}) collective-permute-start(bf16[256,1024]{1,0:T(8,128)(2,1)S(1)} %collective-permute-done.4.refs_5_), channel_id=1, source_target_pairs={{0,4},{1,5},{2,6},{3,7},{4,8},{5,9},{6,10},{7,11},{8,12},{9,13},{1... | collective-permute-start | bytes 1572872 | tf_op jit(solution)/shard_map/ppermute | solution.py:24
  30.1 7.9 %copy-start.1 = (bf16[1,176,4096]{2,1,0:T(8,128)(2,1)S(1)}, bf16[1,176,4096]{2,1,0:T(8,128)(2,1)}, u32[]{:S(2)}) copy-start(bf16[1,176,4096]{2,1,0:T(8,128)(2,1)} %param.7) | copy-start | bytes 4325380
  32.4 11.4 %collective-permute-start.9 = (bf16[176,1024]{1,0:T(8,128)(2,1)S(1)}, bf16[176,1024]{1,0:T(8,128)(2,1)S(1)}, u32[]{:S(2)}, u32[]{:S(2)}) collective-permute-start(bf16[176,1024]{1,0:T(8,128)(2,1)S(1)} %get-tuple-element.61), channel_id=1, source_target_pairs={{0,2},{1,3},{2,0},{3,1},{4,6},{5,7},{6,4},{7,5},{8,10},{9,11},{10,... | collective-permute-start | bytes 1081352 | tf_op jit(solution)/shard_map/ppermute | solution.py:24
  33.9 16.0 %collective-permute-start.10 = (bf16[176,1024]{1,0:T(8,128)(2,1)S(1)}, bf16[176,1024]{1,0:T(8,128)(2,1)S(1)}, u32[]{:S(2)}, u32[]{:S(2)}) collective-permute-start(bf16[176,1024]{1,0:T(8,128)(2,1)S(1)} %get-tuple-element.62), channel_id=1, source_target_pairs={{0,18},{1,19},{2,16},{3,17},{4,22},{5,23},{6,20},{7,21},{8,26},{9,... | collective-permute-start | bytes 1081352 | tf_op jit(solution)/shard_map/ppermute | solution.py:24
  34.4 3.6 %collective-permute-start.8 = (bf16[64,2048]{1,0:T(8,128)(2,1)S(1)}, bf16[64,2048]{1,0:T(8,128)(2,1)S(1)}, u32[]{:S(2)}, u32[]{:S(2)}) collective-permute-start(bf16[64,2048]{1,0:T(8,128)(2,1)S(1)} %collective-permute-done.7.refs_5_), channel_id=1, source_target_pairs={{0,1},{1,0},{2,3},{3,2},{4,5},{5,4},{6,7},{7,6},{8,9},{9,8},{10,11... | collective-permute-start | bytes 786440 | tf_op jit(solution)/shard_map/ppermute | solution.py:24
  34.4 21.3 %collective-permute-start.13 = (bf16[256,1024]{1,0:T(8,128)(2,1)S(1)}, bf16[256,1024]{1,0:T(8,128)(2,1)S(1)}, u32[]{:S(2)}, u32[]{:S(2)}) collective-permute-start(bf16[256,1024]{1,0:T(8,128)(2,1)S(1)} %dynamic-slice_bitcast_fusion), channel_id=1, source_target_pairs={{0,12},{1,13},{2,14},{3,15},{4,0},{5,1},{6,2},{7,3},{8,4},{9,5},{1... | collective-permute-start | bytes 1572872 | tf_op jit(solution)/shard_map/ppermute | solution.py:24
  49.9 4.0 %collective-permute-start.11 = (bf16[64,2560]{1,0:T(8,128)(2,1)S(1)}, bf16[64,2560]{1,0:T(8,128)(2,1)S(1)}, u32[]{:S(2)}, u32[]{:S(2)}) collective-permute-start(bf16[64,2560]{1,0:T(8,128)(2,1)S(1)} %get-tuple-element.63), channel_id=1, source_target_pairs={{0,1},{1,0},{2,3},{3,2},{4,5},{5,4},{6,7},{7,6},{8,9},{9,8},{10,11... | collective-permute-start | bytes 983048 | tf_op jit(solution)/shard_map/ppermute | solution.py:24
  49.9 4.0 %collective-permute-start.12 = (bf16[64,2560]{1,0:T(8,128)(2,1)S(1)}, bf16[64,2560]{1,0:T(8,128)(2,1)S(1)}, u32[]{:S(2)}, u32[]{:S(2)}) collective-permute-start(bf16[64,2560]{1,0:T(8,128)(2,1)S(1)} %get-tuple-element.65), channel_id=1, source_target_pairs={{0,1},{1,0},{2,3},{3,2},{4,5},{5,4},{6,7},{7,6},{8,9},{9,8},{10,11... | collective-permute-start | bytes 983048 | tf_op jit(solution)/shard_map/ppermute | solution.py:24
  50.5 1.9 %collective-permute-start.18 = (bf16[128,1024]{1,0:T(8,128)(2,1)S(1)}, bf16[128,1024]{1,0:T(8,128)(2,1)S(1)}, u32[]{:S(2)}, u32[]{:S(2)}) collective-permute-start(bf16[128,1024]{1,0:T(8,128)(2,1)S(1)} %get-tuple-element.78), channel_id=1, source_target_pairs={{0,1},{1,0},{2,3},{3,2},{4,5},{5,4},{6,7},{7,6},{8,9},{9,8},{10,11... | collective-permute-start | bytes 786440 | tf_op jit(solution)/shard_map/ppermute | solution.py:24
  50.6 2.2 %collective-permute-start.19 = (bf16[128,1024]{1,0:T(8,128)(2,1)S(1)}, bf16[128,1024]{1,0:T(8,128)(2,1)S(1)}, u32[]{:S(2)}, u32[]{:S(2)}) collective-permute-start(bf16[128,1024]{1,0:T(8,128)(2,1)S(1)} %get-tuple-element.80), channel_id=1, source_target_pairs={{0,1},{1,0},{2,3},{3,2},{4,5},{5,4},{6,7},{7,6},{8,9},{9,8},{10,11... | collective-permute-start | bytes 786440 | tf_op jit(solution)/shard_map/ppermute | solution.py:24
  54.1 10.5 %collective-permute-start.20 = (bf16[352,512]{1,0:T(8,128)(2,1)S(1)}, bf16[352,512]{1,0:T(8,128)(2,1)S(1)}, u32[]{:S(2)}, u32[]{:S(2)}) collective-permute-start(bf16[352,512]{1,0:T(8,128)(2,1)S(1)} %shard_map.102), channel_id=1, source_target_pairs={{0,2},{1,3},{2,0},{3,1},{4,6},{5,7},{6,4},{7,5},{8,10},{9,11},{10,... | collective-permute-start | bytes 1081352 | tf_op jit(solution)/shard_map/ppermute | solution.py:24
  55.7 4.2 %collective-permute-start.22 = (bf16[128,1024]{1,0:T(8,128)(2,1)S(1)}, bf16[128,1024]{1,0:T(8,128)(2,1)S(1)}, u32[]{:S(2)}, u32[]{:S(2)}) collective-permute-start(bf16[128,1024]{1,0:T(8,128)(2,1)S(1)} %get-tuple-element.84), channel_id=1, source_target_pairs={{0,1},{1,0},{2,3},{3,2},{4,5},{5,4},{6,7},{7,6},{8,9},{9,8},{10,11... | collective-permute-start | bytes 786440 | tf_op jit(solution)/shard_map/ppermute | solution.py:24
  55.8 5.1 %collective-permute-start.23 = (bf16[128,1024]{1,0:T(8,128)(2,1)S(1)}, bf16[128,1024]{1,0:T(8,128)(2,1)S(1)}, u32[]{:S(2)}, u32[]{:S(2)}) collective-permute-start(bf16[128,1024]{1,0:T(8,128)(2,1)S(1)} %get-tuple-element.86), channel_id=1, source_target_pairs={{0,1},{1,0},{2,3},{3,2},{4,5},{5,4},{6,7},{7,6},{8,9},{9,8},{10,11... | collective-permute-start | bytes 786440 | tf_op jit(solution)/shard_map/ppermute | solution.py:24
  56.3 11.7 %collective-permute-start.14 = (bf16[16,5120]{1,0:T(8,128)(2,1)S(1)}, bf16[16,5120]{1,0:T(8,128)(2,1)S(1)}, u32[]{:S(2)}, u32[]{:S(2)}) collective-permute-start(bf16[16,5120]{1,0:T(8,128)(2,1)S(1)} %get-tuple-element.70), channel_id=1, source_target_pairs={{0,4},{1,5},{2,6},{3,7},{4,8},{5,9},{6,10},{7,11},{8,12},{9,13},{1... | collective-permute-start | bytes 491528 | tf_op jit(solution)/shard_map/ppermute | solution.py:24
  58.2 13.2 %collective-permute-start.15 = (bf16[16,5120]{1,0:T(8,128)(2,1)S(1)}, bf16[16,5120]{1,0:T(8,128)(2,1)S(1)}, u32[]{:S(2)}, u32[]{:S(2)}) collective-permute-start(bf16[16,5120]{1,0:T(8,128)(2,1)S(1)} %get-tuple-element.72), channel_id=1, source_target_pairs={{0,8},{1,9},{2,10},{3,11},{4,12},{5,13},{6,14},{7,15},{8,0},{9,1},... | collective-permute-start | bytes 491528 | tf_op jit(solution)/shard_map/ppermute | solution.py:24
  59.9 11.5 %collective-permute-start.16 = (bf16[16,5120]{1,0:T(8,128)(2,1)S(1)}, bf16[16,5120]{1,0:T(8,128)(2,1)S(1)}, u32[]{:S(2)}, u32[]{:S(2)}) collective-permute-start(bf16[16,5120]{1,0:T(8,128)(2,1)S(1)} %get-tuple-element.74), channel_id=1, source_target_pairs={{0,12},{1,13},{2,14},{3,15},{4,0},{5,1},{6,2},{7,3},{8,4},{9,5},{1... | collective-permute-start | bytes 491528 | tf_op jit(solution)/shard_map/ppermute | solution.py:24
  62.0 10.0 %collective-permute-start.24 = (bf16[176,512]{1,0:T(8,128)(2,1)S(1)}, bf16[176,512]{1,0:T(8,128)(2,1)S(1)}, u32[]{:S(2)}, u32[]{:S(2)}) collective-permute-start(bf16[176,512]{1,0:T(8,128)(2,1)S(1)} %get-tuple-element.87), channel_id=1, source_target_pairs={{0,18},{1,19},{2,16},{3,17},{4,22},{5,23},{6,20},{7,21},{8,26},{9,... | collective-permute-start | bytes 540680 | tf_op jit(solution)/shard_map/ppermute | solution.py:24
  64.6 8.0 %collective-permute-start.25 = (bf16[176,512]{1,0:T(8,128)(2,1)S(1)}, bf16[176,512]{1,0:T(8,128)(2,1)S(1)}, u32[]{:S(2)}, u32[]{:S(2)}) collective-permute-start(bf16[176,512]{1,0:T(8,128)(2,1)S(1)} %get-tuple-element.88), channel_id=1, source_target_pairs={{0,2},{1,3},{2,0},{3,1},{4,6},{5,7},{6,4},{7,5},{8,10},{9,11},{10,... | collective-permute-start | bytes 540680 | tf_op jit(solution)/shard_map/ppermute | solution.py:24
  68.0 5.6 %collective-permute-start.21 = (bf16[176,512]{1,0:T(8,128)(2,1)S(1)}, bf16[176,512]{1,0:T(8,128)(2,1)S(1)}, u32[]{:S(2)}, u32[]{:S(2)}) collective-permute-start(bf16[176,512]{1,0:T(8,128)(2,1)S(1)} %get-tuple-element.82), channel_id=1, source_target_pairs={{0,16},{1,17},{2,18},{3,19},{4,20},{5,21},{6,22},{7,23},{8,24},{9,... | collective-permute-start | bytes 540680 | tf_op jit(solution)/shard_map/ppermute | solution.py:24
  71.5 2.9 %collective-permute-start.26 = (bf16[16,2560]{1,0:T(8,128)(2,1)S(1)}, bf16[16,2560]{1,0:T(8,128)(2,1)S(1)}, u32[]{:S(2)}, u32[]{:S(2)}) collective-permute-start(bf16[16,2560]{1,0:T(8,128)(2,1)S(1)} %get-tuple-element.91.refs_0_), channel_id=1, source_target_pairs={{0,1},{1,0},{2,3},{3,2},{4,5},{5,4},{6,7},{7,6},{8,9},{9,8},{10,11... | collective-permute-start | bytes 245768 | tf_op jit(solution)/shard_map/ppermute | solution.py:24
  71.6 2.9 %collective-permute-start.27 = (bf16[16,2560]{1,0:T(8,128)(2,1)S(1)}, bf16[16,2560]{1,0:T(8,128)(2,1)S(1)}, u32[]{:S(2)}, u32[]{:S(2)}) collective-permute-start(bf16[16,2560]{1,0:T(8,128)(2,1)S(1)} %get-tuple-element.92.refs_1_), channel_id=1, source_target_pairs={{0,1},{1,0},{2,3},{3,2},{4,5},{5,4},{6,7},{7,6},{8,9},{9,8},{10,11... | collective-permute-start | bytes 245768 | tf_op jit(solution)/shard_map/ppermute | solution.py:24
  (3 other events, 2.2 us)

commit v24 on v21

--- a/solution.py
+++ b/solution.py
@@ -451,6 +451,7 @@
     totals = list(total)
     for dr in range(1, replicas):
         totals += [moved(x, lambda g, z, s, r: (g, z, s, r + dr)) for x in total]
+    totals[0], passed = lax.optimization_barrier((totals[0], passed))
     down_grad, up_grad = call(
         functools.partial(spread_kernel, width, replicas),
         [

time: 76.8 us -> 77.6 us (1.010)
  the two profiles are of different devices: /device:TPU:9 before, /device:TPU:0 now
where the time goes in v24:
time: 77.6 us; the launch traced here: 77.4 us
  waiting for transfers between devices  31.4 us (40%)
  starting transfers between devices  30.1 us (39%)
  Pallas kernels  9.75 us (13%)
  local copies, waits for them, and re-layouts  5.37 us (7%)
  between operations  0.82 us (1%)
    ppermute x28, waiting for transfers between devices, moved(): return lax.ppermute(x, AXES, pairs)  31.4 us
    ppermute x28, starting transfers between devices, moved(): return lax.ppermute(x, AXES, pairs)  30.1 us
    pallas_call x13, Pallas kernels, call(): pl.pallas_call(kernel, out_shape=out_shape, in_specs=[pl.BlockSpec(memory...  8.91 us
    unnamed x14, local copies, waits for them, and re-layouts  4.12 us
  transfers between devices with their start and end apart: 28, of which 11 were waited for; matrix products, arithmetic and copies ran while one was open for 0% of the time, Pallas kernels for 12%

profile of v24, /device:TPU:0, one launch (start us, length us, event | category | flops | bytes accessed | tf_op | source)
XLA Modules:
  0.0 77.4 jit_solution(15796922811674804469)
XLA Ops:
  0.6 1.2 %dynamic-slice_bitcast_fusion = bf16[256,1024]{1,0:T(8,128)(2,1)S(1)} fusion(bf16[1,1024,1024]{2,1,0:T(8,128)(2,1)} %param.11, s32[]{:T(128)S(6)} %select_n.3), kind=kLoop, calls=%fused_computation | loop fusion | bytes 1048580 | tf_op jit(solution)/shard_map/dynamic_slice | solution.py:302
  1.9 3.1 %collective-permute-start.4 = (bf16[256,1024]{1,0:T(8,128)(2,1)S(1)}, bf16[256,1024]{1,0:T(8,128)(2,1)S(1)}, u32[]{:S(2)}, u32[]{:S(2)}) collective-permute-start(bf16[256,1024]{1,0:T(8,128)(2,1)S(1)} %dynamic-slice_bitcast_fusion), channel_id=1, source_target_pairs={{0,4},{1,5},{2,6},{3,7},{4,8},{5,9},{6,10},{7,11},{8,12},{9,13},{1... | collective-permute-start | bytes 1572872 | tf_op jit(solution)/shard_map/ppermute | solution.py:24
  5.0 1.0 %copy-done.2 = bf16[1,176,1024]{2,1,0:T(8,128)(2,1)S(1)} copy-done((bf16[1,176,1024]{2,1,0:T(8,128)(2,1)S(1)}, bf16[1,176,1024]{2,1,0:T(8,128)(2,1)}, u32[]{:S(2)}) %copy-start.2) | copy-done | bytes 360472
  5.9 0.7 copy-done.5
  7.3 0.8 shard_map.94.refs_0_.refs_1_
  8.0 1.6 %collective-permute-start.3 = (bf16[176,1152]{1,0:T(8,128)(2,1)S(1)}, bf16[176,1152]{1,0:T(8,128)(2,1)S(1)}, u32[]{:S(2)}, u32[]{:S(2)}) collective-permute-start(bf16[176,1152]{1,0:T(8,128)(2,1)S(1)} %shard_map.94.refs_0_.refs_1_), channel_id=1, source_target_pairs={{0,16},{1,17},{2,18},{3,19},{4,20},{5,21},{6,22},{7,23},{8,24},{9,... | collective-permute-start | bytes 1216520 | tf_op jit(solution)/shard_map/ppermute | solution.py:24
  9.6 0.9 %copy-done.3 = bf16[1,2,16,4096]{3,2,1,0:T(8,128)(2,1)S(1)} copy-done((bf16[1,2,16,4096]{3,2,1,0:T(8,128)(2,1)S(1)}, bf16[1,2,16,4096]{3,2,1,0:T(8,128)(2,1)}, u32[]{:S(2)}) %copy-start.3) | copy-done | bytes 262168
  10.6 0.8 %copy-done.4 = bf16[1,2,16,1024]{3,2,1,0:T(8,128)(2,1)S(1)} copy-done((bf16[1,2,16,1024]{3,2,1,0:T(8,128)(2,1)S(1)}, bf16[1,2,16,1024]{3,2,1,0:T(8,128)(2,1)}, u32[]{:S(2)}) %copy-start.4) | copy-done | bytes 65560
  11.4 1.6 %collective-permute-start = (bf16[16,3072]{1,0:T(8,128)(2,1)S(1)}, bf16[16,3072]{1,0:T(8,128)(2,1)S(1)}, u32[]{:S(2)}, u32[]{:S(2)}) collective-permute-start(bf16[16,3072]{1,0:T(8,128)(2,1)S(1)} %shard_map.95.refs_0_), channel_id=1, source_target_pairs={{0,4},{1,5},{2,6},{3,7},{4,8},{5,9},{6,10},{7,11},{8,12},{9,13},{1... | collective-permute-start | bytes 294920 | tf_op jit(solution)/shard_map/ppermute | solution.py:24
  13.1 1.2 %collective-permute-start.1 = (bf16[16,3072]{1,0:T(8,128)(2,1)S(1)}, bf16[16,3072]{1,0:T(8,128)(2,1)S(1)}, u32[]{:S(2)}, u32[]{:S(2)}) collective-permute-start(bf16[16,3072]{1,0:T(8,128)(2,1)S(1)} %shard_map.95.refs_0_), channel_id=1, source_target_pairs={{0,8},{1,9},{2,10},{3,11},{4,12},{5,13},{6,14},{7,15},{8,0},{9,1},... | collective-permute-start | bytes 294920 | tf_op jit(solution)/shard_map/ppermute | solution.py:24
  14.3 2.7 %collective-permute-start.2 = (bf16[16,3072]{1,0:T(8,128)(2,1)S(1)}, bf16[16,3072]{1,0:T(8,128)(2,1)S(1)}, u32[]{:S(2)}, u32[]{:S(2)}) collective-permute-start(bf16[16,3072]{1,0:T(8,128)(2,1)S(1)} %shard_map.95.refs_0_), channel_id=1, source_target_pairs={{0,12},{1,13},{2,14},{3,15},{4,0},{5,1},{6,2},{7,3},{8,4},{9,5},{1... | collective-permute-start | bytes 294920 | tf_op jit(solution)/shard_map/ppermute | solution.py:24
  17.0 5.0 %collective-permute-done.refs_1_ = bf16[16,3072]{1,0:T(8,128)(2,1)S(1)} collective-permute-done((bf16[16,3072]{1,0:T(8,128)(2,1)S(1)}, bf16[16,3072]{1,0:T(8,128)(2,1)S(1)}, u32[]{:S(2)}, u32[]{:S(2)}) %collective-permute-start) | collective-permute-done | bytes 98336 | tf_op jit(solution)/shard_map/ppermute | solution.py:24
  22.0 3.4 %collective-permute-done.1.refs_2_ = bf16[16,3072]{1,0:T(8,128)(2,1)S(1)} collective-permute-done((bf16[16,3072]{1,0:T(8,128)(2,1)S(1)}, bf16[16,3072]{1,0:T(8,128)(2,1)S(1)}, u32[]{:S(2)}, u32[]{:S(2)}) %collective-permute-start.1) | collective-permute-done | bytes 98336 | tf_op jit(solution)/shard_map/ppermute | solution.py:24
  26.1 2.5 %collective-permute-start.17 = (bf16[256,1024]{1,0:T(8,128)(2,1)S(1)}, bf16[256,1024]{1,0:T(8,128)(2,1)S(1)}, u32[]{:S(2)}, u32[]{:S(2)}) collective-permute-start(bf16[256,1024]{1,0:T(8,128)(2,1)S(1)} %collective-permute-done.4.refs_5_), channel_id=1, source_target_pairs={{0,4},{1,5},{2,6},{3,7},{4,8},{5,9},{6,10},{7,11},{8,12},{9,13},{1... | collective-permute-start | bytes 1572872 | tf_op jit(solution)/shard_map/ppermute | solution.py:24
  28.6 2.2 %shard_map.97 = (bf16[176,1024]{1,0:T(8,128)(2,1)S(1)}, bf16[176,1024]{1,0:T(8,128)(2,1)S(1)}, bf16[352,128]{1,0:T(8,128)(2,1)S(1)}) custom-call(bf16[176,1152]{1,0:T(8,128)(2,1)S(1)} %shard_map.94.refs_0_.refs_1_, bf16[176,1152]{1,0:T(8,128)(2,1)S(1)} %collective-permute-done.3.refs_1_, bf16[64,3072]{1,0:T(8,128)(2,1)S(1)} %get-tuple-element.54.refs_2_.refs_3_, ...), custom_call_target="tpu_custom_call" | custom-call | flops 1000 | bytes 1000 | tf_op jit(solution)/shard_map/pallas_call | solution.py:41
  30.8 1.6 %collective-permute-start.9 = (bf16[176,1024]{1,0:T(8,128)(2,1)S(1)}, bf16[176,1024]{1,0:T(8,128)(2,1)S(1)}, u32[]{:S(2)}, u32[]{:S(2)}) collective-permute-start(bf16[176,1024]{1,0:T(8,128)(2,1)S(1)} %get-tuple-element.60), channel_id=1, source_target_pairs={{0,2},{1,3},{2,0},{3,1},{4,6},{5,7},{6,4},{7,5},{8,10},{9,11},{10,... | collective-permute-start | bytes 1081352 | tf_op jit(solution)/shard_map/ppermute | solution.py:24
  32.4 1.5 %collective-permute-start.10 = (bf16[176,1024]{1,0:T(8,128)(2,1)S(1)}, bf16[176,1024]{1,0:T(8,128)(2,1)S(1)}, u32[]{:S(2)}, u32[]{:S(2)}) collective-permute-start(bf16[176,1024]{1,0:T(8,128)(2,1)S(1)} %get-tuple-element.61), channel_id=1, source_target_pairs={{0,18},{1,19},{2,16},{3,17},{4,22},{5,23},{6,20},{7,21},{8,26},{9,... | collective-permute-start | bytes 1081352 | tf_op jit(solution)/shard_map/ppermute | solution.py:24
  34.4 2.9 %collective-permute-start.13 = (bf16[256,1024]{1,0:T(8,128)(2,1)S(1)}, bf16[256,1024]{1,0:T(8,128)(2,1)S(1)}, u32[]{:S(2)}, u32[]{:S(2)}) collective-permute-start(bf16[256,1024]{1,0:T(8,128)(2,1)S(1)} %dynamic-slice_bitcast_fusion), channel_id=1, source_target_pairs={{0,12},{1,13},{2,14},{3,15},{4,0},{5,1},{6,2},{7,3},{8,4},{9,5},{1... | collective-permute-start | bytes 1572872 | tf_op jit(solution)/shard_map/ppermute | solution.py:24
  37.3 4.6 %collective-permute-done.7.refs_5_ = bf16[64,2048]{1,0:T(8,128)(2,1)S(1)} collective-permute-done((bf16[64,2048]{1,0:T(8,128)(2,1)S(1)}, bf16[64,2048]{1,0:T(8,128)(2,1)S(1)}, u32[]{:S(2)}, u32[]{:S(2)}) %collective-permute-start.7) | collective-permute-done | bytes 262176 | tf_op jit(solution)/shard_map/ppermute | solution.py:24
  41.9 0.8 %collective-permute-done.17.block_ref.refs_5_ = bf16[256,1024]{1,0:T(8,128)(2,1)S(1)} collective-permute-done((bf16[256,1024]{1,0:T(8,128)(2,1)S(1)}, bf16[256,1024]{1,0:T(8,128)(2,1)S(1)}, u32[]{:S(2)}, u32[]{:S(2)}) %collective-permute-start.17) | collective-permute-done | bytes 524320 | tf_op jit(solution)/shard_map/ppermute | solution.py:24
  42.7 7.0 %collective-permute-done.10.refs_1_ = bf16[176,1024]{1,0:T(8,128)(2,1)S(1)} collective-permute-done((bf16[176,1024]{1,0:T(8,128)(2,1)S(1)}, bf16[176,1024]{1,0:T(8,128)(2,1)S(1)}, u32[]{:S(2)}, u32[]{:S(2)}) %collective-permute-start.10) | collective-permute-done | bytes 360480 | tf_op jit(solution)/shard_map/ppermute | solution.py:24
  50.2 1.3 %shard_map.98 = (f32[64,5120]{1,0:T(8,128)S(1)}, bf16[64,2560]{1,0:T(8,128)(2,1)S(1)}, bf16[64,2560]{1,0:T(8,128)(2,1)S(1)}) custom-call(bf16[176,4096]{1,0:T(8,128)(2,1)S(1)} %bitcast.12, bf16[176,1152]{1,0:T(8,128)(2,1)S(1)} %shard_map.94.refs_0_.refs_1_, bf16[352,128]{1,0:T(8,128)(2,1)S(1)} %get-tuple-element.56.refs_2_.refs_4_, ...), custom_call_target="tpu_custom_call" | custom-call | flops 1000 | bytes 1000 | tf_op jit(solution)/shard_map/pallas_call | solution.py:41
  51.6 1.2 %shard_map.102 = bf16[352,512]{1,0:T(8,128)(2,1)S(1)} custom-call(bf16[176,1152]{1,0:T(8,128)(2,1)S(1)} %shard_map.94.refs_0_.refs_1_, bf16[176,1152]{1,0:T(8,128)(2,1)S(1)} %collective-permute-done.3.refs_1_, bf16[64,3072]{1,0:T(8,128)(2,1)S(1)} %get-tuple-element.54.refs_2_.refs_3_, bf16[64,3072]{1,0:T(8,128)(2,1)S(1)} %collective-permute-done.5.refs_3_.refs_4_, ...), custom_call_target="tpu_custom_call" | custom-call | flops 1000 | bytes 1000 | tf_op jit(solution)/shard_map/pallas_call | solution.py:41
  52.8 1.6 %collective-permute-start.20 = (bf16[352,512]{1,0:T(8,128)(2,1)S(1)}, bf16[352,512]{1,0:T(8,128)(2,1)S(1)}, u32[]{:S(2)}, u32[]{:S(2)}) collective-permute-start(bf16[352,512]{1,0:T(8,128)(2,1)S(1)} %shard_map.102), channel_id=1, source_target_pairs={{0,2},{1,3},{2,0},{3,1},{4,6},{5,7},{6,4},{7,5},{8,10},{9,11},{10,... | collective-permute-start | bytes 1081352 | tf_op jit(solution)/shard_map/ppermute | solution.py:24
  56.6 3.3 %collective-permute-start.14 = (bf16[16,5120]{1,0:T(8,128)(2,1)S(1)}, bf16[16,5120]{1,0:T(8,128)(2,1)S(1)}, u32[]{:S(2)}, u32[]{:S(2)}) collective-permute-start(bf16[16,5120]{1,0:T(8,128)(2,1)S(1)} %get-tuple-element.69), channel_id=1, source_target_pairs={{0,12},{1,13},{2,14},{3,15},{4,0},{5,1},{6,2},{7,3},{8,4},{9,5},{1... | collective-permute-start | bytes 491528 | tf_op jit(solution)/shard_map/ppermute | solution.py:24
  60.5 1.2 %shard_map.105 = (bf16[176,512]{1,0:T(8,128)(2,1)S(1)}, bf16[176,512]{1,0:T(8,128)(2,1)S(1)}) custom-call(bf16[176,1152]{1,0:T(8,128)(2,1)S(1)} %shard_map.94.refs_0_.refs_1_, bf16[176,1152]{1,0:T(8,128)(2,1)S(1)} %collective-permute-done.3.refs_1_, bf16[64,3072]{1,0:T(8,128)(2,1)S(1)} %get-tuple-element.54.refs_2_.refs_3_, ...), custom_call_target="tpu_custom_call" | custom-call | flops 1000 | bytes 1000 | tf_op jit(solution)/shard_map/pallas_call | solution.py:41
  62.3 1.0 %collective-permute-done.20 = bf16[352,512]{1,0:T(8,128)(2,1)S(1)} collective-permute-done((bf16[352,512]{1,0:T(8,128)(2,1)S(1)}, bf16[352,512]{1,0:T(8,128)(2,1)S(1)}, u32[]{:S(2)}, u32[]{:S(2)}) %collective-permute-start.20) | collective-permute-done | bytes 360480 | tf_op jit(solution)/shard_map/ppermute | solution.py:24
  63.3 1.8 %collective-permute-start.25 = (bf16[176,512]{1,0:T(8,128)(2,1)S(1)}, bf16[176,512]{1,0:T(8,128)(2,1)S(1)}, u32[]{:S(2)}, u32[]{:S(2)}) collective-permute-start(bf16[176,512]{1,0:T(8,128)(2,1)S(1)} %get-tuple-element.86), channel_id=1, source_target_pairs={{0,2},{1,3},{2,0},{3,1},{4,6},{5,7},{6,4},{7,5},{8,10},{9,11},{10,... | collective-permute-start | bytes 540680 | tf_op jit(solution)/shard_map/ppermute | solution.py:24
  65.1 1.2 %shard_map.103.refs_3_ = bf16[176,4096]{1,0:T(8,128)(2,1)} custom-call(bf16[176,1024]{1,0:T(8,128)(2,1)S(1)} %collective-permute-done.9.refs_0_, bf16[176,1024]{1,0:T(8,128)(2,1)S(1)} %collective-permute-done.10.refs_1_, bf16[176,512]{1,0:T(8,128)(2,1)S(1)} %get-tuple-element.94.refs_2_), custom_call_target="tpu_custom_call" | custom-call | flops 1000 | bytes 1000 | tf_op jit(solution)/shard_map/pallas_call | solution.py:41
  66.5 8.5 %collective-permute-done.15.refs_2_ = bf16[16,5120]{1,0:T(8,128)(2,1)S(1)} collective-permute-done((bf16[16,5120]{1,0:T(8,128)(2,1)S(1)}, bf16[16,5120]{1,0:T(8,128)(2,1)S(1)}, u32[]{:S(2)}, u32[]{:S(2)}) %collective-permute-start.15) | collective-permute-done | bytes 163872 | tf_op jit(solution)/shard_map/ppermute | solution.py:24
  75.7 0.8 %shard_map.106 = bf16[176,4096]{1,0:T(8,128)(2,1)} custom-call(bf16[176,512]{1,0:T(8,128)(2,1)S(1)} %collective-permute-done.21.refs_0_, bf16[176,512]{1,0:T(8,128)(2,1)S(1)} %collective-permute-done.24.refs_1_, bf16[176,512]{1,0:T(8,128)(2,1)S(1)} %collective-permute-done.25.refs_2_, ...), custom_call_target="tpu_custom_call", output_to_operand_aliasing={{}: (3, {})} | custom-call | flops 1000 | bytes 1000 | tf_op jit(solution)/shard_map/pallas_call | solution.py:426
  76.6 0.7 shard_map.107
  (54 shorter events, 6.9 us)
Async XLA Ops:
  0.6 27.9 %copy-start = (bf16[1,1024,1024]{2,1,0:T(8,128)(2,1)S(1)}, bf16[1,1024,1024]{2,1,0:T(8,128)(2,1)}, u32[]{:S(2)}) copy-start(bf16[1,1024,1024]{2,1,0:T(8,128)(2,1)} %param.11) | copy-start | bytes 6291460
  1.9 23.5 %collective-permute-start.4 = (bf16[256,1024]{1,0:T(8,128)(2,1)S(1)}, bf16[256,1024]{1,0:T(8,128)(2,1)S(1)}, u32[]{:S(2)}, u32[]{:S(2)}) collective-permute-start(bf16[256,1024]{1,0:T(8,128)(2,1)S(1)} %dynamic-slice_bitcast_fusion), channel_id=1, source_target_pairs={{0,4},{1,5},{2,6},{3,7},{4,8},{5,9},{6,10},{7,11},{8,12},{9,13},{1... | collective-permute-start | bytes 1572872 | tf_op jit(solution)/shard_map/ppermute | solution.py:24
  5.0 1.0 %copy-start.2 = (bf16[1,176,1024]{2,1,0:T(8,128)(2,1)S(1)}, bf16[1,176,1024]{2,1,0:T(8,128)(2,1)}, u32[]{:S(2)}) copy-start(bf16[1,176,1024]{2,1,0:T(8,128)(2,1)} %param.8) | copy-start | bytes 1081348
  8.0 17.3 %collective-permute-start.3 = (bf16[176,1152]{1,0:T(8,128)(2,1)S(1)}, bf16[176,1152]{1,0:T(8,128)(2,1)S(1)}, u32[]{:S(2)}, u32[]{:S(2)}) collective-permute-start(bf16[176,1152]{1,0:T(8,128)(2,1)S(1)} %shard_map.94.refs_0_.refs_1_), channel_id=1, source_target_pairs={{0,16},{1,17},{2,18},{3,19},{4,20},{5,21},{6,22},{7,23},{8,24},{9,... | collective-permute-start | bytes 1216520 | tf_op jit(solution)/shard_map/ppermute | solution.py:24
  9.6 0.9 %copy-start.3 = (bf16[1,2,16,4096]{3,2,1,0:T(8,128)(2,1)S(1)}, bf16[1,2,16,4096]{3,2,1,0:T(8,128)(2,1)}, u32[]{:S(2)}) copy-start(bf16[1,2,16,4096]{3,2,1,0:T(8,128)(2,1)} %param.12) | copy-start | bytes 786436
  11.4 10.5 %collective-permute-start = (bf16[16,3072]{1,0:T(8,128)(2,1)S(1)}, bf16[16,3072]{1,0:T(8,128)(2,1)S(1)}, u32[]{:S(2)}, u32[]{:S(2)}) collective-permute-start(bf16[16,3072]{1,0:T(8,128)(2,1)S(1)} %shard_map.95.refs_0_), channel_id=1, source_target_pairs={{0,4},{1,5},{2,6},{3,7},{4,8},{5,9},{6,10},{7,11},{8,12},{9,13},{1... | collective-permute-start | bytes 294920 | tf_op jit(solution)/shard_map/ppermute | solution.py:24
  13.1 12.3 %collective-permute-start.1 = (bf16[16,3072]{1,0:T(8,128)(2,1)S(1)}, bf16[16,3072]{1,0:T(8,128)(2,1)S(1)}, u32[]{:S(2)}, u32[]{:S(2)}) collective-permute-start(bf16[16,3072]{1,0:T(8,128)(2,1)S(1)} %shard_map.95.refs_0_), channel_id=1, source_target_pairs={{0,8},{1,9},{2,10},{3,11},{4,12},{5,13},{6,14},{7,15},{8,0},{9,1},... | collective-permute-start | bytes 294920 | tf_op jit(solution)/shard_map/ppermute | solution.py:24
  14.3 11.1 %collective-permute-start.2 = (bf16[16,3072]{1,0:T(8,128)(2,1)S(1)}, bf16[16,3072]{1,0:T(8,128)(2,1)S(1)}, u32[]{:S(2)}, u32[]{:S(2)}) collective-permute-start(bf16[16,3072]{1,0:T(8,128)(2,1)S(1)} %shard_map.95.refs_0_), channel_id=1, source_target_pairs={{0,12},{1,13},{2,14},{3,15},{4,0},{5,1},{6,2},{7,3},{8,4},{9,5},{1... | collective-permute-start | bytes 294920 | tf_op jit(solution)/shard_map/ppermute | solution.py:24
  25.4 3.2 %collective-permute-start.6 = (bf16[256,1024]{1,0:T(8,128)(2,1)S(1)}, bf16[256,1024]{1,0:T(8,128)(2,1)S(1)}, u32[]{:S(2)}, u32[]{:S(2)}) collective-permute-start(bf16[256,1024]{1,0:T(8,128)(2,1)S(1)} %collective-permute-done.4.refs_5_), channel_id=1, source_target_pairs={{0,1},{1,0},{2,3},{3,2},{4,5},{5,4},{6,7},{7,6},{8,9},{9,8},{10,11... | collective-permute-start | bytes 1572872 | tf_op jit(solution)/shard_map/ppermute | solution.py:24
  25.5 3.1 %collective-permute-start.5 = (bf16[64,3072]{1,0:T(8,128)(2,1)S(1)}, bf16[64,3072]{1,0:T(8,128)(2,1)S(1)}, u32[]{:S(2)}, u32[]{:S(2)}) collective-permute-start(bf16[64,3072]{1,0:T(8,128)(2,1)S(1)} %get-tuple-element.54.refs_2_.refs_3_), channel_id=1, source_target_pairs={{0,1},{1,0},{2,3},{3,2},{4,5},{5,4},{6,7},{7,6},{8,9},{9,8},{10,11... | collective-permute-start | bytes 1179656 | tf_op jit(solution)/shard_map/ppermute | solution.py:24
  26.1 16.6 %collective-permute-start.17 = (bf16[256,1024]{1,0:T(8,128)(2,1)S(1)}, bf16[256,1024]{1,0:T(8,128)(2,1)S(1)}, u32[]{:S(2)}, u32[]{:S(2)}) collective-permute-start(bf16[256,1024]{1,0:T(8,128)(2,1)S(1)} %collective-permute-done.4.refs_5_), channel_id=1, source_target_pairs={{0,4},{1,5},{2,6},{3,7},{4,8},{5,9},{6,10},{7,11},{8,12},{9,13},{1... | collective-permute-start | bytes 1572872 | tf_op jit(solution)/shard_map/ppermute | solution.py:24
  28.6 21.6 %copy-start.1 = (bf16[1,176,4096]{2,1,0:T(8,128)(2,1)S(1)}, bf16[1,176,4096]{2,1,0:T(8,128)(2,1)}, u32[]{:S(2)}) copy-start(bf16[1,176,4096]{2,1,0:T(8,128)(2,1)} %param.7) | copy-start | bytes 4325380
  30.8 11.9 %collective-permute-start.9 = (bf16[176,1024]{1,0:T(8,128)(2,1)S(1)}, bf16[176,1024]{1,0:T(8,128)(2,1)S(1)}, u32[]{:S(2)}, u32[]{:S(2)}) collective-permute-start(bf16[176,1024]{1,0:T(8,128)(2,1)S(1)} %get-tuple-element.60), channel_id=1, source_target_pairs={{0,2},{1,3},{2,0},{3,1},{4,6},{5,7},{6,4},{7,5},{8,10},{9,11},{10,... | collective-permute-start | bytes 1081352 | tf_op jit(solution)/shard_map/ppermute | solution.py:24
  32.4 17.3 %collective-permute-start.10 = (bf16[176,1024]{1,0:T(8,128)(2,1)S(1)}, bf16[176,1024]{1,0:T(8,128)(2,1)S(1)}, u32[]{:S(2)}, u32[]{:S(2)}) collective-permute-start(bf16[176,1024]{1,0:T(8,128)(2,1)S(1)} %get-tuple-element.61), channel_id=1, source_target_pairs={{0,18},{1,19},{2,16},{3,17},{4,22},{5,23},{6,20},{7,21},{8,26},{9,... | collective-permute-start | bytes 1081352 | tf_op jit(solution)/shard_map/ppermute | solution.py:24
  33.9 8.0 %collective-permute-start.7 = (bf16[64,2048]{1,0:T(8,128)(2,1)S(1)}, bf16[64,2048]{1,0:T(8,128)(2,1)S(1)}, u32[]{:S(2)}, u32[]{:S(2)}) collective-permute-start(bf16[64,2048]{1,0:T(8,128)(2,1)S(1)} %get-tuple-element.57), channel_id=1, source_target_pairs={{0,16},{1,17},{2,18},{3,19},{4,20},{5,21},{6,22},{7,23},{8,24},{9,... | collective-permute-start | bytes 786440 | tf_op jit(solution)/shard_map/ppermute | solution.py:24
  34.4 20.5 %collective-permute-start.13 = (bf16[256,1024]{1,0:T(8,128)(2,1)S(1)}, bf16[256,1024]{1,0:T(8,128)(2,1)S(1)}, u32[]{:S(2)}, u32[]{:S(2)}) collective-permute-start(bf16[256,1024]{1,0:T(8,128)(2,1)S(1)} %dynamic-slice_bitcast_fusion), channel_id=1, source_target_pairs={{0,12},{1,13},{2,14},{3,15},{4,0},{5,1},{6,2},{7,3},{8,4},{9,5},{1... | collective-permute-start | bytes 1572872 | tf_op jit(solution)/shard_map/ppermute | solution.py:24
  41.9 8.3 %collective-permute-start.8 = (bf16[64,2048]{1,0:T(8,128)(2,1)S(1)}, bf16[64,2048]{1,0:T(8,128)(2,1)S(1)}, u32[]{:S(2)}, u32[]{:S(2)}) collective-permute-start(bf16[64,2048]{1,0:T(8,128)(2,1)S(1)} %collective-permute-done.7.refs_5_), channel_id=1, source_target_pairs={{0,1},{1,0},{2,3},{3,2},{4,5},{5,4},{6,7},{7,6},{8,9},{9,8},{10,11... | collective-permute-start | bytes 786440 | tf_op jit(solution)/shard_map/ppermute | solution.py:24
  49.7 1.8 %collective-permute-start.18 = (bf16[128,1024]{1,0:T(8,128)(2,1)S(1)}, bf16[128,1024]{1,0:T(8,128)(2,1)S(1)}, u32[]{:S(2)}, u32[]{:S(2)}) collective-permute-start(bf16[128,1024]{1,0:T(8,128)(2,1)S(1)} %get-tuple-element.77), channel_id=1, source_target_pairs={{0,1},{1,0},{2,3},{3,2},{4,5},{5,4},{6,7},{7,6},{8,9},{9,8},{10,11... | collective-permute-start | bytes 786440 | tf_op jit(solution)/shard_map/ppermute | solution.py:24
  49.7 1.9 %collective-permute-start.19 = (bf16[128,1024]{1,0:T(8,128)(2,1)S(1)}, bf16[128,1024]{1,0:T(8,128)(2,1)S(1)}, u32[]{:S(2)}, u32[]{:S(2)}) collective-permute-start(bf16[128,1024]{1,0:T(8,128)(2,1)S(1)} %get-tuple-element.79), channel_id=1, source_target_pairs={{0,1},{1,0},{2,3},{3,2},{4,5},{5,4},{6,7},{7,6},{8,9},{9,8},{10,11... | collective-permute-start | bytes 786440 | tf_op jit(solution)/shard_map/ppermute | solution.py:24
  52.8 10.5 %collective-permute-start.20 = (bf16[352,512]{1,0:T(8,128)(2,1)S(1)}, bf16[352,512]{1,0:T(8,128)(2,1)S(1)}, u32[]{:S(2)}, u32[]{:S(2)}) collective-permute-start(bf16[352,512]{1,0:T(8,128)(2,1)S(1)} %shard_map.102), channel_id=1, source_target_pairs={{0,2},{1,3},{2,0},{3,1},{4,6},{5,7},{6,4},{7,5},{8,10},{9,11},{10,... | collective-permute-start | bytes 1081352 | tf_op jit(solution)/shard_map/ppermute | solution.py:24
  54.3 1.6 %collective-permute-start.11 = (bf16[64,2560]{1,0:T(8,128)(2,1)S(1)}, bf16[64,2560]{1,0:T(8,128)(2,1)S(1)}, u32[]{:S(2)}, u32[]{:S(2)}) collective-permute-start(bf16[64,2560]{1,0:T(8,128)(2,1)S(1)} %get-tuple-element.62), channel_id=1, source_target_pairs={{0,1},{1,0},{2,3},{3,2},{4,5},{5,4},{6,7},{7,6},{8,9},{9,8},{10,11... | collective-permute-start | bytes 983048 | tf_op jit(solution)/shard_map/ppermute | solution.py:24
  54.3 2.1 %collective-permute-start.12 = (bf16[64,2560]{1,0:T(8,128)(2,1)S(1)}, bf16[64,2560]{1,0:T(8,128)(2,1)S(1)}, u32[]{:S(2)}, u32[]{:S(2)}) collective-permute-start(bf16[64,2560]{1,0:T(8,128)(2,1)S(1)} %get-tuple-element.64), channel_id=1, source_target_pairs={{0,1},{1,0},{2,3},{3,2},{4,5},{5,4},{6,7},{7,6},{8,9},{9,8},{10,11... | collective-permute-start | bytes 983048 | tf_op jit(solution)/shard_map/ppermute | solution.py:24
  54.9 5.4 %collective-permute-start.22 = (bf16[128,1024]{1,0:T(8,128)(2,1)S(1)}, bf16[128,1024]{1,0:T(8,128)(2,1)S(1)}, u32[]{:S(2)}, u32[]{:S(2)}) collective-permute-start(bf16[128,1024]{1,0:T(8,128)(2,1)S(1)} %get-tuple-element.82), channel_id=1, source_target_pairs={{0,1},{1,0},{2,3},{3,2},{4,5},{5,4},{6,7},{7,6},{8,9},{9,8},{10,11... | collective-permute-start | bytes 786440 | tf_op jit(solution)/shard_map/ppermute | solution.py:24
  55.0 5.6 %collective-permute-start.23 = (bf16[128,1024]{1,0:T(8,128)(2,1)S(1)}, bf16[128,1024]{1,0:T(8,128)(2,1)S(1)}, u32[]{:S(2)}, u32[]{:S(2)}) collective-permute-start(bf16[128,1024]{1,0:T(8,128)(2,1)S(1)} %get-tuple-element.84), channel_id=1, source_target_pairs={{0,1},{1,0},{2,3},{3,2},{4,5},{5,4},{6,7},{7,6},{8,9},{9,8},{10,11... | collective-permute-start | bytes 786440 | tf_op jit(solution)/shard_map/ppermute | solution.py:24
  56.6 9.7 %collective-permute-start.14 = (bf16[16,5120]{1,0:T(8,128)(2,1)S(1)}, bf16[16,5120]{1,0:T(8,128)(2,1)S(1)}, u32[]{:S(2)}, u32[]{:S(2)}) collective-permute-start(bf16[16,5120]{1,0:T(8,128)(2,1)S(1)} %get-tuple-element.69), channel_id=1, source_target_pairs={{0,12},{1,13},{2,14},{3,15},{4,0},{5,1},{6,2},{7,3},{8,4},{9,5},{1... | collective-permute-start | bytes 491528 | tf_op jit(solution)/shard_map/ppermute | solution.py:24
  59.9 15.1 %collective-permute-start.15 = (bf16[16,5120]{1,0:T(8,128)(2,1)S(1)}, bf16[16,5120]{1,0:T(8,128)(2,1)S(1)}, u32[]{:S(2)}, u32[]{:S(2)}) collective-permute-start(bf16[16,5120]{1,0:T(8,128)(2,1)S(1)} %get-tuple-element.71), channel_id=1, source_target_pairs={{0,8},{1,9},{2,10},{3,11},{4,12},{5,13},{6,14},{7,15},{8,0},{9,1},... | collective-permute-start | bytes 491528 | tf_op jit(solution)/shard_map/ppermute | solution.py:24
  60.3 14.7 %collective-permute-start.16 = (bf16[16,5120]{1,0:T(8,128)(2,1)S(1)}, bf16[16,5120]{1,0:T(8,128)(2,1)S(1)}, u32[]{:S(2)}, u32[]{:S(2)}) collective-permute-start(bf16[16,5120]{1,0:T(8,128)(2,1)S(1)} %get-tuple-element.73), channel_id=1, source_target_pairs={{0,4},{1,5},{2,6},{3,7},{4,8},{5,9},{6,10},{7,11},{8,12},{9,13},{1... | collective-permute-start | bytes 491528 | tf_op jit(solution)/shard_map/ppermute | solution.py:24
  61.7 14.0 %collective-permute-start.24 = (bf16[176,512]{1,0:T(8,128)(2,1)S(1)}, bf16[176,512]{1,0:T(8,128)(2,1)S(1)}, u32[]{:S(2)}, u32[]{:S(2)}) collective-permute-start(bf16[176,512]{1,0:T(8,128)(2,1)S(1)} %get-tuple-element.85), channel_id=1, source_target_pairs={{0,18},{1,19},{2,16},{3,17},{4,22},{5,23},{6,20},{7,21},{8,26},{9,... | collective-permute-start | bytes 540680 | tf_op jit(solution)/shard_map/ppermute | solution.py:24
  63.3 12.4 %collective-permute-start.25 = (bf16[176,512]{1,0:T(8,128)(2,1)S(1)}, bf16[176,512]{1,0:T(8,128)(2,1)S(1)}, u32[]{:S(2)}, u32[]{:S(2)}) collective-permute-start(bf16[176,512]{1,0:T(8,128)(2,1)S(1)} %get-tuple-element.86), channel_id=1, source_target_pairs={{0,2},{1,3},{2,0},{3,1},{4,6},{5,7},{6,4},{7,5},{8,10},{9,11},{10,... | collective-permute-start | bytes 540680 | tf_op jit(solution)/shard_map/ppermute | solution.py:24
  66.3 9.4 %collective-permute-start.21 = (bf16[176,512]{1,0:T(8,128)(2,1)S(1)}, bf16[176,512]{1,0:T(8,128)(2,1)S(1)}, u32[]{:S(2)}, u32[]{:S(2)}) collective-permute-start(bf16[176,512]{1,0:T(8,128)(2,1)S(1)} %get-tuple-element.80), channel_id=1, source_target_pairs={{0,16},{1,17},{2,18},{3,19},{4,20},{5,21},{6,22},{7,23},{8,24},{9,... | collective-permute-start | bytes 540680 | tf_op jit(solution)/shard_map/ppermute | solution.py:24
  75.1 1.4 %collective-permute-start.26 = (bf16[16,2560]{1,0:T(8,128)(2,1)S(1)}, bf16[16,2560]{1,0:T(8,128)(2,1)S(1)}, u32[]{:S(2)}, u32[]{:S(2)}) collective-permute-start(bf16[16,2560]{1,0:T(8,128)(2,1)S(1)} %get-tuple-element.89.refs_0_), channel_id=1, source_target_pairs={{0,1},{1,0},{2,3},{3,2},{4,5},{5,4},{6,7},{7,6},{8,9},{9,8},{10,11... | collective-permute-start | bytes 245768 | tf_op jit(solution)/shard_map/ppermute | solution.py:24
  75.2 1.4 %collective-permute-start.27 = (bf16[16,2560]{1,0:T(8,128)(2,1)S(1)}, bf16[16,2560]{1,0:T(8,128)(2,1)S(1)}, u32[]{:S(2)}, u32[]{:S(2)}) collective-permute-start(bf16[16,2560]{1,0:T(8,128)(2,1)S(1)} %get-tuple-element.90.refs_1_), channel_id=1, source_target_pairs={{0,1},{1,0},{2,3},{3,2},{4,5},{5,4},{6,7},{7,6},{8,9},{9,8},{10,11... | collective-permute-start | bytes 245768 | tf_op jit(solution)/shard_map/ppermute | solution.py:24
  (3 other events, 2.2 us)

commit v25 on v24

--- a/solution.py
+++ b/solution.py
@@ -445,7 +445,7 @@
 
     sums = [chip[0]] + [
         moved(after(chip[k], ring[-1]), lambda g, z, s, r: (g, z - k, s, r))
-        for k in range(1, holders)
+        for k in [holders - 1, *range(1, holders - 1)]
     ]
     total = call(total_kernel, [jax.ShapeDtypeStruct((rows, cols // 2), BF16)] * 2, sums)
     totals = list(total)

time: 77.6 us -> 77.8 us (level)
  transfers between devices with their start and end apart: 28 -> 28, of which waited for: 11 -> 12; matrix products, arithmetic and copies ran while one was open for 0% -> 0% of each run, Pallas kernels for 12% -> 12%
where the time goes in v25:
time: 77.8 us; the launch traced here: 77.5 us
  waiting for transfers between devices  31.6 us (41%)
  starting transfers between devices  30 us (39%)
  Pallas kernels  9.75 us (13%)
  local copies, waits for them, and re-layouts  5.37 us (7%)
  between operations  0.81 us (1%)
    ppermute x28, waiting for transfers between devices, moved(): return lax.ppermute(x, AXES, pairs)  31.6 us
    ppermute x28, starting transfers between devices, moved(): return lax.ppermute(x, AXES, pairs)  30 us
    pallas_call x13, Pallas kernels, call(): pl.pallas_call(kernel, out_shape=out_shape, in_specs=[pl.BlockSpec(memory...  8.91 us
    unnamed x14, local copies, waits for them, and re-layouts  4.12 us
  transfers between devices with their start and end apart: 28, of which 12 were waited for; matrix products, arithmetic and copies ran while one was open for 0% of the time, Pallas kernels for 12%

profile of v25, /device:TPU:0, one launch (start us, length us, event | category | flops | bytes accessed | tf_op | source)
XLA Modules:
  0.0 77.5 jit_solution(17631175698891388807)
XLA Ops:
  0.6 1.2 %dynamic-slice_bitcast_fusion = bf16[256,1024]{1,0:T(8,128)(2,1)S(1)} fusion(bf16[1,1024,1024]{2,1,0:T(8,128)(2,1)} %param.11, s32[]{:T(128)S(6)} %select_n.3), kind=kLoop, calls=%fused_computation | loop fusion | bytes 1048580 | tf_op jit(solution)/shard_map/dynamic_slice | solution.py:302
  1.9 3.1 %collective-permute-start.4 = (bf16[256,1024]{1,0:T(8,128)(2,1)S(1)}, bf16[256,1024]{1,0:T(8,128)(2,1)S(1)}, u32[]{:S(2)}, u32[]{:S(2)}) collective-permute-start(bf16[256,1024]{1,0:T(8,128)(2,1)S(1)} %dynamic-slice_bitcast_fusion), channel_id=1, source_target_pairs={{0,4},{1,5},{2,6},{3,7},{4,8},{5,9},{6,10},{7,11},{8,12},{9,13},{1... | collective-permute-start | bytes 1572872 | tf_op jit(solution)/shard_map/ppermute | solution.py:24
  5.0 1.0 %copy-done.2 = bf16[1,176,1024]{2,1,0:T(8,128)(2,1)S(1)} copy-done((bf16[1,176,1024]{2,1,0:T(8,128)(2,1)S(1)}, bf16[1,176,1024]{2,1,0:T(8,128)(2,1)}, u32[]{:S(2)}) %copy-start.2) | copy-done | bytes 360472
  7.3 0.8 shard_map.94.refs_0_.refs_1_
  8.0 1.6 %collective-permute-start.3 = (bf16[176,1152]{1,0:T(8,128)(2,1)S(1)}, bf16[176,1152]{1,0:T(8,128)(2,1)S(1)}, u32[]{:S(2)}, u32[]{:S(2)}) collective-permute-start(bf16[176,1152]{1,0:T(8,128)(2,1)S(1)} %shard_map.94.refs_0_.refs_1_), channel_id=1, source_target_pairs={{0,16},{1,17},{2,18},{3,19},{4,20},{5,21},{6,22},{7,23},{8,24},{9,... | collective-permute-start | bytes 1216520 | tf_op jit(solution)/shard_map/ppermute | solution.py:24
  9.6 0.9 %copy-done.3 = bf16[1,2,16,4096]{3,2,1,0:T(8,128)(2,1)S(1)} copy-done((bf16[1,2,16,4096]{3,2,1,0:T(8,128)(2,1)S(1)}, bf16[1,2,16,4096]{3,2,1,0:T(8,128)(2,1)}, u32[]{:S(2)}) %copy-start.3) | copy-done | bytes 262168
  10.6 0.8 %copy-done.4 = bf16[1,2,16,1024]{3,2,1,0:T(8,128)(2,1)S(1)} copy-done((bf16[1,2,16,1024]{3,2,1,0:T(8,128)(2,1)S(1)}, bf16[1,2,16,1024]{3,2,1,0:T(8,128)(2,1)}, u32[]{:S(2)}) %copy-start.4) | copy-done | bytes 65560
  11.4 1.6 %collective-permute-start = (bf16[16,3072]{1,0:T(8,128)(2,1)S(1)}, bf16[16,3072]{1,0:T(8,128)(2,1)S(1)}, u32[]{:S(2)}, u32[]{:S(2)}) collective-permute-start(bf16[16,3072]{1,0:T(8,128)(2,1)S(1)} %shard_map.95.refs_0_), channel_id=1, source_target_pairs={{0,4},{1,5},{2,6},{3,7},{4,8},{5,9},{6,10},{7,11},{8,12},{9,13},{1... | collective-permute-start | bytes 294920 | tf_op jit(solution)/shard_map/ppermute | solution.py:24
  13.1 1.2 %collective-permute-start.1 = (bf16[16,3072]{1,0:T(8,128)(2,1)S(1)}, bf16[16,3072]{1,0:T(8,128)(2,1)S(1)}, u32[]{:S(2)}, u32[]{:S(2)}) collective-permute-start(bf16[16,3072]{1,0:T(8,128)(2,1)S(1)} %shard_map.95.refs_0_), channel_id=1, source_target_pairs={{0,8},{1,9},{2,10},{3,11},{4,12},{5,13},{6,14},{7,15},{8,0},{9,1},... | collective-permute-start | bytes 294920 | tf_op jit(solution)/shard_map/ppermute | solution.py:24
  14.3 2.7 %collective-permute-start.2 = (bf16[16,3072]{1,0:T(8,128)(2,1)S(1)}, bf16[16,3072]{1,0:T(8,128)(2,1)S(1)}, u32[]{:S(2)}, u32[]{:S(2)}) collective-permute-start(bf16[16,3072]{1,0:T(8,128)(2,1)S(1)} %shard_map.95.refs_0_), channel_id=1, source_target_pairs={{0,12},{1,13},{2,14},{3,15},{4,0},{5,1},{6,2},{7,3},{8,4},{9,5},{1... | collective-permute-start | bytes 294920 | tf_op jit(solution)/shard_map/ppermute | solution.py:24
  17.0 5.0 %collective-permute-done.refs_1_ = bf16[16,3072]{1,0:T(8,128)(2,1)S(1)} collective-permute-done((bf16[16,3072]{1,0:T(8,128)(2,1)S(1)}, bf16[16,3072]{1,0:T(8,128)(2,1)S(1)}, u32[]{:S(2)}, u32[]{:S(2)}) %collective-permute-start) | collective-permute-done | bytes 98336 | tf_op jit(solution)/shard_map/ppermute | solution.py:24
  22.0 3.4 %collective-permute-done.1.refs_2_ = bf16[16,3072]{1,0:T(8,128)(2,1)S(1)} collective-permute-done((bf16[16,3072]{1,0:T(8,128)(2,1)S(1)}, bf16[16,3072]{1,0:T(8,128)(2,1)S(1)}, u32[]{:S(2)}, u32[]{:S(2)}) %collective-permute-start.1) | collective-permute-done | bytes 98336 | tf_op jit(solution)/shard_map/ppermute | solution.py:24
  26.1 2.5 %collective-permute-start.17 = (bf16[256,1024]{1,0:T(8,128)(2,1)S(1)}, bf16[256,1024]{1,0:T(8,128)(2,1)S(1)}, u32[]{:S(2)}, u32[]{:S(2)}) collective-permute-start(bf16[256,1024]{1,0:T(8,128)(2,1)S(1)} %collective-permute-done.4.refs_5_), channel_id=1, source_target_pairs={{0,4},{1,5},{2,6},{3,7},{4,8},{5,9},{6,10},{7,11},{8,12},{9,13},{1... | collective-permute-start | bytes 1572872 | tf_op jit(solution)/shard_map/ppermute | solution.py:24
  28.6 2.2 %shard_map.97 = (bf16[176,1024]{1,0:T(8,128)(2,1)S(1)}, bf16[176,1024]{1,0:T(8,128)(2,1)S(1)}, bf16[352,128]{1,0:T(8,128)(2,1)S(1)}) custom-call(bf16[176,1152]{1,0:T(8,128)(2,1)S(1)} %shard_map.94.refs_0_.refs_1_, bf16[176,1152]{1,0:T(8,128)(2,1)S(1)} %collective-permute-done.3.refs_1_, bf16[64,3072]{1,0:T(8,128)(2,1)S(1)} %get-tuple-element.54.refs_2_.refs_3_, ...), custom_call_target="tpu_custom_call" | custom-call | flops 1000 | bytes 1000 | tf_op jit(solution)/shard_map/pallas_call | solution.py:41
  30.8 1.6 %collective-permute-start.9 = (bf16[176,1024]{1,0:T(8,128)(2,1)S(1)}, bf16[176,1024]{1,0:T(8,128)(2,1)S(1)}, u32[]{:S(2)}, u32[]{:S(2)}) collective-permute-start(bf16[176,1024]{1,0:T(8,128)(2,1)S(1)} %get-tuple-element.60), channel_id=1, source_target_pairs={{0,2},{1,3},{2,0},{3,1},{4,6},{5,7},{6,4},{7,5},{8,10},{9,11},{10,... | collective-permute-start | bytes 1081352 | tf_op jit(solution)/shard_map/ppermute | solution.py:24
  32.4 1.5 %collective-permute-start.10 = (bf16[176,1024]{1,0:T(8,128)(2,1)S(1)}, bf16[176,1024]{1,0:T(8,128)(2,1)S(1)}, u32[]{:S(2)}, u32[]{:S(2)}) collective-permute-start(bf16[176,1024]{1,0:T(8,128)(2,1)S(1)} %get-tuple-element.61), channel_id=1, source_target_pairs={{0,18},{1,19},{2,16},{3,17},{4,22},{5,23},{6,20},{7,21},{8,26},{9,... | collective-permute-start | bytes 1081352 | tf_op jit(solution)/shard_map/ppermute | solution.py:24
  34.4 2.9 %collective-permute-start.13 = (bf16[256,1024]{1,0:T(8,128)(2,1)S(1)}, bf16[256,1024]{1,0:T(8,128)(2,1)S(1)}, u32[]{:S(2)}, u32[]{:S(2)}) collective-permute-start(bf16[256,1024]{1,0:T(8,128)(2,1)S(1)} %dynamic-slice_bitcast_fusion), channel_id=1, source_target_pairs={{0,12},{1,13},{2,14},{3,15},{4,0},{5,1},{6,2},{7,3},{8,4},{9,5},{1... | collective-permute-start | bytes 1572872 | tf_op jit(solution)/shard_map/ppermute | solution.py:24
  37.3 4.6 %collective-permute-done.7.refs_5_ = bf16[64,2048]{1,0:T(8,128)(2,1)S(1)} collective-permute-done((bf16[64,2048]{1,0:T(8,128)(2,1)S(1)}, bf16[64,2048]{1,0:T(8,128)(2,1)S(1)}, u32[]{:S(2)}, u32[]{:S(2)}) %collective-permute-start.7) | collective-permute-done | bytes 262176 | tf_op jit(solution)/shard_map/ppermute | solution.py:24
  41.9 0.8 %collective-permute-done.17.block_ref.refs_5_ = bf16[256,1024]{1,0:T(8,128)(2,1)S(1)} collective-permute-done((bf16[256,1024]{1,0:T(8,128)(2,1)S(1)}, bf16[256,1024]{1,0:T(8,128)(2,1)S(1)}, u32[]{:S(2)}, u32[]{:S(2)}) %collective-permute-start.17) | collective-permute-done | bytes 524320 | tf_op jit(solution)/shard_map/ppermute | solution.py:24
  42.7 7.0 %collective-permute-done.10.refs_1_ = bf16[176,1024]{1,0:T(8,128)(2,1)S(1)} collective-permute-done((bf16[176,1024]{1,0:T(8,128)(2,1)S(1)}, bf16[176,1024]{1,0:T(8,128)(2,1)S(1)}, u32[]{:S(2)}, u32[]{:S(2)}) %collective-permute-start.10) | collective-permute-done | bytes 360480 | tf_op jit(solution)/shard_map/ppermute | solution.py:24
  50.2 1.3 %shard_map.98 = (f32[64,5120]{1,0:T(8,128)S(1)}, bf16[64,2560]{1,0:T(8,128)(2,1)S(1)}, bf16[64,2560]{1,0:T(8,128)(2,1)S(1)}) custom-call(bf16[176,4096]{1,0:T(8,128)(2,1)S(1)} %bitcast.12, bf16[176,1152]{1,0:T(8,128)(2,1)S(1)} %shard_map.94.refs_0_.refs_1_, bf16[352,128]{1,0:T(8,128)(2,1)S(1)} %get-tuple-element.56.refs_2_.refs_4_, ...), custom_call_target="tpu_custom_call" | custom-call | flops 1000 | bytes 1000 | tf_op jit(solution)/shard_map/pallas_call | solution.py:41
  51.6 1.2 %shard_map.102 = bf16[352,512]{1,0:T(8,128)(2,1)S(1)} custom-call(bf16[176,1152]{1,0:T(8,128)(2,1)S(1)} %shard_map.94.refs_0_.refs_1_, bf16[176,1152]{1,0:T(8,128)(2,1)S(1)} %collective-permute-done.3.refs_1_, bf16[64,3072]{1,0:T(8,128)(2,1)S(1)} %get-tuple-element.54.refs_2_.refs_3_, bf16[64,3072]{1,0:T(8,128)(2,1)S(1)} %collective-permute-done.5.refs_3_.refs_4_, ...), custom_call_target="tpu_custom_call" | custom-call | flops 1000 | bytes 1000 | tf_op jit(solution)/shard_map/pallas_call | solution.py:41
  52.8 1.6 %collective-permute-start.20 = (bf16[352,512]{1,0:T(8,128)(2,1)S(1)}, bf16[352,512]{1,0:T(8,128)(2,1)S(1)}, u32[]{:S(2)}, u32[]{:S(2)}) collective-permute-start(bf16[352,512]{1,0:T(8,128)(2,1)S(1)} %shard_map.102), channel_id=1, source_target_pairs={{0,2},{1,3},{2,0},{3,1},{4,6},{5,7},{6,4},{7,5},{8,10},{9,11},{10,... | collective-permute-start | bytes 1081352 | tf_op jit(solution)/shard_map/ppermute | solution.py:24
  56.6 2.2 %collective-permute-start.14 = (bf16[16,5120]{1,0:T(8,128)(2,1)S(1)}, bf16[16,5120]{1,0:T(8,128)(2,1)S(1)}, u32[]{:S(2)}, u32[]{:S(2)}) collective-permute-start(bf16[16,5120]{1,0:T(8,128)(2,1)S(1)} %get-tuple-element.69), channel_id=1, source_target_pairs={{0,4},{1,5},{2,6},{3,7},{4,8},{5,9},{6,10},{7,11},{8,12},{9,13},{1... | collective-permute-start | bytes 491528 | tf_op jit(solution)/shard_map/ppermute | solution.py:24
  58.8 1.6 %collective-permute-start.15 = (bf16[16,5120]{1,0:T(8,128)(2,1)S(1)}, bf16[16,5120]{1,0:T(8,128)(2,1)S(1)}, u32[]{:S(2)}, u32[]{:S(2)}) collective-permute-start(bf16[16,5120]{1,0:T(8,128)(2,1)S(1)} %get-tuple-element.71), channel_id=1, source_target_pairs={{0,12},{1,13},{2,14},{3,15},{4,0},{5,1},{6,2},{7,3},{8,4},{9,5},{1... | collective-permute-start | bytes 491528 | tf_op jit(solution)/shard_map/ppermute | solution.py:24
  60.5 1.2 %shard_map.105 = (bf16[176,512]{1,0:T(8,128)(2,1)S(1)}, bf16[176,512]{1,0:T(8,128)(2,1)S(1)}) custom-call(bf16[176,1152]{1,0:T(8,128)(2,1)S(1)} %shard_map.94.refs_0_.refs_1_, bf16[176,1152]{1,0:T(8,128)(2,1)S(1)} %collective-permute-done.3.refs_1_, bf16[64,3072]{1,0:T(8,128)(2,1)S(1)} %get-tuple-element.54.refs_2_.refs_3_, ...), custom_call_target="tpu_custom_call" | custom-call | flops 1000 | bytes 1000 | tf_op jit(solution)/shard_map/pallas_call | solution.py:41
  62.2 1.1 %collective-permute-done.20 = bf16[352,512]{1,0:T(8,128)(2,1)S(1)} collective-permute-done((bf16[352,512]{1,0:T(8,128)(2,1)S(1)}, bf16[352,512]{1,0:T(8,128)(2,1)S(1)}, u32[]{:S(2)}, u32[]{:S(2)}) %collective-permute-start.20) | collective-permute-done | bytes 360480 | tf_op jit(solution)/shard_map/ppermute | solution.py:24
  63.3 1.9 %collective-permute-start.25 = (bf16[176,512]{1,0:T(8,128)(2,1)S(1)}, bf16[176,512]{1,0:T(8,128)(2,1)S(1)}, u32[]{:S(2)}, u32[]{:S(2)}) collective-permute-start(bf16[176,512]{1,0:T(8,128)(2,1)S(1)} %get-tuple-element.86), channel_id=1, source_target_pairs={{0,2},{1,3},{2,0},{3,1},{4,6},{5,7},{6,4},{7,5},{8,10},{9,11},{10,... | collective-permute-start | bytes 540680 | tf_op jit(solution)/shard_map/ppermute | solution.py:24
  65.2 1.2 %shard_map.103.refs_3_ = bf16[176,4096]{1,0:T(8,128)(2,1)} custom-call(bf16[176,1024]{1,0:T(8,128)(2,1)S(1)} %collective-permute-done.9.refs_0_, bf16[176,1024]{1,0:T(8,128)(2,1)S(1)} %collective-permute-done.10.refs_1_, bf16[176,512]{1,0:T(8,128)(2,1)S(1)} %get-tuple-element.94.refs_2_), custom_call_target="tpu_custom_call" | custom-call | flops 1000 | bytes 1000 | tf_op jit(solution)/shard_map/pallas_call | solution.py:41
  66.5 1.7 %collective-permute-done.15.refs_2_ = bf16[16,5120]{1,0:T(8,128)(2,1)S(1)} collective-permute-done((bf16[16,5120]{1,0:T(8,128)(2,1)S(1)}, bf16[16,5120]{1,0:T(8,128)(2,1)S(1)}, u32[]{:S(2)}, u32[]{:S(2)}) %collective-permute-start.15) | collective-permute-done | bytes 163872 | tf_op jit(solution)/shard_map/ppermute | solution.py:24
  68.2 7.0 %collective-permute-done.16.refs_3_ = bf16[16,5120]{1,0:T(8,128)(2,1)S(1)} collective-permute-done((bf16[16,5120]{1,0:T(8,128)(2,1)S(1)}, bf16[16,5120]{1,0:T(8,128)(2,1)S(1)}, u32[]{:S(2)}, u32[]{:S(2)}) %collective-permute-start.16) | collective-permute-done | bytes 163872 | tf_op jit(solution)/shard_map/ppermute | solution.py:24
  75.9 0.8 %shard_map.106 = bf16[176,4096]{1,0:T(8,128)(2,1)} custom-call(bf16[176,512]{1,0:T(8,128)(2,1)S(1)} %collective-permute-done.21.refs_0_, bf16[176,512]{1,0:T(8,128)(2,1)S(1)} %collective-permute-done.24.refs_1_, bf16[176,512]{1,0:T(8,128)(2,1)S(1)} %collective-permute-done.25.refs_2_, ...), custom_call_target="tpu_custom_call", output_to_operand_aliasing={{}: (3, {})} | custom-call | flops 1000 | bytes 1000 | tf_op jit(solution)/shard_map/pallas_call | solution.py:426
  (54 shorter events, 7.6 us)
Async XLA Ops:
  0.6 27.9 %copy-start = (bf16[1,1024,1024]{2,1,0:T(8,128)(2,1)S(1)}, bf16[1,1024,1024]{2,1,0:T(8,128)(2,1)}, u32[]{:S(2)}) copy-start(bf16[1,1024,1024]{2,1,0:T(8,128)(2,1)} %param.11) | copy-start | bytes 6291460
  1.9 23.5 %collective-permute-start.4 = (bf16[256,1024]{1,0:T(8,128)(2,1)S(1)}, bf16[256,1024]{1,0:T(8,128)(2,1)S(1)}, u32[]{:S(2)}, u32[]{:S(2)}) collective-permute-start(bf16[256,1024]{1,0:T(8,128)(2,1)S(1)} %dynamic-slice_bitcast_fusion), channel_id=1, source_target_pairs={{0,4},{1,5},{2,6},{3,7},{4,8},{5,9},{6,10},{7,11},{8,12},{9,13},{1... | collective-permute-start | bytes 1572872 | tf_op jit(solution)/shard_map/ppermute | solution.py:24
  5.0 1.0 %copy-start.2 = (bf16[1,176,1024]{2,1,0:T(8,128)(2,1)S(1)}, bf16[1,176,1024]{2,1,0:T(8,128)(2,1)}, u32[]{:S(2)}) copy-start(bf16[1,176,1024]{2,1,0:T(8,128)(2,1)} %param.8) | copy-start | bytes 1081348
  8.0 17.3 %collective-permute-start.3 = (bf16[176,1152]{1,0:T(8,128)(2,1)S(1)}, bf16[176,1152]{1,0:T(8,128)(2,1)S(1)}, u32[]{:S(2)}, u32[]{:S(2)}) collective-permute-start(bf16[176,1152]{1,0:T(8,128)(2,1)S(1)} %shard_map.94.refs_0_.refs_1_), channel_id=1, source_target_pairs={{0,16},{1,17},{2,18},{3,19},{4,20},{5,21},{6,22},{7,23},{8,24},{9,... | collective-permute-start | bytes 1216520 | tf_op jit(solution)/shard_map/ppermute | solution.py:24
  9.6 0.9 %copy-start.3 = (bf16[1,2,16,4096]{3,2,1,0:T(8,128)(2,1)S(1)}, bf16[1,2,16,4096]{3,2,1,0:T(8,128)(2,1)}, u32[]{:S(2)}) copy-start(bf16[1,2,16,4096]{3,2,1,0:T(8,128)(2,1)} %param.12) | copy-start | bytes 786436
  11.4 10.5 %collective-permute-start = (bf16[16,3072]{1,0:T(8,128)(2,1)S(1)}, bf16[16,3072]{1,0:T(8,128)(2,1)S(1)}, u32[]{:S(2)}, u32[]{:S(2)}) collective-permute-start(bf16[16,3072]{1,0:T(8,128)(2,1)S(1)} %shard_map.95.refs_0_), channel_id=1, source_target_pairs={{0,4},{1,5},{2,6},{3,7},{4,8},{5,9},{6,10},{7,11},{8,12},{9,13},{1... | collective-permute-start | bytes 294920 | tf_op jit(solution)/shard_map/ppermute | solution.py:24
  13.1 12.3 %collective-permute-start.1 = (bf16[16,3072]{1,0:T(8,128)(2,1)S(1)}, bf16[16,3072]{1,0:T(8,128)(2,1)S(1)}, u32[]{:S(2)}, u32[]{:S(2)}) collective-permute-start(bf16[16,3072]{1,0:T(8,128)(2,1)S(1)} %shard_map.95.refs_0_), channel_id=1, source_target_pairs={{0,8},{1,9},{2,10},{3,11},{4,12},{5,13},{6,14},{7,15},{8,0},{9,1},... | collective-permute-start | bytes 294920 | tf_op jit(solution)/shard_map/ppermute | solution.py:24
  14.3 11.1 %collective-permute-start.2 = (bf16[16,3072]{1,0:T(8,128)(2,1)S(1)}, bf16[16,3072]{1,0:T(8,128)(2,1)S(1)}, u32[]{:S(2)}, u32[]{:S(2)}) collective-permute-start(bf16[16,3072]{1,0:T(8,128)(2,1)S(1)} %shard_map.95.refs_0_), channel_id=1, source_target_pairs={{0,12},{1,13},{2,14},{3,15},{4,0},{5,1},{6,2},{7,3},{8,4},{9,5},{1... | collective-permute-start | bytes 294920 | tf_op jit(solution)/shard_map/ppermute | solution.py:24
  25.4 3.2 %collective-permute-start.6 = (bf16[256,1024]{1,0:T(8,128)(2,1)S(1)}, bf16[256,1024]{1,0:T(8,128)(2,1)S(1)}, u32[]{:S(2)}, u32[]{:S(2)}) collective-permute-start(bf16[256,1024]{1,0:T(8,128)(2,1)S(1)} %collective-permute-done.4.refs_5_), channel_id=1, source_target_pairs={{0,1},{1,0},{2,3},{3,2},{4,5},{5,4},{6,7},{7,6},{8,9},{9,8},{10,11... | collective-permute-start | bytes 1572872 | tf_op jit(solution)/shard_map/ppermute | solution.py:24
  25.5 3.1 %collective-permute-start.5 = (bf16[64,3072]{1,0:T(8,128)(2,1)S(1)}, bf16[64,3072]{1,0:T(8,128)(2,1)S(1)}, u32[]{:S(2)}, u32[]{:S(2)}) collective-permute-start(bf16[64,3072]{1,0:T(8,128)(2,1)S(1)} %get-tuple-element.54.refs_2_.refs_3_), channel_id=1, source_target_pairs={{0,1},{1,0},{2,3},{3,2},{4,5},{5,4},{6,7},{7,6},{8,9},{9,8},{10,11... | collective-permute-start | bytes 1179656 | tf_op jit(solution)/shard_map/ppermute | solution.py:24
  26.1 16.6 %collective-permute-start.17 = (bf16[256,1024]{1,0:T(8,128)(2,1)S(1)}, bf16[256,1024]{1,0:T(8,128)(2,1)S(1)}, u32[]{:S(2)}, u32[]{:S(2)}) collective-permute-start(bf16[256,1024]{1,0:T(8,128)(2,1)S(1)} %collective-permute-done.4.refs_5_), channel_id=1, source_target_pairs={{0,4},{1,5},{2,6},{3,7},{4,8},{5,9},{6,10},{7,11},{8,12},{9,13},{1... | collective-permute-start | bytes 1572872 | tf_op jit(solution)/shard_map/ppermute | solution.py:24
  28.6 21.6 %copy-start.1 = (bf16[1,176,4096]{2,1,0:T(8,128)(2,1)S(1)}, bf16[1,176,4096]{2,1,0:T(8,128)(2,1)}, u32[]{:S(2)}) copy-start(bf16[1,176,4096]{2,1,0:T(8,128)(2,1)} %param.7) | copy-start | bytes 4325380
  30.8 11.9 %collective-permute-start.9 = (bf16[176,1024]{1,0:T(8,128)(2,1)S(1)}, bf16[176,1024]{1,0:T(8,128)(2,1)S(1)}, u32[]{:S(2)}, u32[]{:S(2)}) collective-permute-start(bf16[176,1024]{1,0:T(8,128)(2,1)S(1)} %get-tuple-element.60), channel_id=1, source_target_pairs={{0,2},{1,3},{2,0},{3,1},{4,6},{5,7},{6,4},{7,5},{8,10},{9,11},{10,... | collective-permute-start | bytes 1081352 | tf_op jit(solution)/shard_map/ppermute | solution.py:24
  32.4 17.3 %collective-permute-start.10 = (bf16[176,1024]{1,0:T(8,128)(2,1)S(1)}, bf16[176,1024]{1,0:T(8,128)(2,1)S(1)}, u32[]{:S(2)}, u32[]{:S(2)}) collective-permute-start(bf16[176,1024]{1,0:T(8,128)(2,1)S(1)} %get-tuple-element.61), channel_id=1, source_target_pairs={{0,18},{1,19},{2,16},{3,17},{4,22},{5,23},{6,20},{7,21},{8,26},{9,... | collective-permute-start | bytes 1081352 | tf_op jit(solution)/shard_map/ppermute | solution.py:24
  33.9 8.0 %collective-permute-start.7 = (bf16[64,2048]{1,0:T(8,128)(2,1)S(1)}, bf16[64,2048]{1,0:T(8,128)(2,1)S(1)}, u32[]{:S(2)}, u32[]{:S(2)}) collective-permute-start(bf16[64,2048]{1,0:T(8,128)(2,1)S(1)} %get-tuple-element.57), channel_id=1, source_target_pairs={{0,16},{1,17},{2,18},{3,19},{4,20},{5,21},{6,22},{7,23},{8,24},{9,... | collective-permute-start | bytes 786440 | tf_op jit(solution)/shard_map/ppermute | solution.py:24
  34.4 20.5 %collective-permute-start.13 = (bf16[256,1024]{1,0:T(8,128)(2,1)S(1)}, bf16[256,1024]{1,0:T(8,128)(2,1)S(1)}, u32[]{:S(2)}, u32[]{:S(2)}) collective-permute-start(bf16[256,1024]{1,0:T(8,128)(2,1)S(1)} %dynamic-slice_bitcast_fusion), channel_id=1, source_target_pairs={{0,12},{1,13},{2,14},{3,15},{4,0},{5,1},{6,2},{7,3},{8,4},{9,5},{1... | collective-permute-start | bytes 1572872 | tf_op jit(solution)/shard_map/ppermute | solution.py:24
  41.9 8.3 %collective-permute-start.8 = (bf16[64,2048]{1,0:T(8,128)(2,1)S(1)}, bf16[64,2048]{1,0:T(8,128)(2,1)S(1)}, u32[]{:S(2)}, u32[]{:S(2)}) collective-permute-start(bf16[64,2048]{1,0:T(8,128)(2,1)S(1)} %collective-permute-done.7.refs_5_), channel_id=1, source_target_pairs={{0,1},{1,0},{2,3},{3,2},{4,5},{5,4},{6,7},{7,6},{8,9},{9,8},{10,11... | collective-permute-start | bytes 786440 | tf_op jit(solution)/shard_map/ppermute | solution.py:24
  49.7 1.8 %collective-permute-start.18 = (bf16[128,1024]{1,0:T(8,128)(2,1)S(1)}, bf16[128,1024]{1,0:T(8,128)(2,1)S(1)}, u32[]{:S(2)}, u32[]{:S(2)}) collective-permute-start(bf16[128,1024]{1,0:T(8,128)(2,1)S(1)} %get-tuple-element.77), channel_id=1, source_target_pairs={{0,1},{1,0},{2,3},{3,2},{4,5},{5,4},{6,7},{7,6},{8,9},{9,8},{10,11... | collective-permute-start | bytes 786440 | tf_op jit(solution)/shard_map/ppermute | solution.py:24
  49.7 1.9 %collective-permute-start.19 = (bf16[128,1024]{1,0:T(8,128)(2,1)S(1)}, bf16[128,1024]{1,0:T(8,128)(2,1)S(1)}, u32[]{:S(2)}, u32[]{:S(2)}) collective-permute-start(bf16[128,1024]{1,0:T(8,128)(2,1)S(1)} %get-tuple-element.79), channel_id=1, source_target_pairs={{0,1},{1,0},{2,3},{3,2},{4,5},{5,4},{6,7},{7,6},{8,9},{9,8},{10,11... | collective-permute-start | bytes 786440 | tf_op jit(solution)/shard_map/ppermute | solution.py:24
  52.8 10.5 %collective-permute-start.20 = (bf16[352,512]{1,0:T(8,128)(2,1)S(1)}, bf16[352,512]{1,0:T(8,128)(2,1)S(1)}, u32[]{:S(2)}, u32[]{:S(2)}) collective-permute-start(bf16[352,512]{1,0:T(8,128)(2,1)S(1)} %shard_map.102), channel_id=1, source_target_pairs={{0,2},{1,3},{2,0},{3,1},{4,6},{5,7},{6,4},{7,5},{8,10},{9,11},{10,... | collective-permute-start | bytes 1081352 | tf_op jit(solution)/shard_map/ppermute | solution.py:24
  54.3 1.6 %collective-permute-start.11 = (bf16[64,2560]{1,0:T(8,128)(2,1)S(1)}, bf16[64,2560]{1,0:T(8,128)(2,1)S(1)}, u32[]{:S(2)}, u32[]{:S(2)}) collective-permute-start(bf16[64,2560]{1,0:T(8,128)(2,1)S(1)} %get-tuple-element.62), channel_id=1, source_target_pairs={{0,1},{1,0},{2,3},{3,2},{4,5},{5,4},{6,7},{7,6},{8,9},{9,8},{10,11... | collective-permute-start | bytes 983048 | tf_op jit(solution)/shard_map/ppermute | solution.py:24
  54.3 2.1 %collective-permute-start.12 = (bf16[64,2560]{1,0:T(8,128)(2,1)S(1)}, bf16[64,2560]{1,0:T(8,128)(2,1)S(1)}, u32[]{:S(2)}, u32[]{:S(2)}) collective-permute-start(bf16[64,2560]{1,0:T(8,128)(2,1)S(1)} %get-tuple-element.64), channel_id=1, source_target_pairs={{0,1},{1,0},{2,3},{3,2},{4,5},{5,4},{6,7},{7,6},{8,9},{9,8},{10,11... | collective-permute-start | bytes 983048 | tf_op jit(solution)/shard_map/ppermute | solution.py:24
  54.9 5.6 %collective-permute-start.22 = (bf16[128,1024]{1,0:T(8,128)(2,1)S(1)}, bf16[128,1024]{1,0:T(8,128)(2,1)S(1)}, u32[]{:S(2)}, u32[]{:S(2)}) collective-permute-start(bf16[128,1024]{1,0:T(8,128)(2,1)S(1)} %get-tuple-element.82), channel_id=1, source_target_pairs={{0,1},{1,0},{2,3},{3,2},{4,5},{5,4},{6,7},{7,6},{8,9},{9,8},{10,11... | collective-permute-start | bytes 786440 | tf_op jit(solution)/shard_map/ppermute | solution.py:24
  55.0 5.5 %collective-permute-start.23 = (bf16[128,1024]{1,0:T(8,128)(2,1)S(1)}, bf16[128,1024]{1,0:T(8,128)(2,1)S(1)}, u32[]{:S(2)}, u32[]{:S(2)}) collective-permute-start(bf16[128,1024]{1,0:T(8,128)(2,1)S(1)} %get-tuple-element.84), channel_id=1, source_target_pairs={{0,1},{1,0},{2,3},{3,2},{4,5},{5,4},{6,7},{7,6},{8,9},{9,8},{10,11... | collective-permute-start | bytes 786440 | tf_op jit(solution)/shard_map/ppermute | solution.py:24
  56.6 9.8 %collective-permute-start.14 = (bf16[16,5120]{1,0:T(8,128)(2,1)S(1)}, bf16[16,5120]{1,0:T(8,128)(2,1)S(1)}, u32[]{:S(2)}, u32[]{:S(2)}) collective-permute-start(bf16[16,5120]{1,0:T(8,128)(2,1)S(1)} %get-tuple-element.69), channel_id=1, source_target_pairs={{0,4},{1,5},{2,6},{3,7},{4,8},{5,9},{6,10},{7,11},{8,12},{9,13},{1... | collective-permute-start | bytes 491528 | tf_op jit(solution)/shard_map/ppermute | solution.py:24
  58.8 9.4 %collective-permute-start.15 = (bf16[16,5120]{1,0:T(8,128)(2,1)S(1)}, bf16[16,5120]{1,0:T(8,128)(2,1)S(1)}, u32[]{:S(2)}, u32[]{:S(2)}) collective-permute-start(bf16[16,5120]{1,0:T(8,128)(2,1)S(1)} %get-tuple-element.71), channel_id=1, source_target_pairs={{0,12},{1,13},{2,14},{3,15},{4,0},{5,1},{6,2},{7,3},{8,4},{9,5},{1... | collective-permute-start | bytes 491528 | tf_op jit(solution)/shard_map/ppermute | solution.py:24
  60.4 14.7 %collective-permute-start.16 = (bf16[16,5120]{1,0:T(8,128)(2,1)S(1)}, bf16[16,5120]{1,0:T(8,128)(2,1)S(1)}, u32[]{:S(2)}, u32[]{:S(2)}) collective-permute-start(bf16[16,5120]{1,0:T(8,128)(2,1)S(1)} %get-tuple-element.73), channel_id=1, source_target_pairs={{0,8},{1,9},{2,10},{3,11},{4,12},{5,13},{6,14},{7,15},{8,0},{9,1},... | collective-permute-start | bytes 491528 | tf_op jit(solution)/shard_map/ppermute | solution.py:24
  61.6 14.2 %collective-permute-start.24 = (bf16[176,512]{1,0:T(8,128)(2,1)S(1)}, bf16[176,512]{1,0:T(8,128)(2,1)S(1)}, u32[]{:S(2)}, u32[]{:S(2)}) collective-permute-start(bf16[176,512]{1,0:T(8,128)(2,1)S(1)} %get-tuple-element.85), channel_id=1, source_target_pairs={{0,18},{1,19},{2,16},{3,17},{4,22},{5,23},{6,20},{7,21},{8,26},{9,... | collective-permute-start | bytes 540680 | tf_op jit(solution)/shard_map/ppermute | solution.py:24
  63.3 12.6 %collective-permute-start.25 = (bf16[176,512]{1,0:T(8,128)(2,1)S(1)}, bf16[176,512]{1,0:T(8,128)(2,1)S(1)}, u32[]{:S(2)}, u32[]{:S(2)}) collective-permute-start(bf16[176,512]{1,0:T(8,128)(2,1)S(1)} %get-tuple-element.86), channel_id=1, source_target_pairs={{0,2},{1,3},{2,0},{3,1},{4,6},{5,7},{6,4},{7,5},{8,10},{9,11},{10,... | collective-permute-start | bytes 540680 | tf_op jit(solution)/shard_map/ppermute | solution.py:24
  66.4 9.5 %collective-permute-start.21 = (bf16[176,512]{1,0:T(8,128)(2,1)S(1)}, bf16[176,512]{1,0:T(8,128)(2,1)S(1)}, u32[]{:S(2)}, u32[]{:S(2)}) collective-permute-start(bf16[176,512]{1,0:T(8,128)(2,1)S(1)} %get-tuple-element.80), channel_id=1, source_target_pairs={{0,16},{1,17},{2,18},{3,19},{4,20},{5,21},{6,22},{7,23},{8,24},{9,... | collective-permute-start | bytes 540680 | tf_op jit(solution)/shard_map/ppermute | solution.py:24
  75.3 1.4 %collective-permute-start.26 = (bf16[16,2560]{1,0:T(8,128)(2,1)S(1)}, bf16[16,2560]{1,0:T(8,128)(2,1)S(1)}, u32[]{:S(2)}, u32[]{:S(2)}) collective-permute-start(bf16[16,2560]{1,0:T(8,128)(2,1)S(1)} %get-tuple-element.89.refs_0_), channel_id=1, source_target_pairs={{0,1},{1,0},{2,3},{3,2},{4,5},{5,4},{6,7},{7,6},{8,9},{9,8},{10,11... | collective-permute-start | bytes 245768 | tf_op jit(solution)/shard_map/ppermute | solution.py:24
  75.4 1.4 %collective-permute-start.27 = (bf16[16,2560]{1,0:T(8,128)(2,1)S(1)}, bf16[16,2560]{1,0:T(8,128)(2,1)S(1)}, u32[]{:S(2)}, u32[]{:S(2)}) collective-permute-start(bf16[16,2560]{1,0:T(8,128)(2,1)S(1)} %get-tuple-element.90.refs_1_), channel_id=1, source_target_pairs={{0,1},{1,0},{2,3},{3,2},{4,5},{5,4},{6,7},{7,6},{8,9},{9,8},{10,11... | collective-permute-start | bytes 245768 | tf_op jit(solution)/shard_map/ppermute | solution.py:24
  (3 other events, 2.2 us)
